TPU v7x, 128 devices: a whole 4x4x4 slice. The times are simulated.
128 devices in a mesh: img: 2 (over x_lo), ctx: 16 (over z, y), tp: 4 (over x_hi, core).
Axes of the slice: x: 4 (x_hi: 2, x_lo: 2; x = x_hi * 2 + x_lo), y: 4, z: 4, core: 2. Of those that a mesh axis runs over, the one named last changes fastest.
Arguments:
- features: bfloat16 [1, 32768, 1152], P(None, ('img', 'ctx')), may hold values from -60 to 60
- ln_gain: bfloat16 [1, 4, 1152], replicated, may hold values from 0.099609375 to 1.8984375
- ln_bias: bfloat16 [1, 4, 1152], replicated, may hold values from -3 to 3
- projection: bfloat16 [1, 4, 1152, 4096], P(None, None, 'ctx', 'tp'), may hold values from -0.09375 to 0.09375
- stream: bfloat16 [16384, 4096], P(('img', 'ctx'), 'tp'), may hold values from -12 to 12
- norm_gain: bfloat16 [1, 4096], P(None, 'tp'), may hold values from 0.099609375 to 1.8984375
- cotangent: bfloat16 [1, 16384, 4096], P(None, ('img', 'ctx'), 'tp'), may hold values from -6 to 6
- slots: int32 [8192], P(('img', 'ctx')), may hold values from 0 to 16383, as said below
Outputs:
- new_stream: bfloat16 [16384, 4096], P(('img', 'ctx'), 'tp')
- feature_grad: bfloat16 [1, 32768, 1152], P(None, ('img', 'ctx'))
Inputs may be any that keep to these rules, and one draw needn't show every extreme that they name: `slots`: the 8192 positions are distinct. Of the 256 tokens of one device of img+ctx, at most 16 fall into any aligned block of 512 positions, and in every draw one block holds exactly 16 tokens of every device.
All inputs are finite; a program needn't handle non-finite values.
Results may differ from a plain program's by a relative error of at most 0.0049.
Values may be sent and summed in bfloat16 or wider, within the bound.
No kernel may reach another device: no remote copies, remote signals or barrier semaphores. Data moves between devices by JAX's collectives and lax.ppermute only.
A program may use at most 128 MiB of HBM per device.

v0:
```python
import jax
import jax.numpy as jnp
from jax import lax
from jax.sharding import PartitionSpec as P


def one_hot_rows(count, index):
    return (jnp.arange(count)[:, None] == index[None, :]).astype(jnp.bfloat16)


def shards(features, ln_gain, ln_bias, projection, stream, norm_gain, cotangent, slots):
    n_img = lax.axis_size("img")
    n_ctx = lax.axis_size("ctx")
    n_tp = lax.axis_size("tp")
    depth_count = features.shape[0]
    merged = slots.shape[0]
    window = ln_gain.shape[1]
    vision_width = features.shape[2]
    full_in = window * vision_width
    tok_rows = stream.shape[0]
    width_tp = stream.shape[1]
    full_width = width_tp * n_tp
    owners = n_img * n_ctx
    capacity = 2 * merged // owners
    slot_count = owners * capacity
    owner_index = lax.axis_index("img") * n_ctx + lax.axis_index("ctx")
    target = slots // tok_rows
    row_ids = jnp.arange(merged)
    earlier = (target[:, None] == target[None, :]) & (row_ids[None, :] < row_ids[:, None])
    slot_rank = jnp.sum(earlier.astype(jnp.int32), axis=1)
    pack = one_hot_rows(slot_count, target * capacity + slot_rank)
    packed_pos = jnp.max(jnp.where(pack > 0, slots[None, :], -1), axis=1)
    weight_held = lax.all_gather(projection, "ctx", axis=2, tiled=True)
    current = stream.astype(jnp.float32)
    depth_index = 0
    windows = features[depth_index].reshape(merged, full_in).astype(jnp.float32)
    row_mean = jnp.mean(windows, axis=1, keepdims=True)
    square_mean = jnp.mean(windows * windows, axis=1, keepdims=True)
    inv_std = lax.rsqrt(square_mean - row_mean * row_mean + 1e-05)
    normed = (windows - row_mean) * inv_std
    gain_row = ln_gain[depth_index].reshape(1, full_in).astype(jnp.float32)
    bias_row = ln_bias[depth_index].reshape(1, full_in).astype(jnp.float32)
    lifted = (normed * gain_row + bias_row).astype(jnp.bfloat16)
    weights = weight_held[depth_index].reshape(full_in, -1)
    visual = jnp.dot(lifted, weights, preferred_element_type=jnp.float32).astype(jnp.bfloat16)
    sendable = jnp.dot(pack, visual, preferred_element_type=jnp.float32).astype(jnp.bfloat16)
    arrived = lax.all_to_all(
        sendable.reshape(owners, capacity, width_tp),
        ("img", "ctx"),
        split_axis=0,
        concat_axis=0,
        tiled=True,
    )
    arrived_pos = lax.all_to_all(
        packed_pos.reshape(owners, capacity),
        ("img", "ctx"),
        split_axis=0,
        concat_axis=0,
        tiled=True,
    )
    placing = one_hot_rows(tok_rows, arrived_pos.reshape(slot_count) - owner_index * tok_rows)
    current = current + jnp.dot(
        placing, arrived.reshape(slot_count, width_tp), preferred_element_type=jnp.float32
    )
    streams = [current]
    saved = [(normed, inv_std, placing)]
    new_stream = current.astype(jnp.bfloat16)
    stream_grad = jnp.zeros((tok_rows, width_tp), jnp.float32)
    feature_grads = [None] * depth_count
    for depth_index in reversed(range(depth_count)):
        state = streams[depth_index]
        normed, inv_std, placing = saved[depth_index]
        upstream = norm_gain[depth_index].astype(jnp.float32)[None, :] * cotangent[
            depth_index
        ].astype(jnp.float32)
        square_sum, inner_sum = lax.psum(
            (jnp.sum(state * state, axis=1), jnp.sum(upstream * state, axis=1)), "tp"
        )
        inv_rms = lax.rsqrt(square_sum / full_width + 1e-06)
        inner_mean = inner_sum / full_width
        stream_grad = (
            inv_rms[:, None] * upstream
            - state * (inv_rms * inv_rms * inv_rms * inner_mean)[:, None]
        )
        picked = jnp.einsum(
            "tr,tc->rc", placing.astype(jnp.float32), stream_grad, precision=lax.Precision.HIGHEST
        ).astype(jnp.bfloat16)
        returned = lax.all_to_all(
            picked.reshape(owners, capacity, width_tp),
            ("img", "ctx"),
            split_axis=0,
            concat_axis=0,
            tiled=True,
        )
        grad_tokens = jnp.einsum(
            "sm,sc->mc",
            pack,
            returned.reshape(slot_count, width_tp),
            preferred_element_type=jnp.float32,
        ).astype(jnp.bfloat16)
        weights = weight_held[depth_index].reshape(full_in, -1)
        partial_in = lax.dot_general(
            grad_tokens, weights, (((1,), (1,)), ((), ())), preferred_element_type=jnp.float32
        )
        lifted_grad = lax.psum(partial_in, "tp")
        gain_row = ln_gain[depth_index].reshape(1, full_in).astype(jnp.float32)
        scaled = lifted_grad * gain_row
        centered = (
            scaled
            - jnp.mean(scaled, axis=1, keepdims=True)
            - normed * jnp.mean(scaled * normed, axis=1, keepdims=True)
        )
        feature_grads[depth_index] = (
            (inv_std * centered).reshape(merged * window, vision_width).astype(jnp.bfloat16)
        )
    return (new_stream, jnp.stack(feature_grads))


def solution(mesh):
    placed = (
        P(None, ("img", "ctx"), None),
        P(),
        P(),
        P(None, None, "ctx", "tp"),
        P(("img", "ctx"), "tp"),
        P(None, "tp"),
        P(None, ("img", "ctx"), "tp"),
        P(("img", "ctx")),
    )
    return jax.shard_map(
        shards,
        mesh=mesh,
        in_specs=placed,
        out_specs=(P(("img", "ctx"), "tp"), P(None, ("img", "ctx"), None)),
        check_vma=False,
    )
```

profile of v0, /device:TPU:1, one launch (start us, length us, event | category | flops | bytes accessed | tf_op | source)
XLA Modules:
  0.0 284.4 jit_solution(9043801947587600273)
XLA Ops:
  7.2 0.0 all-gather.2.cloned.1.call-start
  7.2 0.7 all-gather.2.cloned.1.call-update
  7.9 0.7 and_select_fusion
  8.6 0.2 convert_reduce_fusion.1
  8.8 0.7 multiply_add_fusion
  9.5 0.9 select_reduce_fusion
  10.3 0.7 all_to_all.12
  11.0 9.8 %all-to-all-start = ((s32[32,1,16]{2,1,0:T(1,128)}), s32[32,1,16]{2,1,0:T(1,128)S(1)}, u32[]{:S(2)}, u32[]{:S(2)}) async-start(s32[32,1,16]{2,1,0:T(1,128)} %bitcast), calls=%async_computation | async-start | bytes 32768 | tf_op jit(solution)/shard_map/all_to_all | solution.py:54
  20.8 2.4 convert_reduce_fusion
  23.3 0.1 reduce_sum.79
  23.4 0.1 reduce_sum.82
  23.5 0.1 reduce_sum.80
  23.7 0.1 reduce_sum.83
  23.8 0.1 mul.127
  23.9 0.1 mul.128
  24.0 0.1 sub.62
  24.1 0.1 sub.63
  24.2 0.7 bitcast_convert_fusion
  24.9 2.7 add.48
  27.7 0.0 copy-start.3
  27.7 6.3 %add.49 = f32[1,1024,1152]{2,1,0:T(8,128)} reshape(f32[256,4,1152]{2,1,0:T(4,128)} %add.48) | data formatting | bytes 9437184 | tf_op jit(solution)/shard_map/add | solution.py:43
  34.0 0.0 copy-done.3
  34.0 2.8 mul.131
  36.8 6.4 %mul.132 = f32[1,1024,1152]{2,1,0:T(8,128)} reshape(f32[256,4,1152]{2,1,0:T(4,128)} %mul.131) | data formatting | bytes 9437184 | tf_op jit(solution)/shard_map/mul | solution.py:43
  43.2 0.0 copy-done.1
  43.2 5.4 %add_convert_fusion = bf16[1,1024,1152]{2,1,0:T(8,128)(2,1)} fusion(f32[1,1024,1152]{2,1,0:T(8,128)} %add.49, f32[1,1024,1152]{2,1,0:T(8,128)} %mul.132, bf16[1,1024,1152]{2,1,0:T(8,128)(2,1)S(1)} %copy-done.1, f32[1024]{0:T(1024)S(1)} %mul.128, f32[1024]{0:T(1024)S(1)} %sub.63), kind=kLoop, calls=%fused_computation.3 | loop fusion | flops 7077888 | bytes 14163968 | tf_op jit(solution)/shard_map/convert_element_type | solution.py:43
  48.6 4.5 %convert_element_type.102 = bf16[256,4608]{1,0:T(8,128)(2,1)} reshape(bf16[1,1024,1152]{2,1,0:T(8,128)(2,1)} %add_convert_fusion) | data formatting | bytes 4718592 | tf_op jit(solution)/shard_map/convert_element_type | solution.py:43
  53.1 36.0 %all-gather.2.cloned.1.call-done = bf16[1,4,1152,1024]{3,2,1,0:T(8,128)(2,1)} async-done(((bf16[1,4,72,1024]{3,2,1,0:T(8,128)(2,1)}), bf16[1,4,1152,1024]{3,2,1,0:T(8,128)(2,1)}) %all-gather.2.cloned.1.call-update) | async-done | bytes 9437200 | tf_op jit(solution)/shard_map/all_gather | solution.py:33
  89.1 8.2 %convolution_convert_fusion = bf16[512,1024]{1,0:T(8,128)(2,1)} fusion(bf16[256,4608]{1,0:T(8,128)(2,1)} %convert_element_type.102, bf16[4608,1024]{1,0:T(8,128)(2,1)} %bitcast.30, s32[256]{0:T(256)S(1)} %multiply_add_fusion), kind=kOutput, calls=%fused_computation.17 | convolution fusion | flops 2685272064 | bytes 12846080 | tf_op jit(solution)/shard_map/dot_general | solution.py:46
  97.3 0.0 all-to-all-done
  97.3 6.2 %all-to-all-start.1 = ((bf16[32,16,1024]{2,1,0:T(8,128)(2,1)}), bf16[32,16,1024]{2,1,0:T(8,128)(2,1)S(1)}, u32[]{:S(2)}, u32[]{:S(2)}) async-start(bf16[32,16,1024]{2,1,0:T(8,128)(2,1)} %bitcast.25), calls=%async_computation.1 | async-start | bytes 2097152 | tf_op jit(solution)/shard_map/all_to_all | solution.py:47
  103.5 0.0 all-reduce.3.cloned.1.call-start
  103.6 0.0 copy-done.4
  103.7 0.1 sub.61
  103.8 14.6 %all-to-all-done.1 = bf16[32,16,1024]{2,1,0:T(8,128)(2,1)S(1)} async-done(((bf16[32,16,1024]{2,1,0:T(8,128)(2,1)}), bf16[32,16,1024]{2,1,0:T(8,128)(2,1)S(1)}, u32[]{:S(2)}, u32[]{:S(2)}) %all-to-all-start.1) | async-done | bytes 1048608 | tf_op jit(solution)/shard_map/all_to_all | solution.py:47
  118.4 4.2 %multiply_reduce_fusion.3 = (f32[512]{0:T(512)S(1)}, f32[512]{0:T(512)S(1)}, bf16[512,1024]{1,0:T(8,128)(2,1)}, f32[512,1024]{1,0:T(8,128)}) fusion(bf16[1,512,1024]{2,1,0:T(8,128)(2,1)} %param.14, f32[1024]{0:T(1024)S(1)} %bitcast.28, bf16[512,1024]{1,0:T(8,128)(2,1)S(1)} %bitcast.24, s32[512]{0:T(512)S(1)} %sub.61, bf16[512,1024]{1,0:T(8,128)(2,1)} %param.12), kind=kOutput, calls=%fused_computation.14 | convolution fusion | flops 541850624 | bytes 6301696 | tf_op jit(solution)/shard_map/dot_general | solution.py:62
  122.6 9.3 %all-reduce = (f32[512]{0:T(512)S(1)}, f32[512]{0:T(512)S(1)}) all-reduce(f32[512]{0:T(512)S(1)} %get-tuple-element.7, f32[512]{0:T(512)S(1)} %get-tuple-element.6), channel_id=1, replica_groups=mesh['img'=2,'ctx'=16,'tp'=4] {'tp'}, use_global_device_ids=true, to_apply=%region_9.10 | all-reduce | flops 1024 | bytes 8192 | tf_op jit(solution)/shard_map/psum | solution.py:76
  131.9 4.3 %fusion.7 = bf16[512,1024]{1,0:T(8,128)(2,1)S(1)} fusion(f32[512,1024]{1,0:T(8,128)} %get-tuple-element.15, bf16[1,512,1024]{2,1,0:T(8,128)(2,1)} %param.14, f32[512]{0:T(512)S(1)} %get-tuple-element.12, f32[1024]{0:T(1024)S(1)} %bitcast.29, f32[512]{0:T(512)S(1)} %get-tuple-element.11, s32[512]{0:T(512)S(1)} %sub.61), kind=kOutput, calls=%fused_computation.16 | convolution fusion | flops 3224633344 | bytes 4204544 | tf_op jit(solution)/shard_map/tr,tc->rc/dot_general | solution.py:85
  136.2 18.1 %all_to_all.19 = bf16[32,16,1024]{2,1,0:T(8,128)(2,1)S(1)} all-to-all(bf16[32,16,1024]{2,1,0:T(8,128)(2,1)S(1)} %bitcast.26), channel_id=1, replica_groups=mesh['img'=2,'ctx'=16,'tp'=4] {'img','ctx'}, dimensions={0} | all-to-all | bytes 2097152 | tf_op jit(solution)/shard_map/all_to_all | solution.py:88
  154.3 8.8 %fusion.10 = f32[256,4608]{1,0:T(8,128)} fusion(bf16[4608,1024]{1,0:T(8,128)(2,1)} %bitcast.31, bf16[512,1024]{1,0:T(8,128)(2,1)S(1)} %bitcast.27, s32[256]{0:T(256)S(1)} %multiply_add_fusion), kind=kOutput, calls=%fused_computation.20 | convolution fusion | flops 2684747776 | bytes 15205376 | tf_op jit(solution)/shard_map/dot_general | solution.py:102
  163.2 0.0 all-reduce.3.cloned.1.call-update
  163.2 3.2 %reshape.136 = f32[256,4608]{1,0:T(8,128)} reshape(bf16[1,1024,1152]{2,1,0:T(8,128)(2,1)S(1)} %copy-done.1) | data formatting | bytes 7077888 | tf_op jit(solution)/shard_map/convert_element_type | solution.py:36
  166.4 100.1 %all-reduce.3.cloned.1.call-done = f32[256,4608]{1,0:T(8,128)} async-done(((f32[256,4608]{1,0:T(8,128)}), f32[256,4608]{1,0:T(8,128)}) %all-reduce.3.cloned.1.call-update) | async-done | bytes 4718608 | tf_op jit(solution)/shard_map/psum | solution.py:105
  266.5 5.1 %multiply_reduce_fusion.2 = (f32[256]{0:T(256)S(1)}, f32[256]{0:T(256)S(1)}) fusion(f32[256,4608]{1,0:T(8,128)} %all-reduce.3.cloned.1.call-done, f32[4608]{0:T(1024)S(1)} %reshape.135, f32[256]{0:T(256)S(1)} %get-tuple-element.14, f32[256,4608]{1,0:T(8,128)} %reshape.136, f32[256]{0:T(256)S(1)} %get-tuple-element.13), kind=kLoop, calls=%fused_computation.5 | loop fusion | flops 7077376 | bytes 9459712 | tf_op jit(solution)/shard_map/reduce_sum | solution.py:110
  271.7 0.0 copy-done
  271.7 1.4 copy-done.2
  273.1 1.8 multiply_convert_fusion
  274.8 2.7 convert_element_type.115
  (11 shorter events, 0.1 us)
Async XLA Ops:
  7.2 81.9 %all-gather.2.cloned.1.call-start = ((), (), s32[]{:S(2)}) async-start(), calls=%async_computation.3 | async-start | bytes 10027008 | tf_op jit(solution)/shard_map/all_gather | solution.py:33
  11.0 86.3 %all-to-all-start = ((s32[32,1,16]{2,1,0:T(1,128)}), s32[32,1,16]{2,1,0:T(1,128)S(1)}, u32[]{:S(2)}, u32[]{:S(2)}) async-start(s32[32,1,16]{2,1,0:T(1,128)} %bitcast), calls=%async_computation | async-start | bytes 32768 | tf_op jit(solution)/shard_map/all_to_all | solution.py:54
  27.7 6.3 %copy-start.3 = (bf16[1,4,1152]{2,1,0:T(4,128)(2,1)S(1)}, bf16[1,4,1152]{2,1,0:T(4,128)(2,1)}, u32[]{:S(2)}) copy-start(bf16[1,4,1152]{2,1,0:T(4,128)(2,1)} %param.9) | copy-start | bytes 27652
  36.8 6.4 %copy-start.1 = (bf16[1,1024,1152]{2,1,0:T(8,128)(2,1)S(1)}, bf16[1,1024,1152]{2,1,0:T(8,128)(2,1)}, u32[]{:S(2)}) copy-start(bf16[1,1024,1152]{2,1,0:T(8,128)(2,1)} %param.8) | copy-start | bytes 7077892
  89.1 14.5 %copy-start.4 = (bf16[1,1024]{1,0:T(2,128)(2,1)S(1)}, bf16[1,1024]{1,0:T(2,128)(2,1)}, u32[]{:S(2)}) copy-start(bf16[1,1024]{1,0:T(2,128)(2,1)} %param.13) | copy-start | bytes 6148
  97.3 21.1 %all-to-all-start.1 = ((bf16[32,16,1024]{2,1,0:T(8,128)(2,1)}), bf16[32,16,1024]{2,1,0:T(8,128)(2,1)S(1)}, u32[]{:S(2)}, u32[]{:S(2)}) async-start(bf16[32,16,1024]{2,1,0:T(8,128)(2,1)} %bitcast.25), calls=%async_computation.1 | async-start | bytes 2097152 | tf_op jit(solution)/shard_map/all_to_all | solution.py:47
  103.5 163.0 %all-reduce.3.cloned.1.call-start = ((), (), s32[]{:S(2)}) async-start(), calls=%async_computation.4 | async-start | bytes 9437184 | tf_op jit(solution)/shard_map/psum | solution.py:105
  266.5 5.1 %copy-start = (f32[256,4608]{1,0:T(8,128)S(1)}, f32[256,4608]{1,0:T(8,128)}, u32[]{:S(2)}) copy-start(f32[256,4608]{1,0:T(8,128)} %reshape.136) | copy-start | bytes 14155780
  266.5 6.5 %copy-start.2 = (f32[256,4608]{1,0:T(8,128)S(1)}, f32[256,4608]{1,0:T(8,128)}, u32[]{:S(2)}) copy-start(f32[256,4608]{1,0:T(8,128)} %all-reduce.3.cloned.1.call-done) | copy-start | bytes 14155780
Sparse Core Ops, SparseCore 0:
  10.1 78.8 all-gather.1
  163.3 103.1 all-reduce.2
where the time goes:
time: 285 us; the launch traced here: 284 us
  waiting for transfers between devices  151 us (53%)
  local copies, waits for them, and re-layouts  31.5 us (11%)
  blocking collectives  27.4 us (10%)
  matrix products  25.6 us (9%)
  other arithmetic  18.1 us (6%)
  starting transfers between devices  16.1 us (6%)
  between operations  14.2 us (5%)
    psum x1, waiting for transfers between devices, shards(): lifted_grad = lax.psum(partial_in, 'tp')  100 us
    all_gather x1, waiting for transfers between devices, shards(): weight_held = lax.all_gather(projection, 'ctx', axis=2, tiled=True)  36 us
    all_to_all x1, blocking collectives, shards(): lax.all_to_all(picked.reshape(owners, capacity, width_tp), ('img', 'ctx')...  18.1 us
    all_to_all x1, waiting for transfers between devices, shards(): lax.all_to_all(sendable.reshape(owners, capacity, width_tp), ('img', 'ctx...  14.6 us
    all_to_all x1, starting transfers between devices, shards(): lax.all_to_all(packed_pos.reshape(owners, capacity), ('img', 'ctx'), spli...  9.81 us
    psum x1, blocking collectives, shards(): lax.psum((jnp.sum(state * state, axis=1), jnp.sum(upstream * state, axis=...  9.29 us
    mul x2, local copies, waits for them, and re-layouts, shards(): lifted = (normed * gain_row + bias_row).astype(jnp.bfloat16)  9.21 us
    add x2, local copies, waits for them, and re-layouts, shards(): lifted = (normed * gain_row + bias_row).astype(jnp.bfloat16)  9.04 us
  transfers between devices with their start and end apart: 4, of which 3 were waited for; matrix products, arithmetic and copies ran while one was open for 16% of the time, Pallas kernels for 0%

commit v1 on v0

v1 whole, which is shorter than its diff:
```python
import jax
import jax.numpy as jnp
from jax import lax
from jax.experimental import pallas as pl
from jax.experimental.pallas import tpu as pltpu
from jax.sharding import PartitionSpec as P

BF = jnp.bfloat16
F32 = jnp.float32
VMEM_LIMIT = 48 * 1024 * 1024
VMEM = pltpu.VMEM
SMEM = pltpu.SMEM


def params():
    return pltpu.CompilerParams(vmem_limit_bytes=VMEM_LIMIT)


def whole():
    return pl.BlockSpec(memory_space=VMEM)


def cost(flops, moved):
    return pl.CostEstimate(flops=flops, bytes_accessed=moved, transcendentals=0)


def eq_hot(shape, dim, index):
    return (lax.broadcasted_iota(jnp.int32, shape, dim) == index).astype(BF)


def window_major(tokens, window):
    n = tokens * window
    row = lax.broadcasted_iota(jnp.int32, (n, n), 0)
    col = lax.broadcasted_iota(jnp.int32, (n, n), 1)
    return (col == (row % tokens) * window + row // tokens).astype(BF)


def patch_major(tokens, window):
    n = tokens * window
    row = lax.broadcasted_iota(jnp.int32, (n, n), 0)
    col = lax.broadcasted_iota(jnp.int32, (n, n), 1)
    return (col == (row % window) * tokens + row // window).astype(BF)


def norm_kernel(x_ref, gain_ref, bias_ref, lifted_ref, xw_ref, stat_ref):
    window = gain_ref.shape[0]
    tokens = x_ref.shape[0] // window
    full = window * x_ref.shape[1]
    x = jnp.dot(
        window_major(tokens, window), x_ref[...], preferred_element_type=F32
    )
    parts = [x[w * tokens : (w + 1) * tokens] for w in range(window)]
    total = sum(jnp.sum(p, axis=1, keepdims=True) for p in parts)
    squares = sum(jnp.sum(p * p, axis=1, keepdims=True) for p in parts)
    mean = total / full
    inv = lax.rsqrt(squares / full - mean * mean + 1e-05)
    for w, p in enumerate(parts):
        normed = (p - mean) * inv
        lifted_ref[w] = (
            normed * gain_ref[w : w + 1].astype(F32) + bias_ref[w : w + 1].astype(F32)
        ).astype(BF)
        xw_ref[w] = p.astype(BF)
    lane = lax.broadcasted_iota(jnp.int32, stat_ref.shape, 1)
    stat_ref[...] = jnp.where(lane == 0, mean, inv)


def layer_norm(features, gain, bias):
    rows, width = features.shape
    window = gain.shape[0]
    merged = rows // window
    block = 64
    return pl.pallas_call(
        norm_kernel,
        grid=(merged // block,),
        in_specs=[
            pl.BlockSpec((block * window, width), lambda i: (i, 0)),
            pl.BlockSpec((window, width), lambda i: (0, 0)),
            pl.BlockSpec((window, width), lambda i: (0, 0)),
        ],
        out_specs=[
            pl.BlockSpec((window, block, width), lambda i: (0, i, 0)),
            pl.BlockSpec((window, block, width), lambda i: (0, i, 0)),
            pl.BlockSpec((block, 128), lambda i: (i, 0)),
        ],
        out_shape=[
            jax.ShapeDtypeStruct((window, merged, width), BF),
            jax.ShapeDtypeStruct((window, merged, width), BF),
            jax.ShapeDtypeStruct((merged, 128), F32),
        ],
        compiler_params=params(),
        cost_estimate=cost(2 * rows * block * window * width, 6 * rows * width),
        name="layer_norm",
    )(features, gain, bias)


def collect_kernel(pos_ref, stream_ref, cot_ref, out_ref):
    slots = pos_ref.shape[0]
    rows, width = stream_ref.shape
    pick = eq_hot((slots, rows), 1, pos_ref[...])
    out_ref[:, :width] = jnp.dot(pick, stream_ref[...], preferred_element_type=F32).astype(BF)
    out_ref[:, width:] = jnp.dot(pick, cot_ref[...], preferred_element_type=F32).astype(BF)


def collect(pos, stream, cot):
    slots = pos.shape[0]
    rows, width = stream.shape
    return pl.pallas_call(
        collect_kernel,
        in_specs=[whole()] * 3,
        out_specs=whole(),
        out_shape=jax.ShapeDtypeStruct((slots, 2 * width), BF),
        compiler_params=params(),
        cost_estimate=cost(4 * slots * rows * width, 8 * rows * width),
        name="collect",
    )(pos, stream, cot)


def forward_kernel(lifted_ref, w_ref, row_ref, came_ref, ngain_ref,
                   state_ref, up_ref, send_ref, stat_ref, acc_ref):
    step = pl.program_id(0) * pl.num_programs(1) + pl.program_id(1)
    last = pl.num_programs(0) * pl.num_programs(1) - 1
    part = jnp.dot(lifted_ref[0], w_ref[0], preferred_element_type=F32)

    @pl.when(step == 0)
    def _():
        acc_ref[...] = part

    @pl.when(step > 0)
    def _():
        acc_ref[...] += part

    @pl.when(step == last)
    def _():
        slots = came_ref.shape[0]
        tokens, width = acc_ref.shape
        pack = eq_hot((slots, tokens), 0, row_ref[...])
        visual = acc_ref[...].astype(BF)
        send_ref[...] = jnp.dot(pack, visual, preferred_element_type=F32).astype(BF)
        held = lax.dot_general(
            pack, came_ref[...], (((0,), (0,)), ((), ())), preferred_element_type=F32
        )
        state = held[:, :width] + visual.astype(F32)
        up = held[:, width:] * ngain_ref[...].astype(F32)
        state_ref[...] = state
        up_ref[...] = up
        lane = lax.broadcasted_iota(jnp.int32, stat_ref.shape, 1)
        stat_ref[...] = jnp.where(
            lane == 0,
            jnp.sum(state * state, axis=1, keepdims=True),
            jnp.sum(up * state, axis=1, keepdims=True),
        )


def forward(lifted, weight, slot_row, came, ngain):
    window, tokens, depth = lifted.shape
    width = weight.shape[2]
    slots = came.shape[0]
    block = 384
    return pl.pallas_call(
        forward_kernel,
        grid=(window, depth // block),
        in_specs=[
            pl.BlockSpec((1, tokens, block), lambda w, k: (w, 0, k)),
            pl.BlockSpec((1, block, width), lambda w, k: (w, k, 0)),
            pl.BlockSpec((1, tokens), lambda w, k: (0, 0)),
            pl.BlockSpec((slots, 2 * width), lambda w, k: (0, 0)),
            pl.BlockSpec((1, width), lambda w, k: (0, 0)),
        ],
        out_specs=[
            pl.BlockSpec((tokens, width), lambda w, k: (0, 0)),
            pl.BlockSpec((tokens, width), lambda w, k: (0, 0)),
            pl.BlockSpec((slots, width), lambda w, k: (0, 0)),
            pl.BlockSpec((tokens, 128), lambda w, k: (0, 0)),
        ],
        out_shape=[
            jax.ShapeDtypeStruct((tokens, width), F32),
            jax.ShapeDtypeStruct((tokens, width), F32),
            jax.ShapeDtypeStruct((slots, width), BF),
            jax.ShapeDtypeStruct((tokens, 128), F32),
        ],
        scratch_shapes=[pltpu.VMEM((tokens, width), F32)],
        compiler_params=params(),
        cost_estimate=cost(2 * window * depth * tokens * width, 2 * window * depth * width),
        name="forward",
    )(lifted, weight, slot_row, came, ngain)


def backward_kernel(full_width, chunk, rows, core_ref, state_ref, up_ref, stat_a_ref, stat_b_ref, w_ref,
                    mine_ref, other_ref, picked_ref):
    step = pl.program_id(0) * pl.num_programs(1) + pl.program_id(1)
    tokens = state_ref.shape[0]
    half = tokens // 2

    @pl.when(step == 0)
    def _():
        core = core_ref[0]
        for place, owner in enumerate((core, 1 - core)):
            start = pl.multiple_of(owner * half + chunk * rows, rows)
            at = pl.ds(start, rows)
            sums = stat_a_ref[at, :] + stat_b_ref[at, :]
            inv = lax.rsqrt(sums[:, 0:1] / full_width + 1e-06)
            inner = sums[:, 1:2] / full_width
            grad = inv * up_ref[at, :] - state_ref[at, :] * (inv * inv * inv * inner)
            picked_ref[place * rows : (place + 1) * rows, :] = grad.astype(BF)

    both = lax.dot_general(
        picked_ref[...], w_ref[0], (((1,), (1,)), ((), ())), preferred_element_type=F32
    )
    mine_ref[0] = both[:rows]
    other_ref[0] = both[rows:].astype(BF)


def backward(core, state, up, stat_a, stat_b, weight, chunk, rows, full_width):
    window, depth, width = weight.shape
    tokens = state.shape[0]
    block = 384
    fixed = lambda w, k: (0, 0)
    return pl.pallas_call(
        lambda *refs: backward_kernel(full_width, chunk, rows, *refs),
        grid=(window, depth // block),
        in_specs=[
            pl.BlockSpec(memory_space=SMEM),
            pl.BlockSpec((tokens, width), fixed),
            pl.BlockSpec((tokens, width), fixed),
            pl.BlockSpec((tokens, 128), fixed),
            pl.BlockSpec((tokens, 128), fixed),
            pl.BlockSpec((1, block, width), lambda w, k: (w, k, 0)),
        ],
        out_specs=[
            pl.BlockSpec((1, rows, block), lambda w, k: (w, 0, k)),
            pl.BlockSpec((1, rows, block), lambda w, k: (w, 0, k)),
        ],
        out_shape=[
            jax.ShapeDtypeStruct((window, rows, depth), F32),
            jax.ShapeDtypeStruct((window, rows, depth), BF),
        ],
        scratch_shapes=[pltpu.VMEM((2 * rows, width), BF)],
        compiler_params=params(),
        cost_estimate=cost(4 * window * depth * rows * width, 2 * window * depth * width),
        name="backward",
    )(core, state, up, stat_a, stat_b, weight)


def finish_kernel(block_ref, own_ref, far_ref, xw_ref, stat_ref, gain_ref, out_ref):
    window, tokens, width = own_ref.shape
    full = window * width
    mean = stat_ref[:, 0:1]
    inv = stat_ref[:, 1:2]
    scaled = []
    total = 0.0
    inner = 0.0
    for w in range(window):
        g = (own_ref[w].astype(F32) + far_ref[w].astype(F32)) * gain_ref[w : w + 1].astype(F32)
        normed = (xw_ref[w].astype(F32) - mean) * inv
        total = total + jnp.sum(g, axis=1, keepdims=True)
        inner = inner + jnp.sum(g * normed, axis=1, keepdims=True)
        scaled.append((g, normed))
    total = total / full
    inner = inner / full
    rows = jnp.concatenate(
        [(inv * (g - total - normed * inner)).astype(BF) for g, normed in scaled], axis=0
    )
    out_ref[...] = jnp.dot(
        patch_major(tokens, window), rows, preferred_element_type=F32
    ).astype(BF)


def finish(block, own, far, xw, stat, gain):
    window, tokens, width = own.shape
    return pl.pallas_call(
        finish_kernel,
        grid_spec=pltpu.PrefetchScalarGridSpec(
            num_scalar_prefetch=1,
            grid=(1,),
            in_specs=[
                pl.BlockSpec((window, tokens, width), lambda i, b: (0, 0, 0)),
                pl.BlockSpec((window, tokens, width), lambda i, b: (0, 0, 0)),
                pl.BlockSpec((window, tokens, width), lambda i, b: (0, b[0], 0)),
                pl.BlockSpec((tokens, 128), lambda i, b: (b[0], 0)),
                pl.BlockSpec((window, width), lambda i, b: (0, 0)),
            ],
            out_specs=pl.BlockSpec((tokens * window, width), lambda i, b: (0, 0)),
        ),
        out_shape=jax.ShapeDtypeStruct((tokens * window, width), BF),
        compiler_params=params(),
        cost_estimate=cost(2 * (tokens * window) ** 2 * width, 8 * window * tokens * width),
        name="finish",
    )(block, own, far, xw, stat, gain)


def place_kernel(pos_ref, came_ref, stream_ref, out_ref):
    slots = came_ref.shape[0]
    rows, width = stream_ref.shape
    put = eq_hot((rows, slots), 0, pos_ref[...])
    out_ref[...] = (
        stream_ref[...].astype(F32) + jnp.dot(put, came_ref[...], preferred_element_type=F32)
    ).astype(BF)


def place(pos, came, stream):
    rows, width = stream.shape
    return pl.pallas_call(
        place_kernel,
        in_specs=[whole()] * 3,
        out_specs=whole(),
        out_shape=jax.ShapeDtypeStruct((rows, width), BF),
        compiler_params=params(),
        cost_estimate=cost(2 * came.shape[0] * rows * width, 6 * rows * width),
        name="place",
    )(pos, came, stream)


def shards(features, ln_gain, ln_bias, projection, stream, norm_gain, cotangent, slots):
    n_img = lax.axis_size("img")
    n_ctx = lax.axis_size("ctx")
    n_tp = lax.axis_size("tp")
    merged = slots.shape[0]
    window = ln_gain.shape[1]
    tok_rows, width = stream.shape
    owners = n_img * n_ctx
    capacity = 2 * merged // owners
    slot_count = owners * capacity
    full_width = width * n_tp

    core_pairs = [(t, t ^ 1) for t in range(n_tp)]
    far_pairs = [(t, t ^ 2) for t in range(n_tp)]
    core = lax.axis_index("tp") % 2

    weight = lax.all_gather(projection, "ctx", axis=2, tiled=True)[0]

    target = slots // tok_rows
    ids = jnp.arange(merged)
    earlier = (target[:, None] == target[None, :]) & (ids[:, None] < ids[None, :])
    rank = jnp.sum(earlier.astype(jnp.int32), axis=0)
    slot = target * capacity + rank
    local = slots - target * tok_rows
    packed = jnp.max(
        jnp.where(jnp.arange(slot_count)[:, None] == slot[None, :], local[None, :], -1), axis=1
    )
    asked = lax.all_to_all(
        packed.reshape(owners, capacity), ("img", "ctx"), split_axis=0, concat_axis=0, tiled=True
    )

    held = collect(asked.reshape(slot_count, 1), stream, cotangent[0])
    came = lax.all_to_all(
        held.reshape(owners, capacity, 2 * width),
        ("img", "ctx"), split_axis=0, concat_axis=0, tiled=True,
    ).reshape(slot_count, 2 * width)

    gain = ln_gain[0]
    lifted, xw, stat = layer_norm(features[0], gain, ln_bias[0])

    state, up, send, sums = forward(lifted, weight, slot.reshape(1, merged), came, norm_gain)

    near = sums + lax.ppermute(sums, "tp", core_pairs)
    far = lax.ppermute(near, "tp", far_pairs)

    arrived = lax.all_to_all(
        send.reshape(owners, capacity, width),
        ("img", "ctx"), split_axis=0, concat_axis=0, tiled=True,
    ).reshape(slot_count, width)
    new_stream = place(asked.reshape(1, slot_count), arrived, stream)

    chunks = 2
    rows = merged // 2 // chunks
    core_in = core.reshape(1).astype(jnp.int32)
    own_out, got_out = [], []
    for chunk in range(chunks):
        mine, other = backward(core_in, state, up, near, far, weight, chunk, rows, full_width)
        got = lax.ppermute(other, "tp", core_pairs)
        pair = (mine + got.astype(F32)).astype(BF)
        beyond = lax.ppermute(pair, "tp", far_pairs)
        out = finish((core_in * chunks + chunk), pair, beyond, xw, stat, gain)
        own_out.append(out)
        got_out.append(lax.ppermute(out, "tp", core_pairs))
    first = core == 0
    own = jnp.concatenate(own_out, axis=0)
    got = jnp.concatenate(got_out, axis=0)
    grad = jnp.concatenate([jnp.where(first, own, got), jnp.where(first, got, own)], axis=0)
    return (new_stream, grad[None])


def solution(mesh):
    placed = (
        P(None, ("img", "ctx"), None),
        P(),
        P(),
        P(None, None, "ctx", "tp"),
        P(("img", "ctx"), "tp"),
        P(None, "tp"),
        P(None, ("img", "ctx"), "tp"),
        P(("img", "ctx")),
    )
    return jax.shard_map(
        shards,
        mesh=mesh,
        in_specs=placed,
        out_specs=(P(("img", "ctx"), "tp"), P(None, ("img", "ctx"), None)),
        check_vma=False,
    )
```

time: 285 us -> 218 us (0.76)
  waiting for transfers between devices: 151 us -> 95.6 us
  Pallas kernels: 0 us -> 48.6 us
  matrix products: 25.6 us -> 0 us
  local copies, waits for them, and re-layouts: 31.5 us -> 11.8 us
  blocking collectives: 27.4 us -> 16.7 us
  other arithmetic: 18.1 us -> 7.46 us
  starting transfers between devices: 16.1 us -> 22.3 us
    psum x1 -> x0, waiting for transfers between devices: 100 us -> none  [shards(): lifted_grad = lax.psum(partial_in, 'tp')]
    pallas_call x0 -> x8, Pallas kernels: none -> 48.6 us  [the longest x2 21.8 us: backward(): pl.pallas_call(lambda *refs: backward_kernel(full_width, chunk, rows, *re...]
    ppermute x0 -> x8, waiting for transfers between devices: none -> 34.5 us  [the longest x2 29.9 us: shards(): beyond = lax.ppermute(pair, 'tp', far_pairs)]
    dot_general x4 -> x0, matrix products: 25.6 us -> none  [the longest x1 8.84 us: shards(): lax.dot_general(grad_tokens, weights, (((1,), (1,)), ((), ())), preferred...]
    ppermute x0 -> x8, starting transfers between devices: none -> 10.9 us  [the longest x2 3.17 us: shards(): got_out.append(lax.ppermute(out, 'tp', core_pairs))]
    convert_element_type x4 -> x0, local copies, waits for them, and re-layouts: 10.4 us -> none  [the longest x1 4.5 us: shards(): lifted = (normed * gain_row + bias_row).astype(jnp.bfloat16)]
    unnamed x10 -> x37, local copies, waits for them, and re-layouts: 1.4 us -> 10.8 us
    mul x4 -> x0, local copies, waits for them, and re-layouts: 9.43 us -> none  [the longest x2 9.21 us: shards(): lifted = (normed * gain_row + bias_row).astype(jnp.bfloat16)]
  transfers between devices with their start and end apart: 4 -> 11, of which waited for: 3 -> 6; matrix products, arithmetic and copies ran while one was open for 16% -> 3% of each run, Pallas kernels for 0% -> 11%
where the time goes in v1:
time: 218 us; the launch traced here: 217 us
  waiting for transfers between devices  95.6 us (44%)
  Pallas kernels  48.6 us (22%)
  starting transfers between devices  22.3 us (10%)
  blocking collectives  16.7 us (8%)
  between operations  14.2 us (7%)
  local copies, waits for them, and re-layouts  11.8 us (5%)
  other arithmetic  7.46 us (3%)
    all_gather x1, waiting for transfers between devices, shards(): weight = lax.all_gather(projection, 'ctx', axis=2, tiled=True)[0]  42.3 us
    ppermute x2, waiting for transfers between devices, shards(): beyond = lax.ppermute(pair, 'tp', far_pairs)  29.9 us
    pallas_call x2, Pallas kernels, backward(): pl.pallas_call(lambda *refs: backward_kernel(full_width, chunk, rows, *re...  21.8 us
    all_to_all x1, waiting for transfers between devices, shards(): lax.all_to_all(held.reshape(owners, capacity, 2 * width), ('img', 'ctx'),...  18.1 us
    all_to_all x1, blocking collectives, shards(): lax.all_to_all(packed.reshape(owners, capacity), ('img', 'ctx'), split_ax...  16.7 us
    pallas_call x1, Pallas kernels, forward(): pl.pallas_call(forward_kernel, grid=(window, depth // block), in_specs=[p...  13.2 us
    unnamed x37, local copies, waits for them, and re-layouts  10.8 us
    all_to_all x1, starting transfers between devices, shards(): lax.all_to_all(send.reshape(owners, capacity, width), ('img', 'ctx'), spl...  6.48 us
  transfers between devices with their start and end apart: 11, of which 6 were waited for; matrix products, arithmetic and copies ran while one was open for 3% of the time, Pallas kernels for 11%

profile of v1, /device:TPU:1, one launch (start us, length us, event | category | flops | bytes accessed | tf_op | source)
XLA Modules:
  0.0 216.7 jit_solution(5116928573045077461)
XLA Ops:
  7.2 0.7 all-gather.2.cloned.1.call-update
  7.9 0.7 multiply_subtract_fusion
  8.6 0.1 convert_reduce_fusion
  8.7 0.2 select_reduce_fusion
  8.9 0.1 all_to_all.12
  8.9 16.7 %all_to_all.19 = s32[32,1,16]{2,1,0:T(1,128)S(1)} all-to-all(s32[32,1,16]{2,1,0:T(1,128)S(1)} %bitcast.27), channel_id=1, replica_groups=mesh['img'=2,'ctx'=16,'tp'=4] {'img','ctx'}, dimensions={0} | all-to-all | bytes 4096 | tf_op jit(solution)/shard_map/all_to_all | solution.py:340
  25.7 0.2 reshape.43.pos_ref
  25.9 1.2 copy-done.2
  27.1 1.2 copy-done.9
  28.3 2.7 %collect.1 = bf16[512,2048]{1,0:T(8,128)(2,1)} custom-call(s32[512,1]{1,0:T(8,128)S(1)} %reshape.43.pos_ref, bf16[512,1024]{1,0:T(8,128)(2,1)S(1)} %copy-done.2, bf16[512,1024]{1,0:T(8,128)(2,1)S(1)} %bitcast.15), custom_call_target="tpu_custom_call" | custom-call | flops 1073741824 | bytes 4194304 | tf_op jit(solution)/shard_map/collect/pallas_call | solution.py:107
  31.0 4.9 %all-to-all-start.1 = ((bf16[32,16,2048]{2,1,0:T(8,128)(2,1)}), bf16[32,16,2048]{2,1,0:T(8,128)(2,1)}, u32[]{:S(2)}, u32[]{:S(2)}) async-start(bf16[32,16,2048]{2,1,0:T(8,128)(2,1)} %bitcast.7), calls=%async_computation.1 | async-start | bytes 4194304 | tf_op jit(solution)/shard_map/all_to_all | solution.py:345
  36.0 4.5 %layer_norm.1 = (bf16[4,256,1152]{2,1,0:T(8,128)(2,1)S(1)}, bf16[4,256,1152]{2,1,0:T(8,128)(2,1)S(1)}, f32[256,128]{1,0:T(8,128)S(1)}) custom-call(bf16[1024,1152]{1,0:T(8,128)(2,1)} %bitcast.25, bf16[4,1152]{1,0:T(4,128)(2,1)S(1)} %bitcast.17, bf16[4,1152]{1,0:T(4,128)(2,1)S(1)} %bitcast.20), custom_call_target="tpu_custom_call" | custom-call | flops 603979776 | bytes 7077888 | tf_op jit(solution)/shard_map/layer_norm/pallas_call | solution.py:72
  40.4 1.4 copy-done.4
  41.8 0.6 copy-done.11
  42.5 18.1 %all-to-all-done.1 = bf16[32,16,2048]{2,1,0:T(8,128)(2,1)} async-done(((bf16[32,16,2048]{2,1,0:T(8,128)(2,1)}), bf16[32,16,2048]{2,1,0:T(8,128)(2,1)}, u32[]{:S(2)}, u32[]{:S(2)}) %all-to-all-start.1) | async-done | bytes 2097184 | tf_op jit(solution)/shard_map/all_to_all | solution.py:345
  60.6 42.3 %all-gather.2.cloned.1.call-done = bf16[1,4,1152,1024]{3,2,1,0:T(8,128)(2,1)} async-done(((bf16[1,4,72,1024]{3,2,1,0:T(8,128)(2,1)}), bf16[1,4,1152,1024]{3,2,1,0:T(8,128)(2,1)}) %all-gather.2.cloned.1.call-update) | async-done | bytes 9437200 | tf_op jit(solution)/shard_map/all_gather | solution.py:329
  102.9 13.2 %forward.1 = (f32[256,1024]{1,0:T(8,128)S(1)}, f32[256,1024]{1,0:T(8,128)S(1)}, bf16[512,1024]{1,0:T(8,128)(2,1)S(1)}, f32[256,128]{1,0:T(8,128)S(1)}) custom-call(bf16[4,256,1152]{2,1,0:T(8,128)(2,1)} %copy-done.4, bf16[4,1152,1024]{2,1,0:T(8,128)(2,1)} %bitcast.22, s32[1,256]{1,0:T(1,128)S(1)} %bitcast.21, bf16[512,2048]{1,0:T(8,128)(2,1)} %bitcast.8.came_ref, ...), custom_call_target="tpu_custom_call" | custom-call | flops 2415919104 | bytes 9437184 | tf_op jit(solution)/shard_map/forward/pallas_call | solution.py:159
  116.1 1.0 copy-done
  117.1 1.0 copy-done.10
  118.0 0.7 collective-permute-start
  118.7 1.0 collective-permute-done
  119.7 2.8 %collective-permute-start.1 = (f32[256,128]{1,0:T(8,128)S(1)}, f32[256,128]{1,0:T(8,128)}, u32[]{:S(2)}, u32[]{:S(2)}) collective-permute-start(f32[256,128]{1,0:T(8,128)S(1)} %add.22.refs_3_), channel_id=1, source_target_pairs={{0,2},{1,3},{2,0},{3,1},{4,6},{5,7},{6,4},{7,5},{8,10},{9,11},{10,... | collective-permute-start | bytes 393224 | tf_op jit(solution)/shard_map/ppermute | solution.py:356
  122.5 3.7 %collective-permute-done.1.refs_4_ = f32[256,128]{1,0:T(8,128)} collective-permute-done((f32[256,128]{1,0:T(8,128)S(1)}, f32[256,128]{1,0:T(8,128)}, u32[]{:S(2)}, u32[]{:S(2)}) %collective-permute-start.1) | collective-permute-done | bytes 131104 | tf_op jit(solution)/shard_map/ppermute | solution.py:356
  126.1 1.2 copy-done.1
  127.3 10.9 %backward.2 = (f32[4,64,1152]{2,1,0:T(8,128)S(1)}, bf16[4,64,1152]{2,1,0:T(8,128)(2,1)}) custom-call(s32[1]{0:T(128)} %bitcast.11.refs_0_, f32[256,1024]{1,0:T(8,128)S(1)} %get-tuple-element.15.refs_1_, f32[256,1024]{1,0:T(8,128)S(1)} %copy-done.1, f32[256,128]{1,0:T(8,128)S(1)} %add.22.refs_3_, f32[256,128]{1,0:T(8,128)} %collective-permute-done.1.refs_4_, ...), custom_call_target="tpu_custom_call" | custom-call | flops 1207959552 | bytes 9437184 | tf_op jit(solution)/shard_map/backward/pallas_call | solution.py:218
  138.2 1.0 copy-done.7
  139.3 1.2 collective-permute-start.2
  140.4 10.9 %backward.3 = (f32[4,64,1152]{2,1,0:T(8,128)S(1)}, bf16[4,64,1152]{2,1,0:T(8,128)(2,1)}) custom-call(s32[1]{0:T(128)} %bitcast.11.refs_0_, f32[256,1024]{1,0:T(8,128)S(1)} %get-tuple-element.15.refs_1_, f32[256,1024]{1,0:T(8,128)S(1)} %copy-done.1, f32[256,128]{1,0:T(8,128)S(1)} %add.22.refs_3_, f32[256,128]{1,0:T(8,128)} %collective-permute-done.1.refs_4_, ...), custom_call_target="tpu_custom_call" | custom-call | flops 1207959552 | bytes 9437184 | tf_op jit(solution)/shard_map/backward/pallas_call | solution.py:218
  151.4 1.0 copy-done.5
  152.4 6.5 %all-to-all-start.2 = ((bf16[32,16,1024]{2,1,0:T(8,128)(2,1)}), bf16[32,16,1024]{2,1,0:T(8,128)(2,1)}, u32[]{:S(2)}, u32[]{:S(2)}) async-start(bf16[32,16,1024]{2,1,0:T(8,128)(2,1)} %bitcast.16), calls=%async_computation.2 | async-start | bytes 2097152 | tf_op jit(solution)/shard_map/all_to_all | solution.py:358
  158.9 1.3 add_convert_fusion.1.own_ref
  160.2 2.5 %collective-permute-start.3 = (bf16[4,64,1152]{2,1,0:T(8,128)(2,1)S(1)}, bf16[4,64,1152]{2,1,0:T(8,128)(2,1)S(1)}, u32[]{:S(2)}, u32[]{:S(2)}) collective-permute-start(bf16[4,64,1152]{2,1,0:T(8,128)(2,1)S(1)} %add_convert_fusion.1.own_ref), channel_id=1, source_target_pairs={{0,2},{1,3},{2,0},{3,1},{4,6},{5,7},{6,4},{7,5},{8,10},{9,11},{10,... | collective-permute-start | bytes 1769480 | tf_op jit(solution)/shard_map/ppermute | solution.py:372
  162.7 1.2 add_convert_fusion.own_ref
  163.9 0.6 collective-permute-start.5
  164.5 21.0 %collective-permute-done.3.far_ref = bf16[4,64,1152]{2,1,0:T(8,128)(2,1)S(1)} collective-permute-done((bf16[4,64,1152]{2,1,0:T(8,128)(2,1)S(1)}, bf16[4,64,1152]{2,1,0:T(8,128)(2,1)S(1)}, u32[]{:S(2)}, u32[]{:S(2)}) %collective-permute-start.3) | collective-permute-done | bytes 589856 | tf_op jit(solution)/shard_map/ppermute | solution.py:372
  185.5 1.7 finish.2
  187.2 2.0 collective-permute-start.6
  189.2 8.9 %collective-permute-done.5.far_ref = bf16[4,64,1152]{2,1,0:T(8,128)(2,1)S(1)} collective-permute-done((bf16[4,64,1152]{2,1,0:T(8,128)(2,1)S(1)}, bf16[4,64,1152]{2,1,0:T(8,128)(2,1)S(1)}, u32[]{:S(2)}, u32[]{:S(2)}) %collective-permute-start.5) | collective-permute-done | bytes 589856 | tf_op jit(solution)/shard_map/ppermute | solution.py:372
  198.1 1.7 finish.3
  199.9 1.2 collective-permute-start.7
  201.1 0.6 broadcast.19
  201.7 0.7 reduce.5
  202.4 0.1 reshape.36.pos_ref
  202.5 2.9 %place.1 = bf16[512,1024]{1,0:T(8,128)(2,1)} custom-call(s32[1,512]{1,0:T(1,128)S(1)} %reshape.36.pos_ref, bf16[512,1024]{1,0:T(8,128)(2,1)} %bitcast.10.came_ref, bf16[512,1024]{1,0:T(8,128)(2,1)S(1)} %copy-done.3), custom_call_target="tpu_custom_call" | custom-call | flops 536870912 | bytes 3145728 | tf_op jit(solution)/shard_map/place/pallas_call | solution.py:302
  205.4 1.1 constant_dynamic-update-slice_fusion.1
  206.5 0.1 constant_dynamic-update-slice_fusion
  206.6 1.7 broadcast_select_fusion.1
  208.3 1.6 maximum_bitcast_fusion
  (36 shorter events, 0.1 us)
Async XLA Ops:
  7.2 95.7 %all-gather.2.cloned.1.call-start = ((), (), s32[]{:S(2)}) async-start(), calls=%async_computation.3 | async-start | bytes 10027008 | tf_op jit(solution)/shard_map/all_gather | solution.py:329
  25.7 5.3 %copy-start.16 = (s32[32,1,16]{2,1,0:T(1,128)}, s32[32,1,16]{2,1,0:T(1,128)S(1)}, u32[]{:S(2)}) copy-start(s32[32,1,16]{2,1,0:T(1,128)S(1)} %all_to_all.19) | copy-start | bytes 6148
  25.8 1.2 copy-start.2
  27.1 1.2 copy-start.9
  31.0 4.9 %copy-start.13 = (bf16[1,4,1152]{2,1,0:T(4,128)(2,1)S(1)}, bf16[1,4,1152]{2,1,0:T(4,128)(2,1)}, u32[]{:S(2)}) copy-start(bf16[1,4,1152]{2,1,0:T(4,128)(2,1)} %param.9) | copy-start | bytes 27652
  31.0 4.9 %copy-start.14 = (bf16[1,4,1152]{2,1,0:T(4,128)(2,1)S(1)}, bf16[1,4,1152]{2,1,0:T(4,128)(2,1)}, u32[]{:S(2)}) copy-start(bf16[1,4,1152]{2,1,0:T(4,128)(2,1)} %param.10) | copy-start | bytes 27652
  31.0 29.5 %all-to-all-start.1 = ((bf16[32,16,2048]{2,1,0:T(8,128)(2,1)}), bf16[32,16,2048]{2,1,0:T(8,128)(2,1)}, u32[]{:S(2)}, u32[]{:S(2)}) async-start(bf16[32,16,2048]{2,1,0:T(8,128)(2,1)} %bitcast.7), calls=%async_computation.1 | async-start | bytes 4194304 | tf_op jit(solution)/shard_map/all_to_all | solution.py:345
  36.0 66.9 %copy-start.15 = (bf16[1,1024]{1,0:T(2,128)(2,1)S(1)}, bf16[1,1024]{1,0:T(2,128)(2,1)}, u32[]{:S(2)}) copy-start(bf16[1,1024]{1,0:T(2,128)(2,1)} %ngain_ref.1) | copy-start | bytes 6148
  40.4 1.4 copy-start.4
  41.8 0.6 copy-start.11
  116.1 1.0 copy-start
  117.1 1.0 copy-start.10
  118.0 1.6 collective-permute-start
  119.7 6.4 %collective-permute-start.1 = (f32[256,128]{1,0:T(8,128)S(1)}, f32[256,128]{1,0:T(8,128)}, u32[]{:S(2)}, u32[]{:S(2)}) collective-permute-start(f32[256,128]{1,0:T(8,128)S(1)} %add.22.refs_3_), channel_id=1, source_target_pairs={{0,2},{1,3},{2,0},{3,1},{4,6},{5,7},{6,4},{7,5},{8,10},{9,11},{10,... | collective-permute-start | bytes 393224 | tf_op jit(solution)/shard_map/ppermute | solution.py:356
  126.1 1.2 copy-start.1
  138.2 1.0 copy-start.7
  139.3 19.6 %collective-permute-start.2 = (bf16[4,64,1152]{2,1,0:T(8,128)(2,1)}, bf16[4,64,1152]{2,1,0:T(8,128)(2,1)}, u32[]{:S(2)}, u32[]{:S(2)}) collective-permute-start(bf16[4,64,1152]{2,1,0:T(8,128)(2,1)} %get-tuple-element.19), channel_id=1, source_target_pairs={{0,1},{1,0},{2,3},{3,2},{4,5},{5,4},{6,7},{7,6},{8,9},{9,8},{10,11... | collective-permute-start | bytes 1769480 | tf_op jit(solution)/shard_map/ppermute | solution.py:370
  151.3 1.0 copy-start.5
  152.4 6.5 %copy-start.8 = (f32[4,64,1152]{2,1,0:T(8,128)S(1)}, f32[4,64,1152]{2,1,0:T(8,128)}, u32[]{:S(2)}) copy-start(f32[4,64,1152]{2,1,0:T(8,128)} %copy-done.7) | copy-start | bytes 3538948
  152.4 10.3 %collective-permute-start.4 = (bf16[4,64,1152]{2,1,0:T(8,128)(2,1)}, bf16[4,64,1152]{2,1,0:T(8,128)(2,1)}, u32[]{:S(2)}, u32[]{:S(2)}) collective-permute-start(bf16[4,64,1152]{2,1,0:T(8,128)(2,1)} %get-tuple-element.23), channel_id=1, source_target_pairs={{0,1},{1,0},{2,3},{3,2},{4,5},{5,4},{6,7},{7,6},{8,9},{9,8},{10,11... | collective-permute-start | bytes 1769480 | tf_op jit(solution)/shard_map/ppermute | solution.py:370
  152.4 50.1 %all-to-all-start.2 = ((bf16[32,16,1024]{2,1,0:T(8,128)(2,1)}), bf16[32,16,1024]{2,1,0:T(8,128)(2,1)}, u32[]{:S(2)}, u32[]{:S(2)}) async-start(bf16[32,16,1024]{2,1,0:T(8,128)(2,1)} %bitcast.16), calls=%async_computation.2 | async-start | bytes 2097152 | tf_op jit(solution)/shard_map/all_to_all | solution.py:358
  158.9 3.8 %copy-start.6 = (f32[4,64,1152]{2,1,0:T(8,128)S(1)}, f32[4,64,1152]{2,1,0:T(8,128)}, u32[]{:S(2)}) copy-start(f32[4,64,1152]{2,1,0:T(8,128)} %copy-done.5) | copy-start | bytes 3538948
  160.2 25.3 %collective-permute-start.3 = (bf16[4,64,1152]{2,1,0:T(8,128)(2,1)S(1)}, bf16[4,64,1152]{2,1,0:T(8,128)(2,1)S(1)}, u32[]{:S(2)}, u32[]{:S(2)}) collective-permute-start(bf16[4,64,1152]{2,1,0:T(8,128)(2,1)S(1)} %add_convert_fusion.1.own_ref), channel_id=1, source_target_pairs={{0,2},{1,3},{2,0},{3,1},{4,6},{5,7},{6,4},{7,5},{8,10},{9,11},{10,... | collective-permute-start | bytes 1769480 | tf_op jit(solution)/shard_map/ppermute | solution.py:372
  162.7 22.8 %copy-start.12 = (f32[256,128]{1,0:T(8,128)S(1)}, f32[256,128]{1,0:T(8,128)}, u32[]{:S(2)}) copy-start(f32[256,128]{1,0:T(8,128)} %copy-done.11) | copy-start | bytes 393220
  163.9 34.2 %collective-permute-start.5 = (bf16[4,64,1152]{2,1,0:T(8,128)(2,1)S(1)}, bf16[4,64,1152]{2,1,0:T(8,128)(2,1)S(1)}, u32[]{:S(2)}, u32[]{:S(2)}) collective-permute-start(bf16[4,64,1152]{2,1,0:T(8,128)(2,1)S(1)} %add_convert_fusion.own_ref), channel_id=1, source_target_pairs={{0,2},{1,3},{2,0},{3,1},{4,6},{5,7},{6,4},{7,5},{8,10},{9,11},{10,... | collective-permute-start | bytes 1769480 | tf_op jit(solution)/shard_map/ppermute | solution.py:372
  187.2 18.2 %collective-permute-start.6 = (bf16[256,1152]{1,0:T(8,128)(2,1)}, bf16[256,1152]{1,0:T(8,128)(2,1)}, u32[]{:S(2)}, u32[]{:S(2)}) collective-permute-start(bf16[256,1152]{1,0:T(8,128)(2,1)} %finish.2), channel_id=1, source_target_pairs={{0,1},{1,0},{2,3},{3,2},{4,5},{5,4},{6,7},{7,6},{8,9},{9,8},{10,11... | collective-permute-start | bytes 1769480 | tf_op jit(solution)/shard_map/ppermute | solution.py:375
  189.2 12.5 %copy-start.17 = (s32[32,1,16]{2,1,0:T(1,128)S(1)}, s32[32,1,16]{2,1,0:T(1,128)}, u32[]{:S(2)}) copy-start(s32[32,1,16]{2,1,0:T(1,128)} %copy-done.16) | copy-start | bytes 6148
  189.2 13.3 %copy-start.3 = (bf16[512,1024]{1,0:T(8,128)(2,1)S(1)}, bf16[512,1024]{1,0:T(8,128)(2,1)}, u32[]{:S(2)}) copy-start(bf16[512,1024]{1,0:T(8,128)(2,1)} %stream_ref.3) | copy-start | bytes 3145732
  199.9 6.7 %collective-permute-start.7 = (bf16[256,1152]{1,0:T(8,128)(2,1)}, bf16[256,1152]{1,0:T(8,128)(2,1)S(1)}, u32[]{:S(2)}, u32[]{:S(2)}) collective-permute-start(bf16[256,1152]{1,0:T(8,128)(2,1)} %finish.3), channel_id=1, source_target_pairs={{0,1},{1,0},{2,3},{3,2},{4,5},{5,4},{6,7},{7,6},{8,9},{9,8},{10,11... | collective-permute-start | bytes 1769480 | tf_op jit(solution)/shard_map/ppermute | solution.py:375
Sparse Core Ops, SparseCore 0:
  10.1 92.7 all-gather.1

commit v2 on v1

v2 whole, which is shorter than its diff:
```python
import jax
import jax.numpy as jnp
from jax import lax
from jax.experimental import pallas as pl
from jax.experimental.pallas import tpu as pltpu
from jax.sharding import PartitionSpec as P

BF = jnp.bfloat16
F32 = jnp.float32
VMEM = pltpu.VMEM
SMEM = pltpu.SMEM


def params(mib):
    return pltpu.CompilerParams(vmem_limit_bytes=mib * 1024 * 1024)


def whole():
    return pl.BlockSpec(memory_space=VMEM)


def cost(flops, moved):
    return pl.CostEstimate(flops=flops, bytes_accessed=moved, transcendentals=0)


def eq_hot(shape, dim, index):
    return (lax.broadcasted_iota(jnp.int32, shape, dim) == index).astype(BF)


def window_major(tokens, window):
    n = tokens * window
    row = lax.broadcasted_iota(jnp.int32, (n, n), 0)
    col = lax.broadcasted_iota(jnp.int32, (n, n), 1)
    return (col == (row % tokens) * window + row // tokens).astype(BF)


def patch_major(tokens, window):
    n = tokens * window
    row = lax.broadcasted_iota(jnp.int32, (n, n), 0)
    col = lax.broadcasted_iota(jnp.int32, (n, n), 1)
    return (col == (row % window) * tokens + row // window).astype(BF)


SIDE = 4


def piece_slices(window, share):
    half = window // 2
    pieces = []
    for first in range(SIDE):
        pieces.append([(w, (first * SIDE + y) * share) for y in range(SIDE) for w in range(half)])
    for first in range(SIDE):
        pieces.append(
            [(w, (z * SIDE + first) * share) for z in range(SIDE) for w in range(half, window)]
        )
    return pieces


def norm_kernel(x_ref, gain_ref, bias_ref, lifted_ref, xw_ref, stat_ref):
    window, width = gain_ref.shape
    tokens = x_ref.shape[0] // window
    full = window * width
    share = width // (SIDE * SIDE)
    x = jnp.dot(
        window_major(tokens, window), x_ref[...], preferred_element_type=F32
    )
    parts = [x[w * tokens : (w + 1) * tokens] for w in range(window)]
    total = sum(jnp.sum(p, axis=1, keepdims=True) for p in parts)
    squares = sum(jnp.sum(p * p, axis=1, keepdims=True) for p in parts)
    mean = total / full
    inv = lax.rsqrt(squares / full - mean * mean + 1e-05)
    lifted = []
    for w, p in enumerate(parts):
        normed = (p - mean) * inv
        lifted.append(
            normed * gain_ref[w : w + 1].astype(F32) + bias_ref[w : w + 1].astype(F32)
        )
        xw_ref[w] = p.astype(BF)
    for index, piece in enumerate(piece_slices(window, share)):
        lifted_ref[index] = jnp.concatenate(
            [lifted[w][:, at : at + share] for w, at in piece], axis=1
        ).astype(BF)
    lane = lax.broadcasted_iota(jnp.int32, stat_ref.shape, 1)
    stat_ref[...] = jnp.where(lane == 0, mean, inv)


def layer_norm(features, gain, bias):
    rows, width = features.shape
    window = gain.shape[0]
    merged = rows // window
    block = 64
    piece = window * width // (2 * SIDE)
    return pl.pallas_call(
        norm_kernel,
        grid=(merged // block,),
        in_specs=[
            pl.BlockSpec((block * window, width), lambda i: (i, 0)),
            pl.BlockSpec((window, width), lambda i: (0, 0)),
            pl.BlockSpec((window, width), lambda i: (0, 0)),
        ],
        out_specs=[
            pl.BlockSpec((2 * SIDE, block, piece), lambda i: (0, i, 0)),
            pl.BlockSpec((window, block, width), lambda i: (0, i, 0)),
            pl.BlockSpec((block, 128), lambda i: (i, 0)),
        ],
        out_shape=[
            jax.ShapeDtypeStruct((2 * SIDE, merged, piece), BF),
            jax.ShapeDtypeStruct((window, merged, width), BF),
            jax.ShapeDtypeStruct((merged, 128), F32),
        ],
        compiler_params=params(24),
        cost_estimate=cost(2 * rows * block * window * width, 6 * rows * width),
        name="layer_norm",
    )(features, gain, bias)


def collect_kernel(pos_ref, stream_ref, cot_ref, out_ref):
    slots = pos_ref.shape[0]
    rows, width = stream_ref.shape
    pick = eq_hot((slots, rows), 1, pos_ref[...])
    out_ref[:, :width] = jnp.dot(pick, stream_ref[...], preferred_element_type=F32).astype(BF)
    out_ref[:, width:] = jnp.dot(pick, cot_ref[...], preferred_element_type=F32).astype(BF)


def collect(pos, stream, cot):
    slots = pos.shape[0]
    rows, width = stream.shape
    return pl.pallas_call(
        collect_kernel,
        in_specs=[whole()] * 3,
        out_specs=whole(),
        out_shape=jax.ShapeDtypeStruct((slots, 2 * width), BF),
        compiler_params=params(24),
        cost_estimate=cost(4 * slots * rows * width, 8 * rows * width),
        name="collect",
    )(pos, stream, cot)


def unpack_kernel(slot_ref, came_ref, ngain_ref, base_ref, up_ref):
    tokens, width = base_ref.shape
    slots = came_ref.shape[0]
    take = eq_hot((tokens, slots), 1, slot_ref[...])
    base_ref[...] = jnp.dot(take, came_ref[:, :width], preferred_element_type=F32)
    up_ref[...] = jnp.dot(take, came_ref[:, width:], preferred_element_type=F32) * ngain_ref[
        ...
    ].astype(F32)


def unpack(slot_col, came, ngain):
    tokens = slot_col.shape[0]
    slots, both = came.shape
    width = both // 2
    return pl.pallas_call(
        unpack_kernel,
        in_specs=[whole()] * 3,
        out_specs=[whole()] * 2,
        out_shape=[jax.ShapeDtypeStruct((tokens, width), F32)] * 2,
        compiler_params=params(16),
        cost_estimate=cost(4 * slots * tokens * width, 8 * tokens * width),
        name="unpack",
    )(slot_col, came, ngain)


def stack_kernel(me_ref, *refs):
    out_ref = refs[-1]
    me = me_ref[0]
    for away, ref in zip((0, SIDE - 1, 1, 2), refs[:-1]):
        out_ref[lax.rem(me + away, SIDE)] = ref[...]


def stack(me, blocks):
    rows, width = blocks[0].shape
    return pl.pallas_call(
        stack_kernel,
        in_specs=[pl.BlockSpec(memory_space=SMEM)] + [whole()] * 4,
        out_specs=whole(),
        out_shape=jax.ShapeDtypeStruct((SIDE, rows, width), BF),
        compiler_params=params(8),
        cost_estimate=cost(0, 16 * rows * width),
        name="stack",
    )(me, *blocks)


def multiply_kernel(plan, count, zy_ref, lifted_ref, *refs):
    total = None
    if len(refs) > count + 1:
        total = refs[count][...]
    for (axis, away, start, stop), ref in zip(plan, refs[:count]):
        index = axis * SIDE + lax.rem(zy_ref[axis] + away, SIDE)
        rows = ref.shape[0]
        left = lifted_ref[index][:, start:stop]
        part = jnp.dot(left, ref[...], preferred_element_type=F32)
        total = part if total is None else total + part
    refs[-1][...] = total


def multiply(zy, lifted, pieces, plan, before=None):
    tokens = lifted.shape[1]
    width = pieces[0].shape[1]
    extra = [] if before is None else [before]
    depth = sum(p.shape[0] for p in pieces)
    return pl.pallas_call(
        lambda *refs: multiply_kernel(plan, len(pieces), *refs),
        in_specs=[pl.BlockSpec(memory_space=SMEM)] + [whole()] * (1 + len(pieces) + len(extra)),
        out_specs=whole(),
        out_shape=jax.ShapeDtypeStruct((tokens, width), F32),
        compiler_params=params(24),
        cost_estimate=cost(2 * depth * tokens * width, 2 * depth * width),
        name="multiply",
    )(zy, lifted, *pieces, *extra)


def merge_kernel(acc_ref, base_ref, up_ref, visual_ref, state_ref, stat_ref):
    visual = acc_ref[...].astype(BF)
    visual_ref[...] = visual
    state = base_ref[...] + visual.astype(F32)
    state_ref[...] = state
    lane = lax.broadcasted_iota(jnp.int32, stat_ref.shape, 1)
    stat_ref[...] = jnp.where(
        lane == 0,
        jnp.sum(state * state, axis=1, keepdims=True),
        jnp.sum(up_ref[...] * state, axis=1, keepdims=True),
    )


def merge(acc, base, up):
    tokens, width = acc.shape
    return pl.pallas_call(
        merge_kernel,
        in_specs=[whole()] * 3,
        out_specs=[whole()] * 3,
        out_shape=[
            jax.ShapeDtypeStruct((tokens, width), BF),
            jax.ShapeDtypeStruct((tokens, width), F32),
            jax.ShapeDtypeStruct((tokens, 128), F32),
        ],
        compiler_params=params(16),
        cost_estimate=cost(8 * tokens * width, 18 * tokens * width),
        name="merge",
    )(acc, base, up)


def pack_kernel(slot_ref, visual_ref, out_ref):
    slots = out_ref.shape[0]
    tokens = visual_ref.shape[0]
    put = eq_hot((slots, tokens), 0, slot_ref[...])
    out_ref[...] = jnp.dot(put, visual_ref[...], preferred_element_type=F32).astype(BF)


def pack(slot_row, visual, slots):
    tokens, width = visual.shape
    return pl.pallas_call(
        pack_kernel,
        in_specs=[whole()] * 2,
        out_specs=whole(),
        out_shape=jax.ShapeDtypeStruct((slots, width), BF),
        compiler_params=params(16),
        cost_estimate=cost(2 * slots * tokens * width, 2 * (slots + tokens) * width),
        name="pack",
    )(slot_row, visual)


def assemble_kernel(plan, zy_ref, *refs):
    out_ref = refs[-1]
    for (axis, away, start, stop), ref in zip(plan, refs[:-1]):
        index = axis * SIDE + lax.rem(zy_ref[axis] + away, SIDE)
        out_ref[index, start:stop, :] = ref[...]


def assemble(zy, pieces, plan):
    depth = sum(p.shape[0] for p in pieces)
    width = pieces[0].shape[1]
    return pl.pallas_call(
        lambda *refs: assemble_kernel(plan, *refs),
        in_specs=[pl.BlockSpec(memory_space=SMEM)] + [whole()] * len(pieces),
        out_specs=whole(),
        out_shape=jax.ShapeDtypeStruct((2 * SIDE, depth // (2 * SIDE), width), BF),
        compiler_params=params(32),
        cost_estimate=cost(0, 4 * depth * width),
        name="assemble",
    )(zy, *pieces)


def backward_kernel(full_width, chunks, core_ref, state_ref, up_ref, stat_a_ref, stat_b_ref, w_ref, *refs):
    picked_ref = refs[-1]
    tokens = state_ref.shape[0]
    half = tokens // 2
    rows = half // chunks
    core = core_ref[0]
    for place, owner in enumerate((core, 1 - core)):
        at = pl.ds(pl.multiple_of(owner * half, half), half)
        sums = stat_a_ref[at, :] + stat_b_ref[at, :]
        inv = lax.rsqrt(sums[:, 0:1] / full_width + 1e-06)
        inner = sums[:, 1:2] / full_width
        grad = inv * up_ref[at, :] - state_ref[at, :] * (inv * inv * inv * inner)
        picked_ref[place * half : (place + 1) * half, :] = grad.astype(BF)
    depth = w_ref.shape[0]
    block = depth // SIDE
    for step in range(SIDE):
        cols = slice(step * block, (step + 1) * block)
        both = lax.dot_general(
            picked_ref[...], w_ref[cols, :], (((1,), (1,)), ((), ())), preferred_element_type=F32
        )
        for chunk in range(chunks):
            refs[chunk][:, cols] = both[chunk * rows : (chunk + 1) * rows]
            refs[chunks + chunk][:, cols] = both[
                half + chunk * rows : half + (chunk + 1) * rows
            ].astype(BF)


def backward(core, state, up, stat_a, stat_b, weight, chunks, full_width):
    depth, width = weight.shape
    tokens = state.shape[0]
    rows = tokens // 2 // chunks
    return pl.pallas_call(
        lambda *refs: backward_kernel(full_width, chunks, *refs),
        in_specs=[pl.BlockSpec(memory_space=SMEM)] + [whole()] * 5,
        out_specs=[whole()] * (2 * chunks),
        out_shape=[jax.ShapeDtypeStruct((rows, depth), F32)] * chunks
        + [jax.ShapeDtypeStruct((rows, depth), BF)] * chunks,
        scratch_shapes=[pltpu.VMEM((tokens, width), BF)],
        compiler_params=params(32),
        cost_estimate=cost(2 * depth * tokens * width, 2 * depth * width),
        name="backward",
    )(core, state, up, stat_a, stat_b, weight)


def finish_kernel(block_ref, own_ref, far_ref, xw_ref, stat_ref, gain_ref, out_ref):
    window, tokens, width = xw_ref.shape
    full = window * width
    share = width // (SIDE * SIDE)
    piece = full // (2 * SIDE)
    mean = stat_ref[:, 0:1]
    inv = stat_ref[:, 1:2]
    lifted = own_ref[...].astype(F32) + far_ref[...].astype(F32)
    where = {}
    for index, slices in enumerate(piece_slices(window, share)):
        for place, key in enumerate(slices):
            where[key] = index * piece + place * share
    scaled = []
    total = 0.0
    inner = 0.0
    for w in range(window):
        starts = [where[(w, at)] for at in range(0, width, share)]
        g = jnp.concatenate([lifted[:, at : at + share] for at in starts], axis=1)
        g = g * gain_ref[w : w + 1].astype(F32)
        normed = (xw_ref[w].astype(F32) - mean) * inv
        total = total + jnp.sum(g, axis=1, keepdims=True)
        inner = inner + jnp.sum(g * normed, axis=1, keepdims=True)
        scaled.append((g, normed))
    total = total / full
    inner = inner / full
    rows = jnp.concatenate(
        [(inv * (g - total - normed * inner)).astype(BF) for g, normed in scaled], axis=0
    )
    out_ref[...] = jnp.dot(
        patch_major(tokens, window), rows, preferred_element_type=F32
    ).astype(BF)


def finish(block, own, far, xw, stat, gain):
    tokens, full = own.shape
    window, width = gain.shape
    return pl.pallas_call(
        finish_kernel,
        grid_spec=pltpu.PrefetchScalarGridSpec(
            num_scalar_prefetch=1,
            grid=(1,),
            in_specs=[
                pl.BlockSpec((tokens, full), lambda i, b: (0, 0)),
                pl.BlockSpec((tokens, full), lambda i, b: (0, 0)),
                pl.BlockSpec((window, tokens, width), lambda i, b: (0, b[0], 0)),
                pl.BlockSpec((tokens, 128), lambda i, b: (b[0], 0)),
                pl.BlockSpec((window, width), lambda i, b: (0, 0)),
            ],
            out_specs=pl.BlockSpec((tokens * window, width), lambda i, b: (0, 0)),
        ),
        out_shape=jax.ShapeDtypeStruct((tokens * window, width), BF),
        compiler_params=params(24),
        cost_estimate=cost(2 * (tokens * window) ** 2 * width, 8 * window * tokens * width),
        name="finish",
    )(block, own, far, xw, stat, gain)


def place_kernel(pos_ref, came_ref, stream_ref, out_ref):
    slots = came_ref.shape[0]
    rows, width = stream_ref.shape
    put = eq_hot((rows, slots), 0, pos_ref[...])
    out_ref[...] = (
        stream_ref[...].astype(F32) + jnp.dot(put, came_ref[...], preferred_element_type=F32)
    ).astype(BF)


def place(pos, came, stream):
    rows, width = stream.shape
    return pl.pallas_call(
        place_kernel,
        in_specs=[whole()] * 3,
        out_specs=whole(),
        out_shape=jax.ShapeDtypeStruct((rows, width), BF),
        compiler_params=params(16),
        cost_estimate=cost(2 * came.shape[0] * rows * width, 6 * rows * width),
        name="place",
    )(pos, came, stream)


def shards(features, ln_gain, ln_bias, projection, stream, norm_gain, cotangent, slots):
    n_img = lax.axis_size("img")
    n_ctx = lax.axis_size("ctx")
    n_tp = lax.axis_size("tp")
    merged = slots.shape[0]
    window = ln_gain.shape[1]
    tok_rows, width = stream.shape
    owners = n_img * n_ctx
    capacity = 2 * merged // owners
    slot_count = owners * capacity
    full_width = width * n_tp

    core_pairs = [(t, t ^ 1) for t in range(n_tp)]
    far_pairs = [(t, t ^ 2) for t in range(n_tp)]
    core = (lax.axis_index("tp") % 2).astype(jnp.int32).reshape(1)

    zy = jnp.stack([lax.axis_index("ctx") // SIDE, lax.axis_index("ctx") % SIDE]).astype(jnp.int32)

    def moved(array, axis, by):
        pairs = []
        for z in range(SIDE):
            for y in range(SIDE):
                to = ((z + by) % SIDE, y) if axis == 0 else (z, (y + by) % SIDE)
                pairs.append((z * SIDE + y, to[0] * SIDE + to[1]))
        return lax.ppermute(array, "ctx", pairs)

    half = window // 2
    share = projection.shape[2]
    mine_a = projection[0, :half].reshape(half * share, width)
    mine_b = projection[0, half:].reshape(half * share, width)
    first_a = [mine_a] + [moved(mine_a, 1, by) for by in (1, -1, 2)]
    first_b = [mine_b] + [moved(mine_b, 0, by) for by in (1, -1, 2)]

    target = slots // tok_rows
    ids = jnp.arange(merged)
    earlier = (target[:, None] == target[None, :]) & (ids[:, None] < ids[None, :])
    rank = jnp.sum(earlier.astype(jnp.int32), axis=0)
    slot = target * capacity + rank
    local = slots - target * tok_rows
    packed = jnp.max(
        jnp.where(jnp.arange(slot_count)[:, None] == slot[None, :], local[None, :], -1), axis=1
    )
    asked = lax.all_to_all(
        packed.reshape(owners, capacity), ("img", "ctx"), split_axis=0, concat_axis=0, tiled=True
    )
    held = collect(asked.reshape(slot_count, 1), stream, cotangent[0])
    came = lax.all_to_all(
        held.reshape(owners, capacity, 2 * width),
        ("img", "ctx"), split_axis=0, concat_axis=0, tiled=True,
    ).reshape(slot_count, 2 * width)

    gain = ln_gain[0]
    lifted, xw, stat = layer_norm(features[0], gain, ln_bias[0])

    stack_a = stack(zy[1:], first_a).reshape(SIDE * half * share, width)
    stack_b = stack(zy[:1], first_b).reshape(SIDE * half * share, width)
    pieces, plan, far_pieces, far_plan = [], [], [], []
    for axis, block in ((0, stack_a), (1, stack_b)):
        rows = block.shape[0]
        before = moved(block, axis, 1)
        after = moved(block, axis, -1)
        pieces += [block, before, after]
        plan += [(axis, 0, 0, rows), (axis, SIDE - 1, 0, rows), (axis, 1, 0, rows)]
        far_pieces += [moved(before[: rows // 2], axis, 1), moved(after[rows // 2 :], axis, -1)]
        far_plan += [(axis, 2, 0, rows // 2), (axis, 2, rows // 2, rows)]

    base, up = unpack(slot.reshape(merged, 1), came, norm_gain)
    acc = multiply(zy, lifted, pieces, plan)
    acc = multiply(zy, lifted, far_pieces, far_plan, acc)
    visual, state, sums = merge(acc, base, up)

    near = sums + lax.ppermute(sums, "tp", core_pairs)
    far = lax.ppermute(near, "tp", far_pairs)
    weight = assemble(zy, pieces + far_pieces, plan + far_plan).reshape(-1, width)

    send = pack(slot.reshape(1, merged), visual, slot_count)
    arrived = lax.all_to_all(
        send.reshape(owners, capacity, width),
        ("img", "ctx"), split_axis=0, concat_axis=0, tiled=True,
    ).reshape(slot_count, width)
    new_stream = place(asked.reshape(1, slot_count), arrived, stream)

    chunks = 2
    parts = backward(core, state, up, near, far, weight, chunks, full_width)
    own_out, got_out = [], []
    for chunk in range(chunks):
        got = lax.ppermute(parts[chunks + chunk], "tp", core_pairs)
        pair = (parts[chunk] + got.astype(F32)).astype(BF)
        beyond = lax.ppermute(pair, "tp", far_pairs)
        out = finish(core * chunks + chunk, pair, beyond, xw, stat, gain)
        own_out.append(out)
        got_out.append(lax.ppermute(out, "tp", core_pairs))
    first = core[0] == 0
    own = jnp.concatenate(own_out, axis=0)
    got = jnp.concatenate(got_out, axis=0)
    grad = jnp.concatenate([jnp.where(first, own, got), jnp.where(first, got, own)], axis=0)
    return (new_stream, grad[None])


def solution(mesh):
    placed = (
        P(None, ("img", "ctx"), None),
        P(),
        P(),
        P(None, None, "ctx", "tp"),
        P(("img", "ctx"), "tp"),
        P(None, "tp"),
        P(None, ("img", "ctx"), "tp"),
        P(("img", "ctx")),
    )
    return jax.shard_map(
        shards,
        mesh=mesh,
        in_specs=placed,
        out_specs=(P(("img", "ctx"), "tp"), P(None, ("img", "ctx"), None)),
        check_vma=False,
    )
```

time: 218 us -> 205 us (0.940)
  starting transfers between devices: 22.3 us -> 44.9 us
  Pallas kernels: 48.6 us -> 30.6 us
  local copies, waits for them, and re-layouts: 11.8 us -> 29.8 us
  waiting for transfers between devices: 95.6 us -> 79.2 us
  between operations: 14.2 us -> 1 us
  blocking collectives: 16.7 us -> 12.9 us
    ppermute x2 -> x16, waiting for transfers between devices: 0.01 us -> 47.3 us  [the longest x14 47.3 us: moved(): return lax.ppermute(array, 'ctx', pairs)]
    all_gather x1 -> x0, waiting for transfers between devices: 42.3 us -> none  [shards(): weight = lax.all_gather(projection, 'ctx', axis=2, tiled=True)[0]]
    ppermute x2 -> x16, starting transfers between devices: 1.19 us -> 22.6 us  [the longest x14 21.6 us: moved(): return lax.ppermute(array, 'ctx', pairs)]
    all_to_all x1, waiting for transfers between devices: 18.1 us -> 0.01 us  [shards(): lax.all_to_all(held.reshape(owners, capacity, 2 * width), ('img', 'ctx'),...]
    pallas_call x3 -> x9, Pallas kernels: 35 us -> 18.8 us  [the longest x2 6.02 us: multiply(): pl.pallas_call(lambda *refs: multiply_kernel(plan, len(pieces), *refs), i...]
    unnamed x37 -> x81, local copies, waits for them, and re-layouts: 10.8 us -> 22.3 us
    slice x0 -> x5, local copies, waits for them, and re-layouts: none -> 4.74 us  [the longest x2 1.85 us: shards(): before[:rows // 2]]
    all_to_all x1, blocking collectives: 16.7 us -> 12.9 us  [shards(): lax.all_to_all(packed.reshape(owners, capacity), ('img', 'ctx'), split_ax...]
  transfers between devices with their start and end apart: 11 -> 24, of which waited for: 6 -> 8; matrix products, arithmetic and copies ran while one was open for 3% -> 4% of each run, Pallas kernels for 11% -> 11%
where the time goes in v2:
time: 205 us; the launch traced here: 204 us
  waiting for transfers between devices  79.2 us (39%)
  starting transfers between devices  44.9 us (22%)
  Pallas kernels  30.6 us (15%)
  local copies, waits for them, and re-layouts  29.8 us (15%)
  blocking collectives  12.9 us (6%)
  other arithmetic  5.45 us (3%)
    ppermute x14, waiting for transfers between devices, moved(): return lax.ppermute(array, 'ctx', pairs)  47.3 us
    ppermute x2, waiting for transfers between devices, shards(): beyond = lax.ppermute(pair, 'tp', far_pairs)  30.9 us
    unnamed x81, local copies, waits for them, and re-layouts  22.3 us
    ppermute x14, starting transfers between devices, moved(): return lax.ppermute(array, 'ctx', pairs)  21.6 us
    all_to_all x1, blocking collectives, shards(): lax.all_to_all(packed.reshape(owners, capacity), ('img', 'ctx'), split_ax...  12.9 us
    all_to_all x1, starting transfers between devices, shards(): lax.all_to_all(send.reshape(owners, capacity, width), ('img', 'ctx'), spl...  6.54 us
    pallas_call x2, Pallas kernels, multiply(): pl.pallas_call(lambda *refs: multiply_kernel(plan, len(pieces), *refs), i...  6.02 us
    pallas_call x1, Pallas kernels, backward(): pl.pallas_call(lambda *refs: backward_kernel(full_width, chunks, *refs),...  4.92 us
  transfers between devices with their start and end apart: 24, of which 8 were waited for; matrix products, arithmetic and copies ran while one was open for 4% of the time, Pallas kernels for 11%

profile of v2, /device:TPU:1, one launch (start us, length us, event | category | flops | bytes accessed | tf_op | source)
XLA Modules:
  0.0 203.9 jit_solution(10381577783756823270)
XLA Ops:
  0.7 1.2 fusion.1
  1.8 4.5 %collective-permute-start.9 = (bf16[144,1024]{1,0:T(8,128)(2,1)S(1)}, bf16[144,1024]{1,0:T(8,128)(2,1)S(1)}, u32[]{:S(2)}, u32[]{:S(2)}) collective-permute-start(bf16[144,1024]{1,0:T(8,128)(2,1)S(1)} %bitcast.37), channel_id=1, source_target_pairs={{0,32},{4,36},{8,40},{12,44},{16,48},{20,52},{24,56},{28,60},{32,0... | collective-permute-start | bytes 884744 | tf_op jit(solution)/shard_map/ppermute | solution.py:431
  6.7 12.9 %all_to_all.19 = s32[32,1,16]{2,1,0:T(1,128)S(1)} all-to-all(s32[32,1,16]{2,1,0:T(1,128)S(1)} %bitcast.49), channel_id=1, replica_groups=mesh['img'=2,'ctx'=16,'tp'=4] {'img','ctx'}, dimensions={0} | all-to-all | bytes 4096 | tf_op jit(solution)/shard_map/all_to_all | solution.py:449
  19.8 1.2 copy-done.23
  21.0 2.6 %collect.1 = bf16[512,2048]{1,0:T(8,128)(2,1)} custom-call(s32[512,1]{1,0:T(8,128)S(1)} %reshape.59.pos_ref, bf16[512,1024]{1,0:T(8,128)(2,1)S(1)} %copy-done.15, bf16[512,1024]{1,0:T(8,128)(2,1)S(1)} %bitcast.41), custom_call_target="tpu_custom_call" | custom-call | flops 1073741824 | bytes 4194304 | tf_op jit(solution)/shard_map/collect/pallas_call | solution.py:128
  23.6 4.8 %all-to-all-start.1 = ((bf16[32,16,2048]{2,1,0:T(8,128)(2,1)}), bf16[32,16,2048]{2,1,0:T(8,128)(2,1)}, u32[]{:S(2)}, u32[]{:S(2)}) async-start(bf16[32,16,2048]{2,1,0:T(8,128)(2,1)} %bitcast.13), calls=%async_computation.1 | async-start | bytes 4194304 | tf_op jit(solution)/shard_map/all_to_all | solution.py:453
  28.4 2.4 %collective-permute-start.8 = (bf16[144,1024]{1,0:T(8,128)(2,1)S(1)}, bf16[144,1024]{1,0:T(8,128)(2,1)S(1)}, u32[]{:S(2)}, u32[]{:S(2)}) collective-permute-start(bf16[144,1024]{1,0:T(8,128)(2,1)S(1)} %bitcast.38), channel_id=1, source_target_pairs={{0,48},{4,52},{8,56},{12,60},{16,0},{20,4},{24,8},{28,12},{32,16},... | collective-permute-start | bytes 884744 | tf_op jit(solution)/shard_map/ppermute | solution.py:431
  30.8 2.7 %collective-permute-start.2 = (bf16[144,1024]{1,0:T(8,128)(2,1)S(1)}, bf16[144,1024]{1,0:T(8,128)(2,1)}, u32[]{:S(2)}, u32[]{:S(2)}) collective-permute-start(bf16[144,1024]{1,0:T(8,128)(2,1)S(1)} %bitcast.33), channel_id=1, source_target_pairs={{0,8},{4,12},{8,0},{12,4},{16,24},{20,28},{24,16},{28,20},{32,40},... | collective-permute-start | bytes 884744 | tf_op jit(solution)/shard_map/ppermute | solution.py:431
  35.0 22.0 %collective-permute-done.8.refs_2_ = bf16[144,1024]{1,0:T(8,128)(2,1)S(1)} collective-permute-done((bf16[144,1024]{1,0:T(8,128)(2,1)S(1)}, bf16[144,1024]{1,0:T(8,128)(2,1)S(1)}, u32[]{:S(2)}, u32[]{:S(2)}) %collective-permute-start.8) | collective-permute-done | bytes 294944 | tf_op jit(solution)/shard_map/ppermute | solution.py:431
  57.0 3.0 %collective-permute-done.7.refs_1_ = bf16[144,1024]{1,0:T(8,128)(2,1)S(1)} collective-permute-done((bf16[144,1024]{1,0:T(8,128)(2,1)S(1)}, bf16[144,1024]{1,0:T(8,128)(2,1)S(1)}, u32[]{:S(2)}, u32[]{:S(2)}) %collective-permute-start.7) | collective-permute-done | bytes 294944 | tf_op jit(solution)/shard_map/ppermute | solution.py:431
  60.1 2.8 %collective-permute-start.12 = (bf16[576,1024]{1,0:T(8,128)(2,1)S(1)}, bf16[576,1024]{1,0:T(8,128)(2,1)S(1)}, u32[]{:S(2)}, u32[]{:S(2)}) collective-permute-start(bf16[576,1024]{1,0:T(8,128)(2,1)S(1)} %bitcast.23), channel_id=1, source_target_pairs={{0,12},{4,0},{8,4},{12,8},{16,28},{20,16},{24,20},{28,24},{32,44},... | collective-permute-start | bytes 3538952 | tf_op jit(solution)/shard_map/ppermute | solution.py:431
  62.9 1.2 collective-permute-done.1.refs_2_
  65.0 1.2 stack.14
  66.2 2.9 %collective-permute-start.5 = (bf16[576,1024]{1,0:T(8,128)(2,1)S(1)}, bf16[576,1024]{1,0:T(8,128)(2,1)S(1)}, u32[]{:S(2)}, u32[]{:S(2)}) collective-permute-start(bf16[576,1024]{1,0:T(8,128)(2,1)S(1)} %bitcast.27), channel_id=1, source_target_pairs={{0,48},{4,52},{8,56},{12,60},{16,0},{20,4},{24,8},{28,12},{32,16},... | collective-permute-start | bytes 3538952 | tf_op jit(solution)/shard_map/ppermute | solution.py:431
  69.1 20.2 %collective-permute-done.12.refs_7_.refs_6_ = bf16[576,1024]{1,0:T(8,128)(2,1)S(1)} collective-permute-done((bf16[576,1024]{1,0:T(8,128)(2,1)S(1)}, bf16[576,1024]{1,0:T(8,128)(2,1)S(1)}, u32[]{:S(2)}, u32[]{:S(2)}) %collective-permute-start.12) | collective-permute-done | bytes 1179680 | tf_op jit(solution)/shard_map/ppermute | solution.py:431
  90.1 2.4 %collective-permute-start.13 = (bf16[288,1024]{1,0:T(8,128)(2,1)}, bf16[288,1024]{1,0:T(8,128)(2,1)}, u32[]{:S(2)}, u32[]{:S(2)}) collective-permute-start(bf16[288,1024]{1,0:T(8,128)(2,1)} %slice.27), channel_id=1, source_target_pairs={{0,12},{4,0},{8,4},{12,8},{16,28},{20,16},{24,20},{28,24},{32,44},... | collective-permute-start | bytes 1769480 | tf_op jit(solution)/shard_map/ppermute | solution.py:431
  94.3 2.4 %collective-permute-start.6 = (bf16[288,1024]{1,0:T(8,128)(2,1)}, bf16[288,1024]{1,0:T(8,128)(2,1)}, u32[]{:S(2)}, u32[]{:S(2)}) collective-permute-start(bf16[288,1024]{1,0:T(8,128)(2,1)} %slice.25), channel_id=1, source_target_pairs={{0,48},{4,52},{8,56},{12,60},{16,0},{20,4},{24,8},{28,12},{32,16},... | collective-permute-start | bytes 1769480 | tf_op jit(solution)/shard_map/ppermute | solution.py:431
  98.8 1.7 copy-done.19
  101.1 4.5 %layer_norm.1 = (bf16[8,256,576]{2,1,0:T(8,128)(2,1)S(1)}, bf16[4,256,1152]{2,1,0:T(8,128)(2,1)S(1)}, f32[256,128]{1,0:T(8,128)S(1)}) custom-call(bf16[1024,1152]{1,0:T(8,128)(2,1)S(1)} %bitcast.32, bf16[4,1152]{1,0:T(4,128)(2,1)S(1)} %bitcast.42, bf16[4,1152]{1,0:T(4,128)(2,1)S(1)} %bitcast.47), custom_call_target="tpu_custom_call" | custom-call | flops 603979776 | bytes 7077888 | tf_op jit(solution)/shard_map/layer_norm/pallas_call | solution.py:93
  105.6 1.4 copy-done.2
  108.3 1.3 copy-done.11
  109.5 3.2 %multiply.2.refs_6_ = f32[256,1024]{1,0:T(8,128)S(1)} custom-call(s32[2]{0:T(128)S(1)} %pad_add_fusion.refs_0_, bf16[8,256,576]{2,1,0:T(8,128)(2,1)S(1)} %get-tuple-element.14.refs_1_, bf16[576,1024]{1,0:T(8,128)(2,1)S(1)} %bitcast.29, bf16[576,1024]{1,0:T(8,128)(2,1)S(1)} %copy-done.11, bf16[576,1024]{1,0:T(8,128)(2,1)S(1)} %copy-done.8, ...), custom_call_target="tpu_custom_call" | custom-call | flops 1811939328 | bytes 7077888 | tf_op jit(solution)/shard_map/multiply/pallas_call | solution.py:202
  112.7 1.5 copy-done
  116.8 2.3 %unpack.1 = (f32[256,1024]{1,0:T(8,128)S(1)}, f32[256,1024]{1,0:T(8,128)S(1)}) custom-call(s32[256,1]{1,0:T(8,128)S(1)} %copy-done.28, bf16[512,2048]{1,0:T(8,128)(2,1)} %bitcast.14.came_ref, bf16[1,1024]{1,0:T(2,128)(2,1)S(1)} %copy-done.36), custom_call_target="tpu_custom_call" | custom-call | flops 536870912 | bytes 2097152 | tf_op jit(solution)/shard_map/unpack/pallas_call | solution.py:153
  119.3 2.1 %copy-done.1 = bf16[8,256,576]{2,1,0:T(8,128)(2,1)S(1)} copy-done((bf16[8,256,576]{2,1,0:T(8,128)(2,1)S(1)}, bf16[8,256,576]{2,1,0:T(8,128)(2,1)}, u32[]{:S(2)}) %copy-start.1) | copy-done | bytes 2359320
  121.3 2.8 %multiply.3.acc_ref = f32[256,1024]{1,0:T(8,128)S(1)} custom-call(s32[2]{0:T(128)S(1)} %copy-done.34, bf16[8,256,576]{2,1,0:T(8,128)(2,1)S(1)} %copy-done.1, bf16[288,1024]{1,0:T(8,128)(2,1)} %collective-permute-done.4.refs_2_.refs_7_, bf16[288,1024]{1,0:T(8,128)(2,1)} %collective-permute-done.6.refs_3_.refs_8_, ...), custom_call_target="tpu_custom_call" | custom-call | flops 603979776 | bytes 2359296 | tf_op jit(solution)/shard_map/multiply/pallas_call | solution.py:202
  126.4 3.1 %collective-permute-start.14 = (f32[256,128]{1,0:T(8,128)S(1)}, f32[256,128]{1,0:T(8,128)S(1)}, u32[]{:S(2)}, u32[]{:S(2)}) collective-permute-start(f32[256,128]{1,0:T(8,128)S(1)} %get-tuple-element.19), channel_id=1, source_target_pairs={{0,1},{1,0},{2,3},{3,2},{4,5},{5,4},{6,7},{7,6},{8,9},{9,8},{10,11... | collective-permute-start | bytes 393224 | tf_op jit(solution)/shard_map/ppermute | solution.py:478
  131.1 2.4 %collective-permute-start.15 = (f32[256,128]{1,0:T(8,128)}, f32[256,128]{1,0:T(8,128)}, u32[]{:S(2)}, u32[]{:S(2)}) collective-permute-start(f32[256,128]{1,0:T(8,128)} %add.27.refs_3_), channel_id=1, source_target_pairs={{0,2},{1,3},{2,0},{3,1},{4,6},{5,7},{6,4},{7,5},{8,10},{9,11},{10,... | collective-permute-start | bytes 393224 | tf_op jit(solution)/shard_map/ppermute | solution.py:479
  133.6 1.3 copy-done.6
  134.9 1.3 copy-done.9
  136.1 1.3 copy-done.12
  138.0 2.4 %assemble.1 = bf16[8,576,1024]{2,1,0:T(8,128)(2,1)S(1)} custom-call(s32[2]{0:T(128)S(1)} %copy-done.35, bf16[576,1024]{1,0:T(8,128)(2,1)S(1)} %bitcast.30, bf16[576,1024]{1,0:T(8,128)(2,1)S(1)} %copy-done.12, bf16[576,1024]{1,0:T(8,128)(2,1)S(1)} %copy-done.9, bf16[576,1024]{1,0:T(8,128)(2,1)S(1)} %bitcast.26, bf16[576,1024]{1,0:T(8,128)(2,1)S(1)} %copy-done.6, ...), custom_call_target="tpu_custom_call" | custom-call | bytes 18874368 | tf_op jit(solution)/shard_map/assemble/pallas_call | solution.py:273
  140.4 4.9 %backward.1 = (f32[64,4608]{1,0:T(8,128)S(1)}, f32[64,4608]{1,0:T(8,128)S(1)}, bf16[64,4608]{1,0:T(8,128)(2,1)}, bf16[64,4608]{1,0:T(8,128)(2,1)S(1)}) custom-call(s32[1]{0:T(128)} %bitcast.17.refs_0_, f32[256,1024]{1,0:T(8,128)S(1)} %copy-done.25, f32[256,1024]{1,0:T(8,128)S(1)} %copy-done.14, f32[256,128]{1,0:T(8,128)} %add.27.refs_3_, ...), custom_call_target="tpu_custom_call" | custom-call | flops 2415919104 | bytes 9437184 | tf_op jit(solution)/shard_map/backward/pallas_call | solution.py:315
  145.3 1.1 copy-done.22
  147.1 1.4 pack.1
  148.5 6.5 %all-to-all-start.2 = ((bf16[32,16,1024]{2,1,0:T(8,128)(2,1)}), bf16[32,16,1024]{2,1,0:T(8,128)(2,1)S(1)}, u32[]{:S(2)}, u32[]{:S(2)}) async-start(bf16[32,16,1024]{2,1,0:T(8,128)(2,1)} %bitcast.15), calls=%async_computation.2 | async-start | bytes 2097152 | tf_op jit(solution)/shard_map/all_to_all | solution.py:483
  155.4 1.6 add_convert_fusion.1.own_ref
  156.9 1.8 collective-permute-start.17
  158.9 1.3 collective-permute-start.19
  160.2 21.3 %collective-permute-done.17.far_ref = bf16[64,4608]{1,0:T(8,128)(2,1)S(1)} collective-permute-done((bf16[64,4608]{1,0:T(8,128)(2,1)S(1)}, bf16[64,4608]{1,0:T(8,128)(2,1)S(1)}, u32[]{:S(2)}, u32[]{:S(2)}) %collective-permute-start.17) | collective-permute-done | bytes 589856 | tf_op jit(solution)/shard_map/ppermute | solution.py:495
  181.5 1.6 finish.2
  183.1 1.5 collective-permute-start.20
  184.5 9.6 %collective-permute-done.19.far_ref = bf16[64,4608]{1,0:T(8,128)(2,1)S(1)} collective-permute-done((bf16[64,4608]{1,0:T(8,128)(2,1)S(1)}, bf16[64,4608]{1,0:T(8,128)(2,1)S(1)}, u32[]{:S(2)}, u32[]{:S(2)}) %collective-permute-start.19) | collective-permute-done | bytes 589856 | tf_op jit(solution)/shard_map/ppermute | solution.py:495
  194.1 1.5 finish.3
  197.9 1.7 place.1
  199.6 1.1 constant_dynamic-update-slice_fusion.1
  200.7 1.1 constant_dynamic-update-slice_fusion
  202.3 1.6 maximum_bitcast_fusion
  (118 shorter events, 20.5 us)
Async XLA Ops:
  0.6 5.7 %copy-start.39 = (s32[256]{0:T(256)S(1)}, s32[256]{0:T(256)}, u32[]{:S(2)}) copy-start(s32[256]{0:T(256)} %param.15) | copy-start | bytes 3076
  0.6 19.1 %copy-start.15 = (bf16[512,1024]{1,0:T(8,128)(2,1)S(1)}, bf16[512,1024]{1,0:T(8,128)(2,1)}, u32[]{:S(2)}) copy-start(bf16[512,1024]{1,0:T(8,128)(2,1)} %stream_ref.3) | copy-start | bytes 3145732
  1.8 32.6 %copy-start.20 = (bf16[1,2,72,1024]{3,2,1,0:T(8,128)(2,1)}, bf16[1,2,72,1024]{3,2,1,0:T(8,128)(2,1)S(1)}, u32[]{:S(2)}) copy-start(bf16[1,2,72,1024]{3,2,1,0:T(8,128)(2,1)S(1)} %get-tuple-element.31) | copy-start | bytes 884740
  1.8 32.6 %collective-permute-start.9 = (bf16[144,1024]{1,0:T(8,128)(2,1)S(1)}, bf16[144,1024]{1,0:T(8,128)(2,1)S(1)}, u32[]{:S(2)}, u32[]{:S(2)}) collective-permute-start(bf16[144,1024]{1,0:T(8,128)(2,1)S(1)} %bitcast.37), channel_id=1, source_target_pairs={{0,32},{4,36},{8,40},{12,44},{16,48},{20,52},{24,56},{28,60},{32,0... | collective-permute-start | bytes 884744 | tf_op jit(solution)/shard_map/ppermute | solution.py:431
  19.6 4.0 %copy-start.37 = (s32[32,1,16]{2,1,0:T(1,128)}, s32[32,1,16]{2,1,0:T(1,128)S(1)}, u32[]{:S(2)}) copy-start(s32[32,1,16]{2,1,0:T(1,128)S(1)} %all_to_all.19) | copy-start | bytes 6148
  23.6 91.5 %all-to-all-start.1 = ((bf16[32,16,2048]{2,1,0:T(8,128)(2,1)}), bf16[32,16,2048]{2,1,0:T(8,128)(2,1)}, u32[]{:S(2)}, u32[]{:S(2)}) async-start(bf16[32,16,2048]{2,1,0:T(8,128)(2,1)} %bitcast.13), calls=%async_computation.1 | async-start | bytes 4194304 | tf_op jit(solution)/shard_map/all_to_all | solution.py:453
  28.4 28.6 %collective-permute-start.8 = (bf16[144,1024]{1,0:T(8,128)(2,1)S(1)}, bf16[144,1024]{1,0:T(8,128)(2,1)S(1)}, u32[]{:S(2)}, u32[]{:S(2)}) collective-permute-start(bf16[144,1024]{1,0:T(8,128)(2,1)S(1)} %bitcast.38), channel_id=1, source_target_pairs={{0,48},{4,52},{8,56},{12,60},{16,0},{20,4},{24,8},{28,12},{32,16},... | collective-permute-start | bytes 884744 | tf_op jit(solution)/shard_map/ppermute | solution.py:431
  30.8 29.2 %collective-permute-start.7 = (bf16[144,1024]{1,0:T(8,128)(2,1)S(1)}, bf16[144,1024]{1,0:T(8,128)(2,1)S(1)}, u32[]{:S(2)}, u32[]{:S(2)}) collective-permute-start(bf16[144,1024]{1,0:T(8,128)(2,1)S(1)} %bitcast.39), channel_id=1, source_target_pairs={{0,16},{4,20},{8,24},{12,28},{16,32},{20,36},{24,40},{28,44},{32,4... | collective-permute-start | bytes 884744 | tf_op jit(solution)/shard_map/ppermute | solution.py:431
  30.8 32.1 %collective-permute-start.2 = (bf16[144,1024]{1,0:T(8,128)(2,1)S(1)}, bf16[144,1024]{1,0:T(8,128)(2,1)}, u32[]{:S(2)}, u32[]{:S(2)}) collective-permute-start(bf16[144,1024]{1,0:T(8,128)(2,1)S(1)} %bitcast.33), channel_id=1, source_target_pairs={{0,8},{4,12},{8,0},{12,4},{16,24},{20,28},{24,16},{28,20},{32,40},... | collective-permute-start | bytes 884744 | tf_op jit(solution)/shard_map/ppermute | solution.py:431
  33.5 30.6 %collective-permute-start.1 = (bf16[144,1024]{1,0:T(8,128)(2,1)S(1)}, bf16[144,1024]{1,0:T(8,128)(2,1)}, u32[]{:S(2)}, u32[]{:S(2)}) collective-permute-start(bf16[144,1024]{1,0:T(8,128)(2,1)S(1)} %bitcast.34), channel_id=1, source_target_pairs={{0,12},{4,0},{8,4},{12,8},{16,28},{20,16},{24,20},{28,24},{32,44},... | collective-permute-start | bytes 884744 | tf_op jit(solution)/shard_map/ppermute | solution.py:431
  34.4 30.6 %collective-permute-start = (bf16[144,1024]{1,0:T(8,128)(2,1)S(1)}, bf16[144,1024]{1,0:T(8,128)(2,1)}, u32[]{:S(2)}, u32[]{:S(2)}) collective-permute-start(bf16[144,1024]{1,0:T(8,128)(2,1)S(1)} %bitcast.35), channel_id=1, source_target_pairs={{0,4},{4,8},{8,12},{12,0},{16,20},{20,24},{24,28},{28,16},{32,36},... | collective-permute-start | bytes 884744 | tf_op jit(solution)/shard_map/ppermute | solution.py:431
  60.0 5.0 %copy-start.21 = (bf16[1,2,72,1024]{3,2,1,0:T(8,128)(2,1)S(1)}, bf16[1,2,72,1024]{3,2,1,0:T(8,128)(2,1)}, u32[]{:S(2)}) copy-start(bf16[1,2,72,1024]{3,2,1,0:T(8,128)(2,1)} %copy-done.20) | copy-start | bytes 884740
  60.1 29.2 %collective-permute-start.12 = (bf16[576,1024]{1,0:T(8,128)(2,1)S(1)}, bf16[576,1024]{1,0:T(8,128)(2,1)S(1)}, u32[]{:S(2)}, u32[]{:S(2)}) collective-permute-start(bf16[576,1024]{1,0:T(8,128)(2,1)S(1)} %bitcast.23), channel_id=1, source_target_pairs={{0,12},{4,0},{8,4},{12,8},{16,28},{20,16},{24,20},{28,24},{32,44},... | collective-permute-start | bytes 3538952 | tf_op jit(solution)/shard_map/ppermute | solution.py:431
  62.9 29.6 %collective-permute-start.10 = (bf16[576,1024]{1,0:T(8,128)(2,1)S(1)}, bf16[576,1024]{1,0:T(8,128)(2,1)S(1)}, u32[]{:S(2)}, u32[]{:S(2)}) collective-permute-start(bf16[576,1024]{1,0:T(8,128)(2,1)S(1)} %bitcast.24), channel_id=1, source_target_pairs={{0,4},{4,8},{8,12},{12,0},{16,20},{20,24},{24,28},{28,16},{32,36},... | collective-permute-start | bytes 3538952 | tf_op jit(solution)/shard_map/ppermute | solution.py:431
  66.2 27.2 %collective-permute-start.5 = (bf16[576,1024]{1,0:T(8,128)(2,1)S(1)}, bf16[576,1024]{1,0:T(8,128)(2,1)S(1)}, u32[]{:S(2)}, u32[]{:S(2)}) collective-permute-start(bf16[576,1024]{1,0:T(8,128)(2,1)S(1)} %bitcast.27), channel_id=1, source_target_pairs={{0,48},{4,52},{8,56},{12,60},{16,0},{20,4},{24,8},{28,12},{32,16},... | collective-permute-start | bytes 3538952 | tf_op jit(solution)/shard_map/ppermute | solution.py:431
  69.1 27.7 %collective-permute-start.3 = (bf16[576,1024]{1,0:T(8,128)(2,1)S(1)}, bf16[576,1024]{1,0:T(8,128)(2,1)S(1)}, u32[]{:S(2)}, u32[]{:S(2)}) collective-permute-start(bf16[576,1024]{1,0:T(8,128)(2,1)S(1)} %bitcast.28), channel_id=1, source_target_pairs={{0,16},{4,20},{8,24},{12,28},{16,32},{20,36},{24,40},{28,44},{32,4... | collective-permute-start | bytes 3538952 | tf_op jit(solution)/shard_map/ppermute | solution.py:431
  90.1 29.1 %collective-permute-start.13 = (bf16[288,1024]{1,0:T(8,128)(2,1)}, bf16[288,1024]{1,0:T(8,128)(2,1)}, u32[]{:S(2)}, u32[]{:S(2)}) collective-permute-start(bf16[288,1024]{1,0:T(8,128)(2,1)} %slice.27), channel_id=1, source_target_pairs={{0,12},{4,0},{8,4},{12,8},{16,28},{20,16},{24,20},{28,24},{32,44},... | collective-permute-start | bytes 1769480 | tf_op jit(solution)/shard_map/ppermute | solution.py:431
  92.5 1.8 copy-start.4
  93.4 5.3 %copy-start.31 = (bf16[1,4,1152]{2,1,0:T(4,128)(2,1)S(1)}, bf16[1,4,1152]{2,1,0:T(4,128)(2,1)}, u32[]{:S(2)}) copy-start(bf16[1,4,1152]{2,1,0:T(4,128)(2,1)} %param.9) | copy-start | bytes 27652
  93.4 25.8 %collective-permute-start.11 = (bf16[288,1024]{1,0:T(8,128)(2,1)}, bf16[288,1024]{1,0:T(8,128)(2,1)}, u32[]{:S(2)}, u32[]{:S(2)}) collective-permute-start(bf16[288,1024]{1,0:T(8,128)(2,1)} %slice.26), channel_id=1, source_target_pairs={{0,4},{4,8},{8,12},{12,0},{16,20},{20,24},{24,28},{28,16},{32,36},... | collective-permute-start | bytes 1769480 | tf_op jit(solution)/shard_map/ppermute | solution.py:431
  93.5 4.2 %copy-start.7 = (bf16[576,1024]{1,0:T(8,128)(2,1)}, bf16[576,1024]{1,0:T(8,128)(2,1)S(1)}, u32[]{:S(2)}) copy-start(bf16[576,1024]{1,0:T(8,128)(2,1)S(1)} %collective-permute-done.5.refs_4_.refs_3_) | copy-start | bytes 3538948
  94.3 24.9 %collective-permute-start.6 = (bf16[288,1024]{1,0:T(8,128)(2,1)}, bf16[288,1024]{1,0:T(8,128)(2,1)}, u32[]{:S(2)}, u32[]{:S(2)}) collective-permute-start(bf16[288,1024]{1,0:T(8,128)(2,1)} %slice.25), channel_id=1, source_target_pairs={{0,48},{4,52},{8,56},{12,60},{16,0},{20,4},{24,8},{28,12},{32,16},... | collective-permute-start | bytes 1769480 | tf_op jit(solution)/shard_map/ppermute | solution.py:431
  97.7 21.5 %collective-permute-start.4 = (bf16[288,1024]{1,0:T(8,128)(2,1)}, bf16[288,1024]{1,0:T(8,128)(2,1)}, u32[]{:S(2)}, u32[]{:S(2)}) collective-permute-start(bf16[288,1024]{1,0:T(8,128)(2,1)} %slice.24), channel_id=1, source_target_pairs={{0,16},{4,20},{8,24},{12,28},{16,32},{20,36},{24,40},{28,44},{32,4... | collective-permute-start | bytes 1769480 | tf_op jit(solution)/shard_map/ppermute | solution.py:431
  98.8 1.7 copy-start.19
  101.1 7.1 %copy-start.5 = (bf16[576,1024]{1,0:T(8,128)(2,1)S(1)}, bf16[576,1024]{1,0:T(8,128)(2,1)}, u32[]{:S(2)}) copy-start(bf16[576,1024]{1,0:T(8,128)(2,1)} %copy-done.4) | copy-start | bytes 3538948
  101.1 7.1 %copy-start.8 = (bf16[576,1024]{1,0:T(8,128)(2,1)S(1)}, bf16[576,1024]{1,0:T(8,128)(2,1)}, u32[]{:S(2)}) copy-start(bf16[576,1024]{1,0:T(8,128)(2,1)} %copy-done.7) | copy-start | bytes 3538948
  105.6 1.4 copy-start.2
  112.7 1.5 copy-start
  115.2 4.1 %copy-start.18 = (f32[256,1024]{1,0:T(8,128)S(1)}, f32[256,1024]{1,0:T(8,128)}, u32[]{:S(2)}) copy-start(f32[256,1024]{1,0:T(8,128)} %copy-done.17) | copy-start | bytes 3145732
  116.8 2.4 %copy-start.34 = (s32[2]{0:T(128)S(1)}, s32[2]{0:T(128)}, u32[]{:S(2)}) copy-start(s32[2]{0:T(128)} %copy-done.33) | copy-start | bytes 28
  119.2 5.0 %copy-start.13 = (f32[256,1024]{1,0:T(8,128)}, f32[256,1024]{1,0:T(8,128)S(1)}, u32[]{:S(2)}) copy-start(f32[256,1024]{1,0:T(8,128)S(1)} %get-tuple-element.16.up_ref.refs_2_) | copy-start | bytes 3145732
  119.3 2.1 %copy-start.1 = (bf16[8,256,576]{2,1,0:T(8,128)(2,1)S(1)}, bf16[8,256,576]{2,1,0:T(8,128)(2,1)}, u32[]{:S(2)}) copy-start(bf16[8,256,576]{2,1,0:T(8,128)(2,1)} %copy-done) | copy-start | bytes 7077892
  126.4 4.1 %collective-permute-start.14 = (f32[256,128]{1,0:T(8,128)S(1)}, f32[256,128]{1,0:T(8,128)S(1)}, u32[]{:S(2)}, u32[]{:S(2)}) collective-permute-start(f32[256,128]{1,0:T(8,128)S(1)} %get-tuple-element.19), channel_id=1, source_target_pairs={{0,1},{1,0},{2,3},{3,2},{4,5},{5,4},{6,7},{7,6},{8,9},{9,8},{10,11... | collective-permute-start | bytes 393224 | tf_op jit(solution)/shard_map/ppermute | solution.py:478
  131.1 9.2 %collective-permute-start.15 = (f32[256,128]{1,0:T(8,128)}, f32[256,128]{1,0:T(8,128)}, u32[]{:S(2)}, u32[]{:S(2)}) collective-permute-start(f32[256,128]{1,0:T(8,128)} %add.27.refs_3_), channel_id=1, source_target_pairs={{0,2},{1,3},{2,0},{3,1},{4,6},{5,7},{6,4},{7,5},{8,10},{9,11},{10,... | collective-permute-start | bytes 393224 | tf_op jit(solution)/shard_map/ppermute | solution.py:479
  138.0 2.4 %copy-start.14 = (f32[256,1024]{1,0:T(8,128)S(1)}, f32[256,1024]{1,0:T(8,128)}, u32[]{:S(2)}) copy-start(f32[256,1024]{1,0:T(8,128)} %copy-done.13) | copy-start | bytes 3145732
  138.0 2.4 %copy-start.25 = (f32[256,1024]{1,0:T(8,128)S(1)}, f32[256,1024]{1,0:T(8,128)}, u32[]{:S(2)}) copy-start(f32[256,1024]{1,0:T(8,128)} %copy-done.24) | copy-start | bytes 3145732
  140.4 6.6 %copy-start.30 = (bf16[256,1024]{1,0:T(8,128)(2,1)S(1)}, bf16[256,1024]{1,0:T(8,128)(2,1)}, u32[]{:S(2)}) copy-start(bf16[256,1024]{1,0:T(8,128)(2,1)} %copy-done.29) | copy-start | bytes 1572868
  146.4 9.0 %collective-permute-start.16 = (bf16[64,4608]{1,0:T(8,128)(2,1)}, bf16[64,4608]{1,0:T(8,128)(2,1)}, u32[]{:S(2)}, u32[]{:S(2)}) collective-permute-start(bf16[64,4608]{1,0:T(8,128)(2,1)} %get-tuple-element.21), channel_id=1, source_target_pairs={{0,1},{1,0},{2,3},{3,2},{4,5},{5,4},{6,7},{7,6},{8,9},{9,8},{10,11... | collective-permute-start | bytes 1769480 | tf_op jit(solution)/shard_map/ppermute | solution.py:493
  148.5 49.4 %all-to-all-start.2 = ((bf16[32,16,1024]{2,1,0:T(8,128)(2,1)}), bf16[32,16,1024]{2,1,0:T(8,128)(2,1)S(1)}, u32[]{:S(2)}, u32[]{:S(2)}) async-start(bf16[32,16,1024]{2,1,0:T(8,128)(2,1)} %bitcast.15), calls=%async_computation.2 | async-start | bytes 2097152 | tf_op jit(solution)/shard_map/all_to_all | solution.py:483
  155.0 3.7 %collective-permute-start.18 = (bf16[64,4608]{1,0:T(8,128)(2,1)S(1)}, bf16[64,4608]{1,0:T(8,128)(2,1)S(1)}, u32[]{:S(2)}, u32[]{:S(2)}) collective-permute-start(bf16[64,4608]{1,0:T(8,128)(2,1)S(1)} %get-tuple-element.25), channel_id=1, source_target_pairs={{0,1},{1,0},{2,3},{3,2},{4,5},{5,4},{6,7},{7,6},{8,9},{9,8},{10,11... | collective-permute-start | bytes 1769480 | tf_op jit(solution)/shard_map/ppermute | solution.py:493
  155.4 26.1 %copy-start.27 = (f32[256,128]{1,0:T(8,128)S(1)}, f32[256,128]{1,0:T(8,128)}, u32[]{:S(2)}) copy-start(f32[256,128]{1,0:T(8,128)} %copy-done.26) | copy-start | bytes 393220
  156.9 24.6 %collective-permute-start.17 = (bf16[64,4608]{1,0:T(8,128)(2,1)S(1)}, bf16[64,4608]{1,0:T(8,128)(2,1)S(1)}, u32[]{:S(2)}, u32[]{:S(2)}) collective-permute-start(bf16[64,4608]{1,0:T(8,128)(2,1)S(1)} %add_convert_fusion.1.own_ref), channel_id=1, source_target_pairs={{0,2},{1,3},{2,0},{3,1},{4,6},{5,7},{6,4},{7,5},{8,10},{9,11},{10,... | collective-permute-start | bytes 1769480 | tf_op jit(solution)/shard_map/ppermute | solution.py:495
  158.8 22.7 %copy-start.3 = (bf16[4,256,1152]{2,1,0:T(8,128)(2,1)S(1)}, bf16[4,256,1152]{2,1,0:T(8,128)(2,1)}, u32[]{:S(2)}) copy-start(bf16[4,256,1152]{2,1,0:T(8,128)(2,1)} %copy-done.2) | copy-start | bytes 7077892
  158.9 35.2 %collective-permute-start.19 = (bf16[64,4608]{1,0:T(8,128)(2,1)S(1)}, bf16[64,4608]{1,0:T(8,128)(2,1)S(1)}, u32[]{:S(2)}, u32[]{:S(2)}) collective-permute-start(bf16[64,4608]{1,0:T(8,128)(2,1)S(1)} %add_convert_fusion.own_ref), channel_id=1, source_target_pairs={{0,2},{1,3},{2,0},{3,1},{4,6},{5,7},{6,4},{7,5},{8,10},{9,11},{10,... | collective-permute-start | bytes 1769480 | tf_op jit(solution)/shard_map/ppermute | solution.py:495
  183.1 16.5 %collective-permute-start.20 = (bf16[256,1152]{1,0:T(8,128)(2,1)S(1)}, bf16[256,1152]{1,0:T(8,128)(2,1)}, u32[]{:S(2)}, u32[]{:S(2)}) collective-permute-start(bf16[256,1152]{1,0:T(8,128)(2,1)S(1)} %finish.2), channel_id=1, source_target_pairs={{0,1},{1,0},{2,3},{3,2},{4,5},{5,4},{6,7},{7,6},{8,9},{9,8},{10,11... | collective-permute-start | bytes 1769480 | tf_op jit(solution)/shard_map/ppermute | solution.py:498
  184.5 12.5 %copy-start.38 = (s32[32,1,16]{2,1,0:T(1,128)S(1)}, s32[32,1,16]{2,1,0:T(1,128)}, u32[]{:S(2)}) copy-start(s32[32,1,16]{2,1,0:T(1,128)} %copy-done.37) | copy-start | bytes 6148
  184.5 13.3 %copy-start.16 = (bf16[512,1024]{1,0:T(8,128)(2,1)S(1)}, bf16[512,1024]{1,0:T(8,128)(2,1)}, u32[]{:S(2)}) copy-start(bf16[512,1024]{1,0:T(8,128)(2,1)} %stream_ref.3) | copy-start | bytes 3145732
  195.7 5.0 %collective-permute-start.21 = (bf16[256,1152]{1,0:T(8,128)(2,1)S(1)}, bf16[256,1152]{1,0:T(8,128)(2,1)}, u32[]{:S(2)}, u32[]{:S(2)}) collective-permute-start(bf16[256,1152]{1,0:T(8,128)(2,1)S(1)} %finish.3), channel_id=1, source_target_pairs={{0,1},{1,0},{2,3},{3,2},{4,5},{5,4},{6,7},{7,6},{8,9},{9,8},{10,11... | collective-permute-start | bytes 1769480 | tf_op jit(solution)/shard_map/ppermute | solution.py:498
  (16 other events, 15.5 us)

commit v3 on v2

--- a/solution.py
+++ b/solution.py
@@ -42,17 +42,20 @@
 
 
 SIDE = 4
+HALVES = 4 * SIDE
 
 
 def piece_slices(window, share):
     half = window // 2
     pieces = []
-    for first in range(SIDE):
-        pieces.append([(w, (first * SIDE + y) * share) for y in range(SIDE) for w in range(half)])
-    for first in range(SIDE):
-        pieces.append(
-            [(w, (z * SIDE + first) * share) for z in range(SIDE) for w in range(half, window)]
-        )
+    for part in range(2):
+        for first in range(SIDE):
+            for side in range(2):
+                piece = []
+                for second in (2 * side, 2 * side + 1):
+                    ctx = first * SIDE + second if part == 0 else second * SIDE + first
+                    piece += [(w, ctx * share) for w in range(part * half, part * half + half)]
+                pieces.append(piece)
     return pieces
 
 
@@ -89,7 +92,7 @@
     window = gain.shape[0]
     merged = rows // window
     block = 64
-    piece = window * width // (2 * SIDE)
+    piece = window * width // HALVES
     return pl.pallas_call(
         norm_kernel,
         grid=(merged // block,),
@@ -99,16 +102,16 @@
             pl.BlockSpec((window, width), lambda i: (0, 0)),
         ],
         out_specs=[
-            pl.BlockSpec((2 * SIDE, block, piece), lambda i: (0, i, 0)),
+            pl.BlockSpec((HALVES, block, piece), lambda i: (0, i, 0)),
             pl.BlockSpec((window, block, width), lambda i: (0, i, 0)),
             pl.BlockSpec((block, 128), lambda i: (i, 0)),
         ],
         out_shape=[
-            jax.ShapeDtypeStruct((2 * SIDE, merged, piece), BF),
+            jax.ShapeDtypeStruct((HALVES, merged, piece), BF),
             jax.ShapeDtypeStruct((window, merged, width), BF),
             jax.ShapeDtypeStruct((merged, 128), F32),
         ],
-        compiler_params=params(24),
+        compiler_params=params(12),
         cost_estimate=cost(2 * rows * block * window * width, 6 * rows * width),
         name="layer_norm",
     )(features, gain, bias)
@@ -130,7 +133,7 @@
         in_specs=[whole()] * 3,
         out_specs=whole(),
         out_shape=jax.ShapeDtypeStruct((slots, 2 * width), BF),
-        compiler_params=params(24),
+        compiler_params=params(12),
         cost_estimate=cost(4 * slots * rows * width, 8 * rows * width),
         name="collect",
     )(pos, stream, cot)
@@ -155,96 +158,111 @@
         in_specs=[whole()] * 3,
         out_specs=[whole()] * 2,
         out_shape=[jax.ShapeDtypeStruct((tokens, width), F32)] * 2,
-        compiler_params=params(16),
+        compiler_params=params(12),
         cost_estimate=cost(4 * slots * tokens * width, 8 * tokens * width),
         name="unpack",
     )(slot_col, came, ngain)
 
 
 def stack_kernel(me_ref, *refs):
-    out_ref = refs[-1]
     me = me_ref[0]
-    for away, ref in zip((0, SIDE - 1, 1, 2), refs[:-1]):
-        out_ref[lax.rem(me + away, SIDE)] = ref[...]
+    for away, ref in zip((0, SIDE - 1, 1, 2), refs[:SIDE]):
+        place = lax.rem(me + away, SIDE)
+        for side in range(2):
+
+            @pl.when(place // 2 == side)
+            def _():
+                refs[SIDE + side][lax.rem(place, 2)] = ref[...]
 
 
 def stack(me, blocks):
     rows, width = blocks[0].shape
-    return pl.pallas_call(
+    halves = pl.pallas_call(
         stack_kernel,
-        in_specs=[pl.BlockSpec(memory_space=SMEM)] + [whole()] * 4,
-        out_specs=whole(),
-        out_shape=jax.ShapeDtypeStruct((SIDE, rows, width), BF),
-        compiler_params=params(8),
+        in_specs=[pl.BlockSpec(memory_space=SMEM)] + [whole()] * SIDE,
+        out_specs=[whole()] * 2,
+        out_shape=[jax.ShapeDtypeStruct((2, rows, width), BF)] * 2,
+        compiler_params=params(6),
         cost_estimate=cost(0, 16 * rows * width),
         name="stack",
     )(me, *blocks)
-
-
-def multiply_kernel(plan, count, zy_ref, lifted_ref, *refs):
+    return [h.reshape(2 * rows, width) for h in halves]
+
+
+def place_of(zy_ref, entry):
+    part, away, side = entry
+    return part * 2 * SIDE + 2 * lax.rem(zy_ref[part] + away, SIDE) + side
+
+
+def product(plan, zy_ref, lifted_ref, refs):
     total = None
-    if len(refs) > count + 1:
-        total = refs[count][...]
-    for (axis, away, start, stop), ref in zip(plan, refs[:count]):
-        index = axis * SIDE + lax.rem(zy_ref[axis] + away, SIDE)
-        rows = ref.shape[0]
-        left = lifted_ref[index][:, start:stop]
-        part = jnp.dot(left, ref[...], preferred_element_type=F32)
+    for entry, ref in zip(plan, refs):
+        part = jnp.dot(
+            lifted_ref[place_of(zy_ref, entry)], ref[...], preferred_element_type=F32
+        )
         total = part if total is None else total + part
-    refs[-1][...] = total
-
-
-def multiply(zy, lifted, pieces, plan, before=None):
+    return total
+
+
+def multiply_kernel(plan, zy_ref, lifted_ref, *refs):
+    refs[-1][...] = product(plan, zy_ref, lifted_ref, refs[:-1])
+
+
+def multiply(zy, lifted, pieces, plan):
     tokens = lifted.shape[1]
     width = pieces[0].shape[1]
-    extra = [] if before is None else [before]
     depth = sum(p.shape[0] for p in pieces)
     return pl.pallas_call(
-        lambda *refs: multiply_kernel(plan, len(pieces), *refs),
-        in_specs=[pl.BlockSpec(memory_space=SMEM)] + [whole()] * (1 + len(pieces) + len(extra)),
+        lambda *refs: multiply_kernel(plan, *refs),
+        in_specs=[pl.BlockSpec(memory_space=SMEM)] + [whole()] * (1 + len(pieces)),
         out_specs=whole(),
         out_shape=jax.ShapeDtypeStruct((tokens, width), F32),
-        compiler_params=params(24),
+        compiler_params=params(16),
         cost_estimate=cost(2 * depth * tokens * width, 2 * depth * width),
         name="multiply",
-    )(zy, lifted, *pieces, *extra)
-
-
-def merge_kernel(acc_ref, base_ref, up_ref, visual_ref, state_ref, stat_ref):
-    visual = acc_ref[...].astype(BF)
+    )(zy, lifted, *pieces)
+
+
+def merge_kernel(plan, zy_ref, lifted_ref, *refs):
+    acc_ref, base_ref, up_ref, visual_ref, state_ref, stat_ref = refs[len(plan) :]
+    total = acc_ref[...] + product(plan, zy_ref, lifted_ref, refs[: len(plan)])
+    visual = total.astype(BF)
     visual_ref[...] = visual
     state = base_ref[...] + visual.astype(F32)
     state_ref[...] = state
-    lane = lax.broadcasted_iota(jnp.int32, stat_ref.shape, 1)
-    stat_ref[...] = jnp.where(
+    lane = lax.broadcasted_iota(jnp.int32, (state.shape[0], 128), 1)
+    sums = jnp.where(
         lane == 0,
         jnp.sum(state * state, axis=1, keepdims=True),
         jnp.sum(up_ref[...] * state, axis=1, keepdims=True),
     )
-
-
-def merge(acc, base, up):
+    stat_ref[...] = sums.T[: stat_ref.shape[0]]
+
+
+def merge(zy, lifted, pieces, plan, acc, base, up):
     tokens, width = acc.shape
-    return pl.pallas_call(
-        merge_kernel,
-        in_specs=[whole()] * 3,
+    depth = sum(p.shape[0] for p in pieces)
+    return pl.pallas_call(
+        lambda *refs: merge_kernel(plan, *refs),
+        in_specs=[pl.BlockSpec(memory_space=SMEM)] + [whole()] * (4 + len(pieces)),
         out_specs=[whole()] * 3,
         out_shape=[
             jax.ShapeDtypeStruct((tokens, width), BF),
             jax.ShapeDtypeStruct((tokens, width), F32),
-            jax.ShapeDtypeStruct((tokens, 128), F32),
+            jax.ShapeDtypeStruct((8, tokens), F32),
         ],
         compiler_params=params(16),
-        cost_estimate=cost(8 * tokens * width, 18 * tokens * width),
+        cost_estimate=cost(2 * depth * tokens * width, 18 * tokens * width),
         name="merge",
-    )(acc, base, up)
-
-
-def pack_kernel(slot_ref, visual_ref, out_ref):
-    slots = out_ref.shape[0]
+    )(zy, lifted, *pieces, acc, base, up)
+
+
+def pack_kernel(slot_ref, visual_ref, stay_ref, cross_ref):
     tokens = visual_ref.shape[0]
-    put = eq_hot((slots, tokens), 0, slot_ref[...])
-    out_ref[...] = jnp.dot(put, visual_ref[...], preferred_element_type=F32).astype(BF)
+    slots = stay_ref.shape[0]
+    for shift, out_ref in ((0, stay_ref), (slots, cross_ref)):
+        put = eq_hot((slots, tokens), 0, slot_ref[...] - shift)
+        out_ref[...] = jnp.dot(put, visual_ref[...], preferred_element_type=F32).astype(BF)
 
 
 def pack(slot_row, visual, slots):
@@ -252,44 +270,42 @@
     return pl.pallas_call(
         pack_kernel,
         in_specs=[whole()] * 2,
-        out_specs=whole(),
-        out_shape=jax.ShapeDtypeStruct((slots, width), BF),
-        compiler_params=params(16),
+        out_specs=[whole()] * 2,
+        out_shape=[jax.ShapeDtypeStruct((slots // 2, width), BF)] * 2,
+        compiler_params=params(8),
         cost_estimate=cost(2 * slots * tokens * width, 2 * (slots + tokens) * width),
         name="pack",
     )(slot_row, visual)
 
 
 def assemble_kernel(plan, zy_ref, *refs):
-    out_ref = refs[-1]
-    for (axis, away, start, stop), ref in zip(plan, refs[:-1]):
-        index = axis * SIDE + lax.rem(zy_ref[axis] + away, SIDE)
-        out_ref[index, start:stop, :] = ref[...]
+    for entry, ref in zip(plan, refs[:-1]):
+        refs[-1][place_of(zy_ref, entry)] = ref[...]
 
 
 def assemble(zy, pieces, plan):
-    depth = sum(p.shape[0] for p in pieces)
-    width = pieces[0].shape[1]
+    rows, width = pieces[0].shape
     return pl.pallas_call(
         lambda *refs: assemble_kernel(plan, *refs),
         in_specs=[pl.BlockSpec(memory_space=SMEM)] + [whole()] * len(pieces),
         out_specs=whole(),
-        out_shape=jax.ShapeDtypeStruct((2 * SIDE, depth // (2 * SIDE), width), BF),
-        compiler_params=params(32),
-        cost_estimate=cost(0, 4 * depth * width),
+        out_shape=jax.ShapeDtypeStruct((HALVES, rows, width), BF),
+        compiler_params=params(22),
+        cost_estimate=cost(0, 4 * HALVES * rows * width),
         name="assemble",
     )(zy, *pieces)
 
 
 def backward_kernel(full_width, chunks, core_ref, state_ref, up_ref, stat_a_ref, stat_b_ref, w_ref, *refs):
-    picked_ref = refs[-1]
+    picked_ref, sums_ref = refs[-2:]
     tokens = state_ref.shape[0]
     half = tokens // 2
     rows = half // chunks
     core = core_ref[0]
+    sums_ref[...] = (stat_a_ref[...] + stat_b_ref[...]).T
     for place, owner in enumerate((core, 1 - core)):
         at = pl.ds(pl.multiple_of(owner * half, half), half)
-        sums = stat_a_ref[at, :] + stat_b_ref[at, :]
+        sums = sums_ref[at, :]
         inv = lax.rsqrt(sums[:, 0:1] / full_width + 1e-06)
         inner = sums[:, 1:2] / full_width
         grad = inv * up_ref[at, :] - state_ref[at, :] * (inv * inv * inv * inner)
@@ -318,8 +334,8 @@
         out_specs=[whole()] * (2 * chunks),
         out_shape=[jax.ShapeDtypeStruct((rows, depth), F32)] * chunks
         + [jax.ShapeDtypeStruct((rows, depth), BF)] * chunks,
-        scratch_shapes=[pltpu.VMEM((tokens, width), BF)],
-        compiler_params=params(32),
+        scratch_shapes=[pltpu.VMEM((tokens, width), BF), pltpu.VMEM((tokens, 8), F32)],
+        compiler_params=params(22),
         cost_estimate=cost(2 * depth * tokens * width, 2 * depth * width),
         name="backward",
     )(core, state, up, stat_a, stat_b, weight)
@@ -329,7 +345,7 @@
     window, tokens, width = xw_ref.shape
     full = window * width
     share = width // (SIDE * SIDE)
-    piece = full // (2 * SIDE)
+    piece = full // HALVES
     mean = stat_ref[:, 0:1]
     inv = stat_ref[:, 1:2]
     lifted = own_ref[...].astype(F32) + far_ref[...].astype(F32)
@@ -376,7 +392,7 @@
             out_specs=pl.BlockSpec((tokens * window, width), lambda i, b: (0, 0)),
         ),
         out_shape=jax.ShapeDtypeStruct((tokens * window, width), BF),
-        compiler_params=params(24),
+        compiler_params=params(12),
         cost_estimate=cost(2 * (tokens * window) ** 2 * width, 8 * window * tokens * width),
         name="finish",
     )(block, own, far, xw, stat, gain)
@@ -398,10 +414,39 @@
         in_specs=[whole()] * 3,
         out_specs=whole(),
         out_shape=jax.ShapeDtypeStruct((rows, width), BF),
-        compiler_params=params(16),
+        compiler_params=params(12),
         cost_estimate=cost(2 * came.shape[0] * rows * width, 6 * rows * width),
         name="place",
     )(pos, came, stream)
+
+
+def lay_kernel(core_ref, *refs):
+    out_ref, sems = refs[-2:]
+    chunks = (len(refs) - 2) // 2
+    rows = refs[0].shape[0]
+    copies = []
+    for index, ref in enumerate(refs[:-2]):
+        owner = core_ref[0] if index < chunks else 1 - core_ref[0]
+        start = pl.multiple_of((owner * chunks + index % chunks) * rows, rows)
+        copies.append(pltpu.make_async_copy(ref, out_ref.at[pl.ds(start, rows)], sems.at[index]))
+    for copy in copies:
+        copy.start()
+    for copy in copies:
+        copy.wait()
+
+
+def lay(core, blocks):
+    rows, width = blocks[0].shape
+    return pl.pallas_call(
+        lay_kernel,
+        in_specs=[pl.BlockSpec(memory_space=SMEM)] + [whole()] * len(blocks),
+        out_specs=pl.BlockSpec(memory_space=pl.ANY),
+        out_shape=jax.ShapeDtypeStruct((len(blocks) * rows, width), BF),
+        scratch_shapes=[pltpu.SemaphoreType.DMA((len(blocks),))],
+        compiler_params=params(6),
+        cost_estimate=cost(0, 4 * len(blocks) * rows * width),
+        name="lay",
+    )(core, *blocks)
 
 
 def shards(features, ln_gain, ln_bias, projection, stream, norm_gain, cotangent, slots):
@@ -449,6 +494,12 @@
     asked = lax.all_to_all(
         packed.reshape(owners, capacity), ("img", "ctx"), split_axis=0, concat_axis=0, tiled=True
     )
+    asked, first_a, first_b = lax.optimization_barrier((asked, first_a, first_b))
+
+    halves = [stack(zy[1:], first_a), stack(zy[:1], first_b)]
+    before = [[moved(h, part, 1) for h in halves[part]] for part in range(2)]
+    after = [[moved(h, part, -1) for h in halves[part]] for part in range(2)]
+
     held = collect(asked.reshape(slot_count, 1), stream, cotangent[0])
     came = lax.all_to_all(
         held.reshape(owners, capacity, 2 * width),
@@ -457,49 +508,57 @@
 
     gain = ln_gain[0]
     lifted, xw, stat = layer_norm(features[0], gain, ln_bias[0])
-
-    stack_a = stack(zy[1:], first_a).reshape(SIDE * half * share, width)
-    stack_b = stack(zy[:1], first_b).reshape(SIDE * half * share, width)
+    lifted, before, after = lax.optimization_barrier((lifted, before, after))
+
     pieces, plan, far_pieces, far_plan = [], [], [], []
-    for axis, block in ((0, stack_a), (1, stack_b)):
-        rows = block.shape[0]
-        before = moved(block, axis, 1)
-        after = moved(block, axis, -1)
-        pieces += [block, before, after]
-        plan += [(axis, 0, 0, rows), (axis, SIDE - 1, 0, rows), (axis, 1, 0, rows)]
-        far_pieces += [moved(before[: rows // 2], axis, 1), moved(after[rows // 2 :], axis, -1)]
-        far_plan += [(axis, 2, 0, rows // 2), (axis, 2, rows // 2, rows)]
-
+    for part in range(2):
+        for away, sides in ((0, halves[part]), (SIDE - 1, before[part]), (1, after[part])):
+            pieces += sides
+            plan += [(part, away, 0), (part, away, 1)]
+        far_pieces += [moved(before[part][0], part, 1), moved(after[part][1], part, -1)]
+        far_plan += [(part, 2, 0), (part, 2, 1)]
+
+    acc = multiply(zy, lifted, pieces, plan)
     base, up = unpack(slot.reshape(merged, 1), came, norm_gain)
-    acc = multiply(zy, lifted, pieces, plan)
-    acc = multiply(zy, lifted, far_pieces, far_plan, acc)
-    visual, state, sums = merge(acc, base, up)
+    visual, state, sums = merge(zy, lifted, far_pieces, far_plan, acc, base, up)
 
     near = sums + lax.ppermute(sums, "tp", core_pairs)
     far = lax.ppermute(near, "tp", far_pairs)
     weight = assemble(zy, pieces + far_pieces, plan + far_plan).reshape(-1, width)
 
-    send = pack(slot.reshape(1, merged), visual, slot_count)
-    arrived = lax.all_to_all(
-        send.reshape(owners, capacity, width),
-        ("img", "ctx"), split_axis=0, concat_axis=0, tiled=True,
-    ).reshape(slot_count, width)
-    new_stream = place(asked.reshape(1, slot_count), arrived, stream)
+    img = lax.axis_index("img").astype(jnp.int32)
+    in_img = slot_count // n_img
+    relative = lax.rem(slot + img * in_img, slot_count)
+    stay, cross = pack(relative.reshape(1, merged), visual, slot_count)
+    crossed = lax.ppermute(cross, "img", [(i, 1 - i) for i in range(n_img)])
 
     chunks = 2
     parts = backward(core, state, up, near, far, weight, chunks, full_width)
+    pairs = []
+    for chunk in range(chunks):
+        got = lax.ppermute(parts[chunks + chunk], "tp", core_pairs)
+        pairs.append((parts[chunk] + got.astype(F32)).astype(BF))
+    beyond = [lax.ppermute(pair, "tp", far_pairs) for pair in pairs]
+
+    stay, crossed, pairs[0] = lax.optimization_barrier((stay, crossed, pairs[0]))
+    send = jnp.concatenate(
+        [x.reshape(n_ctx, capacity, width) for x in (stay, crossed)], axis=1
+    )
+    arrived = lax.all_to_all(send, "ctx", split_axis=0, concat_axis=0, tiled=True)
+    by_img = jnp.stack([
+        lax.dynamic_index_in_dim(asked.reshape(n_img, n_ctx, capacity), i, 0, keepdims=False)
+        for i in (img, 1 - img)
+    ], axis=1)
+    new_stream = place(
+        by_img.reshape(1, slot_count), arrived.reshape(slot_count, width), stream
+    )
+
     own_out, got_out = [], []
     for chunk in range(chunks):
-        got = lax.ppermute(parts[chunks + chunk], "tp", core_pairs)
-        pair = (parts[chunk] + got.astype(F32)).astype(BF)
-        beyond = lax.ppermute(pair, "tp", far_pairs)
-        out = finish(core * chunks + chunk, pair, beyond, xw, stat, gain)
+        out = finish(core * chunks + chunk, pairs[chunk], beyond[chunk], xw, stat, gain)
         own_out.append(out)
         got_out.append(lax.ppermute(out, "tp", core_pairs))
-    first = core[0] == 0
-    own = jnp.concatenate(own_out, axis=0)
-    got = jnp.concatenate(got_out, axis=0)
-    grad = jnp.concatenate([jnp.where(first, own, got), jnp.where(first, got, own)], axis=0)
+    grad = lay(core, own_out + got_out)
     return (new_stream, grad[None])
 
 

time: 205 us -> 204 us (level)
  waiting for transfers between devices: 79.2 us -> 65.2 us
  Pallas kernels: 30.6 us -> 38 us
  starting transfers between devices: 44.9 us -> 48.7 us
  blocking collectives: 12.9 us -> 15.5 us
  other arithmetic: 5.45 us -> 3.21 us
    ppermute x2 -> x3, waiting for transfers between devices: 30.9 us -> 23.3 us  [the longest x2 15 us: shards(): beyond = [lax.ppermute(pair, 'tp', far_pairs) for pair in pairs]]
    ppermute x14 -> x18, waiting for transfers between devices: 47.3 us -> 39.8 us  [moved(): return lax.ppermute(array, 'ctx', pairs)]
    unnamed x81 -> x86, local copies, waits for them, and re-layouts: 22.3 us -> 29.7 us
    ppermute x14 -> x18, starting transfers between devices: 21.6 us -> 27.6 us  [moved(): return lax.ppermute(array, 'ctx', pairs)]
    pallas_call x4, Pallas kernels: 7.84 us -> 11.9 us  [the longest x1 5.2 us: multiply(): pl.pallas_call(lambda *refs: multiply_kernel(plan, *refs), in_specs=[pl.B...]
    slice x4 -> x0, local copies, waits for them, and re-layouts: 3.56 us -> none  [the longest x2 1.85 us: shards(): before[:rows // 2]]
    pallas_call x2, Pallas kernels: 3.1 us -> 5.97 us  [finish(): pl.pallas_call(finish_kernel, grid_spec=pltpu.PrefetchScalarGridSpec(num_...]
    all_to_all x1, blocking collectives: 12.9 us -> 15.5 us  [shards(): lax.all_to_all(packed.reshape(owners, capacity), ('img', 'ctx'), split_ax...]
  transfers between devices with their start and end apart: 24 -> 29, of which waited for: 8 -> 10; matrix products, arithmetic and copies ran while one was open for 4% -> 2% of each run, Pallas kernels for 11% -> 13%
where the time goes in v3:
time: 204 us; the launch traced here: 203 us
  waiting for transfers between devices  65.2 us (32%)
  starting transfers between devices  48.7 us (24%)
  Pallas kernels  38 us (19%)
  local copies, waits for them, and re-layouts  31.3 us (15%)
  blocking collectives  15.5 us (8%)
  other arithmetic  3.21 us (2%)
    ppermute x18, waiting for transfers between devices, moved(): return lax.ppermute(array, 'ctx', pairs)  39.8 us
    unnamed x86, local copies, waits for them, and re-layouts  29.7 us
    ppermute x18, starting transfers between devices, moved(): return lax.ppermute(array, 'ctx', pairs)  27.6 us
    all_to_all x1, blocking collectives, shards(): lax.all_to_all(packed.reshape(owners, capacity), ('img', 'ctx'), split_ax...  15.5 us
    ppermute x2, waiting for transfers between devices, shards(): beyond = [lax.ppermute(pair, 'tp', far_pairs) for pair in pairs]  15 us
    ppermute x1, waiting for transfers between devices, shards(): crossed = lax.ppermute(cross, 'img', [(i, 1 - i) for i in range(n_img)])  8.29 us
    pallas_call x2, Pallas kernels, finish(): pl.pallas_call(finish_kernel, grid_spec=pltpu.PrefetchScalarGridSpec(num_...  5.97 us
    pallas_call x1, Pallas kernels, multiply(): pl.pallas_call(lambda *refs: multiply_kernel(plan, *refs), in_specs=[pl.B...  5.2 us
  transfers between devices with their start and end apart: 29, of which 10 were waited for; matrix products, arithmetic and copies ran while one was open for 2% of the time, Pallas kernels for 13%

profile of v3, /device:TPU:1, one launch (start us, length us, event | category | flops | bytes accessed | tf_op | source)
XLA Modules:
  0.0 203.1 jit_solution(14589229743379132501)
XLA Ops:
  0.6 1.1 fusion.2
  1.7 3.8 %collective-permute-start.2 = (bf16[144,1024]{1,0:T(8,128)(2,1)S(1)}, bf16[144,1024]{1,0:T(8,128)(2,1)S(1)}, u32[]{:S(2)}, u32[]{:S(2)}) collective-permute-start(bf16[144,1024]{1,0:T(8,128)(2,1)S(1)} %bitcast.45), channel_id=1, source_target_pairs={{0,8},{4,12},{8,0},{12,4},{16,24},{20,28},{24,16},{28,20},{32,40},... | collective-permute-start | bytes 884744 | tf_op jit(solution)/shard_map/ppermute | solution.py:476
  7.0 3.6 %collective-permute-start.5 = (bf16[144,1024]{1,0:T(8,128)(2,1)S(1)}, bf16[144,1024]{1,0:T(8,128)(2,1)S(1)}, u32[]{:S(2)}, u32[]{:S(2)}) collective-permute-start(bf16[144,1024]{1,0:T(8,128)(2,1)S(1)} %bitcast.41), channel_id=1, source_target_pairs={{0,32},{4,36},{8,40},{12,44},{16,48},{20,52},{24,56},{28,60},{32,0... | collective-permute-start | bytes 884744 | tf_op jit(solution)/shard_map/ppermute | solution.py:476
  12.0 1.6 collective-permute-start.3
  13.9 15.5 %all_to_all.22 = s32[32,1,16]{2,1,0:T(1,128)S(1)} all-to-all(s32[32,1,16]{2,1,0:T(1,128)S(1)} %bitcast.60), channel_id=1, replica_groups=mesh['img'=2,'ctx'=16,'tp'=4] {'img','ctx'}, dimensions={0} | all-to-all | bytes 4096 | tf_op jit(solution)/shard_map/all_to_all | solution.py:494
  29.6 1.2 copy-done.4
  30.8 1.2 copy-done.30
  32.0 2.7 %collect.1 = bf16[512,2048]{1,0:T(8,128)(2,1)} custom-call(s32[512,1]{1,0:T(8,128)S(1)} %reshape.79.pos_ref, bf16[512,1024]{1,0:T(8,128)(2,1)S(1)} %copy-done.4, bf16[512,1024]{1,0:T(8,128)(2,1)S(1)} %bitcast.49), custom_call_target="tpu_custom_call" | custom-call | flops 1073741824 | bytes 4194304 | tf_op jit(solution)/shard_map/collect/pallas_call | solution.py:131
  34.7 4.8 %all-to-all-start.1 = ((bf16[32,16,2048]{2,1,0:T(8,128)(2,1)}), bf16[32,16,2048]{2,1,0:T(8,128)(2,1)}, u32[]{:S(2)}, u32[]{:S(2)}) async-start(bf16[32,16,2048]{2,1,0:T(8,128)(2,1)} %bitcast.19), calls=%async_computation.1 | async-start | bytes 4194304 | tf_op jit(solution)/shard_map/all_to_all | solution.py:504
  40.5 2.3 %collective-permute-start.11 = (bf16[288,1024]{1,0:T(8,128)(2,1)S(1)}, bf16[288,1024]{1,0:T(8,128)(2,1)}, u32[]{:S(2)}, u32[]{:S(2)}) collective-permute-start(bf16[288,1024]{1,0:T(8,128)(2,1)S(1)} %bitcast.28), channel_id=1, source_target_pairs={{0,48},{4,52},{8,56},{12,60},{16,0},{20,4},{24,8},{28,12},{32,16},... | collective-permute-start | bytes 1769480 | tf_op jit(solution)/shard_map/ppermute | solution.py:476
  42.9 2.7 %collective-permute-start.10 = (bf16[288,1024]{1,0:T(8,128)(2,1)}, bf16[288,1024]{1,0:T(8,128)(2,1)S(1)}, u32[]{:S(2)}, u32[]{:S(2)}) collective-permute-start(bf16[288,1024]{1,0:T(8,128)(2,1)} %bitcast.13.refs_2_.refs_1_), channel_id=1, source_target_pairs={{0,48},{4,52},{8,56},{12,60},{16,0},{20,4},{24,8},{28,12},{32,16},... | collective-permute-start | bytes 1769480 | tf_op jit(solution)/shard_map/ppermute | solution.py:476
  45.7 2.5 %collective-permute-start.13 = (bf16[288,1024]{1,0:T(8,128)(2,1)S(1)}, bf16[288,1024]{1,0:T(8,128)(2,1)}, u32[]{:S(2)}, u32[]{:S(2)}) collective-permute-start(bf16[288,1024]{1,0:T(8,128)(2,1)S(1)} %bitcast.36), channel_id=1, source_target_pairs={{0,12},{4,0},{8,4},{12,8},{16,28},{20,16},{24,20},{28,24},{32,44},... | collective-permute-start | bytes 1769480 | tf_op jit(solution)/shard_map/ppermute | solution.py:476
  48.2 28.7 %collective-permute-done.11.refs_7_.refs_6_ = bf16[288,1024]{1,0:T(8,128)(2,1)} collective-permute-done((bf16[288,1024]{1,0:T(8,128)(2,1)S(1)}, bf16[288,1024]{1,0:T(8,128)(2,1)}, u32[]{:S(2)}, u32[]{:S(2)}) %collective-permute-start.11) | collective-permute-done | bytes 589856 | tf_op jit(solution)/shard_map/ppermute | solution.py:476
  76.9 1.1 collective-permute-start.9
  79.6 1.6 collective-permute-start.12
  81.2 8.3 %collective-permute-done.10.refs_6_.refs_5_ = bf16[288,1024]{1,0:T(8,128)(2,1)S(1)} collective-permute-done((bf16[288,1024]{1,0:T(8,128)(2,1)}, bf16[288,1024]{1,0:T(8,128)(2,1)S(1)}, u32[]{:S(2)}, u32[]{:S(2)}) %collective-permute-start.10) | collective-permute-done | bytes 589856 | tf_op jit(solution)/shard_map/ppermute | solution.py:476
  90.3 1.1 collective-permute-start.8
  92.3 1.7 copy-done.29
  94.0 4.5 %layer_norm.1 = (bf16[16,256,288]{2,1,0:T(8,128)(2,1)S(1)}, bf16[4,256,1152]{2,1,0:T(8,128)(2,1)S(1)}, f32[256,128]{1,0:T(8,128)S(1)}) custom-call(bf16[1024,1152]{1,0:T(8,128)(2,1)S(1)} %bitcast.40, bf16[4,1152]{1,0:T(4,128)(2,1)S(1)} %bitcast.51, bf16[4,1152]{1,0:T(4,128)(2,1)S(1)} %bitcast.54), custom_call_target="tpu_custom_call" | custom-call | flops 603979776 | bytes 7077888 | tf_op jit(solution)/shard_map/layer_norm/pallas_call | solution.py:96
  98.5 1.4 copy-done
  102.2 2.6 %collective-permute-done.8.refs_10_.refs_9_ = bf16[288,1024]{1,0:T(8,128)(2,1)} collective-permute-done((bf16[288,1024]{1,0:T(8,128)(2,1)S(1)}, bf16[288,1024]{1,0:T(8,128)(2,1)}, u32[]{:S(2)}, u32[]{:S(2)}) %collective-permute-start.8) | collective-permute-done | bytes 589856 | tf_op jit(solution)/shard_map/ppermute | solution.py:476
  105.0 2.4 %collective-permute-start.15 = (bf16[288,1024]{1,0:T(8,128)(2,1)}, bf16[288,1024]{1,0:T(8,128)(2,1)}, u32[]{:S(2)}, u32[]{:S(2)}) collective-permute-start(bf16[288,1024]{1,0:T(8,128)(2,1)} %collective-permute-done.11.refs_7_.refs_6_), channel_id=1, source_target_pairs={{0,48},{4,52},{8,56},{12,60},{16,0},{20,4},{24,8},{28,12},{32,16},... | collective-permute-start | bytes 1769480 | tf_op jit(solution)/shard_map/ppermute | solution.py:476
  107.4 1.1 collective-permute-start.16
  108.5 1.6 collective-permute-start.17
  110.3 1.1 copy-done.9
  111.4 1.1 copy-done.12
  112.5 1.1 copy-done.15
  116.7 1.1 copy-done.27
  117.8 5.2 %multiply.1.refs_6_ = f32[256,1024]{1,0:T(8,128)S(1)} custom-call(s32[2]{0:T(128)S(1)} %pad_add_fusion.1.refs_0_, bf16[16,256,288]{2,1,0:T(8,128)(2,1)S(1)} %get-tuple-element.55.refs_1_, bf16[288,1024]{1,0:T(8,128)(2,1)} %bitcast.13.refs_2_.refs_1_, bf16[288,1024]{1,0:T(8,128)(2,1)S(1)} %bitcast.30, ...), custom_call_target="tpu_custom_call" | custom-call | flops 1811939328 | bytes 7077888 | tf_op jit(solution)/shard_map/multiply/pallas_call | solution.py:215
  124.0 2.4 %unpack.1 = (f32[256,1024]{1,0:T(8,128)S(1)}, f32[256,1024]{1,0:T(8,128)S(1)}) custom-call(s32[256,1]{1,0:T(8,128)S(1)} %copy.17.slot_ref, bf16[512,2048]{1,0:T(8,128)(2,1)} %bitcast.20.came_ref, bf16[1,1024]{1,0:T(2,128)(2,1)S(1)} %copy-done.38), custom_call_target="tpu_custom_call" | custom-call | flops 536870912 | bytes 2097152 | tf_op jit(solution)/shard_map/unpack/pallas_call | solution.py:156
  126.5 3.4 %merge.1 = (bf16[256,1024]{1,0:T(8,128)(2,1)S(1)}, f32[256,1024]{1,0:T(8,128)S(1)}, f32[8,256]{1,0:T(8,128)S(1)}) custom-call(s32[2]{0:T(128)S(1)} %pad_add_fusion.1.refs_0_, bf16[16,256,288]{2,1,0:T(8,128)(2,1)S(1)} %get-tuple-element.55.refs_1_, bf16[288,1024]{1,0:T(8,128)(2,1)} %collective-permute-done.14.refs_2_.refs_13_, ...), custom_call_target="tpu_custom_call" | custom-call | flops 603979776 | bytes 4718592 | tf_op jit(solution)/shard_map/merge/pallas_call | solution.py:245
  131.7 3.7 %collective-permute-start.19 = (f32[8,256]{1,0:T(8,128)S(1)}, f32[8,256]{1,0:T(8,128)S(1)}, u32[]{:S(2)}, u32[]{:S(2)}) collective-permute-start(f32[8,256]{1,0:T(8,128)S(1)} %get-tuple-element.70), channel_id=1, source_target_pairs={{0,1},{1,0},{2,3},{3,2},{4,5},{5,4},{6,7},{7,6},{8,9},{9,8},{10,11... | collective-permute-start | bytes 24584 | tf_op jit(solution)/shard_map/ppermute | solution.py:525
  136.3 2.5 %collective-permute-start.20 = (f32[8,256]{1,0:T(8,128)S(1)}, f32[8,256]{1,0:T(8,128)S(1)}, u32[]{:S(2)}, u32[]{:S(2)}) collective-permute-start(f32[8,256]{1,0:T(8,128)S(1)} %add.45.refs_3_), channel_id=1, source_target_pairs={{0,2},{1,3},{2,0},{3,1},{4,6},{5,7},{6,4},{7,5},{8,10},{9,11},{10,... | collective-permute-start | bytes 24584 | tf_op jit(solution)/shard_map/ppermute | solution.py:526
  141.9 1.1 copy-done.19
  143.0 1.1 copy-done.22
  146.2 3.3 %assemble.1 = bf16[16,288,1024]{2,1,0:T(8,128)(2,1)S(1)} custom-call(s32[2]{0:T(128)S(1)} %pad_add_fusion.1.refs_0_, bf16[288,1024]{1,0:T(8,128)(2,1)} %bitcast.13.refs_2_.refs_1_, bf16[288,1024]{1,0:T(8,128)(2,1)S(1)} %bitcast.31, bf16[288,1024]{1,0:T(8,128)(2,1)} %collective-permute-done.6.refs_4_.refs_3_, bf16[288,1024]{1,0:T(8,128)(2,1)S(1)} %copy-done.13, ...), custom_call_target="tpu_custom_call" | custom-call | bytes 18874368 | tf_op jit(solution)/shard_map/assemble/pallas_call | solution.py:288
  149.5 3.3 %backward.1 = (f32[64,4608]{1,0:T(8,128)S(1)}, f32[64,4608]{1,0:T(8,128)S(1)}, bf16[64,4608]{1,0:T(8,128)(2,1)S(1)}, bf16[64,4608]{1,0:T(8,128)(2,1)S(1)}) custom-call(s32[1]{0:T(128)} %bitcast.21.refs_0_.core_ref, f32[256,1024]{1,0:T(8,128)S(1)} %copy-done.32, f32[256,1024]{1,0:T(8,128)S(1)} %copy-done.3, f32[8,256]{1,0:T(8,128)S(1)} %add.45.refs_3_, ...), custom_call_target="tpu_custom_call" | custom-call | flops 2415919104 | bytes 9437184 | tf_op jit(solution)/shard_map/backward/pallas_call | solution.py:331
  157.0 2.2 %collective-permute-start.24 = (bf16[64,4608]{1,0:T(8,128)(2,1)}, bf16[64,4608]{1,0:T(8,128)(2,1)}, u32[]{:S(2)}, u32[]{:S(2)}) collective-permute-start(bf16[64,4608]{1,0:T(8,128)(2,1)} %add_convert_fusion.own_ref), channel_id=1, source_target_pairs={{0,2},{1,3},{2,0},{3,1},{4,6},{5,7},{6,4},{7,5},{8,10},{9,11},{10,... | collective-permute-start | bytes 1769480 | tf_op jit(solution)/shard_map/ppermute | solution.py:541
  159.2 8.3 %collective-permute-done.18 = bf16[256,1024]{1,0:T(8,128)(2,1)S(1)} collective-permute-done((bf16[256,1024]{1,0:T(8,128)(2,1)S(1)}, bf16[256,1024]{1,0:T(8,128)(2,1)S(1)}, u32[]{:S(2)}, u32[]{:S(2)}) %collective-permute-start.18) | collective-permute-done | bytes 524320 | tf_op jit(solution)/shard_map/ppermute | solution.py:533
  167.5 1.1 pad_maximum_fusion
  168.6 4.5 %all-to-all-start.2 = ((bf16[16,32,1024]{2,1,0:T(8,128)(2,1)}), bf16[16,32,1024]{2,1,0:T(8,128)(2,1)}, u32[]{:S(2)}, u32[]{:S(2)}) async-start(bf16[16,32,1024]{2,1,0:T(8,128)(2,1)} %pad_maximum_fusion), calls=%async_computation.2 | async-start | bytes 2097152 | tf_op jit(solution)/shard_map/all_to_all | solution.py:547
  173.1 6.8 %collective-permute-done.22.far_ref = bf16[64,4608]{1,0:T(8,128)(2,1)S(1)} collective-permute-done((bf16[64,4608]{1,0:T(8,128)(2,1)S(1)}, bf16[64,4608]{1,0:T(8,128)(2,1)S(1)}, u32[]{:S(2)}, u32[]{:S(2)}) %collective-permute-start.22) | collective-permute-done | bytes 589856 | tf_op jit(solution)/shard_map/ppermute | solution.py:541
  180.8 2.4 %finish.2.refs_0_ = bf16[256,1152]{1,0:T(8,128)(2,1)} custom-call(s32[1]{0:T(128)S(6)} %mul.20.block_ref, bf16[64,4608]{1,0:T(8,128)(2,1)S(1)} %add_convert_fusion.1.own_ref, bf16[64,4608]{1,0:T(8,128)(2,1)S(1)} %collective-permute-done.22.far_ref, bf16[4,256,1152]{2,1,0:T(8,128)(2,1)S(1)} %copy-done.1, f32[256,128]{1,0:T(8,128)S(1)} %copy-done.34, ...), custom_call_target="tpu_custom_call" | custom-call | flops 150994944 | bytes 2359296 | tf_op jit(solution)/shard_map/finish/pallas_call | solution.py:380
  183.2 1.2 collective-permute-start.25
  184.4 8.3 %collective-permute-done.24.far_ref = bf16[64,4608]{1,0:T(8,128)(2,1)} collective-permute-done((bf16[64,4608]{1,0:T(8,128)(2,1)}, bf16[64,4608]{1,0:T(8,128)(2,1)}, u32[]{:S(2)}, u32[]{:S(2)}) %collective-permute-start.24) | collective-permute-done | bytes 589856 | tf_op jit(solution)/shard_map/ppermute | solution.py:541
  192.6 3.6 %finish.3.refs_1_ = bf16[256,1152]{1,0:T(8,128)(2,1)} custom-call(s32[1]{0:T(128)S(6)} %add.47.block_ref, bf16[64,4608]{1,0:T(8,128)(2,1)} %add_convert_fusion.own_ref, bf16[64,4608]{1,0:T(8,128)(2,1)} %collective-permute-done.24.far_ref, bf16[4,256,1152]{2,1,0:T(8,128)(2,1)S(1)} %copy-done.1, f32[256,128]{1,0:T(8,128)S(1)} %copy-done.35, ...), custom_call_target="tpu_custom_call" | custom-call | flops 150994944 | bytes 2359296 | tf_op jit(solution)/shard_map/finish/pallas_call | solution.py:380
  197.1 2.9 %place.1 = bf16[512,1024]{1,0:T(8,128)(2,1)} custom-call(s32[1,512]{1,0:T(1,128)S(1)} %reshape.64.pos_ref, bf16[512,1024]{1,0:T(8,128)(2,1)} %bitcast.25.came_ref, bf16[512,1024]{1,0:T(8,128)(2,1)S(1)} %copy-done.5), custom_call_target="tpu_custom_call" | custom-call | flops 536870912 | bytes 3145728 | tf_op jit(solution)/shard_map/place/pallas_call | solution.py:412
  200.1 2.9 %lay.1 = bf16[1024,1152]{1,0:T(8,128)(2,1)} custom-call(s32[1]{0:T(128)} %bitcast.21.refs_0_.core_ref, bf16[256,1152]{1,0:T(8,128)(2,1)} %finish.2.refs_0_, bf16[256,1152]{1,0:T(8,128)(2,1)} %finish.3.refs_1_, bf16[256,1152]{1,0:T(8,128)(2,1)} %collective-permute-done.25.refs_2_, bf16[256,1152]{1,0:T(8,128)(2,1)S(1)} %collective-permute-done.26.refs_3_), custom_call_target="tpu_custom_call" | custom-call | bytes 4718592 | tf_op jit(solution)/shard_map/lay/pallas_call | solution.py:440
  (127 shorter events, 28.8 us)
Async XLA Ops:
  1.7 10.3 %collective-permute-start.2 = (bf16[144,1024]{1,0:T(8,128)(2,1)S(1)}, bf16[144,1024]{1,0:T(8,128)(2,1)S(1)}, u32[]{:S(2)}, u32[]{:S(2)}) collective-permute-start(bf16[144,1024]{1,0:T(8,128)(2,1)S(1)} %bitcast.45), channel_id=1, source_target_pairs={{0,8},{4,12},{8,0},{12,4},{16,24},{20,28},{24,16},{28,20},{32,40},... | collective-permute-start | bytes 884744 | tf_op jit(solution)/shard_map/ppermute | solution.py:476
  5.5 23.8 %collective-permute-start.1 = (bf16[144,1024]{1,0:T(8,128)(2,1)S(1)}, bf16[144,1024]{1,0:T(8,128)(2,1)S(1)}, u32[]{:S(2)}, u32[]{:S(2)}) collective-permute-start(bf16[144,1024]{1,0:T(8,128)(2,1)S(1)} %bitcast.46), channel_id=1, source_target_pairs={{0,12},{4,0},{8,4},{12,8},{16,28},{20,16},{24,20},{28,24},{32,44},... | collective-permute-start | bytes 884744 | tf_op jit(solution)/shard_map/ppermute | solution.py:476
  6.3 23.1 %collective-permute-start = (bf16[144,1024]{1,0:T(8,128)(2,1)S(1)}, bf16[144,1024]{1,0:T(8,128)(2,1)S(1)}, u32[]{:S(2)}, u32[]{:S(2)}) collective-permute-start(bf16[144,1024]{1,0:T(8,128)(2,1)S(1)} %bitcast.47), channel_id=1, source_target_pairs={{0,4},{4,8},{8,12},{12,0},{16,20},{20,24},{24,28},{28,16},{32,36},... | collective-permute-start | bytes 884744 | tf_op jit(solution)/shard_map/ppermute | solution.py:476
  7.0 22.4 %collective-permute-start.5 = (bf16[144,1024]{1,0:T(8,128)(2,1)S(1)}, bf16[144,1024]{1,0:T(8,128)(2,1)S(1)}, u32[]{:S(2)}, u32[]{:S(2)}) collective-permute-start(bf16[144,1024]{1,0:T(8,128)(2,1)S(1)} %bitcast.41), channel_id=1, source_target_pairs={{0,32},{4,36},{8,40},{12,44},{16,48},{20,52},{24,56},{28,60},{32,0... | collective-permute-start | bytes 884744 | tf_op jit(solution)/shard_map/ppermute | solution.py:476
  10.6 18.8 %collective-permute-start.4 = (bf16[144,1024]{1,0:T(8,128)(2,1)S(1)}, bf16[144,1024]{1,0:T(8,128)(2,1)S(1)}, u32[]{:S(2)}, u32[]{:S(2)}) collective-permute-start(bf16[144,1024]{1,0:T(8,128)(2,1)S(1)} %bitcast.42), channel_id=1, source_target_pairs={{0,48},{4,52},{8,56},{12,60},{16,0},{20,4},{24,8},{28,12},{32,16},... | collective-permute-start | bytes 884744 | tf_op jit(solution)/shard_map/ppermute | solution.py:476
  12.0 17.4 %collective-permute-start.3 = (bf16[144,1024]{1,0:T(8,128)(2,1)S(1)}, bf16[144,1024]{1,0:T(8,128)(2,1)S(1)}, u32[]{:S(2)}, u32[]{:S(2)}) collective-permute-start(bf16[144,1024]{1,0:T(8,128)(2,1)S(1)} %bitcast.43), channel_id=1, source_target_pairs={{0,16},{4,20},{8,24},{12,28},{16,32},{20,36},{24,40},{28,44},{32,4... | collective-permute-start | bytes 884744 | tf_op jit(solution)/shard_map/ppermute | solution.py:476
  29.4 5.3 %copy-start.41 = (s32[32,1,16]{2,1,0:T(1,128)}, s32[32,1,16]{2,1,0:T(1,128)S(1)}, u32[]{:S(2)}) copy-start(s32[32,1,16]{2,1,0:T(1,128)S(1)} %all_to_all.22) | copy-start | bytes 6148
  29.6 1.2 copy-start.4
  30.8 1.2 copy-start.30
  34.7 89.3 %all-to-all-start.1 = ((bf16[32,16,2048]{2,1,0:T(8,128)(2,1)}), bf16[32,16,2048]{2,1,0:T(8,128)(2,1)}, u32[]{:S(2)}, u32[]{:S(2)}) async-start(bf16[32,16,2048]{2,1,0:T(8,128)(2,1)} %bitcast.19), calls=%async_computation.1 | async-start | bytes 4194304 | tf_op jit(solution)/shard_map/all_to_all | solution.py:504
  39.5 52.8 %copy-start.36 = (bf16[1,4,1152]{2,1,0:T(4,128)(2,1)S(1)}, bf16[1,4,1152]{2,1,0:T(4,128)(2,1)}, u32[]{:S(2)}) copy-start(bf16[1,4,1152]{2,1,0:T(4,128)(2,1)} %param.9) | copy-start | bytes 27652
  39.5 52.8 %copy-start.37 = (bf16[1,4,1152]{2,1,0:T(4,128)(2,1)S(1)}, bf16[1,4,1152]{2,1,0:T(4,128)(2,1)}, u32[]{:S(2)}) copy-start(bf16[1,4,1152]{2,1,0:T(4,128)(2,1)} %param.10) | copy-start | bytes 27652
  40.5 51.8 %copy-start.8 = (bf16[2,144,1024]{2,1,0:T(8,128)(2,1)}, bf16[2,144,1024]{2,1,0:T(8,128)(2,1)S(1)}, u32[]{:S(2)}) copy-start(bf16[2,144,1024]{2,1,0:T(8,128)(2,1)S(1)} %get-tuple-element.48) | copy-start | bytes 1769476
  40.5 36.3 %collective-permute-start.11 = (bf16[288,1024]{1,0:T(8,128)(2,1)S(1)}, bf16[288,1024]{1,0:T(8,128)(2,1)}, u32[]{:S(2)}, u32[]{:S(2)}) collective-permute-start(bf16[288,1024]{1,0:T(8,128)(2,1)S(1)} %bitcast.28), channel_id=1, source_target_pairs={{0,48},{4,52},{8,56},{12,60},{16,0},{20,4},{24,8},{28,12},{32,16},... | collective-permute-start | bytes 1769480 | tf_op jit(solution)/shard_map/ppermute | solution.py:476
  42.9 35.9 %collective-permute-start.7 = (bf16[288,1024]{1,0:T(8,128)(2,1)S(1)}, bf16[288,1024]{1,0:T(8,128)(2,1)S(1)}, u32[]{:S(2)}, u32[]{:S(2)}) collective-permute-start(bf16[288,1024]{1,0:T(8,128)(2,1)S(1)} %bitcast.29), channel_id=1, source_target_pairs={{0,16},{4,20},{8,24},{12,28},{16,32},{20,36},{24,40},{28,44},{32,4... | collective-permute-start | bytes 1769480 | tf_op jit(solution)/shard_map/ppermute | solution.py:476
  42.9 46.6 %collective-permute-start.10 = (bf16[288,1024]{1,0:T(8,128)(2,1)}, bf16[288,1024]{1,0:T(8,128)(2,1)S(1)}, u32[]{:S(2)}, u32[]{:S(2)}) collective-permute-start(bf16[288,1024]{1,0:T(8,128)(2,1)} %bitcast.13.refs_2_.refs_1_), channel_id=1, source_target_pairs={{0,48},{4,52},{8,56},{12,60},{16,0},{20,4},{24,8},{28,12},{32,16},... | collective-permute-start | bytes 1769480 | tf_op jit(solution)/shard_map/ppermute | solution.py:476
  45.5 55.0 %collective-permute-start.6 = (bf16[288,1024]{1,0:T(8,128)(2,1)}, bf16[288,1024]{1,0:T(8,128)(2,1)}, u32[]{:S(2)}, u32[]{:S(2)}) collective-permute-start(bf16[288,1024]{1,0:T(8,128)(2,1)} %bitcast.13.refs_2_.refs_1_), channel_id=1, source_target_pairs={{0,16},{4,20},{8,24},{12,28},{16,32},{20,36},{24,40},{28,44},{32,4... | collective-permute-start | bytes 1769480 | tf_op jit(solution)/shard_map/ppermute | solution.py:476
  45.7 54.8 %collective-permute-start.13 = (bf16[288,1024]{1,0:T(8,128)(2,1)S(1)}, bf16[288,1024]{1,0:T(8,128)(2,1)}, u32[]{:S(2)}, u32[]{:S(2)}) collective-permute-start(bf16[288,1024]{1,0:T(8,128)(2,1)S(1)} %bitcast.36), channel_id=1, source_target_pairs={{0,12},{4,0},{8,4},{12,8},{16,28},{20,16},{24,20},{28,24},{32,44},... | collective-permute-start | bytes 1769480 | tf_op jit(solution)/shard_map/ppermute | solution.py:476
  76.9 23.7 %collective-permute-start.9 = (bf16[288,1024]{1,0:T(8,128)(2,1)S(1)}, bf16[288,1024]{1,0:T(8,128)(2,1)S(1)}, u32[]{:S(2)}, u32[]{:S(2)}) collective-permute-start(bf16[288,1024]{1,0:T(8,128)(2,1)S(1)} %bitcast.37), channel_id=1, source_target_pairs={{0,4},{4,8},{8,12},{12,0},{16,20},{20,24},{24,28},{28,16},{32,36},... | collective-permute-start | bytes 1769480 | tf_op jit(solution)/shard_map/ppermute | solution.py:476
  79.6 21.8 %collective-permute-start.12 = (bf16[288,1024]{1,0:T(8,128)(2,1)S(1)}, bf16[288,1024]{1,0:T(8,128)(2,1)S(1)}, u32[]{:S(2)}, u32[]{:S(2)}) collective-permute-start(bf16[288,1024]{1,0:T(8,128)(2,1)S(1)} %bitcast.32), channel_id=1, source_target_pairs={{0,12},{4,0},{8,4},{12,8},{16,28},{20,16},{24,20},{28,24},{32,44},... | collective-permute-start | bytes 1769480 | tf_op jit(solution)/shard_map/ppermute | solution.py:476
  90.3 14.4 %collective-permute-start.8 = (bf16[288,1024]{1,0:T(8,128)(2,1)S(1)}, bf16[288,1024]{1,0:T(8,128)(2,1)}, u32[]{:S(2)}, u32[]{:S(2)}) collective-permute-start(bf16[288,1024]{1,0:T(8,128)(2,1)S(1)} %bitcast.33), channel_id=1, source_target_pairs={{0,4},{4,8},{8,12},{12,0},{16,20},{20,24},{24,28},{28,16},{32,36},... | collective-permute-start | bytes 1769480 | tf_op jit(solution)/shard_map/ppermute | solution.py:476
  92.3 1.7 copy-start.29
  98.5 1.4 copy-start
  104.8 21.7 %collective-permute-start.14 = (bf16[288,1024]{1,0:T(8,128)(2,1)}, bf16[288,1024]{1,0:T(8,128)(2,1)}, u32[]{:S(2)}, u32[]{:S(2)}) collective-permute-start(bf16[288,1024]{1,0:T(8,128)(2,1)} %collective-permute-done.6.refs_4_.refs_3_), channel_id=1, source_target_pairs={{0,16},{4,20},{8,24},{12,28},{16,32},{20,36},{24,40},{28,44},{32,4... | collective-permute-start | bytes 1769480 | tf_op jit(solution)/shard_map/ppermute | solution.py:476
  105.0 21.4 %collective-permute-start.15 = (bf16[288,1024]{1,0:T(8,128)(2,1)}, bf16[288,1024]{1,0:T(8,128)(2,1)}, u32[]{:S(2)}, u32[]{:S(2)}) collective-permute-start(bf16[288,1024]{1,0:T(8,128)(2,1)} %collective-permute-done.11.refs_7_.refs_6_), channel_id=1, source_target_pairs={{0,48},{4,52},{8,56},{12,60},{16,0},{20,4},{24,8},{28,12},{32,16},... | collective-permute-start | bytes 1769480 | tf_op jit(solution)/shard_map/ppermute | solution.py:476
  107.4 19.0 %collective-permute-start.16 = (bf16[288,1024]{1,0:T(8,128)(2,1)}, bf16[288,1024]{1,0:T(8,128)(2,1)}, u32[]{:S(2)}, u32[]{:S(2)}) collective-permute-start(bf16[288,1024]{1,0:T(8,128)(2,1)} %collective-permute-done.8.refs_10_.refs_9_), channel_id=1, source_target_pairs={{0,4},{4,8},{8,12},{12,0},{16,20},{20,24},{24,28},{28,16},{32,36},... | collective-permute-start | bytes 1769480 | tf_op jit(solution)/shard_map/ppermute | solution.py:476
  108.5 17.9 %collective-permute-start.17 = (bf16[288,1024]{1,0:T(8,128)(2,1)}, bf16[288,1024]{1,0:T(8,128)(2,1)}, u32[]{:S(2)}, u32[]{:S(2)}) collective-permute-start(bf16[288,1024]{1,0:T(8,128)(2,1)} %collective-permute-done.13.refs_13_.refs_12_), channel_id=1, source_target_pairs={{0,12},{4,0},{8,4},{12,8},{16,28},{20,16},{24,20},{28,24},{32,44},... | collective-permute-start | bytes 1769480 | tf_op jit(solution)/shard_map/ppermute | solution.py:476
  110.3 1.1 copy-start.9
  117.8 6.2 %copy-start.38 = (bf16[1,1024]{1,0:T(2,128)(2,1)S(1)}, bf16[1,1024]{1,0:T(2,128)(2,1)}, u32[]{:S(2)}) copy-start(bf16[1,1024]{1,0:T(2,128)(2,1)} %ngain_ref.1) | copy-start | bytes 6148
  124.0 2.5 %copy-start.7 = (f32[256,1024]{1,0:T(8,128)S(1)}, f32[256,1024]{1,0:T(8,128)}, u32[]{:S(2)}) copy-start(f32[256,1024]{1,0:T(8,128)} %copy-done.6) | copy-start | bytes 3145732
  126.4 3.5 %copy-start.2 = (f32[256,1024]{1,0:T(8,128)}, f32[256,1024]{1,0:T(8,128)S(1)}, u32[]{:S(2)}) copy-start(f32[256,1024]{1,0:T(8,128)S(1)} %get-tuple-element.65.refs_8_.refs_2_) | copy-start | bytes 3145732
  131.7 4.6 %collective-permute-start.19 = (f32[8,256]{1,0:T(8,128)S(1)}, f32[8,256]{1,0:T(8,128)S(1)}, u32[]{:S(2)}, u32[]{:S(2)}) collective-permute-start(f32[8,256]{1,0:T(8,128)S(1)} %get-tuple-element.70), channel_id=1, source_target_pairs={{0,1},{1,0},{2,3},{3,2},{4,5},{5,4},{6,7},{7,6},{8,9},{9,8},{10,11... | collective-permute-start | bytes 24584 | tf_op jit(solution)/shard_map/ppermute | solution.py:525
  136.3 13.2 %collective-permute-start.20 = (f32[8,256]{1,0:T(8,128)S(1)}, f32[8,256]{1,0:T(8,128)S(1)}, u32[]{:S(2)}, u32[]{:S(2)}) collective-permute-start(f32[8,256]{1,0:T(8,128)S(1)} %add.45.refs_3_), channel_id=1, source_target_pairs={{0,2},{1,3},{2,0},{3,1},{4,6},{5,7},{6,4},{7,5},{8,10},{9,11},{10,... | collective-permute-start | bytes 24584 | tf_op jit(solution)/shard_map/ppermute | solution.py:526
  146.2 3.3 %copy-start.3 = (f32[256,1024]{1,0:T(8,128)S(1)}, f32[256,1024]{1,0:T(8,128)}, u32[]{:S(2)}) copy-start(f32[256,1024]{1,0:T(8,128)} %copy-done.2) | copy-start | bytes 3145732
  146.2 3.3 %copy-start.32 = (f32[256,1024]{1,0:T(8,128)S(1)}, f32[256,1024]{1,0:T(8,128)}, u32[]{:S(2)}) copy-start(f32[256,1024]{1,0:T(8,128)} %copy-done.31) | copy-start | bytes 3145732
  149.5 4.0 %copy-start.40 = (bf16[256,1024]{1,0:T(8,128)(2,1)S(1)}, bf16[256,1024]{1,0:T(8,128)(2,1)}, u32[]{:S(2)}) copy-start(bf16[256,1024]{1,0:T(8,128)(2,1)} %copy-done.39) | copy-start | bytes 1572868
  152.8 2.3 %collective-permute-start.21 = (bf16[64,4608]{1,0:T(8,128)(2,1)S(1)}, bf16[64,4608]{1,0:T(8,128)(2,1)S(1)}, u32[]{:S(2)}, u32[]{:S(2)}) collective-permute-start(bf16[64,4608]{1,0:T(8,128)(2,1)S(1)} %get-tuple-element.72), channel_id=1, source_target_pairs={{0,1},{1,0},{2,3},{3,2},{4,5},{5,4},{6,7},{7,6},{8,9},{9,8},{10,11... | collective-permute-start | bytes 1769480 | tf_op jit(solution)/shard_map/ppermute | solution.py:539
  153.9 13.6 %collective-permute-start.18 = (bf16[256,1024]{1,0:T(8,128)(2,1)S(1)}, bf16[256,1024]{1,0:T(8,128)(2,1)S(1)}, u32[]{:S(2)}, u32[]{:S(2)}) collective-permute-start(bf16[256,1024]{1,0:T(8,128)(2,1)S(1)} %get-tuple-element.68), channel_id=1, source_target_pairs={{0,64},{64,0},{1,65},{65,1},{2,66},{66,2},{3,67},{67,3},{4,68},{68... | collective-permute-start | bytes 1572872 | tf_op jit(solution)/shard_map/ppermute | solution.py:533
  154.0 2.1 %collective-permute-start.23 = (bf16[64,4608]{1,0:T(8,128)(2,1)S(1)}, bf16[64,4608]{1,0:T(8,128)(2,1)S(1)}, u32[]{:S(2)}, u32[]{:S(2)}) collective-permute-start(bf16[64,4608]{1,0:T(8,128)(2,1)S(1)} %get-tuple-element.79), channel_id=1, source_target_pairs={{0,1},{1,0},{2,3},{3,2},{4,5},{5,4},{6,7},{7,6},{8,9},{9,8},{10,11... | collective-permute-start | bytes 1769480 | tf_op jit(solution)/shard_map/ppermute | solution.py:539
  155.2 24.6 %collective-permute-start.22 = (bf16[64,4608]{1,0:T(8,128)(2,1)S(1)}, bf16[64,4608]{1,0:T(8,128)(2,1)S(1)}, u32[]{:S(2)}, u32[]{:S(2)}) collective-permute-start(bf16[64,4608]{1,0:T(8,128)(2,1)S(1)} %add_convert_fusion.1.own_ref), channel_id=1, source_target_pairs={{0,2},{1,3},{2,0},{3,1},{4,6},{5,7},{6,4},{7,5},{8,10},{9,11},{10,... | collective-permute-start | bytes 1769480 | tf_op jit(solution)/shard_map/ppermute | solution.py:541
  157.0 35.6 %collective-permute-start.24 = (bf16[64,4608]{1,0:T(8,128)(2,1)}, bf16[64,4608]{1,0:T(8,128)(2,1)}, u32[]{:S(2)}, u32[]{:S(2)}) collective-permute-start(bf16[64,4608]{1,0:T(8,128)(2,1)} %add_convert_fusion.own_ref), channel_id=1, source_target_pairs={{0,2},{1,3},{2,0},{3,1},{4,6},{5,7},{6,4},{7,5},{8,10},{9,11},{10,... | collective-permute-start | bytes 1769480 | tf_op jit(solution)/shard_map/ppermute | solution.py:541
  167.5 12.3 %copy-start.1 = (bf16[4,256,1152]{2,1,0:T(8,128)(2,1)S(1)}, bf16[4,256,1152]{2,1,0:T(8,128)(2,1)}, u32[]{:S(2)}) copy-start(bf16[4,256,1152]{2,1,0:T(8,128)(2,1)} %copy-done) | copy-start | bytes 7077892
  168.6 28.5 %all-to-all-start.2 = ((bf16[16,32,1024]{2,1,0:T(8,128)(2,1)}), bf16[16,32,1024]{2,1,0:T(8,128)(2,1)}, u32[]{:S(2)}, u32[]{:S(2)}) async-start(bf16[16,32,1024]{2,1,0:T(8,128)(2,1)} %pad_maximum_fusion), calls=%async_computation.2 | async-start | bytes 2097152 | tf_op jit(solution)/shard_map/all_to_all | solution.py:547
  180.8 11.8 %copy-start.35 = (f32[256,128]{1,0:T(8,128)S(1)}, f32[256,128]{1,0:T(8,128)}, u32[]{:S(2)}) copy-start(f32[256,128]{1,0:T(8,128)} %copy-done.33) | copy-start | bytes 393220
  183.2 13.9 %copy-start.42 = (s32[32,1,16]{2,1,0:T(1,128)S(1)}, s32[32,1,16]{2,1,0:T(1,128)}, u32[]{:S(2)}) copy-start(s32[32,1,16]{2,1,0:T(1,128)} %copy-done.41) | copy-start | bytes 6148
  183.2 14.0 %copy-start.5 = (bf16[512,1024]{1,0:T(8,128)(2,1)S(1)}, bf16[512,1024]{1,0:T(8,128)(2,1)}, u32[]{:S(2)}) copy-start(bf16[512,1024]{1,0:T(8,128)(2,1)} %stream_ref.3) | copy-start | bytes 3145732
  183.2 16.9 %collective-permute-start.25 = (bf16[256,1152]{1,0:T(8,128)(2,1)}, bf16[256,1152]{1,0:T(8,128)(2,1)}, u32[]{:S(2)}, u32[]{:S(2)}) collective-permute-start(bf16[256,1152]{1,0:T(8,128)(2,1)} %finish.2.refs_0_), channel_id=1, source_target_pairs={{0,1},{1,0},{2,3},{3,2},{4,5},{5,4},{6,7},{7,6},{8,9},{9,8},{10,11... | collective-permute-start | bytes 1769480 | tf_op jit(solution)/shard_map/ppermute | solution.py:560
  196.2 3.9 %collective-permute-start.26 = (bf16[256,1152]{1,0:T(8,128)(2,1)}, bf16[256,1152]{1,0:T(8,128)(2,1)S(1)}, u32[]{:S(2)}, u32[]{:S(2)}) collective-permute-start(bf16[256,1152]{1,0:T(8,128)(2,1)} %finish.3.refs_1_), channel_id=1, source_target_pairs={{0,1},{1,0},{2,3},{3,2},{4,5},{5,4},{6,7},{7,6},{8,9},{9,8},{10,11... | collective-permute-start | bytes 1769480 | tf_op jit(solution)/shard_map/ppermute | solution.py:560
  (24 other events, 23.1 us)

commit v4 on v3

--- a/solution.py
+++ b/solution.py
@@ -42,24 +42,14 @@
 
 
 SIDE = 4
-HALVES = 4 * SIDE
-
-
-def piece_slices(window, share):
-    half = window // 2
-    pieces = []
-    for part in range(2):
-        for first in range(SIDE):
-            for side in range(2):
-                piece = []
-                for second in (2 * side, 2 * side + 1):
-                    ctx = first * SIDE + second if part == 0 else second * SIDE + first
-                    piece += [(w, ctx * share) for w in range(part * half, part * half + half)]
-                pieces.append(piece)
-    return pieces
-
-
-def norm_kernel(x_ref, gain_ref, bias_ref, lifted_ref, xw_ref, stat_ref):
+
+
+def second_half(window, share):
+    blocks = SIDE * SIDE
+    return [(w, c * share) for c in range(blocks) for w in range(window // 2, window)]
+
+
+def norm_kernel(x_ref, gain_ref, bias_ref, first_ref, second_ref, xw_ref, stat_ref):
     window, width = gain_ref.shape
     tokens = x_ref.shape[0] // window
     full = window * width
@@ -79,10 +69,11 @@
             normed * gain_ref[w : w + 1].astype(F32) + bias_ref[w : w + 1].astype(F32)
         )
         xw_ref[w] = p.astype(BF)
-    for index, piece in enumerate(piece_slices(window, share)):
-        lifted_ref[index] = jnp.concatenate(
-            [lifted[w][:, at : at + share] for w, at in piece], axis=1
-        ).astype(BF)
+    for w in range(window // 2):
+        first_ref[:, w * width : (w + 1) * width] = lifted[w].astype(BF)
+    second_ref[...] = jnp.concatenate(
+        [lifted[w][:, at : at + share] for w, at in second_half(window, share)], axis=1
+    ).astype(BF)
     lane = lax.broadcasted_iota(jnp.int32, stat_ref.shape, 1)
     stat_ref[...] = jnp.where(lane == 0, mean, inv)
 
@@ -92,7 +83,7 @@
     window = gain.shape[0]
     merged = rows // window
     block = 64
-    piece = window * width // HALVES
+    half = window * width // 2
     return pl.pallas_call(
         norm_kernel,
         grid=(merged // block,),
@@ -102,12 +93,14 @@
             pl.BlockSpec((window, width), lambda i: (0, 0)),
         ],
         out_specs=[
-            pl.BlockSpec((HALVES, block, piece), lambda i: (0, i, 0)),
+            pl.BlockSpec((block, half), lambda i: (i, 0)),
+            pl.BlockSpec((block, half), lambda i: (i, 0)),
             pl.BlockSpec((window, block, width), lambda i: (0, i, 0)),
             pl.BlockSpec((block, 128), lambda i: (i, 0)),
         ],
         out_shape=[
-            jax.ShapeDtypeStruct((HALVES, merged, piece), BF),
+            jax.ShapeDtypeStruct((merged, half), BF),
+            jax.ShapeDtypeStruct((merged, half), BF),
             jax.ShapeDtypeStruct((window, merged, width), BF),
             jax.ShapeDtypeStruct((merged, 128), F32),
         ],
@@ -164,68 +157,89 @@
     )(slot_col, came, ngain)
 
 
+AWAY = (0, SIDE - 1, 1, 2)
+
+
 def stack_kernel(me_ref, *refs):
-    me = me_ref[0]
-    for away, ref in zip((0, SIDE - 1, 1, 2), refs[:SIDE]):
-        place = lax.rem(me + away, SIDE)
-        for side in range(2):
-
-            @pl.when(place // 2 == side)
-            def _():
-                refs[SIDE + side][lax.rem(place, 2)] = ref[...]
+    for away, ref in zip(AWAY, refs[:SIDE]):
+        refs[SIDE][lax.rem(me_ref[0] + away, SIDE)] = ref[...]
 
 
 def stack(me, blocks):
     rows, width = blocks[0].shape
-    halves = pl.pallas_call(
+    return pl.pallas_call(
         stack_kernel,
         in_specs=[pl.BlockSpec(memory_space=SMEM)] + [whole()] * SIDE,
-        out_specs=[whole()] * 2,
-        out_shape=[jax.ShapeDtypeStruct((2, rows, width), BF)] * 2,
-        compiler_params=params(6),
+        out_specs=whole(),
+        out_shape=jax.ShapeDtypeStruct((SIDE, rows, width), BF),
+        compiler_params=params(4),
         cost_estimate=cost(0, 16 * rows * width),
         name="stack",
     )(me, *blocks)
-    return [h.reshape(2 * rows, width) for h in halves]
-
-
-def place_of(zy_ref, entry):
-    part, away, side = entry
-    return part * 2 * SIDE + 2 * lax.rem(zy_ref[part] + away, SIDE) + side
-
-
-def product(plan, zy_ref, lifted_ref, refs):
-    total = None
-    for entry, ref in zip(plan, refs):
-        part = jnp.dot(
-            lifted_ref[place_of(zy_ref, entry)], ref[...], preferred_element_type=F32
-        )
-        total = part if total is None else total + part
-    return total
-
-
-def multiply_kernel(plan, zy_ref, lifted_ref, *refs):
-    refs[-1][...] = product(plan, zy_ref, lifted_ref, refs[:-1])
-
-
-def multiply(zy, lifted, pieces, plan):
-    tokens = lifted.shape[1]
-    width = pieces[0].shape[1]
-    depth = sum(p.shape[0] for p in pieces)
-    return pl.pallas_call(
-        lambda *refs: multiply_kernel(plan, *refs),
-        in_specs=[pl.BlockSpec(memory_space=SMEM)] + [whole()] * (1 + len(pieces)),
-        out_specs=whole(),
-        out_shape=jax.ShapeDtypeStruct((tokens, width), F32),
+
+
+def second_kernel(zy_ref, lifted_ref, *refs):
+    acc_ref, out_ref, held_ref, sems, out_sem = refs[2 * SIDE :]
+    cut = refs[0].shape[2]
+    copies = []
+    for index, ref in enumerate(refs[: 2 * SIDE]):
+        part, away = index // SIDE, AWAY[index % SIDE]
+        place = lax.rem(zy_ref[part] + away, SIDE)
+        to = held_ref.at[place, :, :, :cut] if part == 0 else held_ref.at[:, place, :, cut:]
+        copies.append(pltpu.make_async_copy(ref, to, sems.at[index]))
+    for copy in copies:
+        copy.start()
+    for copy in copies:
+        copy.wait()
+    keep = pltpu.make_async_copy(held_ref, out_ref, out_sem)
+    keep.start()
+    depth = lifted_ref.shape[1]
+    acc_ref[...] = jnp.dot(
+        lifted_ref[...], held_ref[...].reshape(depth, -1), preferred_element_type=F32
+    )
+    keep.wait()
+
+
+def second(zy, lifted, pieces):
+    tokens, depth = lifted.shape
+    rows, cut = pieces[0].shape[1:]
+    width = 2 * cut
+    held = (SIDE, SIDE, rows, width)
+    return pl.pallas_call(
+        second_kernel,
+        in_specs=[pl.BlockSpec(memory_space=SMEM), whole()]
+        + [pl.BlockSpec(memory_space=pl.ANY)] * len(pieces),
+        out_specs=[whole(), pl.BlockSpec(memory_space=pl.ANY)],
+        out_shape=[
+            jax.ShapeDtypeStruct((tokens, width), F32),
+            jax.ShapeDtypeStruct(held, BF),
+        ],
+        scratch_shapes=[
+            pltpu.VMEM(held, BF),
+            pltpu.SemaphoreType.DMA((len(pieces),)),
+            pltpu.SemaphoreType.DMA,
+        ],
         compiler_params=params(16),
-        cost_estimate=cost(2 * depth * tokens * width, 2 * depth * width),
-        name="multiply",
+        cost_estimate=cost(2 * depth * tokens * width, 6 * depth * width),
+        name="second",
     )(zy, lifted, *pieces)
 
 
-def merge_kernel(plan, zy_ref, lifted_ref, *refs):
-    acc_ref, base_ref, up_ref, visual_ref, state_ref, stat_ref = refs[len(plan) :]
-    total = acc_ref[...] + product(plan, zy_ref, lifted_ref, refs[: len(plan)])
+BLOCK = 768
+
+
+def merge_kernel(lifted_ref, acc_ref, base_ref, up_ref, w_ref, visual_ref, state_ref, stat_ref, held_ref, sems):
+    steps = range(w_ref.shape[0] // BLOCK)
+    copies = []
+    for step in steps:
+        at = pl.ds(step * BLOCK, BLOCK)
+        copies.append(pltpu.make_async_copy(w_ref.at[at], held_ref.at[at], sems.at[step]))
+        copies[step].start()
+    total = acc_ref[...]
+    for step in steps:
+        at = slice(step * BLOCK, (step + 1) * BLOCK)
+        copies[step].wait()
+        total = total + jnp.dot(lifted_ref[:, at], held_ref[at, :], preferred_element_type=F32)
     visual = total.astype(BF)
     visual_ref[...] = visual
     state = base_ref[...] + visual.astype(F32)
@@ -239,22 +253,26 @@
     stat_ref[...] = sums.T[: stat_ref.shape[0]]
 
 
-def merge(zy, lifted, pieces, plan, acc, base, up):
+def merge(lifted, acc, base, up, weight):
     tokens, width = acc.shape
-    depth = sum(p.shape[0] for p in pieces)
-    return pl.pallas_call(
-        lambda *refs: merge_kernel(plan, *refs),
-        in_specs=[pl.BlockSpec(memory_space=SMEM)] + [whole()] * (4 + len(pieces)),
+    depth = weight.shape[0]
+    return pl.pallas_call(
+        merge_kernel,
+        in_specs=[whole()] * 4 + [pl.BlockSpec(memory_space=pl.ANY)],
         out_specs=[whole()] * 3,
         out_shape=[
             jax.ShapeDtypeStruct((tokens, width), BF),
             jax.ShapeDtypeStruct((tokens, width), F32),
             jax.ShapeDtypeStruct((8, tokens), F32),
         ],
-        compiler_params=params(16),
-        cost_estimate=cost(2 * depth * tokens * width, 18 * tokens * width),
+        scratch_shapes=[
+            pltpu.VMEM((depth, width), BF),
+            pltpu.SemaphoreType.DMA((depth // BLOCK,)),
+        ],
+        compiler_params=params(18),
+        cost_estimate=cost(2 * depth * tokens * width, 2 * depth * width),
         name="merge",
-    )(zy, lifted, *pieces, acc, base, up)
+    )(lifted, acc, base, up, weight)
 
 
 def pack_kernel(slot_ref, visual_ref, stay_ref, cross_ref):
@@ -278,26 +296,19 @@
     )(slot_row, visual)
 
 
-def assemble_kernel(plan, zy_ref, *refs):
-    for entry, ref in zip(plan, refs[:-1]):
-        refs[-1][place_of(zy_ref, entry)] = ref[...]
-
-
-def assemble(zy, pieces, plan):
-    rows, width = pieces[0].shape
-    return pl.pallas_call(
-        lambda *refs: assemble_kernel(plan, *refs),
-        in_specs=[pl.BlockSpec(memory_space=SMEM)] + [whole()] * len(pieces),
-        out_specs=whole(),
-        out_shape=jax.ShapeDtypeStruct((HALVES, rows, width), BF),
-        compiler_params=params(22),
-        cost_estimate=cost(0, 4 * HALVES * rows * width),
-        name="assemble",
-    )(zy, *pieces)
-
-
-def backward_kernel(full_width, chunks, core_ref, state_ref, up_ref, stat_a_ref, stat_b_ref, w_ref, *refs):
-    picked_ref, sums_ref = refs[-2:]
+def backward_kernel(full_width, chunks, core_ref, state_ref, up_ref, stat_a_ref, stat_b_ref, *refs):
+    weights, outs = refs[:2], refs[2 : 2 + 2 * chunks]
+    picked_ref, sums_ref, held_ref, sems = refs[2 + 2 * chunks :]
+    copies = []
+    for ref in weights:
+        for start in range(0, ref.shape[0], BLOCK):
+            step = len(copies)
+            copies.append(
+                pltpu.make_async_copy(
+                    ref.at[pl.ds(start, BLOCK)], held_ref.at[pl.ds(step * BLOCK, BLOCK)], sems.at[step]
+                )
+            )
+            copies[step].start()
     tokens = state_ref.shape[0]
     half = tokens // 2
     rows = half // chunks
@@ -310,55 +321,60 @@
         inner = sums[:, 1:2] / full_width
         grad = inv * up_ref[at, :] - state_ref[at, :] * (inv * inv * inv * inner)
         picked_ref[place * half : (place + 1) * half, :] = grad.astype(BF)
-    depth = w_ref.shape[0]
-    block = depth // SIDE
-    for step in range(SIDE):
-        cols = slice(step * block, (step + 1) * block)
+    for step, copy in enumerate(copies):
+        cols = slice(step * BLOCK, (step + 1) * BLOCK)
+        copy.wait()
         both = lax.dot_general(
-            picked_ref[...], w_ref[cols, :], (((1,), (1,)), ((), ())), preferred_element_type=F32
+            picked_ref[...], held_ref[cols, :], (((1,), (1,)), ((), ())), preferred_element_type=F32
         )
         for chunk in range(chunks):
-            refs[chunk][:, cols] = both[chunk * rows : (chunk + 1) * rows]
-            refs[chunks + chunk][:, cols] = both[
+            outs[chunk][:, cols] = both[chunk * rows : (chunk + 1) * rows]
+            outs[chunks + chunk][:, cols] = both[
                 half + chunk * rows : half + (chunk + 1) * rows
             ].astype(BF)
 
 
-def backward(core, state, up, stat_a, stat_b, weight, chunks, full_width):
-    depth, width = weight.shape
+def backward(core, state, up, stat_a, stat_b, weights, chunks, full_width):
+    width = weights[0].shape[1]
+    depth = sum(w.shape[0] for w in weights)
     tokens = state.shape[0]
     rows = tokens // 2 // chunks
     return pl.pallas_call(
         lambda *refs: backward_kernel(full_width, chunks, *refs),
-        in_specs=[pl.BlockSpec(memory_space=SMEM)] + [whole()] * 5,
+        in_specs=[pl.BlockSpec(memory_space=SMEM)] + [whole()] * 4
+        + [pl.BlockSpec(memory_space=pl.ANY)] * 2,
         out_specs=[whole()] * (2 * chunks),
         out_shape=[jax.ShapeDtypeStruct((rows, depth), F32)] * chunks
         + [jax.ShapeDtypeStruct((rows, depth), BF)] * chunks,
-        scratch_shapes=[pltpu.VMEM((tokens, width), BF), pltpu.VMEM((tokens, 8), F32)],
-        compiler_params=params(22),
+        scratch_shapes=[
+            pltpu.VMEM((tokens, width), BF),
+            pltpu.VMEM((tokens, 8), F32),
+            pltpu.VMEM((depth, width), BF),
+            pltpu.SemaphoreType.DMA((depth // BLOCK,)),
+        ],
+        compiler_params=params(24),
         cost_estimate=cost(2 * depth * tokens * width, 2 * depth * width),
         name="backward",
-    )(core, state, up, stat_a, stat_b, weight)
+    )(core, state, up, stat_a, stat_b, *weights)
 
 
 def finish_kernel(block_ref, own_ref, far_ref, xw_ref, stat_ref, gain_ref, out_ref):
     window, tokens, width = xw_ref.shape
     full = window * width
     share = width // (SIDE * SIDE)
-    piece = full // HALVES
     mean = stat_ref[:, 0:1]
     inv = stat_ref[:, 1:2]
     lifted = own_ref[...].astype(F32) + far_ref[...].astype(F32)
-    where = {}
-    for index, slices in enumerate(piece_slices(window, share)):
-        for place, key in enumerate(slices):
-            where[key] = index * piece + place * share
+    order = second_half(window, share)
     scaled = []
     total = 0.0
     inner = 0.0
     for w in range(window):
-        starts = [where[(w, at)] for at in range(0, width, share)]
-        g = jnp.concatenate([lifted[:, at : at + share] for at in starts], axis=1)
+        if w < window // 2:
+            g = lifted[:, w * width : (w + 1) * width]
+        else:
+            starts = [full // 2 + i * share for i, (v, _) in enumerate(order) if v == w]
+            g = jnp.concatenate([lifted[:, at : at + share] for at in starts], axis=1)
         g = g * gain_ref[w : w + 1].astype(F32)
         normed = (xw_ref[w].astype(F32) - mean) * inv
         total = total + jnp.sum(g, axis=1, keepdims=True)
@@ -477,10 +493,12 @@
 
     half = window // 2
     share = projection.shape[2]
-    mine_a = projection[0, :half].reshape(half * share, width)
-    mine_b = projection[0, half:].reshape(half * share, width)
-    first_a = [mine_a] + [moved(mine_a, 1, by) for by in (1, -1, 2)]
-    first_b = [mine_b] + [moved(mine_b, 0, by) for by in (1, -1, 2)]
+    first_weight = lax.all_gather(projection[0, :half], "ctx", axis=1, tiled=True)
+    first_weight = first_weight.reshape(-1, width)
+    block = projection[0, half:].reshape(half * share, width)
+    cuts = (block[:, : width // 2], block[:, width // 2 :])
+    moves = (1, -1, 2)
+    near_blocks = [[cuts[part]] + [moved(cuts[part], 1 - part, by) for by in moves] for part in range(2)]
 
     target = slots // tok_rows
     ids = jnp.arange(merged)
@@ -494,11 +512,7 @@
     asked = lax.all_to_all(
         packed.reshape(owners, capacity), ("img", "ctx"), split_axis=0, concat_axis=0, tiled=True
     )
-    asked, first_a, first_b = lax.optimization_barrier((asked, first_a, first_b))
-
-    halves = [stack(zy[1:], first_a), stack(zy[:1], first_b)]
-    before = [[moved(h, part, 1) for h in halves[part]] for part in range(2)]
-    after = [[moved(h, part, -1) for h in halves[part]] for part in range(2)]
+    asked, near_blocks = lax.optimization_barrier((asked, near_blocks))
 
     held = collect(asked.reshape(slot_count, 1), stream, cotangent[0])
     came = lax.all_to_all(
@@ -506,25 +520,20 @@
         ("img", "ctx"), split_axis=0, concat_axis=0, tiled=True,
     ).reshape(slot_count, 2 * width)
 
+    pieces = []
+    for part in range(2):
+        stacked = stack(zy[1 - part : 2 - part], near_blocks[part])
+        pieces += [stacked] + [moved(stacked, part, by) for by in moves]
+
     gain = ln_gain[0]
-    lifted, xw, stat = layer_norm(features[0], gain, ln_bias[0])
-    lifted, before, after = lax.optimization_barrier((lifted, before, after))
-
-    pieces, plan, far_pieces, far_plan = [], [], [], []
-    for part in range(2):
-        for away, sides in ((0, halves[part]), (SIDE - 1, before[part]), (1, after[part])):
-            pieces += sides
-            plan += [(part, away, 0), (part, away, 1)]
-        far_pieces += [moved(before[part][0], part, 1), moved(after[part][1], part, -1)]
-        far_plan += [(part, 2, 0), (part, 2, 1)]
-
-    acc = multiply(zy, lifted, pieces, plan)
+    lifted_first, lifted_second, xw, stat = layer_norm(features[0], gain, ln_bias[0])
+    acc, second_weight = second(zy, lifted_second, pieces)
+    second_weight = second_weight.reshape(-1, width)
     base, up = unpack(slot.reshape(merged, 1), came, norm_gain)
-    visual, state, sums = merge(zy, lifted, far_pieces, far_plan, acc, base, up)
+    visual, state, sums = merge(lifted_first, acc, base, up, first_weight)
 
     near = sums + lax.ppermute(sums, "tp", core_pairs)
     far = lax.ppermute(near, "tp", far_pairs)
-    weight = assemble(zy, pieces + far_pieces, plan + far_plan).reshape(-1, width)
 
     img = lax.axis_index("img").astype(jnp.int32)
     in_img = slot_count // n_img
@@ -533,7 +542,9 @@
     crossed = lax.ppermute(cross, "img", [(i, 1 - i) for i in range(n_img)])
 
     chunks = 2
-    parts = backward(core, state, up, near, far, weight, chunks, full_width)
+    weights = (first_weight, second_weight)
+    parts = backward(core, state, up, near, far, weights, chunks, full_width)
+    parts, crossed = lax.optimization_barrier((parts, crossed))
     pairs = []
     for chunk in range(chunks):
         got = lax.ppermute(parts[chunks + chunk], "tp", core_pairs)

time: 204 us -> 215 us (1.054)
  between operations: 1.18 us -> 14.4 us
  waiting for transfers between devices: 65.2 us -> 73 us
  Pallas kernels: 38 us -> 32.5 us
  blocking collectives: 15.5 us -> 12.3 us
  local copies, waits for them, and re-layouts: 31.3 us -> 29 us
    ppermute x18 -> x12, waiting for transfers between devices: 39.8 us -> 51 us  [moved(): return lax.ppermute(array, 'ctx', pairs)]
    ppermute x1, waiting for transfers between devices: 8.29 us -> 0.01 us  [shards(): crossed = lax.ppermute(cross, 'img', [(i, 1 - i) for i in range(n_img)])]
    ppermute x1, waiting for transfers between devices: 0.01 us -> 6.14 us  [shards(): far = lax.ppermute(near, 'tp', far_pairs)]
    pallas_call x3 -> x2, Pallas kernels: 11.9 us -> 6.41 us  [the longest x1 4.24 us: second(): pl.pallas_call(second_kernel, in_specs=[pl.BlockSpec(memory_space=SMEM),...]
    ppermute x18 -> x12, starting transfers between devices: 27.6 us -> 22.1 us  [moved(): return lax.ppermute(array, 'ctx', pairs)]
    unnamed x86 -> x76, local copies, waits for them, and re-layouts: 29.7 us -> 25.9 us
    all_to_all x1, blocking collectives: 15.5 us -> 12.3 us  [shards(): lax.all_to_all(packed.reshape(owners, capacity), ('img', 'ctx'), split_ax...]
    ppermute x2, starting transfers between devices: 0.8 us -> 3.78 us  [shards(): got = lax.ppermute(parts[chunks + chunk], 'tp', core_pairs)]
  transfers between devices with their start and end apart: 29 -> 24, of which waited for: 10 -> 8; matrix products, arithmetic and copies ran while one was open for 2% -> 3% of each run, Pallas kernels for 13% -> 12%
where the time goes in v4:
time: 215 us
  waiting for transfers between devices  73 us (34%)
  starting transfers between devices  48.5 us (23%)
  Pallas kernels  32.5 us (15%)
  local copies, waits for them, and re-layouts  29 us (13%)
  between operations  14.4 us (7%)
  blocking collectives  12.3 us (6%)
  other arithmetic  4.84 us (2%)
    ppermute x12, waiting for transfers between devices, moved(): return lax.ppermute(array, 'ctx', pairs)  51 us
    unnamed x76, local copies, waits for them, and re-layouts  25.9 us
    ppermute x12, starting transfers between devices, moved(): return lax.ppermute(array, 'ctx', pairs)  22.1 us
    ppermute x2, waiting for transfers between devices, shards(): beyond = [lax.ppermute(pair, 'tp', far_pairs) for pair in pairs]  13.4 us
    all_to_all x1, blocking collectives, shards(): lax.all_to_all(packed.reshape(owners, capacity), ('img', 'ctx'), split_ax...  12.3 us
    ppermute x1, waiting for transfers between devices, shards(): far = lax.ppermute(near, 'tp', far_pairs)  6.14 us
    pallas_call x1, Pallas kernels, backward(): pl.pallas_call(lambda *refs: backward_kernel(full_width, chunks, *refs),...  5.55 us
    pallas_call x2, Pallas kernels, finish(): pl.pallas_call(finish_kernel, grid_spec=pltpu.PrefetchScalarGridSpec(num_...  4.94 us
  transfers between devices with their start and end apart: 24, of which 8 were waited for; matrix products, arithmetic and copies ran while one was open for 3% of the time, Pallas kernels for 12%

profile of v4, /device:TPU:1, one launch (start us, length us, event | category | flops | bytes accessed | tf_op | source)
XLA Modules:
  0.0 214.5 jit_solution(324339945168570873)
XLA Ops:
  7.2 1.9 fusion.2
  9.2 2.2 %collective-permute-start = (bf16[144,512]{1,0:T(8,128)(2,1)S(1)}, bf16[144,512]{1,0:T(8,128)(2,1)S(1)}, u32[]{:S(2)}, u32[]{:S(2)}) collective-permute-start(bf16[144,512]{1,0:T(8,128)(2,1)S(1)} %get-tuple-element.39.refs_0_), channel_id=1, source_target_pairs={{0,4},{4,8},{8,12},{12,0},{16,20},{20,24},{24,28},{28,16},{32,36},... | collective-permute-start | bytes 442376 | tf_op jit(solution)/shard_map/ppermute | solution.py:492
  11.4 1.5 collective-permute-start.1
  12.9 1.6 collective-permute-start.2
  15.2 1.6 collective-permute-start.3
  16.8 2.1 collective-permute-start.4
  20.4 1.3 collective-permute-start.5
  22.5 12.3 %all_to_all.22 = s32[32,1,16]{2,1,0:T(1,128)S(1)} all-to-all(s32[32,1,16]{2,1,0:T(1,128)S(1)} %bitcast.38), channel_id=1, replica_groups=mesh['img'=2,'ctx'=16,'tp'=4] {'img','ctx'}, dimensions={0} | all-to-all | bytes 4096 | tf_op jit(solution)/shard_map/all_to_all | solution.py:512
  35.0 2.6 %collect.1 = bf16[512,2048]{1,0:T(8,128)(2,1)} custom-call(s32[512,1]{1,0:T(8,128)S(1)} %reshape.69.pos_ref, bf16[512,1024]{1,0:T(8,128)(2,1)S(1)} %copy-done.4, bf16[512,1024]{1,0:T(8,128)(2,1)S(1)} %bitcast.27), custom_call_target="tpu_custom_call" | custom-call | flops 1073741824 | bytes 4194304 | tf_op jit(solution)/shard_map/collect/pallas_call | solution.py:124
  37.7 4.9 %all-to-all-start.1 = ((bf16[32,16,2048]{2,1,0:T(8,128)(2,1)}), bf16[32,16,2048]{2,1,0:T(8,128)(2,1)}, u32[]{:S(2)}, u32[]{:S(2)}) async-start(bf16[32,16,2048]{2,1,0:T(8,128)(2,1)} %bitcast.14), calls=%async_computation.1 | async-start | bytes 4194304 | tf_op jit(solution)/shard_map/all_to_all | solution.py:518
  42.7 2.3 %collective-permute-start.10 = (bf16[4,144,512]{2,1,0:T(8,128)(2,1)S(1)}, bf16[4,144,512]{2,1,0:T(8,128)(2,1)S(1)}, u32[]{:S(2)}, u32[]{:S(2)}) collective-permute-start(bf16[4,144,512]{2,1,0:T(8,128)(2,1)S(1)} %stack.27.refs_4_), channel_id=1, source_target_pairs={{0,12},{4,0},{8,4},{12,8},{16,28},{20,16},{24,20},{28,24},{32,44},... | collective-permute-start | bytes 1769480 | tf_op jit(solution)/shard_map/ppermute | solution.py:492
  46.3 1.3 collective-permute-start.6
  47.5 1.5 collective-permute-start.7
  49.0 46.6 %collective-permute-done.10.refs_6_ = bf16[4,144,512]{2,1,0:T(8,128)(2,1)S(1)} collective-permute-done((bf16[4,144,512]{2,1,0:T(8,128)(2,1)S(1)}, bf16[4,144,512]{2,1,0:T(8,128)(2,1)S(1)}, u32[]{:S(2)}, u32[]{:S(2)}) %collective-permute-start.10) | collective-permute-done | bytes 589856 | tf_op jit(solution)/shard_map/ppermute | solution.py:492
  96.4 5.6 %collective-permute-start.8 = (bf16[4,144,512]{2,1,0:T(8,128)(2,1)S(1)}, bf16[4,144,512]{2,1,0:T(8,128)(2,1)}, u32[]{:S(2)}, u32[]{:S(2)}) collective-permute-start(bf16[4,144,512]{2,1,0:T(8,128)(2,1)S(1)} %stack.26.refs_0_), channel_id=1, source_target_pairs={{0,32},{4,36},{8,40},{12,44},{16,48},{20,52},{24,56},{28,60},{32,0... | collective-permute-start | bytes 1769480 | tf_op jit(solution)/shard_map/ppermute | solution.py:492
  102.8 1.7 copy-done.6
  105.1 3.5 %layer_norm.1 = (bf16[256,2304]{1,0:T(8,128)(2,1)S(1)}, bf16[256,2304]{1,0:T(8,128)(2,1)S(1)}, bf16[4,256,1152]{2,1,0:T(8,128)(2,1)S(1)}, f32[256,128]{1,0:T(8,128)S(1)}) custom-call(bf16[1024,1152]{1,0:T(8,128)(2,1)S(1)} %bitcast.26, bf16[4,1152]{1,0:T(4,128)(2,1)S(1)} %bitcast.29, bf16[4,1152]{1,0:T(4,128)(2,1)S(1)} %bitcast.32), custom_call_target="tpu_custom_call" | custom-call | flops 603979776 | bytes 7077888 | tf_op jit(solution)/shard_map/layer_norm/pallas_call | solution.py:87
  110.5 4.4 %collective-permute-done.8.refs_3_ = bf16[4,144,512]{2,1,0:T(8,128)(2,1)} collective-permute-done((bf16[4,144,512]{2,1,0:T(8,128)(2,1)S(1)}, bf16[4,144,512]{2,1,0:T(8,128)(2,1)}, u32[]{:S(2)}, u32[]{:S(2)}) %collective-permute-start.8) | collective-permute-done | bytes 589856 | tf_op jit(solution)/shard_map/ppermute | solution.py:492
  114.9 4.2 %second.1 = (f32[256,1024]{1,0:T(8,128)S(1)}, bf16[4,4,144,1024]{3,2,1,0:T(8,128)(2,1)S(1)}) custom-call(s32[2]{0:T(128)S(1)} %pad_add_fusion.1.zy_ref, bf16[256,2304]{1,0:T(8,128)(2,1)S(1)} %get-tuple-element.38.lifted_ref, bf16[4,144,512]{2,1,0:T(8,128)(2,1)S(1)} %stack.26.refs_0_, bf16[4,144,512]{2,1,0:T(8,128)(2,1)} %collective-permute-done.6.refs_1_, ...), custom_call_target="tpu_custom_call" | custom-call | flops 1207959552 | bytes 14155776 | tf_op jit(solution)/shard_map/second/pallas_call | solution.py:208
  119.2 2.2 %copy-done.2 = bf16[4,4,144,1024]{3,2,1,0:T(8,128)(2,1)} copy-done((bf16[4,4,144,1024]{3,2,1,0:T(8,128)(2,1)}, bf16[4,4,144,1024]{3,2,1,0:T(8,128)(2,1)S(1)}, u32[]{:S(2)}) %copy-start.2) | copy-done | bytes 4718616
  123.2 2.3 %unpack.1 = (f32[256,1024]{1,0:T(8,128)S(1)}, f32[256,1024]{1,0:T(8,128)S(1)}) custom-call(s32[256,1]{1,0:T(8,128)S(1)} %copy-done.23, bf16[512,2048]{1,0:T(8,128)(2,1)} %bitcast.15.came_ref, bf16[1,1024]{1,0:T(2,128)(2,1)S(1)} %copy-done.34), custom_call_target="tpu_custom_call" | custom-call | flops 536870912 | bytes 2097152 | tf_op jit(solution)/shard_map/unpack/pallas_call | solution.py:149
  126.5 2.3 %copy-done = bf16[1,2,1152,1024]{3,2,1,0:T(8,128)(2,1)S(1)} copy-done((bf16[1,2,1152,1024]{3,2,1,0:T(8,128)(2,1)S(1)}, bf16[1,2,1152,1024]{3,2,1,0:T(8,128)(2,1)}, u32[]{:S(2)}) %copy-start) | copy-done | bytes 4718616
  128.9 1.3 copy-done.8
  130.1 1.2 copy-done.13
  131.4 1.2 copy-done.15
  132.6 2.2 %merge.1 = (bf16[256,1024]{1,0:T(8,128)(2,1)S(1)}, f32[256,1024]{1,0:T(8,128)S(1)}, f32[8,256]{1,0:T(8,128)S(1)}) custom-call(bf16[256,2304]{1,0:T(8,128)(2,1)S(1)} %copy-done.8, f32[256,1024]{1,0:T(8,128)S(1)} %copy-done.13, f32[256,1024]{1,0:T(8,128)S(1)} %copy-done.15, f32[256,1024]{1,0:T(8,128)S(1)} %get-tuple-element.49.up_ref.refs_2_, ...), custom_call_target="tpu_custom_call" | custom-call | flops 1207959552 | bytes 4718592 | tf_op jit(solution)/shard_map/merge/pallas_call | solution.py:259
  135.7 1.2 pack.1
  137.8 1.8 collective-permute-start.14
  139.6 2.7 %collective-permute-start.12 = (f32[8,256]{1,0:T(8,128)S(1)}, f32[8,256]{1,0:T(8,128)S(1)}, u32[]{:S(2)}, u32[]{:S(2)}) collective-permute-start(f32[8,256]{1,0:T(8,128)S(1)} %get-tuple-element.53), channel_id=1, source_target_pairs={{0,1},{1,0},{2,3},{3,2},{4,5},{5,4},{6,7},{7,6},{8,9},{9,8},{10,11... | collective-permute-start | bytes 24584 | tf_op jit(solution)/shard_map/ppermute | solution.py:535
  143.1 2.5 %collective-permute-start.13 = (f32[8,256]{1,0:T(8,128)S(1)}, f32[8,256]{1,0:T(8,128)S(1)}, u32[]{:S(2)}, u32[]{:S(2)}) collective-permute-start(f32[8,256]{1,0:T(8,128)S(1)} %add.45.refs_3_), channel_id=1, source_target_pairs={{0,2},{1,3},{2,0},{3,1},{4,6},{5,7},{6,4},{7,5},{8,10},{9,11},{10,... | collective-permute-start | bytes 24584 | tf_op jit(solution)/shard_map/ppermute | solution.py:536
  145.5 6.1 %collective-permute-done.13.refs_4_ = f32[8,256]{1,0:T(8,128)S(1)} collective-permute-done((f32[8,256]{1,0:T(8,128)S(1)}, f32[8,256]{1,0:T(8,128)S(1)}, u32[]{:S(2)}, u32[]{:S(2)}) %collective-permute-start.13) | collective-permute-done | bytes 8224 | tf_op jit(solution)/shard_map/ppermute | solution.py:536
  151.7 2.3 %copy-done.1 = bf16[1,2,1152,1024]{3,2,1,0:T(8,128)(2,1)S(1)} copy-done((bf16[1,2,1152,1024]{3,2,1,0:T(8,128)(2,1)S(1)}, bf16[1,2,1152,1024]{3,2,1,0:T(8,128)(2,1)}, u32[]{:S(2)}) %copy-start.1) | copy-done | bytes 4718616
  154.0 2.3 %copy-done.3 = bf16[4,4,144,1024]{3,2,1,0:T(8,128)(2,1)S(1)} copy-done((bf16[4,4,144,1024]{3,2,1,0:T(8,128)(2,1)S(1)}, bf16[4,4,144,1024]{3,2,1,0:T(8,128)(2,1)}, u32[]{:S(2)}) %copy-start.3) | copy-done | bytes 4718616
  156.3 1.2 copy-done.11
  157.6 5.5 %backward.1 = (f32[64,4608]{1,0:T(8,128)S(1)}, f32[64,4608]{1,0:T(8,128)S(1)}, bf16[64,4608]{1,0:T(8,128)(2,1)S(1)}, bf16[64,4608]{1,0:T(8,128)(2,1)S(1)}) custom-call(s32[1]{0:T(128)} %bitcast.17.refs_0_.core_ref, f32[256,1024]{1,0:T(8,128)S(1)} %copy-done.11, f32[256,1024]{1,0:T(8,128)S(1)} %get-tuple-element.49.up_ref.refs_2_, f32[8,256]{1,0:T(8,128)S(1)} %add.45.refs_3_, ...), custom_call_target="tpu_custom_call" | custom-call | flops 2415919104 | bytes 9437184 | tf_op jit(solution)/shard_map/backward/pallas_call | solution.py:342
  163.1 3.7 %collective-permute-start.17 = (bf16[64,4608]{1,0:T(8,128)(2,1)S(1)}, bf16[64,4608]{1,0:T(8,128)(2,1)S(1)}, u32[]{:S(2)}, u32[]{:S(2)}) collective-permute-start(bf16[64,4608]{1,0:T(8,128)(2,1)S(1)} %get-tuple-element.69), channel_id=1, source_target_pairs={{0,1},{1,0},{2,3},{3,2},{4,5},{5,4},{6,7},{7,6},{8,9},{9,8},{10,11... | collective-permute-start | bytes 1769480 | tf_op jit(solution)/shard_map/ppermute | solution.py:550
  166.9 1.5 collective-permute-done.17
  170.2 2.3 %collective-permute-start.16 = (bf16[64,4608]{1,0:T(8,128)(2,1)}, bf16[64,4608]{1,0:T(8,128)(2,1)}, u32[]{:S(2)}, u32[]{:S(2)}) collective-permute-start(bf16[64,4608]{1,0:T(8,128)(2,1)} %add_convert_fusion.1.own_ref), channel_id=1, source_target_pairs={{0,2},{1,3},{2,0},{3,1},{4,6},{5,7},{6,4},{7,5},{8,10},{9,11},{10,... | collective-permute-start | bytes 1769480 | tf_op jit(solution)/shard_map/ppermute | solution.py:552
  172.6 2.1 pad_maximum_fusion
  174.7 4.6 %all-to-all-start.2 = ((bf16[16,32,1024]{2,1,0:T(8,128)(2,1)}), bf16[16,32,1024]{2,1,0:T(8,128)(2,1)}, u32[]{:S(2)}, u32[]{:S(2)}) async-start(bf16[16,32,1024]{2,1,0:T(8,128)(2,1)} %pad_maximum_fusion), calls=%async_computation.2 | async-start | bytes 2097152 | tf_op jit(solution)/shard_map/all_to_all | solution.py:558
  179.3 5.4 %collective-permute-done.18.far_ref = bf16[64,4608]{1,0:T(8,128)(2,1)S(1)} collective-permute-done((bf16[64,4608]{1,0:T(8,128)(2,1)S(1)}, bf16[64,4608]{1,0:T(8,128)(2,1)S(1)}, u32[]{:S(2)}, u32[]{:S(2)}) %collective-permute-start.18) | collective-permute-done | bytes 589856 | tf_op jit(solution)/shard_map/ppermute | solution.py:552
  185.6 1.9 finish.3.refs_1_
  187.5 2.0 collective-permute-start.20
  189.5 8.0 %collective-permute-done.16.far_ref = bf16[64,4608]{1,0:T(8,128)(2,1)} collective-permute-done((bf16[64,4608]{1,0:T(8,128)(2,1)}, bf16[64,4608]{1,0:T(8,128)(2,1)}, u32[]{:S(2)}, u32[]{:S(2)}) %collective-permute-start.16) | collective-permute-done | bytes 589856 | tf_op jit(solution)/shard_map/ppermute | solution.py:552
  197.5 3.1 %finish.2.refs_0_ = bf16[256,1152]{1,0:T(8,128)(2,1)} custom-call(s32[1]{0:T(128)S(6)} %mul.20.block_ref, bf16[64,4608]{1,0:T(8,128)(2,1)} %add_convert_fusion.1.own_ref, bf16[64,4608]{1,0:T(8,128)(2,1)} %collective-permute-done.16.far_ref, bf16[4,256,1152]{2,1,0:T(8,128)(2,1)S(1)} %get-tuple-element.66.xw_ref, f32[256,128]{1,0:T(8,128)S(1)} %copy-done.22, ...), custom_call_target="tpu_custom_call" | custom-call | flops 150994944 | bytes 2359296 | tf_op jit(solution)/shard_map/finish/pallas_call | solution.py:396
  200.6 1.2 collective-permute-start.19
  201.9 2.9 %place.1 = bf16[512,1024]{1,0:T(8,128)(2,1)} custom-call(s32[1,512]{1,0:T(1,128)S(1)} %reshape.55.pos_ref, bf16[512,1024]{1,0:T(8,128)(2,1)} %bitcast.21.came_ref, bf16[512,1024]{1,0:T(8,128)(2,1)S(1)} %copy-done.5), custom_call_target="tpu_custom_call" | custom-call | flops 536870912 | bytes 3145728 | tf_op jit(solution)/shard_map/place/pallas_call | solution.py:428
  204.8 2.9 %lay.1 = bf16[1024,1152]{1,0:T(8,128)(2,1)} custom-call(s32[1]{0:T(128)} %bitcast.17.refs_0_.core_ref, bf16[256,1152]{1,0:T(8,128)(2,1)} %finish.2.refs_0_, bf16[256,1152]{1,0:T(8,128)(2,1)} %finish.3.refs_1_, bf16[256,1152]{1,0:T(8,128)(2,1)S(1)} %collective-permute-done.19.refs_2_, bf16[256,1152]{1,0:T(8,128)(2,1)} %collective-permute-done.20.refs_3_), custom_call_target="tpu_custom_call" | custom-call | bytes 4718592 | tf_op jit(solution)/shard_map/lay/pallas_call | solution.py:456
  (108 shorter events, 17.0 us)
Async XLA Ops:
  7.2 27.9 %copy-start.9 = (bf16[1,512,1024]{2,1,0:T(8,128)(2,1)S(1)}, bf16[1,512,1024]{2,1,0:T(8,128)(2,1)}, u32[]{:S(2)}) copy-start(bf16[1,512,1024]{2,1,0:T(8,128)(2,1)} %param.14) | copy-start | bytes 3145732
  7.2 27.9 %copy-start.4 = (bf16[512,1024]{1,0:T(8,128)(2,1)S(1)}, bf16[512,1024]{1,0:T(8,128)(2,1)}, u32[]{:S(2)}) copy-start(bf16[512,1024]{1,0:T(8,128)(2,1)} %stream_ref.3) | copy-start | bytes 3145732
  7.2 119.3 %all-gather.3.cloned.1.call-start = ((), (), s32[]{:S(2)}) async-start(), calls=%async_computation.3 | async-start | bytes 5013504 | tf_op jit(solution)/shard_map/all_gather | solution.py:496
  9.2 10.5 %collective-permute-start = (bf16[144,512]{1,0:T(8,128)(2,1)S(1)}, bf16[144,512]{1,0:T(8,128)(2,1)S(1)}, u32[]{:S(2)}, u32[]{:S(2)}) collective-permute-start(bf16[144,512]{1,0:T(8,128)(2,1)S(1)} %get-tuple-element.39.refs_0_), channel_id=1, source_target_pairs={{0,4},{4,8},{8,12},{12,0},{16,20},{20,24},{24,28},{28,16},{32,36},... | collective-permute-start | bytes 442376 | tf_op jit(solution)/shard_map/ppermute | solution.py:492
  11.4 23.4 %collective-permute-start.1 = (bf16[144,512]{1,0:T(8,128)(2,1)S(1)}, bf16[144,512]{1,0:T(8,128)(2,1)S(1)}, u32[]{:S(2)}, u32[]{:S(2)}) collective-permute-start(bf16[144,512]{1,0:T(8,128)(2,1)S(1)} %get-tuple-element.39.refs_0_), channel_id=1, source_target_pairs={{0,12},{4,0},{8,4},{12,8},{16,28},{20,16},{24,20},{28,24},{32,44},... | collective-permute-start | bytes 442376 | tf_op jit(solution)/shard_map/ppermute | solution.py:492
  12.9 21.9 %collective-permute-start.2 = (bf16[144,512]{1,0:T(8,128)(2,1)S(1)}, bf16[144,512]{1,0:T(8,128)(2,1)S(1)}, u32[]{:S(2)}, u32[]{:S(2)}) collective-permute-start(bf16[144,512]{1,0:T(8,128)(2,1)S(1)} %get-tuple-element.39.refs_0_), channel_id=1, source_target_pairs={{0,8},{4,12},{8,0},{12,4},{16,24},{20,28},{24,16},{28,20},{32,40},... | collective-permute-start | bytes 442376 | tf_op jit(solution)/shard_map/ppermute | solution.py:492
  15.2 19.7 %collective-permute-start.3 = (bf16[144,512]{1,0:T(8,128)(2,1)S(1)}, bf16[144,512]{1,0:T(8,128)(2,1)S(1)}, u32[]{:S(2)}, u32[]{:S(2)}) collective-permute-start(bf16[144,512]{1,0:T(8,128)(2,1)S(1)} %get-tuple-element.43.refs_0_), channel_id=1, source_target_pairs={{0,16},{4,20},{8,24},{12,28},{16,32},{20,36},{24,40},{28,44},{32,4... | collective-permute-start | bytes 442376 | tf_op jit(solution)/shard_map/ppermute | solution.py:492
  16.8 18.1 %collective-permute-start.4 = (bf16[144,512]{1,0:T(8,128)(2,1)S(1)}, bf16[144,512]{1,0:T(8,128)(2,1)S(1)}, u32[]{:S(2)}, u32[]{:S(2)}) collective-permute-start(bf16[144,512]{1,0:T(8,128)(2,1)S(1)} %get-tuple-element.43.refs_0_), channel_id=1, source_target_pairs={{0,48},{4,52},{8,56},{12,60},{16,0},{20,4},{24,8},{28,12},{32,16},... | collective-permute-start | bytes 442376 | tf_op jit(solution)/shard_map/ppermute | solution.py:492
  20.4 14.5 %collective-permute-start.5 = (bf16[144,512]{1,0:T(8,128)(2,1)S(1)}, bf16[144,512]{1,0:T(8,128)(2,1)S(1)}, u32[]{:S(2)}, u32[]{:S(2)}) collective-permute-start(bf16[144,512]{1,0:T(8,128)(2,1)S(1)} %get-tuple-element.43.refs_0_), channel_id=1, source_target_pairs={{0,32},{4,36},{8,40},{12,44},{16,48},{20,52},{24,56},{28,60},{32,0... | collective-permute-start | bytes 442376 | tf_op jit(solution)/shard_map/ppermute | solution.py:492
  34.8 2.9 %copy-start.36 = (s32[32,1,16]{2,1,0:T(1,128)}, s32[32,1,16]{2,1,0:T(1,128)S(1)}, u32[]{:S(2)}) copy-start(s32[32,1,16]{2,1,0:T(1,128)S(1)} %all_to_all.22) | copy-start | bytes 6148
  34.8 2.9 %copy-start.28 = (bf16[144,512]{1,0:T(8,128)(2,1)}, bf16[144,512]{1,0:T(8,128)(2,1)S(1)}, u32[]{:S(2)}) copy-start(bf16[144,512]{1,0:T(8,128)(2,1)S(1)} %collective-permute-done.1.refs_2_) | copy-start | bytes 442372
  34.8 2.9 %copy-start.30 = (bf16[144,512]{1,0:T(8,128)(2,1)}, bf16[144,512]{1,0:T(8,128)(2,1)S(1)}, u32[]{:S(2)}) copy-start(bf16[144,512]{1,0:T(8,128)(2,1)S(1)} %collective-permute-done.2.refs_3_) | copy-start | bytes 442372
  37.7 8.5 %copy-start.19 = (bf16[144,512]{1,0:T(8,128)(2,1)S(1)}, bf16[144,512]{1,0:T(8,128)(2,1)}, u32[]{:S(2)}) copy-start(bf16[144,512]{1,0:T(8,128)(2,1)} %copy-done.18) | copy-start | bytes 442372
  37.7 8.5 %copy-start.27 = (bf16[144,512]{1,0:T(8,128)(2,1)S(1)}, bf16[144,512]{1,0:T(8,128)(2,1)}, u32[]{:S(2)}) copy-start(bf16[144,512]{1,0:T(8,128)(2,1)} %copy-done.26) | copy-start | bytes 442372
  37.7 8.5 %copy-start.29 = (bf16[144,512]{1,0:T(8,128)(2,1)S(1)}, bf16[144,512]{1,0:T(8,128)(2,1)}, u32[]{:S(2)}) copy-start(bf16[144,512]{1,0:T(8,128)(2,1)} %copy-done.28) | copy-start | bytes 442372
  37.7 8.5 %copy-start.31 = (bf16[144,512]{1,0:T(8,128)(2,1)S(1)}, bf16[144,512]{1,0:T(8,128)(2,1)}, u32[]{:S(2)}) copy-start(bf16[144,512]{1,0:T(8,128)(2,1)} %copy-done.30) | copy-start | bytes 442372
  37.7 84.6 %all-to-all-start.1 = ((bf16[32,16,2048]{2,1,0:T(8,128)(2,1)}), bf16[32,16,2048]{2,1,0:T(8,128)(2,1)}, u32[]{:S(2)}, u32[]{:S(2)}) async-start(bf16[32,16,2048]{2,1,0:T(8,128)(2,1)} %bitcast.14), calls=%async_computation.1 | async-start | bytes 4194304 | tf_op jit(solution)/shard_map/all_to_all | solution.py:518
  42.6 60.1 %copy-start.32 = (bf16[1,4,1152]{2,1,0:T(4,128)(2,1)S(1)}, bf16[1,4,1152]{2,1,0:T(4,128)(2,1)}, u32[]{:S(2)}) copy-start(bf16[1,4,1152]{2,1,0:T(4,128)(2,1)} %param.9) | copy-start | bytes 27652
  42.7 52.9 %collective-permute-start.10 = (bf16[4,144,512]{2,1,0:T(8,128)(2,1)S(1)}, bf16[4,144,512]{2,1,0:T(8,128)(2,1)S(1)}, u32[]{:S(2)}, u32[]{:S(2)}) collective-permute-start(bf16[4,144,512]{2,1,0:T(8,128)(2,1)S(1)} %stack.27.refs_4_), channel_id=1, source_target_pairs={{0,12},{4,0},{8,4},{12,8},{16,28},{20,16},{24,20},{28,24},{32,44},... | collective-permute-start | bytes 1769480 | tf_op jit(solution)/shard_map/ppermute | solution.py:492
  45.1 65.4 %collective-permute-start.11 = (bf16[4,144,512]{2,1,0:T(8,128)(2,1)S(1)}, bf16[4,144,512]{2,1,0:T(8,128)(2,1)}, u32[]{:S(2)}, u32[]{:S(2)}) collective-permute-start(bf16[4,144,512]{2,1,0:T(8,128)(2,1)S(1)} %stack.27.refs_4_), channel_id=1, source_target_pairs={{0,8},{4,12},{8,0},{12,4},{16,24},{20,28},{24,16},{28,20},{32,40},... | collective-permute-start | bytes 1769480 | tf_op jit(solution)/shard_map/ppermute | solution.py:492
  45.6 64.9 %collective-permute-start.9 = (bf16[4,144,512]{2,1,0:T(8,128)(2,1)S(1)}, bf16[4,144,512]{2,1,0:T(8,128)(2,1)}, u32[]{:S(2)}, u32[]{:S(2)}) collective-permute-start(bf16[4,144,512]{2,1,0:T(8,128)(2,1)S(1)} %stack.27.refs_4_), channel_id=1, source_target_pairs={{0,4},{4,8},{8,12},{12,0},{16,20},{20,24},{24,28},{28,16},{32,36},... | collective-permute-start | bytes 1769480 | tf_op jit(solution)/shard_map/ppermute | solution.py:492
  46.3 64.2 %collective-permute-start.6 = (bf16[4,144,512]{2,1,0:T(8,128)(2,1)S(1)}, bf16[4,144,512]{2,1,0:T(8,128)(2,1)}, u32[]{:S(2)}, u32[]{:S(2)}) collective-permute-start(bf16[4,144,512]{2,1,0:T(8,128)(2,1)S(1)} %stack.26.refs_0_), channel_id=1, source_target_pairs={{0,16},{4,20},{8,24},{12,28},{16,32},{20,36},{24,40},{28,44},{32,4... | collective-permute-start | bytes 1769480 | tf_op jit(solution)/shard_map/ppermute | solution.py:492
  47.5 62.9 %collective-permute-start.7 = (bf16[4,144,512]{2,1,0:T(8,128)(2,1)S(1)}, bf16[4,144,512]{2,1,0:T(8,128)(2,1)}, u32[]{:S(2)}, u32[]{:S(2)}) collective-permute-start(bf16[4,144,512]{2,1,0:T(8,128)(2,1)S(1)} %stack.26.refs_0_), channel_id=1, source_target_pairs={{0,48},{4,52},{8,56},{12,60},{16,0},{20,4},{24,8},{28,12},{32,16},... | collective-permute-start | bytes 1769480 | tf_op jit(solution)/shard_map/ppermute | solution.py:492
  96.4 18.5 %collective-permute-start.8 = (bf16[4,144,512]{2,1,0:T(8,128)(2,1)S(1)}, bf16[4,144,512]{2,1,0:T(8,128)(2,1)}, u32[]{:S(2)}, u32[]{:S(2)}) collective-permute-start(bf16[4,144,512]{2,1,0:T(8,128)(2,1)S(1)} %stack.26.refs_0_), channel_id=1, source_target_pairs={{0,32},{4,36},{8,40},{12,44},{16,48},{20,52},{24,56},{28,60},{32,0... | collective-permute-start | bytes 1769480 | tf_op jit(solution)/shard_map/ppermute | solution.py:492
  102.8 1.7 copy-start.6
  105.1 9.8 %copy-start.17 = (bf16[4,144,512]{2,1,0:T(8,128)(2,1)S(1)}, bf16[4,144,512]{2,1,0:T(8,128)(2,1)}, u32[]{:S(2)}) copy-start(bf16[4,144,512]{2,1,0:T(8,128)(2,1)} %copy-done.16) | copy-start | bytes 1769476
  114.9 7.4 %copy-start.34 = (bf16[1,1024]{1,0:T(2,128)(2,1)S(1)}, bf16[1,1024]{1,0:T(2,128)(2,1)}, u32[]{:S(2)}) copy-start(bf16[1,1024]{1,0:T(2,128)(2,1)} %ngain_ref.1) | copy-start | bytes 6148
  119.2 2.2 %copy-start.2 = (bf16[4,4,144,1024]{3,2,1,0:T(8,128)(2,1)}, bf16[4,4,144,1024]{3,2,1,0:T(8,128)(2,1)S(1)}, u32[]{:S(2)}) copy-start(bf16[4,4,144,1024]{3,2,1,0:T(8,128)(2,1)S(1)} %get-tuple-element.54) | copy-start | bytes 14155780
  126.5 2.3 %copy-start = (bf16[1,2,1152,1024]{3,2,1,0:T(8,128)(2,1)S(1)}, bf16[1,2,1152,1024]{3,2,1,0:T(8,128)(2,1)}, u32[]{:S(2)}) copy-start(bf16[1,2,1152,1024]{3,2,1,0:T(8,128)(2,1)} %all-gather.3.cloned.1.call-done) | copy-start | bytes 14155780
  128.9 1.3 copy-start.8
  130.1 1.2 copy-start.13
  132.6 3.2 %copy-start.35 = (s32[256]{0:T(256)S(1)}, s32[256]{0:T(256)}, u32[]{:S(2)}) copy-start(s32[256]{0:T(256)} %get-tuple-element.70) | copy-start | bytes 3076
  137.8 25.3 %collective-permute-start.14 = (bf16[256,1024]{1,0:T(8,128)(2,1)}, bf16[256,1024]{1,0:T(8,128)(2,1)}, u32[]{:S(2)}, u32[]{:S(2)}) collective-permute-start(bf16[256,1024]{1,0:T(8,128)(2,1)} %get-tuple-element.59), channel_id=1, source_target_pairs={{0,64},{64,0},{1,65},{65,1},{2,66},{66,2},{3,67},{67,3},{4,68},{68... | collective-permute-start | bytes 1572872 | tf_op jit(solution)/shard_map/ppermute | solution.py:542
  139.6 3.5 %collective-permute-start.12 = (f32[8,256]{1,0:T(8,128)S(1)}, f32[8,256]{1,0:T(8,128)S(1)}, u32[]{:S(2)}, u32[]{:S(2)}) collective-permute-start(f32[8,256]{1,0:T(8,128)S(1)} %get-tuple-element.53), channel_id=1, source_target_pairs={{0,1},{1,0},{2,3},{3,2},{4,5},{5,4},{6,7},{7,6},{8,9},{9,8},{10,11... | collective-permute-start | bytes 24584 | tf_op jit(solution)/shard_map/ppermute | solution.py:535
  143.1 8.6 %collective-permute-start.13 = (f32[8,256]{1,0:T(8,128)S(1)}, f32[8,256]{1,0:T(8,128)S(1)}, u32[]{:S(2)}, u32[]{:S(2)}) collective-permute-start(f32[8,256]{1,0:T(8,128)S(1)} %add.45.refs_3_), channel_id=1, source_target_pairs={{0,2},{1,3},{2,0},{3,1},{4,6},{5,7},{6,4},{7,5},{8,10},{9,11},{10,... | collective-permute-start | bytes 24584 | tf_op jit(solution)/shard_map/ppermute | solution.py:536
  151.7 2.3 %copy-start.1 = (bf16[1,2,1152,1024]{3,2,1,0:T(8,128)(2,1)S(1)}, bf16[1,2,1152,1024]{3,2,1,0:T(8,128)(2,1)}, u32[]{:S(2)}) copy-start(bf16[1,2,1152,1024]{3,2,1,0:T(8,128)(2,1)} %all-gather.3.cloned.1.call-done) | copy-start | bytes 14155780
  154.0 2.3 %copy-start.3 = (bf16[4,4,144,1024]{3,2,1,0:T(8,128)(2,1)S(1)}, bf16[4,4,144,1024]{3,2,1,0:T(8,128)(2,1)}, u32[]{:S(2)}) copy-start(bf16[4,4,144,1024]{3,2,1,0:T(8,128)(2,1)} %copy-done.2) | copy-start | bytes 14155780
  163.1 9.5 %copy-start.25 = (bf16[256,1024]{1,0:T(8,128)(2,1)S(1)}, bf16[256,1024]{1,0:T(8,128)(2,1)}, u32[]{:S(2)}) copy-start(bf16[256,1024]{1,0:T(8,128)(2,1)} %copy-done.24) | copy-start | bytes 1572868
  163.1 5.3 %collective-permute-start.17 = (bf16[64,4608]{1,0:T(8,128)(2,1)S(1)}, bf16[64,4608]{1,0:T(8,128)(2,1)S(1)}, u32[]{:S(2)}, u32[]{:S(2)}) collective-permute-start(bf16[64,4608]{1,0:T(8,128)(2,1)S(1)} %get-tuple-element.69), channel_id=1, source_target_pairs={{0,1},{1,0},{2,3},{3,2},{4,5},{5,4},{6,7},{7,6},{8,9},{9,8},{10,11... | collective-permute-start | bytes 1769480 | tf_op jit(solution)/shard_map/ppermute | solution.py:550
  166.8 2.5 %collective-permute-start.15 = (bf16[64,4608]{1,0:T(8,128)(2,1)S(1)}, bf16[64,4608]{1,0:T(8,128)(2,1)S(1)}, u32[]{:S(2)}, u32[]{:S(2)}) collective-permute-start(bf16[64,4608]{1,0:T(8,128)(2,1)S(1)} %get-tuple-element.62), channel_id=1, source_target_pairs={{0,1},{1,0},{2,3},{3,2},{4,5},{5,4},{6,7},{7,6},{8,9},{9,8},{10,11... | collective-permute-start | bytes 1769480 | tf_op jit(solution)/shard_map/ppermute | solution.py:550
  168.6 16.1 %collective-permute-start.18 = (bf16[64,4608]{1,0:T(8,128)(2,1)S(1)}, bf16[64,4608]{1,0:T(8,128)(2,1)S(1)}, u32[]{:S(2)}, u32[]{:S(2)}) collective-permute-start(bf16[64,4608]{1,0:T(8,128)(2,1)S(1)} %add_convert_fusion.own_ref), channel_id=1, source_target_pairs={{0,2},{1,3},{2,0},{3,1},{4,6},{5,7},{6,4},{7,5},{8,10},{9,11},{10,... | collective-permute-start | bytes 1769480 | tf_op jit(solution)/shard_map/ppermute | solution.py:552
  170.2 27.2 %collective-permute-start.16 = (bf16[64,4608]{1,0:T(8,128)(2,1)}, bf16[64,4608]{1,0:T(8,128)(2,1)}, u32[]{:S(2)}, u32[]{:S(2)}) collective-permute-start(bf16[64,4608]{1,0:T(8,128)(2,1)} %add_convert_fusion.1.own_ref), channel_id=1, source_target_pairs={{0,2},{1,3},{2,0},{3,1},{4,6},{5,7},{6,4},{7,5},{8,10},{9,11},{10,... | collective-permute-start | bytes 1769480 | tf_op jit(solution)/shard_map/ppermute | solution.py:552
  174.7 27.2 %all-to-all-start.2 = ((bf16[16,32,1024]{2,1,0:T(8,128)(2,1)}), bf16[16,32,1024]{2,1,0:T(8,128)(2,1)}, u32[]{:S(2)}, u32[]{:S(2)}) async-start(bf16[16,32,1024]{2,1,0:T(8,128)(2,1)} %pad_maximum_fusion), calls=%async_computation.2 | async-start | bytes 2097152 | tf_op jit(solution)/shard_map/all_to_all | solution.py:558
  185.6 11.8 %copy-start.22 = (f32[256,128]{1,0:T(8,128)S(1)}, f32[256,128]{1,0:T(8,128)}, u32[]{:S(2)}) copy-start(f32[256,128]{1,0:T(8,128)} %copy-done.20) | copy-start | bytes 393220
  187.5 14.3 %copy-start.37 = (s32[32,1,16]{2,1,0:T(1,128)S(1)}, s32[32,1,16]{2,1,0:T(1,128)}, u32[]{:S(2)}) copy-start(s32[32,1,16]{2,1,0:T(1,128)} %copy-done.36) | copy-start | bytes 6148
  187.5 14.4 %copy-start.5 = (bf16[512,1024]{1,0:T(8,128)(2,1)S(1)}, bf16[512,1024]{1,0:T(8,128)(2,1)}, u32[]{:S(2)}) copy-start(bf16[512,1024]{1,0:T(8,128)(2,1)} %stream_ref.3) | copy-start | bytes 3145732
  187.5 17.3 %collective-permute-start.20 = (bf16[256,1152]{1,0:T(8,128)(2,1)}, bf16[256,1152]{1,0:T(8,128)(2,1)}, u32[]{:S(2)}, u32[]{:S(2)}) collective-permute-start(bf16[256,1152]{1,0:T(8,128)(2,1)} %finish.3.refs_1_), channel_id=1, source_target_pairs={{0,1},{1,0},{2,3},{3,2},{4,5},{5,4},{6,7},{7,6},{8,9},{9,8},{10,11... | collective-permute-start | bytes 1769480 | tf_op jit(solution)/shard_map/ppermute | solution.py:571
  200.6 4.2 %collective-permute-start.19 = (bf16[256,1152]{1,0:T(8,128)(2,1)}, bf16[256,1152]{1,0:T(8,128)(2,1)S(1)}, u32[]{:S(2)}, u32[]{:S(2)}) collective-permute-start(bf16[256,1152]{1,0:T(8,128)(2,1)} %finish.2.refs_0_), channel_id=1, source_target_pairs={{0,1},{1,0},{2,3},{3,2},{4,5},{5,4},{6,7},{7,6},{8,9},{9,8},{10,11... | collective-permute-start | bytes 1769480 | tf_op jit(solution)/shard_map/ppermute | solution.py:571
  (14 other events, 12.5 us)
Sparse Core Ops, SparseCore 0:
  10.2 102.8 all-gather.2

commit v5 on v4

v5 whole, which is shorter than its diff:
```python
import jax
import jax.numpy as jnp
from jax import lax
from jax.experimental import pallas as pl
from jax.experimental.pallas import tpu as pltpu
from jax.sharding import PartitionSpec as P


BF = jnp.bfloat16
F32 = jnp.float32
BLOCK = 768


def params(mib):
    return pltpu.CompilerParams(vmem_limit_bytes=mib * 1024 * 1024)


def whole():
    return pl.BlockSpec(memory_space=pltpu.VMEM)


def scalars():
    return pl.BlockSpec(memory_space=pltpu.SMEM)


def anywhere():
    return pl.BlockSpec(memory_space=pl.ANY)


def cost(flops, moved):
    return pl.CostEstimate(flops=flops, bytes_accessed=moved, transcendentals=0)


def eq_hot(shape, dim, index):
    return (lax.broadcasted_iota(jnp.int32, shape, dim) == index).astype(BF)


def window_major(tokens, window):
    n = tokens * window
    row = lax.broadcasted_iota(jnp.int32, (n, n), 0)
    col = lax.broadcasted_iota(jnp.int32, (n, n), 1)
    return (col == (row % tokens) * window + row // tokens).astype(BF)


def patch_major(tokens, window):
    n = tokens * window
    row = lax.broadcasted_iota(jnp.int32, (n, n), 0)
    col = lax.broadcasted_iota(jnp.int32, (n, n), 1)
    return (col == (row % window) * tokens + row // window).astype(BF)


def norm_kernel(core_ref, x_ref, gain_ref, bias_ref, lifted_ref, xw_ref, stat_ref):
    window, width = gain_ref.shape
    tokens = x_ref.shape[0] // window
    full = window * width
    x = jnp.dot(window_major(tokens, window), x_ref[...], preferred_element_type=F32)
    parts = [x[w * tokens : (w + 1) * tokens] for w in range(window)]
    total = sum(jnp.sum(p, axis=1, keepdims=True) for p in parts)
    squares = sum(jnp.sum(p * p, axis=1, keepdims=True) for p in parts)
    mean = total / full
    inv = lax.rsqrt(squares / full - mean * mean + 1e-05)
    for w, p in enumerate(parts):
        normed = (p - mean) * inv
        lifted_ref[:, w * width : (w + 1) * width] = (
            normed * gain_ref[w : w + 1].astype(F32) + bias_ref[w : w + 1].astype(F32)
        ).astype(BF)
        xw_ref[w] = p.astype(BF)
    lane = lax.broadcasted_iota(jnp.int32, stat_ref.shape, 1)
    stat_ref[...] = jnp.where(lane == 0, mean, inv)


def layer_norm(core, features, gain, bias):
    rows, width = features.shape
    window = gain.shape[0]
    merged = rows // window
    block = 64
    steps = merged // block
    return pl.pallas_call(
        norm_kernel,
        grid_spec=pltpu.PrefetchScalarGridSpec(
            num_scalar_prefetch=1,
            grid=(steps,),
            in_specs=[
                pl.BlockSpec(
                    (block * window, width),
                    lambda i, c: (lax.rem(i + c[0] * (steps // 2), steps), 0),
                ),
                pl.BlockSpec((window, width), lambda i, c: (0, 0)),
                pl.BlockSpec((window, width), lambda i, c: (0, 0)),
            ],
            out_specs=[
                pl.BlockSpec((block, window * width), lambda i, c: (i, 0)),
                pl.BlockSpec((window, block, width), lambda i, c: (0, i, 0)),
                pl.BlockSpec((block, 128), lambda i, c: (i, 0)),
            ],
        ),
        out_shape=[
            jax.ShapeDtypeStruct((merged, window * width), BF),
            jax.ShapeDtypeStruct((window, merged, width), BF),
            jax.ShapeDtypeStruct((merged, 128), F32),
        ],
        compiler_params=params(12),
        cost_estimate=cost(2 * rows * block * window * width, 6 * rows * width),
        name="layer_norm",
    )(core, features, gain, bias)


def collect_kernel(pos_ref, stream_ref, cot_ref, out_ref):
    slots = pos_ref.shape[0]
    rows, width = stream_ref.shape
    cut = width // 2
    pick = eq_hot((slots, rows), 1, pos_ref[...])
    for img in range(2):
        at = slice(img * cut, (img + 1) * cut)
        for place, ref in enumerate((stream_ref, cot_ref)):
            out_ref[img, :, place * cut : (place + 1) * cut] = jnp.dot(
                pick, ref[:, at], preferred_element_type=F32
            ).astype(BF)


def collect(pos, stream, cot):
    slots = pos.shape[0]
    rows, width = stream.shape
    return pl.pallas_call(
        collect_kernel,
        in_specs=[whole()] * 3,
        out_specs=whole(),
        out_shape=jax.ShapeDtypeStruct((2, slots, width), BF),
        compiler_params=params(12),
        cost_estimate=cost(4 * slots * rows * width, 8 * rows * width),
        name="collect",
    )(pos, stream, cot)


def unpack_kernel(slot_ref, came_ref, ngain_ref, base_ref, up_ref):
    tokens, width = base_ref.shape
    slots = came_ref.shape[0]
    take = eq_hot((tokens, slots), 1, slot_ref[...])
    base_ref[...] = jnp.dot(take, came_ref[:, :width], preferred_element_type=F32)
    up_ref[...] = jnp.dot(take, came_ref[:, width:], preferred_element_type=F32) * ngain_ref[
        ...
    ].astype(F32)


def unpack(slot_col, came, ngain):
    tokens = slot_col.shape[0]
    slots, both = came.shape
    width = both // 2
    return pl.pallas_call(
        unpack_kernel,
        in_specs=[whole()] * 3,
        out_specs=[whole()] * 2,
        out_shape=[jax.ShapeDtypeStruct((tokens, width), F32)] * 2,
        compiler_params=params(12),
        cost_estimate=cost(4 * slots * tokens * width, 8 * tokens * width),
        name="unpack",
    )(slot_col, came, ngain)


def merge_kernel(base_ref, up_ref, w_ref, *refs):
    lifted, (visual_ref, state_ref, stat_ref, held_ref, left_ref, sems) = refs[:-6], refs[-6:]
    steps = range(w_ref.shape[0] // BLOCK)
    copies = []
    for step in steps:
        at = pl.ds(step * BLOCK, BLOCK)
        start = 0
        group = []
        for ref in lifted:
            rows = ref.shape[0]
            group.append((ref.at[:, at], left_ref.at[pl.ds(start, rows), at]))
            start += rows
        group.append((w_ref.at[at], held_ref.at[at]))
        copies.append(
            [pltpu.make_async_copy(a, b, sems.at[step, i]) for i, (a, b) in enumerate(group)]
        )
        for copy in copies[step]:
            copy.start()
    total = None
    for step in steps:
        at = slice(step * BLOCK, (step + 1) * BLOCK)
        for copy in copies[step]:
            copy.wait()
        part = jnp.dot(left_ref[:, at], held_ref[at, :], preferred_element_type=F32)
        total = part if total is None else total + part
    visual = total.astype(BF)
    visual_ref[...] = visual
    state = base_ref[...] + visual.astype(F32)
    state_ref[...] = state
    lane = lax.broadcasted_iota(jnp.int32, (state.shape[0], 128), 1)
    sums = jnp.where(
        lane == 0,
        jnp.sum(state * state, axis=1, keepdims=True),
        jnp.sum(up_ref[...] * state, axis=1, keepdims=True),
    )
    stat_ref[...] = sums.T[: stat_ref.shape[0]]


def merge(base, up, weight, lifted):
    tokens, width = base.shape
    depth = weight.shape[0]
    return pl.pallas_call(
        merge_kernel,
        in_specs=[whole()] * 2 + [anywhere()] * (1 + len(lifted)),
        out_specs=[whole()] * 3,
        out_shape=[
            jax.ShapeDtypeStruct((tokens, width), BF),
            jax.ShapeDtypeStruct((tokens, width), F32),
            jax.ShapeDtypeStruct((8, tokens), F32),
        ],
        scratch_shapes=[
            pltpu.VMEM((depth, width), BF),
            pltpu.VMEM((tokens, depth), BF),
            pltpu.SemaphoreType.DMA((depth // BLOCK, 1 + len(lifted))),
        ],
        compiler_params=params(22),
        cost_estimate=cost(2 * depth * tokens * width, 2 * depth * width),
        name="merge",
    )(base, up, weight, *lifted)


def pack_kernel(slot_ref, visual_ref, stay_ref, cross_ref):
    tokens = visual_ref.shape[0]
    slots = stay_ref.shape[0]
    for shift, out_ref in ((0, stay_ref), (slots, cross_ref)):
        put = eq_hot((slots, tokens), 0, slot_ref[...] - shift)
        out_ref[...] = jnp.dot(put, visual_ref[...], preferred_element_type=F32).astype(BF)


def pack(slot_row, visual, slots):
    tokens, width = visual.shape
    return pl.pallas_call(
        pack_kernel,
        in_specs=[whole()] * 2,
        out_specs=[whole()] * 2,
        out_shape=[jax.ShapeDtypeStruct((slots // 2, width), BF)] * 2,
        compiler_params=params(8),
        cost_estimate=cost(2 * slots * tokens * width, 2 * (slots + tokens) * width),
        name="pack",
    )(slot_row, visual)


RING = 4


def backward_kernel(full_width, chunks, at_ref, state_ref, up_ref, w_ref, *refs):
    stats, refs = refs[:RING], refs[RING:]
    outs, (picked_ref, sums_ref, held_ref, sems) = refs[: 3 * chunks], refs[3 * chunks :]
    copies = []
    for step in range(w_ref.shape[0] // BLOCK):
        at = pl.ds(step * BLOCK, BLOCK)
        copies.append(pltpu.make_async_copy(w_ref.at[at], held_ref.at[at], sems.at[step]))
        copies[step].start()
    tokens = state_ref.shape[0]
    rows = tokens // 2 // RING // chunks
    total = stats[0][...]
    for ref in stats[1:]:
        total = total + ref[...]
    sums_ref[...] = total.T
    img, far = at_ref[0], at_ref[1]
    for core in range(2):
        for chunk in range(chunks):
            for away in range(RING):
                there = lax.rem(2 * far + img + away, RING)
                partner = lax.rem(there + img, 2)
                begin = partner * (tokens // 2) + core * (tokens // 4) + (there // 2) * (tokens // 8)
                at = pl.ds(pl.multiple_of(begin + chunk * rows, rows), rows)
                sums = sums_ref[at, :]
                inv = lax.rsqrt(sums[:, 0:1] / full_width + 1e-06)
                inner = sums[:, 1:2] / full_width
                grad = inv * up_ref[at, :] - state_ref[at, :] * (inv * inv * inv * inner)
                to = ((core * chunks + chunk) * RING + away) * rows
                picked_ref[to : to + rows, :] = grad.astype(BF)
    for step, copy in enumerate(copies):
        cols = slice(step * BLOCK, (step + 1) * BLOCK)
        copy.wait()
        both = lax.dot_general(
            picked_ref[...], held_ref[cols, :], (((1,), (1,)), ((), ())), preferred_element_type=F32
        )
        for chunk in range(chunks):
            own, rest, other = outs[chunk], outs[chunks + chunk], outs[2 * chunks + chunk]
            start = chunk * RING * rows
            own[:, cols] = both[start : start + rows]
            rest[:, cols] = both[start + rows : start + RING * rows]
            start += tokens // 2
            other[:, cols] = both[start : start + RING * rows].astype(BF)


def backward(at, state, up, stats, weight, chunks, full_width):
    depth, width = weight.shape
    tokens = state.shape[0]
    rows = tokens // 2 // RING // chunks
    return pl.pallas_call(
        lambda *refs: backward_kernel(full_width, chunks, *refs),
        in_specs=[scalars()] + [whole()] * 2 + [anywhere()] + [whole()] * RING,
        out_specs=[whole()] * (3 * chunks),
        out_shape=[jax.ShapeDtypeStruct((rows, depth), F32)] * chunks
        + [jax.ShapeDtypeStruct(((RING - 1) * rows, depth), F32)] * chunks
        + [jax.ShapeDtypeStruct((RING * rows, depth), BF)] * chunks,
        scratch_shapes=[
            pltpu.VMEM((tokens, width), BF),
            pltpu.VMEM((tokens, 8), F32),
            pltpu.VMEM((depth, width), BF),
            pltpu.SemaphoreType.DMA((depth // BLOCK,)),
        ],
        compiler_params=params(24),
        cost_estimate=cost(2 * depth * tokens * width, 2 * depth * width),
        name="backward",
    )(at, state, up, weight, *stats)


def pair_kernel(rest_ref, got_ref, *outs):
    rows = outs[0].shape[0]
    for away, out in enumerate(outs):
        at = slice(away * rows, (away + 1) * rows)
        got = slice((away + 1) * rows, (away + 2) * rows)
        out[...] = (rest_ref[at, :] + got_ref[got, :].astype(F32)).astype(BF)


def pair(rest, got):
    rows, depth = got.shape[0] // RING, got.shape[1]
    return pl.pallas_call(
        pair_kernel,
        in_specs=[whole()] * 2,
        out_specs=[whole()] * (RING - 1),
        out_shape=[jax.ShapeDtypeStruct((rows, depth), BF)] * (RING - 1),
        compiler_params=params(12),
        cost_estimate=cost(4 * rows * depth, 24 * rows * depth),
        name="pair",
    )(rest, got)


def finish_kernel(block_ref, own_ref, got_ref, *refs):
    came, (xw_ref, stat_ref, gain_ref, out_ref) = refs[: RING - 1], refs[RING - 1 :]
    window, tokens, width = xw_ref.shape
    full = window * width
    mean = stat_ref[:, 0:1]
    inv = stat_ref[:, 1:2]
    lifted = own_ref[...] + got_ref[...].astype(F32)
    for ref in came:
        lifted = lifted + ref[...].astype(F32)
    scaled = []
    total = 0.0
    inner = 0.0
    for w in range(window):
        g = lifted[:, w * width : (w + 1) * width] * gain_ref[w : w + 1].astype(F32)
        normed = (xw_ref[w].astype(F32) - mean) * inv
        total = total + jnp.sum(g, axis=1, keepdims=True)
        inner = inner + jnp.sum(g * normed, axis=1, keepdims=True)
        scaled.append((g, normed))
    total = total / full
    inner = inner / full
    rows = jnp.concatenate(
        [(inv * (g - total - normed * inner)).astype(BF) for g, normed in scaled], axis=0
    )
    out_ref[...] = jnp.dot(
        patch_major(tokens, window), rows, preferred_element_type=F32
    ).astype(BF)


def finish(block, own, got, came, xw, stat, gain):
    tokens, full = own.shape
    window, width = gain.shape
    same = pl.BlockSpec((tokens, full), lambda i, b: (0, 0))
    return pl.pallas_call(
        finish_kernel,
        grid_spec=pltpu.PrefetchScalarGridSpec(
            num_scalar_prefetch=1,
            grid=(1,),
            in_specs=[same] * (1 + RING)
            + [
                pl.BlockSpec((window, tokens, width), lambda i, b: (0, b[0], 0)),
                pl.BlockSpec((tokens, 128), lambda i, b: (b[0], 0)),
                pl.BlockSpec((window, width), lambda i, b: (0, 0)),
            ],
            out_specs=pl.BlockSpec((tokens * window, width), lambda i, b: (0, 0)),
        ),
        out_shape=jax.ShapeDtypeStruct((tokens * window, width), BF),
        compiler_params=params(12),
        cost_estimate=cost(2 * (tokens * window) ** 2 * width, 8 * window * tokens * width),
        name="finish",
    )(block, own, got, *came, xw, stat, gain)


def place_kernel(img_ref, pos_ref, came_ref, stream_ref, out_ref):
    rows, width = stream_ref.shape
    cut = width // 2
    slots = pos_ref.shape[1]
    put = eq_hot((rows, slots), 0, pos_ref[...])
    for relative in range(2):
        start = pl.multiple_of((img_ref[0] ^ relative) * cut, cut)
        at = pl.ds(start, cut)
        out_ref[:, at] = (
            stream_ref[:, at].astype(F32)
            + jnp.dot(put, came_ref[relative], preferred_element_type=F32)
        ).astype(BF)


def place(img, pos, came, stream):
    rows, width = stream.shape
    return pl.pallas_call(
        place_kernel,
        in_specs=[scalars()] + [whole()] * 3,
        out_specs=whole(),
        out_shape=jax.ShapeDtypeStruct((rows, width), BF),
        compiler_params=params(12),
        cost_estimate=cost(2 * pos.shape[1] * rows * width, 6 * rows * width),
        name="place",
    )(img, pos, came, stream)


def lay_kernel(chunks, at_ref, *refs):
    blocks, (out_ref, sems) = refs[:-2], refs[-2:]
    rows = blocks[0].shape[0]
    copies = []
    for index, ref in enumerate(blocks):
        quarter, chunk = index // chunks, index % chunks
        owner = 2 * (at_ref[0] ^ (quarter // 2)) + (at_ref[1] ^ (quarter % 2))
        start = pl.multiple_of((owner * chunks + chunk) * rows, rows)
        copies.append(pltpu.make_async_copy(ref, out_ref.at[pl.ds(start, rows)], sems.at[index]))
    for copy in copies:
        copy.start()
    for copy in copies:
        copy.wait()


def lay(at, blocks, chunks):
    rows, width = blocks[0].shape
    return pl.pallas_call(
        lambda *refs: lay_kernel(chunks, *refs),
        in_specs=[scalars()] + [anywhere()] * len(blocks),
        out_specs=anywhere(),
        out_shape=jax.ShapeDtypeStruct((len(blocks) * rows, width), BF),
        scratch_shapes=[pltpu.SemaphoreType.DMA((len(blocks),))],
        compiler_params=params(4),
        cost_estimate=cost(0, 4 * len(blocks) * rows * width),
        name="lay",
    )(at, *blocks)


def swap_lanes(array, count):
    cuts = [array[:, i : i + count] for i in range(0, array.shape[1], count)]
    return jnp.concatenate([cuts[i ^ 1] for i in range(len(cuts))], axis=1)


def shards(features, ln_gain, ln_bias, projection, stream, norm_gain, cotangent, slots):
    n_img = lax.axis_size("img")
    n_ctx = lax.axis_size("ctx")
    n_tp = lax.axis_size("tp")
    merged = slots.shape[0]
    tok_rows, width = stream.shape
    owners = n_img * n_ctx
    capacity = 2 * merged // owners
    slot_count = owners * capacity
    full_width = width * n_tp
    cut = width // n_img

    img = lax.axis_index("img").astype(jnp.int32)
    tp = lax.axis_index("tp").astype(jnp.int32)
    core, far_half = tp % 2, tp // 2
    core_in = core.reshape(1)

    flip = [(i, 1 - i) for i in range(n_img)]
    core_pairs = [(t, t ^ 1) for t in range(n_tp)]
    far_pairs = [(t, t ^ 2) for t in range(n_tp)]

    def along_x(array, by):
        pairs = []
        for i in range(n_img):
            for t in range(n_tp):
                x = (2 * (t // 2) + i + by) % RING
                pairs.append((i * n_tp + t, (x % 2) * n_tp + 2 * (x // 2) + t % 2))
        return lax.ppermute(array, ("img", "tp"), pairs)

    own_columns = lax.dynamic_slice_in_dim(projection[0], img * cut, cut, axis=2)
    weight = lax.all_gather(own_columns, "ctx", axis=1, tiled=True).reshape(-1, cut)

    slots = jnp.roll(slots, -core * (merged // 2))
    target = slots // tok_rows
    ids = jnp.arange(merged)
    earlier = (target[:, None] == target[None, :]) & (ids[:, None] < ids[None, :])
    rank = jnp.sum(earlier.astype(jnp.int32), axis=0)
    slot = target * capacity + rank
    local = slots - target * tok_rows
    packed = jnp.max(
        jnp.where(jnp.arange(slot_count)[:, None] == slot[None, :], local[None, :], -1), axis=1
    )
    asked = lax.all_to_all(
        packed.reshape(owners, capacity), ("img", "ctx"), split_axis=0, concat_axis=0, tiled=True
    )
    asked = asked.reshape(n_img, n_ctx, capacity).transpose(1, 0, 2)
    held = collect(asked.reshape(slot_count, 1), stream, cotangent[0])
    came = lax.all_to_all(
        held.reshape(owners, n_img * capacity, width),
        ("img", "ctx"), split_axis=0, concat_axis=0, tiled=True,
    ).reshape(n_img * slot_count, width)
    paired = target * (n_img * capacity) + rank + img * capacity
    paired = jnp.concatenate([paired, lax.ppermute(paired, "img", flip)])

    gain = ln_gain[0]
    lifted, xw, stat = layer_norm(core_in, features[0], gain, ln_bias[0])
    next_mine = lax.ppermute(lifted[: merged // 2], "img", flip)
    next_other = lax.ppermute(next_mine, "tp", core_pairs)

    own_gain = lax.dynamic_slice_in_dim(norm_gain, img * cut, cut, axis=1)
    base, up = unpack(paired.reshape(-1, 1), came, own_gain)
    visual, state, sums = merge(base, up, weight, (lifted, next_mine, next_other))

    quarter = merged // 2
    near = sums + lax.ppermute(swap_lanes(sums, quarter), "tp", core_pairs)
    turned = swap_lanes(near, merged)
    stats = [near] + [along_x(near if by == 2 else turned, by) for by in (1, 2, 3)]

    in_img = n_img * slot_count // 2
    relative = lax.rem(paired + img * in_img, 2 * in_img)
    stay, cross = pack(relative.reshape(1, -1), visual, 2 * in_img)
    cross, stats = lax.optimization_barrier((cross, stats))
    crossed = lax.ppermute(cross, "img", flip)

    chunks = 2
    at = jnp.stack([img, far_half])
    parts = backward(at, state, up, stats, weight, chunks, full_width)
    own, rest, other = (parts[i * chunks : (i + 1) * chunks] for i in range(3))
    got = [lax.ppermute(o, "tp", core_pairs) for o in other]
    got[0], crossed = lax.optimization_barrier((got[0], crossed))
    sent = [pair(rest[c], got[c]) for c in range(chunks)]
    came_back = [[along_x(sent[c][by - 1], by) for by in (1, 2, 3)] for c in range(chunks)]

    stay, crossed, sent[0] = lax.optimization_barrier((stay, crossed, sent[0]))
    send = jnp.concatenate(
        [x.reshape(n_ctx, 1, n_img * capacity, cut) for x in (stay, crossed)], axis=1
    )
    arrived = lax.all_to_all(send, "ctx", split_axis=0, concat_axis=0, tiled=True)
    arrived = arrived.transpose(1, 0, 2, 3).reshape(n_img, slot_count, cut)
    new_stream = place(img.reshape(1), asked.reshape(1, slot_count), arrived, stream)

    quarters = [[], [], [], []]
    for c in range(chunks):
        block = (far_half * chunks + c).reshape(1)
        out = finish(block, own[c], got[c], came_back[c], xw, stat, gain)
        beyond = lax.ppermute(out, "tp", far_pairs)
        quarters[0].append(out)
        quarters[1].append(beyond)
        quarters[2].append(lax.ppermute(out, "tp", core_pairs))
        quarters[3].append(lax.ppermute(beyond, "tp", core_pairs))
    grad = lay(jnp.stack([core, far_half]), sum(quarters, []), chunks)
    return (new_stream, grad[None])


def solution(mesh):
    placed = (
        P(None, ("img", "ctx"), None),
        P(),
        P(),
        P(None, None, "ctx", "tp"),
        P(("img", "ctx"), "tp"),
        P(None, "tp"),
        P(None, ("img", "ctx"), "tp"),
        P(("img", "ctx")),
    )
    return jax.shard_map(
        shards,
        mesh=mesh,
        in_specs=placed,
        out_specs=(P(("img", "ctx"), "tp"), P(None, ("img", "ctx"), None)),
        check_vma=False,
    )
```

time: 215 us -> 215 us (level)
  waiting for transfers between devices: 73 us -> 53.9 us
  blocking collectives: 12.3 us -> 31.3 us
  Pallas kernels: 32.5 us -> 38.9 us
  starting transfers between devices: 48.5 us -> 42.1 us
  other arithmetic: 4.84 us -> 1.61 us
    ppermute x21 -> x22, waiting for transfers between devices: 73 us -> 47.5 us  [the longest x1 18.9 us: shards(): paired = jnp.concatenate([paired, lax.ppermute(paired, 'img', flip)])]
    all_to_all x1, blocking collectives: 12.3 us -> 31.3 us  [shards(): lax.all_to_all(packed.reshape(owners, capacity), ('img', 'ctx'), split_ax...]
    pallas_call x7 -> x6, Pallas kernels: 15.8 us -> 23.1 us  [the longest x1 10.7 us: lay(): pl.pallas_call(lambda *refs: lay_kernel(chunks, *refs), in_specs=[scalars...]
    all_to_all x1, waiting for transfers between devices: 0.01 us -> 6.38 us  [shards(): lax.all_to_all(held.reshape(owners, n_img * capacity, width), ('img', 'ct...]
    ppermute x21 -> x22, starting transfers between devices: 38.9 us -> 32.7 us  [the longest x9 12.9 us: along_x(): return lax.ppermute(array, ('img', 'tp'), pairs)]
    unnamed x76 -> x70, local copies, waits for them, and re-layouts: 25.9 us -> 26.1 us
  transfers between devices with their start and end apart: 24 -> 25, of which waited for: 8 -> 9; matrix products, arithmetic and copies ran while one was open for 3% -> 2% of each run, Pallas kernels for 12% -> 12%
where the time goes in v5:
time: 215 us; the launch traced here: 213 us
  waiting for transfers between devices  53.9 us (25%)
  starting transfers between devices  42.1 us (20%)
  Pallas kernels  38.9 us (18%)
  blocking collectives  31.3 us (15%)
  local copies, waits for them, and re-layouts  30.6 us (14%)
  between operations  14.4 us (7%)
    all_to_all x1, blocking collectives, shards(): lax.all_to_all(packed.reshape(owners, capacity), ('img', 'ctx'), split_ax...  31.3 us
    unnamed x70, local copies, waits for them, and re-layouts  26.1 us
    ppermute x1, waiting for transfers between devices, shards(): paired = jnp.concatenate([paired, lax.ppermute(paired, 'img', flip)])  18.9 us
    ppermute x1, waiting for transfers between devices, shards(): crossed = lax.ppermute(cross, 'img', flip)  13.1 us
    ppermute x9, starting transfers between devices, along_x(): return lax.ppermute(array, ('img', 'tp'), pairs)  12.9 us
    ppermute x9, waiting for transfers between devices, along_x(): return lax.ppermute(array, ('img', 'tp'), pairs)  11.7 us
    pallas_call x1, Pallas kernels, lay(): pl.pallas_call(lambda *refs: lay_kernel(chunks, *refs), in_specs=[scalars...  10.7 us
    pallas_call x1, Pallas kernels, backward(): pl.pallas_call(lambda *refs: backward_kernel(full_width, chunks, *refs),...  7.36 us
  transfers between devices with their start and end apart: 25, of which 9 were waited for; matrix products, arithmetic and copies ran while one was open for 2% of the time, Pallas kernels for 12%

profile of v5, /device:TPU:1, one launch (start us, length us, event | category | flops | bytes accessed | tf_op | source)
XLA Modules:
  0.0 212.7 jit_solution(15783293026756136751)
XLA Ops:
  9.0 1.7 copy-done.10
  12.1 2.9 %layer_norm.1 = (bf16[256,4608]{1,0:T(8,128)(2,1)S(1)}, bf16[4,256,1152]{2,1,0:T(8,128)(2,1)S(1)}, f32[256,128]{1,0:T(8,128)S(1)}) custom-call(s32[1]{0:T(128)} %bitcast.12.core_ref, bf16[1024,1152]{1,0:T(8,128)(2,1)S(1)} %bitcast.34, bf16[4,1152]{1,0:T(4,128)(2,1)S(1)} %bitcast.37, bf16[4,1152]{1,0:T(4,128)(2,1)S(1)} %bitcast.40), custom_call_target="tpu_custom_call" | custom-call | flops 603979776 | bytes 7077888 | tf_op jit(solution)/shard_map/layer_norm/pallas_call | solution.py:78
  15.0 1.1 slice.21
  16.0 1.4 copy-done.2
  17.5 2.0 collective-permute-start.1
  20.0 31.3 %all_to_all.19 = s32[32,1,16]{2,1,0:T(1,128)S(1)} all-to-all(s32[32,1,16]{2,1,0:T(1,128)S(1)} %bitcast.45), channel_id=1, replica_groups=mesh['img'=2,'ctx'=16,'tp'=4] {'img','ctx'}, dimensions={0} | all-to-all | bytes 4096 | tf_op jit(solution)/shard_map/all_to_all | solution.py:487
  51.4 1.2 copy-done.8
  52.6 1.2 copy-done.13
  53.9 1.3 collect.1
  55.2 1.4 copy-done.1
  56.6 4.9 %all-to-all-start.1 = ((bf16[32,32,1024]{2,1,0:T(8,128)(2,1)}), bf16[32,32,1024]{2,1,0:T(8,128)(2,1)}, u32[]{:S(2)}, u32[]{:S(2)}) async-start(bf16[32,32,1024]{2,1,0:T(8,128)(2,1)} %bitcast.30), calls=%async_computation.1 | async-start | bytes 4194304 | tf_op jit(solution)/shard_map/all_to_all | solution.py:492
  61.5 2.1 collective-permute-start.2
  63.6 1.5 collective-permute-start
  65.2 18.9 %collective-permute-done = s32[256]{0:T(256)S(1)} collective-permute-done((s32[256]{0:T(256)S(1)}, s32[256]{0:T(256)S(1)}, u32[]{:S(2)}, u32[]{:S(2)}) %collective-permute-start) | collective-permute-done | bytes 1056 | tf_op jit(solution)/shard_map/ppermute | solution.py:497
  84.2 6.4 %all-to-all-done.1 = bf16[32,32,1024]{2,1,0:T(8,128)(2,1)} async-done(((bf16[32,32,1024]{2,1,0:T(8,128)(2,1)}), bf16[32,32,1024]{2,1,0:T(8,128)(2,1)}, u32[]{:S(2)}, u32[]{:S(2)}) %all-to-all-start.1) | async-done | bytes 2097184 | tf_op jit(solution)/shard_map/all_to_all | solution.py:492
  90.5 2.9 %unpack.1 = (f32[512,512]{1,0:T(8,128)S(1)}, f32[512,512]{1,0:T(8,128)S(1)}) custom-call(s32[512,1]{1,0:T(8,128)S(1)} %copy.29.slot_ref, bf16[1024,1024]{1,0:T(8,128)(2,1)} %bitcast.10.came_ref, bf16[1,512]{1,0:T(2,128)(2,1)S(1)} %constant_dynamic-slice_fusion.1.ngain_ref), custom_call_target="tpu_custom_call" | custom-call | flops 1073741824 | bytes 2097152 | tf_op jit(solution)/shard_map/unpack/pallas_call | solution.py:149
  95.4 1.7 copy-done.3
  97.1 2.3 %copy-done.4 = bf16[1,4,1152,512]{3,2,1,0:T(8,128)(2,1)S(1)} copy-done((bf16[1,4,1152,512]{3,2,1,0:T(8,128)(2,1)S(1)}, bf16[1,4,1152,512]{3,2,1,0:T(8,128)(2,1)}, u32[]{:S(2)}) %copy-start.4) | copy-done | bytes 4718616
  99.4 1.2 copy-done.15
  100.6 1.2 copy-done.18
  101.9 4.7 %merge.1 = (bf16[512,512]{1,0:T(8,128)(2,1)S(1)}, f32[512,512]{1,0:T(8,128)S(1)}, f32[8,512]{1,0:T(8,128)S(1)}) custom-call(f32[512,512]{1,0:T(8,128)S(1)} %copy-done.18, f32[512,512]{1,0:T(8,128)S(1)} %copy-done.15, bf16[4608,512]{1,0:T(8,128)(2,1)S(1)} %bitcast.31, bf16[256,4608]{1,0:T(8,128)(2,1)S(1)} %copy-done.3, ...), custom_call_target="tpu_custom_call" | custom-call | flops 2415919104 | bytes 4718592 | tf_op jit(solution)/shard_map/merge/pallas_call | solution.py:201
  106.6 2.0 collective-permute-start.3
  109.5 2.7 %collective-permute-start.5 = (f32[8,512]{1,0:T(8,128)S(1)}, f32[8,512]{1,0:T(8,128)S(1)}, u32[]{:S(2)}, u32[]{:S(2)}) collective-permute-start(f32[8,512]{1,0:T(8,128)S(1)} %add.61.refs_4_), channel_id=1, source_target_pairs={{0,2},{1,3},{2,0},{3,1},{64,66},{65,67},{66,64},{67,65},{4,6},{5,7... | collective-permute-start | bytes 49160 | tf_op jit(solution)/shard_map/ppermute | solution.py:472
  113.0 1.8 collective-permute-start.6
  116.0 7.4 %backward.1 = (f32[32,4608]{1,0:T(8,128)S(1)}, f32[32,4608]{1,0:T(8,128)S(1)}, f32[96,4608]{1,0:T(8,128)S(1)}, f32[96,4608]{1,0:T(8,128)S(1)}, bf16[128,4608]{1,0:T(8,128)(2,1)S(1)}, /*index=5*/bf16[128,4608]{1,0:T(8,128)(2,1)}) custom-call(s32[2]{0:T(128)S(1)} %pad_add_fusion.2.refs_0_, f32[512,512]{1,0:T(8,128)S(1)} %get-tuple-element.38.refs_1_, ...), custom_call_target="tpu_custom_call" | custom-call | flops 2415919104 | bytes 4718592 | tf_op jit(solution)/shard_map/backward/pallas_call | solution.py:292
  123.4 1.9 collective-permute-start.7
  125.5 13.1 %collective-permute-done.8 = bf16[512,512]{1,0:T(8,128)(2,1)S(1)} collective-permute-done((bf16[512,512]{1,0:T(8,128)(2,1)S(1)}, bf16[512,512]{1,0:T(8,128)(2,1)S(1)}, u32[]{:S(2)}, u32[]{:S(2)}) %collective-permute-start.8) | collective-permute-done | bytes 524320 | tf_op jit(solution)/shard_map/ppermute | solution.py:517
  139.4 1.0 copy-done.6
  141.2 1.1 pad_maximum_fusion
  142.3 4.5 %all-to-all-start.2 = ((bf16[16,2,32,512]{3,2,1,0:T(8,128)(2,1)}), bf16[16,2,32,512]{3,2,1,0:T(8,128)(2,1)}, u32[]{:S(2)}, u32[]{:S(2)}) async-start(bf16[16,2,32,512]{3,2,1,0:T(8,128)(2,1)} %pad_maximum_fusion), calls=%async_computation.2 | async-start | bytes 2097152 | tf_op jit(solution)/shard_map/all_to_all | solution.py:532
  146.8 3.3 %collective-permute-start.10 = (bf16[32,4608]{1,0:T(8,128)(2,1)}, bf16[32,4608]{1,0:T(8,128)(2,1)}, u32[]{:S(2)}, u32[]{:S(2)}) collective-permute-start(bf16[32,4608]{1,0:T(8,128)(2,1)} %copy-done.31), channel_id=1, source_target_pairs={{0,2},{1,3},{2,0},{3,1},{64,66},{65,67},{66,64},{67,65},{4,6},{5,7... | collective-permute-start | bytes 884744 | tf_op jit(solution)/shard_map/ppermute | solution.py:472
  151.1 1.5 copy-done.12
  152.5 2.3 %pair.3 = (bf16[32,4608]{1,0:T(8,128)(2,1)}, bf16[32,4608]{1,0:T(8,128)(2,1)}, bf16[32,4608]{1,0:T(8,128)(2,1)}) custom-call(f32[96,4608]{1,0:T(8,128)S(1)} %copy-done.12, bf16[128,4608]{1,0:T(8,128)(2,1)} %collective-permute-done.12.got_ref), custom_call_target="tpu_custom_call" | custom-call | flops 589824 | bytes 3538944 | tf_op jit(solution)/shard_map/pair/pallas_call | solution.py:321
  156.8 2.0 collective-permute-start.15
  158.8 6.0 %collective-permute-done.11.refs_2_ = bf16[32,4608]{1,0:T(8,128)(2,1)} collective-permute-done((bf16[32,4608]{1,0:T(8,128)(2,1)}, bf16[32,4608]{1,0:T(8,128)(2,1)}, u32[]{:S(2)}, u32[]{:S(2)}) %collective-permute-start.11) | collective-permute-done | bytes 294944 | tf_op jit(solution)/shard_map/ppermute | solution.py:472
  164.7 1.3 copy-done.7
  166.0 1.1 copy-done.22
  168.0 1.7 finish.2.refs_1_
  169.8 1.9 collective-permute-start.16
  171.7 5.3 %collective-permute-done.15.refs_2_ = bf16[32,4608]{1,0:T(8,128)(2,1)} collective-permute-done((bf16[32,4608]{1,0:T(8,128)(2,1)}, bf16[32,4608]{1,0:T(8,128)(2,1)}, u32[]{:S(2)}, u32[]{:S(2)}) %collective-permute-start.15) | collective-permute-done | bytes 294944 | tf_op jit(solution)/shard_map/ppermute | solution.py:472
  177.9 1.9 finish.3.refs_2_
  179.7 2.0 collective-permute-start.17
  181.7 2.6 %collective-permute-start.18 = (bf16[128,1152]{1,0:T(8,128)(2,1)S(1)}, bf16[128,1152]{1,0:T(8,128)(2,1)S(1)}, u32[]{:S(2)}, u32[]{:S(2)}) collective-permute-start(bf16[128,1152]{1,0:T(8,128)(2,1)S(1)} %finish.2.refs_1_), channel_id=1, source_target_pairs={{0,1},{1,0},{2,3},{3,2},{4,5},{5,4},{6,7},{7,6},{8,9},{9,8},{10,11... | collective-permute-start | bytes 884744 | tf_op jit(solution)/shard_map/ppermute | solution.py:543
  184.8 2.8 %collective-permute-done.17.refs_4_ = bf16[128,1152]{1,0:T(8,128)(2,1)S(1)} collective-permute-done((bf16[128,1152]{1,0:T(8,128)(2,1)S(1)}, bf16[128,1152]{1,0:T(8,128)(2,1)S(1)}, u32[]{:S(2)}, u32[]{:S(2)}) %collective-permute-start.17) | collective-permute-done | bytes 294944 | tf_op jit(solution)/shard_map/ppermute | solution.py:540
  187.5 3.2 %collective-permute-start.21 = (bf16[128,1152]{1,0:T(8,128)(2,1)S(1)}, bf16[128,1152]{1,0:T(8,128)(2,1)S(1)}, u32[]{:S(2)}, u32[]{:S(2)}) collective-permute-start(bf16[128,1152]{1,0:T(8,128)(2,1)S(1)} %collective-permute-done.17.refs_4_), channel_id=1, source_target_pairs={{0,1},{1,0},{2,3},{3,2},{4,5},{5,4},{6,7},{7,6},{8,9},{9,8},{10,11... | collective-permute-start | bytes 884744 | tf_op jit(solution)/shard_map/ppermute | solution.py:544
  192.0 10.7 %lay.1 = bf16[1024,1152]{1,0:T(8,128)(2,1)} custom-call(s32[2]{0:T(128)S(1)} %pad_add_fusion.3.refs_0_, bf16[128,1152]{1,0:T(8,128)(2,1)S(1)} %finish.2.refs_1_, bf16[128,1152]{1,0:T(8,128)(2,1)S(1)} %finish.3.refs_2_, bf16[128,1152]{1,0:T(8,128)(2,1)} %collective-permute-done.16.refs_3_, bf16[128,1152]{1,0:T(8,128)(2,1)S(1)} %collective-permute-done.17.refs_4_, ...), custom_call_target="tpu_custom_call" | custom-call | bytes 4718592 | tf_op jit(solution)/shard_map/lay/pallas_call | solution.py:428
  202.6 1.4 copy.32
  204.2 1.7 place.1
  (110 shorter events, 17.3 us)
Async XLA Ops:
  7.2 88.2 %all-gather.3.cloned.1.call-start = ((), (), s32[]{:S(2)}) async-start(), calls=%async_computation.3 | async-start | bytes 5013504 | tf_op jit(solution)/shard_map/all_gather | solution.py:475
  9.0 1.7 copy-start.10
  14.9 149.8 %copy-start.23 = (f32[256,128]{1,0:T(8,128)}, f32[256,128]{1,0:T(8,128)S(1)}, u32[]{:S(2)}) copy-start(f32[256,128]{1,0:T(8,128)S(1)} %get-tuple-element.57.refs_4_) | copy-start | bytes 393220
  15.0 4.5 %copy-start.33 = (s32[256]{0:T(256)S(1)}, s32[256]{0:T(256)}, u32[]{:S(2)}) copy-start(s32[256]{0:T(256)} %param.15) | copy-start | bytes 3076
  16.0 1.4 copy-start.2
  17.5 44.0 %collective-permute-start.1 = (bf16[128,4608]{1,0:T(8,128)(2,1)}, bf16[128,4608]{1,0:T(8,128)(2,1)}, u32[]{:S(2)}, u32[]{:S(2)}) collective-permute-start(bf16[128,4608]{1,0:T(8,128)(2,1)} %slice.21), channel_id=1, source_target_pairs={{0,64},{64,0},{1,65},{65,1},{2,66},{66,2},{3,67},{67,3},{4,68},{68... | collective-permute-start | bytes 3538952 | tf_op jit(solution)/shard_map/ppermute | solution.py:501
  51.2 3.9 %copy-start.32 = (s32[2,16,16]{2,0,1:T(2,128)}, s32[2,16,16]{2,0,1:T(2,128)S(1)}, u32[]{:S(2)}) copy-start(s32[2,16,16]{2,0,1:T(2,128)S(1)} %copy.36) | copy-start | bytes 6148
  51.4 1.2 copy-start.8
  52.6 1.2 copy-start.13
  55.2 1.4 copy-start.1
  56.6 8.5 %copy-start.34 = (bf16[1,1024]{1,0:T(2,128)(2,1)S(1)}, bf16[1,1024]{1,0:T(2,128)(2,1)}, u32[]{:S(2)}) copy-start(bf16[1,1024]{1,0:T(2,128)(2,1)} %param.13) | copy-start | bytes 6148
  56.6 34.0 %all-to-all-start.1 = ((bf16[32,32,1024]{2,1,0:T(8,128)(2,1)}), bf16[32,32,1024]{2,1,0:T(8,128)(2,1)}, u32[]{:S(2)}, u32[]{:S(2)}) async-start(bf16[32,32,1024]{2,1,0:T(8,128)(2,1)} %bitcast.30), calls=%async_computation.1 | async-start | bytes 4194304 | tf_op jit(solution)/shard_map/all_to_all | solution.py:492
  61.5 33.9 %collective-permute-start.2 = (bf16[128,4608]{1,0:T(8,128)(2,1)}, bf16[128,4608]{1,0:T(8,128)(2,1)}, u32[]{:S(2)}, u32[]{:S(2)}) collective-permute-start(bf16[128,4608]{1,0:T(8,128)(2,1)} %collective-permute-done.1.refs_1_), channel_id=1, source_target_pairs={{0,1},{1,0},{2,3},{3,2},{4,5},{5,4},{6,7},{7,6},{8,9},{9,8},{10,11... | collective-permute-start | bytes 3538952 | tf_op jit(solution)/shard_map/ppermute | solution.py:502
  63.6 20.4 %collective-permute-start = (s32[256]{0:T(256)S(1)}, s32[256]{0:T(256)S(1)}, u32[]{:S(2)}, u32[]{:S(2)}) collective-permute-start(s32[256]{0:T(256)S(1)} %get-tuple-element.72), channel_id=1, source_target_pairs={{0,64},{64,0},{1,65},{65,1},{2,66},{66,2},{3,67},{67,3},{4,68},{68... | collective-permute-start | bytes 3080 | tf_op jit(solution)/shard_map/ppermute | solution.py:497
  95.4 1.7 copy-start.3
  97.1 2.3 %copy-start.4 = (bf16[1,4,1152,512]{3,2,1,0:T(8,128)(2,1)S(1)}, bf16[1,4,1152,512]{3,2,1,0:T(8,128)(2,1)}, u32[]{:S(2)}) copy-start(bf16[1,4,1152,512]{3,2,1,0:T(8,128)(2,1)} %all-gather.3.cloned.1.call-done) | copy-start | bytes 14155780
  99.4 1.2 copy-start.15
  100.6 1.2 copy-start.18
  101.9 14.1 %copy-start.5 = (bf16[1,4,1152,512]{3,2,1,0:T(8,128)(2,1)S(1)}, bf16[1,4,1152,512]{3,2,1,0:T(8,128)(2,1)}, u32[]{:S(2)}) copy-start(bf16[1,4,1152,512]{3,2,1,0:T(8,128)(2,1)} %all-gather.3.cloned.1.call-done) | copy-start | bytes 14155780
  106.6 9.4 %copy-start.16 = (f32[512,512]{1,0:T(8,128)S(1)}, f32[512,512]{1,0:T(8,128)}, u32[]{:S(2)}) copy-start(f32[512,512]{1,0:T(8,128)} %copy-done.14) | copy-start | bytes 3145732
  106.6 2.9 %collective-permute-start.3 = (f32[8,512]{1,0:T(8,128)S(1)}, f32[8,512]{1,0:T(8,128)S(1)}, u32[]{:S(2)}, u32[]{:S(2)}) collective-permute-start(f32[8,512]{1,0:T(8,128)S(1)} %pad_maximum_fusion.1), channel_id=1, source_target_pairs={{0,1},{1,0},{2,3},{3,2},{4,5},{5,4},{6,7},{7,6},{8,9},{9,8},{10,11... | collective-permute-start | bytes 49160 | tf_op jit(solution)/shard_map/ppermute | solution.py:509
  109.5 6.5 %collective-permute-start.5 = (f32[8,512]{1,0:T(8,128)S(1)}, f32[8,512]{1,0:T(8,128)S(1)}, u32[]{:S(2)}, u32[]{:S(2)}) collective-permute-start(f32[8,512]{1,0:T(8,128)S(1)} %add.61.refs_4_), channel_id=1, source_target_pairs={{0,2},{1,3},{2,0},{3,1},{64,66},{65,67},{66,64},{67,65},{4,6},{5,7... | collective-permute-start | bytes 49160 | tf_op jit(solution)/shard_map/ppermute | solution.py:472
  112.2 3.8 %collective-permute-start.4 = (f32[8,512]{1,0:T(8,128)S(1)}, f32[8,512]{1,0:T(8,128)S(1)}, u32[]{:S(2)}, u32[]{:S(2)}) collective-permute-start(f32[8,512]{1,0:T(8,128)S(1)} %pad_maximum_fusion.2), channel_id=1, source_target_pairs={{0,64},{1,65},{2,66},{3,67},{64,2},{65,3},{66,0},{67,1},{4,68},{5,... | collective-permute-start | bytes 49160 | tf_op jit(solution)/shard_map/ppermute | solution.py:472
  113.0 3.0 %collective-permute-start.6 = (f32[8,512]{1,0:T(8,128)S(1)}, f32[8,512]{1,0:T(8,128)S(1)}, u32[]{:S(2)}, u32[]{:S(2)}) collective-permute-start(f32[8,512]{1,0:T(8,128)S(1)} %pad_maximum_fusion.2), channel_id=1, source_target_pairs={{0,66},{1,67},{2,64},{3,65},{64,0},{65,1},{66,2},{67,3},{4,70},{5,... | collective-permute-start | bytes 49160 | tf_op jit(solution)/shard_map/ppermute | solution.py:472
  123.4 16.0 %copy-start.11 = (f32[96,4608]{1,0:T(8,128)}, f32[96,4608]{1,0:T(8,128)S(1)}, u32[]{:S(2)}) copy-start(f32[96,4608]{1,0:T(8,128)S(1)} %get-tuple-element.60.rest_ref) | copy-start | bytes 5308420
  123.4 17.0 %copy-start.19 = (f32[32,4608]{1,0:T(8,128)}, f32[32,4608]{1,0:T(8,128)S(1)}, u32[]{:S(2)}) copy-start(f32[32,4608]{1,0:T(8,128)S(1)} %get-tuple-element.58.own_ref) | copy-start | bytes 1769476
  123.4 17.0 %copy-start.21 = (f32[32,4608]{1,0:T(8,128)}, f32[32,4608]{1,0:T(8,128)S(1)}, u32[]{:S(2)}) copy-start(f32[32,4608]{1,0:T(8,128)S(1)} %get-tuple-element.55.own_ref) | copy-start | bytes 1769476
  123.4 15.1 %collective-permute-start.7 = (bf16[128,4608]{1,0:T(8,128)(2,1)S(1)}, bf16[128,4608]{1,0:T(8,128)(2,1)S(1)}, u32[]{:S(2)}, u32[]{:S(2)}) collective-permute-start(bf16[128,4608]{1,0:T(8,128)(2,1)S(1)} %get-tuple-element.45), channel_id=1, source_target_pairs={{0,1},{1,0},{2,3},{3,2},{4,5},{5,4},{6,7},{7,6},{8,9},{9,8},{10,11... | collective-permute-start | bytes 3538952 | tf_op jit(solution)/shard_map/ppermute | solution.py:523
  125.3 25.7 %collective-permute-start.12 = (bf16[128,4608]{1,0:T(8,128)(2,1)}, bf16[128,4608]{1,0:T(8,128)(2,1)}, u32[]{:S(2)}, u32[]{:S(2)}) collective-permute-start(bf16[128,4608]{1,0:T(8,128)(2,1)} %get-tuple-element.59), channel_id=1, source_target_pairs={{0,1},{1,0},{2,3},{3,2},{4,5},{5,4},{6,7},{7,6},{8,9},{9,8},{10,11... | collective-permute-start | bytes 3538952 | tf_op jit(solution)/shard_map/ppermute | solution.py:523
  125.4 13.1 %collective-permute-start.8 = (bf16[512,512]{1,0:T(8,128)(2,1)S(1)}, bf16[512,512]{1,0:T(8,128)(2,1)S(1)}, u32[]{:S(2)}, u32[]{:S(2)}) collective-permute-start(bf16[512,512]{1,0:T(8,128)(2,1)S(1)} %get-tuple-element.46), channel_id=1, source_target_pairs={{0,64},{64,0},{1,65},{65,1},{2,66},{66,2},{3,67},{67,3},{4,68},{68... | collective-permute-start | bytes 1572872 | tf_op jit(solution)/shard_map/ppermute | solution.py:517
  140.4 15.7 %collective-permute-start.9 = (bf16[32,4608]{1,0:T(8,128)(2,1)}, bf16[32,4608]{1,0:T(8,128)(2,1)S(1)}, u32[]{:S(2)}, u32[]{:S(2)}) collective-permute-start(bf16[32,4608]{1,0:T(8,128)(2,1)} %get-tuple-element.50), channel_id=1, source_target_pairs={{0,64},{1,65},{2,66},{3,67},{64,2},{65,3},{66,0},{67,1},{4,68},{5,... | collective-permute-start | bytes 884744 | tf_op jit(solution)/shard_map/ppermute | solution.py:472
  142.3 22.4 %copy-start.28 = (bf16[1,4,1152]{2,1,0:T(4,128)(2,1)S(1)}, bf16[1,4,1152]{2,1,0:T(4,128)(2,1)}, u32[]{:S(2)}) copy-start(bf16[1,4,1152]{2,1,0:T(4,128)(2,1)} %param.9) | copy-start | bytes 27652
  142.3 60.3 %all-to-all-start.2 = ((bf16[16,2,32,512]{3,2,1,0:T(8,128)(2,1)}), bf16[16,2,32,512]{3,2,1,0:T(8,128)(2,1)}, u32[]{:S(2)}, u32[]{:S(2)}) async-start(bf16[16,2,32,512]{3,2,1,0:T(8,128)(2,1)} %pad_maximum_fusion), calls=%async_computation.2 | async-start | bytes 2097152 | tf_op jit(solution)/shard_map/all_to_all | solution.py:532
  146.8 12.0 %collective-permute-start.10 = (bf16[32,4608]{1,0:T(8,128)(2,1)}, bf16[32,4608]{1,0:T(8,128)(2,1)}, u32[]{:S(2)}, u32[]{:S(2)}) collective-permute-start(bf16[32,4608]{1,0:T(8,128)(2,1)} %copy-done.31), channel_id=1, source_target_pairs={{0,2},{1,3},{2,0},{3,1},{64,66},{65,67},{66,64},{67,65},{4,6},{5,7... | collective-permute-start | bytes 884744 | tf_op jit(solution)/shard_map/ppermute | solution.py:472
  150.1 14.6 %collective-permute-start.11 = (bf16[32,4608]{1,0:T(8,128)(2,1)}, bf16[32,4608]{1,0:T(8,128)(2,1)}, u32[]{:S(2)}, u32[]{:S(2)}) collective-permute-start(bf16[32,4608]{1,0:T(8,128)(2,1)} %copy-done.30), channel_id=1, source_target_pairs={{0,66},{1,67},{2,64},{3,65},{64,0},{65,1},{66,2},{67,3},{4,70},{5,... | collective-permute-start | bytes 884744 | tf_op jit(solution)/shard_map/ppermute | solution.py:472
  151.1 1.5 copy-start.12
  154.9 16.8 %collective-permute-start.13 = (bf16[32,4608]{1,0:T(8,128)(2,1)}, bf16[32,4608]{1,0:T(8,128)(2,1)}, u32[]{:S(2)}, u32[]{:S(2)}) collective-permute-start(bf16[32,4608]{1,0:T(8,128)(2,1)} %get-tuple-element.61), channel_id=1, source_target_pairs={{0,64},{1,65},{2,66},{3,67},{64,2},{65,3},{66,0},{67,1},{4,68},{5,... | collective-permute-start | bytes 884744 | tf_op jit(solution)/shard_map/ppermute | solution.py:472
  155.4 16.3 %collective-permute-start.14 = (bf16[32,4608]{1,0:T(8,128)(2,1)}, bf16[32,4608]{1,0:T(8,128)(2,1)}, u32[]{:S(2)}, u32[]{:S(2)}) collective-permute-start(bf16[32,4608]{1,0:T(8,128)(2,1)} %get-tuple-element.62), channel_id=1, source_target_pairs={{0,2},{1,3},{2,0},{3,1},{64,66},{65,67},{66,64},{67,65},{4,6},{5,7... | collective-permute-start | bytes 884744 | tf_op jit(solution)/shard_map/ppermute | solution.py:472
  156.8 20.2 %collective-permute-start.15 = (bf16[32,4608]{1,0:T(8,128)(2,1)}, bf16[32,4608]{1,0:T(8,128)(2,1)}, u32[]{:S(2)}, u32[]{:S(2)}) collective-permute-start(bf16[32,4608]{1,0:T(8,128)(2,1)} %get-tuple-element.63), channel_id=1, source_target_pairs={{0,66},{1,67},{2,64},{3,65},{64,0},{65,1},{66,2},{67,3},{4,70},{5,... | collective-permute-start | bytes 884744 | tf_op jit(solution)/shard_map/ppermute | solution.py:472
  164.7 1.3 copy-start.7
  168.0 8.9 %copy-start.20 = (f32[32,4608]{1,0:T(8,128)S(1)}, f32[32,4608]{1,0:T(8,128)}, u32[]{:S(2)}) copy-start(f32[32,4608]{1,0:T(8,128)} %copy-done.19) | copy-start | bytes 1769476
  169.8 14.5 %collective-permute-start.16 = (bf16[128,1152]{1,0:T(8,128)(2,1)S(1)}, bf16[128,1152]{1,0:T(8,128)(2,1)}, u32[]{:S(2)}, u32[]{:S(2)}) collective-permute-start(bf16[128,1152]{1,0:T(8,128)(2,1)S(1)} %finish.2.refs_1_), channel_id=1, source_target_pairs={{0,2},{1,3},{2,0},{3,1},{4,6},{5,7},{6,4},{7,5},{8,10},{9,11},{10,... | collective-permute-start | bytes 884744 | tf_op jit(solution)/shard_map/ppermute | solution.py:540
  179.7 7.8 %collective-permute-start.17 = (bf16[128,1152]{1,0:T(8,128)(2,1)S(1)}, bf16[128,1152]{1,0:T(8,128)(2,1)S(1)}, u32[]{:S(2)}, u32[]{:S(2)}) collective-permute-start(bf16[128,1152]{1,0:T(8,128)(2,1)S(1)} %finish.3.refs_2_), channel_id=1, source_target_pairs={{0,2},{1,3},{2,0},{3,1},{4,6},{5,7},{6,4},{7,5},{8,10},{9,11},{10,... | collective-permute-start | bytes 884744 | tf_op jit(solution)/shard_map/ppermute | solution.py:540
  181.7 9.9 %collective-permute-start.18 = (bf16[128,1152]{1,0:T(8,128)(2,1)S(1)}, bf16[128,1152]{1,0:T(8,128)(2,1)S(1)}, u32[]{:S(2)}, u32[]{:S(2)}) collective-permute-start(bf16[128,1152]{1,0:T(8,128)(2,1)S(1)} %finish.2.refs_1_), channel_id=1, source_target_pairs={{0,1},{1,0},{2,3},{3,2},{4,5},{5,4},{6,7},{7,6},{8,9},{9,8},{10,11... | collective-permute-start | bytes 884744 | tf_op jit(solution)/shard_map/ppermute | solution.py:543
  184.3 7.4 %collective-permute-start.19 = (bf16[128,1152]{1,0:T(8,128)(2,1)S(1)}, bf16[128,1152]{1,0:T(8,128)(2,1)S(1)}, u32[]{:S(2)}, u32[]{:S(2)}) collective-permute-start(bf16[128,1152]{1,0:T(8,128)(2,1)S(1)} %finish.3.refs_2_), channel_id=1, source_target_pairs={{0,1},{1,0},{2,3},{3,2},{4,5},{5,4},{6,7},{7,6},{8,9},{9,8},{10,11... | collective-permute-start | bytes 884744 | tf_op jit(solution)/shard_map/ppermute | solution.py:543
  184.3 7.4 %collective-permute-start.20 = (bf16[128,1152]{1,0:T(8,128)(2,1)}, bf16[128,1152]{1,0:T(8,128)(2,1)S(1)}, u32[]{:S(2)}, u32[]{:S(2)}) collective-permute-start(bf16[128,1152]{1,0:T(8,128)(2,1)} %collective-permute-done.16.refs_3_), channel_id=1, source_target_pairs={{0,1},{1,0},{2,3},{3,2},{4,5},{5,4},{6,7},{7,6},{8,9},{9,8},{10,11... | collective-permute-start | bytes 884744 | tf_op jit(solution)/shard_map/ppermute | solution.py:544
  187.5 4.4 %collective-permute-start.21 = (bf16[128,1152]{1,0:T(8,128)(2,1)S(1)}, bf16[128,1152]{1,0:T(8,128)(2,1)S(1)}, u32[]{:S(2)}, u32[]{:S(2)}) collective-permute-start(bf16[128,1152]{1,0:T(8,128)(2,1)S(1)} %collective-permute-done.17.refs_4_), channel_id=1, source_target_pairs={{0,1},{1,0},{2,3},{3,2},{4,5},{5,4},{6,7},{7,6},{8,9},{9,8},{10,11... | collective-permute-start | bytes 884744 | tf_op jit(solution)/shard_map/ppermute | solution.py:544
  202.6 1.5 copy-start.9
  (12 other events, 10.7 us)
Sparse Core Ops, SparseCore 0:
  10.2 65.3 all-gather.2

commit v6 on v5

--- a/solution.py
+++ b/solution.py
@@ -11,12 +11,20 @@
 BLOCK = 768
 
 
-def params(mib):
-    return pltpu.CompilerParams(vmem_limit_bytes=mib * 1024 * 1024)
-
-
-def whole():
-    return pl.BlockSpec(memory_space=pltpu.VMEM)
+def params():
+    return pltpu.CompilerParams(vmem_limit_bytes=60 * 1024 * 1024)
+
+
+def full(array):
+    return pl.BlockSpec(array.shape, lambda *_: (0,) * len(array.shape))
+
+
+def fulls(arrays):
+    return [full(a) for a in arrays]
+
+
+def shape(dims, kind):
+    return jax.ShapeDtypeStruct(dims, kind)
 
 
 def scalars():
@@ -95,11 +103,11 @@
             ],
         ),
         out_shape=[
-            jax.ShapeDtypeStruct((merged, window * width), BF),
-            jax.ShapeDtypeStruct((window, merged, width), BF),
-            jax.ShapeDtypeStruct((merged, 128), F32),
+            shape((merged, window * width), BF),
+            shape((window, merged, width), BF),
+            shape((merged, 128), F32),
         ],
-        compiler_params=params(12),
+        compiler_params=params(),
         cost_estimate=cost(2 * rows * block * window * width, 6 * rows * width),
         name="layer_norm",
     )(core, features, gain, bias)
@@ -121,43 +129,47 @@
 def collect(pos, stream, cot):
     slots = pos.shape[0]
     rows, width = stream.shape
+    out = shape((2, slots, width), BF)
     return pl.pallas_call(
         collect_kernel,
-        in_specs=[whole()] * 3,
-        out_specs=whole(),
-        out_shape=jax.ShapeDtypeStruct((2, slots, width), BF),
-        compiler_params=params(12),
+        grid=(1,),
+        in_specs=fulls((pos, stream, cot)),
+        out_specs=full(out),
+        out_shape=out,
+        compiler_params=params(),
         cost_estimate=cost(4 * slots * rows * width, 8 * rows * width),
         name="collect",
     )(pos, stream, cot)
 
 
-def unpack_kernel(slot_ref, came_ref, ngain_ref, base_ref, up_ref):
+def unpack_kernel(slot_ref, came_ref, base_ref, cot_ref):
     tokens, width = base_ref.shape
     slots = came_ref.shape[0]
     take = eq_hot((tokens, slots), 1, slot_ref[...])
-    base_ref[...] = jnp.dot(take, came_ref[:, :width], preferred_element_type=F32)
-    up_ref[...] = jnp.dot(take, came_ref[:, width:], preferred_element_type=F32) * ngain_ref[
-        ...
-    ].astype(F32)
-
-
-def unpack(slot_col, came, ngain):
+    for start, out_ref in ((0, base_ref), (width, cot_ref)):
+        out_ref[...] = jnp.dot(
+            take, came_ref[:, start : start + width], preferred_element_type=F32
+        ).astype(BF)
+
+
+def unpack(slot_col, came):
     tokens = slot_col.shape[0]
     slots, both = came.shape
     width = both // 2
+    outs = [shape((tokens, width), BF)] * 2
     return pl.pallas_call(
         unpack_kernel,
-        in_specs=[whole()] * 3,
-        out_specs=[whole()] * 2,
-        out_shape=[jax.ShapeDtypeStruct((tokens, width), F32)] * 2,
-        compiler_params=params(12),
+        grid=(1,),
+        in_specs=fulls((slot_col, came)),
+        out_specs=fulls(outs),
+        out_shape=outs,
+        compiler_params=params(),
         cost_estimate=cost(4 * slots * tokens * width, 8 * tokens * width),
         name="unpack",
-    )(slot_col, came, ngain)
-
-
-def merge_kernel(base_ref, up_ref, w_ref, *refs):
+    )(slot_col, came)
+
+
+def merge_kernel(base_ref, cot_ref, ngain_ref, w_ref, *refs):
     lifted, (visual_ref, state_ref, stat_ref, held_ref, left_ref, sems) = refs[:-6], refs[-6:]
     steps = range(w_ref.shape[0] // BLOCK)
     copies = []
@@ -184,38 +196,37 @@
         total = part if total is None else total + part
     visual = total.astype(BF)
     visual_ref[...] = visual
-    state = base_ref[...] + visual.astype(F32)
+    state = base_ref[...].astype(F32) + visual.astype(F32)
     state_ref[...] = state
+    up = ngain_ref[...].astype(F32) * cot_ref[...].astype(F32)
     lane = lax.broadcasted_iota(jnp.int32, (state.shape[0], 128), 1)
     sums = jnp.where(
         lane == 0,
         jnp.sum(state * state, axis=1, keepdims=True),
-        jnp.sum(up_ref[...] * state, axis=1, keepdims=True),
+        jnp.sum(up * state, axis=1, keepdims=True),
     )
     stat_ref[...] = sums.T[: stat_ref.shape[0]]
 
 
-def merge(base, up, weight, lifted):
+def merge(base, cot, ngain, weight, lifted):
     tokens, width = base.shape
     depth = weight.shape[0]
+    outs = [shape((tokens, width), BF), shape((tokens, width), F32), shape((8, tokens), F32)]
     return pl.pallas_call(
         merge_kernel,
-        in_specs=[whole()] * 2 + [anywhere()] * (1 + len(lifted)),
-        out_specs=[whole()] * 3,
-        out_shape=[
-            jax.ShapeDtypeStruct((tokens, width), BF),
-            jax.ShapeDtypeStruct((tokens, width), F32),
-            jax.ShapeDtypeStruct((8, tokens), F32),
-        ],
+        grid=(1,),
+        in_specs=fulls((base, cot, ngain)) + [anywhere()] * (1 + len(lifted)),
+        out_specs=fulls(outs),
+        out_shape=outs,
         scratch_shapes=[
             pltpu.VMEM((depth, width), BF),
             pltpu.VMEM((tokens, depth), BF),
             pltpu.SemaphoreType.DMA((depth // BLOCK, 1 + len(lifted))),
         ],
-        compiler_params=params(22),
+        compiler_params=params(),
         cost_estimate=cost(2 * depth * tokens * width, 2 * depth * width),
         name="merge",
-    )(base, up, weight, *lifted)
+    )(base, cot, ngain, weight, *lifted)
 
 
 def pack_kernel(slot_ref, visual_ref, stay_ref, cross_ref):
@@ -228,12 +239,14 @@
 
 def pack(slot_row, visual, slots):
     tokens, width = visual.shape
+    outs = [shape((slots // 2, width), BF)] * 2
     return pl.pallas_call(
         pack_kernel,
-        in_specs=[whole()] * 2,
-        out_specs=[whole()] * 2,
-        out_shape=[jax.ShapeDtypeStruct((slots // 2, width), BF)] * 2,
-        compiler_params=params(8),
+        grid=(1,),
+        in_specs=fulls((slot_row, visual)),
+        out_specs=fulls(outs),
+        out_shape=outs,
+        compiler_params=params(),
         cost_estimate=cost(2 * slots * tokens * width, 2 * (slots + tokens) * width),
         name="pack",
     )(slot_row, visual)
@@ -242,70 +255,70 @@
 RING = 4
 
 
-def backward_kernel(full_width, chunks, at_ref, state_ref, up_ref, w_ref, *refs):
+def backward_kernel(full_width, chunks, at_ref, state_ref, cot_ref, ngain_ref, w_ref, *refs):
     stats, refs = refs[:RING], refs[RING:]
-    outs, (picked_ref, sums_ref, held_ref, sems) = refs[: 3 * chunks], refs[3 * chunks :]
-    copies = []
-    for step in range(w_ref.shape[0] // BLOCK):
-        at = pl.ds(step * BLOCK, BLOCK)
-        copies.append(pltpu.make_async_copy(w_ref.at[at], held_ref.at[at], sems.at[step]))
-        copies[step].start()
+    outs, (picked_ref, sums_ref) = refs[: 3 * chunks], refs[3 * chunks :]
     tokens = state_ref.shape[0]
     rows = tokens // 2 // RING // chunks
-    total = stats[0][...]
-    for ref in stats[1:]:
-        total = total + ref[...]
-    sums_ref[...] = total.T
-    img, far = at_ref[0], at_ref[1]
-    for core in range(2):
-        for chunk in range(chunks):
-            for away in range(RING):
-                there = lax.rem(2 * far + img + away, RING)
-                partner = lax.rem(there + img, 2)
-                begin = partner * (tokens // 2) + core * (tokens // 4) + (there // 2) * (tokens // 8)
-                at = pl.ds(pl.multiple_of(begin + chunk * rows, rows), rows)
-                sums = sums_ref[at, :]
-                inv = lax.rsqrt(sums[:, 0:1] / full_width + 1e-06)
-                inner = sums[:, 1:2] / full_width
-                grad = inv * up_ref[at, :] - state_ref[at, :] * (inv * inv * inv * inner)
-                to = ((core * chunks + chunk) * RING + away) * rows
-                picked_ref[to : to + rows, :] = grad.astype(BF)
-    for step, copy in enumerate(copies):
-        cols = slice(step * BLOCK, (step + 1) * BLOCK)
-        copy.wait()
-        both = lax.dot_general(
-            picked_ref[...], held_ref[cols, :], (((1,), (1,)), ((), ())), preferred_element_type=F32
-        )
-        for chunk in range(chunks):
-            own, rest, other = outs[chunk], outs[chunks + chunk], outs[2 * chunks + chunk]
-            start = chunk * RING * rows
-            own[:, cols] = both[start : start + rows]
-            rest[:, cols] = both[start + rows : start + RING * rows]
-            start += tokens // 2
-            other[:, cols] = both[start : start + RING * rows].astype(BF)
-
-
-def backward(at, state, up, stats, weight, chunks, full_width):
+
+    @pl.when(pl.program_id(0) == 0)
+    def _():
+        total = stats[0][...]
+        for ref in stats[1:]:
+            total = total + ref[...]
+        sums_ref[...] = total.T
+        img, far = at_ref[0], at_ref[1]
+        gain = ngain_ref[...].astype(F32)
+        for core in range(2):
+            for chunk in range(chunks):
+                for away in range(RING):
+                    there = lax.rem(2 * far + img + away, RING)
+                    partner = lax.rem(there + img, 2)
+                    begin = partner * (tokens // 2) + core * (tokens // 4) + (there // 2) * (tokens // 8)
+                    at = pl.ds(pl.multiple_of(begin + chunk * rows, rows), rows)
+                    sums = sums_ref[at, :]
+                    inv = lax.rsqrt(sums[:, 0:1] / full_width + 1e-06)
+                    inner = sums[:, 1:2] / full_width
+                    up = gain * cot_ref[at, :].astype(F32)
+                    grad = inv * up - state_ref[at, :] * (inv * inv * inv * inner)
+                    to = ((core * chunks + chunk) * RING + away) * rows
+                    picked_ref[to : to + rows, :] = grad.astype(BF)
+
+    both = lax.dot_general(
+        picked_ref[...], w_ref[...], (((1,), (1,)), ((), ())), preferred_element_type=F32
+    )
+    for chunk in range(chunks):
+        own, rest, other = outs[chunk], outs[chunks + chunk], outs[2 * chunks + chunk]
+        start = chunk * RING * rows
+        own[...] = both[start : start + rows]
+        rest[...] = both[start + rows : start + RING * rows].astype(BF)
+        start += tokens // 2
+        other[...] = both[start : start + RING * rows].astype(BF)
+
+
+def backward(at, state, cot, ngain, stats, weight, chunks, full_width):
     depth, width = weight.shape
     tokens = state.shape[0]
     rows = tokens // 2 // RING // chunks
+    outs = (
+        [shape((rows, depth), F32)] * chunks
+        + [shape(((RING - 1) * rows, depth), BF)] * chunks
+        + [shape((RING * rows, depth), BF)] * chunks
+    )
     return pl.pallas_call(
         lambda *refs: backward_kernel(full_width, chunks, *refs),
-        in_specs=[scalars()] + [whole()] * 2 + [anywhere()] + [whole()] * RING,
-        out_specs=[whole()] * (3 * chunks),
-        out_shape=[jax.ShapeDtypeStruct((rows, depth), F32)] * chunks
-        + [jax.ShapeDtypeStruct(((RING - 1) * rows, depth), F32)] * chunks
-        + [jax.ShapeDtypeStruct((RING * rows, depth), BF)] * chunks,
-        scratch_shapes=[
-            pltpu.VMEM((tokens, width), BF),
-            pltpu.VMEM((tokens, 8), F32),
-            pltpu.VMEM((depth, width), BF),
-            pltpu.SemaphoreType.DMA((depth // BLOCK,)),
-        ],
-        compiler_params=params(24),
+        grid=(depth // BLOCK,),
+        in_specs=[scalars()]
+        + fulls((state, cot, ngain))
+        + [pl.BlockSpec((BLOCK, width), lambda i: (i, 0))]
+        + fulls(stats),
+        out_specs=[pl.BlockSpec((o.shape[0], BLOCK), lambda i: (0, i)) for o in outs],
+        out_shape=outs,
+        scratch_shapes=[pltpu.VMEM((tokens, width), BF), pltpu.VMEM((tokens, 8), F32)],
+        compiler_params=params(),
         cost_estimate=cost(2 * depth * tokens * width, 2 * depth * width),
         name="backward",
-    )(at, state, up, weight, *stats)
+    )(at, state, cot, ngain, weight, *stats)
 
 
 def pair_kernel(rest_ref, got_ref, *outs):
@@ -313,17 +326,20 @@
     for away, out in enumerate(outs):
         at = slice(away * rows, (away + 1) * rows)
         got = slice((away + 1) * rows, (away + 2) * rows)
-        out[...] = (rest_ref[at, :] + got_ref[got, :].astype(F32)).astype(BF)
+        out[...] = (rest_ref[at, :].astype(F32) + got_ref[got, :].astype(F32)).astype(BF)
 
 
 def pair(rest, got):
     rows, depth = got.shape[0] // RING, got.shape[1]
+    cols = depth // 4
+    outs = [shape((rows, depth), BF)] * (RING - 1)
     return pl.pallas_call(
         pair_kernel,
-        in_specs=[whole()] * 2,
-        out_specs=[whole()] * (RING - 1),
-        out_shape=[jax.ShapeDtypeStruct((rows, depth), BF)] * (RING - 1),
-        compiler_params=params(12),
+        grid=(depth // cols,),
+        in_specs=[pl.BlockSpec((a.shape[0], cols), lambda i: (0, i)) for a in (rest, got)],
+        out_specs=[pl.BlockSpec((rows, cols), lambda i: (0, i))] * (RING - 1),
+        out_shape=outs,
+        compiler_params=params(),
         cost_estimate=cost(4 * rows * depth, 24 * rows * depth),
         name="pair",
     )(rest, got)
@@ -358,9 +374,9 @@
 
 
 def finish(block, own, got, came, xw, stat, gain):
-    tokens, full = own.shape
+    tokens, depth = own.shape
     window, width = gain.shape
-    same = pl.BlockSpec((tokens, full), lambda i, b: (0, 0))
+    same = pl.BlockSpec((tokens, depth), lambda i, b: (0, 0))
     return pl.pallas_call(
         finish_kernel,
         grid_spec=pltpu.PrefetchScalarGridSpec(
@@ -374,8 +390,8 @@
             ],
             out_specs=pl.BlockSpec((tokens * window, width), lambda i, b: (0, 0)),
         ),
-        out_shape=jax.ShapeDtypeStruct((tokens * window, width), BF),
-        compiler_params=params(12),
+        out_shape=shape((tokens * window, width), BF),
+        compiler_params=params(),
         cost_estimate=cost(2 * (tokens * window) ** 2 * width, 8 * window * tokens * width),
         name="finish",
     )(block, own, got, *came, xw, stat, gain)
@@ -399,10 +415,11 @@
     rows, width = stream.shape
     return pl.pallas_call(
         place_kernel,
-        in_specs=[scalars()] + [whole()] * 3,
-        out_specs=whole(),
-        out_shape=jax.ShapeDtypeStruct((rows, width), BF),
-        compiler_params=params(12),
+        grid=(1,),
+        in_specs=[scalars()] + fulls((pos, came, stream)),
+        out_specs=full(stream),
+        out_shape=shape((rows, width), BF),
+        compiler_params=params(),
         cost_estimate=cost(2 * pos.shape[1] * rows * width, 6 * rows * width),
         name="place",
     )(img, pos, came, stream)
@@ -427,11 +444,12 @@
     rows, width = blocks[0].shape
     return pl.pallas_call(
         lambda *refs: lay_kernel(chunks, *refs),
-        in_specs=[scalars()] + [anywhere()] * len(blocks),
+        grid=(1,),
+        in_specs=[scalars()] + fulls(blocks),
         out_specs=anywhere(),
-        out_shape=jax.ShapeDtypeStruct((len(blocks) * rows, width), BF),
+        out_shape=shape((len(blocks) * rows, width), BF),
         scratch_shapes=[pltpu.SemaphoreType.DMA((len(blocks),))],
-        compiler_params=params(4),
+        compiler_params=params(),
         cost_estimate=cost(0, 4 * len(blocks) * rows * width),
         name="lay",
     )(at, *blocks)
@@ -488,6 +506,13 @@
         packed.reshape(owners, capacity), ("img", "ctx"), split_axis=0, concat_axis=0, tiled=True
     )
     asked = asked.reshape(n_img, n_ctx, capacity).transpose(1, 0, 2)
+    features, asked = lax.optimization_barrier((features, asked))
+    gain = ln_gain[0]
+    lifted, xw, stat = layer_norm(core_in, features[0], gain, ln_bias[0])
+    sent_on = [lifted[: merged // 4], lifted[merged // 4 : merged // 2]]
+    sent_on, asked = lax.optimization_barrier((sent_on, asked))
+    next_mine = [along_x(sent_on[0], 1), along_x(sent_on[1], -1)]
+    next_other = [lax.ppermute(x, "tp", core_pairs) for x in next_mine]
     held = collect(asked.reshape(slot_count, 1), stream, cotangent[0])
     came = lax.all_to_all(
         held.reshape(owners, n_img * capacity, width),
@@ -496,14 +521,9 @@
     paired = target * (n_img * capacity) + rank + img * capacity
     paired = jnp.concatenate([paired, lax.ppermute(paired, "img", flip)])
 
-    gain = ln_gain[0]
-    lifted, xw, stat = layer_norm(core_in, features[0], gain, ln_bias[0])
-    next_mine = lax.ppermute(lifted[: merged // 2], "img", flip)
-    next_other = lax.ppermute(next_mine, "tp", core_pairs)
-
     own_gain = lax.dynamic_slice_in_dim(norm_gain, img * cut, cut, axis=1)
-    base, up = unpack(paired.reshape(-1, 1), came, own_gain)
-    visual, state, sums = merge(base, up, weight, (lifted, next_mine, next_other))
+    base, cot = unpack(paired.reshape(-1, 1), came)
+    visual, state, sums = merge(base, cot, own_gain, weight, [lifted] + next_mine + next_other)
 
     quarter = merged // 2
     near = sums + lax.ppermute(swap_lanes(sums, quarter), "tp", core_pairs)
@@ -518,20 +538,21 @@
 
     chunks = 2
     at = jnp.stack([img, far_half])
-    parts = backward(at, state, up, stats, weight, chunks, full_width)
+    parts = backward(at, state, cot, own_gain, stats, weight, chunks, full_width)
+    parts, crossed = lax.optimization_barrier((parts, crossed))
     own, rest, other = (parts[i * chunks : (i + 1) * chunks] for i in range(3))
     got = [lax.ppermute(o, "tp", core_pairs) for o in other]
-    got[0], crossed = lax.optimization_barrier((got[0], crossed))
     sent = [pair(rest[c], got[c]) for c in range(chunks)]
+    stay, crossed, sent[1] = lax.optimization_barrier((stay, crossed, sent[1]))
     came_back = [[along_x(sent[c][by - 1], by) for by in (1, 2, 3)] for c in range(chunks)]
-
-    stay, crossed, sent[0] = lax.optimization_barrier((stay, crossed, sent[0]))
     send = jnp.concatenate(
         [x.reshape(n_ctx, 1, n_img * capacity, cut) for x in (stay, crossed)], axis=1
     )
     arrived = lax.all_to_all(send, "ctx", split_axis=0, concat_axis=0, tiled=True)
     arrived = arrived.transpose(1, 0, 2, 3).reshape(n_img, slot_count, cut)
     new_stream = place(img.reshape(1), asked.reshape(1, slot_count), arrived, stream)
+
+    new_stream, came_back[1] = lax.optimization_barrier((new_stream, came_back[1]))
 
     quarters = [[], [], [], []]
     for c in range(chunks):

time: 215 us -> 208 us (0.967)
  local copies, waits for them, and re-layouts: 30.6 us -> 15.9 us
  blocking collectives: 31.3 us -> 16.7 us
  Pallas kernels: 38.9 us -> 52.4 us
  starting transfers between devices: 42.1 us -> 48.5 us
  other arithmetic: 1.61 us -> 5.74 us
    ppermute x9 -> x11, waiting for transfers between devices: 11.7 us -> 44.8 us  [along_x(): return lax.ppermute(array, ('img', 'tp'), pairs)]
    unnamed x70 -> x50, local copies, waits for them, and re-layouts: 26.1 us -> 7.83 us
    ppermute x1, waiting for transfers between devices: 18.9 us -> 2.19 us  [shards(): paired = jnp.concatenate([paired, lax.ppermute(paired, 'img', flip)])]
    all_to_all x1, blocking collectives: 31.3 us -> 16.7 us  [shards(): lax.all_to_all(packed.reshape(owners, capacity), ('img', 'ctx'), split_ax...]
    ppermute x1, waiting for transfers between devices: 13.1 us -> 2.89 us  [shards(): crossed = lax.ppermute(cross, 'img', flip)]
    pallas_call x8, Pallas kernels: 25.1 us -> 31.9 us  [the longest x1 7.54 us: merge(): pl.pallas_call(merge_kernel, grid=(1,), in_specs=fulls((base, cot, ngain)...]
    all_to_all x1, waiting for transfers between devices: 6.38 us -> 0.01 us  [shards(): lax.all_to_all(held.reshape(owners, n_img * capacity, width), ('img', 'ct...]
    ppermute x2, starting transfers between devices: 3.71 us -> 7.94 us  [shards(): quarters[3].append(lax.ppermute(beyond, 'tp', core_pairs))]
  transfers between devices with their start and end apart: 25 -> 27, of which waited for: 9 -> 11; matrix products, arithmetic and copies ran while one was open for 2% -> 6% of each run, Pallas kernels for 12% -> 20%
where the time goes in v6:
time: 208 us; the launch traced here: 207 us
  waiting for transfers between devices  53.4 us (26%)
  Pallas kernels  52.4 us (25%)
  starting transfers between devices  48.5 us (23%)
  blocking collectives  16.7 us (8%)
  local copies, waits for them, and re-layouts  15.9 us (8%)
  between operations  14.3 us (7%)
  other arithmetic  5.74 us (3%)
    ppermute x11, waiting for transfers between devices, along_x(): return lax.ppermute(array, ('img', 'tp'), pairs)  44.8 us
    all_to_all x1, blocking collectives, shards(): lax.all_to_all(packed.reshape(owners, capacity), ('img', 'ctx'), split_ax...  16.7 us
    ppermute x11, starting transfers between devices, along_x(): return lax.ppermute(array, ('img', 'tp'), pairs)  13 us
    pallas_call x1, Pallas kernels, backward(): pl.pallas_call(lambda *refs: backward_kernel(full_width, chunks, *refs),...  8.91 us
    ppermute x2, starting transfers between devices, shards(): quarters[3].append(lax.ppermute(beyond, 'tp', core_pairs))  7.94 us
    unnamed x50, local copies, waits for them, and re-layouts  7.83 us
    pallas_call x1, Pallas kernels, merge(): pl.pallas_call(merge_kernel, grid=(1,), in_specs=fulls((base, cot, ngain)...  7.54 us
    pallas_call x2, Pallas kernels, pair(): pl.pallas_call(pair_kernel, grid=(depth // cols,), in_specs=[pl.BlockSpec...  7.35 us
  transfers between devices with their start and end apart: 27, of which 11 were waited for; matrix products, arithmetic and copies ran while one was open for 6% of the time, Pallas kernels for 20%

profile of v6, /device:TPU:1, one launch (start us, length us, event | category | flops | bytes accessed | tf_op | source)
XLA Modules:
  0.0 207.1 jit_solution(16086739338114556428)
XLA Ops:
  7.2 1.0 copy-done
  10.2 16.7 %all_to_all.19 = s32[32,1,16]{2,1,0:T(1,128)S(1)} all-to-all(s32[32,1,16]{2,1,0:T(1,128)S(1)} %bitcast.42), channel_id=1, replica_groups=mesh['img'=2,'ctx'=16,'tp'=4] {'img','ctx'}, dimensions={0} | all-to-all | bytes 4096 | tf_op jit(solution)/shard_map/all_to_all | solution.py:505
  27.0 5.8 %layer_norm.1 = (bf16[256,4608]{1,0:T(8,128)(2,1)}, bf16[4,256,1152]{2,1,0:T(8,128)(2,1)}, f32[256,128]{1,0:T(8,128)}) custom-call(s32[1]{0:T(128)} %bitcast.1.core_ref, bf16[1024,1152]{1,0:T(8,128)(2,1)} %bitcast.32, bf16[4,1152]{1,0:T(4,128)(2,1)} %bitcast.38, bf16[4,1152]{1,0:T(4,128)(2,1)} %bitcast.44), custom_call_target="tpu_custom_call" | custom-call | flops 603979776 | bytes 7077888 | tf_op jit(solution)/shard_map/layer_norm/pallas_call | solution.py:86
  32.9 2.4 %fusion.2 = (bf16[64,4608]{1,0:T(8,128)(2,1)}, bf16[64,4608]{1,0:T(8,128)(2,1)}) fusion(bf16[256,4608]{1,0:T(8,128)(2,1)} %get-tuple-element.51.refs_0_), kind=kLoop, calls=%fused_computation.25 | loop fusion | bytes 2359296 | tf_op jit(solution)/shard_map/slice | solution.py:512
  35.3 0.9 reshape.120.pos_ref
  36.2 4.3 %collect.1 = bf16[2,512,1024]{2,1,0:T(8,128)(2,1)} custom-call(s32[512,1]{1,0:T(8,128)} %reshape.120.pos_ref, bf16[512,1024]{1,0:T(8,128)(2,1)} %stream_ref.3, bf16[512,1024]{1,0:T(8,128)(2,1)} %bitcast.35), custom_call_target="tpu_custom_call" | custom-call | flops 1073741824 | bytes 4194304 | tf_op jit(solution)/shard_map/collect/pallas_call | solution.py:133
  40.5 4.1 %all-to-all-start.1 = ((bf16[32,32,1024]{2,1,0:T(8,128)(2,1)}), bf16[32,32,1024]{2,1,0:T(8,128)(2,1)S(1)}, u32[]{:S(2)}, u32[]{:S(2)}) async-start(bf16[32,32,1024]{2,1,0:T(8,128)(2,1)} %bitcast.27), calls=%async_computation.1 | async-start | bytes 4194304 | tf_op jit(solution)/shard_map/all_to_all | solution.py:517
  44.7 1.3 collective-permute-start.1
  46.0 1.5 collective-permute-start.2
  47.4 30.6 %collective-permute-done.1.refs_1_ = bf16[64,4608]{1,0:T(8,128)(2,1)S(1)} collective-permute-done((bf16[64,4608]{1,0:T(8,128)(2,1)}, bf16[64,4608]{1,0:T(8,128)(2,1)S(1)}, u32[]{:S(2)}, u32[]{:S(2)}) %collective-permute-start.1) | collective-permute-done | bytes 589856 | tf_op jit(solution)/shard_map/ppermute | solution.py:490
  78.0 2.8 %collective-permute-start.3 = (bf16[64,4608]{1,0:T(8,128)(2,1)S(1)}, bf16[64,4608]{1,0:T(8,128)(2,1)}, u32[]{:S(2)}, u32[]{:S(2)}) collective-permute-start(bf16[64,4608]{1,0:T(8,128)(2,1)S(1)} %collective-permute-done.1.refs_1_), channel_id=1, source_target_pairs={{0,1},{1,0},{2,3},{3,2},{4,5},{5,4},{6,7},{7,6},{8,9},{9,8},{10,11... | collective-permute-start | bytes 1769480 | tf_op jit(solution)/shard_map/ppermute | solution.py:515
  80.8 2.1 %collective-permute-start.4 = (bf16[64,4608]{1,0:T(8,128)(2,1)}, bf16[64,4608]{1,0:T(8,128)(2,1)}, u32[]{:S(2)}, u32[]{:S(2)}) collective-permute-start(bf16[64,4608]{1,0:T(8,128)(2,1)} %collective-permute-done.2.refs_2_), channel_id=1, source_target_pairs={{0,1},{1,0},{2,3},{3,2},{4,5},{5,4},{6,7},{7,6},{8,9},{9,8},{10,11... | collective-permute-start | bytes 1769480 | tf_op jit(solution)/shard_map/ppermute | solution.py:515
  83.6 2.2 %collective-permute-done = s32[256]{0:T(256)S(1)} collective-permute-done((s32[256]{0:T(256)S(1)}, s32[256]{0:T(256)S(1)}, u32[]{:S(2)}, u32[]{:S(2)}) %collective-permute-start) | collective-permute-done | bytes 1056 | tf_op jit(solution)/shard_map/ppermute | solution.py:522
  85.8 0.9 copy.29.slot_ref
  86.6 1.4 copy-done.3
  88.0 3.8 %unpack.1 = (bf16[512,512]{1,0:T(8,128)(2,1)}, bf16[512,512]{1,0:T(8,128)(2,1)}) custom-call(s32[512,1]{1,0:T(8,128)} %copy.29.slot_ref, bf16[1024,1024]{1,0:T(8,128)(2,1)} %bitcast.34), custom_call_target="tpu_custom_call" | custom-call | flops 1073741824 | bytes 2097152 | tf_op jit(solution)/shard_map/unpack/pallas_call | solution.py:160
  91.8 7.5 %merge.1 = (bf16[512,512]{1,0:T(8,128)(2,1)}, f32[512,512]{1,0:T(8,128)}, f32[8,512]{1,0:T(8,128)}) custom-call(bf16[512,512]{1,0:T(8,128)(2,1)} %get-tuple-element.54.base_ref, bf16[512,512]{1,0:T(8,128)(2,1)} %get-tuple-element.55.cot_ref.refs_2_, bf16[1,512]{1,0:T(2,128)(2,1)} %constant_dynamic-slice_fusion.1.ngain_ref.refs_3_, ...), custom_call_target="tpu_custom_call" | custom-call | flops 2415919104 | bytes 4718592 | tf_op jit(solution)/shard_map/merge/pallas_call | solution.py:215
  100.1 0.8 collective-permute-start.5
  102.5 2.5 %collective-permute-start.7 = (f32[8,512]{1,0:T(8,128)S(1)}, f32[8,512]{1,0:T(8,128)S(1)}, u32[]{:S(2)}, u32[]{:S(2)}) collective-permute-start(f32[8,512]{1,0:T(8,128)S(1)} %add.61.refs_5_), channel_id=1, source_target_pairs={{0,2},{1,3},{2,0},{3,1},{64,66},{65,67},{66,64},{67,65},{4,6},{5,7... | collective-permute-start | bytes 49160 | tf_op jit(solution)/shard_map/ppermute | solution.py:490
  105.0 2.7 %collective-permute-start.8 = (f32[8,512]{1,0:T(8,128)S(1)}, f32[8,512]{1,0:T(8,128)S(1)}, u32[]{:S(2)}, u32[]{:S(2)}) collective-permute-start(f32[8,512]{1,0:T(8,128)S(1)} %pad_maximum_fusion.2), channel_id=1, source_target_pairs={{0,66},{1,67},{2,64},{3,65},{64,0},{65,1},{66,2},{67,3},{4,70},{5,... | collective-permute-start | bytes 49160 | tf_op jit(solution)/shard_map/ppermute | solution.py:490
  107.7 2.6 %pack.1 = (bf16[512,512]{1,0:T(8,128)(2,1)}, bf16[512,512]{1,0:T(8,128)(2,1)}) custom-call(s32[1,512]{1,0:T(1,128)} %compare_select_fusion.slot_ref, bf16[512,512]{1,0:T(8,128)(2,1)} %get-tuple-element.58.visual_ref), custom_call_target="tpu_custom_call" | custom-call | flops 536870912 | bytes 1572864 | tf_op jit(solution)/shard_map/pack/pallas_call | solution.py:243
  111.0 8.9 %backward.1 = (f32[32,4608]{1,0:T(8,128)}, f32[32,4608]{1,0:T(8,128)}, bf16[96,4608]{1,0:T(8,128)(2,1)}, bf16[96,4608]{1,0:T(8,128)(2,1)}, bf16[128,4608]{1,0:T(8,128)(2,1)}, /*index=5*/bf16[128,4608]{1,0:T(8,128)(2,1)}) custom-call(s32[2]{0:T(128)} %pad_add_fusion.2.refs_0_, f32[512,512]{1,0:T(8,128)} %get-tuple-element.60.refs_1_, ...), custom_call_target="tpu_custom_call" | custom-call | flops 2415919104 | bytes 4718592 | tf_op jit(solution)/shard_map/backward/pallas_call | solution.py:308
  120.0 2.9 %collective-permute-done.9 = bf16[512,512]{1,0:T(8,128)(2,1)S(1)} collective-permute-done((bf16[512,512]{1,0:T(8,128)(2,1)}, bf16[512,512]{1,0:T(8,128)(2,1)S(1)}, u32[]{:S(2)}, u32[]{:S(2)}) %collective-permute-start.9) | collective-permute-done | bytes 524320 | tf_op jit(solution)/shard_map/ppermute | solution.py:537
  123.7 2.1 %collective-permute-start.10 = (bf16[128,4608]{1,0:T(8,128)(2,1)}, bf16[128,4608]{1,0:T(8,128)(2,1)S(1)}, u32[]{:S(2)}, u32[]{:S(2)}) collective-permute-start(bf16[128,4608]{1,0:T(8,128)(2,1)} %get-tuple-element.76), channel_id=1, source_target_pairs={{0,1},{1,0},{2,3},{3,2},{4,5},{5,4},{6,7},{7,6},{8,9},{9,8},{10,11... | collective-permute-start | bytes 3538952 | tf_op jit(solution)/shard_map/ppermute | solution.py:544
  125.8 2.7 %collective-permute-done.10.got_ref = bf16[128,4608]{1,0:T(8,128)(2,1)S(1)} collective-permute-done((bf16[128,4608]{1,0:T(8,128)(2,1)}, bf16[128,4608]{1,0:T(8,128)(2,1)S(1)}, u32[]{:S(2)}, u32[]{:S(2)}) %collective-permute-start.10) | collective-permute-done | bytes 1179680 | tf_op jit(solution)/shard_map/ppermute | solution.py:544
  128.4 1.1 copy-done.1
  129.5 3.7 %pair.2 = (bf16[32,4608]{1,0:T(8,128)(2,1)}, bf16[32,4608]{1,0:T(8,128)(2,1)}, bf16[32,4608]{1,0:T(8,128)(2,1)}) custom-call(bf16[96,4608]{1,0:T(8,128)(2,1)} %get-tuple-element.75.rest_ref, bf16[128,4608]{1,0:T(8,128)(2,1)} %copy-done.1), custom_call_target="tpu_custom_call" | custom-call | flops 589824 | bytes 3538944 | tf_op jit(solution)/shard_map/pair/pallas_call | solution.py:336
  133.2 2.1 %pad_maximum_fusion = bf16[16,2,32,512]{3,2,1,0:T(8,128)(2,1)} fusion(bf16[16,1,32,512]{3,2,1,0:T(8,128)(2,1)} %bitcast.37, bf16[16,1,32,512]{3,2,1,0:T(8,128)(2,1)S(1)} %bitcast.36), kind=kLoop, calls=%fused_computation | loop fusion | flops 524288 | bytes 2097152 | tf_op jit(solution)/shard_map/concatenate | solution.py:548
  135.3 6.5 %all-to-all-start.2 = ((bf16[16,2,32,512]{3,2,1,0:T(8,128)(2,1)}), bf16[16,2,32,512]{3,2,1,0:T(8,128)(2,1)S(1)}, u32[]{:S(2)}, u32[]{:S(2)}) async-start(bf16[16,2,32,512]{3,2,1,0:T(8,128)(2,1)} %pad_maximum_fusion), calls=%async_computation.2 | async-start | bytes 2097152 | tf_op jit(solution)/shard_map/all_to_all | solution.py:551
  141.8 1.0 copy-done.2
  142.8 3.7 %pair.3 = (bf16[32,4608]{1,0:T(8,128)(2,1)}, bf16[32,4608]{1,0:T(8,128)(2,1)}, bf16[32,4608]{1,0:T(8,128)(2,1)}) custom-call(bf16[96,4608]{1,0:T(8,128)(2,1)} %get-tuple-element.88.rest_ref, bf16[128,4608]{1,0:T(8,128)(2,1)} %copy-done.2), custom_call_target="tpu_custom_call" | custom-call | flops 589824 | bytes 3538944 | tf_op jit(solution)/shard_map/pair/pallas_call | solution.py:336
  146.5 2.3 %collective-permute-start.16 = (bf16[32,4608]{1,0:T(8,128)(2,1)}, bf16[32,4608]{1,0:T(8,128)(2,1)S(1)}, u32[]{:S(2)}, u32[]{:S(2)}) collective-permute-start(bf16[32,4608]{1,0:T(8,128)(2,1)} %get-tuple-element.90), channel_id=1, source_target_pairs={{0,2},{1,3},{2,0},{3,1},{64,66},{65,67},{66,64},{67,65},{4,6},{5,7... | collective-permute-start | bytes 884744 | tf_op jit(solution)/shard_map/ppermute | solution.py:490
  149.4 0.9 collective-permute-start.11
  150.2 1.3 collective-permute-start.12
  151.6 4.7 %collective-permute-done.15.refs_0_ = bf16[32,4608]{1,0:T(8,128)(2,1)S(1)} collective-permute-done((bf16[32,4608]{1,0:T(8,128)(2,1)}, bf16[32,4608]{1,0:T(8,128)(2,1)S(1)}, u32[]{:S(2)}, u32[]{:S(2)}) %collective-permute-start.15) | collective-permute-done | bytes 294944 | tf_op jit(solution)/shard_map/ppermute | solution.py:490
  157.0 4.8 %collective-permute-done.16.refs_1_ = bf16[32,4608]{1,0:T(8,128)(2,1)S(1)} collective-permute-done((bf16[32,4608]{1,0:T(8,128)(2,1)}, bf16[32,4608]{1,0:T(8,128)(2,1)S(1)}, u32[]{:S(2)}, u32[]{:S(2)}) %collective-permute-start.16) | collective-permute-done | bytes 294944 | tf_op jit(solution)/shard_map/ppermute | solution.py:490
  161.8 1.4 collective-permute-done.17.refs_2_
  163.9 2.9 %finish.2.refs_1_ = bf16[128,1152]{1,0:T(8,128)(2,1)} custom-call(s32[1]{0:T(128)} %bitcast.22.block_ref, f32[32,4608]{1,0:T(8,128)} %get-tuple-element.86.own_ref, bf16[128,4608]{1,0:T(8,128)(2,1)} %copy-done.2, bf16[32,4608]{1,0:T(8,128)(2,1)} %copy-done.12, bf16[32,4608]{1,0:T(8,128)(2,1)} %copy-done.14, bf16[32,4608]{1,0:T(8,128)(2,1)} %copy-done.16, ...), custom_call_target="tpu_custom_call" | custom-call | flops 37748736 | bytes 1179648 | tf_op jit(solution)/shard_map/finish/pallas_call | solution.py:380
  166.8 1.3 collective-permute-start.18
  168.0 1.0 copy.32
  169.1 3.2 %place.1 = bf16[512,1024]{1,0:T(8,128)(2,1)} custom-call(s32[1]{0:T(128)} %bitcast.img_ref, s32[1,512]{1,0:T(1,128)} %reshape.107.pos_ref, bf16[2,512,512]{2,1,0:T(8,128)(2,1)} %bitcast.30, bf16[512,1024]{1,0:T(8,128)(2,1)} %stream_ref.3), custom_call_target="tpu_custom_call" | custom-call | flops 536870912 | bytes 3145728 | tf_op jit(solution)/shard_map/place/pallas_call | solution.py:416
  172.3 2.1 %collective-permute-done.12.refs_1_ = bf16[32,4608]{1,0:T(8,128)(2,1)S(1)} collective-permute-done((bf16[32,4608]{1,0:T(8,128)(2,1)}, bf16[32,4608]{1,0:T(8,128)(2,1)S(1)}, u32[]{:S(2)}, u32[]{:S(2)}) %collective-permute-start.12) | collective-permute-done | bytes 294944 | tf_op jit(solution)/shard_map/ppermute | solution.py:490
  174.5 1.1 collective-permute-done.13.refs_2_
  176.3 2.9 %finish.3.refs_2_ = bf16[128,1152]{1,0:T(8,128)(2,1)} custom-call(s32[1]{0:T(128)} %bitcast.23.block_ref, f32[32,4608]{1,0:T(8,128)} %get-tuple-element.94.own_ref, bf16[128,4608]{1,0:T(8,128)(2,1)} %copy-done.1, bf16[32,4608]{1,0:T(8,128)(2,1)} %copy-done.9, bf16[32,4608]{1,0:T(8,128)(2,1)} %copy-done.10, bf16[32,4608]{1,0:T(8,128)(2,1)} %copy-done.11, ...), custom_call_target="tpu_custom_call" | custom-call | flops 37748736 | bytes 1179648 | tf_op jit(solution)/shard_map/finish/pallas_call | solution.py:380
  179.2 1.5 collective-permute-start.19
  180.7 5.9 %collective-permute-start.20 = (bf16[128,1152]{1,0:T(8,128)(2,1)S(1)}, bf16[128,1152]{1,0:T(8,128)(2,1)S(1)}, u32[]{:S(2)}, u32[]{:S(2)}) collective-permute-start(bf16[128,1152]{1,0:T(8,128)(2,1)S(1)} %copy-done.4), channel_id=1, source_target_pairs={{0,1},{1,0},{2,3},{3,2},{4,5},{5,4},{6,7},{7,6},{8,9},{9,8},{10,11... | collective-permute-start | bytes 884744 | tf_op jit(solution)/shard_map/ppermute | solution.py:564
  187.1 7.8 %collective-permute-start.23 = (bf16[128,1152]{1,0:T(8,128)(2,1)S(1)}, bf16[128,1152]{1,0:T(8,128)(2,1)S(1)}, u32[]{:S(2)}, u32[]{:S(2)}) collective-permute-start(bf16[128,1152]{1,0:T(8,128)(2,1)S(1)} %collective-permute-done.19.refs_4_), channel_id=1, source_target_pairs={{0,1},{1,0},{2,3},{3,2},{4,5},{5,4},{6,7},{7,6},{8,9},{9,8},{10,11... | collective-permute-start | bytes 884744 | tf_op jit(solution)/shard_map/ppermute | solution.py:565
  197.2 3.1 %lay.1 = bf16[1024,1152]{1,0:T(8,128)(2,1)} custom-call(s32[2]{0:T(128)} %pad_add_fusion.3.refs_0_, bf16[128,1152]{1,0:T(8,128)(2,1)} %finish.2.refs_1_, bf16[128,1152]{1,0:T(8,128)(2,1)} %finish.3.refs_2_, bf16[128,1152]{1,0:T(8,128)(2,1)} %copy-done.8, bf16[128,1152]{1,0:T(8,128)(2,1)} %copy-done.13, bf16[128,1152]{1,0:T(8,128)(2,1)} %copy-done.15, ...), custom_call_target="tpu_custom_call" | custom-call | bytes 4718592 | tf_op jit(solution)/shard_map/lay/pallas_call | solution.py:445
  (95 shorter events, 12.1 us)
Async XLA Ops:
  7.2 1.1 copy-start
  7.2 84.7 %all-gather.3.cloned.1.call-start = ((), (), s32[]{:S(2)}) async-start(), calls=%async_computation.3 | async-start | bytes 5013504 | tf_op jit(solution)/shard_map/all_gather | solution.py:493
  40.5 42.5 %copy-start.21 = (bf16[1,1024]{1,0:T(2,128)(2,1)S(1)}, bf16[1,1024]{1,0:T(2,128)(2,1)}, u32[]{:S(2)}) copy-start(bf16[1,1024]{1,0:T(2,128)(2,1)} %param.13) | copy-start | bytes 6148
  40.5 46.1 %all-to-all-start.1 = ((bf16[32,32,1024]{2,1,0:T(8,128)(2,1)}), bf16[32,32,1024]{2,1,0:T(8,128)(2,1)S(1)}, u32[]{:S(2)}, u32[]{:S(2)}) async-start(bf16[32,32,1024]{2,1,0:T(8,128)(2,1)} %bitcast.27), calls=%async_computation.1 | async-start | bytes 4194304 | tf_op jit(solution)/shard_map/all_to_all | solution.py:517
  44.7 33.4 %collective-permute-start.1 = (bf16[64,4608]{1,0:T(8,128)(2,1)}, bf16[64,4608]{1,0:T(8,128)(2,1)S(1)}, u32[]{:S(2)}, u32[]{:S(2)}) collective-permute-start(bf16[64,4608]{1,0:T(8,128)(2,1)} %get-tuple-element.56), channel_id=1, source_target_pairs={{0,64},{1,65},{2,66},{3,67},{64,2},{65,3},{66,0},{67,1},{4,68},{5,... | collective-permute-start | bytes 1769480 | tf_op jit(solution)/shard_map/ppermute | solution.py:490
  46.0 34.8 %collective-permute-start.2 = (bf16[64,4608]{1,0:T(8,128)(2,1)}, bf16[64,4608]{1,0:T(8,128)(2,1)}, u32[]{:S(2)}, u32[]{:S(2)}) collective-permute-start(bf16[64,4608]{1,0:T(8,128)(2,1)} %get-tuple-element.57), channel_id=1, source_target_pairs={{0,66},{1,67},{2,64},{3,65},{64,0},{65,1},{66,2},{67,3},{4,70},{5,... | collective-permute-start | bytes 1769480 | tf_op jit(solution)/shard_map/ppermute | solution.py:490
  78.0 13.8 %copy-start.5 = (bf16[64,4608]{1,0:T(8,128)(2,1)}, bf16[64,4608]{1,0:T(8,128)(2,1)S(1)}, u32[]{:S(2)}) copy-start(bf16[64,4608]{1,0:T(8,128)(2,1)S(1)} %collective-permute-done.1.refs_1_) | copy-start | bytes 1769476
  78.0 13.8 %collective-permute-start.3 = (bf16[64,4608]{1,0:T(8,128)(2,1)S(1)}, bf16[64,4608]{1,0:T(8,128)(2,1)}, u32[]{:S(2)}, u32[]{:S(2)}) collective-permute-start(bf16[64,4608]{1,0:T(8,128)(2,1)S(1)} %collective-permute-done.1.refs_1_), channel_id=1, source_target_pairs={{0,1},{1,0},{2,3},{3,2},{4,5},{5,4},{6,7},{7,6},{8,9},{9,8},{10,11... | collective-permute-start | bytes 1769480 | tf_op jit(solution)/shard_map/ppermute | solution.py:515
  80.8 11.0 %collective-permute-start.4 = (bf16[64,4608]{1,0:T(8,128)(2,1)}, bf16[64,4608]{1,0:T(8,128)(2,1)}, u32[]{:S(2)}, u32[]{:S(2)}) collective-permute-start(bf16[64,4608]{1,0:T(8,128)(2,1)} %collective-permute-done.2.refs_2_), channel_id=1, source_target_pairs={{0,1},{1,0},{2,3},{3,2},{4,5},{5,4},{6,7},{7,6},{8,9},{9,8},{10,11... | collective-permute-start | bytes 1769480 | tf_op jit(solution)/shard_map/ppermute | solution.py:515
  82.9 2.8 %collective-permute-start = (s32[256]{0:T(256)S(1)}, s32[256]{0:T(256)S(1)}, u32[]{:S(2)}, u32[]{:S(2)}) collective-permute-start(s32[256]{0:T(256)S(1)} %get-tuple-element.108), channel_id=1, source_target_pairs={{0,64},{64,0},{1,65},{65,1},{2,66},{66,2},{3,67},{67,3},{4,68},{68... | collective-permute-start | bytes 3080 | tf_op jit(solution)/shard_map/ppermute | solution.py:522
  86.6 1.4 copy-start.3
  100.1 1.7 collective-permute-start.5
  102.5 8.6 %copy-start.20 = (f32[8,512]{1,0:T(8,128)}, f32[8,512]{1,0:T(8,128)S(1)}, u32[]{:S(2)}) copy-start(f32[8,512]{1,0:T(8,128)S(1)} %add.61.refs_5_) | copy-start | bytes 49156
  102.5 7.8 %collective-permute-start.7 = (f32[8,512]{1,0:T(8,128)S(1)}, f32[8,512]{1,0:T(8,128)S(1)}, u32[]{:S(2)}, u32[]{:S(2)}) collective-permute-start(f32[8,512]{1,0:T(8,128)S(1)} %add.61.refs_5_), channel_id=1, source_target_pairs={{0,2},{1,3},{2,0},{3,1},{64,66},{65,67},{66,64},{67,65},{4,6},{5,7... | collective-permute-start | bytes 49160 | tf_op jit(solution)/shard_map/ppermute | solution.py:490
  105.0 5.3 %collective-permute-start.6 = (f32[8,512]{1,0:T(8,128)S(1)}, f32[8,512]{1,0:T(8,128)S(1)}, u32[]{:S(2)}, u32[]{:S(2)}) collective-permute-start(f32[8,512]{1,0:T(8,128)S(1)} %pad_maximum_fusion.2), channel_id=1, source_target_pairs={{0,64},{1,65},{2,66},{3,67},{64,2},{65,3},{66,0},{67,1},{4,68},{5,... | collective-permute-start | bytes 49160 | tf_op jit(solution)/shard_map/ppermute | solution.py:490
  105.0 5.3 %collective-permute-start.8 = (f32[8,512]{1,0:T(8,128)S(1)}, f32[8,512]{1,0:T(8,128)S(1)}, u32[]{:S(2)}, u32[]{:S(2)}) collective-permute-start(f32[8,512]{1,0:T(8,128)S(1)} %pad_maximum_fusion.2), channel_id=1, source_target_pairs={{0,66},{1,67},{2,64},{3,65},{64,0},{65,1},{66,2},{67,3},{4,70},{5,... | collective-permute-start | bytes 49160 | tf_op jit(solution)/shard_map/ppermute | solution.py:490
  110.3 0.7 copy-start.23
  110.3 0.7 copy-start.22
  110.3 12.5 %collective-permute-start.9 = (bf16[512,512]{1,0:T(8,128)(2,1)}, bf16[512,512]{1,0:T(8,128)(2,1)S(1)}, u32[]{:S(2)}, u32[]{:S(2)}) collective-permute-start(bf16[512,512]{1,0:T(8,128)(2,1)} %get-tuple-element.73), channel_id=1, source_target_pairs={{0,64},{64,0},{1,65},{65,1},{2,66},{66,2},{3,67},{67,3},{4,68},{68... | collective-permute-start | bytes 1572872 | tf_op jit(solution)/shard_map/ppermute | solution.py:537
  120.0 13.2 %copy-start.6 = (bf16[512,512]{1,0:T(8,128)(2,1)S(1)}, bf16[512,512]{1,0:T(8,128)(2,1)}, u32[]{:S(2)}) copy-start(bf16[512,512]{1,0:T(8,128)(2,1)} %get-tuple-element.80) | copy-start | bytes 1572868
  122.8 0.8 copy-start.7
  123.7 4.8 %collective-permute-start.10 = (bf16[128,4608]{1,0:T(8,128)(2,1)}, bf16[128,4608]{1,0:T(8,128)(2,1)S(1)}, u32[]{:S(2)}, u32[]{:S(2)}) collective-permute-start(bf16[128,4608]{1,0:T(8,128)(2,1)} %get-tuple-element.76), channel_id=1, source_target_pairs={{0,1},{1,0},{2,3},{3,2},{4,5},{5,4},{6,7},{7,6},{8,9},{9,8},{10,11... | collective-permute-start | bytes 3538952 | tf_op jit(solution)/shard_map/ppermute | solution.py:544
  125.8 16.0 %collective-permute-start.14 = (bf16[128,4608]{1,0:T(8,128)(2,1)}, bf16[128,4608]{1,0:T(8,128)(2,1)S(1)}, u32[]{:S(2)}, u32[]{:S(2)}) collective-permute-start(bf16[128,4608]{1,0:T(8,128)(2,1)} %get-tuple-element.87), channel_id=1, source_target_pairs={{0,1},{1,0},{2,3},{3,2},{4,5},{5,4},{6,7},{7,6},{8,9},{9,8},{10,11... | collective-permute-start | bytes 3538952 | tf_op jit(solution)/shard_map/ppermute | solution.py:544
  128.4 1.1 copy-start.1
  135.3 32.8 %all-to-all-start.2 = ((bf16[16,2,32,512]{3,2,1,0:T(8,128)(2,1)}), bf16[16,2,32,512]{3,2,1,0:T(8,128)(2,1)S(1)}, u32[]{:S(2)}, u32[]{:S(2)}) async-start(bf16[16,2,32,512]{3,2,1,0:T(8,128)(2,1)} %pad_maximum_fusion), calls=%async_computation.2 | async-start | bytes 2097152 | tf_op jit(solution)/shard_map/all_to_all | solution.py:551
  141.8 1.0 copy-start.2
  146.5 9.7 %collective-permute-start.15 = (bf16[32,4608]{1,0:T(8,128)(2,1)}, bf16[32,4608]{1,0:T(8,128)(2,1)S(1)}, u32[]{:S(2)}, u32[]{:S(2)}) collective-permute-start(bf16[32,4608]{1,0:T(8,128)(2,1)} %get-tuple-element.89), channel_id=1, source_target_pairs={{0,64},{1,65},{2,66},{3,67},{64,2},{65,3},{66,0},{67,1},{4,68},{5,... | collective-permute-start | bytes 884744 | tf_op jit(solution)/shard_map/ppermute | solution.py:490
  146.5 15.3 %collective-permute-start.16 = (bf16[32,4608]{1,0:T(8,128)(2,1)}, bf16[32,4608]{1,0:T(8,128)(2,1)S(1)}, u32[]{:S(2)}, u32[]{:S(2)}) collective-permute-start(bf16[32,4608]{1,0:T(8,128)(2,1)} %get-tuple-element.90), channel_id=1, source_target_pairs={{0,2},{1,3},{2,0},{3,1},{64,66},{65,67},{66,64},{67,65},{4,6},{5,7... | collective-permute-start | bytes 884744 | tf_op jit(solution)/shard_map/ppermute | solution.py:490
  148.8 14.4 %collective-permute-start.17 = (bf16[32,4608]{1,0:T(8,128)(2,1)}, bf16[32,4608]{1,0:T(8,128)(2,1)S(1)}, u32[]{:S(2)}, u32[]{:S(2)}) collective-permute-start(bf16[32,4608]{1,0:T(8,128)(2,1)} %get-tuple-element.91), channel_id=1, source_target_pairs={{0,66},{1,67},{2,64},{3,65},{64,0},{65,1},{66,2},{67,3},{4,70},{5,... | collective-permute-start | bytes 884744 | tf_op jit(solution)/shard_map/ppermute | solution.py:490
  149.4 22.9 %collective-permute-start.11 = (bf16[32,4608]{1,0:T(8,128)(2,1)}, bf16[32,4608]{1,0:T(8,128)(2,1)S(1)}, u32[]{:S(2)}, u32[]{:S(2)}) collective-permute-start(bf16[32,4608]{1,0:T(8,128)(2,1)} %get-tuple-element.82), channel_id=1, source_target_pairs={{0,64},{1,65},{2,66},{3,67},{64,2},{65,3},{66,0},{67,1},{4,68},{5,... | collective-permute-start | bytes 884744 | tf_op jit(solution)/shard_map/ppermute | solution.py:490
  150.2 24.2 %collective-permute-start.12 = (bf16[32,4608]{1,0:T(8,128)(2,1)}, bf16[32,4608]{1,0:T(8,128)(2,1)S(1)}, u32[]{:S(2)}, u32[]{:S(2)}) collective-permute-start(bf16[32,4608]{1,0:T(8,128)(2,1)} %get-tuple-element.83), channel_id=1, source_target_pairs={{0,2},{1,3},{2,0},{3,1},{64,66},{65,67},{66,64},{67,65},{4,6},{5,7... | collective-permute-start | bytes 884744 | tf_op jit(solution)/shard_map/ppermute | solution.py:490
  156.2 7.0 %copy-start.12 = (bf16[32,4608]{1,0:T(8,128)(2,1)}, bf16[32,4608]{1,0:T(8,128)(2,1)S(1)}, u32[]{:S(2)}) copy-start(bf16[32,4608]{1,0:T(8,128)(2,1)S(1)} %collective-permute-done.15.refs_0_) | copy-start | bytes 884740
  156.2 19.3 %collective-permute-start.13 = (bf16[32,4608]{1,0:T(8,128)(2,1)}, bf16[32,4608]{1,0:T(8,128)(2,1)S(1)}, u32[]{:S(2)}, u32[]{:S(2)}) collective-permute-start(bf16[32,4608]{1,0:T(8,128)(2,1)} %get-tuple-element.84), channel_id=1, source_target_pairs={{0,66},{1,67},{2,64},{3,65},{64,0},{65,1},{66,2},{67,3},{4,70},{5,... | collective-permute-start | bytes 884744 | tf_op jit(solution)/shard_map/ppermute | solution.py:490
  161.8 1.4 copy-start.14
  166.8 19.8 %collective-permute-start.18 = (bf16[128,1152]{1,0:T(8,128)(2,1)}, bf16[128,1152]{1,0:T(8,128)(2,1)S(1)}, u32[]{:S(2)}, u32[]{:S(2)}) collective-permute-start(bf16[128,1152]{1,0:T(8,128)(2,1)} %finish.2.refs_1_), channel_id=1, source_target_pairs={{0,2},{1,3},{2,0},{3,1},{4,6},{5,7},{6,4},{7,5},{8,10},{9,11},{10,... | collective-permute-start | bytes 884744 | tf_op jit(solution)/shard_map/ppermute | solution.py:561
  172.3 3.3 %copy-start.9 = (bf16[32,4608]{1,0:T(8,128)(2,1)}, bf16[32,4608]{1,0:T(8,128)(2,1)S(1)}, u32[]{:S(2)}) copy-start(bf16[32,4608]{1,0:T(8,128)(2,1)S(1)} %collective-permute-done.11.refs_0_) | copy-start | bytes 884740
  174.5 1.1 copy-start.10
  175.6 0.7 copy-start.11
  176.3 4.4 %copy-start.4 = (bf16[128,1152]{1,0:T(8,128)(2,1)S(1)}, bf16[128,1152]{1,0:T(8,128)(2,1)}, u32[]{:S(2)}) copy-start(bf16[128,1152]{1,0:T(8,128)(2,1)} %finish.2.refs_1_) | copy-start | bytes 884740
  179.2 7.9 %collective-permute-start.19 = (bf16[128,1152]{1,0:T(8,128)(2,1)}, bf16[128,1152]{1,0:T(8,128)(2,1)S(1)}, u32[]{:S(2)}, u32[]{:S(2)}) collective-permute-start(bf16[128,1152]{1,0:T(8,128)(2,1)} %finish.3.refs_2_), channel_id=1, source_target_pairs={{0,2},{1,3},{2,0},{3,1},{4,6},{5,7},{6,4},{7,5},{8,10},{9,11},{10,... | collective-permute-start | bytes 884744 | tf_op jit(solution)/shard_map/ppermute | solution.py:561
  180.7 14.8 %collective-permute-start.20 = (bf16[128,1152]{1,0:T(8,128)(2,1)S(1)}, bf16[128,1152]{1,0:T(8,128)(2,1)S(1)}, u32[]{:S(2)}, u32[]{:S(2)}) collective-permute-start(bf16[128,1152]{1,0:T(8,128)(2,1)S(1)} %copy-done.4), channel_id=1, source_target_pairs={{0,1},{1,0},{2,3},{3,2},{4,5},{5,4},{6,7},{7,6},{8,9},{9,8},{10,11... | collective-permute-start | bytes 884744 | tf_op jit(solution)/shard_map/ppermute | solution.py:564
  186.6 9.6 %copy-start.8 = (bf16[128,1152]{1,0:T(8,128)(2,1)}, bf16[128,1152]{1,0:T(8,128)(2,1)S(1)}, u32[]{:S(2)}) copy-start(bf16[128,1152]{1,0:T(8,128)(2,1)S(1)} %collective-permute-done.18.refs_3_) | copy-start | bytes 884740
  186.6 8.9 %collective-permute-start.22 = (bf16[128,1152]{1,0:T(8,128)(2,1)S(1)}, bf16[128,1152]{1,0:T(8,128)(2,1)S(1)}, u32[]{:S(2)}, u32[]{:S(2)}) collective-permute-start(bf16[128,1152]{1,0:T(8,128)(2,1)S(1)} %collective-permute-done.18.refs_3_), channel_id=1, source_target_pairs={{0,1},{1,0},{2,3},{3,2},{4,5},{5,4},{6,7},{7,6},{8,9},{9,8},{10,11... | collective-permute-start | bytes 884744 | tf_op jit(solution)/shard_map/ppermute | solution.py:565
  186.7 8.9 %collective-permute-start.21 = (bf16[128,1152]{1,0:T(8,128)(2,1)}, bf16[128,1152]{1,0:T(8,128)(2,1)S(1)}, u32[]{:S(2)}, u32[]{:S(2)}) collective-permute-start(bf16[128,1152]{1,0:T(8,128)(2,1)} %finish.3.refs_2_), channel_id=1, source_target_pairs={{0,1},{1,0},{2,3},{3,2},{4,5},{5,4},{6,7},{7,6},{8,9},{9,8},{10,11... | collective-permute-start | bytes 884744 | tf_op jit(solution)/shard_map/ppermute | solution.py:564
  187.1 9.0 %copy-start.13 = (bf16[128,1152]{1,0:T(8,128)(2,1)}, bf16[128,1152]{1,0:T(8,128)(2,1)S(1)}, u32[]{:S(2)}) copy-start(bf16[128,1152]{1,0:T(8,128)(2,1)S(1)} %collective-permute-done.19.refs_4_) | copy-start | bytes 884740
  187.1 9.0 %collective-permute-start.23 = (bf16[128,1152]{1,0:T(8,128)(2,1)S(1)}, bf16[128,1152]{1,0:T(8,128)(2,1)S(1)}, u32[]{:S(2)}, u32[]{:S(2)}) collective-permute-start(bf16[128,1152]{1,0:T(8,128)(2,1)S(1)} %collective-permute-done.19.refs_4_), channel_id=1, source_target_pairs={{0,1},{1,0},{2,3},{3,2},{4,5},{5,4},{6,7},{7,6},{8,9},{9,8},{10,11... | collective-permute-start | bytes 884744 | tf_op jit(solution)/shard_map/ppermute | solution.py:565
  195.5 0.8 copy-start.17
  195.5 0.9 copy-start.18
  (4 other events, 2.9 us)
Sparse Core Ops, SparseCore 0:
  10.2 79.9 all-gather.2

commit v7 on v5

v7 whole, which is shorter than its diff:
```python
import jax
import jax.numpy as jnp
from jax import lax
from jax.experimental import pallas as pl
from jax.experimental.pallas import tpu as pltpu
from jax.sharding import PartitionSpec as P


BF = jnp.bfloat16
F32 = jnp.float32
BLOCK = 768
RING = 4
AWAY = (0, 3, 1, 2)


def params(mib):
    return pltpu.CompilerParams(vmem_limit_bytes=mib * 1024 * 1024)


def whole():
    return pl.BlockSpec(memory_space=pltpu.VMEM)


def shape(dims, kind):
    return jax.ShapeDtypeStruct(dims, kind)


def scalars():
    return pl.BlockSpec(memory_space=pltpu.SMEM)


def anywhere():
    return pl.BlockSpec(memory_space=pl.ANY)


def cost(flops, moved):
    return pl.CostEstimate(flops=flops, bytes_accessed=moved, transcendentals=0)


def eq_hot(shape, dim, index):
    return (lax.broadcasted_iota(jnp.int32, shape, dim) == index).astype(BF)


def window_major(tokens, window):
    n = tokens * window
    row = lax.broadcasted_iota(jnp.int32, (n, n), 0)
    col = lax.broadcasted_iota(jnp.int32, (n, n), 1)
    return (col == (row % tokens) * window + row // tokens).astype(BF)


def patch_major(tokens, window):
    n = tokens * window
    row = lax.broadcasted_iota(jnp.int32, (n, n), 0)
    col = lax.broadcasted_iota(jnp.int32, (n, n), 1)
    return (col == (row % window) * tokens + row // window).astype(BF)


def norm_kernel(here_ref, x_ref, gain_ref, bias_ref, after_ref, lifted_ref, xw_ref, stat_ref):
    window, width = gain_ref.shape
    tokens = x_ref.shape[0] // window
    full = window * width
    x = jnp.dot(window_major(tokens, window), x_ref[...], preferred_element_type=F32)
    parts = [x[w * tokens : (w + 1) * tokens] for w in range(window)]
    total = sum(jnp.sum(p, axis=1, keepdims=True) for p in parts)
    squares = sum(jnp.sum(p * p, axis=1, keepdims=True) for p in parts)
    mean = total / full
    inv = lax.rsqrt(squares / full - mean * mean + 1e-05)
    lifted = []
    for w, p in enumerate(parts):
        normed = (p - mean) * inv
        lifted.append(
            normed * gain_ref[w : w + 1].astype(F32) + bias_ref[w : w + 1].astype(F32)
        )
        xw_ref[w] = p.astype(BF)
    share = width // (RING * RING)
    lifted_ref[...] = jnp.concatenate(
        [p[:, at : at + share] for at in range(0, width, share) for p in lifted], axis=1
    ).astype(BF)
    lane = lax.broadcasted_iota(jnp.int32, stat_ref.shape, 1)
    stat_ref[...] = jnp.where(lane == 0, mean, inv)


def layer_norm(here, features, gain, bias, after):
    rows, width = features.shape
    window = gain.shape[0]
    merged = rows // window
    block = 64
    steps = merged // block
    return pl.pallas_call(
        norm_kernel,
        grid_spec=pltpu.PrefetchScalarGridSpec(
            num_scalar_prefetch=1,
            grid=(steps,),
            in_specs=[
                pl.BlockSpec(
                    (block * window, width),
                    lambda i, c: (lax.rem(i + c[0] * (steps // 2), steps), 0),
                ),
                pl.BlockSpec((window, width), lambda i, c: (0, 0)),
                pl.BlockSpec((window, width), lambda i, c: (0, 0)),
                anywhere(),
            ],
            out_specs=[
                pl.BlockSpec((block, window * width), lambda i, c: (i, 0)),
                pl.BlockSpec((window, block, width), lambda i, c: (0, i, 0)),
                pl.BlockSpec((block, 128), lambda i, c: (i, 0)),
            ],
        ),
        out_shape=[
            shape((merged, window * width), BF),
            shape((window, merged, width), BF),
            shape((merged, 128), F32),
        ],
        compiler_params=params(58),
        cost_estimate=cost(2 * rows * block * window * width, 6 * rows * width),
        name="layer_norm",
    )(here, features, gain, bias, after)


def collect_kernel(pos_ref, stream_ref, cot_ref, after_ref, out_ref):
    slots = pos_ref.shape[0]
    rows, width = stream_ref.shape
    cut = width // 2
    pick = eq_hot((slots, rows), 1, pos_ref[...])
    for img in range(2):
        at = slice(img * cut, (img + 1) * cut)
        for place, ref in enumerate((stream_ref, cot_ref)):
            out_ref[img, :, place * cut : (place + 1) * cut] = jnp.dot(
                pick, ref[:, at], preferred_element_type=F32
            ).astype(BF)


def collect(pos, stream, cot, after):
    slots = pos.shape[0]
    rows, width = stream.shape
    out = shape((2, slots, width), BF)
    return pl.pallas_call(
        collect_kernel,
        in_specs=[whole()] * 3 + [anywhere()],
        out_specs=whole(),
        out_shape=out,
        compiler_params=params(20),
        cost_estimate=cost(4 * slots * rows * width, 8 * rows * width),
        name="collect",
    )(pos, stream, cot, after)


def unpack_kernel(slot_ref, came_ref, base_ref, cot_ref):
    tokens, width = base_ref.shape
    slots = came_ref.shape[0]
    take = eq_hot((tokens, slots), 1, slot_ref[...])
    for start, out_ref in ((0, base_ref), (width, cot_ref)):
        out_ref[...] = jnp.dot(
            take, came_ref[:, start : start + width], preferred_element_type=F32
        ).astype(BF)


def unpack(slot_col, came):
    tokens = slot_col.shape[0]
    slots, both = came.shape
    width = both // 2
    outs = [shape((tokens, width), BF)] * 2
    return pl.pallas_call(
        unpack_kernel,
        in_specs=[whole()] * 2,
        out_specs=[whole()] * 2,
        out_shape=outs,
        compiler_params=params(12),
        cost_estimate=cost(4 * slots * tokens * width, 8 * tokens * width),
        name="unpack",
    )(slot_col, came)


def stack_kernel(here_ref, *refs):
    first = jnp.where(here_ref[0] == 0, here_ref[4], here_ref[3])
    for away, ref in zip(AWAY, refs[:RING]):
        refs[RING][lax.rem(first + away, RING)] = ref[...]


def stack(here, blocks):
    rows, width = blocks[0].shape
    return pl.pallas_call(
        stack_kernel,
        in_specs=[scalars()] + [whole()] * RING,
        out_specs=whole(),
        out_shape=shape((RING, rows, width), BF),
        compiler_params=params(6),
        cost_estimate=cost(0, 16 * rows * width),
        name="stack",
    )(here, *blocks)


def fetch(here_ref, stacks, held_ref, sems):
    for index, (away, ref) in enumerate(zip(AWAY, stacks)):

        @pl.when(here_ref[0] == 0)
        def _():
            place = lax.rem(here_ref[3] + away, RING)
            pltpu.make_async_copy(ref, held_ref.at[place], sems.at[index]).start()

        @pl.when(here_ref[0] == 1)
        def _():
            place = lax.rem(here_ref[4] + away, RING)
            pltpu.make_async_copy(ref, held_ref.at[:, place], sems.at[index]).start()

    def wait():
        for index, ref in enumerate(stacks):
            pltpu.make_async_copy(ref, held_ref.at[0], sems.at[index]).wait()

    return wait


def merge_kernel(here_ref, ngain_ref, base_hbm, cot_hbm, *refs):
    stacks, refs = refs[:RING], refs[RING:]
    lifted, refs = refs[:-10], refs[-10:]
    visual_ref, state_ref, stat_ref, held_ref, left_ref, base_ref, cot_ref, w_sems, sems, row_sems = refs
    wait_weight = fetch(here_ref, stacks, held_ref, w_sems)
    depth = left_ref.shape[1]
    steps = range(depth // BLOCK)
    copies = []
    for step in steps:
        at = pl.ds(step * BLOCK, BLOCK)
        start = 0
        group = []
        for index, ref in enumerate(lifted):
            rows = ref.shape[0]
            group.append(
                pltpu.make_async_copy(
                    ref.at[:, at], left_ref.at[pl.ds(start, rows), at], sems.at[step, index]
                )
            )
            group[-1].start()
            start += rows
        copies.append(group)
    row_copies = [
        pltpu.make_async_copy(a, b, row_sems.at[i])
        for i, (a, b) in enumerate(((base_hbm, base_ref), (cot_hbm, cot_ref)))
    ]
    for copy in row_copies:
        copy.start()
    wait_weight()
    weight = held_ref[...].reshape(depth, -1)
    total = None
    for step in steps:
        at = slice(step * BLOCK, (step + 1) * BLOCK)
        for copy in copies[step]:
            copy.wait()
        part = jnp.dot(left_ref[:, at], weight[at], preferred_element_type=F32)
        total = part if total is None else total + part
    for copy in row_copies:
        copy.wait()
    visual = total.astype(BF)
    visual_ref[...] = visual
    state = base_ref[...].astype(F32) + visual.astype(F32)
    state_ref[...] = state
    up = ngain_ref[...].astype(F32) * cot_ref[...].astype(F32)
    lane = lax.broadcasted_iota(jnp.int32, (state.shape[0], 128), 1)
    sums = jnp.where(
        lane == 0,
        jnp.sum(state * state, axis=1, keepdims=True),
        jnp.sum(up * state, axis=1, keepdims=True),
    )
    stat_ref[...] = sums.T[: stat_ref.shape[0]]


def merge(here, base, cot, ngain, stacks, lifted):
    tokens, width = base.shape
    depth = lifted[0].shape[1]
    outs = [shape((tokens, width), BF), shape((tokens, width), F32), shape((8, tokens), F32)]
    return pl.pallas_call(
        merge_kernel,
        in_specs=[scalars(), whole()] + [anywhere()] * (2 + RING + len(lifted)),
        out_specs=[whole()] * 3,
        out_shape=outs,
        scratch_shapes=[
            pltpu.VMEM((RING,) + stacks[0].shape, BF),
            pltpu.VMEM((tokens, depth), BF),
            pltpu.VMEM((tokens, width), BF),
            pltpu.VMEM((tokens, width), BF),
            pltpu.SemaphoreType.DMA((RING,)),
            pltpu.SemaphoreType.DMA((depth // BLOCK, len(lifted))),
            pltpu.SemaphoreType.DMA((2,)),
        ],
        compiler_params=params(56),
        cost_estimate=cost(2 * depth * tokens * width, 2 * depth * width),
        name="merge",
    )(here, ngain, base, cot, *stacks, *lifted)


def add_kernel(sums_ref, got_ref, near_ref, turned_ref):
    count = sums_ref.shape[1] // 4
    cuts = [
        sums_ref[:, i * count : (i + 1) * count] + got_ref[:, (i ^ 1) * count : ((i ^ 1) + 1) * count]
        for i in range(4)
    ]
    near_ref[...] = jnp.concatenate(cuts, axis=1)
    turned_ref[...] = jnp.concatenate(cuts[2:] + cuts[:2], axis=1)


def add(sums, got):
    return pl.pallas_call(
        add_kernel,
        in_specs=[whole()] * 2,
        out_specs=[whole()] * 2,
        out_shape=[shape(sums.shape, F32)] * 2,
        compiler_params=params(4),
        cost_estimate=cost(sums.size, 16 * sums.size),
        name="add",
    )(sums, got)


def pack_kernel(here_ref, slot_ref, visual_ref, after_ref, stay_ref, cross_ref):
    tokens = visual_ref.shape[0]
    slots = stay_ref.shape[0]
    for relative, out_ref in ((0, stay_ref), (1, cross_ref)):
        put = eq_hot((tokens, slots), 1, slot_ref[...] - (here_ref[2] ^ relative) * slots)
        out_ref[...] = lax.dot_general(
            put, visual_ref[...], (((0,), (0,)), ((), ())), preferred_element_type=F32
        ).astype(BF)


def pack(here, slot_col, visual, slots, after):
    tokens, width = visual.shape
    return pl.pallas_call(
        pack_kernel,
        in_specs=[scalars()] + [whole()] * 2 + [anywhere()],
        out_specs=[whole()] * 2,
        out_shape=[shape((slots // 2, width), BF)] * 2,
        compiler_params=params(8),
        cost_estimate=cost(2 * slots * tokens * width, 2 * (slots + tokens) * width),
        name="pack",
    )(here, slot_col, visual, after)


def braid_kernel(stay_ref, crossed_ref, after_ref, out_ref):
    count, _, rows, _ = out_ref.shape
    for c in range(count):
        at = slice(c * rows, (c + 1) * rows)
        out_ref[c, 0] = stay_ref[at, :]
        out_ref[c, 1] = crossed_ref[at, :]


def braid(stay, crossed, count, after):
    rows, width = stay.shape
    return pl.pallas_call(
        braid_kernel,
        in_specs=[whole()] * 2 + [anywhere()],
        out_specs=whole(),
        out_shape=shape((count, 2, rows // count, width), BF),
        compiler_params=params(6),
        cost_estimate=cost(0, 8 * rows * width),
        name="braid",
    )(stay, crossed, after)


def backward_kernel(full_width, chunks, here_ref, state_ref, cot_ref, ngain_ref, *refs):
    stats, stacks, refs = refs[:RING], refs[RING : 2 * RING], refs[2 * RING :]
    outs, (picked_ref, sums_ref, held_ref, sems) = refs[: 3 * chunks], refs[3 * chunks :]
    wait_weight = fetch(here_ref, stacks, held_ref, sems)
    tokens = state_ref.shape[0]
    rows = tokens // 2 // RING // chunks
    total = stats[0][...]
    for ref in stats[1:]:
        total = total + ref[...]
    sums_ref[...] = total.T
    far, img = here_ref[1], here_ref[2]
    gain = ngain_ref[...].astype(F32)
    for core in range(2):
        for away in range(RING):
            there = lax.rem(2 * far + img + away, RING)
            partner = lax.rem(there + img, 2)
            begin = partner * (tokens // 2) + core * (tokens // 4) + (there // 2) * (tokens // 8)
            at = pl.ds(pl.multiple_of(begin, tokens // 8), tokens // 8)
            sums = sums_ref[at, :]
            inv = lax.rsqrt(sums[:, 0:1] / full_width + 1e-06)
            inner = sums[:, 1:2] / full_width
            up = gain * cot_ref[at, :].astype(F32)
            grad = inv * up - state_ref[at, :] * (inv * inv * inv * inner)
            for chunk in range(chunks):
                to = ((core * chunks + chunk) * RING + away) * rows
                picked_ref[to : to + rows, :] = grad[chunk * rows : (chunk + 1) * rows].astype(BF)
    depth = outs[0].shape[1]
    wait_weight()
    weight = held_ref[...].reshape(depth, -1)
    for begin in range(0, depth, BLOCK):
        cols = slice(begin, begin + BLOCK)
        both = lax.dot_general(
            picked_ref[...], weight[cols], (((1,), (1,)), ((), ())), preferred_element_type=F32
        )
        for chunk in range(chunks):
            own, rest, other = outs[chunk], outs[chunks + chunk], outs[2 * chunks + chunk]
            start = chunk * RING * rows
            own[:, cols] = both[start : start + rows]
            rest[:, cols] = both[start + rows : start + RING * rows].astype(BF)
            start += tokens // 2
            other[:, cols] = both[start : start + RING * rows].astype(BF)


def backward(here, state, cot, ngain, stats, stacks, chunks, full_width):
    tokens, width = state.shape
    depth = RING * stacks[0].shape[0] * stacks[0].shape[1]
    rows = tokens // 2 // RING // chunks
    outs = (
        [shape((rows, depth), F32)] * chunks
        + [shape(((RING - 1) * rows, depth), BF)] * chunks
        + [shape((RING * rows, depth), BF)] * chunks
    )
    return pl.pallas_call(
        lambda *refs: backward_kernel(full_width, chunks, *refs),
        in_specs=[scalars()] + [whole()] * (3 + RING) + [anywhere()] * RING,
        out_specs=[whole()] * len(outs),
        out_shape=outs,
        scratch_shapes=[
            pltpu.VMEM((tokens, width), BF),
            pltpu.VMEM((tokens, 8), F32),
            pltpu.VMEM((RING,) + stacks[0].shape, BF),
            pltpu.SemaphoreType.DMA((RING,)),
        ],
        compiler_params=params(24),
        cost_estimate=cost(2 * depth * tokens * width, 2 * depth * width),
        name="backward",
    )(here, state, cot, ngain, *stats, *stacks)


def pair_kernel(rest_ref, got_ref, after_ref, *outs):
    rows = outs[0].shape[0]
    for away, out in enumerate(outs):
        at = slice(away * rows, (away + 1) * rows)
        got = slice((away + 1) * rows, (away + 2) * rows)
        out[...] = (rest_ref[at, :].astype(F32) + got_ref[got, :].astype(F32)).astype(BF)


def pair(rest, got, after):
    rows, depth = got.shape[0] // RING, got.shape[1]
    outs = [shape((rows, depth), BF)] * (RING - 1)
    return pl.pallas_call(
        pair_kernel,
        in_specs=[whole()] * 2 + [anywhere()],
        out_specs=[whole()] * (RING - 1),
        out_shape=outs,
        compiler_params=params(8),
        cost_estimate=cost(4 * rows * depth, 24 * rows * depth),
        name="pair",
    )(rest, got, after)


def finish_kernel(block_ref, own_ref, got_ref, *refs):
    came, (xw_ref, stat_ref, gain_ref, out_ref) = refs[: RING - 1], refs[RING - 1 :]
    window, tokens, width = xw_ref.shape
    full = window * width
    mean = stat_ref[:, 0:1]
    inv = stat_ref[:, 1:2]
    lifted = own_ref[...] + got_ref[...].astype(F32)
    for ref in came:
        lifted = lifted + ref[...].astype(F32)
    share = width // (RING * RING)
    scaled = []
    total = 0.0
    inner = 0.0
    for w in range(window):
        g = jnp.concatenate(
            [lifted[:, at : at + share] for at in range(w * share, full, window * share)], axis=1
        ) * gain_ref[w : w + 1].astype(F32)
        normed = (xw_ref[w].astype(F32) - mean) * inv
        total = total + jnp.sum(g, axis=1, keepdims=True)
        inner = inner + jnp.sum(g * normed, axis=1, keepdims=True)
        scaled.append((g, normed))
    total = total / full
    inner = inner / full
    rows = jnp.concatenate(
        [(inv * (g - total - normed * inner)).astype(BF) for g, normed in scaled], axis=0
    )
    out_ref[...] = jnp.dot(
        patch_major(tokens, window), rows, preferred_element_type=F32
    ).astype(BF)


def finish(block, own, got, came, xw, stat, gain):
    tokens, depth = own.shape
    window, width = gain.shape
    same = pl.BlockSpec((tokens, depth), lambda i, b: (0, 0))
    return pl.pallas_call(
        finish_kernel,
        grid_spec=pltpu.PrefetchScalarGridSpec(
            num_scalar_prefetch=1,
            grid=(1,),
            in_specs=[same] * (1 + RING)
            + [
                pl.BlockSpec((window, tokens, width), lambda i, b: (0, b[0], 0)),
                pl.BlockSpec((tokens, 128), lambda i, b: (b[0], 0)),
                pl.BlockSpec((window, width), lambda i, b: (0, 0)),
            ],
            out_specs=pl.BlockSpec((tokens * window, width), lambda i, b: (0, 0)),
        ),
        out_shape=shape((tokens * window, width), BF),
        compiler_params=params(12),
        cost_estimate=cost(2 * (tokens * window) ** 2 * width, 8 * window * tokens * width),
        name="finish",
    )(block, own, got, *came, xw, stat, gain)


def place_kernel(here_ref, pos_ref, came_ref, stream_ref, out_ref):
    rows, width = stream_ref.shape
    cut = width // 2
    slots = pos_ref.shape[0]
    put = eq_hot((slots, rows), 1, pos_ref[...])
    for relative in range(2):
        start = pl.multiple_of((here_ref[2] ^ relative) * cut, cut)
        at = pl.ds(start, cut)
        out_ref[:, at] = (
            stream_ref[:, at].astype(F32)
            + lax.dot_general(
                put,
                came_ref[:, relative].reshape(slots, cut),
                (((0,), (0,)), ((), ())),
                preferred_element_type=F32,
            )
        ).astype(BF)


def place(here, pos, came, stream):
    rows, width = stream.shape
    return pl.pallas_call(
        place_kernel,
        in_specs=[scalars()] + [whole()] * 3,
        out_specs=whole(),
        out_shape=shape((rows, width), BF),
        compiler_params=params(12),
        cost_estimate=cost(2 * pos.shape[0] * rows * width, 6 * rows * width),
        name="place",
    )(here, pos, came, stream)


def lay_kernel(chunks, at_ref, *refs):
    blocks, (out_ref, sems) = refs[:-2], refs[-2:]
    rows = blocks[0].shape[0]
    copies = []
    for index, ref in enumerate(blocks):
        quarter, chunk = index // chunks, index % chunks
        owner = 2 * (at_ref[0] ^ (quarter // 2)) + (at_ref[1] ^ (quarter % 2))
        start = pl.multiple_of((owner * chunks + chunk) * rows, rows)
        copies.append(pltpu.make_async_copy(ref, out_ref.at[pl.ds(start, rows)], sems.at[index]))
    for copy in copies:
        copy.start()
    for copy in copies:
        copy.wait()


def lay(at, blocks, chunks):
    rows, width = blocks[0].shape
    return pl.pallas_call(
        lambda *refs: lay_kernel(chunks, *refs),
        in_specs=[scalars()] + [whole()] * len(blocks),
        out_specs=anywhere(),
        out_shape=shape((len(blocks) * rows, width), BF),
        scratch_shapes=[pltpu.SemaphoreType.DMA((len(blocks),))],
        compiler_params=params(4),
        cost_estimate=cost(0, 4 * len(blocks) * rows * width),
        name="lay",
    )(at, *blocks)


def shards(features, ln_gain, ln_bias, projection, stream, norm_gain, cotangent, slots):
    n_img = lax.axis_size("img")
    n_ctx = lax.axis_size("ctx")
    n_tp = lax.axis_size("tp")
    merged = slots.shape[0]
    tok_rows, width = stream.shape
    owners = n_img * n_ctx
    capacity = 2 * merged // owners
    slot_count = owners * capacity
    full_width = width * n_tp
    cut = width // n_img

    img = lax.axis_index("img").astype(jnp.int32)
    tp = lax.axis_index("tp").astype(jnp.int32)
    core, far_half = tp % 2, tp // 2
    z, y = lax.axis_index("ctx") // RING, lax.axis_index("ctx") % RING
    here = jnp.stack([core, far_half, img, z, y]).astype(jnp.int32)

    flip = [(i, 1 - i) for i in range(n_img)]
    core_pairs = [(t, t ^ 1) for t in range(n_tp)]
    far_pairs = [(t, t ^ 2) for t in range(n_tp)]

    def along_x(array, by):
        pairs = []
        for i in range(n_img):
            for t in range(n_tp):
                x = (2 * (t // 2) + i + by) % RING
                pairs.append((i * n_tp + t, (x % 2) * n_tp + 2 * (x // 2) + t % 2))
        return lax.ppermute(array, ("img", "tp"), pairs)

    def along_ctx(array, axis, by):
        pairs = []
        for c in range(n_ctx):
            for t in range(n_tp):
                z, y = c // RING, c % RING
                if t % 2 == axis:
                    y = (y + by) % RING
                else:
                    z = (z + by) % RING
                pairs.append((c * n_tp + t, (z * RING + y) * n_tp + t))
        return lax.ppermute(array, ("ctx", "tp"), pairs)

    moves = (1, -1, 2)
    columns = lax.dynamic_slice_in_dim(projection[0], img * cut, cut, axis=2).reshape(-1, cut)
    first = stack(here, [columns] + [along_ctx(columns, 0, by) for by in moves])

    slots = jnp.roll(slots, -core * (merged // 2))
    target = slots // tok_rows
    ids = jnp.arange(merged)
    earlier = (target[:, None] == target[None, :]) & (ids[:, None] < ids[None, :])
    rank = jnp.sum(earlier.astype(jnp.int32), axis=0)
    slot = target * capacity + rank
    local = slots - target * tok_rows
    packed = jnp.max(
        jnp.where(jnp.arange(slot_count)[:, None] == slot[None, :], local[None, :], -1), axis=1
    )
    asked = lax.all_to_all(
        packed.reshape(owners, capacity), ("img", "ctx"), split_axis=0, concat_axis=0, tiled=True
    )
    asked = asked.reshape(n_img, n_ctx, capacity).transpose(1, 0, 2)
    asked = asked.reshape(slot_count, 1)
    held = collect(asked, stream, cotangent[0], first)
    came = lax.all_to_all(
        held.reshape(owners, n_img * capacity, width),
        ("img", "ctx"), split_axis=0, concat_axis=0, tiled=True,
    ).reshape(n_img * slot_count, width)
    paired = target * (n_img * capacity) + rank + img * capacity
    paired = jnp.concatenate([paired, lax.ppermute(paired, "img", flip)]).reshape(-1, 1)

    stacks = [first] + [along_ctx(first, 1, by) for by in moves]

    gain = ln_gain[0]
    lifted, xw, stat = layer_norm(here, features[0], gain, ln_bias[0], held)
    pairs = []
    for i in range(n_img):
        for t in range(n_tp):
            x = (2 * (t // 2) + i + (1 if t % 2 == 0 else -1)) % RING
            pairs.append((i * n_tp + t, (x % 2) * n_tp + 2 * (x // 2) + t % 2))
    next_mine = lax.ppermute(lifted[: merged // 2], ("img", "tp"), pairs)
    next_other = lax.ppermute(next_mine, "tp", core_pairs)

    own_gain = lax.dynamic_slice_in_dim(norm_gain, img * cut, cut, axis=1)
    base, cot = unpack(paired, came)
    visual, state, sums = merge(here, base, cot, own_gain, stacks, [lifted, next_mine, next_other])

    near, turned = add(sums, lax.ppermute(sums, "tp", core_pairs))
    stats = [near] + [along_x(near if by == 2 else turned, by) for by in (1, 2, 3)]
    stay, cross = pack(here, paired, visual, n_img * slot_count, near)
    crossed = lax.ppermute(cross, "img", flip)

    chunks = 2
    parts = backward(here, state, cot, own_gain, stats, stacks, chunks, full_width)
    parts, crossed = lax.optimization_barrier((parts, crossed))
    own, rest, other = (parts[i * chunks : (i + 1) * chunks] for i in range(3))
    got = [lax.ppermute(o, "tp", core_pairs) for o in other]
    sent = [pair(rest[c], got[c], crossed) for c in range(chunks)]
    came_back = [[along_x(sent[c][by - 1], by) for by in (1, 2, 3)] for c in range(chunks)]

    send = braid(stay, crossed, n_ctx, came_back[0][0])
    arrived = lax.all_to_all(send, "ctx", split_axis=0, concat_axis=0, tiled=True)
    new_stream = place(here, asked, arrived, stream)

    quarters = [[], [], [], []]
    for c in range(chunks):
        block = (far_half * chunks + c).reshape(1)
        out = finish(block, own[c], got[c], came_back[c], xw, stat, gain)
        beyond = lax.ppermute(out, "tp", far_pairs)
        quarters[0].append(out)
        quarters[1].append(beyond)
        quarters[2].append(lax.ppermute(out, "tp", core_pairs))
        quarters[3].append(lax.ppermute(beyond, "tp", core_pairs))
    grad = lay(here, sum(quarters, []), chunks)
    return (new_stream, grad[None])


def solution(mesh):
    placed = (
        P(None, ("img", "ctx"), None),
        P(),
        P(),
        P(None, None, "ctx", "tp"),
        P(("img", "ctx"), "tp"),
        P(None, "tp"),
        P(None, ("img", "ctx"), "tp"),
        P(("img", "ctx")),
    )
    return jax.shard_map(
        shards,
        mesh=mesh,
        in_specs=placed,
        out_specs=(P(("img", "ctx"), "tp"), P(None, ("img", "ctx"), None)),
        check_vma=False,
    )
```

time: 215 us -> 212 us (0.986)
  blocking collectives: 31.3 us -> 0 us
  waiting for transfers between devices: 53.9 us -> 83.9 us
  starting transfers between devices: 42.1 us -> 63.3 us
  between operations: 14.4 us -> 1.07 us
  local copies, waits for them, and re-layouts: 30.6 us -> 18.6 us
  Pallas kernels: 38.9 us -> 43.3 us
    all_to_all x1 -> x0, blocking collectives: 31.3 us -> none  [shards(): lax.all_to_all(packed.reshape(owners, capacity), ('img', 'ctx'), split_ax...]
    ppermute x9, waiting for transfers between devices: 11.7 us -> 36.5 us  [along_x(): return lax.ppermute(array, ('img', 'tp'), pairs)]
    ppermute x3 -> x9, waiting for transfers between devices: 19.7 us -> 33.9 us  [the longest x6 15.3 us: along_ctx(): return lax.ppermute(array, ('ctx', 'tp'), pairs)]
    ppermute x1, waiting for transfers between devices: 13.1 us -> 0.01 us  [shards(): crossed = lax.ppermute(cross, 'img', flip)]
    unnamed x70, local copies, waits for them, and re-layouts: 26.1 us -> 14.5 us
    ppermute x3 -> x9, starting transfers between devices: 5.52 us -> 15.6 us  [the longest x6 10.1 us: along_ctx(): return lax.ppermute(array, ('ctx', 'tp'), pairs)]
    pallas_call x1, Pallas kernels: 10.7 us -> 2.01 us  [lay(): pl.pallas_call(lambda *refs: lay_kernel(chunks, *refs), in_specs=[scalars...]
    pallas_call x6 -> x9, Pallas kernels: 12.7 us -> 20.5 us  [the longest x1 9.39 us: merge(): pl.pallas_call(merge_kernel, in_specs=[scalars(), whole()] + [anywhere()]...]
  transfers between devices with their start and end apart: 25 -> 31, of which waited for: 9 -> 16; matrix products, arithmetic and copies ran while one was open for 2% -> 1% of each run, Pallas kernels for 12% -> 9%
where the time goes in v7:
time: 212 us; the launch traced here: 211 us
  waiting for transfers between devices  83.9 us (40%)
  starting transfers between devices  63.3 us (30%)
  Pallas kernels  43.3 us (20%)
  local copies, waits for them, and re-layouts  18.6 us (9%)
    ppermute x9, waiting for transfers between devices, along_x(): return lax.ppermute(array, ('img', 'tp'), pairs)  36.5 us
    ppermute x6, waiting for transfers between devices, along_ctx(): return lax.ppermute(array, ('ctx', 'tp'), pairs)  15.3 us
    unnamed x70, local copies, waits for them, and re-layouts  14.5 us
    ppermute x6, starting transfers between devices, along_ctx(): return lax.ppermute(array, ('ctx', 'tp'), pairs)  10.1 us
    pallas_call x1, Pallas kernels, merge(): pl.pallas_call(merge_kernel, in_specs=[scalars(), whole()] + [anywhere()]...  9.39 us
    ppermute x1, waiting for transfers between devices, shards(): next_mine = lax.ppermute(lifted[:merged // 2], ('img', 'tp'), pairs)  9.18 us
    ppermute x9, starting transfers between devices, along_x(): return lax.ppermute(array, ('img', 'tp'), pairs)  9.02 us
    ppermute x1, waiting for transfers between devices, shards(): lax.ppermute(paired, 'img', flip)  8.44 us
  transfers between devices with their start and end apart: 31, of which 16 were waited for; matrix products, arithmetic and copies ran while one was open for 1% of the time, Pallas kernels for 9%

profile of v7, /device:TPU:1, one launch (start us, length us, event | category | flops | bytes accessed | tf_op | source)
XLA Modules:
  0.0 211.2 jit_solution(11869796908483845530)
XLA Ops:
  1.7 2.5 %collective-permute-start.1 = (bf16[288,512]{1,0:T(8,128)(2,1)S(1)}, bf16[288,512]{1,0:T(8,128)(2,1)S(1)}, u32[]{:S(2)}, u32[]{:S(2)}) collective-permute-start(bf16[288,512]{1,0:T(8,128)(2,1)S(1)} %bitcast.22), channel_id=1, source_target_pairs={{0,4},{1,17},{2,6},{3,19},{4,8},{5,21},{6,10},{7,23},{8,12},{9,25}... | collective-permute-start | bytes 884744 | tf_op jit(solution)/shard_map/ppermute | solution.py:603
  4.3 2.2 %collective-permute-start.2 = (bf16[288,512]{1,0:T(8,128)(2,1)S(1)}, bf16[288,512]{1,0:T(8,128)(2,1)S(1)}, u32[]{:S(2)}, u32[]{:S(2)}) collective-permute-start(bf16[288,512]{1,0:T(8,128)(2,1)S(1)} %bitcast.23), channel_id=1, source_target_pairs={{0,12},{1,49},{2,14},{3,51},{4,0},{5,53},{6,2},{7,55},{8,4},{9,57}... | collective-permute-start | bytes 884744 | tf_op jit(solution)/shard_map/ppermute | solution.py:603
  6.5 1.2 collective-permute-start.3
  9.5 7.0 %all-to-all-start = ((s32[32,1,16]{2,1,0:T(1,128)}), s32[32,1,16]{2,1,0:T(1,128)S(1)}, u32[]{:S(2)}, u32[]{:S(2)}) async-start(s32[32,1,16]{2,1,0:T(1,128)} %bitcast.5), calls=%async_computation | async-start | bytes 32768 | tf_op jit(solution)/shard_map/all_to_all | solution.py:619
  16.6 6.9 %all-to-all-done = s32[32,1,16]{2,1,0:T(1,128)S(1)} async-done(((s32[32,1,16]{2,1,0:T(1,128)}), s32[32,1,16]{2,1,0:T(1,128)S(1)}, u32[]{:S(2)}, u32[]{:S(2)}) %all-to-all-start) | async-done | bytes 2080 | tf_op jit(solution)/shard_map/all_to_all | solution.py:619
  25.4 2.7 %collect.1.after_ref = bf16[2,512,1024]{2,1,0:T(8,128)(2,1)} custom-call(s32[512,1]{1,0:T(8,128)S(1)} %reshape.47.pos_ref, bf16[512,1024]{1,0:T(8,128)(2,1)S(1)} %copy-done.6, bf16[512,1024]{1,0:T(8,128)(2,1)S(1)} %bitcast.26, bf16[4,288,512]{2,1,0:T(8,128)(2,1)S(1)} %stack.25.after_ref.refs_0_.refs_8_), custom_call_target="tpu_custom_call" | custom-call | flops 1073741824 | bytes 4194304 | tf_op jit(solution)/shard_map/collect/pallas_call | solution.py:137
  28.1 7.7 %layer_norm.1 = (bf16[256,4608]{1,0:T(8,128)(2,1)}, bf16[4,256,1152]{2,1,0:T(8,128)(2,1)}, f32[256,128]{1,0:T(8,128)}) custom-call(s32[5]{0:T(128)} %copy-done.26, bf16[1024,1152]{1,0:T(8,128)(2,1)} %bitcast.30, bf16[4,1152]{1,0:T(4,128)(2,1)} %bitcast.27, bf16[4,1152]{1,0:T(4,128)(2,1)} %bitcast.34, bf16[2,512,1024]{2,1,0:T(8,128)(2,1)} %collect.1.after_ref), custom_call_target="tpu_custom_call" | custom-call | flops 603979776 | bytes 7077888 | tf_op jit(solution)/shard_map/layer_norm/pallas_call | solution.py:89
  35.7 2.4 %slice.3 = bf16[128,4608]{1,0:T(8,128)(2,1)} slice(bf16[256,4608]{1,0:T(8,128)(2,1)} %get-tuple-element.35.refs_4_), slice={[0:128], [0:4608]} | slice | bytes 2359296 | tf_op jit(solution)/shard_map/slice | solution.py:641
  38.2 1.6 collective-permute-start.7
  39.7 4.9 %all-to-all-start.1 = ((bf16[32,32,1024]{2,1,0:T(8,128)(2,1)}), bf16[32,32,1024]{2,1,0:T(8,128)(2,1)}, u32[]{:S(2)}, u32[]{:S(2)}) async-start(bf16[32,32,1024]{2,1,0:T(8,128)(2,1)} %bitcast.12), calls=%async_computation.1 | async-start | bytes 4194304 | tf_op jit(solution)/shard_map/all_to_all | solution.py:625
  45.7 1.6 collective-permute-start.5
  47.4 1.3 collective-permute-start.6
  48.7 9.2 %collective-permute-done.7.refs_5_ = bf16[128,4608]{1,0:T(8,128)(2,1)} collective-permute-done((bf16[128,4608]{1,0:T(8,128)(2,1)}, bf16[128,4608]{1,0:T(8,128)(2,1)}, u32[]{:S(2)}, u32[]{:S(2)}) %collective-permute-start.7) | collective-permute-done | bytes 1179680 | tf_op jit(solution)/shard_map/ppermute | solution.py:641
  57.9 7.3 %collective-permute-start.8 = (bf16[128,4608]{1,0:T(8,128)(2,1)}, bf16[128,4608]{1,0:T(8,128)(2,1)}, u32[]{:S(2)}, u32[]{:S(2)}) collective-permute-start(bf16[128,4608]{1,0:T(8,128)(2,1)} %collective-permute-done.7.refs_5_), channel_id=1, source_target_pairs={{0,1},{1,0},{2,3},{3,2},{4,5},{5,4},{6,7},{7,6},{8,9},{9,8},{10,11... | collective-permute-start | bytes 3538952 | tf_op jit(solution)/shard_map/ppermute | solution.py:642
  65.3 2.2 %collective-permute-start = (s32[256]{0:T(256)S(1)}, s32[256]{0:T(256)S(1)}, u32[]{:S(2)}, u32[]{:S(2)}) collective-permute-start(s32[256]{0:T(256)S(1)} %get-tuple-element.66), channel_id=1, source_target_pairs={{0,64},{64,0},{1,65},{65,1},{2,66},{66,2},{3,67},{67,3},{4,68},{68... | collective-permute-start | bytes 3080 | tf_op jit(solution)/shard_map/ppermute | solution.py:630
  68.0 8.4 %collective-permute-done = s32[256]{0:T(256)S(1)} collective-permute-done((s32[256]{0:T(256)S(1)}, s32[256]{0:T(256)S(1)}, u32[]{:S(2)}, u32[]{:S(2)}) %collective-permute-start) | collective-permute-done | bytes 1056 | tf_op jit(solution)/shard_map/ppermute | solution.py:630
  76.6 2.9 %unpack.1 = (bf16[512,512]{1,0:T(8,128)(2,1)S(1)}, bf16[512,512]{1,0:T(8,128)(2,1)S(1)}) custom-call(s32[512,1]{1,0:T(8,128)S(1)} %copy.28.slot_ref, bf16[1024,1024]{1,0:T(8,128)(2,1)} %bitcast.13.came_ref), custom_call_target="tpu_custom_call" | custom-call | flops 1073741824 | bytes 2097152 | tf_op jit(solution)/shard_map/unpack/pallas_call | solution.py:163
  81.1 2.2 %collective-permute-done.4.refs_1_.refs_9_ = bf16[4,288,512]{2,1,0:T(8,128)(2,1)S(1)} collective-permute-done((bf16[4,288,512]{2,1,0:T(8,128)(2,1)S(1)}, bf16[4,288,512]{2,1,0:T(8,128)(2,1)S(1)}, u32[]{:S(2)}, u32[]{:S(2)}) %collective-permute-start.4) | collective-permute-done | bytes 1179680 | tf_op jit(solution)/shard_map/ppermute | solution.py:603
  83.3 13.1 %collective-permute-done.6.refs_3_.refs_11_ = bf16[4,288,512]{2,1,0:T(8,128)(2,1)} collective-permute-done((bf16[4,288,512]{2,1,0:T(8,128)(2,1)S(1)}, bf16[4,288,512]{2,1,0:T(8,128)(2,1)}, u32[]{:S(2)}, u32[]{:S(2)}) %collective-permute-start.6) | collective-permute-done | bytes 1179680 | tf_op jit(solution)/shard_map/ppermute | solution.py:603
  96.4 9.4 %merge.1 = (bf16[512,512]{1,0:T(8,128)(2,1)}, f32[512,512]{1,0:T(8,128)}, f32[8,512]{1,0:T(8,128)}) custom-call(s32[5]{0:T(128)} %copy-done.26, bf16[1,512]{1,0:T(2,128)(2,1)} %constant_dynamic-slice_fusion.1.ngain_ref.refs_3_, bf16[512,512]{1,0:T(8,128)(2,1)} %copy-done.23, bf16[512,512]{1,0:T(8,128)(2,1)} %copy-done.21, bf16[4,288,512]{2,1,0:T(8,128)(2,1)} %copy-done.1, ...), custom_call_target="tpu_custom_call" | custom-call | flops 2415919104 | bytes 4718592 | tf_op jit(solution)/shard_map/merge/pallas_call | solution.py:270
  105.8 1.8 collective-permute-start.9
  110.4 1.4 pack.1
  114.4 1.6 collective-permute-start.12
  116.0 8.1 %collective-permute-done.10.refs_5_ = f32[8,512]{1,0:T(8,128)S(1)} collective-permute-done((f32[8,512]{1,0:T(8,128)S(1)}, f32[8,512]{1,0:T(8,128)S(1)}, u32[]{:S(2)}, u32[]{:S(2)}) %collective-permute-start.10) | collective-permute-done | bytes 16416 | tf_op jit(solution)/shard_map/ppermute | solution.py:591
  124.1 1.9 collective-permute-done.11.refs_6_
  126.0 1.3 copy-done.11
  128.5 6.8 %backward.1 = (f32[32,4608]{1,0:T(8,128)S(1)}, f32[32,4608]{1,0:T(8,128)S(1)}, bf16[96,4608]{1,0:T(8,128)(2,1)S(1)}, bf16[96,4608]{1,0:T(8,128)(2,1)S(1)}, bf16[...) custom-call(s32[5]{0:T(128)S(1)} %copy-done.27, f32[512,512]{1,0:T(8,128)S(1)} %copy-done.30, ...), custom_call_target="tpu_custom_call" | custom-call | flops 2415919104 | bytes 4718592 | tf_op jit(solution)/shard_map/backward/pallas_call | solution.py:408
  137.1 1.7 collective-permute-start.14
  138.9 3.2 %collective-permute-done.14.got_ref = bf16[128,4608]{1,0:T(8,128)(2,1)S(1)} collective-permute-done((bf16[128,4608]{1,0:T(8,128)(2,1)S(1)}, bf16[128,4608]{1,0:T(8,128)(2,1)S(1)}, u32[]{:S(2)}, u32[]{:S(2)}) %collective-permute-start.14) | collective-permute-done | bytes 1179680 | tf_op jit(solution)/shard_map/ppermute | solution.py:657
  143.3 9.3 %collective-permute-done.15.after_ref.refs_0_ = bf16[32,4608]{1,0:T(8,128)(2,1)S(1)} collective-permute-done((bf16[32,4608]{1,0:T(8,128)(2,1)S(1)}, bf16[32,4608]{1,0:T(8,128)(2,1)S(1)}, u32[]{:S(2)}, u32[]{:S(2)}) %collective-permute-start.15) | collective-permute-done | bytes 294944 | tf_op jit(solution)/shard_map/ppermute | solution.py:591
  154.3 4.3 %all-to-all-start.2 = ((bf16[16,2,32,512]{3,2,1,0:T(8,128)(2,1)}), bf16[16,2,32,512]{3,2,1,0:T(8,128)(2,1)}, u32[]{:S(2)}, u32[]{:S(2)}) async-start(bf16[16,2,32,512]{3,2,1,0:T(8,128)(2,1)} %braid.1), calls=%async_computation.2 | async-start | bytes 2097152 | tf_op jit(solution)/shard_map/all_to_all | solution.py:662
  158.7 1.3 copy-done.16
  160.0 2.3 %pair.3 = (bf16[32,4608]{1,0:T(8,128)(2,1)}, bf16[32,4608]{1,0:T(8,128)(2,1)}, bf16[32,4608]{1,0:T(8,128)(2,1)}) custom-call(bf16[96,4608]{1,0:T(8,128)(2,1)S(1)} %copy-done.16, bf16[128,4608]{1,0:T(8,128)(2,1)} %collective-permute-done.18.got_ref, bf16[512,512]{1,0:T(8,128)(2,1)S(1)} %collective-permute-done.13.after_ref.crossed_ref), custom_call_target="tpu_custom_call" | custom-call | flops 589824 | bytes 3538944 | tf_op jit(solution)/shard_map/pair/pallas_call | solution.py:436
  162.3 1.6 collective-permute-start.20
  165.0 2.3 %collective-permute-start.16 = (bf16[32,4608]{1,0:T(8,128)(2,1)}, bf16[32,4608]{1,0:T(8,128)(2,1)S(1)}, u32[]{:S(2)}, u32[]{:S(2)}) collective-permute-start(bf16[32,4608]{1,0:T(8,128)(2,1)} %copy-done.33), channel_id=1, source_target_pairs={{0,2},{1,3},{2,0},{3,1},{64,66},{65,67},{66,64},{67,65},{4,6},{5,7... | collective-permute-start | bytes 884744 | tf_op jit(solution)/shard_map/ppermute | solution.py:591
  167.9 4.1 %collective-permute-done.19.refs_0_ = bf16[32,4608]{1,0:T(8,128)(2,1)} collective-permute-done((bf16[32,4608]{1,0:T(8,128)(2,1)}, bf16[32,4608]{1,0:T(8,128)(2,1)}, u32[]{:S(2)}, u32[]{:S(2)}) %collective-permute-start.19) | collective-permute-done | bytes 294944 | tf_op jit(solution)/shard_map/ppermute | solution.py:591
  172.0 4.5 %collective-permute-done.20.refs_1_ = bf16[32,4608]{1,0:T(8,128)(2,1)} collective-permute-done((bf16[32,4608]{1,0:T(8,128)(2,1)}, bf16[32,4608]{1,0:T(8,128)(2,1)}, u32[]{:S(2)}, u32[]{:S(2)}) %collective-permute-start.20) | collective-permute-done | bytes 294944 | tf_op jit(solution)/shard_map/ppermute | solution.py:591
  176.5 2.4 %collective-permute-done.21.refs_2_ = bf16[32,4608]{1,0:T(8,128)(2,1)} collective-permute-done((bf16[32,4608]{1,0:T(8,128)(2,1)}, bf16[32,4608]{1,0:T(8,128)(2,1)}, u32[]{:S(2)}, u32[]{:S(2)}) %collective-permute-start.21) | collective-permute-done | bytes 294944 | tf_op jit(solution)/shard_map/ppermute | solution.py:591
  180.8 2.3 %finish.3.refs_2_ = bf16[128,1152]{1,0:T(8,128)(2,1)S(1)} custom-call(s32[1]{0:T(128)} %bitcast.18.block_ref, f32[32,4608]{1,0:T(8,128)S(1)} %copy-done.20, bf16[128,4608]{1,0:T(8,128)(2,1)} %collective-permute-done.18.got_ref, bf16[32,4608]{1,0:T(8,128)(2,1)} %collective-permute-done.19.refs_0_, bf16[32,4608]{1,0:T(8,128)(2,1)} %collective-permute-done.20.refs_1_, ...), custom_call_target="tpu_custom_call" | custom-call | flops 37748736 | bytes 1179648 | tf_op jit(solution)/shard_map/finish/pallas_call | solution.py:482
  183.1 2.0 collective-permute-start.23
  185.1 6.3 %collective-permute-done.17.refs_2_ = bf16[32,4608]{1,0:T(8,128)(2,1)S(1)} collective-permute-done((bf16[32,4608]{1,0:T(8,128)(2,1)}, bf16[32,4608]{1,0:T(8,128)(2,1)S(1)}, u32[]{:S(2)}, u32[]{:S(2)}) %collective-permute-start.17) | collective-permute-done | bytes 294944 | tf_op jit(solution)/shard_map/ppermute | solution.py:591
  192.4 2.0 collective-permute-start.22
  194.4 2.5 %collective-permute-start.25 = (bf16[128,1152]{1,0:T(8,128)(2,1)S(1)}, bf16[128,1152]{1,0:T(8,128)(2,1)S(1)}, u32[]{:S(2)}, u32[]{:S(2)}) collective-permute-start(bf16[128,1152]{1,0:T(8,128)(2,1)S(1)} %finish.3.refs_2_), channel_id=1, source_target_pairs={{0,1},{1,0},{2,3},{3,2},{4,5},{5,4},{6,7},{7,6},{8,9},{9,8},{10,11... | collective-permute-start | bytes 884744 | tf_op jit(solution)/shard_map/ppermute | solution.py:672
  196.9 3.0 %collective-permute-start.27 = (bf16[128,1152]{1,0:T(8,128)(2,1)S(1)}, bf16[128,1152]{1,0:T(8,128)(2,1)S(1)}, u32[]{:S(2)}, u32[]{:S(2)}) collective-permute-start(bf16[128,1152]{1,0:T(8,128)(2,1)S(1)} %collective-permute-done.23.refs_4_), channel_id=1, source_target_pairs={{0,1},{1,0},{2,3},{3,2},{4,5},{5,4},{6,7},{7,6},{8,9},{9,8},{10,11... | collective-permute-start | bytes 884744 | tf_op jit(solution)/shard_map/ppermute | solution.py:673
  199.9 2.1 collective-permute-done.22.refs_3_
  202.0 2.9 %collective-permute-start.26 = (bf16[128,1152]{1,0:T(8,128)(2,1)S(1)}, bf16[128,1152]{1,0:T(8,128)(2,1)S(1)}, u32[]{:S(2)}, u32[]{:S(2)}) collective-permute-start(bf16[128,1152]{1,0:T(8,128)(2,1)S(1)} %collective-permute-done.22.refs_3_), channel_id=1, source_target_pairs={{0,1},{1,0},{2,3},{3,2},{4,5},{5,4},{6,7},{7,6},{8,9},{9,8},{10,11... | collective-permute-start | bytes 884744 | tf_op jit(solution)/shard_map/ppermute | solution.py:673
  206.0 2.0 lay.1
  208.1 3.1 %place.1 = bf16[512,1024]{1,0:T(8,128)(2,1)} custom-call(s32[5]{0:T(128)S(1)} %copy-done.27, s32[512,1]{1,0:T(8,128)S(1)} %copy-done.9, bf16[16,2,32,512]{3,2,1,0:T(8,128)(2,1)} %all-to-all-done.2.came_ref, bf16[512,1024]{1,0:T(8,128)(2,1)S(1)} %copy-done.7), custom_call_target="tpu_custom_call" | custom-call | flops 536870912 | bytes 3145728 | tf_op jit(solution)/shard_map/place/pallas_call | solution.py:523
  (113 shorter events, 25.4 us)
Async XLA Ops:
  1.7 22.0 %collective-permute-start.1 = (bf16[288,512]{1,0:T(8,128)(2,1)S(1)}, bf16[288,512]{1,0:T(8,128)(2,1)S(1)}, u32[]{:S(2)}, u32[]{:S(2)}) collective-permute-start(bf16[288,512]{1,0:T(8,128)(2,1)S(1)} %bitcast.22), channel_id=1, source_target_pairs={{0,4},{1,17},{2,6},{3,19},{4,8},{5,21},{6,10},{7,23},{8,12},{9,25}... | collective-permute-start | bytes 884744 | tf_op jit(solution)/shard_map/ppermute | solution.py:603
  4.3 19.5 %collective-permute-start.2 = (bf16[288,512]{1,0:T(8,128)(2,1)S(1)}, bf16[288,512]{1,0:T(8,128)(2,1)S(1)}, u32[]{:S(2)}, u32[]{:S(2)}) collective-permute-start(bf16[288,512]{1,0:T(8,128)(2,1)S(1)} %bitcast.23), channel_id=1, source_target_pairs={{0,12},{1,49},{2,14},{3,51},{4,0},{5,53},{6,2},{7,55},{8,4},{9,57}... | collective-permute-start | bytes 884744 | tf_op jit(solution)/shard_map/ppermute | solution.py:603
  6.5 17.3 %collective-permute-start.3 = (bf16[288,512]{1,0:T(8,128)(2,1)S(1)}, bf16[288,512]{1,0:T(8,128)(2,1)S(1)}, u32[]{:S(2)}, u32[]{:S(2)}) collective-permute-start(bf16[288,512]{1,0:T(8,128)(2,1)S(1)} %bitcast.24), channel_id=1, source_target_pairs={{0,8},{1,33},{2,10},{3,35},{4,12},{5,37},{6,14},{7,39},{8,0},{9,41... | collective-permute-start | bytes 884744 | tf_op jit(solution)/shard_map/ppermute | solution.py:603
  9.5 14.0 %all-to-all-start = ((s32[32,1,16]{2,1,0:T(1,128)}), s32[32,1,16]{2,1,0:T(1,128)S(1)}, u32[]{:S(2)}, u32[]{:S(2)}) async-start(s32[32,1,16]{2,1,0:T(1,128)} %bitcast.5), calls=%async_computation | async-start | bytes 32768 | tf_op jit(solution)/shard_map/all_to_all | solution.py:619
  16.6 7.8 %copy-start.26 = (s32[5]{0:T(128)}, s32[5]{0:T(128)S(1)}, u32[]{:S(2)}) copy-start(s32[5]{0:T(128)S(1)} %stack.24.here_ref.refs_0_) | copy-start | bytes 64
  24.4 23.0 %copy-start.1 = (bf16[4,288,512]{2,1,0:T(8,128)(2,1)}, bf16[4,288,512]{2,1,0:T(8,128)(2,1)S(1)}, u32[]{:S(2)}) copy-start(bf16[4,288,512]{2,1,0:T(8,128)(2,1)S(1)} %stack.25.after_ref.refs_0_.refs_8_) | copy-start | bytes 3538948
  38.2 19.8 %collective-permute-start.7 = (bf16[128,4608]{1,0:T(8,128)(2,1)}, bf16[128,4608]{1,0:T(8,128)(2,1)}, u32[]{:S(2)}, u32[]{:S(2)}) collective-permute-start(bf16[128,4608]{1,0:T(8,128)(2,1)} %slice.3), channel_id=1, source_target_pairs={{0,64},{1,67},{2,66},{3,65},{64,2},{65,1},{66,0},{67,3},{4,68},{5,... | collective-permute-start | bytes 3538952 | tf_op jit(solution)/shard_map/ppermute | solution.py:641
  39.7 27.7 %copy-start.34 = (bf16[1,1024]{1,0:T(2,128)(2,1)S(1)}, bf16[1,1024]{1,0:T(2,128)(2,1)}, u32[]{:S(2)}) copy-start(bf16[1,1024]{1,0:T(2,128)(2,1)} %param.13) | copy-start | bytes 6148
  39.7 36.9 %all-to-all-start.1 = ((bf16[32,32,1024]{2,1,0:T(8,128)(2,1)}), bf16[32,32,1024]{2,1,0:T(8,128)(2,1)}, u32[]{:S(2)}, u32[]{:S(2)}) async-start(bf16[32,32,1024]{2,1,0:T(8,128)(2,1)} %bitcast.12), calls=%async_computation.1 | async-start | bytes 4194304 | tf_op jit(solution)/shard_map/all_to_all | solution.py:625
  44.6 38.7 %collective-permute-start.4 = (bf16[4,288,512]{2,1,0:T(8,128)(2,1)S(1)}, bf16[4,288,512]{2,1,0:T(8,128)(2,1)S(1)}, u32[]{:S(2)}, u32[]{:S(2)}) collective-permute-start(bf16[4,288,512]{2,1,0:T(8,128)(2,1)S(1)} %stack.25.after_ref.refs_0_.refs_8_), channel_id=1, source_target_pairs={{0,16},{1,5},{2,18},{3,7},{4,20},{5,9},{6,22},{7,11},{8,24},{9,13}... | collective-permute-start | bytes 3538952 | tf_op jit(solution)/shard_map/ppermute | solution.py:603
  45.7 37.6 %collective-permute-start.5 = (bf16[4,288,512]{2,1,0:T(8,128)(2,1)S(1)}, bf16[4,288,512]{2,1,0:T(8,128)(2,1)}, u32[]{:S(2)}, u32[]{:S(2)}) collective-permute-start(bf16[4,288,512]{2,1,0:T(8,128)(2,1)S(1)} %stack.25.after_ref.refs_0_.refs_8_), channel_id=1, source_target_pairs={{0,48},{1,13},{2,50},{3,15},{4,52},{5,1},{6,54},{7,3},{8,56},{9,5}... | collective-permute-start | bytes 3538952 | tf_op jit(solution)/shard_map/ppermute | solution.py:603
  47.4 49.0 %collective-permute-start.6 = (bf16[4,288,512]{2,1,0:T(8,128)(2,1)S(1)}, bf16[4,288,512]{2,1,0:T(8,128)(2,1)}, u32[]{:S(2)}, u32[]{:S(2)}) collective-permute-start(bf16[4,288,512]{2,1,0:T(8,128)(2,1)S(1)} %stack.25.after_ref.refs_0_.refs_8_), channel_id=1, source_target_pairs={{0,32},{1,9},{2,34},{3,11},{4,36},{5,13},{6,38},{7,15},{8,40},{9,1... | collective-permute-start | bytes 3538952 | tf_op jit(solution)/shard_map/ppermute | solution.py:603
  57.9 38.5 %collective-permute-start.8 = (bf16[128,4608]{1,0:T(8,128)(2,1)}, bf16[128,4608]{1,0:T(8,128)(2,1)}, u32[]{:S(2)}, u32[]{:S(2)}) collective-permute-start(bf16[128,4608]{1,0:T(8,128)(2,1)} %collective-permute-done.7.refs_5_), channel_id=1, source_target_pairs={{0,1},{1,0},{2,3},{3,2},{4,5},{5,4},{6,7},{7,6},{8,9},{9,8},{10,11... | collective-permute-start | bytes 3538952 | tf_op jit(solution)/shard_map/ppermute | solution.py:642
  65.3 11.2 %collective-permute-start = (s32[256]{0:T(256)S(1)}, s32[256]{0:T(256)S(1)}, u32[]{:S(2)}, u32[]{:S(2)}) collective-permute-start(s32[256]{0:T(256)S(1)} %get-tuple-element.66), channel_id=1, source_target_pairs={{0,64},{64,0},{1,65},{65,1},{2,66},{66,2},{3,67},{67,3},{4,68},{68... | collective-permute-start | bytes 3080 | tf_op jit(solution)/shard_map/ppermute | solution.py:630
  83.3 13.1 %copy-start.10 = (bf16[4,288,512]{2,1,0:T(8,128)(2,1)}, bf16[4,288,512]{2,1,0:T(8,128)(2,1)S(1)}, u32[]{:S(2)}) copy-start(bf16[4,288,512]{2,1,0:T(8,128)(2,1)S(1)} %collective-permute-done.4.refs_1_.refs_9_) | copy-start | bytes 3538948
  96.4 13.0 %copy-start.27 = (s32[5]{0:T(128)S(1)}, s32[5]{0:T(128)}, u32[]{:S(2)}) copy-start(s32[5]{0:T(128)} %copy-done.26) | copy-start | bytes 64
  96.4 29.6 %copy-start.29 = (bf16[1,512]{1,0:T(2,128)(2,1)S(1)}, bf16[1,512]{1,0:T(2,128)(2,1)}, u32[]{:S(2)}) copy-start(bf16[1,512]{1,0:T(2,128)(2,1)} %constant_dynamic-slice_fusion.1.ngain_ref.refs_3_) | copy-start | bytes 3076
  105.8 20.2 %copy-start.2 = (bf16[4,288,512]{2,1,0:T(8,128)(2,1)S(1)}, bf16[4,288,512]{2,1,0:T(8,128)(2,1)}, u32[]{:S(2)}) copy-start(bf16[4,288,512]{2,1,0:T(8,128)(2,1)} %copy-done.1) | copy-start | bytes 3538948
  105.8 20.2 %copy-start.22 = (bf16[512,512]{1,0:T(8,128)(2,1)S(1)}, bf16[512,512]{1,0:T(8,128)(2,1)}, u32[]{:S(2)}) copy-start(bf16[512,512]{1,0:T(8,128)(2,1)} %copy-done.21) | copy-start | bytes 1572868
  105.8 2.8 %collective-permute-start.9 = (f32[8,512]{1,0:T(8,128)}, f32[8,512]{1,0:T(8,128)S(1)}, u32[]{:S(2)}, u32[]{:S(2)}) collective-permute-start(f32[8,512]{1,0:T(8,128)} %get-tuple-element.37.sums_ref), channel_id=1, source_target_pairs={{0,1},{1,0},{2,3},{3,2},{4,5},{5,4},{6,7},{7,6},{8,9},{9,8},{10,11... | collective-permute-start | bytes 49160 | tf_op jit(solution)/shard_map/ppermute | solution.py:648
  111.8 25.3 %collective-permute-start.13 = (bf16[512,512]{1,0:T(8,128)(2,1)S(1)}, bf16[512,512]{1,0:T(8,128)(2,1)S(1)}, u32[]{:S(2)}, u32[]{:S(2)}) collective-permute-start(bf16[512,512]{1,0:T(8,128)(2,1)S(1)} %get-tuple-element.48), channel_id=1, source_target_pairs={{0,64},{64,0},{1,65},{65,1},{2,66},{66,2},{3,67},{67,3},{4,68},{68... | collective-permute-start | bytes 1572872 | tf_op jit(solution)/shard_map/ppermute | solution.py:651
  112.8 11.3 %collective-permute-start.10 = (f32[8,512]{1,0:T(8,128)S(1)}, f32[8,512]{1,0:T(8,128)S(1)}, u32[]{:S(2)}, u32[]{:S(2)}) collective-permute-start(f32[8,512]{1,0:T(8,128)S(1)} %get-tuple-element.41), channel_id=1, source_target_pairs={{0,64},{1,65},{2,66},{3,67},{64,2},{65,3},{66,0},{67,1},{4,68},{5,... | collective-permute-start | bytes 49160 | tf_op jit(solution)/shard_map/ppermute | solution.py:591
  113.4 12.6 %collective-permute-start.11 = (f32[8,512]{1,0:T(8,128)S(1)}, f32[8,512]{1,0:T(8,128)S(1)}, u32[]{:S(2)}, u32[]{:S(2)}) collective-permute-start(f32[8,512]{1,0:T(8,128)S(1)} %get-tuple-element.38.after_ref.refs_4_), channel_id=1, source_target_pairs={{0,2},{1,3},{2,0},{3,1},{64,66},{65,67},{66,64},{67,65},{4,6},{5,7... | collective-permute-start | bytes 49160 | tf_op jit(solution)/shard_map/ppermute | solution.py:591
  114.4 11.6 %collective-permute-start.12 = (f32[8,512]{1,0:T(8,128)S(1)}, f32[8,512]{1,0:T(8,128)S(1)}, u32[]{:S(2)}, u32[]{:S(2)}) collective-permute-start(f32[8,512]{1,0:T(8,128)S(1)} %get-tuple-element.41), channel_id=1, source_target_pairs={{0,66},{1,67},{2,64},{3,65},{64,0},{65,1},{66,2},{67,3},{4,70},{5,... | collective-permute-start | bytes 49160 | tf_op jit(solution)/shard_map/ppermute | solution.py:591
  137.1 5.0 %collective-permute-start.14 = (bf16[128,4608]{1,0:T(8,128)(2,1)S(1)}, bf16[128,4608]{1,0:T(8,128)(2,1)S(1)}, u32[]{:S(2)}, u32[]{:S(2)}) collective-permute-start(bf16[128,4608]{1,0:T(8,128)(2,1)S(1)} %get-tuple-element.51), channel_id=1, source_target_pairs={{0,1},{1,0},{2,3},{3,2},{4,5},{5,4},{6,7},{7,6},{8,9},{9,8},{10,11... | collective-permute-start | bytes 3538952 | tf_op jit(solution)/shard_map/ppermute | solution.py:657
  138.8 19.9 %collective-permute-start.18 = (bf16[128,4608]{1,0:T(8,128)(2,1)}, bf16[128,4608]{1,0:T(8,128)(2,1)}, u32[]{:S(2)}, u32[]{:S(2)}) collective-permute-start(bf16[128,4608]{1,0:T(8,128)(2,1)} %get-tuple-element.59), channel_id=1, source_target_pairs={{0,1},{1,0},{2,3},{3,2},{4,5},{5,4},{6,7},{7,6},{8,9},{9,8},{10,11... | collective-permute-start | bytes 3538952 | tf_op jit(solution)/shard_map/ppermute | solution.py:657
  143.1 10.5 %copy-start.32 = (bf16[32,4608]{1,0:T(8,128)(2,1)}, bf16[32,4608]{1,0:T(8,128)(2,1)S(1)}, u32[]{:S(2)}) copy-start(bf16[32,4608]{1,0:T(8,128)(2,1)S(1)} %get-tuple-element.55) | copy-start | bytes 884740
  143.1 10.5 %copy-start.33 = (bf16[32,4608]{1,0:T(8,128)(2,1)}, bf16[32,4608]{1,0:T(8,128)(2,1)S(1)}, u32[]{:S(2)}) copy-start(bf16[32,4608]{1,0:T(8,128)(2,1)S(1)} %get-tuple-element.54) | copy-start | bytes 884740
  143.1 9.4 %collective-permute-start.15 = (bf16[32,4608]{1,0:T(8,128)(2,1)S(1)}, bf16[32,4608]{1,0:T(8,128)(2,1)S(1)}, u32[]{:S(2)}, u32[]{:S(2)}) collective-permute-start(bf16[32,4608]{1,0:T(8,128)(2,1)S(1)} %get-tuple-element.52), channel_id=1, source_target_pairs={{0,64},{1,65},{2,66},{3,67},{64,2},{65,3},{66,0},{67,1},{4,68},{5,... | collective-permute-start | bytes 884744 | tf_op jit(solution)/shard_map/ppermute | solution.py:591
  154.3 53.7 %all-to-all-start.2 = ((bf16[16,2,32,512]{3,2,1,0:T(8,128)(2,1)}), bf16[16,2,32,512]{3,2,1,0:T(8,128)(2,1)}, u32[]{:S(2)}, u32[]{:S(2)}) async-start(bf16[16,2,32,512]{3,2,1,0:T(8,128)(2,1)} %braid.1), calls=%async_computation.2 | async-start | bytes 2097152 | tf_op jit(solution)/shard_map/all_to_all | solution.py:662
  158.7 20.1 %copy-start.3 = (bf16[4,256,1152]{2,1,0:T(8,128)(2,1)S(1)}, bf16[4,256,1152]{2,1,0:T(8,128)(2,1)}, u32[]{:S(2)}) copy-start(bf16[4,256,1152]{2,1,0:T(8,128)(2,1)} %get-tuple-element.56.refs_3_) | copy-start | bytes 7077892
  160.0 18.8 %copy-start.25 = (bf16[1,4,1152]{2,1,0:T(4,128)(2,1)S(1)}, bf16[1,4,1152]{2,1,0:T(4,128)(2,1)}, u32[]{:S(2)}) copy-start(bf16[1,4,1152]{2,1,0:T(4,128)(2,1)} %param.9) | copy-start | bytes 27652
  162.3 9.7 %collective-permute-start.19 = (bf16[32,4608]{1,0:T(8,128)(2,1)}, bf16[32,4608]{1,0:T(8,128)(2,1)}, u32[]{:S(2)}, u32[]{:S(2)}) collective-permute-start(bf16[32,4608]{1,0:T(8,128)(2,1)} %get-tuple-element.61), channel_id=1, source_target_pairs={{0,64},{1,65},{2,66},{3,67},{64,2},{65,3},{66,0},{67,1},{4,68},{5,... | collective-permute-start | bytes 884744 | tf_op jit(solution)/shard_map/ppermute | solution.py:591
  162.3 14.2 %collective-permute-start.20 = (bf16[32,4608]{1,0:T(8,128)(2,1)}, bf16[32,4608]{1,0:T(8,128)(2,1)}, u32[]{:S(2)}, u32[]{:S(2)}) collective-permute-start(bf16[32,4608]{1,0:T(8,128)(2,1)} %get-tuple-element.62), channel_id=1, source_target_pairs={{0,2},{1,3},{2,0},{3,1},{64,66},{65,67},{66,64},{67,65},{4,6},{5,7... | collective-permute-start | bytes 884744 | tf_op jit(solution)/shard_map/ppermute | solution.py:591
  163.9 14.9 %collective-permute-start.21 = (bf16[32,4608]{1,0:T(8,128)(2,1)}, bf16[32,4608]{1,0:T(8,128)(2,1)}, u32[]{:S(2)}, u32[]{:S(2)}) collective-permute-start(bf16[32,4608]{1,0:T(8,128)(2,1)} %get-tuple-element.63), channel_id=1, source_target_pairs={{0,66},{1,67},{2,64},{3,65},{64,0},{65,1},{66,2},{67,3},{4,70},{5,... | collective-permute-start | bytes 884744 | tf_op jit(solution)/shard_map/ppermute | solution.py:591
  165.0 20.1 %collective-permute-start.16 = (bf16[32,4608]{1,0:T(8,128)(2,1)}, bf16[32,4608]{1,0:T(8,128)(2,1)S(1)}, u32[]{:S(2)}, u32[]{:S(2)}) collective-permute-start(bf16[32,4608]{1,0:T(8,128)(2,1)} %copy-done.33), channel_id=1, source_target_pairs={{0,2},{1,3},{2,0},{3,1},{64,66},{65,67},{66,64},{67,65},{4,6},{5,7... | collective-permute-start | bytes 884744 | tf_op jit(solution)/shard_map/ppermute | solution.py:591
  167.3 24.1 %collective-permute-start.17 = (bf16[32,4608]{1,0:T(8,128)(2,1)}, bf16[32,4608]{1,0:T(8,128)(2,1)S(1)}, u32[]{:S(2)}, u32[]{:S(2)}) collective-permute-start(bf16[32,4608]{1,0:T(8,128)(2,1)} %copy-done.32), channel_id=1, source_target_pairs={{0,66},{1,67},{2,64},{3,65},{64,0},{65,1},{66,2},{67,3},{4,70},{5,... | collective-permute-start | bytes 884744 | tf_op jit(solution)/shard_map/ppermute | solution.py:591
  180.8 10.6 %copy-start.5 = (bf16[128,4608]{1,0:T(8,128)(2,1)S(1)}, bf16[128,4608]{1,0:T(8,128)(2,1)}, u32[]{:S(2)}) copy-start(bf16[128,4608]{1,0:T(8,128)(2,1)} %copy-done.4) | copy-start | bytes 3538948
  180.8 10.6 %copy-start.13 = (bf16[32,4608]{1,0:T(8,128)(2,1)S(1)}, bf16[32,4608]{1,0:T(8,128)(2,1)}, u32[]{:S(2)}) copy-start(bf16[32,4608]{1,0:T(8,128)(2,1)} %copy-done.12) | copy-start | bytes 884740
  180.8 10.6 %copy-start.18 = (f32[32,4608]{1,0:T(8,128)S(1)}, f32[32,4608]{1,0:T(8,128)}, u32[]{:S(2)}) copy-start(f32[32,4608]{1,0:T(8,128)} %copy-done.17) | copy-start | bytes 1769476
  183.1 13.7 %collective-permute-start.23 = (bf16[128,1152]{1,0:T(8,128)(2,1)S(1)}, bf16[128,1152]{1,0:T(8,128)(2,1)S(1)}, u32[]{:S(2)}, u32[]{:S(2)}) collective-permute-start(bf16[128,1152]{1,0:T(8,128)(2,1)S(1)} %finish.3.refs_2_), channel_id=1, source_target_pairs={{0,2},{1,3},{2,0},{3,1},{4,6},{5,7},{6,4},{7,5},{8,10},{9,11},{10,... | collective-permute-start | bytes 884744 | tf_op jit(solution)/shard_map/ppermute | solution.py:669
  192.4 15.7 %copy-start.7 = (bf16[512,1024]{1,0:T(8,128)(2,1)S(1)}, bf16[512,1024]{1,0:T(8,128)(2,1)}, u32[]{:S(2)}) copy-start(bf16[512,1024]{1,0:T(8,128)(2,1)} %stream_ref.3) | copy-start | bytes 3145732
  192.4 15.7 %copy-start.9 = (s32[512,1]{1,0:T(8,128)S(1)}, s32[512,1]{1,0:T(8,128)}, u32[]{:S(2)}) copy-start(s32[512,1]{1,0:T(8,128)} %copy-done.8) | copy-start | bytes 6148
  192.4 9.5 %collective-permute-start.22 = (bf16[128,1152]{1,0:T(8,128)(2,1)S(1)}, bf16[128,1152]{1,0:T(8,128)(2,1)S(1)}, u32[]{:S(2)}, u32[]{:S(2)}) collective-permute-start(bf16[128,1152]{1,0:T(8,128)(2,1)S(1)} %finish.2.refs_1_), channel_id=1, source_target_pairs={{0,2},{1,3},{2,0},{3,1},{4,6},{5,7},{6,4},{7,5},{8,10},{9,11},{10,... | collective-permute-start | bytes 884744 | tf_op jit(solution)/shard_map/ppermute | solution.py:669
  194.4 10.4 %collective-permute-start.25 = (bf16[128,1152]{1,0:T(8,128)(2,1)S(1)}, bf16[128,1152]{1,0:T(8,128)(2,1)S(1)}, u32[]{:S(2)}, u32[]{:S(2)}) collective-permute-start(bf16[128,1152]{1,0:T(8,128)(2,1)S(1)} %finish.3.refs_2_), channel_id=1, source_target_pairs={{0,1},{1,0},{2,3},{3,2},{4,5},{5,4},{6,7},{7,6},{8,9},{9,8},{10,11... | collective-permute-start | bytes 884744 | tf_op jit(solution)/shard_map/ppermute | solution.py:672
  196.9 8.0 %collective-permute-start.24 = (bf16[128,1152]{1,0:T(8,128)(2,1)S(1)}, bf16[128,1152]{1,0:T(8,128)(2,1)S(1)}, u32[]{:S(2)}, u32[]{:S(2)}) collective-permute-start(bf16[128,1152]{1,0:T(8,128)(2,1)S(1)} %finish.2.refs_1_), channel_id=1, source_target_pairs={{0,1},{1,0},{2,3},{3,2},{4,5},{5,4},{6,7},{7,6},{8,9},{9,8},{10,11... | collective-permute-start | bytes 884744 | tf_op jit(solution)/shard_map/ppermute | solution.py:672
  196.9 8.0 %collective-permute-start.27 = (bf16[128,1152]{1,0:T(8,128)(2,1)S(1)}, bf16[128,1152]{1,0:T(8,128)(2,1)S(1)}, u32[]{:S(2)}, u32[]{:S(2)}) collective-permute-start(bf16[128,1152]{1,0:T(8,128)(2,1)S(1)} %collective-permute-done.23.refs_4_), channel_id=1, source_target_pairs={{0,1},{1,0},{2,3},{3,2},{4,5},{5,4},{6,7},{7,6},{8,9},{9,8},{10,11... | collective-permute-start | bytes 884744 | tf_op jit(solution)/shard_map/ppermute | solution.py:673
  202.0 4.1 %collective-permute-start.26 = (bf16[128,1152]{1,0:T(8,128)(2,1)S(1)}, bf16[128,1152]{1,0:T(8,128)(2,1)S(1)}, u32[]{:S(2)}, u32[]{:S(2)}) collective-permute-start(bf16[128,1152]{1,0:T(8,128)(2,1)S(1)} %collective-permute-done.22.refs_3_), channel_id=1, source_target_pairs={{0,1},{1,0},{2,3},{3,2},{4,5},{5,4},{6,7},{7,6},{8,9},{9,8},{10,11... | collective-permute-start | bytes 884744 | tf_op jit(solution)/shard_map/ppermute | solution.py:673
  (18 other events, 22.7 us)

commit v8 on v7

--- a/solution.py
+++ b/solution.py
@@ -8,7 +8,7 @@
 
 BF = jnp.bfloat16
 F32 = jnp.float32
-BLOCK = 768
+FREE = pl.CostEstimate(flops=0, bytes_accessed=0, transcendentals=0)
 RING = 4
 AWAY = (0, 3, 1, 2)
 
@@ -31,10 +31,6 @@
 
 def anywhere():
     return pl.BlockSpec(memory_space=pl.ANY)
-
-
-def cost(flops, moved):
-    return pl.CostEstimate(flops=flops, bytes_accessed=moved, transcendentals=0)
 
 
 def eq_hot(shape, dim, index):
@@ -55,7 +51,7 @@
     return (col == (row % window) * tokens + row // window).astype(BF)
 
 
-def norm_kernel(here_ref, x_ref, gain_ref, bias_ref, after_ref, lifted_ref, xw_ref, stat_ref):
+def norm_kernel(here_ref, x_ref, gain_ref, bias_ref, mine_ref, other_ref, xw_ref, stat_ref):
     window, width = gain_ref.shape
     tokens = x_ref.shape[0] // window
     full = window * width
@@ -73,14 +69,24 @@
         )
         xw_ref[w] = p.astype(BF)
     share = width // (RING * RING)
-    lifted_ref[...] = jnp.concatenate(
+    lifted = jnp.concatenate(
         [p[:, at : at + share] for at in range(0, width, share) for p in lifted], axis=1
     ).astype(BF)
+    half = pl.num_programs(0) // 2
+
+    @pl.when(pl.program_id(0) < half)
+    def _():
+        mine_ref[...] = lifted
+
+    @pl.when(pl.program_id(0) >= half)
+    def _():
+        other_ref[...] = lifted
+
     lane = lax.broadcasted_iota(jnp.int32, stat_ref.shape, 1)
     stat_ref[...] = jnp.where(lane == 0, mean, inv)
 
 
-def layer_norm(here, features, gain, bias, after):
+def layer_norm(here, features, gain, bias):
     rows, width = features.shape
     window = gain.shape[0]
     merged = rows // window
@@ -98,26 +104,27 @@
                 ),
                 pl.BlockSpec((window, width), lambda i, c: (0, 0)),
                 pl.BlockSpec((window, width), lambda i, c: (0, 0)),
-                anywhere(),
             ],
             out_specs=[
-                pl.BlockSpec((block, window * width), lambda i, c: (i, 0)),
+                pl.BlockSpec((block, window * width), lambda i, c: (jnp.minimum(i, steps // 2 - 1), 0)),
+                pl.BlockSpec((block, window * width), lambda i, c: (jnp.maximum(i - steps // 2, 0), 0)),
                 pl.BlockSpec((window, block, width), lambda i, c: (0, i, 0)),
                 pl.BlockSpec((block, 128), lambda i, c: (i, 0)),
             ],
         ),
         out_shape=[
-            shape((merged, window * width), BF),
+            shape((merged // 2, window * width), BF),
+            shape((merged // 2, window * width), BF),
             shape((window, merged, width), BF),
             shape((merged, 128), F32),
         ],
-        compiler_params=params(58),
-        cost_estimate=cost(2 * rows * block * window * width, 6 * rows * width),
+        compiler_params=params(16),
+        cost_estimate=FREE,
         name="layer_norm",
-    )(here, features, gain, bias, after)
-
-
-def collect_kernel(pos_ref, stream_ref, cot_ref, after_ref, out_ref):
+    )(here, features, gain, bias)
+
+
+def collect_kernel(pos_ref, stream_ref, cot_ref, after_ref, norm_ref, out_ref):
     slots = pos_ref.shape[0]
     rows, width = stream_ref.shape
     cut = width // 2
@@ -130,19 +137,19 @@
             ).astype(BF)
 
 
-def collect(pos, stream, cot, after):
+def collect(pos, stream, cot, *after):
     slots = pos.shape[0]
     rows, width = stream.shape
     out = shape((2, slots, width), BF)
     return pl.pallas_call(
         collect_kernel,
-        in_specs=[whole()] * 3 + [anywhere()],
+        in_specs=[whole()] * 3 + [anywhere()] * 2,
         out_specs=whole(),
         out_shape=out,
         compiler_params=params(20),
-        cost_estimate=cost(4 * slots * rows * width, 8 * rows * width),
+        cost_estimate=FREE,
         name="collect",
-    )(pos, stream, cot, after)
+    )(pos, stream, cot, *after)
 
 
 def unpack_kernel(slot_ref, came_ref, base_ref, cot_ref):
@@ -166,7 +173,7 @@
         out_specs=[whole()] * 2,
         out_shape=outs,
         compiler_params=params(12),
-        cost_estimate=cost(4 * slots * tokens * width, 8 * tokens * width),
+        cost_estimate=FREE,
         name="unpack",
     )(slot_col, came)
 
@@ -185,7 +192,7 @@
         out_specs=whole(),
         out_shape=shape((RING, rows, width), BF),
         compiler_params=params(6),
-        cost_estimate=cost(0, 16 * rows * width),
+        cost_estimate=FREE,
         name="stack",
     )(here, *blocks)
 
@@ -216,10 +223,11 @@
     visual_ref, state_ref, stat_ref, held_ref, left_ref, base_ref, cot_ref, w_sems, sems, row_sems = refs
     wait_weight = fetch(here_ref, stacks, held_ref, w_sems)
     depth = left_ref.shape[1]
-    steps = range(depth // BLOCK)
+    block = depth // RING
+    steps = range(RING)
     copies = []
     for step in steps:
-        at = pl.ds(step * BLOCK, BLOCK)
+        at = pl.ds(step * block, block)
         start = 0
         group = []
         for index, ref in enumerate(lifted):
@@ -239,13 +247,15 @@
     for copy in row_copies:
         copy.start()
     wait_weight()
-    weight = held_ref[...].reshape(depth, -1)
     total = None
     for step in steps:
-        at = slice(step * BLOCK, (step + 1) * BLOCK)
         for copy in copies[step]:
             copy.wait()
-        part = jnp.dot(left_ref[:, at], weight[at], preferred_element_type=F32)
+        part = jnp.dot(
+            left_ref[:, step * block : (step + 1) * block],
+            held_ref[step].reshape(block, -1),
+            preferred_element_type=F32,
+        )
         total = part if total is None else total + part
     for copy in row_copies:
         copy.wait()
@@ -278,11 +288,11 @@
             pltpu.VMEM((tokens, width), BF),
             pltpu.VMEM((tokens, width), BF),
             pltpu.SemaphoreType.DMA((RING,)),
-            pltpu.SemaphoreType.DMA((depth // BLOCK, len(lifted))),
+            pltpu.SemaphoreType.DMA((RING, len(lifted))),
             pltpu.SemaphoreType.DMA((2,)),
         ],
         compiler_params=params(56),
-        cost_estimate=cost(2 * depth * tokens * width, 2 * depth * width),
+        cost_estimate=FREE,
         name="merge",
     )(here, ngain, base, cot, *stacks, *lifted)
 
@@ -304,7 +314,7 @@
         out_specs=[whole()] * 2,
         out_shape=[shape(sums.shape, F32)] * 2,
         compiler_params=params(4),
-        cost_estimate=cost(sums.size, 16 * sums.size),
+        cost_estimate=FREE,
         name="add",
     )(sums, got)
 
@@ -327,12 +337,12 @@
         out_specs=[whole()] * 2,
         out_shape=[shape((slots // 2, width), BF)] * 2,
         compiler_params=params(8),
-        cost_estimate=cost(2 * slots * tokens * width, 2 * (slots + tokens) * width),
+        cost_estimate=FREE,
         name="pack",
     )(here, slot_col, visual, after)
 
 
-def braid_kernel(stay_ref, crossed_ref, after_ref, out_ref):
+def braid_kernel(stay_ref, crossed_ref, out_ref):
     count, _, rows, _ = out_ref.shape
     for c in range(count):
         at = slice(c * rows, (c + 1) * rows)
@@ -340,17 +350,17 @@
         out_ref[c, 1] = crossed_ref[at, :]
 
 
-def braid(stay, crossed, count, after):
+def braid(stay, crossed, count):
     rows, width = stay.shape
     return pl.pallas_call(
         braid_kernel,
-        in_specs=[whole()] * 2 + [anywhere()],
+        in_specs=[whole()] * 2,
         out_specs=whole(),
         out_shape=shape((count, 2, rows // count, width), BF),
         compiler_params=params(6),
-        cost_estimate=cost(0, 8 * rows * width),
+        cost_estimate=FREE,
         name="braid",
-    )(stay, crossed, after)
+    )(stay, crossed)
 
 
 def backward_kernel(full_width, chunks, here_ref, state_ref, cot_ref, ngain_ref, *refs):
@@ -381,11 +391,14 @@
                 picked_ref[to : to + rows, :] = grad[chunk * rows : (chunk + 1) * rows].astype(BF)
     depth = outs[0].shape[1]
     wait_weight()
-    weight = held_ref[...].reshape(depth, -1)
-    for begin in range(0, depth, BLOCK):
-        cols = slice(begin, begin + BLOCK)
+    block = depth // RING
+    for step in range(RING):
+        cols = slice(step * block, (step + 1) * block)
         both = lax.dot_general(
-            picked_ref[...], weight[cols], (((1,), (1,)), ((), ())), preferred_element_type=F32
+            picked_ref[...],
+            held_ref[step].reshape(block, -1),
+            (((1,), (1,)), ((), ())),
+            preferred_element_type=F32,
         )
         for chunk in range(chunks):
             own, rest, other = outs[chunk], outs[chunks + chunk], outs[2 * chunks + chunk]
@@ -417,7 +430,7 @@
             pltpu.SemaphoreType.DMA((RING,)),
         ],
         compiler_params=params(24),
-        cost_estimate=cost(2 * depth * tokens * width, 2 * depth * width),
+        cost_estimate=FREE,
         name="backward",
     )(here, state, cot, ngain, *stats, *stacks)
 
@@ -439,7 +452,7 @@
         out_specs=[whole()] * (RING - 1),
         out_shape=outs,
         compiler_params=params(8),
-        cost_estimate=cost(4 * rows * depth, 24 * rows * depth),
+        cost_estimate=FREE,
         name="pair",
     )(rest, got, after)
 
@@ -494,7 +507,7 @@
         ),
         out_shape=shape((tokens * window, width), BF),
         compiler_params=params(12),
-        cost_estimate=cost(2 * (tokens * window) ** 2 * width, 8 * window * tokens * width),
+        cost_estimate=FREE,
         name="finish",
     )(block, own, got, *came, xw, stat, gain)
 
@@ -526,7 +539,7 @@
         out_specs=whole(),
         out_shape=shape((rows, width), BF),
         compiler_params=params(12),
-        cost_estimate=cost(2 * pos.shape[0] * rows * width, 6 * rows * width),
+        cost_estimate=FREE,
         name="place",
     )(here, pos, came, stream)
 
@@ -555,7 +568,7 @@
         out_shape=shape((len(blocks) * rows, width), BF),
         scratch_shapes=[pltpu.SemaphoreType.DMA((len(blocks),))],
         compiler_params=params(4),
-        cost_estimate=cost(0, 4 * len(blocks) * rows * width),
+        cost_estimate=FREE,
         name="lay",
     )(at, *blocks)
 
@@ -621,7 +634,9 @@
     )
     asked = asked.reshape(n_img, n_ctx, capacity).transpose(1, 0, 2)
     asked = asked.reshape(slot_count, 1)
-    held = collect(asked, stream, cotangent[0], first)
+    gain = ln_gain[0]
+    lifted, lifted_other, xw, stat = layer_norm(here, features[0], gain, ln_bias[0])
+    held = collect(asked, stream, cotangent[0], first, stat)
     came = lax.all_to_all(
         held.reshape(owners, n_img * capacity, width),
         ("img", "ctx"), split_axis=0, concat_axis=0, tiled=True,
@@ -631,26 +646,25 @@
 
     stacks = [first] + [along_ctx(first, 1, by) for by in moves]
 
-    gain = ln_gain[0]
-    lifted, xw, stat = layer_norm(here, features[0], gain, ln_bias[0], held)
     pairs = []
     for i in range(n_img):
         for t in range(n_tp):
             x = (2 * (t // 2) + i + (1 if t % 2 == 0 else -1)) % RING
             pairs.append((i * n_tp + t, (x % 2) * n_tp + 2 * (x // 2) + t % 2))
-    next_mine = lax.ppermute(lifted[: merged // 2], ("img", "tp"), pairs)
+    next_mine = lax.ppermute(lifted, ("img", "tp"), pairs)
     next_other = lax.ppermute(next_mine, "tp", core_pairs)
 
     own_gain = lax.dynamic_slice_in_dim(norm_gain, img * cut, cut, axis=1)
     base, cot = unpack(paired, came)
-    visual, state, sums = merge(here, base, cot, own_gain, stacks, [lifted, next_mine, next_other])
+    visual, state, sums = merge(here, base, cot, own_gain, stacks, [lifted, lifted_other, next_mine, next_other])
 
     near, turned = add(sums, lax.ppermute(sums, "tp", core_pairs))
     stats = [near] + [along_x(near if by == 2 else turned, by) for by in (1, 2, 3)]
     stay, cross = pack(here, paired, visual, n_img * slot_count, near)
+    cross, stats = lax.optimization_barrier((cross, stats))
     crossed = lax.ppermute(cross, "img", flip)
 
-    chunks = 2
+    chunks = 1
     parts = backward(here, state, cot, own_gain, stats, stacks, chunks, full_width)
     parts, crossed = lax.optimization_barrier((parts, crossed))
     own, rest, other = (parts[i * chunks : (i + 1) * chunks] for i in range(3))
@@ -658,7 +672,7 @@
     sent = [pair(rest[c], got[c], crossed) for c in range(chunks)]
     came_back = [[along_x(sent[c][by - 1], by) for by in (1, 2, 3)] for c in range(chunks)]
 
-    send = braid(stay, crossed, n_ctx, came_back[0][0])
+    send = braid(stay, crossed, n_ctx)
     arrived = lax.all_to_all(send, "ctx", split_axis=0, concat_axis=0, tiled=True)
     new_stream = place(here, asked, arrived, stream)
 
@@ -667,6 +681,7 @@
         block = (far_half * chunks + c).reshape(1)
         out = finish(block, own[c], got[c], came_back[c], xw, stat, gain)
         beyond = lax.ppermute(out, "tp", far_pairs)
+        beyond, new_stream = lax.optimization_barrier((beyond, new_stream))
         quarters[0].append(out)
         quarters[1].append(beyond)
         quarters[2].append(lax.ppermute(out, "tp", core_pairs))

time: 212 us -> 200 us (0.943)
  starting transfers between devices: 63.3 us -> 45.2 us
  blocking collectives: 0 us -> 16.5 us
  waiting for transfers between devices: 83.9 us -> 75.8 us
  Pallas kernels: 43.3 us -> 38.7 us
  local copies, waits for them, and re-layouts: 18.6 us -> 20.8 us
    all_to_all x0 -> x1, blocking collectives: none -> 16.5 us  [shards(): lax.all_to_all(packed.reshape(owners, capacity), ('img', 'ctx'), split_ax...]
    ppermute x9 -> x6, waiting for transfers between devices: 36.5 us -> 20.6 us  [along_x(): return lax.ppermute(array, ('img', 'tp'), pairs)]
    ppermute x1, waiting for transfers between devices: 9.18 us -> 0.01 us  [shards(): next_mine = lax.ppermute(lifted, ('img', 'tp'), pairs)]
    ppermute x6, waiting for transfers between devices: 15.3 us -> 23.3 us  [along_ctx(): return lax.ppermute(array, ('ctx', 'tp'), pairs)]
    all_to_all x1 -> x0, starting transfers between devices: 6.97 us -> none  [shards(): lax.all_to_all(packed.reshape(owners, capacity), ('img', 'ctx'), split_ax...]
    all_to_all x1 -> x0, waiting for transfers between devices: 6.92 us -> none  [shards(): lax.all_to_all(packed.reshape(owners, capacity), ('img', 'ctx'), split_ax...]
    ppermute x2 -> x1, waiting for transfers between devices: 2.1 us -> 8.13 us  [shards(): beyond = lax.ppermute(out, 'tp', far_pairs)]
    unnamed x70 -> x64, local copies, waits for them, and re-layouts: 14.5 us -> 19.8 us
  transfers between devices with their start and end apart: 31 -> 23, of which waited for: 16 -> 12; matrix products, arithmetic and copies ran while one was open for 1% -> 1% of each run, Pallas kernels for 9% -> 13%
where the time goes in v8:
time: 200 us; the launch traced here: 199 us
  waiting for transfers between devices  75.8 us (38%)
  starting transfers between devices  45.2 us (23%)
  Pallas kernels  38.7 us (19%)
  local copies, waits for them, and re-layouts  20.8 us (10%)
  blocking collectives  16.5 us (8%)
    ppermute x6, waiting for transfers between devices, along_ctx(): return lax.ppermute(array, ('ctx', 'tp'), pairs)  23.3 us
    ppermute x6, waiting for transfers between devices, along_x(): return lax.ppermute(array, ('img', 'tp'), pairs)  20.6 us
    unnamed x64, local copies, waits for them, and re-layouts  19.8 us
    all_to_all x1, blocking collectives, shards(): lax.all_to_all(packed.reshape(owners, capacity), ('img', 'ctx'), split_ax...  16.5 us
    ppermute x1, waiting for transfers between devices, shards(): lax.ppermute(paired, 'img', flip)  12 us
    ppermute x6, starting transfers between devices, along_ctx(): return lax.ppermute(array, ('ctx', 'tp'), pairs)  10.1 us
    pallas_call x1, Pallas kernels, merge(): pl.pallas_call(merge_kernel, in_specs=[scalars(), whole()] + [anywhere()]...  9.35 us
    ppermute x1, waiting for transfers between devices, shards(): beyond = lax.ppermute(out, 'tp', far_pairs)  8.13 us
  transfers between devices with their start and end apart: 23, of which 12 were waited for; matrix products, arithmetic and copies ran while one was open for 1% of the time, Pallas kernels for 13%

profile of v8, /device:TPU:1, one launch (start us, length us, event | category | flops | bytes accessed | tf_op | source)
XLA Modules:
  0.0 198.5 jit_solution(11044723453728491279)
XLA Ops:
  0.7 1.0 copy-done
  1.7 2.5 %collective-permute-start.1 = (bf16[288,512]{1,0:T(8,128)(2,1)S(1)}, bf16[288,512]{1,0:T(8,128)(2,1)S(1)}, u32[]{:S(2)}, u32[]{:S(2)}) collective-permute-start(bf16[288,512]{1,0:T(8,128)(2,1)S(1)} %bitcast.22), channel_id=1, source_target_pairs={{0,4},{1,17},{2,6},{3,19},{4,8},{5,21},{6,10},{7,23},{8,12},{9,25}... | collective-permute-start | bytes 884744 | tf_op jit(solution)/shard_map/ppermute | solution.py:616
  4.3 2.2 %collective-permute-start.2 = (bf16[288,512]{1,0:T(8,128)(2,1)S(1)}, bf16[288,512]{1,0:T(8,128)(2,1)S(1)}, u32[]{:S(2)}, u32[]{:S(2)}) collective-permute-start(bf16[288,512]{1,0:T(8,128)(2,1)S(1)} %bitcast.23), channel_id=1, source_target_pairs={{0,12},{1,49},{2,14},{3,51},{4,0},{5,53},{6,2},{7,55},{8,4},{9,57}... | collective-permute-start | bytes 884744 | tf_op jit(solution)/shard_map/ppermute | solution.py:616
  6.5 1.2 collective-permute-start.3
  7.8 1.7 copy-done.9
  10.8 6.1 %layer_norm.1 = (bf16[128,4608]{1,0:T(8,128)(2,1)}, bf16[128,4608]{1,0:T(8,128)(2,1)S(1)}, bf16[4,256,1152]{2,1,0:T(8,128)(2,1)S(1)}, f32[256,128]{1,0:T(8,128)S(1)}) custom-call(s32[5]{0:T(128)S(1)} %stack.21.here_ref.refs_0_, bf16[1024,1152]{1,0:T(8,128)(2,1)S(1)} %bitcast.21, bf16[4,1152]{1,0:T(4,128)(2,1)S(1)} %bitcast.27, bf16[4,1152]{1,0:T(4,128)(2,1)S(1)} %bitcast.29), custom_call_target="tpu_custom_call" | custom-call | tf_op jit(solution)/shard_map/layer_norm/pallas_call | solution.py:95
  17.0 1.4 copy-done.10
  19.4 2.5 %collective-permute-start.7 = (bf16[128,4608]{1,0:T(8,128)(2,1)}, bf16[128,4608]{1,0:T(8,128)(2,1)}, u32[]{:S(2)}, u32[]{:S(2)}) collective-permute-start(bf16[128,4608]{1,0:T(8,128)(2,1)} %get-tuple-element.35.refs_4_), channel_id=1, source_target_pairs={{0,64},{1,67},{2,66},{3,65},{64,2},{65,1},{66,0},{67,3},{4,68},{5,... | collective-permute-start | bytes 3538952 | tf_op jit(solution)/shard_map/ppermute | solution.py:654
  22.4 16.5 %all_to_all.19 = s32[32,1,16]{2,1,0:T(1,128)S(1)} all-to-all(s32[32,1,16]{2,1,0:T(1,128)S(1)} %bitcast.32), channel_id=1, replica_groups=mesh['img'=2,'ctx'=16,'tp'=4] {'img','ctx'}, dimensions={0} | all-to-all | bytes 4096 | tf_op jit(solution)/shard_map/all_to_all | solution.py:632
  40.6 1.3 collect.1
  41.9 1.4 copy-done.3
  43.3 4.9 %all-to-all-start.1 = ((bf16[32,32,1024]{2,1,0:T(8,128)(2,1)}), bf16[32,32,1024]{2,1,0:T(8,128)(2,1)}, u32[]{:S(2)}, u32[]{:S(2)}) async-start(bf16[32,32,1024]{2,1,0:T(8,128)(2,1)} %bitcast.20), calls=%async_computation.1 | async-start | bytes 4194304 | tf_op jit(solution)/shard_map/all_to_all | solution.py:640
  48.2 1.1 collective-permute-start.4
  49.3 1.6 collective-permute-start.5
  50.9 1.3 collective-permute-start.6
  52.3 4.4 %collective-permute-start.8 = (bf16[128,4608]{1,0:T(8,128)(2,1)}, bf16[128,4608]{1,0:T(8,128)(2,1)}, u32[]{:S(2)}, u32[]{:S(2)}) collective-permute-start(bf16[128,4608]{1,0:T(8,128)(2,1)} %collective-permute-done.7.refs_6_), channel_id=1, source_target_pairs={{0,1},{1,0},{2,3},{3,2},{4,5},{5,4},{6,7},{7,6},{8,9},{9,8},{10,11... | collective-permute-start | bytes 3538952 | tf_op jit(solution)/shard_map/ppermute | solution.py:655
  56.7 1.2 collective-permute-start
  58.5 12.0 %collective-permute-done = s32[256]{0:T(256)S(1)} collective-permute-done((s32[256]{0:T(256)S(1)}, s32[256]{0:T(256)S(1)}, u32[]{:S(2)}, u32[]{:S(2)}) %collective-permute-start) | collective-permute-done | bytes 1056 | tf_op jit(solution)/shard_map/ppermute | solution.py:645
  70.7 1.9 all-to-all-done.1
  72.5 2.9 %unpack.1 = (bf16[512,512]{1,0:T(8,128)(2,1)S(1)}, bf16[512,512]{1,0:T(8,128)(2,1)S(1)}) custom-call(s32[512,1]{1,0:T(8,128)S(1)} %copy.27.slot_ref, bf16[1024,1024]{1,0:T(8,128)(2,1)} %bitcast.16.came_ref), custom_call_target="tpu_custom_call" | custom-call | tf_op jit(solution)/shard_map/unpack/pallas_call | solution.py:170
  77.0 9.8 %collective-permute-done.4.refs_1_.refs_9_ = bf16[4,288,512]{2,1,0:T(8,128)(2,1)S(1)} collective-permute-done((bf16[4,288,512]{2,1,0:T(8,128)(2,1)S(1)}, bf16[4,288,512]{2,1,0:T(8,128)(2,1)S(1)}, u32[]{:S(2)}, u32[]{:S(2)}) %collective-permute-start.4) | collective-permute-done | bytes 1179680 | tf_op jit(solution)/shard_map/ppermute | solution.py:616
  86.8 13.4 %collective-permute-done.6.refs_3_.refs_11_ = bf16[4,288,512]{2,1,0:T(8,128)(2,1)} collective-permute-done((bf16[4,288,512]{2,1,0:T(8,128)(2,1)S(1)}, bf16[4,288,512]{2,1,0:T(8,128)(2,1)}, u32[]{:S(2)}, u32[]{:S(2)}) %collective-permute-start.6) | collective-permute-done | bytes 1179680 | tf_op jit(solution)/shard_map/ppermute | solution.py:616
  100.3 9.4 %merge.1 = (bf16[512,512]{1,0:T(8,128)(2,1)}, f32[512,512]{1,0:T(8,128)}, f32[8,512]{1,0:T(8,128)}) custom-call(s32[5]{0:T(128)} %copy-done.25, bf16[1,512]{1,0:T(2,128)(2,1)} %constant_dynamic-slice_fusion.1.ngain_ref.refs_3_, bf16[512,512]{1,0:T(8,128)(2,1)} %copy-done.21, bf16[512,512]{1,0:T(8,128)(2,1)} %copy-done.12, bf16[4,288,512]{2,1,0:T(8,128)(2,1)} %copy-done.1, ...), custom_call_target="tpu_custom_call" | custom-call | tf_op jit(solution)/shard_map/merge/pallas_call | solution.py:280
  109.7 2.1 %collective-permute-start.9 = (f32[8,512]{1,0:T(8,128)}, f32[8,512]{1,0:T(8,128)S(1)}, u32[]{:S(2)}, u32[]{:S(2)}) collective-permute-start(f32[8,512]{1,0:T(8,128)} %get-tuple-element.39.sums_ref), channel_id=1, source_target_pairs={{0,1},{1,0},{2,3},{3,2},{4,5},{5,4},{6,7},{7,6},{8,9},{9,8},{10,11... | collective-permute-start | bytes 49160 | tf_op jit(solution)/shard_map/ppermute | solution.py:661
  111.8 1.0 collective-permute-done.9.got_ref
  113.6 3.7 %collective-permute-start.11 = (f32[8,512]{1,0:T(8,128)S(1)}, f32[8,512]{1,0:T(8,128)S(1)}, u32[]{:S(2)}, u32[]{:S(2)}) collective-permute-start(f32[8,512]{1,0:T(8,128)S(1)} %get-tuple-element.43.after_ref.refs_4_), channel_id=1, source_target_pairs={{0,2},{1,3},{2,0},{3,1},{64,66},{65,67},{66,64},{67,65},{4,6},{5,7... | collective-permute-start | bytes 49160 | tf_op jit(solution)/shard_map/ppermute | solution.py:604
  119.2 1.4 pack.1
  121.5 1.3 copy-done.5
  122.7 1.2 copy-done.18
  124.0 6.1 %backward.1 = (f32[64,4608]{1,0:T(8,128)S(1)}, bf16[192,4608]{1,0:T(8,128)(2,1)S(1)}, bf16[256,4608]{1,0:T(8,128)(2,1)S(1)}) custom-call(s32[5]{0:T(128)S(1)} %copy-done.26, f32[512,512]{1,0:T(8,128)S(1)} %copy-done.18, bf16[512,512]{1,0:T(8,128)(2,1)S(1)} %copy-done.13, bf16[1,512]{1,0:T(2,128)(2,1)S(1)} %copy-done.27, ...), custom_call_target="tpu_custom_call" | custom-call | tf_op jit(solution)/shard_map/backward/pallas_call | solution.py:421
  130.0 3.1 %collective-permute-done.13.after_ref.crossed_ref = bf16[512,512]{1,0:T(8,128)(2,1)S(1)} collective-permute-done((bf16[512,512]{1,0:T(8,128)(2,1)S(1)}, bf16[512,512]{1,0:T(8,128)(2,1)S(1)}, u32[]{:S(2)}, u32[]{:S(2)}) %collective-permute-start.13) | collective-permute-done | bytes 524320 | tf_op jit(solution)/shard_map/ppermute | solution.py:665
  133.1 2.1 %collective-permute-start.14 = (bf16[256,4608]{1,0:T(8,128)(2,1)S(1)}, bf16[256,4608]{1,0:T(8,128)(2,1)S(1)}, u32[]{:S(2)}, u32[]{:S(2)}) collective-permute-start(bf16[256,4608]{1,0:T(8,128)(2,1)S(1)} %get-tuple-element.52), channel_id=1, source_target_pairs={{0,1},{1,0},{2,3},{3,2},{4,5},{5,4},{6,7},{7,6},{8,9},{9,8},{10,11... | collective-permute-start | bytes 7077896 | tf_op jit(solution)/shard_map/ppermute | solution.py:671
  135.2 4.2 %collective-permute-done.14.got_ref = bf16[256,4608]{1,0:T(8,128)(2,1)S(1)} collective-permute-done((bf16[256,4608]{1,0:T(8,128)(2,1)S(1)}, bf16[256,4608]{1,0:T(8,128)(2,1)S(1)}, u32[]{:S(2)}, u32[]{:S(2)}) %collective-permute-start.14) | collective-permute-done | bytes 2359328 | tf_op jit(solution)/shard_map/ppermute | solution.py:671
  139.4 1.6 pair.1
  141.5 1.7 collective-permute-start.16
  145.0 4.5 %all-to-all-start.2 = ((bf16[16,2,32,512]{3,2,1,0:T(8,128)(2,1)}), bf16[16,2,32,512]{3,2,1,0:T(8,128)(2,1)}, u32[]{:S(2)}, u32[]{:S(2)}) async-start(bf16[16,2,32,512]{3,2,1,0:T(8,128)(2,1)} %copy-done.6), calls=%async_computation.2 | async-start | bytes 2097152 | tf_op jit(solution)/shard_map/all_to_all | solution.py:676
  149.5 8.0 %collective-permute-done.15.refs_0_ = bf16[64,4608]{1,0:T(8,128)(2,1)} collective-permute-done((bf16[64,4608]{1,0:T(8,128)(2,1)}, bf16[64,4608]{1,0:T(8,128)(2,1)}, u32[]{:S(2)}, u32[]{:S(2)}) %collective-permute-start.15) | collective-permute-done | bytes 589856 | tf_op jit(solution)/shard_map/ppermute | solution.py:604
  157.5 11.8 %collective-permute-done.16.refs_1_ = bf16[64,4608]{1,0:T(8,128)(2,1)} collective-permute-done((bf16[64,4608]{1,0:T(8,128)(2,1)}, bf16[64,4608]{1,0:T(8,128)(2,1)}, u32[]{:S(2)}, u32[]{:S(2)}) %collective-permute-start.16) | collective-permute-done | bytes 589856 | tf_op jit(solution)/shard_map/ppermute | solution.py:604
  170.0 1.7 copy-done.11
  171.7 1.3 copy-done.16
  173.0 3.8 %finish.1.refs_1_ = bf16[256,1152]{1,0:T(8,128)(2,1)} custom-call(s32[1]{0:T(128)} %bitcast.block_ref, f32[64,4608]{1,0:T(8,128)S(1)} %copy-done.16, bf16[256,4608]{1,0:T(8,128)(2,1)S(1)} %collective-permute-done.14.got_ref, bf16[64,4608]{1,0:T(8,128)(2,1)} %collective-permute-done.15.refs_0_, bf16[64,4608]{1,0:T(8,128)(2,1)} %collective-permute-done.16.refs_1_, ...), custom_call_target="tpu_custom_call" | custom-call | tf_op jit(solution)/shard_map/finish/pallas_call | solution.py:495
  177.7 1.2 copy-done.8
  178.9 3.1 %place.1 = bf16[512,1024]{1,0:T(8,128)(2,1)} custom-call(s32[5]{0:T(128)S(1)} %copy-done.26, s32[512,1]{1,0:T(8,128)S(1)} %reshape.43.pos_ref, bf16[16,2,32,512]{3,2,1,0:T(8,128)(2,1)} %all-to-all-done.2.came_ref, bf16[512,1024]{1,0:T(8,128)(2,1)S(1)} %copy-done.8), custom_call_target="tpu_custom_call" | custom-call | tf_op jit(solution)/shard_map/place/pallas_call | solution.py:536
  182.0 1.7 collective-permute-start.19
  183.7 8.1 %collective-permute-done.18.refs_2_ = bf16[256,1152]{1,0:T(8,128)(2,1)S(1)} collective-permute-done((bf16[256,1152]{1,0:T(8,128)(2,1)}, bf16[256,1152]{1,0:T(8,128)(2,1)S(1)}, u32[]{:S(2)}, u32[]{:S(2)}) %collective-permute-start.18) | collective-permute-done | bytes 589856 | tf_op jit(solution)/shard_map/ppermute | solution.py:683
  191.8 2.4 %collective-permute-start.20 = (bf16[256,1152]{1,0:T(8,128)(2,1)S(1)}, bf16[256,1152]{1,0:T(8,128)(2,1)S(1)}, u32[]{:S(2)}, u32[]{:S(2)}) collective-permute-start(bf16[256,1152]{1,0:T(8,128)(2,1)S(1)} %collective-permute-done.18.refs_2_), channel_id=1, source_target_pairs={{0,1},{1,0},{2,3},{3,2},{4,5},{5,4},{6,7},{7,6},{8,9},{9,8},{10,11... | collective-permute-start | bytes 1769480 | tf_op jit(solution)/shard_map/ppermute | solution.py:688
  194.2 1.6 collective-permute-done.20.refs_4_
  195.8 2.5 %lay.1 = bf16[1024,1152]{1,0:T(8,128)(2,1)} custom-call(s32[5]{0:T(128)S(1)} %copy-done.26, bf16[256,1152]{1,0:T(8,128)(2,1)} %finish.1.refs_1_, bf16[256,1152]{1,0:T(8,128)(2,1)S(1)} %collective-permute-done.18.refs_2_, bf16[256,1152]{1,0:T(8,128)(2,1)S(1)} %collective-permute-done.19.refs_3_, bf16[256,1152]{1,0:T(8,128)(2,1)S(1)} %collective-permute-done.20.refs_4_), custom_call_target="tpu_custom_call" | custom-call | tf_op jit(solution)/shard_map/lay/pallas_call | solution.py:564
  (89 shorter events, 14.6 us)
Async XLA Ops:
  0.6 1.1 copy-start
  1.7 37.3 %collective-permute-start.1 = (bf16[288,512]{1,0:T(8,128)(2,1)S(1)}, bf16[288,512]{1,0:T(8,128)(2,1)S(1)}, u32[]{:S(2)}, u32[]{:S(2)}) collective-permute-start(bf16[288,512]{1,0:T(8,128)(2,1)S(1)} %bitcast.22), channel_id=1, source_target_pairs={{0,4},{1,17},{2,6},{3,19},{4,8},{5,21},{6,10},{7,23},{8,12},{9,25}... | collective-permute-start | bytes 884744 | tf_op jit(solution)/shard_map/ppermute | solution.py:616
  4.3 34.8 %collective-permute-start.2 = (bf16[288,512]{1,0:T(8,128)(2,1)S(1)}, bf16[288,512]{1,0:T(8,128)(2,1)S(1)}, u32[]{:S(2)}, u32[]{:S(2)}) collective-permute-start(bf16[288,512]{1,0:T(8,128)(2,1)S(1)} %bitcast.23), channel_id=1, source_target_pairs={{0,12},{1,49},{2,14},{3,51},{4,0},{5,53},{6,2},{7,55},{8,4},{9,57}... | collective-permute-start | bytes 884744 | tf_op jit(solution)/shard_map/ppermute | solution.py:616
  6.5 32.6 %collective-permute-start.3 = (bf16[288,512]{1,0:T(8,128)(2,1)S(1)}, bf16[288,512]{1,0:T(8,128)(2,1)S(1)}, u32[]{:S(2)}, u32[]{:S(2)}) collective-permute-start(bf16[288,512]{1,0:T(8,128)(2,1)S(1)} %bitcast.24), channel_id=1, source_target_pairs={{0,8},{1,33},{2,10},{3,35},{4,12},{5,37},{6,14},{7,39},{8,0},{9,41... | collective-permute-start | bytes 884744 | tf_op jit(solution)/shard_map/ppermute | solution.py:616
  7.8 31.3 %copy-start.25 = (s32[5]{0:T(128)}, s32[5]{0:T(128)S(1)}, u32[]{:S(2)}) copy-start(s32[5]{0:T(128)S(1)} %stack.21.here_ref.refs_0_) | copy-start | bytes 64
  7.8 1.7 copy-start.9
  10.8 11.1 %copy-start.30 = (s32[256]{0:T(256)S(1)}, s32[256]{0:T(256)}, u32[]{:S(2)}) copy-start(s32[256]{0:T(256)} %param.15) | copy-start | bytes 3076
  17.0 1.4 copy-start.10
  19.4 20.3 %copy-start.19 = (f32[256,128]{1,0:T(8,128)}, f32[256,128]{1,0:T(8,128)S(1)}, u32[]{:S(2)}) copy-start(f32[256,128]{1,0:T(8,128)S(1)} %get-tuple-element.32.norm_ref.refs_4_) | copy-start | bytes 393220
  19.4 32.9 %collective-permute-start.7 = (bf16[128,4608]{1,0:T(8,128)(2,1)}, bf16[128,4608]{1,0:T(8,128)(2,1)}, u32[]{:S(2)}, u32[]{:S(2)}) collective-permute-start(bf16[128,4608]{1,0:T(8,128)(2,1)} %get-tuple-element.35.refs_4_), channel_id=1, source_target_pairs={{0,64},{1,67},{2,66},{3,65},{64,2},{65,1},{66,0},{67,3},{4,68},{5,... | collective-permute-start | bytes 3538952 | tf_op jit(solution)/shard_map/ppermute | solution.py:654
  39.0 1.2 copy-start.7
  39.0 1.5 copy-start.17
  39.7 11.2 %copy-start.1 = (bf16[4,288,512]{2,1,0:T(8,128)(2,1)}, bf16[4,288,512]{2,1,0:T(8,128)(2,1)S(1)}, u32[]{:S(2)}) copy-start(bf16[4,288,512]{2,1,0:T(8,128)(2,1)S(1)} %stack.22.after_ref.refs_0_.refs_8_) | copy-start | bytes 3538948
  41.9 1.4 copy-start.3
  43.3 14.7 %copy-start.31 = (bf16[1,1024]{1,0:T(2,128)(2,1)S(1)}, bf16[1,1024]{1,0:T(2,128)(2,1)}, u32[]{:S(2)}) copy-start(bf16[1,1024]{1,0:T(2,128)(2,1)} %param.13) | copy-start | bytes 6148
  43.3 29.3 %all-to-all-start.1 = ((bf16[32,32,1024]{2,1,0:T(8,128)(2,1)}), bf16[32,32,1024]{2,1,0:T(8,128)(2,1)}, u32[]{:S(2)}, u32[]{:S(2)}) async-start(bf16[32,32,1024]{2,1,0:T(8,128)(2,1)} %bitcast.20), calls=%async_computation.1 | async-start | bytes 4194304 | tf_op jit(solution)/shard_map/all_to_all | solution.py:640
  48.2 38.7 %collective-permute-start.4 = (bf16[4,288,512]{2,1,0:T(8,128)(2,1)S(1)}, bf16[4,288,512]{2,1,0:T(8,128)(2,1)S(1)}, u32[]{:S(2)}, u32[]{:S(2)}) collective-permute-start(bf16[4,288,512]{2,1,0:T(8,128)(2,1)S(1)} %stack.22.after_ref.refs_0_.refs_8_), channel_id=1, source_target_pairs={{0,16},{1,5},{2,18},{3,7},{4,20},{5,9},{6,22},{7,11},{8,24},{9,13}... | collective-permute-start | bytes 3538952 | tf_op jit(solution)/shard_map/ppermute | solution.py:616
  49.3 37.6 %collective-permute-start.5 = (bf16[4,288,512]{2,1,0:T(8,128)(2,1)S(1)}, bf16[4,288,512]{2,1,0:T(8,128)(2,1)}, u32[]{:S(2)}, u32[]{:S(2)}) collective-permute-start(bf16[4,288,512]{2,1,0:T(8,128)(2,1)S(1)} %stack.22.after_ref.refs_0_.refs_8_), channel_id=1, source_target_pairs={{0,48},{1,13},{2,50},{3,15},{4,52},{5,1},{6,54},{7,3},{8,56},{9,5}... | collective-permute-start | bytes 3538952 | tf_op jit(solution)/shard_map/ppermute | solution.py:616
  50.9 49.3 %collective-permute-start.6 = (bf16[4,288,512]{2,1,0:T(8,128)(2,1)S(1)}, bf16[4,288,512]{2,1,0:T(8,128)(2,1)}, u32[]{:S(2)}, u32[]{:S(2)}) collective-permute-start(bf16[4,288,512]{2,1,0:T(8,128)(2,1)S(1)} %stack.22.after_ref.refs_0_.refs_8_), channel_id=1, source_target_pairs={{0,32},{1,9},{2,34},{3,11},{4,36},{5,13},{6,38},{7,15},{8,40},{9,1... | collective-permute-start | bytes 3538952 | tf_op jit(solution)/shard_map/ppermute | solution.py:616
  52.3 48.0 %collective-permute-start.8 = (bf16[128,4608]{1,0:T(8,128)(2,1)}, bf16[128,4608]{1,0:T(8,128)(2,1)}, u32[]{:S(2)}, u32[]{:S(2)}) collective-permute-start(bf16[128,4608]{1,0:T(8,128)(2,1)} %collective-permute-done.7.refs_6_), channel_id=1, source_target_pairs={{0,1},{1,0},{2,3},{3,2},{4,5},{5,4},{6,7},{7,6},{8,9},{9,8},{10,11... | collective-permute-start | bytes 3538952 | tf_op jit(solution)/shard_map/ppermute | solution.py:655
  56.7 13.8 %collective-permute-start = (s32[256]{0:T(256)S(1)}, s32[256]{0:T(256)S(1)}, u32[]{:S(2)}, u32[]{:S(2)}) collective-permute-start(s32[256]{0:T(256)S(1)} %get-tuple-element.65), channel_id=1, source_target_pairs={{0,64},{64,0},{1,65},{65,1},{2,66},{66,2},{3,67},{67,3},{4,68},{68... | collective-permute-start | bytes 3080 | tf_op jit(solution)/shard_map/ppermute | solution.py:645
  86.8 13.4 %copy-start.4 = (bf16[4,288,512]{2,1,0:T(8,128)(2,1)}, bf16[4,288,512]{2,1,0:T(8,128)(2,1)S(1)}, u32[]{:S(2)}) copy-start(bf16[4,288,512]{2,1,0:T(8,128)(2,1)S(1)} %collective-permute-done.4.refs_1_.refs_9_) | copy-start | bytes 3538948
  100.3 17.9 %copy-start.26 = (s32[5]{0:T(128)S(1)}, s32[5]{0:T(128)}, u32[]{:S(2)}) copy-start(s32[5]{0:T(128)} %copy-done.25) | copy-start | bytes 64
  100.3 21.2 %copy-start.2 = (bf16[4,288,512]{2,1,0:T(8,128)(2,1)S(1)}, bf16[4,288,512]{2,1,0:T(8,128)(2,1)}, u32[]{:S(2)}) copy-start(bf16[4,288,512]{2,1,0:T(8,128)(2,1)} %copy-done.1) | copy-start | bytes 3538948
  100.3 21.2 %copy-start.27 = (bf16[1,512]{1,0:T(2,128)(2,1)S(1)}, bf16[1,512]{1,0:T(2,128)(2,1)}, u32[]{:S(2)}) copy-start(bf16[1,512]{1,0:T(2,128)(2,1)} %constant_dynamic-slice_fusion.1.ngain_ref.refs_3_) | copy-start | bytes 3076
  109.7 11.8 %copy-start.13 = (bf16[512,512]{1,0:T(8,128)(2,1)S(1)}, bf16[512,512]{1,0:T(8,128)(2,1)}, u32[]{:S(2)}) copy-start(bf16[512,512]{1,0:T(8,128)(2,1)} %copy-done.12) | copy-start | bytes 1572868
  109.7 3.1 %collective-permute-start.9 = (f32[8,512]{1,0:T(8,128)}, f32[8,512]{1,0:T(8,128)S(1)}, u32[]{:S(2)}, u32[]{:S(2)}) collective-permute-start(f32[8,512]{1,0:T(8,128)} %get-tuple-element.39.sums_ref), channel_id=1, source_target_pairs={{0,1},{1,0},{2,3},{3,2},{4,5},{5,4},{6,7},{7,6},{8,9},{9,8},{10,11... | collective-permute-start | bytes 49160 | tf_op jit(solution)/shard_map/ppermute | solution.py:661
  113.5 7.1 %collective-permute-start.10 = (f32[8,512]{1,0:T(8,128)S(1)}, f32[8,512]{1,0:T(8,128)S(1)}, u32[]{:S(2)}, u32[]{:S(2)}) collective-permute-start(f32[8,512]{1,0:T(8,128)S(1)} %get-tuple-element.42), channel_id=1, source_target_pairs={{0,64},{1,65},{2,66},{3,67},{64,2},{65,3},{66,0},{67,1},{4,68},{5,... | collective-permute-start | bytes 49160 | tf_op jit(solution)/shard_map/ppermute | solution.py:604
  113.6 7.0 %collective-permute-start.11 = (f32[8,512]{1,0:T(8,128)S(1)}, f32[8,512]{1,0:T(8,128)S(1)}, u32[]{:S(2)}, u32[]{:S(2)}) collective-permute-start(f32[8,512]{1,0:T(8,128)S(1)} %get-tuple-element.43.after_ref.refs_4_), channel_id=1, source_target_pairs={{0,2},{1,3},{2,0},{3,1},{64,66},{65,67},{66,64},{67,65},{4,6},{5,7... | collective-permute-start | bytes 49160 | tf_op jit(solution)/shard_map/ppermute | solution.py:604
  117.3 3.4 %collective-permute-start.12 = (f32[8,512]{1,0:T(8,128)S(1)}, f32[8,512]{1,0:T(8,128)S(1)}, u32[]{:S(2)}, u32[]{:S(2)}) collective-permute-start(f32[8,512]{1,0:T(8,128)S(1)} %get-tuple-element.42), channel_id=1, source_target_pairs={{0,66},{1,67},{2,64},{3,65},{64,0},{65,1},{66,2},{67,3},{4,70},{5,... | collective-permute-start | bytes 49160 | tf_op jit(solution)/shard_map/ppermute | solution.py:604
  118.2 1.0 copy-start.22
  120.6 12.5 %collective-permute-start.13 = (bf16[512,512]{1,0:T(8,128)(2,1)S(1)}, bf16[512,512]{1,0:T(8,128)(2,1)S(1)}, u32[]{:S(2)}, u32[]{:S(2)}) collective-permute-start(bf16[512,512]{1,0:T(8,128)(2,1)S(1)} %get-tuple-element.50), channel_id=1, source_target_pairs={{0,64},{64,0},{1,65},{65,1},{2,66},{66,2},{3,67},{67,3},{4,68},{68... | collective-permute-start | bytes 1572872 | tf_op jit(solution)/shard_map/ppermute | solution.py:665
  121.5 1.3 copy-start.5
  122.7 1.2 copy-start.18
  130.0 10.9 %copy-start.15 = (f32[64,4608]{1,0:T(8,128)}, f32[64,4608]{1,0:T(8,128)S(1)}, u32[]{:S(2)}) copy-start(f32[64,4608]{1,0:T(8,128)S(1)} %get-tuple-element.51.own_ref) | copy-start | bytes 3538948
  133.1 6.3 %collective-permute-start.14 = (bf16[256,4608]{1,0:T(8,128)(2,1)S(1)}, bf16[256,4608]{1,0:T(8,128)(2,1)S(1)}, u32[]{:S(2)}, u32[]{:S(2)}) collective-permute-start(bf16[256,4608]{1,0:T(8,128)(2,1)S(1)} %get-tuple-element.52), channel_id=1, source_target_pairs={{0,1},{1,0},{2,3},{3,2},{4,5},{5,4},{6,7},{7,6},{8,9},{9,8},{10,11... | collective-permute-start | bytes 7077896 | tf_op jit(solution)/shard_map/ppermute | solution.py:671
  141.0 16.5 %collective-permute-start.15 = (bf16[64,4608]{1,0:T(8,128)(2,1)}, bf16[64,4608]{1,0:T(8,128)(2,1)}, u32[]{:S(2)}, u32[]{:S(2)}) collective-permute-start(bf16[64,4608]{1,0:T(8,128)(2,1)} %get-tuple-element.55), channel_id=1, source_target_pairs={{0,64},{1,65},{2,66},{3,67},{64,2},{65,3},{66,0},{67,1},{4,68},{5,... | collective-permute-start | bytes 1769480 | tf_op jit(solution)/shard_map/ppermute | solution.py:604
  141.5 27.8 %collective-permute-start.16 = (bf16[64,4608]{1,0:T(8,128)(2,1)}, bf16[64,4608]{1,0:T(8,128)(2,1)}, u32[]{:S(2)}, u32[]{:S(2)}) collective-permute-start(bf16[64,4608]{1,0:T(8,128)(2,1)} %get-tuple-element.56), channel_id=1, source_target_pairs={{0,2},{1,3},{2,0},{3,1},{64,66},{65,67},{66,64},{67,65},{4,6},{5,7... | collective-permute-start | bytes 1769480 | tf_op jit(solution)/shard_map/ppermute | solution.py:604
  143.2 26.8 %collective-permute-start.17 = (bf16[64,4608]{1,0:T(8,128)(2,1)}, bf16[64,4608]{1,0:T(8,128)(2,1)}, u32[]{:S(2)}, u32[]{:S(2)}) collective-permute-start(bf16[64,4608]{1,0:T(8,128)(2,1)} %get-tuple-element.57), channel_id=1, source_target_pairs={{0,66},{1,67},{2,64},{3,65},{64,0},{65,1},{66,2},{67,3},{4,70},{5,... | collective-permute-start | bytes 1769480 | tf_op jit(solution)/shard_map/ppermute | solution.py:604
  145.0 25.1 %copy-start.20 = (f32[256,128]{1,0:T(8,128)S(1)}, f32[256,128]{1,0:T(8,128)}, u32[]{:S(2)}) copy-start(f32[256,128]{1,0:T(8,128)} %copy-done.19) | copy-start | bytes 393220
  145.0 25.1 %copy-start.24 = (bf16[1,4,1152]{2,1,0:T(4,128)(2,1)S(1)}, bf16[1,4,1152]{2,1,0:T(4,128)(2,1)}, u32[]{:S(2)}) copy-start(bf16[1,4,1152]{2,1,0:T(4,128)(2,1)} %param.9) | copy-start | bytes 27652
  145.0 32.7 %all-to-all-start.2 = ((bf16[16,2,32,512]{3,2,1,0:T(8,128)(2,1)}), bf16[16,2,32,512]{3,2,1,0:T(8,128)(2,1)}, u32[]{:S(2)}, u32[]{:S(2)}) async-start(bf16[16,2,32,512]{3,2,1,0:T(8,128)(2,1)} %copy-done.6), calls=%async_computation.2 | async-start | bytes 2097152 | tf_op jit(solution)/shard_map/all_to_all | solution.py:676
  170.0 1.7 copy-start.11
  171.7 1.3 copy-start.16
  176.7 15.1 %collective-permute-start.18 = (bf16[256,1152]{1,0:T(8,128)(2,1)}, bf16[256,1152]{1,0:T(8,128)(2,1)S(1)}, u32[]{:S(2)}, u32[]{:S(2)}) collective-permute-start(bf16[256,1152]{1,0:T(8,128)(2,1)} %finish.1.refs_1_), channel_id=1, source_target_pairs={{0,2},{1,3},{2,0},{3,1},{4,6},{5,7},{6,4},{7,5},{8,10},{9,11},{10,... | collective-permute-start | bytes 1769480 | tf_op jit(solution)/shard_map/ppermute | solution.py:683
  177.7 1.2 copy-start.8
  182.0 12.2 %collective-permute-start.19 = (bf16[256,1152]{1,0:T(8,128)(2,1)}, bf16[256,1152]{1,0:T(8,128)(2,1)S(1)}, u32[]{:S(2)}, u32[]{:S(2)}) collective-permute-start(bf16[256,1152]{1,0:T(8,128)(2,1)} %finish.1.refs_1_), channel_id=1, source_target_pairs={{0,1},{1,0},{2,3},{3,2},{4,5},{5,4},{6,7},{7,6},{8,9},{9,8},{10,11... | collective-permute-start | bytes 1769480 | tf_op jit(solution)/shard_map/ppermute | solution.py:687
  191.8 4.0 %collective-permute-start.20 = (bf16[256,1152]{1,0:T(8,128)(2,1)S(1)}, bf16[256,1152]{1,0:T(8,128)(2,1)S(1)}, u32[]{:S(2)}, u32[]{:S(2)}) collective-permute-start(bf16[256,1152]{1,0:T(8,128)(2,1)S(1)} %collective-permute-done.18.refs_2_), channel_id=1, source_target_pairs={{0,1},{1,0},{2,3},{3,2},{4,5},{5,4},{6,7},{7,6},{8,9},{9,8},{10,11... | collective-permute-start | bytes 1769480 | tf_op jit(solution)/shard_map/ppermute | solution.py:688
  (7 other events, 5.7 us)

commit v9 on v8

--- a/solution.py
+++ b/solution.py
@@ -124,7 +124,7 @@
     )(here, features, gain, bias)
 
 
-def collect_kernel(pos_ref, stream_ref, cot_ref, after_ref, norm_ref, out_ref):
+def collect_kernel(pos_ref, stream_ref, cot_ref, after_ref, out_ref):
     slots = pos_ref.shape[0]
     rows, width = stream_ref.shape
     cut = width // 2
@@ -137,19 +137,19 @@
             ).astype(BF)
 
 
-def collect(pos, stream, cot, *after):
+def collect(pos, stream, cot, after):
     slots = pos.shape[0]
     rows, width = stream.shape
     out = shape((2, slots, width), BF)
     return pl.pallas_call(
         collect_kernel,
-        in_specs=[whole()] * 3 + [anywhere()] * 2,
+        in_specs=[whole()] * 3 + [anywhere()],
         out_specs=whole(),
         out_shape=out,
         compiler_params=params(20),
         cost_estimate=FREE,
         name="collect",
-    )(pos, stream, cot, *after)
+    )(pos, stream, cot, after)
 
 
 def unpack_kernel(slot_ref, came_ref, base_ref, cot_ref):
@@ -363,33 +363,41 @@
     )(stay, crossed)
 
 
-def backward_kernel(full_width, chunks, here_ref, state_ref, cot_ref, ngain_ref, *refs):
+def backward_kernel(full_width, here_ref, ngain_ref, *refs):
     stats, stacks, refs = refs[:RING], refs[RING : 2 * RING], refs[2 * RING :]
-    outs, (picked_ref, sums_ref, held_ref, sems) = refs[: 3 * chunks], refs[3 * chunks :]
+    state_hbm, cot_hbm, own_ref, other_ref = refs[:4]
+    picked_ref, sums_ref, state_ref, cot_ref, held_ref, row_sems, sems = refs[4:]
+    row_copies = [
+        pltpu.make_async_copy(a, b, row_sems.at[i])
+        for i, (a, b) in enumerate(((state_hbm, state_ref), (cot_hbm, cot_ref)))
+    ]
+    for copy in row_copies:
+        copy.start()
     wait_weight = fetch(here_ref, stacks, held_ref, sems)
     tokens = state_ref.shape[0]
-    rows = tokens // 2 // RING // chunks
+    rows = tokens // 2 // RING
     total = stats[0][...]
     for ref in stats[1:]:
         total = total + ref[...]
     sums_ref[...] = total.T
     far, img = here_ref[1], here_ref[2]
     gain = ngain_ref[...].astype(F32)
+    for copy in row_copies:
+        copy.wait()
     for core in range(2):
         for away in range(RING):
             there = lax.rem(2 * far + img + away, RING)
             partner = lax.rem(there + img, 2)
             begin = partner * (tokens // 2) + core * (tokens // 4) + (there // 2) * (tokens // 8)
-            at = pl.ds(pl.multiple_of(begin, tokens // 8), tokens // 8)
+            at = pl.ds(pl.multiple_of(begin, rows), rows)
             sums = sums_ref[at, :]
             inv = lax.rsqrt(sums[:, 0:1] / full_width + 1e-06)
             inner = sums[:, 1:2] / full_width
             up = gain * cot_ref[at, :].astype(F32)
             grad = inv * up - state_ref[at, :] * (inv * inv * inv * inner)
-            for chunk in range(chunks):
-                to = ((core * chunks + chunk) * RING + away) * rows
-                picked_ref[to : to + rows, :] = grad[chunk * rows : (chunk + 1) * rows].astype(BF)
-    depth = outs[0].shape[1]
+            to = (core * RING + away) * rows
+            picked_ref[to : to + rows, :] = grad.astype(BF)
+    depth = own_ref.shape[1]
     wait_weight()
     block = depth // RING
     for step in range(RING):
@@ -400,50 +408,41 @@
             (((1,), (1,)), ((), ())),
             preferred_element_type=F32,
         )
-        for chunk in range(chunks):
-            own, rest, other = outs[chunk], outs[chunks + chunk], outs[2 * chunks + chunk]
-            start = chunk * RING * rows
-            own[:, cols] = both[start : start + rows]
-            rest[:, cols] = both[start + rows : start + RING * rows].astype(BF)
-            start += tokens // 2
-            other[:, cols] = both[start : start + RING * rows].astype(BF)
-
-
-def backward(here, state, cot, ngain, stats, stacks, chunks, full_width):
+        own_ref[:, cols] = both[: tokens // 2].astype(BF)
+        other_ref[:, cols] = both[tokens // 2 :].astype(BF)
+
+
+def backward(here, state, cot, ngain, stats, stacks, full_width):
     tokens, width = state.shape
     depth = RING * stacks[0].shape[0] * stacks[0].shape[1]
-    rows = tokens // 2 // RING // chunks
-    outs = (
-        [shape((rows, depth), F32)] * chunks
-        + [shape(((RING - 1) * rows, depth), BF)] * chunks
-        + [shape((RING * rows, depth), BF)] * chunks
-    )
-    return pl.pallas_call(
-        lambda *refs: backward_kernel(full_width, chunks, *refs),
-        in_specs=[scalars()] + [whole()] * (3 + RING) + [anywhere()] * RING,
-        out_specs=[whole()] * len(outs),
-        out_shape=outs,
+    return pl.pallas_call(
+        lambda *refs: backward_kernel(full_width, *refs),
+        in_specs=[scalars()] + [whole()] * (1 + RING) + [anywhere()] * (RING + 2),
+        out_specs=[whole()] * 2,
+        out_shape=[shape((tokens // 2, depth), BF)] * 2,
         scratch_shapes=[
             pltpu.VMEM((tokens, width), BF),
             pltpu.VMEM((tokens, 8), F32),
+            pltpu.VMEM((tokens, width), F32),
+            pltpu.VMEM((tokens, width), BF),
             pltpu.VMEM((RING,) + stacks[0].shape, BF),
+            pltpu.SemaphoreType.DMA((2,)),
             pltpu.SemaphoreType.DMA((RING,)),
         ],
-        compiler_params=params(24),
+        compiler_params=params(50),
         cost_estimate=FREE,
         name="backward",
-    )(here, state, cot, ngain, *stats, *stacks)
-
-
-def pair_kernel(rest_ref, got_ref, after_ref, *outs):
+    )(here, ngain, *stats, *stacks, state, cot)
+
+
+def pair_kernel(own_ref, got_ref, after_ref, *outs):
     rows = outs[0].shape[0]
     for away, out in enumerate(outs):
-        at = slice(away * rows, (away + 1) * rows)
-        got = slice((away + 1) * rows, (away + 2) * rows)
-        out[...] = (rest_ref[at, :].astype(F32) + got_ref[got, :].astype(F32)).astype(BF)
-
-
-def pair(rest, got, after):
+        at = slice((away + 1) * rows, (away + 2) * rows)
+        out[...] = (own_ref[at, :].astype(F32) + got_ref[at, :].astype(F32)).astype(BF)
+
+
+def pair(own, got, after):
     rows, depth = got.shape[0] // RING, got.shape[1]
     outs = [shape((rows, depth), BF)] * (RING - 1)
     return pl.pallas_call(
@@ -454,16 +453,16 @@
         compiler_params=params(8),
         cost_estimate=FREE,
         name="pair",
-    )(rest, got, after)
-
-
-def finish_kernel(block_ref, own_ref, got_ref, *refs):
+    )(own, got, after)
+
+
+def finish_kernel(here_ref, own_ref, got_ref, *refs):
     came, (xw_ref, stat_ref, gain_ref, out_ref) = refs[: RING - 1], refs[RING - 1 :]
     window, tokens, width = xw_ref.shape
     full = window * width
     mean = stat_ref[:, 0:1]
     inv = stat_ref[:, 1:2]
-    lifted = own_ref[...] + got_ref[...].astype(F32)
+    lifted = own_ref[...].astype(F32) + got_ref[...].astype(F32)
     for ref in came:
         lifted = lifted + ref[...].astype(F32)
     share = width // (RING * RING)
@@ -488,28 +487,30 @@
     ).astype(BF)
 
 
-def finish(block, own, got, came, xw, stat, gain):
-    tokens, depth = own.shape
+def finish(here, own, got, came, xw, stat, gain):
+    rows, depth = came[0].shape
     window, width = gain.shape
-    same = pl.BlockSpec((tokens, depth), lambda i, b: (0, 0))
+    steps = 2
+    tokens = rows // steps
+    same = pl.BlockSpec((tokens, depth), lambda i, h: (i, 0))
     return pl.pallas_call(
         finish_kernel,
         grid_spec=pltpu.PrefetchScalarGridSpec(
             num_scalar_prefetch=1,
-            grid=(1,),
+            grid=(steps,),
             in_specs=[same] * (1 + RING)
             + [
-                pl.BlockSpec((window, tokens, width), lambda i, b: (0, b[0], 0)),
-                pl.BlockSpec((tokens, 128), lambda i, b: (b[0], 0)),
-                pl.BlockSpec((window, width), lambda i, b: (0, 0)),
+                pl.BlockSpec((window, tokens, width), lambda i, h: (0, h[1] * steps + i, 0)),
+                pl.BlockSpec((tokens, 128), lambda i, h: (h[1] * steps + i, 0)),
+                pl.BlockSpec((window, width), lambda i, h: (0, 0)),
             ],
-            out_specs=pl.BlockSpec((tokens * window, width), lambda i, b: (0, 0)),
+            out_specs=pl.BlockSpec((tokens * window, width), lambda i, h: (i, 0)),
         ),
-        out_shape=shape((tokens * window, width), BF),
-        compiler_params=params(12),
+        out_shape=shape((rows * window, width), BF),
+        compiler_params=params(58),
         cost_estimate=FREE,
         name="finish",
-    )(block, own, got, *came, xw, stat, gain)
+    )(here, own, got, *came, xw, stat, gain)
 
 
 def place_kernel(here_ref, pos_ref, came_ref, stream_ref, out_ref):
@@ -544,14 +545,13 @@
     )(here, pos, came, stream)
 
 
-def lay_kernel(chunks, at_ref, *refs):
+def lay_kernel(here_ref, *refs):
     blocks, (out_ref, sems) = refs[:-2], refs[-2:]
     rows = blocks[0].shape[0]
     copies = []
     for index, ref in enumerate(blocks):
-        quarter, chunk = index // chunks, index % chunks
-        owner = 2 * (at_ref[0] ^ (quarter // 2)) + (at_ref[1] ^ (quarter % 2))
-        start = pl.multiple_of((owner * chunks + chunk) * rows, rows)
+        owner = 2 * (here_ref[0] ^ (index // 2)) + (here_ref[1] ^ (index % 2))
+        start = pl.multiple_of(owner * rows, rows)
         copies.append(pltpu.make_async_copy(ref, out_ref.at[pl.ds(start, rows)], sems.at[index]))
     for copy in copies:
         copy.start()
@@ -559,10 +559,10 @@
         copy.wait()
 
 
-def lay(at, blocks, chunks):
+def lay(here, blocks):
     rows, width = blocks[0].shape
     return pl.pallas_call(
-        lambda *refs: lay_kernel(chunks, *refs),
+        lay_kernel,
         in_specs=[scalars()] + [whole()] * len(blocks),
         out_specs=anywhere(),
         out_shape=shape((len(blocks) * rows, width), BF),
@@ -570,7 +570,7 @@
         compiler_params=params(4),
         cost_estimate=FREE,
         name="lay",
-    )(at, *blocks)
+    )(here, *blocks)
 
 
 def shards(features, ln_gain, ln_bias, projection, stream, norm_gain, cotangent, slots):
@@ -614,10 +614,6 @@
                     z = (z + by) % RING
                 pairs.append((c * n_tp + t, (z * RING + y) * n_tp + t))
         return lax.ppermute(array, ("ctx", "tp"), pairs)
-
-    moves = (1, -1, 2)
-    columns = lax.dynamic_slice_in_dim(projection[0], img * cut, cut, axis=2).reshape(-1, cut)
-    first = stack(here, [columns] + [along_ctx(columns, 0, by) for by in moves])
 
     slots = jnp.roll(slots, -core * (merged // 2))
     target = slots // tok_rows
@@ -632,11 +628,17 @@
     asked = lax.all_to_all(
         packed.reshape(owners, capacity), ("img", "ctx"), split_axis=0, concat_axis=0, tiled=True
     )
+    columns = lax.dynamic_slice_in_dim(projection[0], img * cut, cut, axis=2).reshape(-1, cut)
+    gain = ln_gain[0]
+    lifted, lifted_other, xw, stat = layer_norm(here, features[0], gain, ln_bias[0])
+    columns, asked, lifted, stat = lax.optimization_barrier((columns, asked, lifted, stat))
+    moves = (1, -1, 2)
+    near_blocks = [along_ctx(columns, 0, by) for by in moves]
+
     asked = asked.reshape(n_img, n_ctx, capacity).transpose(1, 0, 2)
     asked = asked.reshape(slot_count, 1)
-    gain = ln_gain[0]
-    lifted, lifted_other, xw, stat = layer_norm(here, features[0], gain, ln_bias[0])
-    held = collect(asked, stream, cotangent[0], first, stat)
+    first = stack(here, [columns] + near_blocks)
+    held = collect(asked, stream, cotangent[0], first)
     came = lax.all_to_all(
         held.reshape(owners, n_img * capacity, width),
         ("img", "ctx"), split_axis=0, concat_axis=0, tiled=True,
@@ -664,29 +666,21 @@
     cross, stats = lax.optimization_barrier((cross, stats))
     crossed = lax.ppermute(cross, "img", flip)
 
-    chunks = 1
-    parts = backward(here, state, cot, own_gain, stats, stacks, chunks, full_width)
-    parts, crossed = lax.optimization_barrier((parts, crossed))
-    own, rest, other = (parts[i * chunks : (i + 1) * chunks] for i in range(3))
-    got = [lax.ppermute(o, "tp", core_pairs) for o in other]
-    sent = [pair(rest[c], got[c], crossed) for c in range(chunks)]
-    came_back = [[along_x(sent[c][by - 1], by) for by in (1, 2, 3)] for c in range(chunks)]
+    own, other = backward(here, state, cot, own_gain, stats, stacks, full_width)
+    own, other, crossed = lax.optimization_barrier((own, other, crossed))
+    got = lax.ppermute(other, "tp", core_pairs)
+    sent = pair(own, got, crossed)
+    came_back = [along_x(sent[by - 1], by) for by in (1, 2, 3)]
 
     send = braid(stay, crossed, n_ctx)
     arrived = lax.all_to_all(send, "ctx", split_axis=0, concat_axis=0, tiled=True)
     new_stream = place(here, asked, arrived, stream)
 
-    quarters = [[], [], [], []]
-    for c in range(chunks):
-        block = (far_half * chunks + c).reshape(1)
-        out = finish(block, own[c], got[c], came_back[c], xw, stat, gain)
-        beyond = lax.ppermute(out, "tp", far_pairs)
-        beyond, new_stream = lax.optimization_barrier((beyond, new_stream))
-        quarters[0].append(out)
-        quarters[1].append(beyond)
-        quarters[2].append(lax.ppermute(out, "tp", core_pairs))
-        quarters[3].append(lax.ppermute(beyond, "tp", core_pairs))
-    grad = lay(here, sum(quarters, []), chunks)
+    out = finish(here, own, got, came_back, xw, stat, gain)
+    beyond = lax.ppermute(out, "tp", far_pairs)
+    beyond, new_stream = lax.optimization_barrier((beyond, new_stream))
+    from_core = [lax.ppermute(x, "tp", core_pairs) for x in (out, beyond)]
+    grad = lay(here, [out, beyond] + from_core)
     return (new_stream, grad[None])
 
 

time: 200 us -> 204 us (1.020)
  blocking collectives: 16.5 us -> 0 us
  waiting for transfers between devices: 75.8 us -> 83.2 us
  starting transfers between devices: 45.2 us -> 52.2 us
  Pallas kernels: 38.7 us -> 41.6 us
  local copies, waits for them, and re-layouts: 20.8 us -> 23.5 us
    all_to_all x1 -> x0, blocking collectives: 16.5 us -> none  [shards(): lax.all_to_all(packed.reshape(owners, capacity), ('img', 'ctx'), split_ax...]
    all_to_all x0 -> x1, starting transfers between devices: none -> 9.81 us  [shards(): lax.all_to_all(packed.reshape(owners, capacity), ('img', 'ctx'), split_ax...]
    ppermute x6, waiting for transfers between devices: 23.3 us -> 28.3 us  [along_ctx(): return lax.ppermute(array, ('ctx', 'tp'), pairs)]
    unnamed x64 -> x70, local copies, waits for them, and re-layouts: 19.8 us -> 21.8 us
  transfers between devices with their start and end apart: 23 -> 24, of which waited for: 12 -> 13; matrix products, arithmetic and copies ran while one was open for 1% -> 0% of each run, Pallas kernels for 13% -> 14%
where the time goes in v9:
time: 204 us; the launch traced here: 203 us
  waiting for transfers between devices  83.2 us (41%)
  starting transfers between devices  52.2 us (26%)
  Pallas kernels  41.6 us (20%)
  local copies, waits for them, and re-layouts  23.5 us (12%)
    ppermute x6, waiting for transfers between devices, along_ctx(): return lax.ppermute(array, ('ctx', 'tp'), pairs)  28.3 us
    unnamed x70, local copies, waits for them, and re-layouts  21.8 us
    ppermute x6, waiting for transfers between devices, along_x(): return lax.ppermute(array, ('img', 'tp'), pairs)  20.8 us
    ppermute x1, waiting for transfers between devices, shards(): lax.ppermute(paired, 'img', flip)  13.4 us
    all_to_all x1, starting transfers between devices, shards(): lax.all_to_all(packed.reshape(owners, capacity), ('img', 'ctx'), split_ax...  9.81 us
    ppermute x1, waiting for transfers between devices, shards(): beyond = lax.ppermute(out, 'tp', far_pairs)  9.67 us
    pallas_call x1, Pallas kernels, merge(): pl.pallas_call(merge_kernel, in_specs=[scalars(), whole()] + [anywhere()]...  9.36 us
    ppermute x6, starting transfers between devices, along_ctx(): return lax.ppermute(array, ('ctx', 'tp'), pairs)  8.38 us
  transfers between devices with their start and end apart: 24, of which 13 were waited for; matrix products, arithmetic and copies ran while one was open for 0% of the time, Pallas kernels for 14%

profile of v9, /device:TPU:1, one launch (start us, length us, event | category | flops | bytes accessed | tf_op | source)
XLA Modules:
  0.0 202.9 jit_solution(6086862073322053721)
XLA Ops:
  2.5 9.8 %all-to-all-start = ((s32[32,1,16]{2,1,0:T(1,128)}), s32[32,1,16]{2,1,0:T(1,128)S(1)}, u32[]{:S(2)}, u32[]{:S(2)}) async-start(s32[32,1,16]{2,1,0:T(1,128)} %bitcast.7), calls=%async_computation | async-start | bytes 32768 | tf_op jit(solution)/shard_map/all_to_all | solution.py:628
  12.5 1.7 copy-done.11
  15.6 6.1 %layer_norm.1 = (bf16[128,4608]{1,0:T(8,128)(2,1)}, bf16[128,4608]{1,0:T(8,128)(2,1)S(1)}, bf16[4,256,1152]{2,1,0:T(8,128)(2,1)S(1)}, f32[256,128]{1,0:T(8,128)S(1)}) custom-call(s32[5]{0:T(128)S(1)} %stack.24.here_ref.refs_0_, bf16[1024,1152]{1,0:T(8,128)(2,1)S(1)} %bitcast.22, bf16[4,1152]{1,0:T(4,128)(2,1)S(1)} %bitcast.29, bf16[4,1152]{1,0:T(4,128)(2,1)S(1)} %bitcast.30), custom_call_target="tpu_custom_call" | custom-call | tf_op jit(solution)/shard_map/layer_norm/pallas_call | solution.py:95
  21.7 1.4 copy-done.12
  24.8 2.5 %collective-permute-start.7 = (bf16[128,4608]{1,0:T(8,128)(2,1)}, bf16[128,4608]{1,0:T(8,128)(2,1)}, u32[]{:S(2)}, u32[]{:S(2)}) collective-permute-start(bf16[128,4608]{1,0:T(8,128)(2,1)} %get-tuple-element.40.refs_4_), channel_id=1, source_target_pairs={{0,64},{1,67},{2,66},{3,65},{64,2},{65,1},{66,0},{67,3},{4,68},{5,... | collective-permute-start | bytes 3538952 | tf_op jit(solution)/shard_map/ppermute | solution.py:656
  28.5 1.5 collective-permute-start.2
  29.9 1.5 collective-permute-start.3
  31.6 2.8 %collective-permute-done.1.refs_1_ = bf16[288,512]{1,0:T(8,128)(2,1)S(1)} collective-permute-done((bf16[288,512]{1,0:T(8,128)(2,1)S(1)}, bf16[288,512]{1,0:T(8,128)(2,1)S(1)}, u32[]{:S(2)}, u32[]{:S(2)}) %collective-permute-start.1) | collective-permute-done | bytes 294944 | tf_op jit(solution)/shard_map/ppermute | solution.py:616
  35.9 2.6 %collective-permute-done.3.refs_3_ = bf16[288,512]{1,0:T(8,128)(2,1)S(1)} collective-permute-done((bf16[288,512]{1,0:T(8,128)(2,1)S(1)}, bf16[288,512]{1,0:T(8,128)(2,1)S(1)}, u32[]{:S(2)}, u32[]{:S(2)}) %collective-permute-start.3) | collective-permute-done | bytes 294944 | tf_op jit(solution)/shard_map/ppermute | solution.py:616
  42.8 1.6 copy-done.16
  44.4 1.3 collect.1
  45.7 1.3 copy-done.5
  47.0 6.9 %all-to-all-start.1 = ((bf16[32,32,1024]{2,1,0:T(8,128)(2,1)}), bf16[32,32,1024]{2,1,0:T(8,128)(2,1)}, u32[]{:S(2)}, u32[]{:S(2)}) async-start(bf16[32,32,1024]{2,1,0:T(8,128)(2,1)} %bitcast.21), calls=%async_computation.1 | async-start | bytes 4194304 | tf_op jit(solution)/shard_map/all_to_all | solution.py:642
  53.9 1.2 collective-permute-start.4
  55.1 1.5 collective-permute-start.5
  56.6 1.4 collective-permute-start.6
  58.1 3.3 %collective-permute-start.8 = (bf16[128,4608]{1,0:T(8,128)(2,1)}, bf16[128,4608]{1,0:T(8,128)(2,1)}, u32[]{:S(2)}, u32[]{:S(2)}) collective-permute-start(bf16[128,4608]{1,0:T(8,128)(2,1)} %collective-permute-done.7.refs_6_), channel_id=1, source_target_pairs={{0,1},{1,0},{2,3},{3,2},{4,5},{5,4},{6,7},{7,6},{8,9},{9,8},{10,11... | collective-permute-start | bytes 3538952 | tf_op jit(solution)/shard_map/ppermute | solution.py:657
  61.4 1.2 collective-permute-start
  63.2 13.4 %collective-permute-done = s32[256]{0:T(256)S(1)} collective-permute-done((s32[256]{0:T(256)S(1)}, s32[256]{0:T(256)S(1)}, u32[]{:S(2)}, u32[]{:S(2)}) %collective-permute-start) | collective-permute-done | bytes 1056 | tf_op jit(solution)/shard_map/ppermute | solution.py:647
  76.8 1.5 all-to-all-done.1
  78.3 2.9 %unpack.1 = (bf16[512,512]{1,0:T(8,128)(2,1)S(1)}, bf16[512,512]{1,0:T(8,128)(2,1)S(1)}) custom-call(s32[512,1]{1,0:T(8,128)S(1)} %copy.28.slot_ref, bf16[1024,1024]{1,0:T(8,128)(2,1)} %bitcast.17.came_ref), custom_call_target="tpu_custom_call" | custom-call | tf_op jit(solution)/shard_map/unpack/pallas_call | solution.py:170
  82.8 9.9 %collective-permute-done.4.refs_1_.refs_7_ = bf16[4,288,512]{2,1,0:T(8,128)(2,1)S(1)} collective-permute-done((bf16[4,288,512]{2,1,0:T(8,128)(2,1)S(1)}, bf16[4,288,512]{2,1,0:T(8,128)(2,1)S(1)}, u32[]{:S(2)}, u32[]{:S(2)}) %collective-permute-start.4) | collective-permute-done | bytes 1179680 | tf_op jit(solution)/shard_map/ppermute | solution.py:616
  92.7 13.1 %collective-permute-done.6.refs_3_.refs_9_ = bf16[4,288,512]{2,1,0:T(8,128)(2,1)} collective-permute-done((bf16[4,288,512]{2,1,0:T(8,128)(2,1)S(1)}, bf16[4,288,512]{2,1,0:T(8,128)(2,1)}, u32[]{:S(2)}, u32[]{:S(2)}) %collective-permute-start.6) | collective-permute-done | bytes 1179680 | tf_op jit(solution)/shard_map/ppermute | solution.py:616
  105.8 9.4 %merge.1 = (bf16[512,512]{1,0:T(8,128)(2,1)}, f32[512,512]{1,0:T(8,128)}, f32[8,512]{1,0:T(8,128)}) custom-call(s32[5]{0:T(128)} %copy-done.27, bf16[1,512]{1,0:T(2,128)(2,1)} %constant_dynamic-slice_fusion.1.ngain_ref.refs_1_, bf16[512,512]{1,0:T(8,128)(2,1)} %copy-done.18, bf16[512,512]{1,0:T(8,128)(2,1)} %copy-done.13, bf16[4,288,512]{2,1,0:T(8,128)(2,1)} %copy-done.1, ...), custom_call_target="tpu_custom_call" | custom-call | tf_op jit(solution)/shard_map/merge/pallas_call | solution.py:280
  115.1 1.8 collective-permute-start.9
  118.7 1.5 collective-permute-start.10
  120.4 2.2 %collective-permute-start.12 = (f32[8,512]{1,0:T(8,128)S(1)}, f32[8,512]{1,0:T(8,128)S(1)}, u32[]{:S(2)}, u32[]{:S(2)}) collective-permute-start(f32[8,512]{1,0:T(8,128)S(1)} %get-tuple-element.46), channel_id=1, source_target_pairs={{0,66},{1,67},{2,64},{3,65},{64,0},{65,1},{66,2},{67,3},{4,70},{5,... | collective-permute-start | bytes 49160 | tf_op jit(solution)/shard_map/ppermute | solution.py:604
  123.7 1.4 pack.1
  125.2 1.3 copy-done.7
  126.5 1.2 copy-done.17
  127.7 7.7 %backward.1 = (bf16[256,4608]{1,0:T(8,128)(2,1)}, bf16[256,4608]{1,0:T(8,128)(2,1)}) custom-call(s32[5]{0:T(128)S(1)} %copy-done.28, bf16[1,512]{1,0:T(2,128)(2,1)S(1)} %copy-done.31, f32[8,512]{1,0:T(8,128)S(1)} %get-tuple-element.47.after_ref.refs_2_, f32[8,512]{1,0:T(8,128)S(1)} %collective-permute-done.10.refs_3_, ...), custom_call_target="tpu_custom_call" | custom-call | tf_op jit(solution)/shard_map/backward/pallas_call | solution.py:418
  135.4 2.3 %collective-permute-done.13.after_ref.crossed_ref = bf16[512,512]{1,0:T(8,128)(2,1)S(1)} collective-permute-done((bf16[512,512]{1,0:T(8,128)(2,1)S(1)}, bf16[512,512]{1,0:T(8,128)(2,1)S(1)}, u32[]{:S(2)}, u32[]{:S(2)}) %collective-permute-start.13) | collective-permute-done | bytes 524320 | tf_op jit(solution)/shard_map/ppermute | solution.py:667
  137.7 1.8 collective-permute-start.14
  139.5 4.4 %collective-permute-done.14.got_ref = bf16[256,4608]{1,0:T(8,128)(2,1)S(1)} collective-permute-done((bf16[256,4608]{1,0:T(8,128)(2,1)}, bf16[256,4608]{1,0:T(8,128)(2,1)S(1)}, u32[]{:S(2)}, u32[]{:S(2)}) %collective-permute-start.14) | collective-permute-done | bytes 2359328 | tf_op jit(solution)/shard_map/ppermute | solution.py:671
  143.9 1.7 copy-done.3
  145.6 1.4 pair.1
  147.2 2.7 %collective-permute-start.16 = (bf16[64,4608]{1,0:T(8,128)(2,1)S(1)}, bf16[64,4608]{1,0:T(8,128)(2,1)}, u32[]{:S(2)}, u32[]{:S(2)}) collective-permute-start(bf16[64,4608]{1,0:T(8,128)(2,1)S(1)} %get-tuple-element.59), channel_id=1, source_target_pairs={{0,2},{1,3},{2,0},{3,1},{64,66},{65,67},{66,64},{67,65},{4,6},{5,7... | collective-permute-start | bytes 1769480 | tf_op jit(solution)/shard_map/ppermute | solution.py:604
  151.5 3.7 %all-to-all-start.2 = ((bf16[16,2,32,512]{3,2,1,0:T(8,128)(2,1)}), bf16[16,2,32,512]{3,2,1,0:T(8,128)(2,1)S(1)}, u32[]{:S(2)}, u32[]{:S(2)}) async-start(bf16[16,2,32,512]{3,2,1,0:T(8,128)(2,1)} %braid.1), calls=%async_computation.2 | async-start | bytes 2097152 | tf_op jit(solution)/shard_map/all_to_all | solution.py:676
  155.2 8.0 %collective-permute-done.15.refs_0_ = bf16[64,4608]{1,0:T(8,128)(2,1)} collective-permute-done((bf16[64,4608]{1,0:T(8,128)(2,1)}, bf16[64,4608]{1,0:T(8,128)(2,1)}, u32[]{:S(2)}, u32[]{:S(2)}) %collective-permute-start.15) | collective-permute-done | bytes 589856 | tf_op jit(solution)/shard_map/ppermute | solution.py:604
  163.2 12.7 %collective-permute-done.16.refs_1_ = bf16[64,4608]{1,0:T(8,128)(2,1)} collective-permute-done((bf16[64,4608]{1,0:T(8,128)(2,1)S(1)}, bf16[64,4608]{1,0:T(8,128)(2,1)}, u32[]{:S(2)}, u32[]{:S(2)}) %collective-permute-start.16) | collective-permute-done | bytes 589856 | tf_op jit(solution)/shard_map/ppermute | solution.py:604
  176.0 4.8 %finish.1.refs_0_ = bf16[256,1152]{1,0:T(8,128)(2,1)} custom-call(s32[5]{0:T(128)} %copy-done.27, bf16[256,4608]{1,0:T(8,128)(2,1)} %get-tuple-element.55.own_ref, bf16[256,4608]{1,0:T(8,128)(2,1)} %copy-done.4, bf16[64,4608]{1,0:T(8,128)(2,1)} %collective-permute-done.15.refs_0_, bf16[64,4608]{1,0:T(8,128)(2,1)} %collective-permute-done.16.refs_1_, ...), custom_call_target="tpu_custom_call" | custom-call | tf_op jit(solution)/shard_map/finish/pallas_call | solution.py:496
  180.8 1.3 collective-permute-start.18
  182.1 2.4 %place.1 = bf16[512,1024]{1,0:T(8,128)(2,1)} custom-call(s32[5]{0:T(128)S(1)} %copy-done.29, s32[512,1]{1,0:T(8,128)S(1)} %reshape.38.pos_ref, bf16[16,2,32,512]{3,2,1,0:T(8,128)(2,1)S(1)} %all-to-all-done.2.came_ref, bf16[512,1024]{1,0:T(8,128)(2,1)S(1)} %copy-done.9), custom_call_target="tpu_custom_call" | custom-call | tf_op jit(solution)/shard_map/place/pallas_call | solution.py:537
  184.5 1.8 collective-permute-start.19
  186.3 9.7 %collective-permute-done.18.refs_1_ = bf16[256,1152]{1,0:T(8,128)(2,1)} collective-permute-done((bf16[256,1152]{1,0:T(8,128)(2,1)}, bf16[256,1152]{1,0:T(8,128)(2,1)}, u32[]{:S(2)}, u32[]{:S(2)}) %collective-permute-start.18) | collective-permute-done | bytes 589856 | tf_op jit(solution)/shard_map/ppermute | solution.py:680
  195.9 2.4 %collective-permute-start.20 = (bf16[256,1152]{1,0:T(8,128)(2,1)}, bf16[256,1152]{1,0:T(8,128)(2,1)S(1)}, u32[]{:S(2)}, u32[]{:S(2)}) collective-permute-start(bf16[256,1152]{1,0:T(8,128)(2,1)} %collective-permute-done.18.refs_1_), channel_id=1, source_target_pairs={{0,1},{1,0},{2,3},{3,2},{4,5},{5,4},{6,7},{7,6},{8,9},{9,8},{10,11... | collective-permute-start | bytes 1769480 | tf_op jit(solution)/shard_map/ppermute | solution.py:682
  198.4 1.8 collective-permute-done.20.refs_3_
  200.2 2.5 %lay.1 = bf16[1024,1152]{1,0:T(8,128)(2,1)} custom-call(s32[5]{0:T(128)S(1)} %copy-done.29, bf16[256,1152]{1,0:T(8,128)(2,1)S(1)} %copy-done.10, bf16[256,1152]{1,0:T(8,128)(2,1)} %collective-permute-done.18.refs_1_, bf16[256,1152]{1,0:T(8,128)(2,1)S(1)} %collective-permute-done.19.refs_2_, bf16[256,1152]{1,0:T(8,128)(2,1)S(1)} %collective-permute-done.20.refs_3_), custom_call_target="tpu_custom_call" | custom-call | tf_op jit(solution)/shard_map/lay/pallas_call | solution.py:564
  (96 shorter events, 19.4 us)
Async XLA Ops:
  0.6 11.7 %copy-start = (bf16[1,4,72,1024]{3,2,1,0:T(8,128)(2,1)S(1)}, bf16[1,4,72,1024]{3,2,1,0:T(8,128)(2,1)}, u32[]{:S(2)}) copy-start(bf16[1,4,72,1024]{3,2,1,0:T(8,128)(2,1)} %param.11) | copy-start | bytes 1769476
  2.5 22.3 %all-to-all-start = ((s32[32,1,16]{2,1,0:T(1,128)}), s32[32,1,16]{2,1,0:T(1,128)S(1)}, u32[]{:S(2)}, u32[]{:S(2)}) async-start(s32[32,1,16]{2,1,0:T(1,128)} %bitcast.7), calls=%async_computation | async-start | bytes 32768 | tf_op jit(solution)/shard_map/all_to_all | solution.py:628
  12.5 30.2 %copy-start.27 = (s32[5]{0:T(128)}, s32[5]{0:T(128)S(1)}, u32[]{:S(2)}) copy-start(s32[5]{0:T(128)S(1)} %stack.24.here_ref.refs_0_) | copy-start | bytes 64
  12.5 1.7 copy-start.11
  15.6 27.2 %copy-start.8 = (bf16[512,1024]{1,0:T(8,128)(2,1)S(1)}, bf16[512,1024]{1,0:T(8,128)(2,1)}, u32[]{:S(2)}) copy-start(bf16[512,1024]{1,0:T(8,128)(2,1)} %stream_ref.3) | copy-start | bytes 3145732
  21.7 1.4 copy-start.12
  23.1 1.0 copy-start.15
  24.8 33.3 %collective-permute-start.7 = (bf16[128,4608]{1,0:T(8,128)(2,1)}, bf16[128,4608]{1,0:T(8,128)(2,1)}, u32[]{:S(2)}, u32[]{:S(2)}) collective-permute-start(bf16[128,4608]{1,0:T(8,128)(2,1)} %get-tuple-element.40.refs_4_), channel_id=1, source_target_pairs={{0,64},{1,67},{2,66},{3,65},{64,2},{65,1},{66,0},{67,3},{4,68},{5,... | collective-permute-start | bytes 3538952 | tf_op jit(solution)/shard_map/ppermute | solution.py:656
  27.3 7.2 %collective-permute-start.1 = (bf16[288,512]{1,0:T(8,128)(2,1)S(1)}, bf16[288,512]{1,0:T(8,128)(2,1)S(1)}, u32[]{:S(2)}, u32[]{:S(2)}) collective-permute-start(bf16[288,512]{1,0:T(8,128)(2,1)S(1)} %bitcast.23), channel_id=1, source_target_pairs={{0,4},{1,17},{2,6},{3,19},{4,8},{5,21},{6,10},{7,23},{8,12},{9,25}... | collective-permute-start | bytes 884744 | tf_op jit(solution)/shard_map/ppermute | solution.py:616
  28.5 6.7 %collective-permute-start.2 = (bf16[288,512]{1,0:T(8,128)(2,1)S(1)}, bf16[288,512]{1,0:T(8,128)(2,1)S(1)}, u32[]{:S(2)}, u32[]{:S(2)}) collective-permute-start(bf16[288,512]{1,0:T(8,128)(2,1)S(1)} %bitcast.24), channel_id=1, source_target_pairs={{0,12},{1,49},{2,14},{3,51},{4,0},{5,53},{6,2},{7,55},{8,4},{9,57}... | collective-permute-start | bytes 884744 | tf_op jit(solution)/shard_map/ppermute | solution.py:616
  29.9 8.5 %collective-permute-start.3 = (bf16[288,512]{1,0:T(8,128)(2,1)S(1)}, bf16[288,512]{1,0:T(8,128)(2,1)S(1)}, u32[]{:S(2)}, u32[]{:S(2)}) collective-permute-start(bf16[288,512]{1,0:T(8,128)(2,1)S(1)} %bitcast.25), channel_id=1, source_target_pairs={{0,8},{1,33},{2,10},{3,35},{4,12},{5,37},{6,14},{7,39},{8,0},{9,41... | collective-permute-start | bytes 884744 | tf_op jit(solution)/shard_map/ppermute | solution.py:616
  39.2 1.0 copy-start.21
  42.7 13.9 %copy-start.1 = (bf16[4,288,512]{2,1,0:T(8,128)(2,1)}, bf16[4,288,512]{2,1,0:T(8,128)(2,1)S(1)}, u32[]{:S(2)}) copy-start(bf16[4,288,512]{2,1,0:T(8,128)(2,1)S(1)} %stack.25.after_ref.refs_0_.refs_6_) | copy-start | bytes 3538948
  42.7 1.7 copy-start.16
  45.7 1.3 copy-start.5
  47.0 15.6 %copy-start.34 = (bf16[1,1024]{1,0:T(2,128)(2,1)S(1)}, bf16[1,1024]{1,0:T(2,128)(2,1)}, u32[]{:S(2)}) copy-start(bf16[1,1024]{1,0:T(2,128)(2,1)} %param.13) | copy-start | bytes 6148
  47.0 31.3 %all-to-all-start.1 = ((bf16[32,32,1024]{2,1,0:T(8,128)(2,1)}), bf16[32,32,1024]{2,1,0:T(8,128)(2,1)}, u32[]{:S(2)}, u32[]{:S(2)}) async-start(bf16[32,32,1024]{2,1,0:T(8,128)(2,1)} %bitcast.21), calls=%async_computation.1 | async-start | bytes 4194304 | tf_op jit(solution)/shard_map/all_to_all | solution.py:642
  53.9 38.8 %collective-permute-start.4 = (bf16[4,288,512]{2,1,0:T(8,128)(2,1)S(1)}, bf16[4,288,512]{2,1,0:T(8,128)(2,1)S(1)}, u32[]{:S(2)}, u32[]{:S(2)}) collective-permute-start(bf16[4,288,512]{2,1,0:T(8,128)(2,1)S(1)} %stack.25.after_ref.refs_0_.refs_6_), channel_id=1, source_target_pairs={{0,16},{1,5},{2,18},{3,7},{4,20},{5,9},{6,22},{7,11},{8,24},{9,13}... | collective-permute-start | bytes 3538952 | tf_op jit(solution)/shard_map/ppermute | solution.py:616
  55.1 37.5 %collective-permute-start.5 = (bf16[4,288,512]{2,1,0:T(8,128)(2,1)S(1)}, bf16[4,288,512]{2,1,0:T(8,128)(2,1)}, u32[]{:S(2)}, u32[]{:S(2)}) collective-permute-start(bf16[4,288,512]{2,1,0:T(8,128)(2,1)S(1)} %stack.25.after_ref.refs_0_.refs_6_), channel_id=1, source_target_pairs={{0,48},{1,13},{2,50},{3,15},{4,52},{5,1},{6,54},{7,3},{8,56},{9,5}... | collective-permute-start | bytes 3538952 | tf_op jit(solution)/shard_map/ppermute | solution.py:616
  56.6 49.1 %collective-permute-start.6 = (bf16[4,288,512]{2,1,0:T(8,128)(2,1)S(1)}, bf16[4,288,512]{2,1,0:T(8,128)(2,1)}, u32[]{:S(2)}, u32[]{:S(2)}) collective-permute-start(bf16[4,288,512]{2,1,0:T(8,128)(2,1)S(1)} %stack.25.after_ref.refs_0_.refs_6_), channel_id=1, source_target_pairs={{0,32},{1,9},{2,34},{3,11},{4,36},{5,13},{6,38},{7,15},{8,40},{9,1... | collective-permute-start | bytes 3538952 | tf_op jit(solution)/shard_map/ppermute | solution.py:616
  58.1 47.6 %collective-permute-start.8 = (bf16[128,4608]{1,0:T(8,128)(2,1)}, bf16[128,4608]{1,0:T(8,128)(2,1)}, u32[]{:S(2)}, u32[]{:S(2)}) collective-permute-start(bf16[128,4608]{1,0:T(8,128)(2,1)} %collective-permute-done.7.refs_6_), channel_id=1, source_target_pairs={{0,1},{1,0},{2,3},{3,2},{4,5},{5,4},{6,7},{7,6},{8,9},{9,8},{10,11... | collective-permute-start | bytes 3538952 | tf_op jit(solution)/shard_map/ppermute | solution.py:657
  61.4 15.2 %collective-permute-start = (s32[256]{0:T(256)S(1)}, s32[256]{0:T(256)S(1)}, u32[]{:S(2)}, u32[]{:S(2)}) collective-permute-start(s32[256]{0:T(256)S(1)} %get-tuple-element.69), channel_id=1, source_target_pairs={{0,64},{64,0},{1,65},{65,1},{2,66},{66,2},{3,67},{67,3},{4,68},{68... | collective-permute-start | bytes 3080 | tf_op jit(solution)/shard_map/ppermute | solution.py:647
  92.7 13.1 %copy-start.6 = (bf16[4,288,512]{2,1,0:T(8,128)(2,1)}, bf16[4,288,512]{2,1,0:T(8,128)(2,1)S(1)}, u32[]{:S(2)}) copy-start(bf16[4,288,512]{2,1,0:T(8,128)(2,1)S(1)} %collective-permute-done.4.refs_1_.refs_7_) | copy-start | bytes 3538948
  105.7 16.9 %copy-start.28 = (s32[5]{0:T(128)S(1)}, s32[5]{0:T(128)}, u32[]{:S(2)}) copy-start(s32[5]{0:T(128)} %copy-done.27) | copy-start | bytes 64
  105.7 19.5 %copy-start.2 = (bf16[4,288,512]{2,1,0:T(8,128)(2,1)S(1)}, bf16[4,288,512]{2,1,0:T(8,128)(2,1)}, u32[]{:S(2)}) copy-start(bf16[4,288,512]{2,1,0:T(8,128)(2,1)} %copy-done.1) | copy-start | bytes 3538948
  105.7 19.5 %copy-start.14 = (bf16[512,512]{1,0:T(8,128)(2,1)S(1)}, bf16[512,512]{1,0:T(8,128)(2,1)}, u32[]{:S(2)}) copy-start(bf16[512,512]{1,0:T(8,128)(2,1)} %copy-done.13) | copy-start | bytes 1572868
  105.8 19.5 %copy-start.31 = (bf16[1,512]{1,0:T(2,128)(2,1)S(1)}, bf16[1,512]{1,0:T(2,128)(2,1)}, u32[]{:S(2)}) copy-start(bf16[1,512]{1,0:T(2,128)(2,1)} %constant_dynamic-slice_fusion.1.ngain_ref.refs_1_) | copy-start | bytes 3076
  115.1 2.8 %collective-permute-start.9 = (f32[8,512]{1,0:T(8,128)}, f32[8,512]{1,0:T(8,128)S(1)}, u32[]{:S(2)}, u32[]{:S(2)}) collective-permute-start(f32[8,512]{1,0:T(8,128)} %get-tuple-element.43.sums_ref), channel_id=1, source_target_pairs={{0,1},{1,0},{2,3},{3,2},{4,5},{5,4},{6,7},{7,6},{8,9},{9,8},{10,11... | collective-permute-start | bytes 49160 | tf_op jit(solution)/shard_map/ppermute | solution.py:663
  118.7 6.4 %collective-permute-start.10 = (f32[8,512]{1,0:T(8,128)S(1)}, f32[8,512]{1,0:T(8,128)S(1)}, u32[]{:S(2)}, u32[]{:S(2)}) collective-permute-start(f32[8,512]{1,0:T(8,128)S(1)} %get-tuple-element.46), channel_id=1, source_target_pairs={{0,64},{1,65},{2,66},{3,67},{64,2},{65,3},{66,0},{67,1},{4,68},{5,... | collective-permute-start | bytes 49160 | tf_op jit(solution)/shard_map/ppermute | solution.py:604
  120.1 4.9 %collective-permute-start.11 = (f32[8,512]{1,0:T(8,128)S(1)}, f32[8,512]{1,0:T(8,128)S(1)}, u32[]{:S(2)}, u32[]{:S(2)}) collective-permute-start(f32[8,512]{1,0:T(8,128)S(1)} %get-tuple-element.47.after_ref.refs_2_), channel_id=1, source_target_pairs={{0,2},{1,3},{2,0},{3,1},{64,66},{65,67},{66,64},{67,65},{4,6},{5,7... | collective-permute-start | bytes 49160 | tf_op jit(solution)/shard_map/ppermute | solution.py:604
  120.4 4.7 %collective-permute-start.12 = (f32[8,512]{1,0:T(8,128)S(1)}, f32[8,512]{1,0:T(8,128)S(1)}, u32[]{:S(2)}, u32[]{:S(2)}) collective-permute-start(f32[8,512]{1,0:T(8,128)S(1)} %get-tuple-element.46), channel_id=1, source_target_pairs={{0,66},{1,67},{2,64},{3,65},{64,0},{65,1},{66,2},{67,3},{4,70},{5,... | collective-permute-start | bytes 49160 | tf_op jit(solution)/shard_map/ppermute | solution.py:604
  122.6 1.0 copy-start.19
  125.1 12.6 %collective-permute-start.13 = (bf16[512,512]{1,0:T(8,128)(2,1)S(1)}, bf16[512,512]{1,0:T(8,128)(2,1)S(1)}, u32[]{:S(2)}, u32[]{:S(2)}) collective-permute-start(bf16[512,512]{1,0:T(8,128)(2,1)S(1)} %get-tuple-element.54), channel_id=1, source_target_pairs={{0,64},{64,0},{1,65},{65,1},{2,66},{66,2},{3,67},{67,3},{4,68},{68... | collective-permute-start | bytes 1572872 | tf_op jit(solution)/shard_map/ppermute | solution.py:667
  125.2 1.3 copy-start.7
  126.5 1.2 copy-start.17
  137.7 6.2 %collective-permute-start.14 = (bf16[256,4608]{1,0:T(8,128)(2,1)}, bf16[256,4608]{1,0:T(8,128)(2,1)S(1)}, u32[]{:S(2)}, u32[]{:S(2)}) collective-permute-start(bf16[256,4608]{1,0:T(8,128)(2,1)} %get-tuple-element.56), channel_id=1, source_target_pairs={{0,1},{1,0},{2,3},{3,2},{4,5},{5,4},{6,7},{7,6},{8,9},{9,8},{10,11... | collective-permute-start | bytes 7077896 | tf_op jit(solution)/shard_map/ppermute | solution.py:671
  143.9 1.7 copy-start.3
  145.5 1.6 copy-start.4
  147.2 16.1 %collective-permute-start.15 = (bf16[64,4608]{1,0:T(8,128)(2,1)}, bf16[64,4608]{1,0:T(8,128)(2,1)}, u32[]{:S(2)}, u32[]{:S(2)}) collective-permute-start(bf16[64,4608]{1,0:T(8,128)(2,1)} %get-tuple-element.58), channel_id=1, source_target_pairs={{0,64},{1,65},{2,66},{3,67},{64,2},{65,3},{66,0},{67,1},{4,68},{5,... | collective-permute-start | bytes 1769480 | tf_op jit(solution)/shard_map/ppermute | solution.py:604
  147.2 28.8 %collective-permute-start.16 = (bf16[64,4608]{1,0:T(8,128)(2,1)S(1)}, bf16[64,4608]{1,0:T(8,128)(2,1)}, u32[]{:S(2)}, u32[]{:S(2)}) collective-permute-start(bf16[64,4608]{1,0:T(8,128)(2,1)S(1)} %get-tuple-element.59), channel_id=1, source_target_pairs={{0,2},{1,3},{2,0},{3,1},{64,66},{65,67},{66,64},{67,65},{4,6},{5,7... | collective-permute-start | bytes 1769480 | tf_op jit(solution)/shard_map/ppermute | solution.py:604
  149.9 26.1 %collective-permute-start.17 = (bf16[64,4608]{1,0:T(8,128)(2,1)S(1)}, bf16[64,4608]{1,0:T(8,128)(2,1)}, u32[]{:S(2)}, u32[]{:S(2)}) collective-permute-start(bf16[64,4608]{1,0:T(8,128)(2,1)S(1)} %get-tuple-element.60), channel_id=1, source_target_pairs={{0,66},{1,67},{2,64},{3,65},{64,0},{65,1},{66,2},{67,3},{4,70},{5,... | collective-permute-start | bytes 1769480 | tf_op jit(solution)/shard_map/ppermute | solution.py:604
  151.5 30.5 %all-to-all-start.2 = ((bf16[16,2,32,512]{3,2,1,0:T(8,128)(2,1)}), bf16[16,2,32,512]{3,2,1,0:T(8,128)(2,1)S(1)}, u32[]{:S(2)}, u32[]{:S(2)}) async-start(bf16[16,2,32,512]{3,2,1,0:T(8,128)(2,1)} %braid.1), calls=%async_computation.2 | async-start | bytes 2097152 | tf_op jit(solution)/shard_map/all_to_all | solution.py:676
  176.0 6.1 %copy-start.9 = (bf16[512,1024]{1,0:T(8,128)(2,1)S(1)}, bf16[512,1024]{1,0:T(8,128)(2,1)}, u32[]{:S(2)}) copy-start(bf16[512,1024]{1,0:T(8,128)(2,1)} %stream_ref.3) | copy-start | bytes 3145732
  176.0 6.1 %copy-start.29 = (s32[5]{0:T(128)S(1)}, s32[5]{0:T(128)}, u32[]{:S(2)}) copy-start(s32[5]{0:T(128)} %copy-done.27) | copy-start | bytes 64
  180.8 3.6 %copy-start.10 = (bf16[256,1152]{1,0:T(8,128)(2,1)S(1)}, bf16[256,1152]{1,0:T(8,128)(2,1)}, u32[]{:S(2)}) copy-start(bf16[256,1152]{1,0:T(8,128)(2,1)} %finish.1.refs_0_) | copy-start | bytes 1769476
  180.8 15.1 %collective-permute-start.18 = (bf16[256,1152]{1,0:T(8,128)(2,1)}, bf16[256,1152]{1,0:T(8,128)(2,1)}, u32[]{:S(2)}, u32[]{:S(2)}) collective-permute-start(bf16[256,1152]{1,0:T(8,128)(2,1)} %finish.1.refs_0_), channel_id=1, source_target_pairs={{0,2},{1,3},{2,0},{3,1},{4,6},{5,7},{6,4},{7,5},{8,10},{9,11},{10,... | collective-permute-start | bytes 1769480 | tf_op jit(solution)/shard_map/ppermute | solution.py:680
  184.5 13.9 %collective-permute-start.19 = (bf16[256,1152]{1,0:T(8,128)(2,1)S(1)}, bf16[256,1152]{1,0:T(8,128)(2,1)S(1)}, u32[]{:S(2)}, u32[]{:S(2)}) collective-permute-start(bf16[256,1152]{1,0:T(8,128)(2,1)S(1)} %copy-done.10), channel_id=1, source_target_pairs={{0,1},{1,0},{2,3},{3,2},{4,5},{5,4},{6,7},{7,6},{8,9},{9,8},{10,11... | collective-permute-start | bytes 1769480 | tf_op jit(solution)/shard_map/ppermute | solution.py:682
  195.9 4.3 %collective-permute-start.20 = (bf16[256,1152]{1,0:T(8,128)(2,1)}, bf16[256,1152]{1,0:T(8,128)(2,1)S(1)}, u32[]{:S(2)}, u32[]{:S(2)}) collective-permute-start(bf16[256,1152]{1,0:T(8,128)(2,1)} %collective-permute-done.18.refs_1_), channel_id=1, source_target_pairs={{0,1},{1,0},{2,3},{3,2},{4,5},{5,4},{6,7},{7,6},{8,9},{9,8},{10,11... | collective-permute-start | bytes 1769480 | tf_op jit(solution)/shard_map/ppermute | solution.py:682
  (11 other events, 8.4 us)

commit v10 on v9

--- a/solution.py
+++ b/solution.py
@@ -27,6 +27,10 @@
 
 def scalars():
     return pl.BlockSpec(memory_space=pltpu.SMEM)
+
+
+def in_hbm():
+    return pl.BlockSpec(memory_space=pltpu.HBM)
 
 
 def anywhere():
@@ -140,12 +144,11 @@
 def collect(pos, stream, cot, after):
     slots = pos.shape[0]
     rows, width = stream.shape
-    out = shape((2, slots, width), BF)
     return pl.pallas_call(
         collect_kernel,
         in_specs=[whole()] * 3 + [anywhere()],
         out_specs=whole(),
-        out_shape=out,
+        out_shape=shape((2, slots, width), BF),
         compiler_params=params(20),
         cost_estimate=FREE,
         name="collect",
@@ -179,18 +182,26 @@
 
 
 def stack_kernel(here_ref, *refs):
+    out_ref, sems = refs[RING:]
     first = jnp.where(here_ref[0] == 0, here_ref[4], here_ref[3])
-    for away, ref in zip(AWAY, refs[:RING]):
-        refs[RING][lax.rem(first + away, RING)] = ref[...]
+    copies = [
+        pltpu.make_async_copy(ref, out_ref.at[lax.rem(first + away, RING)], sems.at[index])
+        for index, (away, ref) in enumerate(zip(AWAY, refs[:RING]))
+    ]
+    for copy in copies:
+        copy.start()
+    for copy in copies:
+        copy.wait()
 
 
 def stack(here, blocks):
     rows, width = blocks[0].shape
     return pl.pallas_call(
         stack_kernel,
-        in_specs=[scalars()] + [whole()] * RING,
+        in_specs=[scalars()] + [in_hbm()] * RING,
         out_specs=whole(),
         out_shape=shape((RING, rows, width), BF),
+        scratch_shapes=[pltpu.SemaphoreType.DMA((RING,))],
         compiler_params=params(6),
         cost_estimate=FREE,
         name="stack",
@@ -279,7 +290,7 @@
     outs = [shape((tokens, width), BF), shape((tokens, width), F32), shape((8, tokens), F32)]
     return pl.pallas_call(
         merge_kernel,
-        in_specs=[scalars(), whole()] + [anywhere()] * (2 + RING + len(lifted)),
+        in_specs=[scalars(), whole()] + [in_hbm()] * (2 + RING + len(lifted)),
         out_specs=[whole()] * 3,
         out_shape=outs,
         scratch_shapes=[
@@ -417,7 +428,7 @@
     depth = RING * stacks[0].shape[0] * stacks[0].shape[1]
     return pl.pallas_call(
         lambda *refs: backward_kernel(full_width, *refs),
-        in_specs=[scalars()] + [whole()] * (1 + RING) + [anywhere()] * (RING + 2),
+        in_specs=[scalars()] + [whole()] * (1 + RING) + [in_hbm()] * (RING + 2),
         out_specs=[whole()] * 2,
         out_shape=[shape((tokens // 2, depth), BF)] * 2,
         scratch_shapes=[
@@ -429,42 +440,73 @@
             pltpu.SemaphoreType.DMA((2,)),
             pltpu.SemaphoreType.DMA((RING,)),
         ],
-        compiler_params=params(50),
+        compiler_params=params(24),
         cost_estimate=FREE,
         name="backward",
     )(here, ngain, *stats, *stacks, state, cot)
 
 
-def pair_kernel(own_ref, got_ref, after_ref, *outs):
-    rows = outs[0].shape[0]
-    for away, out in enumerate(outs):
-        at = slice((away + 1) * rows, (away + 2) * rows)
-        out[...] = (own_ref[at, :].astype(F32) + got_ref[at, :].astype(F32)).astype(BF)
+def pair_kernel(own_ref, got_ref, after_ref, next_ref, last_ref, keep_ref):
+    rows = own_ref.shape[0] // RING
+    half = rows // 2
+
+    def total(start):
+        at = slice(start, start + half)
+        return (own_ref[at, :].astype(F32) + got_ref[at, :].astype(F32)).astype(BF)
+
+    next_ref[:half] = total(2 * rows)
+    next_ref[half:] = total(rows + half)
+    last_ref[:half] = total(2 * rows + half)
+    last_ref[half:] = total(3 * rows)
+    keep_ref[:half] = total(rows)
+    keep_ref[half:] = total(3 * rows + half)
 
 
 def pair(own, got, after):
     rows, depth = got.shape[0] // RING, got.shape[1]
-    outs = [shape((rows, depth), BF)] * (RING - 1)
     return pl.pallas_call(
         pair_kernel,
         in_specs=[whole()] * 2 + [anywhere()],
-        out_specs=[whole()] * (RING - 1),
-        out_shape=outs,
+        out_specs=[whole()] * 3,
+        out_shape=[shape((rows, depth), BF)] * 3,
         compiler_params=params(8),
         cost_estimate=FREE,
         name="pair",
     )(own, got, after)
 
 
-def finish_kernel(here_ref, own_ref, got_ref, *refs):
-    came, (xw_ref, stat_ref, gain_ref, out_ref) = refs[: RING - 1], refs[RING - 1 :]
+def relay_kernel(keep_ref, from_last_ref, from_next_ref, next_ref, last_ref):
+    half = next_ref.shape[0]
+    for at, came_ref, out_ref in (
+        (slice(0, half), from_last_ref, next_ref),
+        (slice(half, 2 * half), from_next_ref, last_ref),
+    ):
+        out_ref[...] = (keep_ref[at, :].astype(F32) + came_ref[:half].astype(F32)).astype(BF)
+
+
+def relay(keep, from_last, from_next):
+    rows, depth = keep.shape
+    return pl.pallas_call(
+        relay_kernel,
+        in_specs=[whole()] * 3,
+        out_specs=[whole()] * 2,
+        out_shape=[shape((rows // 2, depth), BF)] * 2,
+        compiler_params=params(8),
+        cost_estimate=FREE,
+        name="relay",
+    )(keep, from_last, from_next)
+
+
+def finish_kernel(here_ref, own_ref, got_ref, from_last_ref, from_next_ref, late_last_ref, late_next_ref,
+                  xw_ref, stat_ref, gain_ref, out_ref):
     window, tokens, width = xw_ref.shape
     full = window * width
     mean = stat_ref[:, 0:1]
     inv = stat_ref[:, 1:2]
+    early = jnp.where(pl.program_id(0) == 0, from_next_ref[...], from_last_ref[...])
+    late = jnp.where(pl.program_id(0) == 0, late_last_ref[...], late_next_ref[...])
     lifted = own_ref[...].astype(F32) + got_ref[...].astype(F32)
-    for ref in came:
-        lifted = lifted + ref[...].astype(F32)
+    lifted = lifted + early.astype(F32) + late.astype(F32)
     share = width // (RING * RING)
     scaled = []
     total = 0.0
@@ -487,18 +529,20 @@
     ).astype(BF)
 
 
-def finish(here, own, got, came, xw, stat, gain):
-    rows, depth = came[0].shape
+def finish(here, own, got, early, late, xw, stat, gain):
+    rows, depth = early[0].shape
     window, width = gain.shape
     steps = 2
     tokens = rows // steps
     same = pl.BlockSpec((tokens, depth), lambda i, h: (i, 0))
+    second = pl.BlockSpec((tokens, depth), lambda i, h: (1, 0))
+    only = pl.BlockSpec((tokens, depth), lambda i, h: (0, 0))
     return pl.pallas_call(
         finish_kernel,
         grid_spec=pltpu.PrefetchScalarGridSpec(
             num_scalar_prefetch=1,
             grid=(steps,),
-            in_specs=[same] * (1 + RING)
+            in_specs=[same, same, second, second, only, only]
             + [
                 pl.BlockSpec((window, tokens, width), lambda i, h: (0, h[1] * steps + i, 0)),
                 pl.BlockSpec((tokens, 128), lambda i, h: (h[1] * steps + i, 0)),
@@ -510,7 +554,7 @@
         compiler_params=params(58),
         cost_estimate=FREE,
         name="finish",
-    )(here, own, got, *came, xw, stat, gain)
+    )(here, own, got, *early, *late, xw, stat, gain)
 
 
 def place_kernel(here_ref, pos_ref, came_ref, stream_ref, out_ref):
@@ -631,21 +675,22 @@
     columns = lax.dynamic_slice_in_dim(projection[0], img * cut, cut, axis=2).reshape(-1, cut)
     gain = ln_gain[0]
     lifted, lifted_other, xw, stat = layer_norm(here, features[0], gain, ln_bias[0])
-    columns, asked, lifted, stat = lax.optimization_barrier((columns, asked, lifted, stat))
     moves = (1, -1, 2)
     near_blocks = [along_ctx(columns, 0, by) for by in moves]
+    asked, lifted, stat, near_blocks = lax.optimization_barrier((asked, lifted, stat, near_blocks))
+
+    first = stack(here, [columns] + near_blocks)
+    asked, first = lax.optimization_barrier((asked, first))
 
     asked = asked.reshape(n_img, n_ctx, capacity).transpose(1, 0, 2)
     asked = asked.reshape(slot_count, 1)
-    first = stack(here, [columns] + near_blocks)
     held = collect(asked, stream, cotangent[0], first)
+    paired = target * (n_img * capacity) + rank + img * capacity
+    paired = jnp.concatenate([paired, lax.ppermute(paired, "img", flip)]).reshape(-1, 1)
     came = lax.all_to_all(
         held.reshape(owners, n_img * capacity, width),
         ("img", "ctx"), split_axis=0, concat_axis=0, tiled=True,
     ).reshape(n_img * slot_count, width)
-    paired = target * (n_img * capacity) + rank + img * capacity
-    paired = jnp.concatenate([paired, lax.ppermute(paired, "img", flip)]).reshape(-1, 1)
-
     stacks = [first] + [along_ctx(first, 1, by) for by in moves]
 
     pairs = []
@@ -669,14 +714,16 @@
     own, other = backward(here, state, cot, own_gain, stats, stacks, full_width)
     own, other, crossed = lax.optimization_barrier((own, other, crossed))
     got = lax.ppermute(other, "tp", core_pairs)
-    sent = pair(own, got, crossed)
-    came_back = [along_x(sent[by - 1], by) for by in (1, 2, 3)]
+    to_next, to_last, keep = pair(own, got, crossed)
+    from_last, from_next = along_x(to_next, 1), along_x(to_last, -1)
+    to_next, to_last = relay(keep, from_last, from_next)
+    late_last, late_next = along_x(to_next, 1), along_x(to_last, -1)
 
     send = braid(stay, crossed, n_ctx)
     arrived = lax.all_to_all(send, "ctx", split_axis=0, concat_axis=0, tiled=True)
     new_stream = place(here, asked, arrived, stream)
 
-    out = finish(here, own, got, came_back, xw, stat, gain)
+    out = finish(here, own, got, (from_last, from_next), (late_last, late_next), xw, stat, gain)
     beyond = lax.ppermute(out, "tp", far_pairs)
     beyond, new_stream = lax.optimization_barrier((beyond, new_stream))
     from_core = [lax.ppermute(x, "tp", core_pairs) for x in (out, beyond)]

time: 204 us -> 194 us (0.951)
  waiting for transfers between devices: 83.2 us -> 70.8 us
  starting transfers between devices: 52.2 us -> 55.5 us
    ppermute x6 -> x7, waiting for transfers between devices: 20.8 us -> 13.6 us  [along_x(): return lax.ppermute(array, ('img', 'tp'), pairs)]
    ppermute x6, waiting for transfers between devices: 28.3 us -> 22.9 us  [along_ctx(): return lax.ppermute(array, ('ctx', 'tp'), pairs)]
    all_to_all x1, starting transfers between devices: 9.81 us -> 6.97 us  [shards(): lax.all_to_all(packed.reshape(owners, capacity), ('img', 'ctx'), split_ax...]
    ppermute x6 -> x7, starting transfers between devices: 7.28 us -> 9.55 us  [along_x(): return lax.ppermute(array, ('img', 'tp'), pairs)]
    pallas_call x1, Pallas kernels: 7.71 us -> 5.54 us  [backward(): pl.pallas_call(lambda *refs: backward_kernel(full_width, *refs), in_specs...]
    unnamed x70 -> x78, local copies, waits for them, and re-layouts: 21.8 us -> 22.5 us
    pallas_call x2 -> x3, Pallas kernels: 9.99 us -> 10.4 us  [the longest x1 9.39 us: merge(): pl.pallas_call(merge_kernel, in_specs=[scalars(), whole()] + [in_hbm()] *...]
  transfers between devices with their start and end apart: 24 -> 25, of which waited for: 13 -> 11; matrix products, arithmetic and copies ran while one was open for 0% -> 1% of each run, Pallas kernels for 14% -> 14%
where the time goes in v10:
time: 194 us; the launch traced here: 193 us
  waiting for transfers between devices  70.8 us (36%)
  starting transfers between devices  55.5 us (29%)
  Pallas kernels  40.1 us (21%)
  local copies, waits for them, and re-layouts  24.2 us (12%)
    ppermute x6, waiting for transfers between devices, along_ctx(): return lax.ppermute(array, ('ctx', 'tp'), pairs)  22.9 us
    unnamed x78, local copies, waits for them, and re-layouts  22.5 us
    ppermute x1, waiting for transfers between devices, shards(): lax.ppermute(paired, 'img', flip)  14.1 us
    ppermute x7, waiting for transfers between devices, along_x(): return lax.ppermute(array, ('img', 'tp'), pairs)  13.6 us
    ppermute x6, starting transfers between devices, along_ctx(): return lax.ppermute(array, ('ctx', 'tp'), pairs)  10.2 us
    ppermute x7, starting transfers between devices, along_x(): return lax.ppermute(array, ('img', 'tp'), pairs)  9.55 us
    pallas_call x1, Pallas kernels, merge(): pl.pallas_call(merge_kernel, in_specs=[scalars(), whole()] + [in_hbm()] *...  9.39 us
    ppermute x1, waiting for transfers between devices, shards(): beyond = lax.ppermute(out, 'tp', far_pairs)  7.73 us
  transfers between devices with their start and end apart: 25, of which 11 were waited for; matrix products, arithmetic and copies ran while one was open for 1% of the time, Pallas kernels for 14%

profile of v10, /device:TPU:1, one launch (start us, length us, event | category | flops | bytes accessed | tf_op | source)
XLA Modules:
  0.0 192.8 jit_solution(3673090991167552622)
XLA Ops:
  0.7 1.0 copy-done
  1.7 2.5 %collective-permute-start.1 = (bf16[288,512]{1,0:T(8,128)(2,1)S(1)}, bf16[288,512]{1,0:T(8,128)(2,1)S(1)}, u32[]{:S(2)}, u32[]{:S(2)}) collective-permute-start(bf16[288,512]{1,0:T(8,128)(2,1)S(1)} %bitcast.23), channel_id=1, source_target_pairs={{0,4},{1,17},{2,6},{3,19},{4,8},{5,21},{6,10},{7,23},{8,12},{9,25}... | collective-permute-start | bytes 884744 | tf_op jit(solution)/shard_map/ppermute | solution.py:660
  4.3 2.2 %collective-permute-start.2 = (bf16[288,512]{1,0:T(8,128)(2,1)S(1)}, bf16[288,512]{1,0:T(8,128)(2,1)S(1)}, u32[]{:S(2)}, u32[]{:S(2)}) collective-permute-start(bf16[288,512]{1,0:T(8,128)(2,1)S(1)} %bitcast.24), channel_id=1, source_target_pairs={{0,12},{1,49},{2,14},{3,51},{4,0},{5,53},{6,2},{7,55},{8,4},{9,57}... | collective-permute-start | bytes 884744 | tf_op jit(solution)/shard_map/ppermute | solution.py:660
  6.5 1.2 collective-permute-start.3
  9.5 7.0 %all-to-all-start = ((s32[32,1,16]{2,1,0:T(1,128)}), s32[32,1,16]{2,1,0:T(1,128)S(1)}, u32[]{:S(2)}, u32[]{:S(2)}) async-start(s32[32,1,16]{2,1,0:T(1,128)} %bitcast.6), calls=%async_computation | async-start | bytes 32768 | tf_op jit(solution)/shard_map/all_to_all | solution.py:672
  16.6 1.7 copy-done.13
  19.7 6.1 %layer_norm.1 = (bf16[128,4608]{1,0:T(8,128)(2,1)}, bf16[128,4608]{1,0:T(8,128)(2,1)S(1)}, bf16[4,256,1152]{2,1,0:T(8,128)(2,1)S(1)}, f32[256,128]{1,0:T(8,128)S(1)}) custom-call(s32[5]{0:T(128)S(1)} %stack.24.here_ref.refs_0_, bf16[1024,1152]{1,0:T(8,128)(2,1)S(1)} %bitcast.22, bf16[4,1152]{1,0:T(4,128)(2,1)S(1)} %bitcast.29, bf16[4,1152]{1,0:T(4,128)(2,1)S(1)} %bitcast.30), custom_call_target="tpu_custom_call" | custom-call | tf_op jit(solution)/shard_map/layer_norm/pallas_call | solution.py:99
  25.8 1.4 copy-done.14
  30.3 2.5 %collective-permute-start.7 = (bf16[128,4608]{1,0:T(8,128)(2,1)}, bf16[128,4608]{1,0:T(8,128)(2,1)}, u32[]{:S(2)}, u32[]{:S(2)}) collective-permute-start(bf16[128,4608]{1,0:T(8,128)(2,1)} %get-tuple-element.50.refs_4_), channel_id=1, source_target_pairs={{0,64},{1,67},{2,66},{3,65},{64,2},{65,1},{66,0},{67,3},{4,68},{5,... | collective-permute-start | bytes 3538952 | tf_op jit(solution)/shard_map/ppermute | solution.py:701
  35.8 1.4 copy-done.18
  37.3 1.3 collect.1
  38.6 1.3 copy-done.5
  39.9 7.1 %all-to-all-start.1 = ((bf16[32,32,1024]{2,1,0:T(8,128)(2,1)}), bf16[32,32,1024]{2,1,0:T(8,128)(2,1)}, u32[]{:S(2)}, u32[]{:S(2)}) async-start(bf16[32,32,1024]{2,1,0:T(8,128)(2,1)} %bitcast.21), calls=%async_computation.1 | async-start | bytes 4194304 | tf_op jit(solution)/shard_map/all_to_all | solution.py:690
  47.0 1.2 collective-permute-start.4
  48.2 1.5 collective-permute-start.5
  49.7 1.4 collective-permute-start.6
  51.2 2.8 %collective-permute-start.8 = (bf16[128,4608]{1,0:T(8,128)(2,1)}, bf16[128,4608]{1,0:T(8,128)(2,1)}, u32[]{:S(2)}, u32[]{:S(2)}) collective-permute-start(bf16[128,4608]{1,0:T(8,128)(2,1)} %collective-permute-done.7.refs_6_), channel_id=1, source_target_pairs={{0,1},{1,0},{2,3},{3,2},{4,5},{5,4},{6,7},{7,6},{8,9},{9,8},{10,11... | collective-permute-start | bytes 3538952 | tf_op jit(solution)/shard_map/ppermute | solution.py:702
  53.9 1.2 collective-permute-start
  55.8 14.1 %collective-permute-done = s32[256]{0:T(256)S(1)} collective-permute-done((s32[256]{0:T(256)S(1)}, s32[256]{0:T(256)S(1)}, u32[]{:S(2)}, u32[]{:S(2)}) %collective-permute-start) | collective-permute-done | bytes 1056 | tf_op jit(solution)/shard_map/ppermute | solution.py:689
  70.0 1.4 all-to-all-done.1
  71.4 2.9 %unpack.1 = (bf16[512,512]{1,0:T(8,128)(2,1)S(1)}, bf16[512,512]{1,0:T(8,128)(2,1)S(1)}) custom-call(s32[512,1]{1,0:T(8,128)S(1)} %copy.28.slot_ref, bf16[1024,1024]{1,0:T(8,128)(2,1)} %bitcast.17.came_ref), custom_call_target="tpu_custom_call" | custom-call | tf_op jit(solution)/shard_map/unpack/pallas_call | solution.py:173
  75.9 9.8 %collective-permute-done.4.refs_1_.refs_7_ = bf16[4,288,512]{2,1,0:T(8,128)(2,1)S(1)} collective-permute-done((bf16[4,288,512]{2,1,0:T(8,128)(2,1)S(1)}, bf16[4,288,512]{2,1,0:T(8,128)(2,1)S(1)}, u32[]{:S(2)}, u32[]{:S(2)}) %collective-permute-start.4) | collective-permute-done | bytes 1179680 | tf_op jit(solution)/shard_map/ppermute | solution.py:660
  85.7 13.0 %collective-permute-done.6.refs_3_.refs_9_ = bf16[4,288,512]{2,1,0:T(8,128)(2,1)} collective-permute-done((bf16[4,288,512]{2,1,0:T(8,128)(2,1)S(1)}, bf16[4,288,512]{2,1,0:T(8,128)(2,1)}, u32[]{:S(2)}, u32[]{:S(2)}) %collective-permute-start.6) | collective-permute-done | bytes 1179680 | tf_op jit(solution)/shard_map/ppermute | solution.py:660
  98.8 9.4 %merge.1 = (bf16[512,512]{1,0:T(8,128)(2,1)}, f32[512,512]{1,0:T(8,128)}, f32[8,512]{1,0:T(8,128)}) custom-call(s32[5]{0:T(128)} %copy-done.29, bf16[1,512]{1,0:T(2,128)(2,1)} %constant_dynamic-slice_fusion.1.ngain_ref.refs_1_, bf16[512,512]{1,0:T(8,128)(2,1)} %copy-done.22, bf16[512,512]{1,0:T(8,128)(2,1)} %copy-done.15, bf16[4,288,512]{2,1,0:T(8,128)(2,1)} %copy-done.1, ...), custom_call_target="tpu_custom_call" | custom-call | tf_op jit(solution)/shard_map/merge/pallas_call | solution.py:291
  111.8 2.0 %collective-permute-start.11 = (f32[8,512]{1,0:T(8,128)S(1)}, f32[8,512]{1,0:T(8,128)S(1)}, u32[]{:S(2)}, u32[]{:S(2)}) collective-permute-start(f32[8,512]{1,0:T(8,128)S(1)} %get-tuple-element.57.after_ref.refs_2_), channel_id=1, source_target_pairs={{0,2},{1,3},{2,0},{3,1},{64,66},{65,67},{66,64},{67,65},{4,6},{5,7... | collective-permute-start | bytes 49160 | tf_op jit(solution)/shard_map/ppermute | solution.py:648
  113.7 1.3 collective-permute-start.12
  116.1 1.4 pack.1
  117.8 1.3 copy-done.7
  119.1 1.2 copy-done.19
  120.3 5.5 %backward.1 = (bf16[256,4608]{1,0:T(8,128)(2,1)S(1)}, bf16[256,4608]{1,0:T(8,128)(2,1)S(1)}) custom-call(s32[5]{0:T(128)S(1)} %copy-done.30, bf16[1,512]{1,0:T(2,128)(2,1)S(1)} %copy-done.33, f32[8,512]{1,0:T(8,128)S(1)} %get-tuple-element.57.after_ref.refs_2_, f32[8,512]{1,0:T(8,128)S(1)} %collective-permute-done.10.refs_3_, ...), custom_call_target="tpu_custom_call" | custom-call | tf_op jit(solution)/shard_map/backward/pallas_call | solution.py:429
  125.8 4.0 %collective-permute-done.13.after_ref.crossed_ref = bf16[512,512]{1,0:T(8,128)(2,1)S(1)} collective-permute-done((bf16[512,512]{1,0:T(8,128)(2,1)S(1)}, bf16[512,512]{1,0:T(8,128)(2,1)S(1)}, u32[]{:S(2)}, u32[]{:S(2)}) %collective-permute-start.13) | collective-permute-done | bytes 524320 | tf_op jit(solution)/shard_map/ppermute | solution.py:712
  129.9 2.1 %collective-permute-start.14 = (bf16[256,4608]{1,0:T(8,128)(2,1)S(1)}, bf16[256,4608]{1,0:T(8,128)(2,1)S(1)}, u32[]{:S(2)}, u32[]{:S(2)}) collective-permute-start(bf16[256,4608]{1,0:T(8,128)(2,1)S(1)} %get-tuple-element.66), channel_id=1, source_target_pairs={{0,1},{1,0},{2,3},{3,2},{4,5},{5,4},{6,7},{7,6},{8,9},{9,8},{10,11... | collective-permute-start | bytes 7077896 | tf_op jit(solution)/shard_map/ppermute | solution.py:716
  132.0 4.2 %collective-permute-done.14.got_ref = bf16[256,4608]{1,0:T(8,128)(2,1)S(1)} collective-permute-done((bf16[256,4608]{1,0:T(8,128)(2,1)S(1)}, bf16[256,4608]{1,0:T(8,128)(2,1)S(1)}, u32[]{:S(2)}, u32[]{:S(2)}) %collective-permute-start.14) | collective-permute-done | bytes 2359328 | tf_op jit(solution)/shard_map/ppermute | solution.py:716
  136.1 1.6 pair.1
  138.9 2.5 %collective-permute-start.16 = (bf16[64,4608]{1,0:T(8,128)(2,1)}, bf16[64,4608]{1,0:T(8,128)(2,1)S(1)}, u32[]{:S(2)}, u32[]{:S(2)}) collective-permute-start(bf16[64,4608]{1,0:T(8,128)(2,1)} %get-tuple-element.69), channel_id=1, source_target_pairs={{0,66},{1,67},{2,64},{3,65},{64,0},{65,1},{66,2},{67,3},{4,70},{5,... | collective-permute-start | bytes 1769480 | tf_op jit(solution)/shard_map/ppermute | solution.py:648
  142.4 4.5 %all-to-all-start.2 = ((bf16[16,2,32,512]{3,2,1,0:T(8,128)(2,1)}), bf16[16,2,32,512]{3,2,1,0:T(8,128)(2,1)S(1)}, u32[]{:S(2)}, u32[]{:S(2)}) async-start(bf16[16,2,32,512]{3,2,1,0:T(8,128)(2,1)} %braid.1), calls=%async_computation.2 | async-start | bytes 2097152 | tf_op jit(solution)/shard_map/all_to_all | solution.py:723
  146.9 7.8 %collective-permute-done.15.from_last_ref = bf16[64,4608]{1,0:T(8,128)(2,1)S(1)} collective-permute-done((bf16[64,4608]{1,0:T(8,128)(2,1)}, bf16[64,4608]{1,0:T(8,128)(2,1)S(1)}, u32[]{:S(2)}, u32[]{:S(2)}) %collective-permute-start.15) | collective-permute-done | bytes 589856 | tf_op jit(solution)/shard_map/ppermute | solution.py:648
  154.7 1.5 copy-done.21
  156.4 2.7 %collective-permute-start.18 = (bf16[32,4608]{1,0:T(8,128)(2,1)S(1)}, bf16[32,4608]{1,0:T(8,128)(2,1)S(1)}, u32[]{:S(2)}, u32[]{:S(2)}) collective-permute-start(bf16[32,4608]{1,0:T(8,128)(2,1)S(1)} %get-tuple-element.72), channel_id=1, source_target_pairs={{0,66},{1,67},{2,64},{3,65},{64,0},{65,1},{66,2},{67,3},{4,70},{5,... | collective-permute-start | bytes 884744 | tf_op jit(solution)/shard_map/ppermute | solution.py:648
  159.1 5.8 %collective-permute-done.17.late_last_ref = bf16[32,4608]{1,0:T(8,128)(2,1)S(1)} collective-permute-done((bf16[32,4608]{1,0:T(8,128)(2,1)S(1)}, bf16[32,4608]{1,0:T(8,128)(2,1)S(1)}, u32[]{:S(2)}, u32[]{:S(2)}) %collective-permute-start.17) | collective-permute-done | bytes 294944 | tf_op jit(solution)/shard_map/ppermute | solution.py:648
  165.7 5.0 %finish.1.refs_0_ = bf16[256,1152]{1,0:T(8,128)(2,1)} custom-call(s32[5]{0:T(128)} %copy-done.29, bf16[256,4608]{1,0:T(8,128)(2,1)} %copy-done.3, bf16[256,4608]{1,0:T(8,128)(2,1)} %copy-done.4, bf16[64,4608]{1,0:T(8,128)(2,1)} %copy-done.11, bf16[64,4608]{1,0:T(8,128)(2,1)} %copy-done.12, bf16[32,4608]{1,0:T(8,128)(2,1)} %copy-done.36, ...), custom_call_target="tpu_custom_call" | custom-call | tf_op jit(solution)/shard_map/finish/pallas_call | solution.py:540
  170.7 1.4 collective-permute-start.19
  172.1 2.4 %place.1 = bf16[512,1024]{1,0:T(8,128)(2,1)} custom-call(s32[5]{0:T(128)S(1)} %copy-done.31, s32[512,1]{1,0:T(8,128)S(1)} %reshape.38.pos_ref, bf16[16,2,32,512]{3,2,1,0:T(8,128)(2,1)S(1)} %all-to-all-done.2.came_ref, bf16[512,1024]{1,0:T(8,128)(2,1)S(1)} %copy-done.9), custom_call_target="tpu_custom_call" | custom-call | tf_op jit(solution)/shard_map/place/pallas_call | solution.py:581
  174.5 3.0 %collective-permute-start.20 = (bf16[256,1152]{1,0:T(8,128)(2,1)S(1)}, bf16[256,1152]{1,0:T(8,128)(2,1)S(1)}, u32[]{:S(2)}, u32[]{:S(2)}) collective-permute-start(bf16[256,1152]{1,0:T(8,128)(2,1)S(1)} %copy-done.10), channel_id=1, source_target_pairs={{0,1},{1,0},{2,3},{3,2},{4,5},{5,4},{6,7},{7,6},{8,9},{9,8},{10,11... | collective-permute-start | bytes 1769480 | tf_op jit(solution)/shard_map/ppermute | solution.py:729
  177.5 7.7 %collective-permute-done.19.refs_1_ = bf16[256,1152]{1,0:T(8,128)(2,1)} collective-permute-done((bf16[256,1152]{1,0:T(8,128)(2,1)}, bf16[256,1152]{1,0:T(8,128)(2,1)}, u32[]{:S(2)}, u32[]{:S(2)}) %collective-permute-start.19) | collective-permute-done | bytes 589856 | tf_op jit(solution)/shard_map/ppermute | solution.py:727
  185.2 3.0 %collective-permute-start.21 = (bf16[256,1152]{1,0:T(8,128)(2,1)}, bf16[256,1152]{1,0:T(8,128)(2,1)S(1)}, u32[]{:S(2)}, u32[]{:S(2)}) collective-permute-start(bf16[256,1152]{1,0:T(8,128)(2,1)} %collective-permute-done.19.refs_1_), channel_id=1, source_target_pairs={{0,1},{1,0},{2,3},{3,2},{4,5},{5,4},{6,7},{7,6},{8,9},{9,8},{10,11... | collective-permute-start | bytes 1769480 | tf_op jit(solution)/shard_map/ppermute | solution.py:729
  188.3 1.8 collective-permute-done.21.refs_3_
  190.1 2.5 %lay.1 = bf16[1024,1152]{1,0:T(8,128)(2,1)} custom-call(s32[5]{0:T(128)S(1)} %copy-done.31, bf16[256,1152]{1,0:T(8,128)(2,1)S(1)} %copy-done.10, bf16[256,1152]{1,0:T(8,128)(2,1)} %collective-permute-done.19.refs_1_, bf16[256,1152]{1,0:T(8,128)(2,1)S(1)} %collective-permute-done.20.refs_2_, bf16[256,1152]{1,0:T(8,128)(2,1)S(1)} %collective-permute-done.21.refs_3_), custom_call_target="tpu_custom_call" | custom-call | tf_op jit(solution)/shard_map/lay/pallas_call | solution.py:608
  (107 shorter events, 19.8 us)
Async XLA Ops:
  1.7 27.1 %collective-permute-start.1 = (bf16[288,512]{1,0:T(8,128)(2,1)S(1)}, bf16[288,512]{1,0:T(8,128)(2,1)S(1)}, u32[]{:S(2)}, u32[]{:S(2)}) collective-permute-start(bf16[288,512]{1,0:T(8,128)(2,1)S(1)} %bitcast.23), channel_id=1, source_target_pairs={{0,4},{1,17},{2,6},{3,19},{4,8},{5,21},{6,10},{7,23},{8,12},{9,25}... | collective-permute-start | bytes 884744 | tf_op jit(solution)/shard_map/ppermute | solution.py:660
  4.3 24.6 %collective-permute-start.2 = (bf16[288,512]{1,0:T(8,128)(2,1)S(1)}, bf16[288,512]{1,0:T(8,128)(2,1)S(1)}, u32[]{:S(2)}, u32[]{:S(2)}) collective-permute-start(bf16[288,512]{1,0:T(8,128)(2,1)S(1)} %bitcast.24), channel_id=1, source_target_pairs={{0,12},{1,49},{2,14},{3,51},{4,0},{5,53},{6,2},{7,55},{8,4},{9,57}... | collective-permute-start | bytes 884744 | tf_op jit(solution)/shard_map/ppermute | solution.py:660
  6.5 23.1 %collective-permute-start.3 = (bf16[288,512]{1,0:T(8,128)(2,1)S(1)}, bf16[288,512]{1,0:T(8,128)(2,1)S(1)}, u32[]{:S(2)}, u32[]{:S(2)}) collective-permute-start(bf16[288,512]{1,0:T(8,128)(2,1)S(1)} %bitcast.25), channel_id=1, source_target_pairs={{0,8},{1,33},{2,10},{3,35},{4,12},{5,37},{6,14},{7,39},{8,0},{9,41... | collective-permute-start | bytes 884744 | tf_op jit(solution)/shard_map/ppermute | solution.py:660
  9.5 19.4 %all-to-all-start = ((s32[32,1,16]{2,1,0:T(1,128)}), s32[32,1,16]{2,1,0:T(1,128)S(1)}, u32[]{:S(2)}, u32[]{:S(2)}) async-start(s32[32,1,16]{2,1,0:T(1,128)} %bitcast.6), calls=%async_computation | async-start | bytes 32768 | tf_op jit(solution)/shard_map/all_to_all | solution.py:672
  16.6 19.0 %copy-start.29 = (s32[5]{0:T(128)}, s32[5]{0:T(128)S(1)}, u32[]{:S(2)}) copy-start(s32[5]{0:T(128)S(1)} %stack.24.here_ref.refs_0_) | copy-start | bytes 64
  16.6 1.7 copy-start.13
  19.7 16.1 %copy-start.8 = (bf16[512,1024]{1,0:T(8,128)(2,1)S(1)}, bf16[512,1024]{1,0:T(8,128)(2,1)}, u32[]{:S(2)}) copy-start(bf16[512,1024]{1,0:T(8,128)(2,1)} %stream_ref.3) | copy-start | bytes 3145732
  25.8 1.4 copy-start.14
  30.3 20.8 %collective-permute-start.7 = (bf16[128,4608]{1,0:T(8,128)(2,1)}, bf16[128,4608]{1,0:T(8,128)(2,1)}, u32[]{:S(2)}, u32[]{:S(2)}) collective-permute-start(bf16[128,4608]{1,0:T(8,128)(2,1)} %get-tuple-element.50.refs_4_), channel_id=1, source_target_pairs={{0,64},{1,67},{2,66},{3,65},{64,2},{65,1},{66,0},{67,3},{4,68},{5,... | collective-permute-start | bytes 3538952 | tf_op jit(solution)/shard_map/ppermute | solution.py:701
  35.6 14.1 %copy-start.1 = (bf16[4,288,512]{2,1,0:T(8,128)(2,1)}, bf16[4,288,512]{2,1,0:T(8,128)(2,1)S(1)}, u32[]{:S(2)}) copy-start(bf16[4,288,512]{2,1,0:T(8,128)(2,1)S(1)} %stack.25.after_ref.refs_0_.refs_6_) | copy-start | bytes 3538948
  35.8 1.4 copy-start.18
  38.6 1.3 copy-start.5
  39.9 15.3 %copy-start.38 = (bf16[1,1024]{1,0:T(2,128)(2,1)S(1)}, bf16[1,1024]{1,0:T(2,128)(2,1)}, u32[]{:S(2)}) copy-start(bf16[1,1024]{1,0:T(2,128)(2,1)} %param.13) | copy-start | bytes 6148
  39.9 31.5 %all-to-all-start.1 = ((bf16[32,32,1024]{2,1,0:T(8,128)(2,1)}), bf16[32,32,1024]{2,1,0:T(8,128)(2,1)}, u32[]{:S(2)}, u32[]{:S(2)}) async-start(bf16[32,32,1024]{2,1,0:T(8,128)(2,1)} %bitcast.21), calls=%async_computation.1 | async-start | bytes 4194304 | tf_op jit(solution)/shard_map/all_to_all | solution.py:690
  47.0 38.8 %collective-permute-start.4 = (bf16[4,288,512]{2,1,0:T(8,128)(2,1)S(1)}, bf16[4,288,512]{2,1,0:T(8,128)(2,1)S(1)}, u32[]{:S(2)}, u32[]{:S(2)}) collective-permute-start(bf16[4,288,512]{2,1,0:T(8,128)(2,1)S(1)} %stack.25.after_ref.refs_0_.refs_6_), channel_id=1, source_target_pairs={{0,16},{1,5},{2,18},{3,7},{4,20},{5,9},{6,22},{7,11},{8,24},{9,13}... | collective-permute-start | bytes 3538952 | tf_op jit(solution)/shard_map/ppermute | solution.py:660
  48.2 37.5 %collective-permute-start.5 = (bf16[4,288,512]{2,1,0:T(8,128)(2,1)S(1)}, bf16[4,288,512]{2,1,0:T(8,128)(2,1)}, u32[]{:S(2)}, u32[]{:S(2)}) collective-permute-start(bf16[4,288,512]{2,1,0:T(8,128)(2,1)S(1)} %stack.25.after_ref.refs_0_.refs_6_), channel_id=1, source_target_pairs={{0,48},{1,13},{2,50},{3,15},{4,52},{5,1},{6,54},{7,3},{8,56},{9,5}... | collective-permute-start | bytes 3538952 | tf_op jit(solution)/shard_map/ppermute | solution.py:660
  49.7 49.1 %collective-permute-start.6 = (bf16[4,288,512]{2,1,0:T(8,128)(2,1)S(1)}, bf16[4,288,512]{2,1,0:T(8,128)(2,1)}, u32[]{:S(2)}, u32[]{:S(2)}) collective-permute-start(bf16[4,288,512]{2,1,0:T(8,128)(2,1)S(1)} %stack.25.after_ref.refs_0_.refs_6_), channel_id=1, source_target_pairs={{0,32},{1,9},{2,34},{3,11},{4,36},{5,13},{6,38},{7,15},{8,40},{9,1... | collective-permute-start | bytes 3538952 | tf_op jit(solution)/shard_map/ppermute | solution.py:660
  51.2 47.6 %collective-permute-start.8 = (bf16[128,4608]{1,0:T(8,128)(2,1)}, bf16[128,4608]{1,0:T(8,128)(2,1)}, u32[]{:S(2)}, u32[]{:S(2)}) collective-permute-start(bf16[128,4608]{1,0:T(8,128)(2,1)} %collective-permute-done.7.refs_6_), channel_id=1, source_target_pairs={{0,1},{1,0},{2,3},{3,2},{4,5},{5,4},{6,7},{7,6},{8,9},{9,8},{10,11... | collective-permute-start | bytes 3538952 | tf_op jit(solution)/shard_map/ppermute | solution.py:702
  53.9 15.9 %collective-permute-start = (s32[256]{0:T(256)S(1)}, s32[256]{0:T(256)S(1)}, u32[]{:S(2)}, u32[]{:S(2)}) collective-permute-start(s32[256]{0:T(256)S(1)} %get-tuple-element.81), channel_id=1, source_target_pairs={{0,64},{64,0},{1,65},{65,1},{2,66},{66,2},{3,67},{67,3},{4,68},{68... | collective-permute-start | bytes 3080 | tf_op jit(solution)/shard_map/ppermute | solution.py:689
  85.7 13.0 %copy-start.6 = (bf16[4,288,512]{2,1,0:T(8,128)(2,1)}, bf16[4,288,512]{2,1,0:T(8,128)(2,1)S(1)}, u32[]{:S(2)}) copy-start(bf16[4,288,512]{2,1,0:T(8,128)(2,1)S(1)} %collective-permute-done.4.refs_1_.refs_7_) | copy-start | bytes 3538948
  98.8 16.3 %copy-start.30 = (s32[5]{0:T(128)S(1)}, s32[5]{0:T(128)}, u32[]{:S(2)}) copy-start(s32[5]{0:T(128)} %copy-done.29) | copy-start | bytes 64
  98.8 19.0 %copy-start.2 = (bf16[4,288,512]{2,1,0:T(8,128)(2,1)S(1)}, bf16[4,288,512]{2,1,0:T(8,128)(2,1)}, u32[]{:S(2)}) copy-start(bf16[4,288,512]{2,1,0:T(8,128)(2,1)} %copy-done.1) | copy-start | bytes 3538948
  98.8 19.0 %copy-start.16 = (bf16[512,512]{1,0:T(8,128)(2,1)S(1)}, bf16[512,512]{1,0:T(8,128)(2,1)}, u32[]{:S(2)}) copy-start(bf16[512,512]{1,0:T(8,128)(2,1)} %copy-done.15) | copy-start | bytes 1572868
  98.8 19.0 %copy-start.33 = (bf16[1,512]{1,0:T(2,128)(2,1)S(1)}, bf16[1,512]{1,0:T(2,128)(2,1)}, u32[]{:S(2)}) copy-start(bf16[1,512]{1,0:T(2,128)(2,1)} %constant_dynamic-slice_fusion.1.ngain_ref.refs_1_) | copy-start | bytes 3076
  108.2 2.0 %collective-permute-start.9 = (f32[8,512]{1,0:T(8,128)}, f32[8,512]{1,0:T(8,128)S(1)}, u32[]{:S(2)}, u32[]{:S(2)}) collective-permute-start(f32[8,512]{1,0:T(8,128)} %get-tuple-element.53.sums_ref), channel_id=1, source_target_pairs={{0,1},{1,0},{2,3},{3,2},{4,5},{5,4},{6,7},{7,6},{8,9},{9,8},{10,11... | collective-permute-start | bytes 49160 | tf_op jit(solution)/shard_map/ppermute | solution.py:708
  110.9 6.6 %collective-permute-start.10 = (f32[8,512]{1,0:T(8,128)S(1)}, f32[8,512]{1,0:T(8,128)S(1)}, u32[]{:S(2)}, u32[]{:S(2)}) collective-permute-start(f32[8,512]{1,0:T(8,128)S(1)} %get-tuple-element.56), channel_id=1, source_target_pairs={{0,64},{1,65},{2,66},{3,67},{64,2},{65,3},{66,0},{67,1},{4,68},{5,... | collective-permute-start | bytes 49160 | tf_op jit(solution)/shard_map/ppermute | solution.py:648
  111.8 5.7 %collective-permute-start.11 = (f32[8,512]{1,0:T(8,128)S(1)}, f32[8,512]{1,0:T(8,128)S(1)}, u32[]{:S(2)}, u32[]{:S(2)}) collective-permute-start(f32[8,512]{1,0:T(8,128)S(1)} %get-tuple-element.57.after_ref.refs_2_), channel_id=1, source_target_pairs={{0,2},{1,3},{2,0},{3,1},{64,66},{65,67},{66,64},{67,65},{4,6},{5,7... | collective-permute-start | bytes 49160 | tf_op jit(solution)/shard_map/ppermute | solution.py:648
  113.7 3.8 %collective-permute-start.12 = (f32[8,512]{1,0:T(8,128)S(1)}, f32[8,512]{1,0:T(8,128)S(1)}, u32[]{:S(2)}, u32[]{:S(2)}) collective-permute-start(f32[8,512]{1,0:T(8,128)S(1)} %get-tuple-element.56), channel_id=1, source_target_pairs={{0,66},{1,67},{2,64},{3,65},{64,0},{65,1},{66,2},{67,3},{4,70},{5,... | collective-permute-start | bytes 49160 | tf_op jit(solution)/shard_map/ppermute | solution.py:648
  117.5 12.3 %collective-permute-start.13 = (bf16[512,512]{1,0:T(8,128)(2,1)S(1)}, bf16[512,512]{1,0:T(8,128)(2,1)S(1)}, u32[]{:S(2)}, u32[]{:S(2)}) collective-permute-start(bf16[512,512]{1,0:T(8,128)(2,1)S(1)} %get-tuple-element.64), channel_id=1, source_target_pairs={{0,64},{64,0},{1,65},{65,1},{2,66},{66,2},{3,67},{67,3},{4,68},{68... | collective-permute-start | bytes 1572872 | tf_op jit(solution)/shard_map/ppermute | solution.py:712
  117.8 1.3 copy-start.7
  119.0 1.2 copy-start.19
  125.8 11.9 %copy-start.3 = (bf16[256,4608]{1,0:T(8,128)(2,1)}, bf16[256,4608]{1,0:T(8,128)(2,1)S(1)}, u32[]{:S(2)}) copy-start(bf16[256,4608]{1,0:T(8,128)(2,1)S(1)} %get-tuple-element.65.own_ref) | copy-start | bytes 7077892
  129.9 6.3 %collective-permute-start.14 = (bf16[256,4608]{1,0:T(8,128)(2,1)S(1)}, bf16[256,4608]{1,0:T(8,128)(2,1)S(1)}, u32[]{:S(2)}, u32[]{:S(2)}) collective-permute-start(bf16[256,4608]{1,0:T(8,128)(2,1)S(1)} %get-tuple-element.66), channel_id=1, source_target_pairs={{0,1},{1,0},{2,3},{3,2},{4,5},{5,4},{6,7},{7,6},{8,9},{9,8},{10,11... | collective-permute-start | bytes 7077896 | tf_op jit(solution)/shard_map/ppermute | solution.py:716
  136.1 1.8 copy-start.4
  138.7 16.0 %collective-permute-start.15 = (bf16[64,4608]{1,0:T(8,128)(2,1)}, bf16[64,4608]{1,0:T(8,128)(2,1)S(1)}, u32[]{:S(2)}, u32[]{:S(2)}) collective-permute-start(bf16[64,4608]{1,0:T(8,128)(2,1)} %get-tuple-element.68), channel_id=1, source_target_pairs={{0,64},{1,65},{2,66},{3,67},{64,2},{65,3},{66,0},{67,1},{4,68},{5,... | collective-permute-start | bytes 1769480 | tf_op jit(solution)/shard_map/ppermute | solution.py:648
  138.9 15.8 %collective-permute-start.16 = (bf16[64,4608]{1,0:T(8,128)(2,1)}, bf16[64,4608]{1,0:T(8,128)(2,1)S(1)}, u32[]{:S(2)}, u32[]{:S(2)}) collective-permute-start(bf16[64,4608]{1,0:T(8,128)(2,1)} %get-tuple-element.69), channel_id=1, source_target_pairs={{0,66},{1,67},{2,64},{3,65},{64,0},{65,1},{66,2},{67,3},{4,70},{5,... | collective-permute-start | bytes 1769480 | tf_op jit(solution)/shard_map/ppermute | solution.py:648
  142.4 29.7 %all-to-all-start.2 = ((bf16[16,2,32,512]{3,2,1,0:T(8,128)(2,1)}), bf16[16,2,32,512]{3,2,1,0:T(8,128)(2,1)S(1)}, u32[]{:S(2)}, u32[]{:S(2)}) async-start(bf16[16,2,32,512]{3,2,1,0:T(8,128)(2,1)} %braid.1), calls=%async_computation.2 | async-start | bytes 2097152 | tf_op jit(solution)/shard_map/all_to_all | solution.py:723
  154.7 10.2 %copy-start.11 = (bf16[64,4608]{1,0:T(8,128)(2,1)}, bf16[64,4608]{1,0:T(8,128)(2,1)S(1)}, u32[]{:S(2)}) copy-start(bf16[64,4608]{1,0:T(8,128)(2,1)S(1)} %collective-permute-done.15.from_last_ref) | copy-start | bytes 1769476
  154.7 10.2 %copy-start.12 = (bf16[64,4608]{1,0:T(8,128)(2,1)}, bf16[64,4608]{1,0:T(8,128)(2,1)S(1)}, u32[]{:S(2)}) copy-start(bf16[64,4608]{1,0:T(8,128)(2,1)S(1)} %collective-permute-done.16.from_next_ref) | copy-start | bytes 1769476
  154.7 1.5 copy-start.21
  156.3 8.6 %collective-permute-start.17 = (bf16[32,4608]{1,0:T(8,128)(2,1)S(1)}, bf16[32,4608]{1,0:T(8,128)(2,1)S(1)}, u32[]{:S(2)}, u32[]{:S(2)}) collective-permute-start(bf16[32,4608]{1,0:T(8,128)(2,1)S(1)} %get-tuple-element.71), channel_id=1, source_target_pairs={{0,64},{1,65},{2,66},{3,67},{64,2},{65,3},{66,0},{67,1},{4,68},{5,... | collective-permute-start | bytes 884744 | tf_op jit(solution)/shard_map/ppermute | solution.py:648
  156.4 8.5 %collective-permute-start.18 = (bf16[32,4608]{1,0:T(8,128)(2,1)S(1)}, bf16[32,4608]{1,0:T(8,128)(2,1)S(1)}, u32[]{:S(2)}, u32[]{:S(2)}) collective-permute-start(bf16[32,4608]{1,0:T(8,128)(2,1)S(1)} %get-tuple-element.72), channel_id=1, source_target_pairs={{0,66},{1,67},{2,64},{3,65},{64,0},{65,1},{66,2},{67,3},{4,70},{5,... | collective-permute-start | bytes 884744 | tf_op jit(solution)/shard_map/ppermute | solution.py:648
  165.7 6.4 %copy-start.9 = (bf16[512,1024]{1,0:T(8,128)(2,1)S(1)}, bf16[512,1024]{1,0:T(8,128)(2,1)}, u32[]{:S(2)}) copy-start(bf16[512,1024]{1,0:T(8,128)(2,1)} %stream_ref.3) | copy-start | bytes 3145732
  165.7 6.4 %copy-start.31 = (s32[5]{0:T(128)S(1)}, s32[5]{0:T(128)}, u32[]{:S(2)}) copy-start(s32[5]{0:T(128)} %copy-done.29) | copy-start | bytes 64
  170.7 3.8 %copy-start.10 = (bf16[256,1152]{1,0:T(8,128)(2,1)S(1)}, bf16[256,1152]{1,0:T(8,128)(2,1)}, u32[]{:S(2)}) copy-start(bf16[256,1152]{1,0:T(8,128)(2,1)} %finish.1.refs_0_) | copy-start | bytes 1769476
  170.7 14.5 %collective-permute-start.19 = (bf16[256,1152]{1,0:T(8,128)(2,1)}, bf16[256,1152]{1,0:T(8,128)(2,1)}, u32[]{:S(2)}, u32[]{:S(2)}) collective-permute-start(bf16[256,1152]{1,0:T(8,128)(2,1)} %finish.1.refs_0_), channel_id=1, source_target_pairs={{0,2},{1,3},{2,0},{3,1},{4,6},{5,7},{6,4},{7,5},{8,10},{9,11},{10,... | collective-permute-start | bytes 1769480 | tf_op jit(solution)/shard_map/ppermute | solution.py:727
  174.5 13.8 %collective-permute-start.20 = (bf16[256,1152]{1,0:T(8,128)(2,1)S(1)}, bf16[256,1152]{1,0:T(8,128)(2,1)S(1)}, u32[]{:S(2)}, u32[]{:S(2)}) collective-permute-start(bf16[256,1152]{1,0:T(8,128)(2,1)S(1)} %copy-done.10), channel_id=1, source_target_pairs={{0,1},{1,0},{2,3},{3,2},{4,5},{5,4},{6,7},{7,6},{8,9},{9,8},{10,11... | collective-permute-start | bytes 1769480 | tf_op jit(solution)/shard_map/ppermute | solution.py:729
  185.2 4.9 %collective-permute-start.21 = (bf16[256,1152]{1,0:T(8,128)(2,1)}, bf16[256,1152]{1,0:T(8,128)(2,1)S(1)}, u32[]{:S(2)}, u32[]{:S(2)}) collective-permute-start(bf16[256,1152]{1,0:T(8,128)(2,1)} %collective-permute-done.19.refs_1_), channel_id=1, source_target_pairs={{0,1},{1,0},{2,3},{3,2},{4,5},{5,4},{6,7},{7,6},{8,9},{9,8},{10,11... | collective-permute-start | bytes 1769480 | tf_op jit(solution)/shard_map/ppermute | solution.py:729
  (16 other events, 13.1 us)

commit v11 on v10

--- a/solution.py
+++ b/solution.py
@@ -55,7 +55,7 @@
     return (col == (row % window) * tokens + row // window).astype(BF)
 
 
-def norm_kernel(here_ref, x_ref, gain_ref, bias_ref, mine_ref, other_ref, xw_ref, stat_ref):
+def norm_kernel(here_ref, x_ref, gain_ref, bias_ref, lifted_ref, xw_ref, stat_ref):
     window, width = gain_ref.shape
     tokens = x_ref.shape[0] // window
     full = window * width
@@ -73,18 +73,15 @@
         )
         xw_ref[w] = p.astype(BF)
     share = width // (RING * RING)
-    lifted = jnp.concatenate(
-        [p[:, at : at + share] for at in range(0, width, share) for p in lifted], axis=1
-    ).astype(BF)
-    half = pl.num_programs(0) // 2
-
-    @pl.when(pl.program_id(0) < half)
-    def _():
-        mine_ref[...] = lifted
-
-    @pl.when(pl.program_id(0) >= half)
-    def _():
-        other_ref[...] = lifted
+    for core in range(2):
+
+        @pl.when(here_ref[0] == core)
+        def _():
+            blocks = [(a, b) for a in range(RING) for b in range(RING)]
+            starts = [(a * RING + b if core == 0 else b * RING + a) * share for a, b in blocks]
+            lifted_ref[...] = jnp.concatenate(
+                [p[:, at : at + share] for at in starts for p in lifted], axis=1
+            ).astype(BF)
 
     lane = lax.broadcasted_iota(jnp.int32, stat_ref.shape, 1)
     stat_ref[...] = jnp.where(lane == 0, mean, inv)
@@ -110,19 +107,17 @@
                 pl.BlockSpec((window, width), lambda i, c: (0, 0)),
             ],
             out_specs=[
-                pl.BlockSpec((block, window * width), lambda i, c: (jnp.minimum(i, steps // 2 - 1), 0)),
-                pl.BlockSpec((block, window * width), lambda i, c: (jnp.maximum(i - steps // 2, 0), 0)),
+                pl.BlockSpec((block, window * width), lambda i, c: (i, 0)),
                 pl.BlockSpec((window, block, width), lambda i, c: (0, i, 0)),
                 pl.BlockSpec((block, 128), lambda i, c: (i, 0)),
             ],
         ),
         out_shape=[
-            shape((merged // 2, window * width), BF),
-            shape((merged // 2, window * width), BF),
+            shape((merged, window * width), BF),
             shape((window, merged, width), BF),
             shape((merged, 128), F32),
         ],
-        compiler_params=params(16),
+        compiler_params=params(58),
         cost_estimate=FREE,
         name="layer_norm",
     )(here, features, gain, bias)
@@ -228,49 +223,78 @@
     return wait
 
 
-def merge_kernel(here_ref, ngain_ref, base_hbm, cot_hbm, *refs):
-    stacks, refs = refs[:RING], refs[RING:]
-    lifted, refs = refs[:-10], refs[-10:]
-    visual_ref, state_ref, stat_ref, held_ref, left_ref, base_ref, cot_ref, w_sems, sems, row_sems = refs
-    wait_weight = fetch(here_ref, stacks, held_ref, w_sems)
-    depth = left_ref.shape[1]
-    block = depth // RING
-    steps = range(RING)
+def product(here_ref, away, stacks, lifted, held_ref, left_ref, sems):
+    second = jnp.where(here_ref[0] == 0, here_ref[3], here_ref[4])
+    block = left_ref.shape[2]
+    rows = lifted[0].shape[0]
     copies = []
-    for step in steps:
-        at = pl.ds(step * block, block)
-        start = 0
-        group = []
-        for index, ref in enumerate(lifted):
-            rows = ref.shape[0]
-            group.append(
-                pltpu.make_async_copy(
-                    ref.at[:, at], left_ref.at[pl.ds(start, rows), at], sems.at[step, index]
-                )
+    for index, ref in enumerate(stacks):
+        place = lax.rem(second + away[index], RING)
+        at = pl.ds(pl.multiple_of(place * block, block), block)
+        group = [pltpu.make_async_copy(ref, held_ref.at[index], sems.at[index, 0])]
+        for i, part in enumerate(lifted):
+            to = left_ref.at[index, pl.ds(i * rows, rows)]
+            group.append(pltpu.make_async_copy(part.at[:, at], to, sems.at[index, 1 + i]))
+        for copy in group:
+            copy.start()
+        copies.append(group)
+
+    def run(total):
+        for index, group in enumerate(copies):
+            for copy in group:
+                copy.wait()
+            part = jnp.dot(
+                left_ref[index], held_ref[index].reshape(block, -1), preferred_element_type=F32
             )
-            group[-1].start()
-            start += rows
-        copies.append(group)
-    row_copies = [
+            total = part if total is None else total + part
+        return total
+
+    return run
+
+
+def product_scratch(stacks, lifted):
+    count = len(stacks)
+    rows, depth = lifted[0].shape
+    return [
+        pltpu.VMEM((count,) + stacks[0].shape, BF),
+        pltpu.VMEM((count, len(lifted) * rows, depth // RING), BF),
+        pltpu.SemaphoreType.DMA((count, 1 + len(lifted))),
+    ]
+
+
+def multiply_kernel(here_ref, *refs):
+    stacks, lifted, (out_ref, *scratch) = refs[: RING - 1], refs[RING - 1 : RING + 1], refs[RING + 1 :]
+    out_ref[...] = product(here_ref, AWAY[: RING - 1], stacks, lifted, *scratch)(None)
+
+
+def multiply(here, stacks, lifted):
+    tokens, width = 2 * lifted[0].shape[0], stacks[0].shape[2]
+    return pl.pallas_call(
+        multiply_kernel,
+        in_specs=[scalars()] + [in_hbm()] * (len(stacks) + len(lifted)),
+        out_specs=whole(),
+        out_shape=shape((tokens, width), F32),
+        scratch_shapes=product_scratch(stacks, lifted),
+        compiler_params=params(40),
+        cost_estimate=FREE,
+        name="multiply",
+    )(here, *stacks, *lifted)
+
+
+def merge_kernel(here_ref, ngain_ref, acc_hbm, base_hbm, cot_hbm, stack_ref, *refs):
+    lifted, refs = refs[:2], refs[2:]
+    visual_ref, state_ref, stat_ref, acc_ref, base_ref, cot_ref, row_sems, *scratch = refs
+    run = product(here_ref, AWAY[RING - 1 :], (stack_ref,), lifted, *scratch)
+    copies = [
         pltpu.make_async_copy(a, b, row_sems.at[i])
-        for i, (a, b) in enumerate(((base_hbm, base_ref), (cot_hbm, cot_ref)))
+        for i, (a, b) in enumerate(((acc_hbm, acc_ref), (base_hbm, base_ref), (cot_hbm, cot_ref)))
     ]
-    for copy in row_copies:
+    for copy in copies:
         copy.start()
-    wait_weight()
-    total = None
-    for step in steps:
-        for copy in copies[step]:
-            copy.wait()
-        part = jnp.dot(
-            left_ref[:, step * block : (step + 1) * block],
-            held_ref[step].reshape(block, -1),
-            preferred_element_type=F32,
-        )
-        total = part if total is None else total + part
-    for copy in row_copies:
+    total = run(None)
+    for copy in copies:
         copy.wait()
-    visual = total.astype(BF)
+    visual = (acc_ref[...] + total).astype(BF)
     visual_ref[...] = visual
     state = base_ref[...].astype(F32) + visual.astype(F32)
     state_ref[...] = state
@@ -284,28 +308,25 @@
     stat_ref[...] = sums.T[: stat_ref.shape[0]]
 
 
-def merge(here, base, cot, ngain, stacks, lifted):
+def merge(here, ngain, acc, base, cot, stack, lifted):
     tokens, width = base.shape
-    depth = lifted[0].shape[1]
     outs = [shape((tokens, width), BF), shape((tokens, width), F32), shape((8, tokens), F32)]
     return pl.pallas_call(
         merge_kernel,
-        in_specs=[scalars(), whole()] + [in_hbm()] * (2 + RING + len(lifted)),
+        in_specs=[scalars(), whole()] + [in_hbm()] * 6,
         out_specs=[whole()] * 3,
         out_shape=outs,
         scratch_shapes=[
-            pltpu.VMEM((RING,) + stacks[0].shape, BF),
-            pltpu.VMEM((tokens, depth), BF),
+            pltpu.VMEM((tokens, width), F32),
             pltpu.VMEM((tokens, width), BF),
             pltpu.VMEM((tokens, width), BF),
-            pltpu.SemaphoreType.DMA((RING,)),
-            pltpu.SemaphoreType.DMA((RING, len(lifted))),
-            pltpu.SemaphoreType.DMA((2,)),
-        ],
-        compiler_params=params(56),
+            pltpu.SemaphoreType.DMA((3,)),
+        ]
+        + product_scratch((stack,), lifted),
+        compiler_params=params(24),
         cost_estimate=FREE,
         name="merge",
-    )(here, ngain, base, cot, *stacks, *lifted)
+    )(here, ngain, acc, base, cot, stack, *lifted)
 
 
 def add_kernel(sums_ref, got_ref, near_ref, turned_ref):
@@ -673,11 +694,16 @@
         packed.reshape(owners, capacity), ("img", "ctx"), split_axis=0, concat_axis=0, tiled=True
     )
     columns = lax.dynamic_slice_in_dim(projection[0], img * cut, cut, axis=2).reshape(-1, cut)
-    gain = ln_gain[0]
-    lifted, lifted_other, xw, stat = layer_norm(here, features[0], gain, ln_bias[0])
     moves = (1, -1, 2)
     near_blocks = [along_ctx(columns, 0, by) for by in moves]
-    asked, lifted, stat, near_blocks = lax.optimization_barrier((asked, lifted, stat, near_blocks))
+    paired = target * (n_img * capacity) + rank + img * capacity
+    partner = lax.ppermute(paired, "img", flip)
+    gain = ln_gain[0]
+    lifted, xw, stat = layer_norm(here, features[0], gain, ln_bias[0])
+    asked, lifted, stat, near_blocks, partner = lax.optimization_barrier(
+        (asked, lifted, stat, near_blocks, partner)
+    )
+    paired = jnp.concatenate([paired, partner]).reshape(-1, 1)
 
     first = stack(here, [columns] + near_blocks)
     asked, first = lax.optimization_barrier((asked, first))
@@ -685,25 +711,25 @@
     asked = asked.reshape(n_img, n_ctx, capacity).transpose(1, 0, 2)
     asked = asked.reshape(slot_count, 1)
     held = collect(asked, stream, cotangent[0], first)
-    paired = target * (n_img * capacity) + rank + img * capacity
-    paired = jnp.concatenate([paired, lax.ppermute(paired, "img", flip)]).reshape(-1, 1)
     came = lax.all_to_all(
         held.reshape(owners, n_img * capacity, width),
         ("img", "ctx"), split_axis=0, concat_axis=0, tiled=True,
     ).reshape(n_img * slot_count, width)
-    stacks = [first] + [along_ctx(first, 1, by) for by in moves]
+
+    stacks = [first] + [along_ctx(first, 1, by) for by in moves[:2]]
+    stacks.append(along_ctx(stacks[1], 1, 1))
 
     pairs = []
     for i in range(n_img):
         for t in range(n_tp):
             x = (2 * (t // 2) + i + (1 if t % 2 == 0 else -1)) % RING
             pairs.append((i * n_tp + t, (x % 2) * n_tp + 2 * (x // 2) + t % 2))
-    next_mine = lax.ppermute(lifted, ("img", "tp"), pairs)
-    next_other = lax.ppermute(next_mine, "tp", core_pairs)
+    lifted = [lifted, lax.ppermute(lifted, ("img", "tp"), pairs)]
 
     own_gain = lax.dynamic_slice_in_dim(norm_gain, img * cut, cut, axis=1)
     base, cot = unpack(paired, came)
-    visual, state, sums = merge(here, base, cot, own_gain, stacks, [lifted, lifted_other, next_mine, next_other])
+    acc = multiply(here, stacks[: RING - 1], lifted)
+    visual, state, sums = merge(here, own_gain, acc, base, cot, stacks[RING - 1], lifted)
 
     near, turned = add(sums, lax.ppermute(sums, "tp", core_pairs))
     stats = [near] + [along_x(near if by == 2 else turned, by) for by in (1, 2, 3)]

time: 194 us -> 179 us (0.923)
  local copies, waits for them, and re-layouts: 24.2 us -> 9.88 us
    all_to_all x1, waiting for transfers between devices: 1.39 us -> 33.8 us  [shards(): lax.all_to_all(held.reshape(owners, n_img * capacity, width), ('img', 'ct...]
    ppermute x6, waiting for transfers between devices: 22.9 us -> 0.93 us  [along_ctx(): return lax.ppermute(array, ('ctx', 'tp'), pairs)]
    unnamed x78 -> x34, local copies, waits for them, and re-layouts: 22.5 us -> 8.25 us
    ppermute x3 -> x2, waiting for transfers between devices: 14.1 us -> 0.01 us  [the longest x1 0.01 us: shards(): partner = lax.ppermute(paired, 'img', flip)]
    pallas_call x1, Pallas kernels: 9.39 us -> 3.53 us  [merge(): pl.pallas_call(merge_kernel, in_specs=[scalars(), whole()] + [in_hbm()] *...]
    pallas_call x0 -> x1, Pallas kernels: none -> 4.78 us  [multiply(): pl.pallas_call(multiply_kernel, in_specs=[scalars()] + [in_hbm()] * (len(...]
    ppermute x7, starting transfers between devices: 9.55 us -> 13.3 us  [along_x(): return lax.ppermute(array, ('img', 'tp'), pairs)]
    ppermute x3 -> x2, starting transfers between devices: 6.51 us -> 4.13 us  [the longest x1 2.84 us: shards(): lifted = [lifted, lax.ppermute(lifted, ('img', 'tp'), pairs)]]
  transfers between devices with their start and end apart: 25 -> 24, of which waited for: 11 -> 11; matrix products, arithmetic and copies ran while one was open for 1% -> 1% of each run, Pallas kernels for 14% -> 18%
where the time goes in v11:
time: 179 us; the launch traced here: 178 us
  waiting for transfers between devices  70.7 us (39%)
  starting transfers between devices  54.7 us (31%)
  Pallas kernels  40.5 us (23%)
  local copies, waits for them, and re-layouts  9.88 us (6%)
    all_to_all x1, waiting for transfers between devices, shards(): lax.all_to_all(held.reshape(owners, n_img * capacity, width), ('img', 'ct...  33.8 us
    ppermute x7, waiting for transfers between devices, along_x(): return lax.ppermute(array, ('img', 'tp'), pairs)  15.9 us
    ppermute x7, starting transfers between devices, along_x(): return lax.ppermute(array, ('img', 'tp'), pairs)  13.3 us
    ppermute x6, starting transfers between devices, along_ctx(): return lax.ppermute(array, ('ctx', 'tp'), pairs)  9.59 us
    unnamed x34, local copies, waits for them, and re-layouts  8.25 us
    ppermute x1, waiting for transfers between devices, shards(): beyond = lax.ppermute(out, 'tp', far_pairs)  7.75 us
    pallas_call x1, Pallas kernels, layer_norm(): pl.pallas_call(norm_kernel, grid_spec=pltpu.PrefetchScalarGridSpec(num_sc...  7.62 us
    all_to_all x1, starting transfers between devices, shards(): lax.all_to_all(held.reshape(owners, n_img * capacity, width), ('img', 'ct...  6.78 us
  transfers between devices with their start and end apart: 24, of which 11 were waited for; matrix products, arithmetic and copies ran while one was open for 1% of the time, Pallas kernels for 18%

profile of v11, /device:TPU:1, one launch (start us, length us, event | category | flops | bytes accessed | tf_op | source)
XLA Modules:
  0.0 177.9 jit_solution(18134172974474150224)
XLA Ops:
  0.7 1.0 copy-done
  1.7 4.5 %collective-permute-start.2 = (bf16[288,512]{1,0:T(8,128)(2,1)S(1)}, bf16[288,512]{1,0:T(8,128)(2,1)S(1)}, u32[]{:S(2)}, u32[]{:S(2)}) collective-permute-start(bf16[288,512]{1,0:T(8,128)(2,1)S(1)} %bitcast.22), channel_id=1, source_target_pairs={{0,8},{1,33},{2,10},{3,35},{4,12},{5,37},{6,14},{7,39},{8,0},{9,41... | collective-permute-start | bytes 884744 | tf_op jit(solution)/shard_map/ppermute | solution.py:681
  6.7 1.0 collective-permute-start
  7.7 0.8 pad_add_fusion
  8.7 1.3 collective-permute-start.3
  10.8 5.9 %all-to-all-start = ((s32[32,1,16]{2,1,0:T(1,128)}), s32[32,1,16]{2,1,0:T(1,128)S(1)}, u32[]{:S(2)}, u32[]{:S(2)}) async-start(s32[32,1,16]{2,1,0:T(1,128)} %bitcast.5), calls=%async_computation | async-start | bytes 32768 | tf_op jit(solution)/shard_map/all_to_all | solution.py:693
  17.4 7.6 %layer_norm.1 = (bf16[256,4608]{1,0:T(8,128)(2,1)}, bf16[4,256,1152]{2,1,0:T(8,128)(2,1)}, f32[256,128]{1,0:T(8,128)}) custom-call(s32[5]{0:T(128)} %stack.24.here_ref.refs_0_, bf16[1024,1152]{1,0:T(8,128)(2,1)} %bitcast.27, bf16[4,1152]{1,0:T(4,128)(2,1)} %bitcast.31, bf16[4,1152]{1,0:T(4,128)(2,1)} %bitcast.33), custom_call_target="tpu_custom_call" | custom-call | tf_op jit(solution)/shard_map/layer_norm/pallas_call | solution.py:96
  25.1 0.8 stack.25.refs_0_.after_ref.refs_6_
  25.9 2.8 %collective-permute-start.6 = (bf16[256,4608]{1,0:T(8,128)(2,1)}, bf16[256,4608]{1,0:T(8,128)(2,1)}, u32[]{:S(2)}, u32[]{:S(2)}) collective-permute-start(bf16[256,4608]{1,0:T(8,128)(2,1)} %get-tuple-element.48.refs_3_.refs_0_), channel_id=1, source_target_pairs={{0,64},{1,67},{2,66},{3,65},{64,2},{65,1},{66,0},{67,3},{4,68},{5,... | collective-permute-start | bytes 7077896 | tf_op jit(solution)/shard_map/ppermute | solution.py:727
  28.8 1.2 collective-permute-start.4
  30.1 1.2 copy-done.4
  31.3 1.2 copy-done.9
  32.6 1.3 collect.1
  33.9 1.4 copy-done.3
  35.3 6.8 %all-to-all-start.1 = ((bf16[32,32,1024]{2,1,0:T(8,128)(2,1)}), bf16[32,32,1024]{2,1,0:T(8,128)(2,1)}, u32[]{:S(2)}, u32[]{:S(2)}) async-start(bf16[32,32,1024]{2,1,0:T(8,128)(2,1)} %bitcast.21), calls=%async_computation.1 | async-start | bytes 4194304 | tf_op jit(solution)/shard_map/all_to_all | solution.py:714
  42.1 2.4 %collective-permute-start.5 = (bf16[4,288,512]{2,1,0:T(8,128)(2,1)S(1)}, bf16[4,288,512]{2,1,0:T(8,128)(2,1)}, u32[]{:S(2)}, u32[]{:S(2)}) collective-permute-start(bf16[4,288,512]{2,1,0:T(8,128)(2,1)S(1)} %stack.25.refs_0_.after_ref.refs_6_), channel_id=1, source_target_pairs={{0,48},{1,13},{2,50},{3,15},{4,52},{5,1},{6,54},{7,3},{8,56},{9,5}... | collective-permute-start | bytes 3538952 | tf_op jit(solution)/shard_map/ppermute | solution.py:681
  44.5 0.9 collective-permute-done.4.refs_1_.refs_7_
  45.6 33.8 %all-to-all-done.1 = bf16[32,32,1024]{2,1,0:T(8,128)(2,1)} async-done(((bf16[32,32,1024]{2,1,0:T(8,128)(2,1)}), bf16[32,32,1024]{2,1,0:T(8,128)(2,1)}, u32[]{:S(2)}, u32[]{:S(2)}) %all-to-all-start.1) | async-done | bytes 2097184 | tf_op jit(solution)/shard_map/all_to_all | solution.py:714
  79.4 2.9 %unpack.1 = (bf16[512,512]{1,0:T(8,128)(2,1)S(1)}, bf16[512,512]{1,0:T(8,128)(2,1)S(1)}) custom-call(s32[512,1]{1,0:T(8,128)S(1)} %copy.28.slot_ref, bf16[1024,1024]{1,0:T(8,128)(2,1)} %bitcast.17.came_ref), custom_call_target="tpu_custom_call" | custom-call | tf_op jit(solution)/shard_map/unpack/pallas_call | solution.py:168
  82.3 4.8 %multiply.1.acc_hbm = f32[512,512]{1,0:T(8,128)S(1)} custom-call(s32[5]{0:T(128)S(1)} %copy-done.12, bf16[4,288,512]{2,1,0:T(8,128)(2,1)S(1)} %stack.25.refs_0_.after_ref.refs_6_, bf16[4,288,512]{2,1,0:T(8,128)(2,1)S(1)} %collective-permute-done.4.refs_1_.refs_7_, bf16[4,288,512]{2,1,0:T(8,128)(2,1)} %collective-permute-done.5.refs_2_.refs_8_, ...), custom_call_target="tpu_custom_call" | custom-call | tf_op jit(solution)/shard_map/multiply/pallas_call | solution.py:272
  87.1 3.5 %merge.1 = (bf16[512,512]{1,0:T(8,128)(2,1)S(1)}, f32[512,512]{1,0:T(8,128)S(1)}, f32[8,512]{1,0:T(8,128)S(1)}) custom-call(s32[5]{0:T(128)S(1)} %copy-done.12, bf16[1,512]{1,0:T(2,128)(2,1)S(1)} %constant_dynamic-slice_fusion.1.ngain_ref.refs_1_, f32[512,512]{1,0:T(8,128)S(1)} %multiply.1.acc_hbm, bf16[512,512]{1,0:T(8,128)(2,1)S(1)} %get-tuple-element.50.base_hbm, ...), custom_call_target="tpu_custom_call" | custom-call | tf_op jit(solution)/shard_map/merge/pallas_call | solution.py:314
  91.1 0.8 collective-permute-done.8.got_ref
  92.0 6.6 %collective-permute-start.11 = (f32[8,512]{1,0:T(8,128)S(1)}, f32[8,512]{1,0:T(8,128)S(1)}, u32[]{:S(2)}, u32[]{:S(2)}) collective-permute-start(f32[8,512]{1,0:T(8,128)S(1)} %get-tuple-element.56), channel_id=1, source_target_pairs={{0,66},{1,67},{2,64},{3,65},{64,0},{65,1},{66,2},{67,3},{4,70},{5,... | collective-permute-start | bytes 49160 | tf_op jit(solution)/shard_map/ppermute | solution.py:669
  98.6 1.2 collective-permute-start.10
  99.8 1.4 pack.1
  101.2 1.2 collective-permute-done.9.refs_3_
  103.4 5.5 %backward.1 = (bf16[256,4608]{1,0:T(8,128)(2,1)S(1)}, bf16[256,4608]{1,0:T(8,128)(2,1)S(1)}) custom-call(s32[5]{0:T(128)S(1)} %copy-done.12, bf16[1,512]{1,0:T(2,128)(2,1)S(1)} %constant_dynamic-slice_fusion.1.ngain_ref.refs_1_, f32[8,512]{1,0:T(8,128)S(1)} %get-tuple-element.57.after_ref.refs_2_, f32[8,512]{1,0:T(8,128)S(1)} %collective-permute-done.9.refs_3_, ...), custom_call_target="tpu_custom_call" | custom-call | tf_op jit(solution)/shard_map/backward/pallas_call | solution.py:450
  108.9 5.4 %collective-permute-done.12.after_ref.crossed_ref = bf16[512,512]{1,0:T(8,128)(2,1)S(1)} collective-permute-done((bf16[512,512]{1,0:T(8,128)(2,1)S(1)}, bf16[512,512]{1,0:T(8,128)(2,1)S(1)}, u32[]{:S(2)}, u32[]{:S(2)}) %collective-permute-start.12) | collective-permute-done | bytes 524320 | tf_op jit(solution)/shard_map/ppermute | solution.py:738
  114.3 2.7 %collective-permute-start.13 = (bf16[256,4608]{1,0:T(8,128)(2,1)S(1)}, bf16[256,4608]{1,0:T(8,128)(2,1)S(1)}, u32[]{:S(2)}, u32[]{:S(2)}) collective-permute-start(bf16[256,4608]{1,0:T(8,128)(2,1)S(1)} %get-tuple-element.66), channel_id=1, source_target_pairs={{0,1},{1,0},{2,3},{3,2},{4,5},{5,4},{6,7},{7,6},{8,9},{9,8},{10,11... | collective-permute-start | bytes 7077896 | tf_op jit(solution)/shard_map/ppermute | solution.py:742
  117.0 4.2 %collective-permute-done.13.got_ref = bf16[256,4608]{1,0:T(8,128)(2,1)S(1)} collective-permute-done((bf16[256,4608]{1,0:T(8,128)(2,1)S(1)}, bf16[256,4608]{1,0:T(8,128)(2,1)S(1)}, u32[]{:S(2)}, u32[]{:S(2)}) %collective-permute-start.13) | collective-permute-done | bytes 2359328 | tf_op jit(solution)/shard_map/ppermute | solution.py:742
  121.2 1.6 pair.1
  123.0 0.8 copy-done.10
  124.5 2.0 %collective-permute-start.15 = (bf16[64,4608]{1,0:T(8,128)(2,1)}, bf16[64,4608]{1,0:T(8,128)(2,1)S(1)}, u32[]{:S(2)}, u32[]{:S(2)}) collective-permute-start(bf16[64,4608]{1,0:T(8,128)(2,1)} %get-tuple-element.69), channel_id=1, source_target_pairs={{0,66},{1,67},{2,64},{3,65},{64,0},{65,1},{66,2},{67,3},{4,70},{5,... | collective-permute-start | bytes 1769480 | tf_op jit(solution)/shard_map/ppermute | solution.py:669
  126.5 1.0 braid.1
  127.6 3.7 %all-to-all-start.2 = ((bf16[16,2,32,512]{3,2,1,0:T(8,128)(2,1)}), bf16[16,2,32,512]{3,2,1,0:T(8,128)(2,1)S(1)}, u32[]{:S(2)}, u32[]{:S(2)}) async-start(bf16[16,2,32,512]{3,2,1,0:T(8,128)(2,1)} %braid.1), calls=%async_computation.2 | async-start | bytes 2097152 | tf_op jit(solution)/shard_map/all_to_all | solution.py:749
  131.2 8.6 %collective-permute-done.14.from_last_ref = bf16[64,4608]{1,0:T(8,128)(2,1)S(1)} collective-permute-done((bf16[64,4608]{1,0:T(8,128)(2,1)}, bf16[64,4608]{1,0:T(8,128)(2,1)S(1)}, u32[]{:S(2)}, u32[]{:S(2)}) %collective-permute-start.14) | collective-permute-done | bytes 589856 | tf_op jit(solution)/shard_map/ppermute | solution.py:669
  139.8 1.5 copy-done.11
  141.8 2.4 %collective-permute-start.17 = (bf16[32,4608]{1,0:T(8,128)(2,1)S(1)}, bf16[32,4608]{1,0:T(8,128)(2,1)S(1)}, u32[]{:S(2)}, u32[]{:S(2)}) collective-permute-start(bf16[32,4608]{1,0:T(8,128)(2,1)S(1)} %get-tuple-element.72), channel_id=1, source_target_pairs={{0,66},{1,67},{2,64},{3,65},{64,0},{65,1},{66,2},{67,3},{4,70},{5,... | collective-permute-start | bytes 884744 | tf_op jit(solution)/shard_map/ppermute | solution.py:669
  144.2 5.8 %collective-permute-done.16.late_last_ref = bf16[32,4608]{1,0:T(8,128)(2,1)S(1)} collective-permute-done((bf16[32,4608]{1,0:T(8,128)(2,1)S(1)}, bf16[32,4608]{1,0:T(8,128)(2,1)S(1)}, u32[]{:S(2)}, u32[]{:S(2)}) %collective-permute-start.16) | collective-permute-done | bytes 294944 | tf_op jit(solution)/shard_map/ppermute | solution.py:669
  150.1 0.7 copy-done.14
  150.9 5.0 %finish.1.refs_0_ = bf16[256,1152]{1,0:T(8,128)(2,1)} custom-call(s32[5]{0:T(128)} %stack.24.here_ref.refs_0_, bf16[256,4608]{1,0:T(8,128)(2,1)} %copy-done.1, bf16[256,4608]{1,0:T(8,128)(2,1)} %copy-done.2, bf16[64,4608]{1,0:T(8,128)(2,1)} %copy-done.7, bf16[64,4608]{1,0:T(8,128)(2,1)} %copy-done.8, bf16[32,4608]{1,0:T(8,128)(2,1)} %copy-done.14, ...), custom_call_target="tpu_custom_call" | custom-call | tf_op jit(solution)/shard_map/finish/pallas_call | solution.py:561
  155.8 1.4 collective-permute-start.18
  157.2 2.4 %place.1 = bf16[512,1024]{1,0:T(8,128)(2,1)} custom-call(s32[5]{0:T(128)S(1)} %copy-done.13, s32[512,1]{1,0:T(8,128)S(1)} %reshape.38.pos_ref, bf16[16,2,32,512]{3,2,1,0:T(8,128)(2,1)S(1)} %all-to-all-done.2.came_ref, bf16[512,1024]{1,0:T(8,128)(2,1)S(1)} %copy-done.5), custom_call_target="tpu_custom_call" | custom-call | tf_op jit(solution)/shard_map/place/pallas_call | solution.py:602
  159.6 3.0 %collective-permute-start.19 = (bf16[256,1152]{1,0:T(8,128)(2,1)S(1)}, bf16[256,1152]{1,0:T(8,128)(2,1)S(1)}, u32[]{:S(2)}, u32[]{:S(2)}) collective-permute-start(bf16[256,1152]{1,0:T(8,128)(2,1)S(1)} %copy-done.6), channel_id=1, source_target_pairs={{0,1},{1,0},{2,3},{3,2},{4,5},{5,4},{6,7},{7,6},{8,9},{9,8},{10,11... | collective-permute-start | bytes 1769480 | tf_op jit(solution)/shard_map/ppermute | solution.py:755
  162.6 7.7 %collective-permute-done.18.refs_1_ = bf16[256,1152]{1,0:T(8,128)(2,1)} collective-permute-done((bf16[256,1152]{1,0:T(8,128)(2,1)}, bf16[256,1152]{1,0:T(8,128)(2,1)}, u32[]{:S(2)}, u32[]{:S(2)}) %collective-permute-start.18) | collective-permute-done | bytes 589856 | tf_op jit(solution)/shard_map/ppermute | solution.py:753
  170.4 3.0 %collective-permute-start.20 = (bf16[256,1152]{1,0:T(8,128)(2,1)}, bf16[256,1152]{1,0:T(8,128)(2,1)S(1)}, u32[]{:S(2)}, u32[]{:S(2)}) collective-permute-start(bf16[256,1152]{1,0:T(8,128)(2,1)} %collective-permute-done.18.refs_1_), channel_id=1, source_target_pairs={{0,1},{1,0},{2,3},{3,2},{4,5},{5,4},{6,7},{7,6},{8,9},{9,8},{10,11... | collective-permute-start | bytes 1769480 | tf_op jit(solution)/shard_map/ppermute | solution.py:755
  173.4 1.8 %collective-permute-done.20.refs_3_ = bf16[256,1152]{1,0:T(8,128)(2,1)S(1)} collective-permute-done((bf16[256,1152]{1,0:T(8,128)(2,1)}, bf16[256,1152]{1,0:T(8,128)(2,1)S(1)}, u32[]{:S(2)}, u32[]{:S(2)}) %collective-permute-start.20) | collective-permute-done | bytes 589856 | tf_op jit(solution)/shard_map/ppermute | solution.py:755
  175.2 2.5 %lay.1 = bf16[1024,1152]{1,0:T(8,128)(2,1)} custom-call(s32[5]{0:T(128)S(1)} %copy-done.13, bf16[256,1152]{1,0:T(8,128)(2,1)S(1)} %copy-done.6, bf16[256,1152]{1,0:T(8,128)(2,1)} %collective-permute-done.18.refs_1_, bf16[256,1152]{1,0:T(8,128)(2,1)S(1)} %collective-permute-done.19.refs_2_, bf16[256,1152]{1,0:T(8,128)(2,1)S(1)} %collective-permute-done.20.refs_3_), custom_call_target="tpu_custom_call" | custom-call | tf_op jit(solution)/shard_map/lay/pallas_call | solution.py:629
  (62 shorter events, 5.5 us)
Async XLA Ops:
  0.6 1.1 copy-start
  1.7 23.3 %collective-permute-start.2 = (bf16[288,512]{1,0:T(8,128)(2,1)S(1)}, bf16[288,512]{1,0:T(8,128)(2,1)S(1)}, u32[]{:S(2)}, u32[]{:S(2)}) collective-permute-start(bf16[288,512]{1,0:T(8,128)(2,1)S(1)} %bitcast.22), channel_id=1, source_target_pairs={{0,8},{1,33},{2,10},{3,35},{4,12},{5,37},{6,14},{7,39},{8,0},{9,41... | collective-permute-start | bytes 884744 | tf_op jit(solution)/shard_map/ppermute | solution.py:681
  6.2 18.8 %collective-permute-start.1 = (bf16[288,512]{1,0:T(8,128)(2,1)S(1)}, bf16[288,512]{1,0:T(8,128)(2,1)S(1)}, u32[]{:S(2)}, u32[]{:S(2)}) collective-permute-start(bf16[288,512]{1,0:T(8,128)(2,1)S(1)} %bitcast.23), channel_id=1, source_target_pairs={{0,12},{1,49},{2,14},{3,51},{4,0},{5,53},{6,2},{7,55},{8,4},{9,57}... | collective-permute-start | bytes 884744 | tf_op jit(solution)/shard_map/ppermute | solution.py:681
  6.7 18.4 %collective-permute-start = (bf16[288,512]{1,0:T(8,128)(2,1)S(1)}, bf16[288,512]{1,0:T(8,128)(2,1)S(1)}, u32[]{:S(2)}, u32[]{:S(2)}) collective-permute-start(bf16[288,512]{1,0:T(8,128)(2,1)S(1)} %bitcast.24), channel_id=1, source_target_pairs={{0,4},{1,17},{2,6},{3,19},{4,8},{5,21},{6,10},{7,23},{8,12},{9,25}... | collective-permute-start | bytes 884744 | tf_op jit(solution)/shard_map/ppermute | solution.py:681
  8.7 16.3 %collective-permute-start.3 = (s32[256]{0:T(256)S(1)}, s32[256]{0:T(256)S(1)}, u32[]{:S(2)}, u32[]{:S(2)}) collective-permute-start(s32[256]{0:T(256)S(1)} %get-tuple-element.80), channel_id=1, source_target_pairs={{0,64},{64,0},{1,65},{65,1},{2,66},{66,2},{3,67},{67,3},{4,68},{68... | collective-permute-start | bytes 3080 | tf_op jit(solution)/shard_map/ppermute | solution.py:700
  10.8 14.2 %all-to-all-start = ((s32[32,1,16]{2,1,0:T(1,128)}), s32[32,1,16]{2,1,0:T(1,128)S(1)}, u32[]{:S(2)}, u32[]{:S(2)}) async-start(s32[32,1,16]{2,1,0:T(1,128)} %bitcast.5), calls=%async_computation | async-start | bytes 32768 | tf_op jit(solution)/shard_map/all_to_all | solution.py:693
  17.4 7.7 %copy-start.12 = (s32[5]{0:T(128)S(1)}, s32[5]{0:T(128)}, u32[]{:S(2)}) copy-start(s32[5]{0:T(128)} %stack.24.here_ref.refs_0_) | copy-start | bytes 64
  25.9 56.4 %collective-permute-start.6 = (bf16[256,4608]{1,0:T(8,128)(2,1)}, bf16[256,4608]{1,0:T(8,128)(2,1)}, u32[]{:S(2)}, u32[]{:S(2)}) collective-permute-start(bf16[256,4608]{1,0:T(8,128)(2,1)} %get-tuple-element.48.refs_3_.refs_0_), channel_id=1, source_target_pairs={{0,64},{1,67},{2,66},{3,65},{64,2},{65,1},{66,0},{67,3},{4,68},{5,... | collective-permute-start | bytes 7077896 | tf_op jit(solution)/shard_map/ppermute | solution.py:727
  28.8 16.7 %collective-permute-start.4 = (bf16[4,288,512]{2,1,0:T(8,128)(2,1)S(1)}, bf16[4,288,512]{2,1,0:T(8,128)(2,1)S(1)}, u32[]{:S(2)}, u32[]{:S(2)}) collective-permute-start(bf16[4,288,512]{2,1,0:T(8,128)(2,1)S(1)} %stack.25.refs_0_.after_ref.refs_6_), channel_id=1, source_target_pairs={{0,16},{1,5},{2,18},{3,7},{4,20},{5,9},{6,22},{7,11},{8,24},{9,13}... | collective-permute-start | bytes 3538952 | tf_op jit(solution)/shard_map/ppermute | solution.py:681
  30.1 1.2 copy-start.4
  31.3 1.2 copy-start.9
  33.9 1.4 copy-start.3
  35.3 10.2 %copy-start.16 = (bf16[1,1024]{1,0:T(2,128)(2,1)S(1)}, bf16[1,1024]{1,0:T(2,128)(2,1)}, u32[]{:S(2)}) copy-start(bf16[1,1024]{1,0:T(2,128)(2,1)} %param.13) | copy-start | bytes 6148
  35.3 44.1 %all-to-all-start.1 = ((bf16[32,32,1024]{2,1,0:T(8,128)(2,1)}), bf16[32,32,1024]{2,1,0:T(8,128)(2,1)}, u32[]{:S(2)}, u32[]{:S(2)}) async-start(bf16[32,32,1024]{2,1,0:T(8,128)(2,1)} %bitcast.21), calls=%async_computation.1 | async-start | bytes 4194304 | tf_op jit(solution)/shard_map/all_to_all | solution.py:714
  42.1 40.2 %collective-permute-start.5 = (bf16[4,288,512]{2,1,0:T(8,128)(2,1)S(1)}, bf16[4,288,512]{2,1,0:T(8,128)(2,1)}, u32[]{:S(2)}, u32[]{:S(2)}) collective-permute-start(bf16[4,288,512]{2,1,0:T(8,128)(2,1)S(1)} %stack.25.refs_0_.after_ref.refs_6_), channel_id=1, source_target_pairs={{0,48},{1,13},{2,50},{3,15},{4,52},{5,1},{6,54},{7,3},{8,56},{9,5}... | collective-permute-start | bytes 3538952 | tf_op jit(solution)/shard_map/ppermute | solution.py:681
  45.4 41.7 %collective-permute-start.7 = (bf16[4,288,512]{2,1,0:T(8,128)(2,1)S(1)}, bf16[4,288,512]{2,1,0:T(8,128)(2,1)}, u32[]{:S(2)}, u32[]{:S(2)}) collective-permute-start(bf16[4,288,512]{2,1,0:T(8,128)(2,1)S(1)} %collective-permute-done.4.refs_1_.refs_7_), channel_id=1, source_target_pairs={{0,16},{1,5},{2,18},{3,7},{4,20},{5,9},{6,22},{7,11},{8,24},{9,13}... | collective-permute-start | bytes 3538952 | tf_op jit(solution)/shard_map/ppermute | solution.py:681
  90.6 1.3 collective-permute-start.8
  92.0 9.2 %collective-permute-start.11 = (f32[8,512]{1,0:T(8,128)S(1)}, f32[8,512]{1,0:T(8,128)S(1)}, u32[]{:S(2)}, u32[]{:S(2)}) collective-permute-start(f32[8,512]{1,0:T(8,128)S(1)} %get-tuple-element.56), channel_id=1, source_target_pairs={{0,66},{1,67},{2,64},{3,65},{64,0},{65,1},{66,2},{67,3},{4,70},{5,... | collective-permute-start | bytes 49160 | tf_op jit(solution)/shard_map/ppermute | solution.py:669
  98.6 3.8 %collective-permute-start.9 = (f32[8,512]{1,0:T(8,128)S(1)}, f32[8,512]{1,0:T(8,128)S(1)}, u32[]{:S(2)}, u32[]{:S(2)}) collective-permute-start(f32[8,512]{1,0:T(8,128)S(1)} %get-tuple-element.56), channel_id=1, source_target_pairs={{0,64},{1,65},{2,66},{3,67},{64,2},{65,3},{66,0},{67,1},{4,68},{5,... | collective-permute-start | bytes 49160 | tf_op jit(solution)/shard_map/ppermute | solution.py:669
  98.6 4.1 %collective-permute-start.10 = (f32[8,512]{1,0:T(8,128)S(1)}, f32[8,512]{1,0:T(8,128)S(1)}, u32[]{:S(2)}, u32[]{:S(2)}) collective-permute-start(f32[8,512]{1,0:T(8,128)S(1)} %get-tuple-element.57.after_ref.refs_2_), channel_id=1, source_target_pairs={{0,2},{1,3},{2,0},{3,1},{64,66},{65,67},{66,64},{67,65},{4,6},{5,7... | collective-permute-start | bytes 49160 | tf_op jit(solution)/shard_map/ppermute | solution.py:669
  102.7 11.6 %collective-permute-start.12 = (bf16[512,512]{1,0:T(8,128)(2,1)S(1)}, bf16[512,512]{1,0:T(8,128)(2,1)S(1)}, u32[]{:S(2)}, u32[]{:S(2)}) collective-permute-start(bf16[512,512]{1,0:T(8,128)(2,1)S(1)} %get-tuple-element.64), channel_id=1, source_target_pairs={{0,64},{64,0},{1,65},{65,1},{2,66},{66,2},{3,67},{67,3},{4,68},{68... | collective-permute-start | bytes 1572872 | tf_op jit(solution)/shard_map/ppermute | solution.py:738
  108.9 13.9 %copy-start.1 = (bf16[256,4608]{1,0:T(8,128)(2,1)}, bf16[256,4608]{1,0:T(8,128)(2,1)S(1)}, u32[]{:S(2)}) copy-start(bf16[256,4608]{1,0:T(8,128)(2,1)S(1)} %get-tuple-element.65.own_ref) | copy-start | bytes 7077892
  114.3 6.9 %collective-permute-start.13 = (bf16[256,4608]{1,0:T(8,128)(2,1)S(1)}, bf16[256,4608]{1,0:T(8,128)(2,1)S(1)}, u32[]{:S(2)}, u32[]{:S(2)}) collective-permute-start(bf16[256,4608]{1,0:T(8,128)(2,1)S(1)} %get-tuple-element.66), channel_id=1, source_target_pairs={{0,1},{1,0},{2,3},{3,2},{4,5},{5,4},{6,7},{7,6},{8,9},{9,8},{10,11... | collective-permute-start | bytes 7077896 | tf_op jit(solution)/shard_map/ppermute | solution.py:742
  121.2 1.8 %copy-start.2 = (bf16[256,4608]{1,0:T(8,128)(2,1)}, bf16[256,4608]{1,0:T(8,128)(2,1)S(1)}, u32[]{:S(2)}) copy-start(bf16[256,4608]{1,0:T(8,128)(2,1)S(1)} %collective-permute-done.13.got_ref) | copy-start | bytes 7077892
  123.0 0.8 copy-start.10
  123.9 16.0 %collective-permute-start.14 = (bf16[64,4608]{1,0:T(8,128)(2,1)}, bf16[64,4608]{1,0:T(8,128)(2,1)S(1)}, u32[]{:S(2)}, u32[]{:S(2)}) collective-permute-start(bf16[64,4608]{1,0:T(8,128)(2,1)} %get-tuple-element.68), channel_id=1, source_target_pairs={{0,64},{1,65},{2,66},{3,67},{64,2},{65,3},{66,0},{67,1},{4,68},{5,... | collective-permute-start | bytes 1769480 | tf_op jit(solution)/shard_map/ppermute | solution.py:669
  124.5 15.3 %collective-permute-start.15 = (bf16[64,4608]{1,0:T(8,128)(2,1)}, bf16[64,4608]{1,0:T(8,128)(2,1)S(1)}, u32[]{:S(2)}, u32[]{:S(2)}) collective-permute-start(bf16[64,4608]{1,0:T(8,128)(2,1)} %get-tuple-element.69), channel_id=1, source_target_pairs={{0,66},{1,67},{2,64},{3,65},{64,0},{65,1},{66,2},{67,3},{4,70},{5,... | collective-permute-start | bytes 1769480 | tf_op jit(solution)/shard_map/ppermute | solution.py:669
  127.6 29.7 %all-to-all-start.2 = ((bf16[16,2,32,512]{3,2,1,0:T(8,128)(2,1)}), bf16[16,2,32,512]{3,2,1,0:T(8,128)(2,1)S(1)}, u32[]{:S(2)}, u32[]{:S(2)}) async-start(bf16[16,2,32,512]{3,2,1,0:T(8,128)(2,1)} %braid.1), calls=%async_computation.2 | async-start | bytes 2097152 | tf_op jit(solution)/shard_map/all_to_all | solution.py:749
  139.8 10.2 %copy-start.7 = (bf16[64,4608]{1,0:T(8,128)(2,1)}, bf16[64,4608]{1,0:T(8,128)(2,1)S(1)}, u32[]{:S(2)}) copy-start(bf16[64,4608]{1,0:T(8,128)(2,1)S(1)} %collective-permute-done.14.from_last_ref) | copy-start | bytes 1769476
  139.8 10.2 %copy-start.8 = (bf16[64,4608]{1,0:T(8,128)(2,1)}, bf16[64,4608]{1,0:T(8,128)(2,1)S(1)}, u32[]{:S(2)}) copy-start(bf16[64,4608]{1,0:T(8,128)(2,1)S(1)} %collective-permute-done.15.from_next_ref) | copy-start | bytes 1769476
  139.8 1.5 copy-start.11
  141.5 8.6 %collective-permute-start.16 = (bf16[32,4608]{1,0:T(8,128)(2,1)S(1)}, bf16[32,4608]{1,0:T(8,128)(2,1)S(1)}, u32[]{:S(2)}, u32[]{:S(2)}) collective-permute-start(bf16[32,4608]{1,0:T(8,128)(2,1)S(1)} %get-tuple-element.71), channel_id=1, source_target_pairs={{0,64},{1,65},{2,66},{3,67},{64,2},{65,3},{66,0},{67,1},{4,68},{5,... | collective-permute-start | bytes 884744 | tf_op jit(solution)/shard_map/ppermute | solution.py:669
  141.8 8.2 %collective-permute-start.17 = (bf16[32,4608]{1,0:T(8,128)(2,1)S(1)}, bf16[32,4608]{1,0:T(8,128)(2,1)S(1)}, u32[]{:S(2)}, u32[]{:S(2)}) collective-permute-start(bf16[32,4608]{1,0:T(8,128)(2,1)S(1)} %get-tuple-element.72), channel_id=1, source_target_pairs={{0,66},{1,67},{2,64},{3,65},{64,0},{65,1},{66,2},{67,3},{4,70},{5,... | collective-permute-start | bytes 884744 | tf_op jit(solution)/shard_map/ppermute | solution.py:669
  150.0 0.7 copy-start.14
  150.1 0.8 copy-start.15
  150.9 6.4 %copy-start.5 = (bf16[512,1024]{1,0:T(8,128)(2,1)S(1)}, bf16[512,1024]{1,0:T(8,128)(2,1)}, u32[]{:S(2)}) copy-start(bf16[512,1024]{1,0:T(8,128)(2,1)} %stream_ref.3) | copy-start | bytes 3145732
  150.9 6.4 %copy-start.13 = (s32[5]{0:T(128)S(1)}, s32[5]{0:T(128)}, u32[]{:S(2)}) copy-start(s32[5]{0:T(128)} %stack.24.here_ref.refs_0_) | copy-start | bytes 64
  155.8 3.8 %copy-start.6 = (bf16[256,1152]{1,0:T(8,128)(2,1)S(1)}, bf16[256,1152]{1,0:T(8,128)(2,1)}, u32[]{:S(2)}) copy-start(bf16[256,1152]{1,0:T(8,128)(2,1)} %finish.1.refs_0_) | copy-start | bytes 1769476
  155.8 14.5 %collective-permute-start.18 = (bf16[256,1152]{1,0:T(8,128)(2,1)}, bf16[256,1152]{1,0:T(8,128)(2,1)}, u32[]{:S(2)}, u32[]{:S(2)}) collective-permute-start(bf16[256,1152]{1,0:T(8,128)(2,1)} %finish.1.refs_0_), channel_id=1, source_target_pairs={{0,2},{1,3},{2,0},{3,1},{4,6},{5,7},{6,4},{7,5},{8,10},{9,11},{10,... | collective-permute-start | bytes 1769480 | tf_op jit(solution)/shard_map/ppermute | solution.py:753
  159.6 13.8 %collective-permute-start.19 = (bf16[256,1152]{1,0:T(8,128)(2,1)S(1)}, bf16[256,1152]{1,0:T(8,128)(2,1)S(1)}, u32[]{:S(2)}, u32[]{:S(2)}) collective-permute-start(bf16[256,1152]{1,0:T(8,128)(2,1)S(1)} %copy-done.6), channel_id=1, source_target_pairs={{0,1},{1,0},{2,3},{3,2},{4,5},{5,4},{6,7},{7,6},{8,9},{9,8},{10,11... | collective-permute-start | bytes 1769480 | tf_op jit(solution)/shard_map/ppermute | solution.py:755
  170.4 4.9 %collective-permute-start.20 = (bf16[256,1152]{1,0:T(8,128)(2,1)}, bf16[256,1152]{1,0:T(8,128)(2,1)S(1)}, u32[]{:S(2)}, u32[]{:S(2)}) collective-permute-start(bf16[256,1152]{1,0:T(8,128)(2,1)} %collective-permute-done.18.refs_1_), channel_id=1, source_target_pairs={{0,1},{1,0},{2,3},{3,2},{4,5},{5,4},{6,7},{7,6},{8,9},{9,8},{10,11... | collective-permute-start | bytes 1769480 | tf_op jit(solution)/shard_map/ppermute | solution.py:755

commit v12 on v11

--- a/solution.py
+++ b/solution.py
@@ -55,7 +55,7 @@
     return (col == (row % window) * tokens + row // window).astype(BF)
 
 
-def norm_kernel(here_ref, x_ref, gain_ref, bias_ref, lifted_ref, xw_ref, stat_ref):
+def norm_kernel(here_ref, x_ref, gain_ref, bias_ref, first_ref, second_ref, xw_ref, stat_ref):
     window, width = gain_ref.shape
     tokens = x_ref.shape[0] // window
     full = window * width
@@ -79,9 +79,19 @@
         def _():
             blocks = [(a, b) for a in range(RING) for b in range(RING)]
             starts = [(a * RING + b if core == 0 else b * RING + a) * share for a, b in blocks]
-            lifted_ref[...] = jnp.concatenate(
+            ordered = jnp.concatenate(
                 [p[:, at : at + share] for at in starts for p in lifted], axis=1
             ).astype(BF)
+            half = pl.num_programs(0) // 2
+
+            @pl.when(pl.program_id(0) < half)
+            def _():
+                first_ref[...] = ordered
+
+            @pl.when(pl.program_id(0) >= half)
+            def _():
+                second_ref[...] = ordered
+
 
     lane = lax.broadcasted_iota(jnp.int32, stat_ref.shape, 1)
     stat_ref[...] = jnp.where(lane == 0, mean, inv)
@@ -107,13 +117,15 @@
                 pl.BlockSpec((window, width), lambda i, c: (0, 0)),
             ],
             out_specs=[
-                pl.BlockSpec((block, window * width), lambda i, c: (i, 0)),
+                pl.BlockSpec((block, window * width), lambda i, c: (jnp.minimum(i, steps // 2 - 1), 0)),
+                pl.BlockSpec((block, window * width), lambda i, c: (jnp.maximum(i - steps // 2, 0), 0)),
                 pl.BlockSpec((window, block, width), lambda i, c: (0, i, 0)),
                 pl.BlockSpec((block, 128), lambda i, c: (i, 0)),
             ],
         ),
         out_shape=[
-            shape((merged, window * width), BF),
+            shape((merged // 2, window * width), BF),
+            shape((merged // 2, window * width), BF),
             shape((window, merged, width), BF),
             shape((merged, 128), F32),
         ],
@@ -123,7 +135,7 @@
     )(here, features, gain, bias)
 
 
-def collect_kernel(pos_ref, stream_ref, cot_ref, after_ref, out_ref):
+def collect_kernel(pos_ref, stream_ref, cot_ref, out_ref):
     slots = pos_ref.shape[0]
     rows, width = stream_ref.shape
     cut = width // 2
@@ -136,18 +148,18 @@
             ).astype(BF)
 
 
-def collect(pos, stream, cot, after):
+def collect(pos, stream, cot):
     slots = pos.shape[0]
     rows, width = stream.shape
     return pl.pallas_call(
         collect_kernel,
-        in_specs=[whole()] * 3 + [anywhere()],
+        in_specs=[whole()] * 3,
         out_specs=whole(),
         out_shape=shape((2, slots, width), BF),
         compiler_params=params(20),
         cost_estimate=FREE,
         name="collect",
-    )(pos, stream, cot, after)
+    )(pos, stream, cot)
 
 
 def unpack_kernel(slot_ref, came_ref, base_ref, cot_ref):
@@ -263,12 +275,12 @@
 
 
 def multiply_kernel(here_ref, *refs):
-    stacks, lifted, (out_ref, *scratch) = refs[: RING - 1], refs[RING - 1 : RING + 1], refs[RING + 1 :]
+    stacks, lifted, (out_ref, *scratch) = refs[: RING - 1], refs[RING - 1 : RING + 3], refs[RING + 3 :]
     out_ref[...] = product(here_ref, AWAY[: RING - 1], stacks, lifted, *scratch)(None)
 
 
 def multiply(here, stacks, lifted):
-    tokens, width = 2 * lifted[0].shape[0], stacks[0].shape[2]
+    tokens, width = len(lifted) * lifted[0].shape[0], stacks[0].shape[2]
     return pl.pallas_call(
         multiply_kernel,
         in_specs=[scalars()] + [in_hbm()] * (len(stacks) + len(lifted)),
@@ -282,7 +294,7 @@
 
 
 def merge_kernel(here_ref, ngain_ref, acc_hbm, base_hbm, cot_hbm, stack_ref, *refs):
-    lifted, refs = refs[:2], refs[2:]
+    lifted, refs = refs[:4], refs[4:]
     visual_ref, state_ref, stat_ref, acc_ref, base_ref, cot_ref, row_sems, *scratch = refs
     run = product(here_ref, AWAY[RING - 1 :], (stack_ref,), lifted, *scratch)
     copies = [
@@ -313,7 +325,7 @@
     outs = [shape((tokens, width), BF), shape((tokens, width), F32), shape((8, tokens), F32)]
     return pl.pallas_call(
         merge_kernel,
-        in_specs=[scalars(), whole()] + [in_hbm()] * 6,
+        in_specs=[scalars(), whole()] + [in_hbm()] * (4 + len(lifted)),
         out_specs=[whole()] * 3,
         out_shape=outs,
         scratch_shapes=[
@@ -694,23 +706,18 @@
         packed.reshape(owners, capacity), ("img", "ctx"), split_axis=0, concat_axis=0, tiled=True
     )
     columns = lax.dynamic_slice_in_dim(projection[0], img * cut, cut, axis=2).reshape(-1, cut)
+    paired = target * (n_img * capacity) + rank + img * capacity
+    partner = lax.ppermute(paired, "img", flip)
+    columns, asked, partner = lax.optimization_barrier((columns, asked, partner))
+    paired = jnp.concatenate([paired, partner]).reshape(-1, 1)
     moves = (1, -1, 2)
     near_blocks = [along_ctx(columns, 0, by) for by in moves]
-    paired = target * (n_img * capacity) + rank + img * capacity
-    partner = lax.ppermute(paired, "img", flip)
-    gain = ln_gain[0]
-    lifted, xw, stat = layer_norm(here, features[0], gain, ln_bias[0])
-    asked, lifted, stat, near_blocks, partner = lax.optimization_barrier(
-        (asked, lifted, stat, near_blocks, partner)
-    )
-    paired = jnp.concatenate([paired, partner]).reshape(-1, 1)
 
     first = stack(here, [columns] + near_blocks)
-    asked, first = lax.optimization_barrier((asked, first))
 
     asked = asked.reshape(n_img, n_ctx, capacity).transpose(1, 0, 2)
     asked = asked.reshape(slot_count, 1)
-    held = collect(asked, stream, cotangent[0], first)
+    held = collect(asked, stream, cotangent[0])
     came = lax.all_to_all(
         held.reshape(owners, n_img * capacity, width),
         ("img", "ctx"), split_axis=0, concat_axis=0, tiled=True,
@@ -719,12 +726,16 @@
     stacks = [first] + [along_ctx(first, 1, by) for by in moves[:2]]
     stacks.append(along_ctx(stacks[1], 1, 1))
 
-    pairs = []
-    for i in range(n_img):
-        for t in range(n_tp):
-            x = (2 * (t // 2) + i + (1 if t % 2 == 0 else -1)) % RING
-            pairs.append((i * n_tp + t, (x % 2) * n_tp + 2 * (x // 2) + t % 2))
-    lifted = [lifted, lax.ppermute(lifted, ("img", "tp"), pairs)]
+    gain = ln_gain[0]
+    *lifted, xw, stat = layer_norm(here, features[0], gain, ln_bias[0])
+    for part in range(2):
+        pairs = []
+        for i in range(n_img):
+            for t in range(n_tp):
+                in_pair = part == 0 and t % 2 == 1
+                x = (2 * (t // 2) + i + (1 if in_pair == (i == 0) else -1)) % RING
+                pairs.append((i * n_tp + t, (x % 2) * n_tp + 2 * (x // 2) + t % 2))
+        lifted.append(lax.ppermute(lifted[part], ("img", "tp"), pairs))
 
     own_gain = lax.dynamic_slice_in_dim(norm_gain, img * cut, cut, axis=1)
     base, cot = unpack(paired, came)

time: 179 us -> 192 us (1.073)
  starting transfers between devices: 54.7 us -> 62.7 us
  local copies, waits for them, and re-layouts: 9.88 us -> 13 us
    all_to_all x1, waiting for transfers between devices: 33.8 us -> 0.01 us  [shards(): lax.all_to_all(held.reshape(owners, n_img * capacity, width), ('img', 'ct...]
    ppermute x1 -> x2, waiting for transfers between devices: 0.01 us -> 24.7 us  [shards(): lifted.append(lax.ppermute(lifted[part], ('img', 'tp'), pairs))]
    ppermute x1, starting transfers between devices: 0.49 us -> 13.5 us  [shards(): near, turned = add(sums, lax.ppermute(sums, 'tp', core_pairs))]
    all_to_all x1, waiting for transfers between devices: 0.01 us -> 6.99 us  [shards(): lax.all_to_all(packed.reshape(owners, capacity), ('img', 'ctx'), split_ax...]
    ppermute x6, waiting for transfers between devices: 0.93 us -> 7.75 us  [along_ctx(): return lax.ppermute(array, ('ctx', 'tp'), pairs)]
    ppermute x7, starting transfers between devices: 13.3 us -> 8.48 us  [along_x(): return lax.ppermute(array, ('img', 'tp'), pairs)]
    ppermute x6, starting transfers between devices: 9.59 us -> 5.16 us  [along_ctx(): return lax.ppermute(array, ('ctx', 'tp'), pairs)]
    unnamed x34 -> x48, local copies, waits for them, and re-layouts: 8.25 us -> 11.9 us
  transfers between devices with their start and end apart: 24 -> 25, of which waited for: 11 -> 14; matrix products, arithmetic and copies ran while one was open for 1% -> 0% of each run, Pallas kernels for 18% -> 17%
where the time goes in v12:
time: 192 us; the launch traced here: 191 us
  waiting for transfers between devices  72.6 us (38%)
  starting transfers between devices  62.7 us (33%)
  Pallas kernels  40.6 us (21%)
  local copies, waits for them, and re-layouts  13 us (7%)
    ppermute x2, waiting for transfers between devices, shards(): lifted.append(lax.ppermute(lifted[part], ('img', 'tp'), pairs))  24.7 us
    ppermute x1, starting transfers between devices, shards(): near, turned = add(sums, lax.ppermute(sums, 'tp', core_pairs))  13.5 us
    ppermute x7, waiting for transfers between devices, along_x(): return lax.ppermute(array, ('img', 'tp'), pairs)  13.1 us
    unnamed x48, local copies, waits for them, and re-layouts  11.9 us
    ppermute x7, starting transfers between devices, along_x(): return lax.ppermute(array, ('img', 'tp'), pairs)  8.48 us
    all_to_all x1, starting transfers between devices, shards(): lax.all_to_all(packed.reshape(owners, capacity), ('img', 'ctx'), split_ax...  8.05 us
    pallas_call x1, Pallas kernels, layer_norm(): pl.pallas_call(norm_kernel, grid_spec=pltpu.PrefetchScalarGridSpec(num_sc...  7.89 us
    ppermute x6, waiting for transfers between devices, along_ctx(): return lax.ppermute(array, ('ctx', 'tp'), pairs)  7.75 us
  transfers between devices with their start and end apart: 25, of which 14 were waited for; matrix products, arithmetic and copies ran while one was open for 0% of the time, Pallas kernels for 17%

profile of v12, /device:TPU:1, one launch (start us, length us, event | category | flops | bytes accessed | tf_op | source)
XLA Modules:
  0.0 191.2 jit_solution(16786558834401059458)
XLA Ops:
  1.7 2.1 %collective-permute-start = (s32[256]{0:T(256)S(1)}, s32[256]{0:T(256)S(1)}, u32[]{:S(2)}, u32[]{:S(2)}) collective-permute-start(s32[256]{0:T(256)S(1)} %get-tuple-element.70), channel_id=1, source_target_pairs={{0,64},{64,0},{1,65},{65,1},{2,66},{66,2},{3,67},{67,3},{4,68},{68... | collective-permute-start | bytes 3080 | tf_op jit(solution)/shard_map/ppermute | solution.py:710
  4.6 8.1 %all-to-all-start = ((s32[32,1,16]{2,1,0:T(1,128)}), s32[32,1,16]{2,1,0:T(1,128)S(1)}, u32[]{:S(2)}, u32[]{:S(2)}) async-start(s32[32,1,16]{2,1,0:T(1,128)} %bitcast.6), calls=%async_computation | async-start | bytes 32768 | tf_op jit(solution)/shard_map/all_to_all | solution.py:705
  12.7 7.0 %all-to-all-done = s32[32,1,16]{2,1,0:T(1,128)S(1)} async-done(((s32[32,1,16]{2,1,0:T(1,128)}), s32[32,1,16]{2,1,0:T(1,128)S(1)}, u32[]{:S(2)}, u32[]{:S(2)}) %all-to-all-start) | async-done | bytes 2080 | tf_op jit(solution)/shard_map/all_to_all | solution.py:705
  20.7 1.7 collective-permute-start.2
  22.5 4.6 %collective-permute-done.3.refs_3_ = bf16[288,512]{1,0:T(8,128)(2,1)S(1)} collective-permute-done((bf16[288,512]{1,0:T(8,128)(2,1)S(1)}, bf16[288,512]{1,0:T(8,128)(2,1)S(1)}, u32[]{:S(2)}, u32[]{:S(2)}) %collective-permute-start.3) | collective-permute-done | bytes 294944 | tf_op jit(solution)/shard_map/ppermute | solution.py:693
  27.1 1.7 collective-permute-done.2.refs_2_
  28.8 1.5 collective-permute-done.1.refs_1_
  31.4 1.2 copy-done.10
  32.6 1.2 copy-done.15
  33.8 1.3 collect.1
  35.2 1.3 copy-done.3
  36.5 5.2 %all-to-all-start.1 = ((bf16[32,32,1024]{2,1,0:T(8,128)(2,1)}), bf16[32,32,1024]{2,1,0:T(8,128)(2,1)}, u32[]{:S(2)}, u32[]{:S(2)}) async-start(bf16[32,32,1024]{2,1,0:T(8,128)(2,1)} %bitcast.21), calls=%async_computation.1 | async-start | bytes 4194304 | tf_op jit(solution)/shard_map/all_to_all | solution.py:721
  41.7 7.9 %layer_norm.1 = (bf16[128,4608]{1,0:T(8,128)(2,1)}, bf16[128,4608]{1,0:T(8,128)(2,1)}, bf16[4,256,1152]{2,1,0:T(8,128)(2,1)}, f32[256,128]{1,0:T(8,128)}) custom-call(s32[5]{0:T(128)} %copy-done.18, bf16[1024,1152]{1,0:T(8,128)(2,1)} %bitcast.27, bf16[4,1152]{1,0:T(4,128)(2,1)} %bitcast.31, bf16[4,1152]{1,0:T(4,128)(2,1)} %bitcast.33), custom_call_target="tpu_custom_call" | custom-call | tf_op jit(solution)/shard_map/layer_norm/pallas_call | solution.py:106
  49.6 1.2 collective-permute-start.6
  50.7 1.8 collective-permute-start.7
  52.6 2.4 %collective-permute-start.5 = (bf16[4,288,512]{2,1,0:T(8,128)(2,1)S(1)}, bf16[4,288,512]{2,1,0:T(8,128)(2,1)}, u32[]{:S(2)}, u32[]{:S(2)}) collective-permute-start(bf16[4,288,512]{2,1,0:T(8,128)(2,1)S(1)} %stack.25.refs_0_.refs_6_), channel_id=1, source_target_pairs={{0,48},{1,13},{2,50},{3,15},{4,52},{5,1},{6,54},{7,3},{8,56},{9,5}... | collective-permute-start | bytes 3538952 | tf_op jit(solution)/shard_map/ppermute | solution.py:693
  55.1 24.7 %collective-permute-done.6.refs_5_.refs_2_ = bf16[128,4608]{1,0:T(8,128)(2,1)} collective-permute-done((bf16[128,4608]{1,0:T(8,128)(2,1)}, bf16[128,4608]{1,0:T(8,128)(2,1)}, u32[]{:S(2)}, u32[]{:S(2)}) %collective-permute-start.6) | collective-permute-done | bytes 1179680 | tf_op jit(solution)/shard_map/ppermute | solution.py:738
  79.9 1.3 copy-done.4
  81.2 1.3 copy-done.6
  82.4 4.6 %multiply.1.acc_hbm = f32[512,512]{1,0:T(8,128)S(1)} custom-call(s32[5]{0:T(128)S(1)} %copy-done.19, bf16[4,288,512]{2,1,0:T(8,128)(2,1)S(1)} %stack.25.refs_0_.refs_6_, bf16[4,288,512]{2,1,0:T(8,128)(2,1)S(1)} %collective-permute-done.4.refs_1_.refs_7_, bf16[4,288,512]{2,1,0:T(8,128)(2,1)} %collective-permute-done.5.refs_2_.refs_8_, ...), custom_call_target="tpu_custom_call" | custom-call | tf_op jit(solution)/shard_map/multiply/pallas_call | solution.py:284
  88.0 3.0 %unpack.1 = (bf16[512,512]{1,0:T(8,128)(2,1)S(1)}, bf16[512,512]{1,0:T(8,128)(2,1)S(1)}) custom-call(s32[512,1]{1,0:T(8,128)S(1)} %copy.28.slot_ref, bf16[1024,1024]{1,0:T(8,128)(2,1)} %bitcast.17.came_ref), custom_call_target="tpu_custom_call" | custom-call | tf_op jit(solution)/shard_map/unpack/pallas_call | solution.py:180
  91.1 1.2 copy-done.9
  92.3 3.4 %merge.1 = (bf16[512,512]{1,0:T(8,128)(2,1)S(1)}, f32[512,512]{1,0:T(8,128)S(1)}, f32[8,512]{1,0:T(8,128)S(1)}) custom-call(s32[5]{0:T(128)S(1)} %copy-done.19, bf16[1,512]{1,0:T(2,128)(2,1)S(1)} %constant_dynamic-slice_fusion.1.ngain_ref.refs_1_, f32[512,512]{1,0:T(8,128)S(1)} %copy-done.9, bf16[512,512]{1,0:T(8,128)(2,1)S(1)} %get-tuple-element.40.base_hbm, ...), custom_call_target="tpu_custom_call" | custom-call | tf_op jit(solution)/shard_map/merge/pallas_call | solution.py:326
  95.7 13.5 %collective-permute-start.9 = (f32[8,512]{1,0:T(8,128)S(1)}, f32[8,512]{1,0:T(8,128)S(1)}, u32[]{:S(2)}, u32[]{:S(2)}) collective-permute-start(f32[8,512]{1,0:T(8,128)S(1)} %get-tuple-element.43.sums_ref), channel_id=1, source_target_pairs={{0,1},{1,0},{2,3},{3,2},{4,5},{5,4},{6,7},{7,6},{8,9},{9,8},{10,11... | collective-permute-start | bytes 49160 | tf_op jit(solution)/shard_map/ppermute | solution.py:745
  110.0 1.8 collective-permute-start.12
  111.9 1.2 collective-permute-start.11
  113.1 1.4 pack.1
  114.5 1.2 collective-permute-done.10.refs_3_
  116.6 5.5 %backward.1 = (bf16[256,4608]{1,0:T(8,128)(2,1)S(1)}, bf16[256,4608]{1,0:T(8,128)(2,1)S(1)}) custom-call(s32[5]{0:T(128)S(1)} %copy-done.19, bf16[1,512]{1,0:T(2,128)(2,1)S(1)} %constant_dynamic-slice_fusion.1.ngain_ref.refs_1_, f32[8,512]{1,0:T(8,128)S(1)} %get-tuple-element.47.after_ref.refs_2_, f32[8,512]{1,0:T(8,128)S(1)} %collective-permute-done.10.refs_3_, ...), custom_call_target="tpu_custom_call" | custom-call | tf_op jit(solution)/shard_map/backward/pallas_call | solution.py:462
  122.2 5.4 %collective-permute-done.13.after_ref.crossed_ref = bf16[512,512]{1,0:T(8,128)(2,1)S(1)} collective-permute-done((bf16[512,512]{1,0:T(8,128)(2,1)S(1)}, bf16[512,512]{1,0:T(8,128)(2,1)S(1)}, u32[]{:S(2)}, u32[]{:S(2)}) %collective-permute-start.13) | collective-permute-done | bytes 524320 | tf_op jit(solution)/shard_map/ppermute | solution.py:749
  127.6 2.7 %collective-permute-start.14 = (bf16[256,4608]{1,0:T(8,128)(2,1)S(1)}, bf16[256,4608]{1,0:T(8,128)(2,1)S(1)}, u32[]{:S(2)}, u32[]{:S(2)}) collective-permute-start(bf16[256,4608]{1,0:T(8,128)(2,1)S(1)} %get-tuple-element.56), channel_id=1, source_target_pairs={{0,1},{1,0},{2,3},{3,2},{4,5},{5,4},{6,7},{7,6},{8,9},{9,8},{10,11... | collective-permute-start | bytes 7077896 | tf_op jit(solution)/shard_map/ppermute | solution.py:753
  130.3 4.2 %collective-permute-done.14.got_ref = bf16[256,4608]{1,0:T(8,128)(2,1)S(1)} collective-permute-done((bf16[256,4608]{1,0:T(8,128)(2,1)S(1)}, bf16[256,4608]{1,0:T(8,128)(2,1)S(1)}, u32[]{:S(2)}, u32[]{:S(2)}) %collective-permute-start.14) | collective-permute-done | bytes 2359328 | tf_op jit(solution)/shard_map/ppermute | solution.py:753
  134.5 1.6 pair.1
  137.8 2.0 %collective-permute-start.16 = (bf16[64,4608]{1,0:T(8,128)(2,1)}, bf16[64,4608]{1,0:T(8,128)(2,1)S(1)}, u32[]{:S(2)}, u32[]{:S(2)}) collective-permute-start(bf16[64,4608]{1,0:T(8,128)(2,1)} %get-tuple-element.59), channel_id=1, source_target_pairs={{0,66},{1,67},{2,64},{3,65},{64,0},{65,1},{66,2},{67,3},{4,70},{5,... | collective-permute-start | bytes 1769480 | tf_op jit(solution)/shard_map/ppermute | solution.py:681
  139.8 1.0 braid.1
  140.8 6.5 %all-to-all-start.2 = ((bf16[16,2,32,512]{3,2,1,0:T(8,128)(2,1)}), bf16[16,2,32,512]{3,2,1,0:T(8,128)(2,1)S(1)}, u32[]{:S(2)}, u32[]{:S(2)}) async-start(bf16[16,2,32,512]{3,2,1,0:T(8,128)(2,1)} %braid.1), calls=%async_computation.2 | async-start | bytes 2097152 | tf_op jit(solution)/shard_map/all_to_all | solution.py:760
  147.3 5.8 %collective-permute-done.15.from_last_ref = bf16[64,4608]{1,0:T(8,128)(2,1)S(1)} collective-permute-done((bf16[64,4608]{1,0:T(8,128)(2,1)}, bf16[64,4608]{1,0:T(8,128)(2,1)S(1)}, u32[]{:S(2)}, u32[]{:S(2)}) %collective-permute-start.15) | collective-permute-done | bytes 589856 | tf_op jit(solution)/shard_map/ppermute | solution.py:681
  153.1 1.5 copy-done.17
  155.1 2.4 %collective-permute-start.18 = (bf16[32,4608]{1,0:T(8,128)(2,1)S(1)}, bf16[32,4608]{1,0:T(8,128)(2,1)S(1)}, u32[]{:S(2)}, u32[]{:S(2)}) collective-permute-start(bf16[32,4608]{1,0:T(8,128)(2,1)S(1)} %get-tuple-element.62), channel_id=1, source_target_pairs={{0,66},{1,67},{2,64},{3,65},{64,0},{65,1},{66,2},{67,3},{4,70},{5,... | collective-permute-start | bytes 884744 | tf_op jit(solution)/shard_map/ppermute | solution.py:681
  157.5 5.8 %collective-permute-done.17.late_last_ref = bf16[32,4608]{1,0:T(8,128)(2,1)S(1)} collective-permute-done((bf16[32,4608]{1,0:T(8,128)(2,1)S(1)}, bf16[32,4608]{1,0:T(8,128)(2,1)S(1)}, u32[]{:S(2)}, u32[]{:S(2)}) %collective-permute-start.17) | collective-permute-done | bytes 294944 | tf_op jit(solution)/shard_map/ppermute | solution.py:681
  164.1 5.0 %finish.1.refs_0_ = bf16[256,1152]{1,0:T(8,128)(2,1)} custom-call(s32[5]{0:T(128)} %copy-done.18, bf16[256,4608]{1,0:T(8,128)(2,1)} %copy-done.1, bf16[256,4608]{1,0:T(8,128)(2,1)} %copy-done.2, bf16[64,4608]{1,0:T(8,128)(2,1)} %copy-done.13, bf16[64,4608]{1,0:T(8,128)(2,1)} %copy-done.14, bf16[32,4608]{1,0:T(8,128)(2,1)} %copy-done.21, ...), custom_call_target="tpu_custom_call" | custom-call | tf_op jit(solution)/shard_map/finish/pallas_call | solution.py:573
  169.1 1.4 collective-permute-start.19
  170.5 2.4 %place.1 = bf16[512,1024]{1,0:T(8,128)(2,1)} custom-call(s32[5]{0:T(128)S(1)} %copy-done.20, s32[512,1]{1,0:T(8,128)S(1)} %reshape.38.pos_ref, bf16[16,2,32,512]{3,2,1,0:T(8,128)(2,1)S(1)} %all-to-all-done.2.came_ref, bf16[512,1024]{1,0:T(8,128)(2,1)S(1)} %copy-done.11), custom_call_target="tpu_custom_call" | custom-call | tf_op jit(solution)/shard_map/place/pallas_call | solution.py:614
  172.9 3.0 %collective-permute-start.20 = (bf16[256,1152]{1,0:T(8,128)(2,1)S(1)}, bf16[256,1152]{1,0:T(8,128)(2,1)S(1)}, u32[]{:S(2)}, u32[]{:S(2)}) collective-permute-start(bf16[256,1152]{1,0:T(8,128)(2,1)S(1)} %copy-done.12), channel_id=1, source_target_pairs={{0,1},{1,0},{2,3},{3,2},{4,5},{5,4},{6,7},{7,6},{8,9},{9,8},{10,11... | collective-permute-start | bytes 1769480 | tf_op jit(solution)/shard_map/ppermute | solution.py:766
  175.9 7.7 %collective-permute-done.19.refs_1_ = bf16[256,1152]{1,0:T(8,128)(2,1)} collective-permute-done((bf16[256,1152]{1,0:T(8,128)(2,1)}, bf16[256,1152]{1,0:T(8,128)(2,1)}, u32[]{:S(2)}, u32[]{:S(2)}) %collective-permute-start.19) | collective-permute-done | bytes 589856 | tf_op jit(solution)/shard_map/ppermute | solution.py:764
  183.6 3.0 %collective-permute-start.21 = (bf16[256,1152]{1,0:T(8,128)(2,1)}, bf16[256,1152]{1,0:T(8,128)(2,1)S(1)}, u32[]{:S(2)}, u32[]{:S(2)}) collective-permute-start(bf16[256,1152]{1,0:T(8,128)(2,1)} %collective-permute-done.19.refs_1_), channel_id=1, source_target_pairs={{0,1},{1,0},{2,3},{3,2},{4,5},{5,4},{6,7},{7,6},{8,9},{9,8},{10,11... | collective-permute-start | bytes 1769480 | tf_op jit(solution)/shard_map/ppermute | solution.py:766
  186.7 1.8 collective-permute-done.21.refs_3_
  188.5 2.5 %lay.1 = bf16[1024,1152]{1,0:T(8,128)(2,1)} custom-call(s32[5]{0:T(128)S(1)} %copy-done.20, bf16[256,1152]{1,0:T(8,128)(2,1)S(1)} %copy-done.12, bf16[256,1152]{1,0:T(8,128)(2,1)} %collective-permute-done.19.refs_1_, bf16[256,1152]{1,0:T(8,128)(2,1)S(1)} %collective-permute-done.20.refs_2_, bf16[256,1152]{1,0:T(8,128)(2,1)S(1)} %collective-permute-done.21.refs_3_), custom_call_target="tpu_custom_call" | custom-call | tf_op jit(solution)/shard_map/lay/pallas_call | solution.py:641
  (78 shorter events, 10.0 us)
Async XLA Ops:
  0.6 12.1 %copy-start = (bf16[1,4,72,1024]{3,2,1,0:T(8,128)(2,1)S(1)}, bf16[1,4,72,1024]{3,2,1,0:T(8,128)(2,1)}, u32[]{:S(2)}) copy-start(bf16[1,4,72,1024]{3,2,1,0:T(8,128)(2,1)} %param.11) | copy-start | bytes 1769476
  1.7 11.1 %collective-permute-start = (s32[256]{0:T(256)S(1)}, s32[256]{0:T(256)S(1)}, u32[]{:S(2)}, u32[]{:S(2)}) collective-permute-start(s32[256]{0:T(256)S(1)} %get-tuple-element.70), channel_id=1, source_target_pairs={{0,64},{64,0},{1,65},{65,1},{2,66},{66,2},{3,67},{67,3},{4,68},{68... | collective-permute-start | bytes 3080 | tf_op jit(solution)/shard_map/ppermute | solution.py:710
  4.6 15.1 %all-to-all-start = ((s32[32,1,16]{2,1,0:T(1,128)}), s32[32,1,16]{2,1,0:T(1,128)S(1)}, u32[]{:S(2)}, u32[]{:S(2)}) async-start(s32[32,1,16]{2,1,0:T(1,128)} %bitcast.6), calls=%async_computation | async-start | bytes 32768 | tf_op jit(solution)/shard_map/all_to_all | solution.py:705
  19.7 7.4 %collective-permute-start.3 = (bf16[288,512]{1,0:T(8,128)(2,1)S(1)}, bf16[288,512]{1,0:T(8,128)(2,1)S(1)}, u32[]{:S(2)}, u32[]{:S(2)}) collective-permute-start(bf16[288,512]{1,0:T(8,128)(2,1)S(1)} %bitcast.22), channel_id=1, source_target_pairs={{0,8},{1,33},{2,10},{3,35},{4,12},{5,37},{6,14},{7,39},{8,0},{9,41... | collective-permute-start | bytes 884744 | tf_op jit(solution)/shard_map/ppermute | solution.py:693
  20.7 8.1 %collective-permute-start.2 = (bf16[288,512]{1,0:T(8,128)(2,1)S(1)}, bf16[288,512]{1,0:T(8,128)(2,1)S(1)}, u32[]{:S(2)}, u32[]{:S(2)}) collective-permute-start(bf16[288,512]{1,0:T(8,128)(2,1)S(1)} %bitcast.23), channel_id=1, source_target_pairs={{0,12},{1,49},{2,14},{3,51},{4,0},{5,53},{6,2},{7,55},{8,4},{9,57}... | collective-permute-start | bytes 884744 | tf_op jit(solution)/shard_map/ppermute | solution.py:693
  22.4 7.8 %collective-permute-start.1 = (bf16[288,512]{1,0:T(8,128)(2,1)S(1)}, bf16[288,512]{1,0:T(8,128)(2,1)S(1)}, u32[]{:S(2)}, u32[]{:S(2)}) collective-permute-start(bf16[288,512]{1,0:T(8,128)(2,1)S(1)} %bitcast.24), channel_id=1, source_target_pairs={{0,4},{1,17},{2,6},{3,19},{4,8},{5,21},{6,10},{7,23},{8,12},{9,25}... | collective-permute-start | bytes 884744 | tf_op jit(solution)/shard_map/ppermute | solution.py:693
  22.5 12.6 %copy-start.18 = (s32[5]{0:T(128)}, s32[5]{0:T(128)S(1)}, u32[]{:S(2)}) copy-start(s32[5]{0:T(128)S(1)} %stack.24.here_ref.refs_0_) | copy-start | bytes 64
  31.1 23.8 %collective-permute-start.4 = (bf16[4,288,512]{2,1,0:T(8,128)(2,1)S(1)}, bf16[4,288,512]{2,1,0:T(8,128)(2,1)S(1)}, u32[]{:S(2)}, u32[]{:S(2)}) collective-permute-start(bf16[4,288,512]{2,1,0:T(8,128)(2,1)S(1)} %stack.25.refs_0_.refs_6_), channel_id=1, source_target_pairs={{0,16},{1,5},{2,18},{3,7},{4,20},{5,9},{6,22},{7,11},{8,24},{9,13}... | collective-permute-start | bytes 3538952 | tf_op jit(solution)/shard_map/ppermute | solution.py:693
  31.4 1.2 copy-start.10
  32.6 1.2 copy-start.15
  35.1 1.4 copy-start.3
  36.5 51.5 %all-to-all-start.1 = ((bf16[32,32,1024]{2,1,0:T(8,128)(2,1)}), bf16[32,32,1024]{2,1,0:T(8,128)(2,1)}, u32[]{:S(2)}, u32[]{:S(2)}) async-start(bf16[32,32,1024]{2,1,0:T(8,128)(2,1)} %bitcast.21), calls=%async_computation.1 | async-start | bytes 4194304 | tf_op jit(solution)/shard_map/all_to_all | solution.py:721
  41.7 13.3 %copy-start.23 = (bf16[1,1024]{1,0:T(2,128)(2,1)S(1)}, bf16[1,1024]{1,0:T(2,128)(2,1)}, u32[]{:S(2)}) copy-start(bf16[1,1024]{1,0:T(2,128)(2,1)} %param.13) | copy-start | bytes 6148
  41.7 38.2 %copy-start.19 = (s32[5]{0:T(128)S(1)}, s32[5]{0:T(128)}, u32[]{:S(2)}) copy-start(s32[5]{0:T(128)} %copy-done.18) | copy-start | bytes 64
  49.6 30.3 %collective-permute-start.6 = (bf16[128,4608]{1,0:T(8,128)(2,1)}, bf16[128,4608]{1,0:T(8,128)(2,1)}, u32[]{:S(2)}, u32[]{:S(2)}) collective-permute-start(bf16[128,4608]{1,0:T(8,128)(2,1)} %get-tuple-element.37.refs_3_.refs_0_), channel_id=1, source_target_pairs={{0,66},{1,65},{2,64},{3,67},{64,2},{65,1},{66,0},{67,3},{4,70},{5,... | collective-permute-start | bytes 3538952 | tf_op jit(solution)/shard_map/ppermute | solution.py:738
  50.7 29.1 %collective-permute-start.7 = (bf16[128,4608]{1,0:T(8,128)(2,1)}, bf16[128,4608]{1,0:T(8,128)(2,1)}, u32[]{:S(2)}, u32[]{:S(2)}) collective-permute-start(bf16[128,4608]{1,0:T(8,128)(2,1)} %get-tuple-element.38.refs_4_.refs_1_), channel_id=1, source_target_pairs={{0,66},{1,67},{2,64},{3,65},{64,2},{65,3},{66,0},{67,1},{4,70},{5,... | collective-permute-start | bytes 3538952 | tf_op jit(solution)/shard_map/ppermute | solution.py:738
  52.6 27.3 %collective-permute-start.5 = (bf16[4,288,512]{2,1,0:T(8,128)(2,1)S(1)}, bf16[4,288,512]{2,1,0:T(8,128)(2,1)}, u32[]{:S(2)}, u32[]{:S(2)}) collective-permute-start(bf16[4,288,512]{2,1,0:T(8,128)(2,1)S(1)} %stack.25.refs_0_.refs_6_), channel_id=1, source_target_pairs={{0,48},{1,13},{2,50},{3,15},{4,52},{5,1},{6,54},{7,3},{8,56},{9,5}... | collective-permute-start | bytes 3538952 | tf_op jit(solution)/shard_map/ppermute | solution.py:693
  54.9 36.1 %collective-permute-start.8 = (bf16[4,288,512]{2,1,0:T(8,128)(2,1)S(1)}, bf16[4,288,512]{2,1,0:T(8,128)(2,1)}, u32[]{:S(2)}, u32[]{:S(2)}) collective-permute-start(bf16[4,288,512]{2,1,0:T(8,128)(2,1)S(1)} %collective-permute-done.4.refs_1_.refs_7_), channel_id=1, source_target_pairs={{0,16},{1,5},{2,18},{3,7},{4,20},{5,9},{6,22},{7,11},{8,24},{9,13}... | collective-permute-start | bytes 3538952 | tf_op jit(solution)/shard_map/ppermute | solution.py:693
  79.9 1.3 copy-start.4
  81.2 1.3 copy-start.6
  87.0 1.0 copy-start.8
  88.0 3.1 %copy-start.5 = (bf16[128,4608]{1,0:T(8,128)(2,1)S(1)}, bf16[128,4608]{1,0:T(8,128)(2,1)}, u32[]{:S(2)}) copy-start(bf16[128,4608]{1,0:T(8,128)(2,1)} %get-tuple-element.37.refs_3_.refs_0_) | copy-start | bytes 3538948
  88.0 3.1 %copy-start.7 = (bf16[128,4608]{1,0:T(8,128)(2,1)S(1)}, bf16[128,4608]{1,0:T(8,128)(2,1)}, u32[]{:S(2)}) copy-start(bf16[128,4608]{1,0:T(8,128)(2,1)} %get-tuple-element.38.refs_4_.refs_1_) | copy-start | bytes 3538948
  91.1 1.2 copy-start.9
  95.7 14.3 %collective-permute-start.9 = (f32[8,512]{1,0:T(8,128)S(1)}, f32[8,512]{1,0:T(8,128)S(1)}, u32[]{:S(2)}, u32[]{:S(2)}) collective-permute-start(f32[8,512]{1,0:T(8,128)S(1)} %get-tuple-element.43.sums_ref), channel_id=1, source_target_pairs={{0,1},{1,0},{2,3},{3,2},{4,5},{5,4},{6,7},{7,6},{8,9},{9,8},{10,11... | collective-permute-start | bytes 49160 | tf_op jit(solution)/shard_map/ppermute | solution.py:745
  110.0 4.5 %collective-permute-start.12 = (f32[8,512]{1,0:T(8,128)S(1)}, f32[8,512]{1,0:T(8,128)S(1)}, u32[]{:S(2)}, u32[]{:S(2)}) collective-permute-start(f32[8,512]{1,0:T(8,128)S(1)} %get-tuple-element.46), channel_id=1, source_target_pairs={{0,66},{1,67},{2,64},{3,65},{64,0},{65,1},{66,2},{67,3},{4,70},{5,... | collective-permute-start | bytes 49160 | tf_op jit(solution)/shard_map/ppermute | solution.py:681
  111.9 3.8 %collective-permute-start.10 = (f32[8,512]{1,0:T(8,128)S(1)}, f32[8,512]{1,0:T(8,128)S(1)}, u32[]{:S(2)}, u32[]{:S(2)}) collective-permute-start(f32[8,512]{1,0:T(8,128)S(1)} %get-tuple-element.46), channel_id=1, source_target_pairs={{0,64},{1,65},{2,66},{3,67},{64,2},{65,3},{66,0},{67,1},{4,68},{5,... | collective-permute-start | bytes 49160 | tf_op jit(solution)/shard_map/ppermute | solution.py:681
  111.9 4.1 %collective-permute-start.11 = (f32[8,512]{1,0:T(8,128)S(1)}, f32[8,512]{1,0:T(8,128)S(1)}, u32[]{:S(2)}, u32[]{:S(2)}) collective-permute-start(f32[8,512]{1,0:T(8,128)S(1)} %get-tuple-element.47.after_ref.refs_2_), channel_id=1, source_target_pairs={{0,2},{1,3},{2,0},{3,1},{64,66},{65,67},{66,64},{67,65},{4,6},{5,7... | collective-permute-start | bytes 49160 | tf_op jit(solution)/shard_map/ppermute | solution.py:681
  116.0 11.6 %collective-permute-start.13 = (bf16[512,512]{1,0:T(8,128)(2,1)S(1)}, bf16[512,512]{1,0:T(8,128)(2,1)S(1)}, u32[]{:S(2)}, u32[]{:S(2)}) collective-permute-start(bf16[512,512]{1,0:T(8,128)(2,1)S(1)} %get-tuple-element.54), channel_id=1, source_target_pairs={{0,64},{64,0},{1,65},{65,1},{2,66},{66,2},{3,67},{67,3},{4,68},{68... | collective-permute-start | bytes 1572872 | tf_op jit(solution)/shard_map/ppermute | solution.py:749
  122.2 13.9 %copy-start.1 = (bf16[256,4608]{1,0:T(8,128)(2,1)}, bf16[256,4608]{1,0:T(8,128)(2,1)S(1)}, u32[]{:S(2)}) copy-start(bf16[256,4608]{1,0:T(8,128)(2,1)S(1)} %get-tuple-element.55.own_ref) | copy-start | bytes 7077892
  127.6 6.9 %collective-permute-start.14 = (bf16[256,4608]{1,0:T(8,128)(2,1)S(1)}, bf16[256,4608]{1,0:T(8,128)(2,1)S(1)}, u32[]{:S(2)}, u32[]{:S(2)}) collective-permute-start(bf16[256,4608]{1,0:T(8,128)(2,1)S(1)} %get-tuple-element.56), channel_id=1, source_target_pairs={{0,1},{1,0},{2,3},{3,2},{4,5},{5,4},{6,7},{7,6},{8,9},{9,8},{10,11... | collective-permute-start | bytes 7077896 | tf_op jit(solution)/shard_map/ppermute | solution.py:753
  134.5 1.8 copy-start.2
  136.3 0.8 copy-start.16
  137.1 16.0 %collective-permute-start.15 = (bf16[64,4608]{1,0:T(8,128)(2,1)}, bf16[64,4608]{1,0:T(8,128)(2,1)S(1)}, u32[]{:S(2)}, u32[]{:S(2)}) collective-permute-start(bf16[64,4608]{1,0:T(8,128)(2,1)} %get-tuple-element.58), channel_id=1, source_target_pairs={{0,64},{1,65},{2,66},{3,67},{64,2},{65,3},{66,0},{67,1},{4,68},{5,... | collective-permute-start | bytes 1769480 | tf_op jit(solution)/shard_map/ppermute | solution.py:681
  137.8 15.3 %collective-permute-start.16 = (bf16[64,4608]{1,0:T(8,128)(2,1)}, bf16[64,4608]{1,0:T(8,128)(2,1)S(1)}, u32[]{:S(2)}, u32[]{:S(2)}) collective-permute-start(bf16[64,4608]{1,0:T(8,128)(2,1)} %get-tuple-element.59), channel_id=1, source_target_pairs={{0,66},{1,67},{2,64},{3,65},{64,0},{65,1},{66,2},{67,3},{4,70},{5,... | collective-permute-start | bytes 1769480 | tf_op jit(solution)/shard_map/ppermute | solution.py:681
  140.8 29.7 %all-to-all-start.2 = ((bf16[16,2,32,512]{3,2,1,0:T(8,128)(2,1)}), bf16[16,2,32,512]{3,2,1,0:T(8,128)(2,1)S(1)}, u32[]{:S(2)}, u32[]{:S(2)}) async-start(bf16[16,2,32,512]{3,2,1,0:T(8,128)(2,1)} %braid.1), calls=%async_computation.2 | async-start | bytes 2097152 | tf_op jit(solution)/shard_map/all_to_all | solution.py:760
  153.1 10.2 %copy-start.13 = (bf16[64,4608]{1,0:T(8,128)(2,1)}, bf16[64,4608]{1,0:T(8,128)(2,1)S(1)}, u32[]{:S(2)}) copy-start(bf16[64,4608]{1,0:T(8,128)(2,1)S(1)} %collective-permute-done.15.from_last_ref) | copy-start | bytes 1769476
  153.1 10.2 %copy-start.14 = (bf16[64,4608]{1,0:T(8,128)(2,1)}, bf16[64,4608]{1,0:T(8,128)(2,1)S(1)}, u32[]{:S(2)}) copy-start(bf16[64,4608]{1,0:T(8,128)(2,1)S(1)} %collective-permute-done.16.from_next_ref) | copy-start | bytes 1769476
  153.1 1.5 copy-start.17
  154.7 8.6 %collective-permute-start.17 = (bf16[32,4608]{1,0:T(8,128)(2,1)S(1)}, bf16[32,4608]{1,0:T(8,128)(2,1)S(1)}, u32[]{:S(2)}, u32[]{:S(2)}) collective-permute-start(bf16[32,4608]{1,0:T(8,128)(2,1)S(1)} %get-tuple-element.61), channel_id=1, source_target_pairs={{0,64},{1,65},{2,66},{3,67},{64,2},{65,3},{66,0},{67,1},{4,68},{5,... | collective-permute-start | bytes 884744 | tf_op jit(solution)/shard_map/ppermute | solution.py:681
  155.1 8.2 %collective-permute-start.18 = (bf16[32,4608]{1,0:T(8,128)(2,1)S(1)}, bf16[32,4608]{1,0:T(8,128)(2,1)S(1)}, u32[]{:S(2)}, u32[]{:S(2)}) collective-permute-start(bf16[32,4608]{1,0:T(8,128)(2,1)S(1)} %get-tuple-element.62), channel_id=1, source_target_pairs={{0,66},{1,67},{2,64},{3,65},{64,0},{65,1},{66,2},{67,3},{4,70},{5,... | collective-permute-start | bytes 884744 | tf_op jit(solution)/shard_map/ppermute | solution.py:681
  163.3 0.8 copy-start.22
  164.1 6.4 %copy-start.11 = (bf16[512,1024]{1,0:T(8,128)(2,1)S(1)}, bf16[512,1024]{1,0:T(8,128)(2,1)}, u32[]{:S(2)}) copy-start(bf16[512,1024]{1,0:T(8,128)(2,1)} %stream_ref.3) | copy-start | bytes 3145732
  164.1 6.4 %copy-start.20 = (s32[5]{0:T(128)S(1)}, s32[5]{0:T(128)}, u32[]{:S(2)}) copy-start(s32[5]{0:T(128)} %copy-done.18) | copy-start | bytes 64
  169.1 3.8 %copy-start.12 = (bf16[256,1152]{1,0:T(8,128)(2,1)S(1)}, bf16[256,1152]{1,0:T(8,128)(2,1)}, u32[]{:S(2)}) copy-start(bf16[256,1152]{1,0:T(8,128)(2,1)} %finish.1.refs_0_) | copy-start | bytes 1769476
  169.1 14.5 %collective-permute-start.19 = (bf16[256,1152]{1,0:T(8,128)(2,1)}, bf16[256,1152]{1,0:T(8,128)(2,1)}, u32[]{:S(2)}, u32[]{:S(2)}) collective-permute-start(bf16[256,1152]{1,0:T(8,128)(2,1)} %finish.1.refs_0_), channel_id=1, source_target_pairs={{0,2},{1,3},{2,0},{3,1},{4,6},{5,7},{6,4},{7,5},{8,10},{9,11},{10,... | collective-permute-start | bytes 1769480 | tf_op jit(solution)/shard_map/ppermute | solution.py:764
  172.9 13.8 %collective-permute-start.20 = (bf16[256,1152]{1,0:T(8,128)(2,1)S(1)}, bf16[256,1152]{1,0:T(8,128)(2,1)S(1)}, u32[]{:S(2)}, u32[]{:S(2)}) collective-permute-start(bf16[256,1152]{1,0:T(8,128)(2,1)S(1)} %copy-done.12), channel_id=1, source_target_pairs={{0,1},{1,0},{2,3},{3,2},{4,5},{5,4},{6,7},{7,6},{8,9},{9,8},{10,11... | collective-permute-start | bytes 1769480 | tf_op jit(solution)/shard_map/ppermute | solution.py:766
  183.6 4.9 %collective-permute-start.21 = (bf16[256,1152]{1,0:T(8,128)(2,1)}, bf16[256,1152]{1,0:T(8,128)(2,1)S(1)}, u32[]{:S(2)}, u32[]{:S(2)}) collective-permute-start(bf16[256,1152]{1,0:T(8,128)(2,1)} %collective-permute-done.19.refs_1_), channel_id=1, source_target_pairs={{0,1},{1,0},{2,3},{3,2},{4,5},{5,4},{6,7},{7,6},{8,9},{9,8},{10,11... | collective-permute-start | bytes 1769480 | tf_op jit(solution)/shard_map/ppermute | solution.py:766
  (1 other events, 0.7 us)

commit v13 on v11

--- a/solution.py
+++ b/solution.py
@@ -150,7 +150,7 @@
     )(pos, stream, cot, after)
 
 
-def unpack_kernel(slot_ref, came_ref, base_ref, cot_ref):
+def unpack_kernel(slot_ref, came_ref, after_ref, base_ref, cot_ref):
     tokens, width = base_ref.shape
     slots = came_ref.shape[0]
     take = eq_hot((tokens, slots), 1, slot_ref[...])
@@ -160,20 +160,20 @@
         ).astype(BF)
 
 
-def unpack(slot_col, came):
+def unpack(slot_col, came, after):
     tokens = slot_col.shape[0]
     slots, both = came.shape
     width = both // 2
     outs = [shape((tokens, width), BF)] * 2
     return pl.pallas_call(
         unpack_kernel,
-        in_specs=[whole()] * 2,
+        in_specs=[whole()] * 2 + [anywhere()],
         out_specs=[whole()] * 2,
         out_shape=outs,
         compiler_params=params(12),
         cost_estimate=FREE,
         name="unpack",
-    )(slot_col, came)
+    )(slot_col, came, after)
 
 
 def stack_kernel(here_ref, *refs):
@@ -722,13 +722,13 @@
     pairs = []
     for i in range(n_img):
         for t in range(n_tp):
-            x = (2 * (t // 2) + i + (1 if t % 2 == 0 else -1)) % RING
+            x = (2 * (t // 2) + i + (1 if i == 1 else -1)) % RING
             pairs.append((i * n_tp + t, (x % 2) * n_tp + 2 * (x // 2) + t % 2))
     lifted = [lifted, lax.ppermute(lifted, ("img", "tp"), pairs)]
 
     own_gain = lax.dynamic_slice_in_dim(norm_gain, img * cut, cut, axis=1)
-    base, cot = unpack(paired, came)
     acc = multiply(here, stacks[: RING - 1], lifted)
+    base, cot = unpack(paired, came, acc)
     visual, state, sums = merge(here, own_gain, acc, base, cot, stacks[RING - 1], lifted)
 
     near, turned = add(sums, lax.ppermute(sums, "tp", core_pairs))

time: 179 us -> 183 us (1.022)
  local copies, waits for them, and re-layouts: 9.88 us -> 16 us
    all_to_all x1, waiting for transfers between devices: 33.8 us -> 0.01 us  [shards(): lax.all_to_all(held.reshape(owners, n_img * capacity, width), ('img', 'ct...]
    ppermute x6, waiting for transfers between devices: 0.93 us -> 34.4 us  [along_ctx(): return lax.ppermute(array, ('ctx', 'tp'), pairs)]
    unnamed x34 -> x52, local copies, waits for them, and re-layouts: 8.25 us -> 14.4 us
    ppermute x7, starting transfers between devices: 13.3 us -> 9.52 us  [along_x(): return lax.ppermute(array, ('img', 'tp'), pairs)]
    all_to_all x1, starting transfers between devices: 3.66 us -> 5.98 us  [shards(): lax.all_to_all(send, 'ctx', split_axis=0, concat_axis=0, tiled=True)]
  transfers between devices with their start and end apart: 24 -> 24, of which waited for: 11 -> 10; matrix products, arithmetic and copies ran while one was open for 1% -> 1% of each run, Pallas kernels for 18% -> 18%
where the time goes in v13:
time: 183 us; the launch traced here: 182 us
  waiting for transfers between devices  69.4 us (38%)
  starting transfers between devices  53.6 us (29%)
  Pallas kernels  40.4 us (22%)
  local copies, waits for them, and re-layouts  16 us (9%)
    ppermute x6, waiting for transfers between devices, along_ctx(): return lax.ppermute(array, ('ctx', 'tp'), pairs)  34.4 us
    ppermute x7, waiting for transfers between devices, along_x(): return lax.ppermute(array, ('img', 'tp'), pairs)  14.5 us
    unnamed x52, local copies, waits for them, and re-layouts  14.4 us
    ppermute x6, starting transfers between devices, along_ctx(): return lax.ppermute(array, ('ctx', 'tp'), pairs)  10.4 us
    ppermute x7, starting transfers between devices, along_x(): return lax.ppermute(array, ('img', 'tp'), pairs)  9.52 us
    ppermute x1, waiting for transfers between devices, shards(): beyond = lax.ppermute(out, 'tp', far_pairs)  7.73 us
    pallas_call x1, Pallas kernels, layer_norm(): pl.pallas_call(norm_kernel, grid_spec=pltpu.PrefetchScalarGridSpec(num_sc...  7.63 us
    all_to_all x1, starting transfers between devices, shards(): lax.all_to_all(held.reshape(owners, n_img * capacity, width), ('img', 'ct...  7.08 us
  transfers between devices with their start and end apart: 24, of which 10 were waited for; matrix products, arithmetic and copies ran while one was open for 1% of the time, Pallas kernels for 18%

profile of v13, /device:TPU:1, one launch (start us, length us, event | category | flops | bytes accessed | tf_op | source)
XLA Modules:
  0.0 181.7 jit_solution(13327867896037725260)
XLA Ops:
  0.7 1.0 copy-done
  1.7 2.5 %collective-permute-start = (bf16[288,512]{1,0:T(8,128)(2,1)S(1)}, bf16[288,512]{1,0:T(8,128)(2,1)S(1)}, u32[]{:S(2)}, u32[]{:S(2)}) collective-permute-start(bf16[288,512]{1,0:T(8,128)(2,1)S(1)} %bitcast.22), channel_id=1, source_target_pairs={{0,4},{1,17},{2,6},{3,19},{4,8},{5,21},{6,10},{7,23},{8,12},{9,25}... | collective-permute-start | bytes 884744 | tf_op jit(solution)/shard_map/ppermute | solution.py:681
  4.3 2.2 %collective-permute-start.1 = (bf16[288,512]{1,0:T(8,128)(2,1)S(1)}, bf16[288,512]{1,0:T(8,128)(2,1)S(1)}, u32[]{:S(2)}, u32[]{:S(2)}) collective-permute-start(bf16[288,512]{1,0:T(8,128)(2,1)S(1)} %bitcast.23), channel_id=1, source_target_pairs={{0,12},{1,49},{2,14},{3,51},{4,0},{5,53},{6,2},{7,55},{8,4},{9,57}... | collective-permute-start | bytes 884744 | tf_op jit(solution)/shard_map/ppermute | solution.py:681
  6.5 1.2 collective-permute-start.2
  9.5 7.0 %all-to-all-start = ((s32[32,1,16]{2,1,0:T(1,128)}), s32[32,1,16]{2,1,0:T(1,128)S(1)}, u32[]{:S(2)}, u32[]{:S(2)}) async-start(s32[32,1,16]{2,1,0:T(1,128)} %bitcast.5), calls=%async_computation | async-start | bytes 32768 | tf_op jit(solution)/shard_map/all_to_all | solution.py:693
  16.5 1.3 collective-permute-start.3
  18.4 7.6 %layer_norm.1 = (bf16[256,4608]{1,0:T(8,128)(2,1)}, bf16[4,256,1152]{2,1,0:T(8,128)(2,1)}, f32[256,128]{1,0:T(8,128)}) custom-call(s32[5]{0:T(128)} %stack.24.here_ref.refs_0_, bf16[1024,1152]{1,0:T(8,128)(2,1)} %bitcast.27, bf16[4,1152]{1,0:T(4,128)(2,1)} %bitcast.31, bf16[4,1152]{1,0:T(4,128)(2,1)} %bitcast.33), custom_call_target="tpu_custom_call" | custom-call | tf_op jit(solution)/shard_map/layer_norm/pallas_call | solution.py:96
  27.5 1.5 collective-permute-start.6
  29.0 1.0 copy-done.18
  30.0 1.0 copy-done.20
  31.8 1.3 collective-permute-start.4
  33.3 1.2 copy-done.14
  34.5 1.3 collect.1
  35.8 1.4 copy-done.5
  37.2 7.1 %all-to-all-start.1 = ((bf16[32,32,1024]{2,1,0:T(8,128)(2,1)}), bf16[32,32,1024]{2,1,0:T(8,128)(2,1)}, u32[]{:S(2)}, u32[]{:S(2)}) async-start(bf16[32,32,1024]{2,1,0:T(8,128)(2,1)} %bitcast.21), calls=%async_computation.1 | async-start | bytes 4194304 | tf_op jit(solution)/shard_map/all_to_all | solution.py:714
  44.3 2.4 %collective-permute-start.5 = (bf16[4,288,512]{2,1,0:T(8,128)(2,1)S(1)}, bf16[4,288,512]{2,1,0:T(8,128)(2,1)S(1)}, u32[]{:S(2)}, u32[]{:S(2)}) collective-permute-start(bf16[4,288,512]{2,1,0:T(8,128)(2,1)S(1)} %stack.25.refs_0_.after_ref.refs_6_), channel_id=1, source_target_pairs={{0,48},{1,13},{2,50},{3,15},{4,52},{5,1},{6,54},{7,3},{8,56},{9,5}... | collective-permute-start | bytes 3538952 | tf_op jit(solution)/shard_map/ppermute | solution.py:681
  46.8 1.8 collective-permute-done.4.refs_1_.refs_7_
  49.4 32.6 %collective-permute-done.5.refs_2_.refs_8_ = bf16[4,288,512]{2,1,0:T(8,128)(2,1)S(1)} collective-permute-done((bf16[4,288,512]{2,1,0:T(8,128)(2,1)S(1)}, bf16[4,288,512]{2,1,0:T(8,128)(2,1)S(1)}, u32[]{:S(2)}, u32[]{:S(2)}) %collective-permute-start.5) | collective-permute-done | bytes 1179680 | tf_op jit(solution)/shard_map/ppermute | solution.py:681
  82.0 1.1 copy-done.6
  83.1 1.7 copy-done.1
  84.8 1.3 copy-done.7
  86.0 4.8 %multiply.1.after_ref.acc_hbm = f32[512,512]{1,0:T(8,128)S(1)} custom-call(s32[5]{0:T(128)S(1)} %copy-done.21, bf16[4,288,512]{2,1,0:T(8,128)(2,1)S(1)} %stack.25.refs_0_.after_ref.refs_6_, bf16[4,288,512]{2,1,0:T(8,128)(2,1)} %collective-permute-done.4.refs_1_.refs_7_, bf16[4,288,512]{2,1,0:T(8,128)(2,1)S(1)} %copy-done.7, bf16[256,4608]{1,0:T(8,128)(2,1)S(1)} %copy-done.1, ...), custom_call_target="tpu_custom_call" | custom-call | tf_op jit(solution)/shard_map/multiply/pallas_call | solution.py:272
  90.8 3.0 %unpack.1 = (bf16[512,512]{1,0:T(8,128)(2,1)S(1)}, bf16[512,512]{1,0:T(8,128)(2,1)S(1)}) custom-call(s32[512,1]{1,0:T(8,128)S(1)} %copy.28.slot_ref, bf16[1024,1024]{1,0:T(8,128)(2,1)} %bitcast.17.came_ref, f32[512,512]{1,0:T(8,128)S(1)} %multiply.1.after_ref.acc_hbm), custom_call_target="tpu_custom_call" | custom-call | tf_op jit(solution)/shard_map/unpack/pallas_call | solution.py:168
  93.9 3.4 %merge.1 = (bf16[512,512]{1,0:T(8,128)(2,1)S(1)}, f32[512,512]{1,0:T(8,128)S(1)}, f32[8,512]{1,0:T(8,128)S(1)}) custom-call(s32[5]{0:T(128)S(1)} %copy-done.21, bf16[1,512]{1,0:T(2,128)(2,1)S(1)} %constant_dynamic-slice_fusion.1.ngain_ref.refs_1_, f32[512,512]{1,0:T(8,128)S(1)} %multiply.1.after_ref.acc_hbm, ...), custom_call_target="tpu_custom_call" | custom-call | tf_op jit(solution)/shard_map/merge/pallas_call | solution.py:314
  98.6 1.9 %collective-permute-start.10 = (f32[8,512]{1,0:T(8,128)S(1)}, f32[8,512]{1,0:T(8,128)S(1)}, u32[]{:S(2)}, u32[]{:S(2)}) collective-permute-start(f32[8,512]{1,0:T(8,128)S(1)} %get-tuple-element.57.after_ref.refs_2_), channel_id=1, source_target_pairs={{0,2},{1,3},{2,0},{3,1},{64,66},{65,67},{66,64},{67,65},{4,6},{5,7... | collective-permute-start | bytes 49160 | tf_op jit(solution)/shard_map/ppermute | solution.py:669
  100.4 2.2 %collective-permute-start.11 = (f32[8,512]{1,0:T(8,128)S(1)}, f32[8,512]{1,0:T(8,128)S(1)}, u32[]{:S(2)}, u32[]{:S(2)}) collective-permute-start(f32[8,512]{1,0:T(8,128)S(1)} %get-tuple-element.56), channel_id=1, source_target_pairs={{0,66},{1,67},{2,64},{3,65},{64,0},{65,1},{66,2},{67,3},{4,70},{5,... | collective-permute-start | bytes 49160 | tf_op jit(solution)/shard_map/ppermute | solution.py:669
  102.7 1.4 pack.1
  104.1 2.4 %collective-permute-done.9.refs_3_ = f32[8,512]{1,0:T(8,128)S(1)} collective-permute-done((f32[8,512]{1,0:T(8,128)S(1)}, f32[8,512]{1,0:T(8,128)S(1)}, u32[]{:S(2)}, u32[]{:S(2)}) %collective-permute-start.9) | collective-permute-done | bytes 16416 | tf_op jit(solution)/shard_map/ppermute | solution.py:669
  106.5 5.4 %backward.1 = (bf16[256,4608]{1,0:T(8,128)(2,1)S(1)}, bf16[256,4608]{1,0:T(8,128)(2,1)S(1)}) custom-call(s32[5]{0:T(128)S(1)} %copy-done.21, bf16[1,512]{1,0:T(2,128)(2,1)S(1)} %constant_dynamic-slice_fusion.1.ngain_ref.refs_1_, f32[8,512]{1,0:T(8,128)S(1)} %get-tuple-element.57.after_ref.refs_2_, f32[8,512]{1,0:T(8,128)S(1)} %collective-permute-done.9.refs_3_, ...), custom_call_target="tpu_custom_call" | custom-call | tf_op jit(solution)/shard_map/backward/pallas_call | solution.py:450
  111.9 5.9 %collective-permute-done.12.after_ref.crossed_ref = bf16[512,512]{1,0:T(8,128)(2,1)S(1)} collective-permute-done((bf16[512,512]{1,0:T(8,128)(2,1)S(1)}, bf16[512,512]{1,0:T(8,128)(2,1)S(1)}, u32[]{:S(2)}, u32[]{:S(2)}) %collective-permute-start.12) | collective-permute-done | bytes 524320 | tf_op jit(solution)/shard_map/ppermute | solution.py:738
  117.8 3.0 %collective-permute-start.13 = (bf16[256,4608]{1,0:T(8,128)(2,1)S(1)}, bf16[256,4608]{1,0:T(8,128)(2,1)S(1)}, u32[]{:S(2)}, u32[]{:S(2)}) collective-permute-start(bf16[256,4608]{1,0:T(8,128)(2,1)S(1)} %get-tuple-element.66), channel_id=1, source_target_pairs={{0,1},{1,0},{2,3},{3,2},{4,5},{5,4},{6,7},{7,6},{8,9},{9,8},{10,11... | collective-permute-start | bytes 7077896 | tf_op jit(solution)/shard_map/ppermute | solution.py:742
  120.8 4.2 %collective-permute-done.13.got_ref = bf16[256,4608]{1,0:T(8,128)(2,1)S(1)} collective-permute-done((bf16[256,4608]{1,0:T(8,128)(2,1)S(1)}, bf16[256,4608]{1,0:T(8,128)(2,1)S(1)}, u32[]{:S(2)}, u32[]{:S(2)}) %collective-permute-start.13) | collective-permute-done | bytes 2359328 | tf_op jit(solution)/shard_map/ppermute | solution.py:742
  125.0 1.6 pair.1
  127.6 2.7 %collective-permute-start.15 = (bf16[64,4608]{1,0:T(8,128)(2,1)}, bf16[64,4608]{1,0:T(8,128)(2,1)S(1)}, u32[]{:S(2)}, u32[]{:S(2)}) collective-permute-start(bf16[64,4608]{1,0:T(8,128)(2,1)} %get-tuple-element.69), channel_id=1, source_target_pairs={{0,66},{1,67},{2,64},{3,65},{64,0},{65,1},{66,2},{67,3},{4,70},{5,... | collective-permute-start | bytes 1769480 | tf_op jit(solution)/shard_map/ppermute | solution.py:669
  130.3 1.0 braid.1
  131.3 6.0 %all-to-all-start.2 = ((bf16[16,2,32,512]{3,2,1,0:T(8,128)(2,1)}), bf16[16,2,32,512]{3,2,1,0:T(8,128)(2,1)S(1)}, u32[]{:S(2)}, u32[]{:S(2)}) async-start(bf16[16,2,32,512]{3,2,1,0:T(8,128)(2,1)} %braid.1), calls=%async_computation.2 | async-start | bytes 2097152 | tf_op jit(solution)/shard_map/all_to_all | solution.py:749
  137.3 6.3 %collective-permute-done.14.from_last_ref = bf16[64,4608]{1,0:T(8,128)(2,1)S(1)} collective-permute-done((bf16[64,4608]{1,0:T(8,128)(2,1)}, bf16[64,4608]{1,0:T(8,128)(2,1)S(1)}, u32[]{:S(2)}, u32[]{:S(2)}) %collective-permute-start.14) | collective-permute-done | bytes 589856 | tf_op jit(solution)/shard_map/ppermute | solution.py:669
  143.6 1.5 copy-done.16
  145.3 2.7 %collective-permute-start.17 = (bf16[32,4608]{1,0:T(8,128)(2,1)S(1)}, bf16[32,4608]{1,0:T(8,128)(2,1)S(1)}, u32[]{:S(2)}, u32[]{:S(2)}) collective-permute-start(bf16[32,4608]{1,0:T(8,128)(2,1)S(1)} %get-tuple-element.72), channel_id=1, source_target_pairs={{0,66},{1,67},{2,64},{3,65},{64,0},{65,1},{66,2},{67,3},{4,70},{5,... | collective-permute-start | bytes 884744 | tf_op jit(solution)/shard_map/ppermute | solution.py:669
  148.0 5.8 %collective-permute-done.16.late_last_ref = bf16[32,4608]{1,0:T(8,128)(2,1)S(1)} collective-permute-done((bf16[32,4608]{1,0:T(8,128)(2,1)S(1)}, bf16[32,4608]{1,0:T(8,128)(2,1)S(1)}, u32[]{:S(2)}, u32[]{:S(2)}) %collective-permute-start.16) | collective-permute-done | bytes 294944 | tf_op jit(solution)/shard_map/ppermute | solution.py:669
  154.6 5.0 %finish.1.refs_0_ = bf16[256,1152]{1,0:T(8,128)(2,1)} custom-call(s32[5]{0:T(128)} %stack.24.here_ref.refs_0_, bf16[256,4608]{1,0:T(8,128)(2,1)} %copy-done.3, bf16[256,4608]{1,0:T(8,128)(2,1)} %copy-done.4, bf16[64,4608]{1,0:T(8,128)(2,1)} %copy-done.12, bf16[64,4608]{1,0:T(8,128)(2,1)} %copy-done.13, bf16[32,4608]{1,0:T(8,128)(2,1)} %copy-done.23, ...), custom_call_target="tpu_custom_call" | custom-call | tf_op jit(solution)/shard_map/finish/pallas_call | solution.py:561
  159.6 1.4 collective-permute-start.18
  161.0 2.4 %place.1 = bf16[512,1024]{1,0:T(8,128)(2,1)} custom-call(s32[5]{0:T(128)S(1)} %copy-done.22, s32[512,1]{1,0:T(8,128)S(1)} %reshape.38.pos_ref, bf16[16,2,32,512]{3,2,1,0:T(8,128)(2,1)S(1)} %all-to-all-done.2.came_ref, bf16[512,1024]{1,0:T(8,128)(2,1)S(1)} %copy-done.10), custom_call_target="tpu_custom_call" | custom-call | tf_op jit(solution)/shard_map/place/pallas_call | solution.py:602
  163.4 3.0 %collective-permute-start.19 = (bf16[256,1152]{1,0:T(8,128)(2,1)S(1)}, bf16[256,1152]{1,0:T(8,128)(2,1)S(1)}, u32[]{:S(2)}, u32[]{:S(2)}) collective-permute-start(bf16[256,1152]{1,0:T(8,128)(2,1)S(1)} %copy-done.11), channel_id=1, source_target_pairs={{0,1},{1,0},{2,3},{3,2},{4,5},{5,4},{6,7},{7,6},{8,9},{9,8},{10,11... | collective-permute-start | bytes 1769480 | tf_op jit(solution)/shard_map/ppermute | solution.py:755
  166.4 7.7 %collective-permute-done.18.refs_1_ = bf16[256,1152]{1,0:T(8,128)(2,1)} collective-permute-done((bf16[256,1152]{1,0:T(8,128)(2,1)}, bf16[256,1152]{1,0:T(8,128)(2,1)}, u32[]{:S(2)}, u32[]{:S(2)}) %collective-permute-start.18) | collective-permute-done | bytes 589856 | tf_op jit(solution)/shard_map/ppermute | solution.py:753
  174.1 3.0 %collective-permute-start.20 = (bf16[256,1152]{1,0:T(8,128)(2,1)}, bf16[256,1152]{1,0:T(8,128)(2,1)S(1)}, u32[]{:S(2)}, u32[]{:S(2)}) collective-permute-start(bf16[256,1152]{1,0:T(8,128)(2,1)} %collective-permute-done.18.refs_1_), channel_id=1, source_target_pairs={{0,1},{1,0},{2,3},{3,2},{4,5},{5,4},{6,7},{7,6},{8,9},{9,8},{10,11... | collective-permute-start | bytes 1769480 | tf_op jit(solution)/shard_map/ppermute | solution.py:755
  177.1 1.8 %collective-permute-done.20.refs_3_ = bf16[256,1152]{1,0:T(8,128)(2,1)S(1)} collective-permute-done((bf16[256,1152]{1,0:T(8,128)(2,1)}, bf16[256,1152]{1,0:T(8,128)(2,1)S(1)}, u32[]{:S(2)}, u32[]{:S(2)}) %collective-permute-start.20) | collective-permute-done | bytes 589856 | tf_op jit(solution)/shard_map/ppermute | solution.py:755
  179.0 2.5 %lay.1 = bf16[1024,1152]{1,0:T(8,128)(2,1)} custom-call(s32[5]{0:T(128)S(1)} %copy-done.22, bf16[256,1152]{1,0:T(8,128)(2,1)S(1)} %copy-done.11, bf16[256,1152]{1,0:T(8,128)(2,1)} %collective-permute-done.18.refs_1_, bf16[256,1152]{1,0:T(8,128)(2,1)S(1)} %collective-permute-done.19.refs_2_, bf16[256,1152]{1,0:T(8,128)(2,1)S(1)} %collective-permute-done.20.refs_3_), custom_call_target="tpu_custom_call" | custom-call | tf_op jit(solution)/shard_map/lay/pallas_call | solution.py:629
  (80 shorter events, 9.2 us)
Async XLA Ops:
  0.6 1.1 copy-start
  1.7 24.3 %collective-permute-start = (bf16[288,512]{1,0:T(8,128)(2,1)S(1)}, bf16[288,512]{1,0:T(8,128)(2,1)S(1)}, u32[]{:S(2)}, u32[]{:S(2)}) collective-permute-start(bf16[288,512]{1,0:T(8,128)(2,1)S(1)} %bitcast.22), channel_id=1, source_target_pairs={{0,4},{1,17},{2,6},{3,19},{4,8},{5,21},{6,10},{7,23},{8,12},{9,25}... | collective-permute-start | bytes 884744 | tf_op jit(solution)/shard_map/ppermute | solution.py:681
  4.3 21.8 %collective-permute-start.1 = (bf16[288,512]{1,0:T(8,128)(2,1)S(1)}, bf16[288,512]{1,0:T(8,128)(2,1)S(1)}, u32[]{:S(2)}, u32[]{:S(2)}) collective-permute-start(bf16[288,512]{1,0:T(8,128)(2,1)S(1)} %bitcast.23), channel_id=1, source_target_pairs={{0,12},{1,49},{2,14},{3,51},{4,0},{5,53},{6,2},{7,55},{8,4},{9,57}... | collective-permute-start | bytes 884744 | tf_op jit(solution)/shard_map/ppermute | solution.py:681
  6.5 20.3 %collective-permute-start.2 = (bf16[288,512]{1,0:T(8,128)(2,1)S(1)}, bf16[288,512]{1,0:T(8,128)(2,1)S(1)}, u32[]{:S(2)}, u32[]{:S(2)}) collective-permute-start(bf16[288,512]{1,0:T(8,128)(2,1)S(1)} %bitcast.24), channel_id=1, source_target_pairs={{0,8},{1,33},{2,10},{3,35},{4,12},{5,37},{6,14},{7,39},{8,0},{9,41... | collective-permute-start | bytes 884744 | tf_op jit(solution)/shard_map/ppermute | solution.py:681
  9.5 16.5 %all-to-all-start = ((s32[32,1,16]{2,1,0:T(1,128)}), s32[32,1,16]{2,1,0:T(1,128)S(1)}, u32[]{:S(2)}, u32[]{:S(2)}) async-start(s32[32,1,16]{2,1,0:T(1,128)} %bitcast.5), calls=%async_computation | async-start | bytes 32768 | tf_op jit(solution)/shard_map/all_to_all | solution.py:693
  16.5 9.6 %collective-permute-start.3 = (s32[256]{0:T(256)S(1)}, s32[256]{0:T(256)S(1)}, u32[]{:S(2)}, u32[]{:S(2)}) collective-permute-start(s32[256]{0:T(256)S(1)} %get-tuple-element.80), channel_id=1, source_target_pairs={{0,64},{64,0},{1,65},{65,1},{2,66},{66,2},{3,67},{67,3},{4,68},{68... | collective-permute-start | bytes 3080 | tf_op jit(solution)/shard_map/ppermute | solution.py:700
  18.4 10.6 %copy-start.21 = (s32[5]{0:T(128)S(1)}, s32[5]{0:T(128)}, u32[]{:S(2)}) copy-start(s32[5]{0:T(128)} %stack.24.here_ref.refs_0_) | copy-start | bytes 64
  18.4 14.9 %copy-start.9 = (bf16[512,1024]{1,0:T(8,128)(2,1)S(1)}, bf16[512,1024]{1,0:T(8,128)(2,1)}, u32[]{:S(2)}) copy-start(bf16[512,1024]{1,0:T(8,128)(2,1)} %stream_ref.3) | copy-start | bytes 3145732
  26.8 0.7 copy-start.19
  27.5 55.6 %collective-permute-start.6 = (bf16[256,4608]{1,0:T(8,128)(2,1)}, bf16[256,4608]{1,0:T(8,128)(2,1)}, u32[]{:S(2)}, u32[]{:S(2)}) collective-permute-start(bf16[256,4608]{1,0:T(8,128)(2,1)} %get-tuple-element.48.refs_3_.refs_0_), channel_id=1, source_target_pairs={{0,66},{1,67},{2,64},{3,65},{64,2},{65,3},{66,0},{67,1},{4,70},{5,... | collective-permute-start | bytes 7077896 | tf_op jit(solution)/shard_map/ppermute | solution.py:727
  29.0 1.0 copy-start.18
  30.0 1.0 copy-start.20
  31.8 16.7 %collective-permute-start.4 = (bf16[4,288,512]{2,1,0:T(8,128)(2,1)S(1)}, bf16[4,288,512]{2,1,0:T(8,128)(2,1)}, u32[]{:S(2)}, u32[]{:S(2)}) collective-permute-start(bf16[4,288,512]{2,1,0:T(8,128)(2,1)S(1)} %stack.25.refs_0_.after_ref.refs_6_), channel_id=1, source_target_pairs={{0,16},{1,5},{2,18},{3,7},{4,20},{5,9},{6,22},{7,11},{8,24},{9,13}... | collective-permute-start | bytes 3538952 | tf_op jit(solution)/shard_map/ppermute | solution.py:681
  33.3 1.2 copy-start.14
  35.8 1.4 copy-start.5
  37.2 12.0 %copy-start.25 = (bf16[1,1024]{1,0:T(2,128)(2,1)S(1)}, bf16[1,1024]{1,0:T(2,128)(2,1)}, u32[]{:S(2)}) copy-start(bf16[1,1024]{1,0:T(2,128)(2,1)} %param.13) | copy-start | bytes 6148
  37.2 53.6 %all-to-all-start.1 = ((bf16[32,32,1024]{2,1,0:T(8,128)(2,1)}), bf16[32,32,1024]{2,1,0:T(8,128)(2,1)}, u32[]{:S(2)}, u32[]{:S(2)}) async-start(bf16[32,32,1024]{2,1,0:T(8,128)(2,1)} %bitcast.21), calls=%async_computation.1 | async-start | bytes 4194304 | tf_op jit(solution)/shard_map/all_to_all | solution.py:714
  44.3 37.7 %collective-permute-start.5 = (bf16[4,288,512]{2,1,0:T(8,128)(2,1)S(1)}, bf16[4,288,512]{2,1,0:T(8,128)(2,1)S(1)}, u32[]{:S(2)}, u32[]{:S(2)}) collective-permute-start(bf16[4,288,512]{2,1,0:T(8,128)(2,1)S(1)} %stack.25.refs_0_.after_ref.refs_6_), channel_id=1, source_target_pairs={{0,48},{1,13},{2,50},{3,15},{4,52},{5,1},{6,54},{7,3},{8,56},{9,5}... | collective-permute-start | bytes 3538952 | tf_op jit(solution)/shard_map/ppermute | solution.py:681
  48.5 45.4 %collective-permute-start.7 = (bf16[4,288,512]{2,1,0:T(8,128)(2,1)}, bf16[4,288,512]{2,1,0:T(8,128)(2,1)}, u32[]{:S(2)}, u32[]{:S(2)}) collective-permute-start(bf16[4,288,512]{2,1,0:T(8,128)(2,1)} %collective-permute-done.4.refs_1_.refs_7_), channel_id=1, source_target_pairs={{0,16},{1,5},{2,18},{3,7},{4,20},{5,9},{6,22},{7,11},{8,24},{9,13}... | collective-permute-start | bytes 3538952 | tf_op jit(solution)/shard_map/ppermute | solution.py:681
  82.0 1.1 copy-start.6
  83.1 1.7 copy-start.1
  84.8 1.3 copy-start.7
  90.8 3.0 %copy-start.2 = (bf16[256,4608]{1,0:T(8,128)(2,1)S(1)}, bf16[256,4608]{1,0:T(8,128)(2,1)}, u32[]{:S(2)}) copy-start(bf16[256,4608]{1,0:T(8,128)(2,1)} %get-tuple-element.48.refs_3_.refs_0_) | copy-start | bytes 7077892
  93.9 12.6 %copy-start.8 = (bf16[4,288,512]{2,1,0:T(8,128)(2,1)S(1)}, bf16[4,288,512]{2,1,0:T(8,128)(2,1)}, u32[]{:S(2)}) copy-start(bf16[4,288,512]{2,1,0:T(8,128)(2,1)} %copy-done.6) | copy-start | bytes 3538948
  97.3 1.3 collective-permute-start.8
  98.6 5.5 %collective-permute-start.10 = (f32[8,512]{1,0:T(8,128)S(1)}, f32[8,512]{1,0:T(8,128)S(1)}, u32[]{:S(2)}, u32[]{:S(2)}) collective-permute-start(f32[8,512]{1,0:T(8,128)S(1)} %get-tuple-element.57.after_ref.refs_2_), channel_id=1, source_target_pairs={{0,2},{1,3},{2,0},{3,1},{64,66},{65,67},{66,64},{67,65},{4,6},{5,7... | collective-permute-start | bytes 49160 | tf_op jit(solution)/shard_map/ppermute | solution.py:669
  100.4 3.7 %collective-permute-start.11 = (f32[8,512]{1,0:T(8,128)S(1)}, f32[8,512]{1,0:T(8,128)S(1)}, u32[]{:S(2)}, u32[]{:S(2)}) collective-permute-start(f32[8,512]{1,0:T(8,128)S(1)} %get-tuple-element.56), channel_id=1, source_target_pairs={{0,66},{1,67},{2,64},{3,65},{64,0},{65,1},{66,2},{67,3},{4,70},{5,... | collective-permute-start | bytes 49160 | tf_op jit(solution)/shard_map/ppermute | solution.py:669
  102.7 3.8 %collective-permute-start.9 = (f32[8,512]{1,0:T(8,128)S(1)}, f32[8,512]{1,0:T(8,128)S(1)}, u32[]{:S(2)}, u32[]{:S(2)}) collective-permute-start(f32[8,512]{1,0:T(8,128)S(1)} %get-tuple-element.56), channel_id=1, source_target_pairs={{0,64},{1,65},{2,66},{3,67},{64,2},{65,3},{66,0},{67,1},{4,68},{5,... | collective-permute-start | bytes 49160 | tf_op jit(solution)/shard_map/ppermute | solution.py:669
  106.5 11.4 %collective-permute-start.12 = (bf16[512,512]{1,0:T(8,128)(2,1)S(1)}, bf16[512,512]{1,0:T(8,128)(2,1)S(1)}, u32[]{:S(2)}, u32[]{:S(2)}) collective-permute-start(bf16[512,512]{1,0:T(8,128)(2,1)S(1)} %get-tuple-element.64), channel_id=1, source_target_pairs={{0,64},{64,0},{1,65},{65,1},{2,66},{66,2},{3,67},{67,3},{4,68},{68... | collective-permute-start | bytes 1572872 | tf_op jit(solution)/shard_map/ppermute | solution.py:738
  111.9 14.7 %copy-start.3 = (bf16[256,4608]{1,0:T(8,128)(2,1)}, bf16[256,4608]{1,0:T(8,128)(2,1)S(1)}, u32[]{:S(2)}) copy-start(bf16[256,4608]{1,0:T(8,128)(2,1)S(1)} %get-tuple-element.65.own_ref) | copy-start | bytes 7077892
  117.8 7.1 %collective-permute-start.13 = (bf16[256,4608]{1,0:T(8,128)(2,1)S(1)}, bf16[256,4608]{1,0:T(8,128)(2,1)S(1)}, u32[]{:S(2)}, u32[]{:S(2)}) collective-permute-start(bf16[256,4608]{1,0:T(8,128)(2,1)S(1)} %get-tuple-element.66), channel_id=1, source_target_pairs={{0,1},{1,0},{2,3},{3,2},{4,5},{5,4},{6,7},{7,6},{8,9},{9,8},{10,11... | collective-permute-start | bytes 7077896 | tf_op jit(solution)/shard_map/ppermute | solution.py:742
  125.0 1.8 copy-start.4
  126.8 0.8 copy-start.15
  127.6 16.0 %collective-permute-start.14 = (bf16[64,4608]{1,0:T(8,128)(2,1)}, bf16[64,4608]{1,0:T(8,128)(2,1)S(1)}, u32[]{:S(2)}, u32[]{:S(2)}) collective-permute-start(bf16[64,4608]{1,0:T(8,128)(2,1)} %get-tuple-element.68), channel_id=1, source_target_pairs={{0,64},{1,65},{2,66},{3,67},{64,2},{65,3},{66,0},{67,1},{4,68},{5,... | collective-permute-start | bytes 1769480 | tf_op jit(solution)/shard_map/ppermute | solution.py:669
  127.6 16.0 %collective-permute-start.15 = (bf16[64,4608]{1,0:T(8,128)(2,1)}, bf16[64,4608]{1,0:T(8,128)(2,1)S(1)}, u32[]{:S(2)}, u32[]{:S(2)}) collective-permute-start(bf16[64,4608]{1,0:T(8,128)(2,1)} %get-tuple-element.69), channel_id=1, source_target_pairs={{0,66},{1,67},{2,64},{3,65},{64,0},{65,1},{66,2},{67,3},{4,70},{5,... | collective-permute-start | bytes 1769480 | tf_op jit(solution)/shard_map/ppermute | solution.py:669
  131.3 29.7 %all-to-all-start.2 = ((bf16[16,2,32,512]{3,2,1,0:T(8,128)(2,1)}), bf16[16,2,32,512]{3,2,1,0:T(8,128)(2,1)S(1)}, u32[]{:S(2)}, u32[]{:S(2)}) async-start(bf16[16,2,32,512]{3,2,1,0:T(8,128)(2,1)} %braid.1), calls=%async_computation.2 | async-start | bytes 2097152 | tf_op jit(solution)/shard_map/all_to_all | solution.py:749
  143.6 10.2 %copy-start.12 = (bf16[64,4608]{1,0:T(8,128)(2,1)}, bf16[64,4608]{1,0:T(8,128)(2,1)S(1)}, u32[]{:S(2)}) copy-start(bf16[64,4608]{1,0:T(8,128)(2,1)S(1)} %collective-permute-done.14.from_last_ref) | copy-start | bytes 1769476
  143.6 10.2 %copy-start.13 = (bf16[64,4608]{1,0:T(8,128)(2,1)}, bf16[64,4608]{1,0:T(8,128)(2,1)S(1)}, u32[]{:S(2)}) copy-start(bf16[64,4608]{1,0:T(8,128)(2,1)S(1)} %collective-permute-done.15.from_next_ref) | copy-start | bytes 1769476
  143.6 1.5 copy-start.16
  145.2 8.6 %collective-permute-start.16 = (bf16[32,4608]{1,0:T(8,128)(2,1)S(1)}, bf16[32,4608]{1,0:T(8,128)(2,1)S(1)}, u32[]{:S(2)}, u32[]{:S(2)}) collective-permute-start(bf16[32,4608]{1,0:T(8,128)(2,1)S(1)} %get-tuple-element.71), channel_id=1, source_target_pairs={{0,64},{1,65},{2,66},{3,67},{64,2},{65,3},{66,0},{67,1},{4,68},{5,... | collective-permute-start | bytes 884744 | tf_op jit(solution)/shard_map/ppermute | solution.py:669
  145.3 8.5 %collective-permute-start.17 = (bf16[32,4608]{1,0:T(8,128)(2,1)S(1)}, bf16[32,4608]{1,0:T(8,128)(2,1)S(1)}, u32[]{:S(2)}, u32[]{:S(2)}) collective-permute-start(bf16[32,4608]{1,0:T(8,128)(2,1)S(1)} %get-tuple-element.72), channel_id=1, source_target_pairs={{0,66},{1,67},{2,64},{3,65},{64,0},{65,1},{66,2},{67,3},{4,70},{5,... | collective-permute-start | bytes 884744 | tf_op jit(solution)/shard_map/ppermute | solution.py:669
  153.8 0.8 copy-start.24
  154.6 6.4 %copy-start.10 = (bf16[512,1024]{1,0:T(8,128)(2,1)S(1)}, bf16[512,1024]{1,0:T(8,128)(2,1)}, u32[]{:S(2)}) copy-start(bf16[512,1024]{1,0:T(8,128)(2,1)} %stream_ref.3) | copy-start | bytes 3145732
  154.6 6.4 %copy-start.22 = (s32[5]{0:T(128)S(1)}, s32[5]{0:T(128)}, u32[]{:S(2)}) copy-start(s32[5]{0:T(128)} %stack.24.here_ref.refs_0_) | copy-start | bytes 64
  159.6 3.8 %copy-start.11 = (bf16[256,1152]{1,0:T(8,128)(2,1)S(1)}, bf16[256,1152]{1,0:T(8,128)(2,1)}, u32[]{:S(2)}) copy-start(bf16[256,1152]{1,0:T(8,128)(2,1)} %finish.1.refs_0_) | copy-start | bytes 1769476
  159.6 14.5 %collective-permute-start.18 = (bf16[256,1152]{1,0:T(8,128)(2,1)}, bf16[256,1152]{1,0:T(8,128)(2,1)}, u32[]{:S(2)}, u32[]{:S(2)}) collective-permute-start(bf16[256,1152]{1,0:T(8,128)(2,1)} %finish.1.refs_0_), channel_id=1, source_target_pairs={{0,2},{1,3},{2,0},{3,1},{4,6},{5,7},{6,4},{7,5},{8,10},{9,11},{10,... | collective-permute-start | bytes 1769480 | tf_op jit(solution)/shard_map/ppermute | solution.py:753
  163.4 13.8 %collective-permute-start.19 = (bf16[256,1152]{1,0:T(8,128)(2,1)S(1)}, bf16[256,1152]{1,0:T(8,128)(2,1)S(1)}, u32[]{:S(2)}, u32[]{:S(2)}) collective-permute-start(bf16[256,1152]{1,0:T(8,128)(2,1)S(1)} %copy-done.11), channel_id=1, source_target_pairs={{0,1},{1,0},{2,3},{3,2},{4,5},{5,4},{6,7},{7,6},{8,9},{9,8},{10,11... | collective-permute-start | bytes 1769480 | tf_op jit(solution)/shard_map/ppermute | solution.py:755
  174.1 4.9 %collective-permute-start.20 = (bf16[256,1152]{1,0:T(8,128)(2,1)}, bf16[256,1152]{1,0:T(8,128)(2,1)S(1)}, u32[]{:S(2)}, u32[]{:S(2)}) collective-permute-start(bf16[256,1152]{1,0:T(8,128)(2,1)} %collective-permute-done.18.refs_1_), channel_id=1, source_target_pairs={{0,1},{1,0},{2,3},{3,2},{4,5},{5,4},{6,7},{7,6},{8,9},{9,8},{10,11... | collective-permute-start | bytes 1769480 | tf_op jit(solution)/shard_map/ppermute | solution.py:755
  (2 other events, 1.4 us)

commit v14 on v13

--- a/solution.py
+++ b/solution.py
@@ -177,16 +177,18 @@
 
 
 def stack_kernel(here_ref, *refs):
-    out_ref, sems = refs[RING:]
+    halves, sems = refs[RING : RING + 2], refs[RING + 2]
     first = jnp.where(here_ref[0] == 0, here_ref[4], here_ref[3])
-    copies = [
-        pltpu.make_async_copy(ref, out_ref.at[lax.rem(first + away, RING)], sems.at[index])
-        for index, (away, ref) in enumerate(zip(AWAY, refs[:RING]))
-    ]
-    for copy in copies:
-        copy.start()
-    for copy in copies:
-        copy.wait()
+    for index, (away, ref) in enumerate(zip(AWAY, refs[:RING])):
+        place = lax.rem(first + away, RING)
+        for side, half in enumerate(halves):
+
+            @pl.when(place // 2 == side)
+            def _():
+                pltpu.make_async_copy(ref, half.at[lax.rem(place, 2)], sems.at[index]).start()
+
+    for index, ref in enumerate(refs[:RING]):
+        pltpu.make_async_copy(ref, halves[0].at[0], sems.at[index]).wait()
 
 
 def stack(here, blocks):
@@ -194,8 +196,8 @@
     return pl.pallas_call(
         stack_kernel,
         in_specs=[scalars()] + [in_hbm()] * RING,
-        out_specs=whole(),
-        out_shape=shape((RING, rows, width), BF),
+        out_specs=[whole()] * 2,
+        out_shape=[shape((2, rows, width), BF)] * 2,
         scratch_shapes=[pltpu.SemaphoreType.DMA((RING,))],
         compiler_params=params(6),
         cost_estimate=FREE,
@@ -204,21 +206,22 @@
 
 
 def fetch(here_ref, stacks, held_ref, sems):
-    for index, (away, ref) in enumerate(zip(AWAY, stacks)):
+    for index, ref in enumerate(stacks):
+        away, side = AWAY[index // 2], pl.ds(2 * (index % 2), 2)
 
         @pl.when(here_ref[0] == 0)
         def _():
             place = lax.rem(here_ref[3] + away, RING)
-            pltpu.make_async_copy(ref, held_ref.at[place], sems.at[index]).start()
+            pltpu.make_async_copy(ref, held_ref.at[place, side], sems.at[index]).start()
 
         @pl.when(here_ref[0] == 1)
         def _():
             place = lax.rem(here_ref[4] + away, RING)
-            pltpu.make_async_copy(ref, held_ref.at[:, place], sems.at[index]).start()
+            pltpu.make_async_copy(ref, held_ref.at[side, place], sems.at[index]).start()
 
     def wait():
         for index, ref in enumerate(stacks):
-            pltpu.make_async_copy(ref, held_ref.at[0], sems.at[index]).wait()
+            pltpu.make_async_copy(ref, held_ref.at[0, pl.ds(0, 2)], sems.at[index]).wait()
 
     return wait
 
@@ -228,13 +231,18 @@
     block = left_ref.shape[2]
     rows = lifted[0].shape[0]
     copies = []
-    for index, ref in enumerate(stacks):
+    for index in range(len(stacks) // 2):
         place = lax.rem(second + away[index], RING)
         at = pl.ds(pl.multiple_of(place * block, block), block)
-        group = [pltpu.make_async_copy(ref, held_ref.at[index], sems.at[index, 0])]
+        group = [
+            pltpu.make_async_copy(
+                stacks[2 * index + side], held_ref.at[index, pl.ds(2 * side, 2)], sems.at[index, side]
+            )
+            for side in range(2)
+        ]
         for i, part in enumerate(lifted):
             to = left_ref.at[index, pl.ds(i * rows, rows)]
-            group.append(pltpu.make_async_copy(part.at[:, at], to, sems.at[index, 1 + i]))
+            group.append(pltpu.make_async_copy(part.at[:, at], to, sems.at[index, 2 + i]))
         for copy in group:
             copy.start()
         copies.append(group)
@@ -253,17 +261,19 @@
 
 
 def product_scratch(stacks, lifted):
-    count = len(stacks)
+    count = len(stacks) // 2
     rows, depth = lifted[0].shape
+    _, block_rows, width = stacks[0].shape
     return [
-        pltpu.VMEM((count,) + stacks[0].shape, BF),
+        pltpu.VMEM((count, RING, block_rows, width), BF),
         pltpu.VMEM((count, len(lifted) * rows, depth // RING), BF),
-        pltpu.SemaphoreType.DMA((count, 1 + len(lifted))),
+        pltpu.SemaphoreType.DMA((count, 2 + len(lifted))),
     ]
 
 
 def multiply_kernel(here_ref, *refs):
-    stacks, lifted, (out_ref, *scratch) = refs[: RING - 1], refs[RING - 1 : RING + 1], refs[RING + 1 :]
+    count = 2 * (RING - 1)
+    stacks, lifted, (out_ref, *scratch) = refs[:count], refs[count : count + 2], refs[count + 2 :]
     out_ref[...] = product(here_ref, AWAY[: RING - 1], stacks, lifted, *scratch)(None)
 
 
@@ -281,10 +291,10 @@
     )(here, *stacks, *lifted)
 
 
-def merge_kernel(here_ref, ngain_ref, acc_hbm, base_hbm, cot_hbm, stack_ref, *refs):
-    lifted, refs = refs[:2], refs[2:]
+def merge_kernel(here_ref, ngain_ref, acc_hbm, base_hbm, cot_hbm, *refs):
+    stacks, lifted, refs = refs[:2], refs[2:4], refs[4:]
     visual_ref, state_ref, stat_ref, acc_ref, base_ref, cot_ref, row_sems, *scratch = refs
-    run = product(here_ref, AWAY[RING - 1 :], (stack_ref,), lifted, *scratch)
+    run = product(here_ref, AWAY[RING - 1 :], stacks, lifted, *scratch)
     copies = [
         pltpu.make_async_copy(a, b, row_sems.at[i])
         for i, (a, b) in enumerate(((acc_hbm, acc_ref), (base_hbm, base_ref), (cot_hbm, cot_ref)))
@@ -308,12 +318,12 @@
     stat_ref[...] = sums.T[: stat_ref.shape[0]]
 
 
-def merge(here, ngain, acc, base, cot, stack, lifted):
+def merge(here, ngain, acc, base, cot, stacks, lifted):
     tokens, width = base.shape
     outs = [shape((tokens, width), BF), shape((tokens, width), F32), shape((8, tokens), F32)]
     return pl.pallas_call(
         merge_kernel,
-        in_specs=[scalars(), whole()] + [in_hbm()] * 6,
+        in_specs=[scalars(), whole()] + [in_hbm()] * 7,
         out_specs=[whole()] * 3,
         out_shape=outs,
         scratch_shapes=[
@@ -322,11 +332,11 @@
             pltpu.VMEM((tokens, width), BF),
             pltpu.SemaphoreType.DMA((3,)),
         ]
-        + product_scratch((stack,), lifted),
+        + product_scratch(stacks, lifted),
         compiler_params=params(24),
         cost_estimate=FREE,
         name="merge",
-    )(here, ngain, acc, base, cot, stack, *lifted)
+    )(here, ngain, acc, base, cot, *stacks, *lifted)
 
 
 def add_kernel(sums_ref, got_ref, near_ref, turned_ref):
@@ -396,7 +406,7 @@
 
 
 def backward_kernel(full_width, here_ref, ngain_ref, *refs):
-    stats, stacks, refs = refs[:RING], refs[RING : 2 * RING], refs[2 * RING :]
+    stats, stacks, refs = refs[:RING], refs[RING : 3 * RING], refs[3 * RING :]
     state_hbm, cot_hbm, own_ref, other_ref = refs[:4]
     picked_ref, sums_ref, state_ref, cot_ref, held_ref, row_sems, sems = refs[4:]
     row_copies = [
@@ -446,10 +456,11 @@
 
 def backward(here, state, cot, ngain, stats, stacks, full_width):
     tokens, width = state.shape
-    depth = RING * stacks[0].shape[0] * stacks[0].shape[1]
+    _, block_rows, _ = stacks[0].shape
+    depth = RING * RING * block_rows
     return pl.pallas_call(
         lambda *refs: backward_kernel(full_width, *refs),
-        in_specs=[scalars()] + [whole()] * (1 + RING) + [in_hbm()] * (RING + 2),
+        in_specs=[scalars()] + [whole()] * (1 + RING) + [in_hbm()] * (2 * RING + 2),
         out_specs=[whole()] * 2,
         out_shape=[shape((tokens // 2, depth), BF)] * 2,
         scratch_shapes=[
@@ -457,9 +468,9 @@
             pltpu.VMEM((tokens, 8), F32),
             pltpu.VMEM((tokens, width), F32),
             pltpu.VMEM((tokens, width), BF),
-            pltpu.VMEM((RING,) + stacks[0].shape, BF),
+            pltpu.VMEM((RING, RING, block_rows, width), BF),
             pltpu.SemaphoreType.DMA((2,)),
-            pltpu.SemaphoreType.DMA((RING,)),
+            pltpu.SemaphoreType.DMA((2 * RING,)),
         ],
         compiler_params=params(24),
         cost_estimate=FREE,
@@ -710,26 +721,27 @@
 
     asked = asked.reshape(n_img, n_ctx, capacity).transpose(1, 0, 2)
     asked = asked.reshape(slot_count, 1)
-    held = collect(asked, stream, cotangent[0], first)
+    held = collect(asked, stream, cotangent[0], first[0])
     came = lax.all_to_all(
         held.reshape(owners, n_img * capacity, width),
         ("img", "ctx"), split_axis=0, concat_axis=0, tiled=True,
     ).reshape(n_img * slot_count, width)
 
-    stacks = [first] + [along_ctx(first, 1, by) for by in moves[:2]]
-    stacks.append(along_ctx(stacks[1], 1, 1))
+    before = [along_ctx(half, 1, 1) for half in first]
+    after = [along_ctx(half, 1, -1) for half in first]
+    far = [along_ctx(before[0], 1, 1), along_ctx(after[1], 1, -1)]
 
     pairs = []
     for i in range(n_img):
         for t in range(n_tp):
-            x = (2 * (t // 2) + i + (1 if i == 1 else -1)) % RING
+            x = (2 * (t // 2) + i + (1 if t % 2 == 0 else -1)) % RING
             pairs.append((i * n_tp + t, (x % 2) * n_tp + 2 * (x // 2) + t % 2))
     lifted = [lifted, lax.ppermute(lifted, ("img", "tp"), pairs)]
 
     own_gain = lax.dynamic_slice_in_dim(norm_gain, img * cut, cut, axis=1)
-    acc = multiply(here, stacks[: RING - 1], lifted)
+    acc = multiply(here, [*first, *before, *after], lifted)
     base, cot = unpack(paired, came, acc)
-    visual, state, sums = merge(here, own_gain, acc, base, cot, stacks[RING - 1], lifted)
+    visual, state, sums = merge(here, own_gain, acc, base, cot, far, lifted)
 
     near, turned = add(sums, lax.ppermute(sums, "tp", core_pairs))
     stats = [near] + [along_x(near if by == 2 else turned, by) for by in (1, 2, 3)]
@@ -737,7 +749,9 @@
     cross, stats = lax.optimization_barrier((cross, stats))
     crossed = lax.ppermute(cross, "img", flip)
 
-    own, other = backward(here, state, cot, own_gain, stats, stacks, full_width)
+    own, other = backward(
+        here, state, cot, own_gain, stats, [*first, *before, *after, *far], full_width
+    )
     own, other, crossed = lax.optimization_barrier((own, other, crossed))
     got = lax.ppermute(other, "tp", core_pairs)
     to_next, to_last, keep = pair(own, got, crossed)

time: 183 us -> 179 us (0.978)
  waiting for transfers between devices: 69.4 us -> 64.2 us
  starting transfers between devices: 53.6 us -> 55.5 us
    ppermute x6 -> x9, waiting for transfers between devices: 34.4 us -> 30.6 us  [along_ctx(): return lax.ppermute(array, ('ctx', 'tp'), pairs)]
    ppermute x6 -> x9, starting transfers between devices: 10.4 us -> 12.7 us  [along_ctx(): return lax.ppermute(array, ('ctx', 'tp'), pairs)]
    unnamed x52 -> x58, local copies, waits for them, and re-layouts: 14.4 us -> 12.6 us
  transfers between devices with their start and end apart: 24 -> 27, of which waited for: 10 -> 9; matrix products, arithmetic and copies ran while one was open for 1% -> 2% of each run, Pallas kernels for 18% -> 19%
where the time goes in v14:
time: 179 us; the launch traced here: 178 us
  waiting for transfers between devices  64.2 us (36%)
  starting transfers between devices  55.5 us (31%)
  Pallas kernels  40.8 us (23%)
  local copies, waits for them, and re-layouts  15.1 us (8%)
    ppermute x9, waiting for transfers between devices, along_ctx(): return lax.ppermute(array, ('ctx', 'tp'), pairs)  30.6 us
    ppermute x7, waiting for transfers between devices, along_x(): return lax.ppermute(array, ('img', 'tp'), pairs)  13 us
    ppermute x9, starting transfers between devices, along_ctx(): return lax.ppermute(array, ('ctx', 'tp'), pairs)  12.7 us
    unnamed x58, local copies, waits for them, and re-layouts  12.6 us
    ppermute x7, starting transfers between devices, along_x(): return lax.ppermute(array, ('img', 'tp'), pairs)  9.49 us
    ppermute x1, waiting for transfers between devices, shards(): beyond = lax.ppermute(out, 'tp', far_pairs)  7.73 us
    pallas_call x1, Pallas kernels, layer_norm(): pl.pallas_call(norm_kernel, grid_spec=pltpu.PrefetchScalarGridSpec(num_sc...  7.62 us
    all_to_all x1, starting transfers between devices, shards(): lax.all_to_all(held.reshape(owners, n_img * capacity, width), ('img', 'ct...  7.07 us
  transfers between devices with their start and end apart: 27, of which 9 were waited for; matrix products, arithmetic and copies ran while one was open for 2% of the time, Pallas kernels for 19%

profile of v14, /device:TPU:1, one launch (start us, length us, event | category | flops | bytes accessed | tf_op | source)
XLA Modules:
  0.0 178.5 jit_solution(772225542810580228)
XLA Ops:
  0.7 1.0 copy-done
  1.7 2.5 %collective-permute-start = (bf16[288,512]{1,0:T(8,128)(2,1)S(1)}, bf16[288,512]{1,0:T(8,128)(2,1)S(1)}, u32[]{:S(2)}, u32[]{:S(2)}) collective-permute-start(bf16[288,512]{1,0:T(8,128)(2,1)S(1)} %bitcast.22), channel_id=1, source_target_pairs={{0,4},{1,17},{2,6},{3,19},{4,8},{5,21},{6,10},{7,23},{8,12},{9,25}... | collective-permute-start | bytes 884744 | tf_op jit(solution)/shard_map/ppermute | solution.py:692
  4.3 2.2 %collective-permute-start.1 = (bf16[288,512]{1,0:T(8,128)(2,1)S(1)}, bf16[288,512]{1,0:T(8,128)(2,1)S(1)}, u32[]{:S(2)}, u32[]{:S(2)}) collective-permute-start(bf16[288,512]{1,0:T(8,128)(2,1)S(1)} %bitcast.23), channel_id=1, source_target_pairs={{0,12},{1,49},{2,14},{3,51},{4,0},{5,53},{6,2},{7,55},{8,4},{9,57}... | collective-permute-start | bytes 884744 | tf_op jit(solution)/shard_map/ppermute | solution.py:692
  6.5 1.2 collective-permute-start.2
  9.5 7.0 %all-to-all-start = ((s32[32,1,16]{2,1,0:T(1,128)}), s32[32,1,16]{2,1,0:T(1,128)S(1)}, u32[]{:S(2)}, u32[]{:S(2)}) async-start(s32[32,1,16]{2,1,0:T(1,128)} %bitcast.5), calls=%async_computation | async-start | bytes 32768 | tf_op jit(solution)/shard_map/all_to_all | solution.py:704
  16.5 1.3 collective-permute-start.3
  18.5 7.6 %layer_norm.1 = (bf16[256,4608]{1,0:T(8,128)(2,1)}, bf16[4,256,1152]{2,1,0:T(8,128)(2,1)}, f32[256,128]{1,0:T(8,128)}) custom-call(s32[5]{0:T(128)} %stack.24.here_ref.refs_0_, bf16[1024,1152]{1,0:T(8,128)(2,1)} %bitcast.27, bf16[4,1152]{1,0:T(4,128)(2,1)} %bitcast.31, bf16[4,1152]{1,0:T(4,128)(2,1)} %bitcast.33), custom_call_target="tpu_custom_call" | custom-call | tf_op jit(solution)/shard_map/layer_norm/pallas_call | solution.py:96
  26.1 1.6 collective-permute-start.8
  29.6 1.2 copy-done.20
  30.8 1.3 collect.1
  32.1 1.3 copy-done.7
  34.2 7.1 %all-to-all-start.1 = ((bf16[32,32,1024]{2,1,0:T(8,128)(2,1)}), bf16[32,32,1024]{2,1,0:T(8,128)(2,1)}, u32[]{:S(2)}, u32[]{:S(2)}) async-start(bf16[32,32,1024]{2,1,0:T(8,128)(2,1)} %bitcast.21), calls=%async_computation.1 | async-start | bytes 4194304 | tf_op jit(solution)/shard_map/all_to_all | solution.py:725
  41.2 2.4 %collective-permute-start.7 = (bf16[2,288,512]{2,1,0:T(8,128)(2,1)}, bf16[2,288,512]{2,1,0:T(8,128)(2,1)}, u32[]{:S(2)}, u32[]{:S(2)}) collective-permute-start(bf16[2,288,512]{2,1,0:T(8,128)(2,1)} %copy-done.10), channel_id=1, source_target_pairs={{0,48},{1,13},{2,50},{3,15},{4,52},{5,1},{6,54},{7,3},{8,56},{9,5}... | collective-permute-start | bytes 1769480 | tf_op jit(solution)/shard_map/ppermute | solution.py:692
  43.9 2.5 %collective-permute-start.6 = (bf16[2,288,512]{2,1,0:T(8,128)(2,1)S(1)}, bf16[2,288,512]{2,1,0:T(8,128)(2,1)}, u32[]{:S(2)}, u32[]{:S(2)}) collective-permute-start(bf16[2,288,512]{2,1,0:T(8,128)(2,1)S(1)} %get-tuple-element.52.refs_0_.after_ref.refs_6_), channel_id=1, source_target_pairs={{0,48},{1,13},{2,50},{3,15},{4,52},{5,1},{6,54},{7,3},{8,56},{9,5}... | collective-permute-start | bytes 1769480 | tf_op jit(solution)/shard_map/ppermute | solution.py:692
  46.4 22.3 %collective-permute-done.7.refs_5_.refs_11_ = bf16[2,288,512]{2,1,0:T(8,128)(2,1)} collective-permute-done((bf16[2,288,512]{2,1,0:T(8,128)(2,1)}, bf16[2,288,512]{2,1,0:T(8,128)(2,1)}, u32[]{:S(2)}, u32[]{:S(2)}) %collective-permute-start.7) | collective-permute-done | bytes 589856 | tf_op jit(solution)/shard_map/ppermute | solution.py:692
  68.7 1.6 collective-permute-start.10
  71.9 8.2 %collective-permute-done.5.refs_3_.refs_9_ = bf16[2,288,512]{2,1,0:T(8,128)(2,1)} collective-permute-done((bf16[2,288,512]{2,1,0:T(8,128)(2,1)}, bf16[2,288,512]{2,1,0:T(8,128)(2,1)}, u32[]{:S(2)}, u32[]{:S(2)}) %collective-permute-start.5) | collective-permute-done | bytes 589856 | tf_op jit(solution)/shard_map/ppermute | solution.py:692
  80.1 1.1 copy-done.11
  81.2 4.8 %multiply.1.after_ref.acc_hbm = f32[512,512]{1,0:T(8,128)S(1)} custom-call(s32[5]{0:T(128)S(1)} %copy-done.23, bf16[2,288,512]{2,1,0:T(8,128)(2,1)S(1)} %get-tuple-element.52.refs_0_.after_ref.refs_6_, bf16[2,288,512]{2,1,0:T(8,128)(2,1)S(1)} %copy-done.11, bf16[2,288,512]{2,1,0:T(8,128)(2,1)} %collective-permute-done.4.refs_2_.refs_8_, ...), custom_call_target="tpu_custom_call" | custom-call | tf_op jit(solution)/shard_map/multiply/pallas_call | solution.py:282
  86.0 1.0 copy-done.2
  87.0 1.2 copy-done.3
  88.2 0.9 copy-done.18
  89.1 3.0 %unpack.1 = (bf16[512,512]{1,0:T(8,128)(2,1)S(1)}, bf16[512,512]{1,0:T(8,128)(2,1)S(1)}) custom-call(s32[512,1]{1,0:T(8,128)S(1)} %copy-done.18, bf16[1024,1024]{1,0:T(8,128)(2,1)} %bitcast.17.came_ref, f32[512,512]{1,0:T(8,128)S(1)} %copy-done.3), custom_call_target="tpu_custom_call" | custom-call | tf_op jit(solution)/shard_map/unpack/pallas_call | solution.py:168
  92.2 3.4 %merge.1 = (bf16[512,512]{1,0:T(8,128)(2,1)S(1)}, f32[512,512]{1,0:T(8,128)S(1)}, f32[8,512]{1,0:T(8,128)S(1)}) custom-call(s32[5]{0:T(128)S(1)} %copy-done.23, bf16[1,512]{1,0:T(2,128)(2,1)S(1)} %constant_dynamic-slice_fusion.1.ngain_ref.refs_1_, f32[512,512]{1,0:T(8,128)S(1)} %copy-done.4, bf16[512,512]{1,0:T(8,128)(2,1)S(1)} %get-tuple-element.56.base_hbm, ...), custom_call_target="tpu_custom_call" | custom-call | tf_op jit(solution)/shard_map/merge/pallas_call | solution.py:324
  95.6 1.3 collective-permute-start.11
  97.7 2.1 %collective-permute-start.13 = (f32[8,512]{1,0:T(8,128)S(1)}, f32[8,512]{1,0:T(8,128)S(1)}, u32[]{:S(2)}, u32[]{:S(2)}) collective-permute-start(f32[8,512]{1,0:T(8,128)S(1)} %get-tuple-element.63.after_ref.refs_2_), channel_id=1, source_target_pairs={{0,2},{1,3},{2,0},{3,1},{64,66},{65,67},{66,64},{67,65},{4,6},{5,7... | collective-permute-start | bytes 49160 | tf_op jit(solution)/shard_map/ppermute | solution.py:680
  99.8 2.0 %collective-permute-start.14 = (f32[8,512]{1,0:T(8,128)S(1)}, f32[8,512]{1,0:T(8,128)S(1)}, u32[]{:S(2)}, u32[]{:S(2)}) collective-permute-start(f32[8,512]{1,0:T(8,128)S(1)} %get-tuple-element.62), channel_id=1, source_target_pairs={{0,66},{1,67},{2,64},{3,65},{64,0},{65,1},{66,2},{67,3},{4,70},{5,... | collective-permute-start | bytes 49160 | tf_op jit(solution)/shard_map/ppermute | solution.py:680
  101.8 1.4 pack.1
  103.7 5.8 %backward.1 = (bf16[256,4608]{1,0:T(8,128)(2,1)S(1)}, bf16[256,4608]{1,0:T(8,128)(2,1)S(1)}) custom-call(s32[5]{0:T(128)S(1)} %copy-done.23, bf16[1,512]{1,0:T(2,128)(2,1)S(1)} %constant_dynamic-slice_fusion.1.ngain_ref.refs_1_, f32[8,512]{1,0:T(8,128)S(1)} %get-tuple-element.63.after_ref.refs_2_, f32[8,512]{1,0:T(8,128)S(1)} %collective-permute-done.12.refs_3_, ...), custom_call_target="tpu_custom_call" | custom-call | tf_op jit(solution)/shard_map/backward/pallas_call | solution.py:461
  109.5 6.0 %collective-permute-done.15.after_ref.crossed_ref = bf16[512,512]{1,0:T(8,128)(2,1)S(1)} collective-permute-done((bf16[512,512]{1,0:T(8,128)(2,1)S(1)}, bf16[512,512]{1,0:T(8,128)(2,1)S(1)}, u32[]{:S(2)}, u32[]{:S(2)}) %collective-permute-start.15) | collective-permute-done | bytes 524320 | tf_op jit(solution)/shard_map/ppermute | solution.py:750
  115.5 2.1 %collective-permute-start.16 = (bf16[256,4608]{1,0:T(8,128)(2,1)S(1)}, bf16[256,4608]{1,0:T(8,128)(2,1)S(1)}, u32[]{:S(2)}, u32[]{:S(2)}) collective-permute-start(bf16[256,4608]{1,0:T(8,128)(2,1)S(1)} %get-tuple-element.72), channel_id=1, source_target_pairs={{0,1},{1,0},{2,3},{3,2},{4,5},{5,4},{6,7},{7,6},{8,9},{9,8},{10,11... | collective-permute-start | bytes 7077896 | tf_op jit(solution)/shard_map/ppermute | solution.py:756
  117.6 4.2 %collective-permute-done.16.got_ref = bf16[256,4608]{1,0:T(8,128)(2,1)S(1)} collective-permute-done((bf16[256,4608]{1,0:T(8,128)(2,1)S(1)}, bf16[256,4608]{1,0:T(8,128)(2,1)S(1)}, u32[]{:S(2)}, u32[]{:S(2)}) %collective-permute-start.16) | collective-permute-done | bytes 2359328 | tf_op jit(solution)/shard_map/ppermute | solution.py:756
  121.8 1.6 pair.1
  124.8 2.3 %collective-permute-start.18 = (bf16[64,4608]{1,0:T(8,128)(2,1)}, bf16[64,4608]{1,0:T(8,128)(2,1)S(1)}, u32[]{:S(2)}, u32[]{:S(2)}) collective-permute-start(bf16[64,4608]{1,0:T(8,128)(2,1)} %get-tuple-element.75), channel_id=1, source_target_pairs={{0,66},{1,67},{2,64},{3,65},{64,0},{65,1},{66,2},{67,3},{4,70},{5,... | collective-permute-start | bytes 1769480 | tf_op jit(solution)/shard_map/ppermute | solution.py:680
  127.1 1.0 braid.1
  128.1 5.1 %all-to-all-start.2 = ((bf16[16,2,32,512]{3,2,1,0:T(8,128)(2,1)}), bf16[16,2,32,512]{3,2,1,0:T(8,128)(2,1)S(1)}, u32[]{:S(2)}, u32[]{:S(2)}) async-start(bf16[16,2,32,512]{3,2,1,0:T(8,128)(2,1)} %braid.1), calls=%async_computation.2 | async-start | bytes 2097152 | tf_op jit(solution)/shard_map/all_to_all | solution.py:763
  133.2 7.1 %collective-permute-done.17.from_last_ref = bf16[64,4608]{1,0:T(8,128)(2,1)S(1)} collective-permute-done((bf16[64,4608]{1,0:T(8,128)(2,1)}, bf16[64,4608]{1,0:T(8,128)(2,1)S(1)}, u32[]{:S(2)}, u32[]{:S(2)}) %collective-permute-start.17) | collective-permute-done | bytes 589856 | tf_op jit(solution)/shard_map/ppermute | solution.py:680
  140.4 1.5 copy-done.22
  142.3 2.5 %collective-permute-start.20 = (bf16[32,4608]{1,0:T(8,128)(2,1)S(1)}, bf16[32,4608]{1,0:T(8,128)(2,1)S(1)}, u32[]{:S(2)}, u32[]{:S(2)}) collective-permute-start(bf16[32,4608]{1,0:T(8,128)(2,1)S(1)} %get-tuple-element.78), channel_id=1, source_target_pairs={{0,66},{1,67},{2,64},{3,65},{64,0},{65,1},{66,2},{67,3},{4,70},{5,... | collective-permute-start | bytes 884744 | tf_op jit(solution)/shard_map/ppermute | solution.py:680
  144.8 5.8 %collective-permute-done.19.late_last_ref = bf16[32,4608]{1,0:T(8,128)(2,1)S(1)} collective-permute-done((bf16[32,4608]{1,0:T(8,128)(2,1)S(1)}, bf16[32,4608]{1,0:T(8,128)(2,1)S(1)}, u32[]{:S(2)}, u32[]{:S(2)}) %collective-permute-start.19) | collective-permute-done | bytes 294944 | tf_op jit(solution)/shard_map/ppermute | solution.py:680
  151.4 5.0 %finish.1.refs_0_ = bf16[256,1152]{1,0:T(8,128)(2,1)} custom-call(s32[5]{0:T(128)} %stack.24.here_ref.refs_0_, bf16[256,4608]{1,0:T(8,128)(2,1)} %copy-done.5, bf16[256,4608]{1,0:T(8,128)(2,1)} %copy-done.6, bf16[64,4608]{1,0:T(8,128)(2,1)} %copy-done.14, bf16[64,4608]{1,0:T(8,128)(2,1)} %copy-done.15, bf16[32,4608]{1,0:T(8,128)(2,1)} %copy-done.25, ...), custom_call_target="tpu_custom_call" | custom-call | tf_op jit(solution)/shard_map/finish/pallas_call | solution.py:572
  156.4 1.4 collective-permute-start.21
  157.8 2.4 %place.1 = bf16[512,1024]{1,0:T(8,128)(2,1)} custom-call(s32[5]{0:T(128)S(1)} %copy-done.24, s32[512,1]{1,0:T(8,128)S(1)} %copy-done.17, bf16[16,2,32,512]{3,2,1,0:T(8,128)(2,1)S(1)} %all-to-all-done.2.came_ref, bf16[512,1024]{1,0:T(8,128)(2,1)S(1)} %copy-done.9), custom_call_target="tpu_custom_call" | custom-call | tf_op jit(solution)/shard_map/place/pallas_call | solution.py:613
  160.2 3.0 %collective-permute-start.22 = (bf16[256,1152]{1,0:T(8,128)(2,1)S(1)}, bf16[256,1152]{1,0:T(8,128)(2,1)S(1)}, u32[]{:S(2)}, u32[]{:S(2)}) collective-permute-start(bf16[256,1152]{1,0:T(8,128)(2,1)S(1)} %copy-done.13), channel_id=1, source_target_pairs={{0,1},{1,0},{2,3},{3,2},{4,5},{5,4},{6,7},{7,6},{8,9},{9,8},{10,11... | collective-permute-start | bytes 1769480 | tf_op jit(solution)/shard_map/ppermute | solution.py:769
  163.2 7.7 %collective-permute-done.21.refs_1_ = bf16[256,1152]{1,0:T(8,128)(2,1)} collective-permute-done((bf16[256,1152]{1,0:T(8,128)(2,1)}, bf16[256,1152]{1,0:T(8,128)(2,1)}, u32[]{:S(2)}, u32[]{:S(2)}) %collective-permute-start.21) | collective-permute-done | bytes 589856 | tf_op jit(solution)/shard_map/ppermute | solution.py:767
  170.9 3.0 %collective-permute-start.23 = (bf16[256,1152]{1,0:T(8,128)(2,1)}, bf16[256,1152]{1,0:T(8,128)(2,1)S(1)}, u32[]{:S(2)}, u32[]{:S(2)}) collective-permute-start(bf16[256,1152]{1,0:T(8,128)(2,1)} %collective-permute-done.21.refs_1_), channel_id=1, source_target_pairs={{0,1},{1,0},{2,3},{3,2},{4,5},{5,4},{6,7},{7,6},{8,9},{9,8},{10,11... | collective-permute-start | bytes 1769480 | tf_op jit(solution)/shard_map/ppermute | solution.py:769
  174.0 1.8 %collective-permute-done.23.refs_3_ = bf16[256,1152]{1,0:T(8,128)(2,1)S(1)} collective-permute-done((bf16[256,1152]{1,0:T(8,128)(2,1)}, bf16[256,1152]{1,0:T(8,128)(2,1)S(1)}, u32[]{:S(2)}, u32[]{:S(2)}) %collective-permute-start.23) | collective-permute-done | bytes 589856 | tf_op jit(solution)/shard_map/ppermute | solution.py:769
  175.8 2.5 %lay.1 = bf16[1024,1152]{1,0:T(8,128)(2,1)} custom-call(s32[5]{0:T(128)S(1)} %copy-done.24, bf16[256,1152]{1,0:T(8,128)(2,1)S(1)} %copy-done.13, bf16[256,1152]{1,0:T(8,128)(2,1)} %collective-permute-done.21.refs_1_, bf16[256,1152]{1,0:T(8,128)(2,1)S(1)} %collective-permute-done.22.refs_2_, bf16[256,1152]{1,0:T(8,128)(2,1)S(1)} %collective-permute-done.23.refs_3_), custom_call_target="tpu_custom_call" | custom-call | tf_op jit(solution)/shard_map/lay/pallas_call | solution.py:640
  (92 shorter events, 10.8 us)
Async XLA Ops:
  0.6 1.1 copy-start
  0.6 29.0 %copy-start.8 = (bf16[512,1024]{1,0:T(8,128)(2,1)S(1)}, bf16[512,1024]{1,0:T(8,128)(2,1)}, u32[]{:S(2)}) copy-start(bf16[512,1024]{1,0:T(8,128)(2,1)} %stream_ref.3) | copy-start | bytes 3145732
  1.7 24.4 %collective-permute-start = (bf16[288,512]{1,0:T(8,128)(2,1)S(1)}, bf16[288,512]{1,0:T(8,128)(2,1)S(1)}, u32[]{:S(2)}, u32[]{:S(2)}) collective-permute-start(bf16[288,512]{1,0:T(8,128)(2,1)S(1)} %bitcast.22), channel_id=1, source_target_pairs={{0,4},{1,17},{2,6},{3,19},{4,8},{5,21},{6,10},{7,23},{8,12},{9,25}... | collective-permute-start | bytes 884744 | tf_op jit(solution)/shard_map/ppermute | solution.py:692
  4.3 21.9 %collective-permute-start.1 = (bf16[288,512]{1,0:T(8,128)(2,1)S(1)}, bf16[288,512]{1,0:T(8,128)(2,1)S(1)}, u32[]{:S(2)}, u32[]{:S(2)}) collective-permute-start(bf16[288,512]{1,0:T(8,128)(2,1)S(1)} %bitcast.23), channel_id=1, source_target_pairs={{0,12},{1,49},{2,14},{3,51},{4,0},{5,53},{6,2},{7,55},{8,4},{9,57}... | collective-permute-start | bytes 884744 | tf_op jit(solution)/shard_map/ppermute | solution.py:692
  6.5 19.7 %collective-permute-start.2 = (bf16[288,512]{1,0:T(8,128)(2,1)S(1)}, bf16[288,512]{1,0:T(8,128)(2,1)S(1)}, u32[]{:S(2)}, u32[]{:S(2)}) collective-permute-start(bf16[288,512]{1,0:T(8,128)(2,1)S(1)} %bitcast.24), channel_id=1, source_target_pairs={{0,8},{1,33},{2,10},{3,35},{4,12},{5,37},{6,14},{7,39},{8,0},{9,41... | collective-permute-start | bytes 884744 | tf_op jit(solution)/shard_map/ppermute | solution.py:692
  9.5 16.6 %all-to-all-start = ((s32[32,1,16]{2,1,0:T(1,128)}), s32[32,1,16]{2,1,0:T(1,128)S(1)}, u32[]{:S(2)}, u32[]{:S(2)}) async-start(s32[32,1,16]{2,1,0:T(1,128)} %bitcast.5), calls=%async_computation | async-start | bytes 32768 | tf_op jit(solution)/shard_map/all_to_all | solution.py:704
  16.5 9.6 %collective-permute-start.3 = (s32[256]{0:T(256)S(1)}, s32[256]{0:T(256)S(1)}, u32[]{:S(2)}, u32[]{:S(2)}) collective-permute-start(s32[256]{0:T(256)S(1)} %get-tuple-element.86), channel_id=1, source_target_pairs={{0,64},{64,0},{1,65},{65,1},{2,66},{66,2},{3,67},{67,3},{4,68},{68... | collective-permute-start | bytes 3080 | tf_op jit(solution)/shard_map/ppermute | solution.py:711
  18.5 9.2 %copy-start.23 = (s32[5]{0:T(128)S(1)}, s32[5]{0:T(128)}, u32[]{:S(2)}) copy-start(s32[5]{0:T(128)} %stack.24.here_ref.refs_0_) | copy-start | bytes 64
  26.1 44.2 %copy-start.28 = (s32[256]{0:T(256)}, s32[256]{0:T(256)S(1)}, u32[]{:S(2)}) copy-start(s32[256]{0:T(256)S(1)} %collective-permute-done.3) | copy-start | bytes 3076
  26.1 54.0 %collective-permute-start.8 = (bf16[256,4608]{1,0:T(8,128)(2,1)}, bf16[256,4608]{1,0:T(8,128)(2,1)}, u32[]{:S(2)}, u32[]{:S(2)}) collective-permute-start(bf16[256,4608]{1,0:T(8,128)(2,1)} %get-tuple-element.54.refs_6_.refs_2_), channel_id=1, source_target_pairs={{0,64},{1,67},{2,66},{3,65},{64,2},{65,1},{66,0},{67,3},{4,68},{5,... | collective-permute-start | bytes 7077896 | tf_op jit(solution)/shard_map/ppermute | solution.py:739
  29.6 1.2 copy-start.20
  32.1 1.3 copy-start.7
  34.1 36.2 %copy-start.27 = (bf16[1,1024]{1,0:T(2,128)(2,1)S(1)}, bf16[1,1024]{1,0:T(2,128)(2,1)}, u32[]{:S(2)}) copy-start(bf16[1,1024]{1,0:T(2,128)(2,1)} %param.13) | copy-start | bytes 6148
  34.2 46.0 %copy-start.1 = (bf16[256,4608]{1,0:T(8,128)(2,1)S(1)}, bf16[256,4608]{1,0:T(8,128)(2,1)}, u32[]{:S(2)}) copy-start(bf16[256,4608]{1,0:T(8,128)(2,1)} %get-tuple-element.54.refs_6_.refs_2_) | copy-start | bytes 7077892
  34.2 52.8 %all-to-all-start.1 = ((bf16[32,32,1024]{2,1,0:T(8,128)(2,1)}), bf16[32,32,1024]{2,1,0:T(8,128)(2,1)}, u32[]{:S(2)}, u32[]{:S(2)}) async-start(bf16[32,32,1024]{2,1,0:T(8,128)(2,1)} %bitcast.21), calls=%async_computation.1 | async-start | bytes 4194304 | tf_op jit(solution)/shard_map/all_to_all | solution.py:725
  41.2 27.5 %collective-permute-start.7 = (bf16[2,288,512]{2,1,0:T(8,128)(2,1)}, bf16[2,288,512]{2,1,0:T(8,128)(2,1)}, u32[]{:S(2)}, u32[]{:S(2)}) collective-permute-start(bf16[2,288,512]{2,1,0:T(8,128)(2,1)} %copy-done.10), channel_id=1, source_target_pairs={{0,48},{1,13},{2,50},{3,15},{4,52},{5,1},{6,54},{7,3},{8,56},{9,5}... | collective-permute-start | bytes 1769480 | tf_op jit(solution)/shard_map/ppermute | solution.py:692
  43.7 26.6 %collective-permute-start.4 = (bf16[2,288,512]{2,1,0:T(8,128)(2,1)S(1)}, bf16[2,288,512]{2,1,0:T(8,128)(2,1)}, u32[]{:S(2)}, u32[]{:S(2)}) collective-permute-start(bf16[2,288,512]{2,1,0:T(8,128)(2,1)S(1)} %get-tuple-element.52.refs_0_.after_ref.refs_6_), channel_id=1, source_target_pairs={{0,16},{1,5},{2,18},{3,7},{4,20},{5,9},{6,22},{7,11},{8,24},{9,13}... | collective-permute-start | bytes 1769480 | tf_op jit(solution)/shard_map/ppermute | solution.py:692
  43.7 36.4 %collective-permute-start.5 = (bf16[2,288,512]{2,1,0:T(8,128)(2,1)}, bf16[2,288,512]{2,1,0:T(8,128)(2,1)}, u32[]{:S(2)}, u32[]{:S(2)}) collective-permute-start(bf16[2,288,512]{2,1,0:T(8,128)(2,1)} %copy-done.10), channel_id=1, source_target_pairs={{0,16},{1,5},{2,18},{3,7},{4,20},{5,9},{6,22},{7,11},{8,24},{9,13}... | collective-permute-start | bytes 1769480 | tf_op jit(solution)/shard_map/ppermute | solution.py:692
  43.9 36.2 %collective-permute-start.6 = (bf16[2,288,512]{2,1,0:T(8,128)(2,1)S(1)}, bf16[2,288,512]{2,1,0:T(8,128)(2,1)}, u32[]{:S(2)}, u32[]{:S(2)}) collective-permute-start(bf16[2,288,512]{2,1,0:T(8,128)(2,1)S(1)} %get-tuple-element.52.refs_0_.after_ref.refs_6_), channel_id=1, source_target_pairs={{0,48},{1,13},{2,50},{3,15},{4,52},{5,1},{6,54},{7,3},{8,56},{9,5}... | collective-permute-start | bytes 1769480 | tf_op jit(solution)/shard_map/ppermute | solution.py:692
  68.7 23.4 %collective-permute-start.10 = (bf16[2,288,512]{2,1,0:T(8,128)(2,1)}, bf16[2,288,512]{2,1,0:T(8,128)(2,1)}, u32[]{:S(2)}, u32[]{:S(2)}) collective-permute-start(bf16[2,288,512]{2,1,0:T(8,128)(2,1)} %collective-permute-done.7.refs_5_.refs_11_), channel_id=1, source_target_pairs={{0,48},{1,13},{2,50},{3,15},{4,52},{5,1},{6,54},{7,3},{8,56},{9,5}... | collective-permute-start | bytes 1769480 | tf_op jit(solution)/shard_map/ppermute | solution.py:692
  70.3 21.8 %collective-permute-start.9 = (bf16[2,288,512]{2,1,0:T(8,128)(2,1)}, bf16[2,288,512]{2,1,0:T(8,128)(2,1)}, u32[]{:S(2)}, u32[]{:S(2)}) collective-permute-start(bf16[2,288,512]{2,1,0:T(8,128)(2,1)} %collective-permute-done.4.refs_2_.refs_8_), channel_id=1, source_target_pairs={{0,16},{1,5},{2,18},{3,7},{4,20},{5,9},{6,22},{7,11},{8,24},{9,13}... | collective-permute-start | bytes 1769480 | tf_op jit(solution)/shard_map/ppermute | solution.py:692
  87.0 1.2 copy-start.3
  89.1 3.0 %copy-start.4 = (f32[512,512]{1,0:T(8,128)S(1)}, f32[512,512]{1,0:T(8,128)}, u32[]{:S(2)}) copy-start(f32[512,512]{1,0:T(8,128)} %copy-done.2) | copy-start | bytes 3145732
  92.1 9.7 %copy-start.19 = (s32[512,1]{1,0:T(8,128)S(1)}, s32[512,1]{1,0:T(8,128)}, u32[]{:S(2)}) copy-start(s32[512,1]{1,0:T(8,128)} %copy.28.slot_ref) | copy-start | bytes 6148
  92.1 11.5 %copy-start.12 = (bf16[2,288,512]{2,1,0:T(8,128)(2,1)S(1)}, bf16[2,288,512]{2,1,0:T(8,128)(2,1)}, u32[]{:S(2)}) copy-start(bf16[2,288,512]{2,1,0:T(8,128)(2,1)} %copy-done.10) | copy-start | bytes 1769476
  95.6 2.2 %collective-permute-start.11 = (f32[8,512]{1,0:T(8,128)S(1)}, f32[8,512]{1,0:T(8,128)S(1)}, u32[]{:S(2)}, u32[]{:S(2)}) collective-permute-start(f32[8,512]{1,0:T(8,128)S(1)} %get-tuple-element.59.sums_ref), channel_id=1, source_target_pairs={{0,1},{1,0},{2,3},{3,2},{4,5},{5,4},{6,7},{7,6},{8,9},{9,8},{10,11... | collective-permute-start | bytes 49160 | tf_op jit(solution)/shard_map/ppermute | solution.py:746
  97.7 5.5 %collective-permute-start.12 = (f32[8,512]{1,0:T(8,128)S(1)}, f32[8,512]{1,0:T(8,128)S(1)}, u32[]{:S(2)}, u32[]{:S(2)}) collective-permute-start(f32[8,512]{1,0:T(8,128)S(1)} %get-tuple-element.62), channel_id=1, source_target_pairs={{0,64},{1,65},{2,66},{3,67},{64,2},{65,3},{66,0},{67,1},{4,68},{5,... | collective-permute-start | bytes 49160 | tf_op jit(solution)/shard_map/ppermute | solution.py:680
  97.7 5.5 %collective-permute-start.13 = (f32[8,512]{1,0:T(8,128)S(1)}, f32[8,512]{1,0:T(8,128)S(1)}, u32[]{:S(2)}, u32[]{:S(2)}) collective-permute-start(f32[8,512]{1,0:T(8,128)S(1)} %get-tuple-element.63.after_ref.refs_2_), channel_id=1, source_target_pairs={{0,2},{1,3},{2,0},{3,1},{64,66},{65,67},{66,64},{67,65},{4,6},{5,7... | collective-permute-start | bytes 49160 | tf_op jit(solution)/shard_map/ppermute | solution.py:680
  99.8 3.4 %collective-permute-start.14 = (f32[8,512]{1,0:T(8,128)S(1)}, f32[8,512]{1,0:T(8,128)S(1)}, u32[]{:S(2)}, u32[]{:S(2)}) collective-permute-start(f32[8,512]{1,0:T(8,128)S(1)} %get-tuple-element.62), channel_id=1, source_target_pairs={{0,66},{1,67},{2,64},{3,65},{64,0},{65,1},{66,2},{67,3},{4,70},{5,... | collective-permute-start | bytes 49160 | tf_op jit(solution)/shard_map/ppermute | solution.py:680
  103.2 12.3 %collective-permute-start.15 = (bf16[512,512]{1,0:T(8,128)(2,1)S(1)}, bf16[512,512]{1,0:T(8,128)(2,1)S(1)}, u32[]{:S(2)}, u32[]{:S(2)}) collective-permute-start(bf16[512,512]{1,0:T(8,128)(2,1)S(1)} %get-tuple-element.70), channel_id=1, source_target_pairs={{0,64},{64,0},{1,65},{65,1},{2,66},{66,2},{3,67},{67,3},{4,68},{68... | collective-permute-start | bytes 1572872 | tf_op jit(solution)/shard_map/ppermute | solution.py:750
  109.5 13.9 %copy-start.5 = (bf16[256,4608]{1,0:T(8,128)(2,1)}, bf16[256,4608]{1,0:T(8,128)(2,1)S(1)}, u32[]{:S(2)}) copy-start(bf16[256,4608]{1,0:T(8,128)(2,1)S(1)} %get-tuple-element.71.own_ref) | copy-start | bytes 7077892
  115.5 6.3 %collective-permute-start.16 = (bf16[256,4608]{1,0:T(8,128)(2,1)S(1)}, bf16[256,4608]{1,0:T(8,128)(2,1)S(1)}, u32[]{:S(2)}, u32[]{:S(2)}) collective-permute-start(bf16[256,4608]{1,0:T(8,128)(2,1)S(1)} %get-tuple-element.72), channel_id=1, source_target_pairs={{0,1},{1,0},{2,3},{3,2},{4,5},{5,4},{6,7},{7,6},{8,9},{9,8},{10,11... | collective-permute-start | bytes 7077896 | tf_op jit(solution)/shard_map/ppermute | solution.py:756
  121.8 1.8 %copy-start.6 = (bf16[256,4608]{1,0:T(8,128)(2,1)}, bf16[256,4608]{1,0:T(8,128)(2,1)S(1)}, u32[]{:S(2)}) copy-start(bf16[256,4608]{1,0:T(8,128)(2,1)S(1)} %collective-permute-done.16.got_ref) | copy-start | bytes 7077892
  124.4 16.0 %collective-permute-start.17 = (bf16[64,4608]{1,0:T(8,128)(2,1)}, bf16[64,4608]{1,0:T(8,128)(2,1)S(1)}, u32[]{:S(2)}, u32[]{:S(2)}) collective-permute-start(bf16[64,4608]{1,0:T(8,128)(2,1)} %get-tuple-element.74), channel_id=1, source_target_pairs={{0,64},{1,65},{2,66},{3,67},{64,2},{65,3},{66,0},{67,1},{4,68},{5,... | collective-permute-start | bytes 1769480 | tf_op jit(solution)/shard_map/ppermute | solution.py:680
  124.8 15.6 %collective-permute-start.18 = (bf16[64,4608]{1,0:T(8,128)(2,1)}, bf16[64,4608]{1,0:T(8,128)(2,1)S(1)}, u32[]{:S(2)}, u32[]{:S(2)}) collective-permute-start(bf16[64,4608]{1,0:T(8,128)(2,1)} %get-tuple-element.75), channel_id=1, source_target_pairs={{0,66},{1,67},{2,64},{3,65},{64,0},{65,1},{66,2},{67,3},{4,70},{5,... | collective-permute-start | bytes 1769480 | tf_op jit(solution)/shard_map/ppermute | solution.py:680
  128.1 29.7 %all-to-all-start.2 = ((bf16[16,2,32,512]{3,2,1,0:T(8,128)(2,1)}), bf16[16,2,32,512]{3,2,1,0:T(8,128)(2,1)S(1)}, u32[]{:S(2)}, u32[]{:S(2)}) async-start(bf16[16,2,32,512]{3,2,1,0:T(8,128)(2,1)} %braid.1), calls=%async_computation.2 | async-start | bytes 2097152 | tf_op jit(solution)/shard_map/all_to_all | solution.py:763
  140.4 10.2 %copy-start.14 = (bf16[64,4608]{1,0:T(8,128)(2,1)}, bf16[64,4608]{1,0:T(8,128)(2,1)S(1)}, u32[]{:S(2)}) copy-start(bf16[64,4608]{1,0:T(8,128)(2,1)S(1)} %collective-permute-done.17.from_last_ref) | copy-start | bytes 1769476
  140.4 10.2 %copy-start.15 = (bf16[64,4608]{1,0:T(8,128)(2,1)}, bf16[64,4608]{1,0:T(8,128)(2,1)S(1)}, u32[]{:S(2)}) copy-start(bf16[64,4608]{1,0:T(8,128)(2,1)S(1)} %collective-permute-done.18.from_next_ref) | copy-start | bytes 1769476
  140.4 1.5 copy-start.22
  142.0 8.6 %collective-permute-start.19 = (bf16[32,4608]{1,0:T(8,128)(2,1)S(1)}, bf16[32,4608]{1,0:T(8,128)(2,1)S(1)}, u32[]{:S(2)}, u32[]{:S(2)}) collective-permute-start(bf16[32,4608]{1,0:T(8,128)(2,1)S(1)} %get-tuple-element.77), channel_id=1, source_target_pairs={{0,64},{1,65},{2,66},{3,67},{64,2},{65,3},{66,0},{67,1},{4,68},{5,... | collective-permute-start | bytes 884744 | tf_op jit(solution)/shard_map/ppermute | solution.py:680
  142.3 8.3 %collective-permute-start.20 = (bf16[32,4608]{1,0:T(8,128)(2,1)S(1)}, bf16[32,4608]{1,0:T(8,128)(2,1)S(1)}, u32[]{:S(2)}, u32[]{:S(2)}) collective-permute-start(bf16[32,4608]{1,0:T(8,128)(2,1)S(1)} %get-tuple-element.78), channel_id=1, source_target_pairs={{0,66},{1,67},{2,64},{3,65},{64,0},{65,1},{66,2},{67,3},{4,70},{5,... | collective-permute-start | bytes 884744 | tf_op jit(solution)/shard_map/ppermute | solution.py:680
  151.4 6.4 %copy-start.9 = (bf16[512,1024]{1,0:T(8,128)(2,1)S(1)}, bf16[512,1024]{1,0:T(8,128)(2,1)}, u32[]{:S(2)}) copy-start(bf16[512,1024]{1,0:T(8,128)(2,1)} %stream_ref.3) | copy-start | bytes 3145732
  151.4 6.4 %copy-start.17 = (s32[512,1]{1,0:T(8,128)S(1)}, s32[512,1]{1,0:T(8,128)}, u32[]{:S(2)}) copy-start(s32[512,1]{1,0:T(8,128)} %copy-done.16) | copy-start | bytes 6148
  151.4 6.4 %copy-start.24 = (s32[5]{0:T(128)S(1)}, s32[5]{0:T(128)}, u32[]{:S(2)}) copy-start(s32[5]{0:T(128)} %stack.24.here_ref.refs_0_) | copy-start | bytes 64
  156.4 3.8 %copy-start.13 = (bf16[256,1152]{1,0:T(8,128)(2,1)S(1)}, bf16[256,1152]{1,0:T(8,128)(2,1)}, u32[]{:S(2)}) copy-start(bf16[256,1152]{1,0:T(8,128)(2,1)} %finish.1.refs_0_) | copy-start | bytes 1769476
  156.4 14.5 %collective-permute-start.21 = (bf16[256,1152]{1,0:T(8,128)(2,1)}, bf16[256,1152]{1,0:T(8,128)(2,1)}, u32[]{:S(2)}, u32[]{:S(2)}) collective-permute-start(bf16[256,1152]{1,0:T(8,128)(2,1)} %finish.1.refs_0_), channel_id=1, source_target_pairs={{0,2},{1,3},{2,0},{3,1},{4,6},{5,7},{6,4},{7,5},{8,10},{9,11},{10,... | collective-permute-start | bytes 1769480 | tf_op jit(solution)/shard_map/ppermute | solution.py:767
  160.2 13.8 %collective-permute-start.22 = (bf16[256,1152]{1,0:T(8,128)(2,1)S(1)}, bf16[256,1152]{1,0:T(8,128)(2,1)S(1)}, u32[]{:S(2)}, u32[]{:S(2)}) collective-permute-start(bf16[256,1152]{1,0:T(8,128)(2,1)S(1)} %copy-done.13), channel_id=1, source_target_pairs={{0,1},{1,0},{2,3},{3,2},{4,5},{5,4},{6,7},{7,6},{8,9},{9,8},{10,11... | collective-permute-start | bytes 1769480 | tf_op jit(solution)/shard_map/ppermute | solution.py:769
  170.9 4.9 %collective-permute-start.23 = (bf16[256,1152]{1,0:T(8,128)(2,1)}, bf16[256,1152]{1,0:T(8,128)(2,1)S(1)}, u32[]{:S(2)}, u32[]{:S(2)}) collective-permute-start(bf16[256,1152]{1,0:T(8,128)(2,1)} %collective-permute-done.21.refs_1_), channel_id=1, source_target_pairs={{0,1},{1,0},{2,3},{3,2},{4,5},{5,4},{6,7},{7,6},{8,9},{9,8},{10,11... | collective-permute-start | bytes 1769480 | tf_op jit(solution)/shard_map/ppermute | solution.py:769
  (8 other events, 6.8 us)

commit v15 on v13

--- a/solution.py
+++ b/solution.py
@@ -275,7 +275,7 @@
         out_specs=whole(),
         out_shape=shape((tokens, width), F32),
         scratch_shapes=product_scratch(stacks, lifted),
-        compiler_params=params(40),
+        compiler_params=params(60),
         cost_estimate=FREE,
         name="multiply",
     )(here, *stacks, *lifted)
@@ -706,7 +706,7 @@
     paired = jnp.concatenate([paired, partner]).reshape(-1, 1)
 
     first = stack(here, [columns] + near_blocks)
-    asked, first = lax.optimization_barrier((asked, first))
+    asked, first, lifted = lax.optimization_barrier((asked, first, lifted))
 
     asked = asked.reshape(n_img, n_ctx, capacity).transpose(1, 0, 2)
     asked = asked.reshape(slot_count, 1)
@@ -722,7 +722,7 @@
     pairs = []
     for i in range(n_img):
         for t in range(n_tp):
-            x = (2 * (t // 2) + i + (1 if i == 1 else -1)) % RING
+            x = (2 * (t // 2) + i + (1 if t % 2 == 0 else -1)) % RING
             pairs.append((i * n_tp + t, (x % 2) * n_tp + 2 * (x // 2) + t % 2))
     lifted = [lifted, lax.ppermute(lifted, ("img", "tp"), pairs)]
 

time: 183 us -> 179 us (0.978)
  local copies, waits for them, and re-layouts: 16 us -> 11.1 us
  Pallas kernels: 40.4 us -> 42.3 us
    unnamed x52 -> x48, local copies, waits for them, and re-layouts: 14.4 us -> 9.44 us
  transfers between devices with their start and end apart: 24 -> 24, of which waited for: 10 -> 10; matrix products, arithmetic and copies ran while one was open for 1% -> 1% of each run, Pallas kernels for 18% -> 19%
where the time goes in v15:
time: 179 us; the launch traced here: 178 us
  waiting for transfers between devices  70.1 us (39%)
  starting transfers between devices  52.4 us (29%)
  Pallas kernels  42.3 us (24%)
  local copies, waits for them, and re-layouts  11.1 us (6%)
    ppermute x6, waiting for transfers between devices, along_ctx(): return lax.ppermute(array, ('ctx', 'tp'), pairs)  35.1 us
    ppermute x7, waiting for transfers between devices, along_x(): return lax.ppermute(array, ('img', 'tp'), pairs)  14.5 us
    ppermute x6, starting transfers between devices, along_ctx(): return lax.ppermute(array, ('ctx', 'tp'), pairs)  9.65 us
    unnamed x48, local copies, waits for them, and re-layouts  9.44 us
    ppermute x7, starting transfers between devices, along_x(): return lax.ppermute(array, ('img', 'tp'), pairs)  9.26 us
    ppermute x1, waiting for transfers between devices, shards(): beyond = lax.ppermute(out, 'tp', far_pairs)  7.73 us
    pallas_call x1, Pallas kernels, layer_norm(): pl.pallas_call(norm_kernel, grid_spec=pltpu.PrefetchScalarGridSpec(num_sc...  7.66 us
    all_to_all x1, starting transfers between devices, shards(): lax.all_to_all(packed.reshape(owners, capacity), ('img', 'ctx'), split_ax...  6.97 us
  transfers between devices with their start and end apart: 24, of which 10 were waited for; matrix products, arithmetic and copies ran while one was open for 1% of the time, Pallas kernels for 19%

profile of v15, /device:TPU:1, one launch (start us, length us, event | category | flops | bytes accessed | tf_op | source)
XLA Modules:
  0.0 178.2 jit_solution(1728867796610907306)
XLA Ops:
  0.7 1.0 copy-done
  1.7 2.5 %collective-permute-start = (bf16[288,512]{1,0:T(8,128)(2,1)S(1)}, bf16[288,512]{1,0:T(8,128)(2,1)S(1)}, u32[]{:S(2)}, u32[]{:S(2)}) collective-permute-start(bf16[288,512]{1,0:T(8,128)(2,1)S(1)} %bitcast.22), channel_id=1, source_target_pairs={{0,4},{1,17},{2,6},{3,19},{4,8},{5,21},{6,10},{7,23},{8,12},{9,25}... | collective-permute-start | bytes 884744 | tf_op jit(solution)/shard_map/ppermute | solution.py:681
  4.3 2.2 %collective-permute-start.1 = (bf16[288,512]{1,0:T(8,128)(2,1)S(1)}, bf16[288,512]{1,0:T(8,128)(2,1)S(1)}, u32[]{:S(2)}, u32[]{:S(2)}) collective-permute-start(bf16[288,512]{1,0:T(8,128)(2,1)S(1)} %bitcast.23), channel_id=1, source_target_pairs={{0,12},{1,49},{2,14},{3,51},{4,0},{5,53},{6,2},{7,55},{8,4},{9,57}... | collective-permute-start | bytes 884744 | tf_op jit(solution)/shard_map/ppermute | solution.py:681
  6.5 1.2 collective-permute-start.2
  9.5 7.0 %all-to-all-start = ((s32[32,1,16]{2,1,0:T(1,128)}), s32[32,1,16]{2,1,0:T(1,128)S(1)}, u32[]{:S(2)}, u32[]{:S(2)}) async-start(s32[32,1,16]{2,1,0:T(1,128)} %bitcast.5), calls=%async_computation | async-start | bytes 32768 | tf_op jit(solution)/shard_map/all_to_all | solution.py:693
  16.5 1.3 collective-permute-start.3
  18.5 7.7 %layer_norm.1 = (bf16[256,4608]{1,0:T(8,128)(2,1)}, bf16[4,256,1152]{2,1,0:T(8,128)(2,1)}, f32[256,128]{1,0:T(8,128)}) custom-call(s32[5]{0:T(128)} %stack.24.here_ref.refs_0_, bf16[1024,1152]{1,0:T(8,128)(2,1)} %bitcast.27, bf16[4,1152]{1,0:T(4,128)(2,1)} %bitcast.31, bf16[4,1152]{1,0:T(4,128)(2,1)} %bitcast.33), custom_call_target="tpu_custom_call" | custom-call | tf_op jit(solution)/shard_map/layer_norm/pallas_call | solution.py:96
  26.2 0.8 stack.25.refs_0_.after_ref.refs_6_
  27.0 1.6 collective-permute-start.6
  28.6 1.2 collective-permute-start.4
  30.0 1.2 copy-done.10
  31.2 1.2 copy-done.15
  32.5 1.3 collect.1
  33.8 1.4 copy-done.7
  35.2 6.7 %all-to-all-start.1 = ((bf16[32,32,1024]{2,1,0:T(8,128)(2,1)}), bf16[32,32,1024]{2,1,0:T(8,128)(2,1)}, u32[]{:S(2)}, u32[]{:S(2)}) async-start(bf16[32,32,1024]{2,1,0:T(8,128)(2,1)} %bitcast.21), calls=%async_computation.1 | async-start | bytes 4194304 | tf_op jit(solution)/shard_map/all_to_all | solution.py:714
  41.9 2.4 %collective-permute-start.5 = (bf16[4,288,512]{2,1,0:T(8,128)(2,1)S(1)}, bf16[4,288,512]{2,1,0:T(8,128)(2,1)}, u32[]{:S(2)}, u32[]{:S(2)}) collective-permute-start(bf16[4,288,512]{2,1,0:T(8,128)(2,1)S(1)} %stack.25.refs_0_.after_ref.refs_6_), channel_id=1, source_target_pairs={{0,48},{1,13},{2,50},{3,15},{4,52},{5,1},{6,54},{7,3},{8,56},{9,5}... | collective-permute-start | bytes 3538952 | tf_op jit(solution)/shard_map/ppermute | solution.py:681
  44.4 0.9 collective-permute-done.4.refs_1_.refs_7_
  45.5 34.1 %collective-permute-done.5.refs_2_.refs_8_ = bf16[4,288,512]{2,1,0:T(8,128)(2,1)} collective-permute-done((bf16[4,288,512]{2,1,0:T(8,128)(2,1)S(1)}, bf16[4,288,512]{2,1,0:T(8,128)(2,1)}, u32[]{:S(2)}, u32[]{:S(2)}) %collective-permute-start.5) | collective-permute-done | bytes 1179680 | tf_op jit(solution)/shard_map/ppermute | solution.py:681
  79.6 6.3 %multiply.1.after_ref.acc_hbm = f32[512,512]{1,0:T(8,128)} custom-call(s32[5]{0:T(128)} %stack.24.here_ref.refs_0_, bf16[4,288,512]{2,1,0:T(8,128)(2,1)} %copy-done.1, bf16[4,288,512]{2,1,0:T(8,128)(2,1)} %copy-done.8, bf16[4,288,512]{2,1,0:T(8,128)(2,1)} %collective-permute-done.5.refs_2_.refs_8_, bf16[256,4608]{1,0:T(8,128)(2,1)} %get-tuple-element.50.refs_3_.refs_0_, ...), custom_call_target="tpu_custom_call" | custom-call | tf_op jit(solution)/shard_map/multiply/pallas_call | solution.py:272
  85.9 1.2 copy-done.3
  87.1 3.0 %unpack.1 = (bf16[512,512]{1,0:T(8,128)(2,1)S(1)}, bf16[512,512]{1,0:T(8,128)(2,1)S(1)}) custom-call(s32[512,1]{1,0:T(8,128)S(1)} %copy.28.slot_ref, bf16[1024,1024]{1,0:T(8,128)(2,1)} %bitcast.17.came_ref, f32[512,512]{1,0:T(8,128)S(1)} %copy-done.3), custom_call_target="tpu_custom_call" | custom-call | tf_op jit(solution)/shard_map/unpack/pallas_call | solution.py:168
  90.2 3.7 %merge.1 = (bf16[512,512]{1,0:T(8,128)(2,1)S(1)}, f32[512,512]{1,0:T(8,128)S(1)}, f32[8,512]{1,0:T(8,128)S(1)}) custom-call(s32[5]{0:T(128)S(1)} %copy-done.19, bf16[1,512]{1,0:T(2,128)(2,1)S(1)} %constant_dynamic-slice_fusion.1.ngain_ref.refs_1_, f32[512,512]{1,0:T(8,128)S(1)} %copy-done.4, bf16[512,512]{1,0:T(8,128)(2,1)S(1)} %get-tuple-element.52.base_hbm, ...), custom_call_target="tpu_custom_call" | custom-call | tf_op jit(solution)/shard_map/merge/pallas_call | solution.py:314
  94.5 0.8 collective-permute-done.8.got_ref
  95.4 2.1 %collective-permute-start.10 = (f32[8,512]{1,0:T(8,128)S(1)}, f32[8,512]{1,0:T(8,128)S(1)}, u32[]{:S(2)}, u32[]{:S(2)}) collective-permute-start(f32[8,512]{1,0:T(8,128)S(1)} %get-tuple-element.59.after_ref.refs_2_), channel_id=1, source_target_pairs={{0,2},{1,3},{2,0},{3,1},{64,66},{65,67},{66,64},{67,65},{4,6},{5,7... | collective-permute-start | bytes 49160 | tf_op jit(solution)/shard_map/ppermute | solution.py:669
  97.5 1.7 collective-permute-start.11
  99.2 1.4 pack.1
  100.6 2.4 %collective-permute-done.9.refs_3_ = f32[8,512]{1,0:T(8,128)S(1)} collective-permute-done((f32[8,512]{1,0:T(8,128)S(1)}, f32[8,512]{1,0:T(8,128)S(1)}, u32[]{:S(2)}, u32[]{:S(2)}) %collective-permute-start.9) | collective-permute-done | bytes 16416 | tf_op jit(solution)/shard_map/ppermute | solution.py:669
  103.0 5.5 %backward.1 = (bf16[256,4608]{1,0:T(8,128)(2,1)S(1)}, bf16[256,4608]{1,0:T(8,128)(2,1)S(1)}) custom-call(s32[5]{0:T(128)S(1)} %copy-done.19, bf16[1,512]{1,0:T(2,128)(2,1)S(1)} %constant_dynamic-slice_fusion.1.ngain_ref.refs_1_, f32[8,512]{1,0:T(8,128)S(1)} %get-tuple-element.59.after_ref.refs_2_, f32[8,512]{1,0:T(8,128)S(1)} %collective-permute-done.9.refs_3_, ...), custom_call_target="tpu_custom_call" | custom-call | tf_op jit(solution)/shard_map/backward/pallas_call | solution.py:450
  108.6 6.0 %collective-permute-done.12.after_ref.crossed_ref = bf16[512,512]{1,0:T(8,128)(2,1)S(1)} collective-permute-done((bf16[512,512]{1,0:T(8,128)(2,1)S(1)}, bf16[512,512]{1,0:T(8,128)(2,1)S(1)}, u32[]{:S(2)}, u32[]{:S(2)}) %collective-permute-start.12) | collective-permute-done | bytes 524320 | tf_op jit(solution)/shard_map/ppermute | solution.py:738
  114.5 2.8 %collective-permute-start.13 = (bf16[256,4608]{1,0:T(8,128)(2,1)S(1)}, bf16[256,4608]{1,0:T(8,128)(2,1)S(1)}, u32[]{:S(2)}, u32[]{:S(2)}) collective-permute-start(bf16[256,4608]{1,0:T(8,128)(2,1)S(1)} %get-tuple-element.68), channel_id=1, source_target_pairs={{0,1},{1,0},{2,3},{3,2},{4,5},{5,4},{6,7},{7,6},{8,9},{9,8},{10,11... | collective-permute-start | bytes 7077896 | tf_op jit(solution)/shard_map/ppermute | solution.py:742
  117.3 4.2 %collective-permute-done.13.got_ref = bf16[256,4608]{1,0:T(8,128)(2,1)S(1)} collective-permute-done((bf16[256,4608]{1,0:T(8,128)(2,1)S(1)}, bf16[256,4608]{1,0:T(8,128)(2,1)S(1)}, u32[]{:S(2)}, u32[]{:S(2)}) %collective-permute-start.13) | collective-permute-done | bytes 2359328 | tf_op jit(solution)/shard_map/ppermute | solution.py:742
  121.5 1.6 pair.1
  123.3 0.8 copy-done.16
  124.1 2.7 %collective-permute-start.15 = (bf16[64,4608]{1,0:T(8,128)(2,1)}, bf16[64,4608]{1,0:T(8,128)(2,1)S(1)}, u32[]{:S(2)}, u32[]{:S(2)}) collective-permute-start(bf16[64,4608]{1,0:T(8,128)(2,1)} %get-tuple-element.71), channel_id=1, source_target_pairs={{0,66},{1,67},{2,64},{3,65},{64,0},{65,1},{66,2},{67,3},{4,70},{5,... | collective-permute-start | bytes 1769480 | tf_op jit(solution)/shard_map/ppermute | solution.py:669
  126.8 1.0 braid.1
  127.8 6.0 %all-to-all-start.2 = ((bf16[16,2,32,512]{3,2,1,0:T(8,128)(2,1)}), bf16[16,2,32,512]{3,2,1,0:T(8,128)(2,1)S(1)}, u32[]{:S(2)}, u32[]{:S(2)}) async-start(bf16[16,2,32,512]{3,2,1,0:T(8,128)(2,1)} %braid.1), calls=%async_computation.2 | async-start | bytes 2097152 | tf_op jit(solution)/shard_map/all_to_all | solution.py:749
  133.8 6.3 %collective-permute-done.14.from_last_ref = bf16[64,4608]{1,0:T(8,128)(2,1)S(1)} collective-permute-done((bf16[64,4608]{1,0:T(8,128)(2,1)}, bf16[64,4608]{1,0:T(8,128)(2,1)S(1)}, u32[]{:S(2)}, u32[]{:S(2)}) %collective-permute-start.14) | collective-permute-done | bytes 589856 | tf_op jit(solution)/shard_map/ppermute | solution.py:669
  140.1 1.5 copy-done.17
  141.8 2.7 %collective-permute-start.17 = (bf16[32,4608]{1,0:T(8,128)(2,1)S(1)}, bf16[32,4608]{1,0:T(8,128)(2,1)S(1)}, u32[]{:S(2)}, u32[]{:S(2)}) collective-permute-start(bf16[32,4608]{1,0:T(8,128)(2,1)S(1)} %get-tuple-element.74), channel_id=1, source_target_pairs={{0,66},{1,67},{2,64},{3,65},{64,0},{65,1},{66,2},{67,3},{4,70},{5,... | collective-permute-start | bytes 884744 | tf_op jit(solution)/shard_map/ppermute | solution.py:669
  144.5 5.8 %collective-permute-done.16.late_last_ref = bf16[32,4608]{1,0:T(8,128)(2,1)S(1)} collective-permute-done((bf16[32,4608]{1,0:T(8,128)(2,1)S(1)}, bf16[32,4608]{1,0:T(8,128)(2,1)S(1)}, u32[]{:S(2)}, u32[]{:S(2)}) %collective-permute-start.16) | collective-permute-done | bytes 294944 | tf_op jit(solution)/shard_map/ppermute | solution.py:669
  151.1 5.0 %finish.1.refs_0_ = bf16[256,1152]{1,0:T(8,128)(2,1)} custom-call(s32[5]{0:T(128)} %stack.24.here_ref.refs_0_, bf16[256,4608]{1,0:T(8,128)(2,1)} %copy-done.5, bf16[256,4608]{1,0:T(8,128)(2,1)} %copy-done.6, bf16[64,4608]{1,0:T(8,128)(2,1)} %copy-done.13, bf16[64,4608]{1,0:T(8,128)(2,1)} %copy-done.14, bf16[32,4608]{1,0:T(8,128)(2,1)} %copy-done.21, ...), custom_call_target="tpu_custom_call" | custom-call | tf_op jit(solution)/shard_map/finish/pallas_call | solution.py:561
  156.1 1.4 collective-permute-start.18
  157.5 2.4 %place.1 = bf16[512,1024]{1,0:T(8,128)(2,1)} custom-call(s32[5]{0:T(128)S(1)} %copy-done.20, s32[512,1]{1,0:T(8,128)S(1)} %reshape.38.pos_ref, bf16[16,2,32,512]{3,2,1,0:T(8,128)(2,1)S(1)} %all-to-all-done.2.came_ref, bf16[512,1024]{1,0:T(8,128)(2,1)S(1)} %copy-done.11), custom_call_target="tpu_custom_call" | custom-call | tf_op jit(solution)/shard_map/place/pallas_call | solution.py:602
  159.9 3.0 %collective-permute-start.19 = (bf16[256,1152]{1,0:T(8,128)(2,1)S(1)}, bf16[256,1152]{1,0:T(8,128)(2,1)S(1)}, u32[]{:S(2)}, u32[]{:S(2)}) collective-permute-start(bf16[256,1152]{1,0:T(8,128)(2,1)S(1)} %copy-done.12), channel_id=1, source_target_pairs={{0,1},{1,0},{2,3},{3,2},{4,5},{5,4},{6,7},{7,6},{8,9},{9,8},{10,11... | collective-permute-start | bytes 1769480 | tf_op jit(solution)/shard_map/ppermute | solution.py:755
  162.9 7.7 %collective-permute-done.18.refs_1_ = bf16[256,1152]{1,0:T(8,128)(2,1)} collective-permute-done((bf16[256,1152]{1,0:T(8,128)(2,1)}, bf16[256,1152]{1,0:T(8,128)(2,1)}, u32[]{:S(2)}, u32[]{:S(2)}) %collective-permute-start.18) | collective-permute-done | bytes 589856 | tf_op jit(solution)/shard_map/ppermute | solution.py:753
  170.6 3.0 %collective-permute-start.20 = (bf16[256,1152]{1,0:T(8,128)(2,1)}, bf16[256,1152]{1,0:T(8,128)(2,1)S(1)}, u32[]{:S(2)}, u32[]{:S(2)}) collective-permute-start(bf16[256,1152]{1,0:T(8,128)(2,1)} %collective-permute-done.18.refs_1_), channel_id=1, source_target_pairs={{0,1},{1,0},{2,3},{3,2},{4,5},{5,4},{6,7},{7,6},{8,9},{9,8},{10,11... | collective-permute-start | bytes 1769480 | tf_op jit(solution)/shard_map/ppermute | solution.py:755
  173.7 1.8 %collective-permute-done.20.refs_3_ = bf16[256,1152]{1,0:T(8,128)(2,1)S(1)} collective-permute-done((bf16[256,1152]{1,0:T(8,128)(2,1)}, bf16[256,1152]{1,0:T(8,128)(2,1)S(1)}, u32[]{:S(2)}, u32[]{:S(2)}) %collective-permute-start.20) | collective-permute-done | bytes 589856 | tf_op jit(solution)/shard_map/ppermute | solution.py:755
  175.5 2.5 %lay.1 = bf16[1024,1152]{1,0:T(8,128)(2,1)} custom-call(s32[5]{0:T(128)S(1)} %copy-done.20, bf16[256,1152]{1,0:T(8,128)(2,1)S(1)} %copy-done.12, bf16[256,1152]{1,0:T(8,128)(2,1)} %collective-permute-done.18.refs_1_, bf16[256,1152]{1,0:T(8,128)(2,1)S(1)} %collective-permute-done.19.refs_2_, bf16[256,1152]{1,0:T(8,128)(2,1)S(1)} %collective-permute-done.20.refs_3_), custom_call_target="tpu_custom_call" | custom-call | tf_op jit(solution)/shard_map/lay/pallas_call | solution.py:629
  (76 shorter events, 4.8 us)
Async XLA Ops:
  0.6 1.1 copy-start
  1.7 24.4 %collective-permute-start = (bf16[288,512]{1,0:T(8,128)(2,1)S(1)}, bf16[288,512]{1,0:T(8,128)(2,1)S(1)}, u32[]{:S(2)}, u32[]{:S(2)}) collective-permute-start(bf16[288,512]{1,0:T(8,128)(2,1)S(1)} %bitcast.22), channel_id=1, source_target_pairs={{0,4},{1,17},{2,6},{3,19},{4,8},{5,21},{6,10},{7,23},{8,12},{9,25}... | collective-permute-start | bytes 884744 | tf_op jit(solution)/shard_map/ppermute | solution.py:681
  4.3 21.9 %collective-permute-start.1 = (bf16[288,512]{1,0:T(8,128)(2,1)S(1)}, bf16[288,512]{1,0:T(8,128)(2,1)S(1)}, u32[]{:S(2)}, u32[]{:S(2)}) collective-permute-start(bf16[288,512]{1,0:T(8,128)(2,1)S(1)} %bitcast.23), channel_id=1, source_target_pairs={{0,12},{1,49},{2,14},{3,51},{4,0},{5,53},{6,2},{7,55},{8,4},{9,57}... | collective-permute-start | bytes 884744 | tf_op jit(solution)/shard_map/ppermute | solution.py:681
  6.5 19.7 %collective-permute-start.2 = (bf16[288,512]{1,0:T(8,128)(2,1)S(1)}, bf16[288,512]{1,0:T(8,128)(2,1)S(1)}, u32[]{:S(2)}, u32[]{:S(2)}) collective-permute-start(bf16[288,512]{1,0:T(8,128)(2,1)S(1)} %bitcast.24), channel_id=1, source_target_pairs={{0,8},{1,33},{2,10},{3,35},{4,12},{5,37},{6,14},{7,39},{8,0},{9,41... | collective-permute-start | bytes 884744 | tf_op jit(solution)/shard_map/ppermute | solution.py:681
  9.5 16.6 %all-to-all-start = ((s32[32,1,16]{2,1,0:T(1,128)}), s32[32,1,16]{2,1,0:T(1,128)S(1)}, u32[]{:S(2)}, u32[]{:S(2)}) async-start(s32[32,1,16]{2,1,0:T(1,128)} %bitcast.5), calls=%async_computation | async-start | bytes 32768 | tf_op jit(solution)/shard_map/all_to_all | solution.py:693
  16.5 9.6 %collective-permute-start.3 = (s32[256]{0:T(256)S(1)}, s32[256]{0:T(256)S(1)}, u32[]{:S(2)}, u32[]{:S(2)}) collective-permute-start(s32[256]{0:T(256)S(1)} %get-tuple-element.82), channel_id=1, source_target_pairs={{0,64},{64,0},{1,65},{65,1},{2,66},{66,2},{3,67},{67,3},{4,68},{68... | collective-permute-start | bytes 3080 | tf_op jit(solution)/shard_map/ppermute | solution.py:700
  18.5 7.7 %copy-start.18 = (s32[5]{0:T(128)S(1)}, s32[5]{0:T(128)}, u32[]{:S(2)}) copy-start(s32[5]{0:T(128)} %stack.24.here_ref.refs_0_) | copy-start | bytes 64
  27.0 14.9 %copy-start.1 = (bf16[4,288,512]{2,1,0:T(8,128)(2,1)}, bf16[4,288,512]{2,1,0:T(8,128)(2,1)S(1)}, u32[]{:S(2)}) copy-start(bf16[4,288,512]{2,1,0:T(8,128)(2,1)S(1)} %stack.25.refs_0_.after_ref.refs_6_) | copy-start | bytes 3538948
  27.0 52.6 %collective-permute-start.6 = (bf16[256,4608]{1,0:T(8,128)(2,1)}, bf16[256,4608]{1,0:T(8,128)(2,1)}, u32[]{:S(2)}, u32[]{:S(2)}) collective-permute-start(bf16[256,4608]{1,0:T(8,128)(2,1)} %get-tuple-element.50.refs_3_.refs_0_), channel_id=1, source_target_pairs={{0,64},{1,67},{2,66},{3,65},{64,2},{65,1},{66,0},{67,3},{4,68},{5,... | collective-permute-start | bytes 7077896 | tf_op jit(solution)/shard_map/ppermute | solution.py:727
  28.6 16.7 %collective-permute-start.4 = (bf16[4,288,512]{2,1,0:T(8,128)(2,1)S(1)}, bf16[4,288,512]{2,1,0:T(8,128)(2,1)S(1)}, u32[]{:S(2)}, u32[]{:S(2)}) collective-permute-start(bf16[4,288,512]{2,1,0:T(8,128)(2,1)S(1)} %stack.25.refs_0_.after_ref.refs_6_), channel_id=1, source_target_pairs={{0,16},{1,5},{2,18},{3,7},{4,20},{5,9},{6,22},{7,11},{8,24},{9,13}... | collective-permute-start | bytes 3538952 | tf_op jit(solution)/shard_map/ppermute | solution.py:681
  30.0 1.2 copy-start.10
  31.2 1.2 copy-start.15
  33.8 1.4 copy-start.7
  35.2 10.1 %copy-start.23 = (bf16[1,1024]{1,0:T(2,128)(2,1)S(1)}, bf16[1,1024]{1,0:T(2,128)(2,1)}, u32[]{:S(2)}) copy-start(bf16[1,1024]{1,0:T(2,128)(2,1)} %param.13) | copy-start | bytes 6148
  35.2 50.7 %all-to-all-start.1 = ((bf16[32,32,1024]{2,1,0:T(8,128)(2,1)}), bf16[32,32,1024]{2,1,0:T(8,128)(2,1)}, u32[]{:S(2)}, u32[]{:S(2)}) async-start(bf16[32,32,1024]{2,1,0:T(8,128)(2,1)} %bitcast.21), calls=%async_computation.1 | async-start | bytes 4194304 | tf_op jit(solution)/shard_map/all_to_all | solution.py:714
  41.9 37.7 %collective-permute-start.5 = (bf16[4,288,512]{2,1,0:T(8,128)(2,1)S(1)}, bf16[4,288,512]{2,1,0:T(8,128)(2,1)}, u32[]{:S(2)}, u32[]{:S(2)}) collective-permute-start(bf16[4,288,512]{2,1,0:T(8,128)(2,1)S(1)} %stack.25.refs_0_.after_ref.refs_6_), channel_id=1, source_target_pairs={{0,48},{1,13},{2,50},{3,15},{4,52},{5,1},{6,54},{7,3},{8,56},{9,5}... | collective-permute-start | bytes 3538952 | tf_op jit(solution)/shard_map/ppermute | solution.py:681
  45.3 34.4 %copy-start.8 = (bf16[4,288,512]{2,1,0:T(8,128)(2,1)}, bf16[4,288,512]{2,1,0:T(8,128)(2,1)S(1)}, u32[]{:S(2)}) copy-start(bf16[4,288,512]{2,1,0:T(8,128)(2,1)S(1)} %collective-permute-done.4.refs_1_.refs_7_) | copy-start | bytes 3538948
  45.3 44.9 %collective-permute-start.7 = (bf16[4,288,512]{2,1,0:T(8,128)(2,1)S(1)}, bf16[4,288,512]{2,1,0:T(8,128)(2,1)}, u32[]{:S(2)}, u32[]{:S(2)}) collective-permute-start(bf16[4,288,512]{2,1,0:T(8,128)(2,1)S(1)} %collective-permute-done.4.refs_1_.refs_7_), channel_id=1, source_target_pairs={{0,16},{1,5},{2,18},{3,7},{4,20},{5,9},{6,22},{7,11},{8,24},{9,13}... | collective-permute-start | bytes 3538952 | tf_op jit(solution)/shard_map/ppermute | solution.py:681
  85.9 4.2 %copy-start.19 = (s32[5]{0:T(128)S(1)}, s32[5]{0:T(128)}, u32[]{:S(2)}) copy-start(s32[5]{0:T(128)} %stack.24.here_ref.refs_0_) | copy-start | bytes 64
  85.9 1.2 copy-start.3
  87.1 3.0 %copy-start.4 = (f32[512,512]{1,0:T(8,128)S(1)}, f32[512,512]{1,0:T(8,128)}, u32[]{:S(2)}) copy-start(f32[512,512]{1,0:T(8,128)} %multiply.1.after_ref.acc_hbm) | copy-start | bytes 3145732
  90.2 12.9 %copy-start.2 = (bf16[4,288,512]{2,1,0:T(8,128)(2,1)S(1)}, bf16[4,288,512]{2,1,0:T(8,128)(2,1)}, u32[]{:S(2)}) copy-start(bf16[4,288,512]{2,1,0:T(8,128)(2,1)} %copy-done.1) | copy-start | bytes 3538948
  90.2 12.9 %copy-start.9 = (bf16[4,288,512]{2,1,0:T(8,128)(2,1)S(1)}, bf16[4,288,512]{2,1,0:T(8,128)(2,1)}, u32[]{:S(2)}) copy-start(bf16[4,288,512]{2,1,0:T(8,128)(2,1)} %copy-done.8) | copy-start | bytes 3538948
  93.9 1.5 collective-permute-start.8
  95.4 5.3 %collective-permute-start.10 = (f32[8,512]{1,0:T(8,128)S(1)}, f32[8,512]{1,0:T(8,128)S(1)}, u32[]{:S(2)}, u32[]{:S(2)}) collective-permute-start(f32[8,512]{1,0:T(8,128)S(1)} %get-tuple-element.59.after_ref.refs_2_), channel_id=1, source_target_pairs={{0,2},{1,3},{2,0},{3,1},{64,66},{65,67},{66,64},{67,65},{4,6},{5,7... | collective-permute-start | bytes 49160 | tf_op jit(solution)/shard_map/ppermute | solution.py:669
  97.5 3.1 %collective-permute-start.11 = (f32[8,512]{1,0:T(8,128)S(1)}, f32[8,512]{1,0:T(8,128)S(1)}, u32[]{:S(2)}, u32[]{:S(2)}) collective-permute-start(f32[8,512]{1,0:T(8,128)S(1)} %get-tuple-element.58), channel_id=1, source_target_pairs={{0,66},{1,67},{2,64},{3,65},{64,0},{65,1},{66,2},{67,3},{4,70},{5,... | collective-permute-start | bytes 49160 | tf_op jit(solution)/shard_map/ppermute | solution.py:669
  99.2 3.8 %collective-permute-start.9 = (f32[8,512]{1,0:T(8,128)S(1)}, f32[8,512]{1,0:T(8,128)S(1)}, u32[]{:S(2)}, u32[]{:S(2)}) collective-permute-start(f32[8,512]{1,0:T(8,128)S(1)} %get-tuple-element.58), channel_id=1, source_target_pairs={{0,64},{1,65},{2,66},{3,67},{64,2},{65,3},{66,0},{67,1},{4,68},{5,... | collective-permute-start | bytes 49160 | tf_op jit(solution)/shard_map/ppermute | solution.py:669
  103.0 11.5 %collective-permute-start.12 = (bf16[512,512]{1,0:T(8,128)(2,1)S(1)}, bf16[512,512]{1,0:T(8,128)(2,1)S(1)}, u32[]{:S(2)}, u32[]{:S(2)}) collective-permute-start(bf16[512,512]{1,0:T(8,128)(2,1)S(1)} %get-tuple-element.66), channel_id=1, source_target_pairs={{0,64},{64,0},{1,65},{65,1},{2,66},{66,2},{3,67},{67,3},{4,68},{68... | collective-permute-start | bytes 1572872 | tf_op jit(solution)/shard_map/ppermute | solution.py:738
  108.6 14.5 %copy-start.5 = (bf16[256,4608]{1,0:T(8,128)(2,1)}, bf16[256,4608]{1,0:T(8,128)(2,1)S(1)}, u32[]{:S(2)}) copy-start(bf16[256,4608]{1,0:T(8,128)(2,1)S(1)} %get-tuple-element.67.own_ref) | copy-start | bytes 7077892
  114.5 7.0 %collective-permute-start.13 = (bf16[256,4608]{1,0:T(8,128)(2,1)S(1)}, bf16[256,4608]{1,0:T(8,128)(2,1)S(1)}, u32[]{:S(2)}, u32[]{:S(2)}) collective-permute-start(bf16[256,4608]{1,0:T(8,128)(2,1)S(1)} %get-tuple-element.68), channel_id=1, source_target_pairs={{0,1},{1,0},{2,3},{3,2},{4,5},{5,4},{6,7},{7,6},{8,9},{9,8},{10,11... | collective-permute-start | bytes 7077896 | tf_op jit(solution)/shard_map/ppermute | solution.py:742
  121.5 1.8 %copy-start.6 = (bf16[256,4608]{1,0:T(8,128)(2,1)}, bf16[256,4608]{1,0:T(8,128)(2,1)S(1)}, u32[]{:S(2)}) copy-start(bf16[256,4608]{1,0:T(8,128)(2,1)S(1)} %collective-permute-done.13.got_ref) | copy-start | bytes 7077892
  123.3 0.8 copy-start.16
  124.1 16.0 %collective-permute-start.14 = (bf16[64,4608]{1,0:T(8,128)(2,1)}, bf16[64,4608]{1,0:T(8,128)(2,1)S(1)}, u32[]{:S(2)}, u32[]{:S(2)}) collective-permute-start(bf16[64,4608]{1,0:T(8,128)(2,1)} %get-tuple-element.70), channel_id=1, source_target_pairs={{0,64},{1,65},{2,66},{3,67},{64,2},{65,3},{66,0},{67,1},{4,68},{5,... | collective-permute-start | bytes 1769480 | tf_op jit(solution)/shard_map/ppermute | solution.py:669
  124.1 16.0 %collective-permute-start.15 = (bf16[64,4608]{1,0:T(8,128)(2,1)}, bf16[64,4608]{1,0:T(8,128)(2,1)S(1)}, u32[]{:S(2)}, u32[]{:S(2)}) collective-permute-start(bf16[64,4608]{1,0:T(8,128)(2,1)} %get-tuple-element.71), channel_id=1, source_target_pairs={{0,66},{1,67},{2,64},{3,65},{64,0},{65,1},{66,2},{67,3},{4,70},{5,... | collective-permute-start | bytes 1769480 | tf_op jit(solution)/shard_map/ppermute | solution.py:669
  127.8 29.7 %all-to-all-start.2 = ((bf16[16,2,32,512]{3,2,1,0:T(8,128)(2,1)}), bf16[16,2,32,512]{3,2,1,0:T(8,128)(2,1)S(1)}, u32[]{:S(2)}, u32[]{:S(2)}) async-start(bf16[16,2,32,512]{3,2,1,0:T(8,128)(2,1)} %braid.1), calls=%async_computation.2 | async-start | bytes 2097152 | tf_op jit(solution)/shard_map/all_to_all | solution.py:749
  140.1 10.2 %copy-start.13 = (bf16[64,4608]{1,0:T(8,128)(2,1)}, bf16[64,4608]{1,0:T(8,128)(2,1)S(1)}, u32[]{:S(2)}) copy-start(bf16[64,4608]{1,0:T(8,128)(2,1)S(1)} %collective-permute-done.14.from_last_ref) | copy-start | bytes 1769476
  140.1 10.2 %copy-start.14 = (bf16[64,4608]{1,0:T(8,128)(2,1)}, bf16[64,4608]{1,0:T(8,128)(2,1)S(1)}, u32[]{:S(2)}) copy-start(bf16[64,4608]{1,0:T(8,128)(2,1)S(1)} %collective-permute-done.15.from_next_ref) | copy-start | bytes 1769476
  140.1 1.5 copy-start.17
  141.7 8.6 %collective-permute-start.16 = (bf16[32,4608]{1,0:T(8,128)(2,1)S(1)}, bf16[32,4608]{1,0:T(8,128)(2,1)S(1)}, u32[]{:S(2)}, u32[]{:S(2)}) collective-permute-start(bf16[32,4608]{1,0:T(8,128)(2,1)S(1)} %get-tuple-element.73), channel_id=1, source_target_pairs={{0,64},{1,65},{2,66},{3,67},{64,2},{65,3},{66,0},{67,1},{4,68},{5,... | collective-permute-start | bytes 884744 | tf_op jit(solution)/shard_map/ppermute | solution.py:669
  141.8 8.5 %collective-permute-start.17 = (bf16[32,4608]{1,0:T(8,128)(2,1)S(1)}, bf16[32,4608]{1,0:T(8,128)(2,1)S(1)}, u32[]{:S(2)}, u32[]{:S(2)}) collective-permute-start(bf16[32,4608]{1,0:T(8,128)(2,1)S(1)} %get-tuple-element.74), channel_id=1, source_target_pairs={{0,66},{1,67},{2,64},{3,65},{64,0},{65,1},{66,2},{67,3},{4,70},{5,... | collective-permute-start | bytes 884744 | tf_op jit(solution)/shard_map/ppermute | solution.py:669
  150.3 0.7 copy-start.21
  150.3 0.8 copy-start.22
  151.1 6.4 %copy-start.11 = (bf16[512,1024]{1,0:T(8,128)(2,1)S(1)}, bf16[512,1024]{1,0:T(8,128)(2,1)}, u32[]{:S(2)}) copy-start(bf16[512,1024]{1,0:T(8,128)(2,1)} %stream_ref.3) | copy-start | bytes 3145732
  151.1 6.4 %copy-start.20 = (s32[5]{0:T(128)S(1)}, s32[5]{0:T(128)}, u32[]{:S(2)}) copy-start(s32[5]{0:T(128)} %stack.24.here_ref.refs_0_) | copy-start | bytes 64
  156.1 3.8 %copy-start.12 = (bf16[256,1152]{1,0:T(8,128)(2,1)S(1)}, bf16[256,1152]{1,0:T(8,128)(2,1)}, u32[]{:S(2)}) copy-start(bf16[256,1152]{1,0:T(8,128)(2,1)} %finish.1.refs_0_) | copy-start | bytes 1769476
  156.1 14.5 %collective-permute-start.18 = (bf16[256,1152]{1,0:T(8,128)(2,1)}, bf16[256,1152]{1,0:T(8,128)(2,1)}, u32[]{:S(2)}, u32[]{:S(2)}) collective-permute-start(bf16[256,1152]{1,0:T(8,128)(2,1)} %finish.1.refs_0_), channel_id=1, source_target_pairs={{0,2},{1,3},{2,0},{3,1},{4,6},{5,7},{6,4},{7,5},{8,10},{9,11},{10,... | collective-permute-start | bytes 1769480 | tf_op jit(solution)/shard_map/ppermute | solution.py:753
  159.9 13.8 %collective-permute-start.19 = (bf16[256,1152]{1,0:T(8,128)(2,1)S(1)}, bf16[256,1152]{1,0:T(8,128)(2,1)S(1)}, u32[]{:S(2)}, u32[]{:S(2)}) collective-permute-start(bf16[256,1152]{1,0:T(8,128)(2,1)S(1)} %copy-done.12), channel_id=1, source_target_pairs={{0,1},{1,0},{2,3},{3,2},{4,5},{5,4},{6,7},{7,6},{8,9},{9,8},{10,11... | collective-permute-start | bytes 1769480 | tf_op jit(solution)/shard_map/ppermute | solution.py:755
  170.6 4.9 %collective-permute-start.20 = (bf16[256,1152]{1,0:T(8,128)(2,1)}, bf16[256,1152]{1,0:T(8,128)(2,1)S(1)}, u32[]{:S(2)}, u32[]{:S(2)}) collective-permute-start(bf16[256,1152]{1,0:T(8,128)(2,1)} %collective-permute-done.18.refs_1_), channel_id=1, source_target_pairs={{0,1},{1,0},{2,3},{3,2},{4,5},{5,4},{6,7},{7,6},{8,9},{9,8},{10,11... | collective-permute-start | bytes 1769480 | tf_op jit(solution)/shard_map/ppermute | solution.py:755

commit v16 on v15

--- a/solution.py
+++ b/solution.py
@@ -11,6 +11,7 @@
 FREE = pl.CostEstimate(flops=0, bytes_accessed=0, transcendentals=0)
 RING = 4
 AWAY = (0, 3, 1, 2)
+EARLY = 2
 
 
 def params(mib):
@@ -263,8 +264,8 @@
 
 
 def multiply_kernel(here_ref, *refs):
-    stacks, lifted, (out_ref, *scratch) = refs[: RING - 1], refs[RING - 1 : RING + 1], refs[RING + 1 :]
-    out_ref[...] = product(here_ref, AWAY[: RING - 1], stacks, lifted, *scratch)(None)
+    stacks, lifted, (out_ref, *scratch) = refs[:EARLY], refs[EARLY : EARLY + 2], refs[EARLY + 2 :]
+    out_ref[...] = product(here_ref, AWAY[:EARLY], stacks, lifted, *scratch)(None)
 
 
 def multiply(here, stacks, lifted):
@@ -281,10 +282,10 @@
     )(here, *stacks, *lifted)
 
 
-def merge_kernel(here_ref, ngain_ref, acc_hbm, base_hbm, cot_hbm, stack_ref, *refs):
-    lifted, refs = refs[:2], refs[2:]
+def merge_kernel(here_ref, ngain_ref, acc_hbm, base_hbm, cot_hbm, *refs):
+    stacks, lifted, refs = refs[: RING - EARLY], refs[RING - EARLY : RING - EARLY + 2], refs[RING - EARLY + 2 :]
     visual_ref, state_ref, stat_ref, acc_ref, base_ref, cot_ref, row_sems, *scratch = refs
-    run = product(here_ref, AWAY[RING - 1 :], (stack_ref,), lifted, *scratch)
+    run = product(here_ref, AWAY[EARLY:], stacks, lifted, *scratch)
     copies = [
         pltpu.make_async_copy(a, b, row_sems.at[i])
         for i, (a, b) in enumerate(((acc_hbm, acc_ref), (base_hbm, base_ref), (cot_hbm, cot_ref)))
@@ -308,12 +309,12 @@
     stat_ref[...] = sums.T[: stat_ref.shape[0]]
 
 
-def merge(here, ngain, acc, base, cot, stack, lifted):
+def merge(here, ngain, acc, base, cot, stacks, lifted):
     tokens, width = base.shape
     outs = [shape((tokens, width), BF), shape((tokens, width), F32), shape((8, tokens), F32)]
     return pl.pallas_call(
         merge_kernel,
-        in_specs=[scalars(), whole()] + [in_hbm()] * 6,
+        in_specs=[scalars(), whole()] + [in_hbm()] * (3 + len(stacks) + len(lifted)),
         out_specs=[whole()] * 3,
         out_shape=outs,
         scratch_shapes=[
@@ -322,11 +323,11 @@
             pltpu.VMEM((tokens, width), BF),
             pltpu.SemaphoreType.DMA((3,)),
         ]
-        + product_scratch((stack,), lifted),
+        + product_scratch(stacks, lifted),
         compiler_params=params(24),
         cost_estimate=FREE,
         name="merge",
-    )(here, ngain, acc, base, cot, stack, *lifted)
+    )(here, ngain, acc, base, cot, *stacks, *lifted)
 
 
 def add_kernel(sums_ref, got_ref, near_ref, turned_ref):
@@ -467,7 +468,7 @@
     )(here, ngain, *stats, *stacks, state, cot)
 
 
-def pair_kernel(own_ref, got_ref, after_ref, next_ref, last_ref, keep_ref):
+def pair_kernel(own_ref, got_ref, after_ref, next_ref, last_ref, keep_hbm, keep_ref, sem):
     rows = own_ref.shape[0] // RING
     half = rows // 2
 
@@ -475,12 +476,15 @@
         at = slice(start, start + half)
         return (own_ref[at, :].astype(F32) + got_ref[at, :].astype(F32)).astype(BF)
 
+    keep_ref[:half] = total(rows)
+    keep_ref[half:] = total(3 * rows + half)
+    copy = pltpu.make_async_copy(keep_ref, keep_hbm, sem)
+    copy.start()
     next_ref[:half] = total(2 * rows)
     next_ref[half:] = total(rows + half)
     last_ref[:half] = total(2 * rows + half)
     last_ref[half:] = total(3 * rows)
-    keep_ref[:half] = total(rows)
-    keep_ref[half:] = total(3 * rows + half)
+    copy.wait()
 
 
 def pair(own, got, after):
@@ -488,15 +492,19 @@
     return pl.pallas_call(
         pair_kernel,
         in_specs=[whole()] * 2 + [anywhere()],
-        out_specs=[whole()] * 3,
+        out_specs=[whole()] * 2 + [anywhere()],
         out_shape=[shape((rows, depth), BF)] * 3,
+        scratch_shapes=[pltpu.VMEM((rows, depth), BF), pltpu.SemaphoreType.DMA],
         compiler_params=params(8),
         cost_estimate=FREE,
         name="pair",
     )(own, got, after)
 
 
-def relay_kernel(keep_ref, from_last_ref, from_next_ref, next_ref, last_ref):
+def relay_kernel(keep_hbm, from_last_ref, from_next_ref, next_ref, last_ref, keep_ref, sem):
+    copy = pltpu.make_async_copy(keep_hbm, keep_ref, sem)
+    copy.start()
+    copy.wait()
     half = next_ref.shape[0]
     for at, came_ref, out_ref in (
         (slice(0, half), from_last_ref, next_ref),
@@ -509,25 +517,23 @@
     rows, depth = keep.shape
     return pl.pallas_call(
         relay_kernel,
-        in_specs=[whole()] * 3,
+        in_specs=[in_hbm()] + [whole()] * 2,
         out_specs=[whole()] * 2,
         out_shape=[shape((rows // 2, depth), BF)] * 2,
+        scratch_shapes=[pltpu.VMEM((rows, depth), BF), pltpu.SemaphoreType.DMA],
         compiler_params=params(8),
         cost_estimate=FREE,
         name="relay",
     )(keep, from_last, from_next)
 
 
-def finish_kernel(here_ref, own_ref, got_ref, from_last_ref, from_next_ref, late_last_ref, late_next_ref,
-                  xw_ref, stat_ref, gain_ref, out_ref):
+def finish_kernel(here_ref, own_ref, got_ref, early_ref, late_ref, xw_ref, stat_ref, gain_ref, out_ref):
     window, tokens, width = xw_ref.shape
     full = window * width
     mean = stat_ref[:, 0:1]
     inv = stat_ref[:, 1:2]
-    early = jnp.where(pl.program_id(0) == 0, from_next_ref[...], from_last_ref[...])
-    late = jnp.where(pl.program_id(0) == 0, late_last_ref[...], late_next_ref[...])
     lifted = own_ref[...].astype(F32) + got_ref[...].astype(F32)
-    lifted = lifted + early.astype(F32) + late.astype(F32)
+    lifted = lifted + early_ref[...].astype(F32) + late_ref[...].astype(F32)
     share = width // (RING * RING)
     scaled = []
     total = 0.0
@@ -550,32 +556,30 @@
     ).astype(BF)
 
 
-def finish(here, own, got, early, late, xw, stat, gain):
-    rows, depth = early[0].shape
+def finish(here, step, own, got, early, late, xw, stat, gain):
+    tokens, depth = late.shape
     window, width = gain.shape
-    steps = 2
-    tokens = rows // steps
-    same = pl.BlockSpec((tokens, depth), lambda i, h: (i, 0))
+    same = pl.BlockSpec((tokens, depth), lambda i, h: (step, 0))
     second = pl.BlockSpec((tokens, depth), lambda i, h: (1, 0))
     only = pl.BlockSpec((tokens, depth), lambda i, h: (0, 0))
     return pl.pallas_call(
         finish_kernel,
         grid_spec=pltpu.PrefetchScalarGridSpec(
             num_scalar_prefetch=1,
-            grid=(steps,),
-            in_specs=[same, same, second, second, only, only]
+            grid=(1,),
+            in_specs=[same, same, second, only]
             + [
-                pl.BlockSpec((window, tokens, width), lambda i, h: (0, h[1] * steps + i, 0)),
-                pl.BlockSpec((tokens, 128), lambda i, h: (h[1] * steps + i, 0)),
+                pl.BlockSpec((window, tokens, width), lambda i, h: (0, h[1] * 2 + step, 0)),
+                pl.BlockSpec((tokens, 128), lambda i, h: (h[1] * 2 + step, 0)),
                 pl.BlockSpec((window, width), lambda i, h: (0, 0)),
             ],
-            out_specs=pl.BlockSpec((tokens * window, width), lambda i, h: (i, 0)),
+            out_specs=pl.BlockSpec((tokens * window, width), lambda i, h: (0, 0)),
         ),
-        out_shape=shape((rows * window, width), BF),
+        out_shape=shape((tokens * window, width), BF),
         compiler_params=params(58),
         cost_estimate=FREE,
         name="finish",
-    )(here, own, got, *early, *late, xw, stat, gain)
+    )(here, own, got, early, late, xw, stat, gain)
 
 
 def place_kernel(here_ref, pos_ref, came_ref, stream_ref, out_ref):
@@ -615,8 +619,9 @@
     rows = blocks[0].shape[0]
     copies = []
     for index, ref in enumerate(blocks):
-        owner = 2 * (here_ref[0] ^ (index // 2)) + (here_ref[1] ^ (index % 2))
-        start = pl.multiple_of(owner * rows, rows)
+        quarter, step = index // 2, index % 2
+        owner = 2 * (here_ref[0] ^ (quarter // 2)) + (here_ref[1] ^ (quarter % 2))
+        start = pl.multiple_of((2 * owner + step) * rows, rows)
         copies.append(pltpu.make_async_copy(ref, out_ref.at[pl.ds(start, rows)], sems.at[index]))
     for copy in copies:
         copy.start()
@@ -727,9 +732,9 @@
     lifted = [lifted, lax.ppermute(lifted, ("img", "tp"), pairs)]
 
     own_gain = lax.dynamic_slice_in_dim(norm_gain, img * cut, cut, axis=1)
-    acc = multiply(here, stacks[: RING - 1], lifted)
+    acc = multiply(here, stacks[:EARLY], lifted)
     base, cot = unpack(paired, came, acc)
-    visual, state, sums = merge(here, own_gain, acc, base, cot, stacks[RING - 1], lifted)
+    visual, state, sums = merge(here, own_gain, acc, base, cot, stacks[EARLY:], lifted)
 
     near, turned = add(sums, lax.ppermute(sums, "tp", core_pairs))
     stats = [near] + [along_x(near if by == 2 else turned, by) for by in (1, 2, 3)]
@@ -749,11 +754,14 @@
     arrived = lax.all_to_all(send, "ctx", split_axis=0, concat_axis=0, tiled=True)
     new_stream = place(here, asked, arrived, stream)
 
-    out = finish(here, own, got, (from_last, from_next), (late_last, late_next), xw, stat, gain)
-    beyond = lax.ppermute(out, "tp", far_pairs)
-    beyond, new_stream = lax.optimization_barrier((beyond, new_stream))
-    from_core = [lax.ppermute(x, "tp", core_pairs) for x in (out, beyond)]
-    grad = lay(here, [out, beyond] + from_core)
+    out = [
+        finish(here, step, own, got, early, late, xw, stat, gain)
+        for step, (early, late) in enumerate(((from_next, late_last), (from_last, late_next)))
+    ]
+    beyond = [lax.ppermute(x, "tp", far_pairs) for x in out]
+    beyond[1], new_stream = lax.optimization_barrier((beyond[1], new_stream))
+    from_core = [lax.ppermute(x, "tp", core_pairs) for x in out + beyond]
+    grad = lay(here, out + beyond + from_core)
     return (new_stream, grad[None])
 
 

time: 179 us -> 174 us (0.972)
  waiting for transfers between devices: 70.1 us -> 61.4 us
  Pallas kernels: 42.3 us -> 45.5 us
    ppermute x6, waiting for transfers between devices: 35.1 us -> 0.9 us  [along_ctx(): return lax.ppermute(array, ('ctx', 'tp'), pairs)]
    ppermute x1, waiting for transfers between devices: 0.01 us -> 16.9 us  [shards(): lifted = [lifted, lax.ppermute(lifted, ('img', 'tp'), pairs)]]
    all_to_all x1, waiting for transfers between devices: 0.01 us -> 12.7 us  [shards(): lax.all_to_all(held.reshape(owners, n_img * capacity, width), ('img', 'ct...]
    ppermute x3 -> x6, waiting for transfers between devices: 9.57 us -> 3.73 us  [the longest x2 1.9 us: shards(): beyond = [lax.ppermute(x, 'tp', far_pairs) for x in out]]
    all_to_all x1, starting transfers between devices: 5.98 us -> 3.66 us  [shards(): lax.all_to_all(send, 'ctx', split_axis=0, concat_axis=0, tiled=True)]
    pallas_call x1 -> x2, Pallas kernels: 4.98 us -> 7.21 us  [finish(): pl.pallas_call(finish_kernel, grid_spec=pltpu.PrefetchScalarGridSpec(num_...]
    ppermute x3 -> x6, starting transfers between devices: 7.46 us -> 8.94 us  [the longest x4 5.97 us: shards(): from_core = [lax.ppermute(x, 'tp', core_pairs) for x in out + beyond]]
    unnamed x48 -> x50, local copies, waits for them, and re-layouts: 9.44 us -> 9.93 us
  transfers between devices with their start and end apart: 24 -> 27, of which waited for: 10 -> 12; matrix products, arithmetic and copies ran while one was open for 1% -> 1% of each run, Pallas kernels for 19% -> 20%
where the time goes in v16:
time: 174 us; the launch traced here: 173 us
  waiting for transfers between devices  61.4 us (35%)
  starting transfers between devices  52.6 us (30%)
  Pallas kernels  45.5 us (26%)
  local copies, waits for them, and re-layouts  11.6 us (7%)
    ppermute x1, waiting for transfers between devices, shards(): lifted = [lifted, lax.ppermute(lifted, ('img', 'tp'), pairs)]  16.9 us
    ppermute x7, waiting for transfers between devices, along_x(): return lax.ppermute(array, ('img', 'tp'), pairs)  16.1 us
    all_to_all x1, waiting for transfers between devices, shards(): lax.all_to_all(held.reshape(owners, n_img * capacity, width), ('img', 'ct...  12.7 us
    ppermute x7, starting transfers between devices, along_x(): return lax.ppermute(array, ('img', 'tp'), pairs)  10.7 us
    unnamed x50, local copies, waits for them, and re-layouts  9.93 us
    ppermute x6, starting transfers between devices, along_ctx(): return lax.ppermute(array, ('ctx', 'tp'), pairs)  9.64 us
    pallas_call x1, Pallas kernels, layer_norm(): pl.pallas_call(norm_kernel, grid_spec=pltpu.PrefetchScalarGridSpec(num_sc...  7.62 us
    pallas_call x2, Pallas kernels, finish(): pl.pallas_call(finish_kernel, grid_spec=pltpu.PrefetchScalarGridSpec(num_...  7.21 us
  transfers between devices with their start and end apart: 27, of which 12 were waited for; matrix products, arithmetic and copies ran while one was open for 1% of the time, Pallas kernels for 20%

profile of v16, /device:TPU:1, one launch (start us, length us, event | category | flops | bytes accessed | tf_op | source)
XLA Modules:
  0.0 173.4 jit_solution(6733821974099012447)
XLA Ops:
  0.7 1.0 copy-done
  1.7 2.5 %collective-permute-start = (bf16[288,512]{1,0:T(8,128)(2,1)S(1)}, bf16[288,512]{1,0:T(8,128)(2,1)S(1)}, u32[]{:S(2)}, u32[]{:S(2)}) collective-permute-start(bf16[288,512]{1,0:T(8,128)(2,1)S(1)} %bitcast.22), channel_id=1, source_target_pairs={{0,4},{1,17},{2,6},{3,19},{4,8},{5,21},{6,10},{7,23},{8,12},{9,25}... | collective-permute-start | bytes 884744 | tf_op jit(solution)/shard_map/ppermute | solution.py:686
  4.3 2.2 %collective-permute-start.1 = (bf16[288,512]{1,0:T(8,128)(2,1)S(1)}, bf16[288,512]{1,0:T(8,128)(2,1)S(1)}, u32[]{:S(2)}, u32[]{:S(2)}) collective-permute-start(bf16[288,512]{1,0:T(8,128)(2,1)S(1)} %bitcast.23), channel_id=1, source_target_pairs={{0,12},{1,49},{2,14},{3,51},{4,0},{5,53},{6,2},{7,55},{8,4},{9,57}... | collective-permute-start | bytes 884744 | tf_op jit(solution)/shard_map/ppermute | solution.py:686
  6.5 1.2 collective-permute-start.2
  9.5 7.0 %all-to-all-start = ((s32[32,1,16]{2,1,0:T(1,128)}), s32[32,1,16]{2,1,0:T(1,128)S(1)}, u32[]{:S(2)}, u32[]{:S(2)}) async-start(s32[32,1,16]{2,1,0:T(1,128)} %bitcast.5), calls=%async_computation | async-start | bytes 32768 | tf_op jit(solution)/shard_map/all_to_all | solution.py:698
  16.5 1.3 collective-permute-start.3
  18.5 7.6 %layer_norm.1 = (bf16[256,4608]{1,0:T(8,128)(2,1)}, bf16[4,256,1152]{2,1,0:T(8,128)(2,1)}, f32[256,128]{1,0:T(8,128)}) custom-call(s32[5]{0:T(128)} %stack.24.here_ref.refs_0_, bf16[1024,1152]{1,0:T(8,128)(2,1)} %bitcast.27, bf16[4,1152]{1,0:T(4,128)(2,1)} %bitcast.29, bf16[4,1152]{1,0:T(4,128)(2,1)} %bitcast.34), custom_call_target="tpu_custom_call" | custom-call | tf_op jit(solution)/shard_map/layer_norm/pallas_call | solution.py:97
  27.0 1.6 collective-permute-start.5
  28.6 1.2 collective-permute-start.4
  30.0 1.2 copy-done.10
  31.2 1.2 copy-done.16
  32.4 1.3 collect.1
  33.8 1.4 copy-done.7
  35.2 6.7 %all-to-all-start.1 = ((bf16[32,32,1024]{2,1,0:T(8,128)(2,1)}), bf16[32,32,1024]{2,1,0:T(8,128)(2,1)}, u32[]{:S(2)}, u32[]{:S(2)}) async-start(bf16[32,32,1024]{2,1,0:T(8,128)(2,1)} %bitcast.21), calls=%async_computation.1 | async-start | bytes 4194304 | tf_op jit(solution)/shard_map/all_to_all | solution.py:719
  41.9 2.4 %collective-permute-start.6 = (bf16[4,288,512]{2,1,0:T(8,128)(2,1)S(1)}, bf16[4,288,512]{2,1,0:T(8,128)(2,1)}, u32[]{:S(2)}, u32[]{:S(2)}) collective-permute-start(bf16[4,288,512]{2,1,0:T(8,128)(2,1)S(1)} %stack.25.refs_0_.after_ref.refs_6_), channel_id=1, source_target_pairs={{0,48},{1,13},{2,50},{3,15},{4,52},{5,1},{6,54},{7,3},{8,56},{9,5}... | collective-permute-start | bytes 3538952 | tf_op jit(solution)/shard_map/ppermute | solution.py:686
  45.4 16.9 %collective-permute-done.5.refs_3_ = bf16[256,4608]{1,0:T(8,128)(2,1)} collective-permute-done((bf16[256,4608]{1,0:T(8,128)(2,1)}, bf16[256,4608]{1,0:T(8,128)(2,1)}, u32[]{:S(2)}, u32[]{:S(2)}) %collective-permute-start.5) | collective-permute-done | bytes 2359328 | tf_op jit(solution)/shard_map/ppermute | solution.py:732
  62.3 5.5 %multiply.1.after_ref.acc_hbm = f32[512,512]{1,0:T(8,128)} custom-call(s32[5]{0:T(128)} %stack.24.here_ref.refs_0_, bf16[4,288,512]{2,1,0:T(8,128)(2,1)} %copy-done.3, bf16[4,288,512]{2,1,0:T(8,128)(2,1)} %copy-done.8, bf16[256,4608]{1,0:T(8,128)(2,1)} %get-tuple-element.50.refs_2_, bf16[256,4608]{1,0:T(8,128)(2,1)} %collective-permute-done.5.refs_3_), custom_call_target="tpu_custom_call" | custom-call | tf_op jit(solution)/shard_map/multiply/pallas_call | solution.py:273
  67.8 12.7 %all-to-all-done.1 = bf16[32,32,1024]{2,1,0:T(8,128)(2,1)} async-done(((bf16[32,32,1024]{2,1,0:T(8,128)(2,1)}), bf16[32,32,1024]{2,1,0:T(8,128)(2,1)}, u32[]{:S(2)}, u32[]{:S(2)}) %all-to-all-start.1) | async-done | bytes 2097184 | tf_op jit(solution)/shard_map/all_to_all | solution.py:719
  80.5 1.2 copy-done.5
  81.7 3.0 %unpack.1 = (bf16[512,512]{1,0:T(8,128)(2,1)S(1)}, bf16[512,512]{1,0:T(8,128)(2,1)S(1)}) custom-call(s32[512,1]{1,0:T(8,128)S(1)} %copy.28.slot_ref, bf16[1024,1024]{1,0:T(8,128)(2,1)} %bitcast.17.came_ref, f32[512,512]{1,0:T(8,128)S(1)} %copy-done.5), custom_call_target="tpu_custom_call" | custom-call | tf_op jit(solution)/shard_map/unpack/pallas_call | solution.py:169
  84.8 5.1 %merge.1 = (bf16[512,512]{1,0:T(8,128)(2,1)S(1)}, f32[512,512]{1,0:T(8,128)S(1)}, f32[8,512]{1,0:T(8,128)S(1)}) custom-call(s32[5]{0:T(128)S(1)} %copy-done.20, bf16[1,512]{1,0:T(2,128)(2,1)S(1)} %constant_dynamic-slice_fusion.1.ngain_ref.refs_1_, f32[512,512]{1,0:T(8,128)S(1)} %copy-done.6, bf16[512,512]{1,0:T(8,128)(2,1)S(1)} %get-tuple-element.52.base_hbm, ...), custom_call_target="tpu_custom_call" | custom-call | tf_op jit(solution)/shard_map/merge/pallas_call | solution.py:315
  89.9 1.2 collective-permute-done.8.got_ref
  91.1 2.6 %collective-permute-start.10 = (f32[8,512]{1,0:T(8,128)S(1)}, f32[8,512]{1,0:T(8,128)S(1)}, u32[]{:S(2)}, u32[]{:S(2)}) collective-permute-start(f32[8,512]{1,0:T(8,128)S(1)} %get-tuple-element.59.after_ref.refs_2_), channel_id=1, source_target_pairs={{0,2},{1,3},{2,0},{3,1},{64,66},{65,67},{66,64},{67,65},{4,6},{5,7... | collective-permute-start | bytes 49160 | tf_op jit(solution)/shard_map/ppermute | solution.py:674
  93.7 3.3 %collective-permute-start.11 = (f32[8,512]{1,0:T(8,128)S(1)}, f32[8,512]{1,0:T(8,128)S(1)}, u32[]{:S(2)}, u32[]{:S(2)}) collective-permute-start(f32[8,512]{1,0:T(8,128)S(1)} %get-tuple-element.58), channel_id=1, source_target_pairs={{0,66},{1,67},{2,64},{3,65},{64,0},{65,1},{66,2},{67,3},{4,70},{5,... | collective-permute-start | bytes 49160 | tf_op jit(solution)/shard_map/ppermute | solution.py:674
  97.0 1.4 pack.1
  98.4 2.4 %collective-permute-done.9.refs_3_ = f32[8,512]{1,0:T(8,128)S(1)} collective-permute-done((f32[8,512]{1,0:T(8,128)S(1)}, f32[8,512]{1,0:T(8,128)S(1)}, u32[]{:S(2)}, u32[]{:S(2)}) %collective-permute-start.9) | collective-permute-done | bytes 16416 | tf_op jit(solution)/shard_map/ppermute | solution.py:674
  100.8 5.5 %backward.1 = (bf16[256,4608]{1,0:T(8,128)(2,1)S(1)}, bf16[256,4608]{1,0:T(8,128)(2,1)S(1)}) custom-call(s32[5]{0:T(128)S(1)} %copy-done.20, bf16[1,512]{1,0:T(2,128)(2,1)S(1)} %constant_dynamic-slice_fusion.1.ngain_ref.refs_1_, f32[8,512]{1,0:T(8,128)S(1)} %get-tuple-element.59.after_ref.refs_2_, f32[8,512]{1,0:T(8,128)S(1)} %collective-permute-done.9.refs_3_, ...), custom_call_target="tpu_custom_call" | custom-call | tf_op jit(solution)/shard_map/backward/pallas_call | solution.py:451
  106.3 5.8 %collective-permute-done.12.after_ref.crossed_ref = bf16[512,512]{1,0:T(8,128)(2,1)S(1)} collective-permute-done((bf16[512,512]{1,0:T(8,128)(2,1)S(1)}, bf16[512,512]{1,0:T(8,128)(2,1)S(1)}, u32[]{:S(2)}, u32[]{:S(2)}) %collective-permute-start.12) | collective-permute-done | bytes 524320 | tf_op jit(solution)/shard_map/ppermute | solution.py:743
  112.1 3.0 %collective-permute-start.13 = (bf16[256,4608]{1,0:T(8,128)(2,1)S(1)}, bf16[256,4608]{1,0:T(8,128)(2,1)S(1)}, u32[]{:S(2)}, u32[]{:S(2)}) collective-permute-start(bf16[256,4608]{1,0:T(8,128)(2,1)S(1)} %get-tuple-element.68), channel_id=1, source_target_pairs={{0,1},{1,0},{2,3},{3,2},{4,5},{5,4},{6,7},{7,6},{8,9},{9,8},{10,11... | collective-permute-start | bytes 7077896 | tf_op jit(solution)/shard_map/ppermute | solution.py:747
  115.1 4.2 %collective-permute-done.13.got_ref = bf16[256,4608]{1,0:T(8,128)(2,1)S(1)} collective-permute-done((bf16[256,4608]{1,0:T(8,128)(2,1)S(1)}, bf16[256,4608]{1,0:T(8,128)(2,1)S(1)}, u32[]{:S(2)}, u32[]{:S(2)}) %collective-permute-start.13) | collective-permute-done | bytes 2359328 | tf_op jit(solution)/shard_map/ppermute | solution.py:747
  119.3 1.8 %pair.1 = (bf16[64,4608]{1,0:T(8,128)(2,1)}, bf16[64,4608]{1,0:T(8,128)(2,1)}, bf16[64,4608]{1,0:T(8,128)(2,1)S(1)}) custom-call(bf16[256,4608]{1,0:T(8,128)(2,1)S(1)} %get-tuple-element.67.own_ref, bf16[256,4608]{1,0:T(8,128)(2,1)S(1)} %collective-permute-done.13.got_ref, bf16[512,512]{1,0:T(8,128)(2,1)S(1)} %collective-permute-done.12.after_ref.crossed_ref), custom_call_target="tpu_custom_call" | custom-call | tf_op jit(solution)/shard_map/pair/pallas_call | solution.py:492
  121.9 2.7 %collective-permute-start.15 = (bf16[64,4608]{1,0:T(8,128)(2,1)}, bf16[64,4608]{1,0:T(8,128)(2,1)S(1)}, u32[]{:S(2)}, u32[]{:S(2)}) collective-permute-start(bf16[64,4608]{1,0:T(8,128)(2,1)} %get-tuple-element.72), channel_id=1, source_target_pairs={{0,66},{1,67},{2,64},{3,65},{64,0},{65,1},{66,2},{67,3},{4,70},{5,... | collective-permute-start | bytes 1769480 | tf_op jit(solution)/shard_map/ppermute | solution.py:674
  124.6 1.0 braid.1
  125.6 3.7 %all-to-all-start.2 = ((bf16[16,2,32,512]{3,2,1,0:T(8,128)(2,1)}), bf16[16,2,32,512]{3,2,1,0:T(8,128)(2,1)S(1)}, u32[]{:S(2)}, u32[]{:S(2)}) async-start(bf16[16,2,32,512]{3,2,1,0:T(8,128)(2,1)} %braid.1), calls=%async_computation.2 | async-start | bytes 2097152 | tf_op jit(solution)/shard_map/all_to_all | solution.py:754
  129.3 8.6 %collective-permute-done.14.from_last_ref.early_ref = bf16[64,4608]{1,0:T(8,128)(2,1)S(1)} collective-permute-done((bf16[64,4608]{1,0:T(8,128)(2,1)}, bf16[64,4608]{1,0:T(8,128)(2,1)S(1)}, u32[]{:S(2)}, u32[]{:S(2)}) %collective-permute-start.14) | collective-permute-done | bytes 589856 | tf_op jit(solution)/shard_map/ppermute | solution.py:674
  137.9 1.5 copy-done.18
  139.6 2.2 %collective-permute-start.16 = (bf16[32,4608]{1,0:T(8,128)(2,1)S(1)}, bf16[32,4608]{1,0:T(8,128)(2,1)S(1)}, u32[]{:S(2)}, u32[]{:S(2)}) collective-permute-start(bf16[32,4608]{1,0:T(8,128)(2,1)S(1)} %get-tuple-element.73), channel_id=1, source_target_pairs={{0,66},{1,67},{2,64},{3,65},{64,0},{65,1},{66,2},{67,3},{4,70},{5,... | collective-permute-start | bytes 884744 | tf_op jit(solution)/shard_map/ppermute | solution.py:674
  141.9 5.2 %collective-permute-done.16.late_ref = bf16[32,4608]{1,0:T(8,128)(2,1)S(1)} collective-permute-done((bf16[32,4608]{1,0:T(8,128)(2,1)S(1)}, bf16[32,4608]{1,0:T(8,128)(2,1)S(1)}, u32[]{:S(2)}, u32[]{:S(2)}) %collective-permute-start.16) | collective-permute-done | bytes 294944 | tf_op jit(solution)/shard_map/ppermute | solution.py:674
  147.7 3.6 %finish.2.refs_1_ = bf16[128,1152]{1,0:T(8,128)(2,1)} custom-call(s32[5]{0:T(128)} %stack.24.here_ref.refs_0_, bf16[256,4608]{1,0:T(8,128)(2,1)} %copy-done.1, bf16[256,4608]{1,0:T(8,128)(2,1)} %copy-done.2, bf16[64,4608]{1,0:T(8,128)(2,1)} %copy-done.13, bf16[32,4608]{1,0:T(8,128)(2,1)} %copy-done.23, bf16[4,256,1152]{2,1,0:T(8,128)(2,1)} %get-tuple-element.74.xw_ref, ...), custom_call_target="tpu_custom_call" | custom-call | tf_op jit(solution)/shard_map/finish/pallas_call | solution.py:565
  151.3 1.8 %collective-permute-start.17 = (bf16[128,1152]{1,0:T(8,128)(2,1)}, bf16[128,1152]{1,0:T(8,128)(2,1)}, u32[]{:S(2)}, u32[]{:S(2)}) collective-permute-start(bf16[128,1152]{1,0:T(8,128)(2,1)} %finish.2.refs_1_), channel_id=1, source_target_pairs={{0,2},{1,3},{2,0},{3,1},{4,6},{5,7},{6,4},{7,5},{8,10},{9,11},{10,... | collective-permute-start | bytes 884744 | tf_op jit(solution)/shard_map/ppermute | solution.py:761
  153.9 3.6 %finish.3.refs_0_ = bf16[128,1152]{1,0:T(8,128)(2,1)} custom-call(s32[5]{0:T(128)} %stack.24.here_ref.refs_0_, bf16[256,4608]{1,0:T(8,128)(2,1)} %copy-done.1, bf16[256,4608]{1,0:T(8,128)(2,1)} %copy-done.2, bf16[64,4608]{1,0:T(8,128)(2,1)} %copy-done.12, bf16[32,4608]{1,0:T(8,128)(2,1)} %copy-done.22, bf16[4,256,1152]{2,1,0:T(8,128)(2,1)} %get-tuple-element.74.xw_ref, ...), custom_call_target="tpu_custom_call" | custom-call | tf_op jit(solution)/shard_map/finish/pallas_call | solution.py:565
  157.5 1.2 collective-permute-start.19
  158.7 2.4 %place.1 = bf16[512,1024]{1,0:T(8,128)(2,1)} custom-call(s32[5]{0:T(128)S(1)} %copy-done.21, s32[512,1]{1,0:T(8,128)S(1)} %reshape.38.pos_ref, bf16[16,2,32,512]{3,2,1,0:T(8,128)(2,1)S(1)} %all-to-all-done.2.came_ref, bf16[512,1024]{1,0:T(8,128)(2,1)S(1)} %copy-done.11), custom_call_target="tpu_custom_call" | custom-call | tf_op jit(solution)/shard_map/place/pallas_call | solution.py:606
  161.0 2.7 %collective-permute-start.20 = (bf16[128,1152]{1,0:T(8,128)(2,1)S(1)}, bf16[128,1152]{1,0:T(8,128)(2,1)S(1)}, u32[]{:S(2)}, u32[]{:S(2)}) collective-permute-start(bf16[128,1152]{1,0:T(8,128)(2,1)S(1)} %copy-done.15), channel_id=1, source_target_pairs={{0,1},{1,0},{2,3},{3,2},{4,5},{5,4},{6,7},{7,6},{8,9},{9,8},{10,11... | collective-permute-start | bytes 884744 | tf_op jit(solution)/shard_map/ppermute | solution.py:763
  163.8 1.9 %collective-permute-done.19.refs_2_ = bf16[128,1152]{1,0:T(8,128)(2,1)} collective-permute-done((bf16[128,1152]{1,0:T(8,128)(2,1)}, bf16[128,1152]{1,0:T(8,128)(2,1)}, u32[]{:S(2)}, u32[]{:S(2)}) %collective-permute-start.19) | collective-permute-done | bytes 294944 | tf_op jit(solution)/shard_map/ppermute | solution.py:761
  165.7 3.2 %collective-permute-start.22 = (bf16[128,1152]{1,0:T(8,128)(2,1)}, bf16[128,1152]{1,0:T(8,128)(2,1)S(1)}, u32[]{:S(2)}, u32[]{:S(2)}) collective-permute-start(bf16[128,1152]{1,0:T(8,128)(2,1)} %collective-permute-done.19.refs_2_), channel_id=1, source_target_pairs={{0,1},{1,0},{2,3},{3,2},{4,5},{5,4},{6,7},{7,6},{8,9},{9,8},{10,11... | collective-permute-start | bytes 884744 | tf_op jit(solution)/shard_map/ppermute | solution.py:763
  168.9 1.4 collective-permute-done.22.refs_6_
  170.7 2.5 %lay.1 = bf16[1024,1152]{1,0:T(8,128)(2,1)} custom-call(s32[5]{0:T(128)S(1)} %copy-done.21, bf16[128,1152]{1,0:T(8,128)(2,1)S(1)} %copy-done.15, bf16[128,1152]{1,0:T(8,128)(2,1)S(1)} %copy-done.14, bf16[128,1152]{1,0:T(8,128)(2,1)} %collective-permute-done.19.refs_2_, bf16[128,1152]{1,0:T(8,128)(2,1)} %collective-permute-done.17.refs_3_, ...), custom_call_target="tpu_custom_call" | custom-call | tf_op jit(solution)/shard_map/lay/pallas_call | solution.py:634
  (85 shorter events, 7.8 us)
Async XLA Ops:
  1.7 24.4 %collective-permute-start = (bf16[288,512]{1,0:T(8,128)(2,1)S(1)}, bf16[288,512]{1,0:T(8,128)(2,1)S(1)}, u32[]{:S(2)}, u32[]{:S(2)}) collective-permute-start(bf16[288,512]{1,0:T(8,128)(2,1)S(1)} %bitcast.22), channel_id=1, source_target_pairs={{0,4},{1,17},{2,6},{3,19},{4,8},{5,21},{6,10},{7,23},{8,12},{9,25}... | collective-permute-start | bytes 884744 | tf_op jit(solution)/shard_map/ppermute | solution.py:686
  4.3 21.9 %collective-permute-start.1 = (bf16[288,512]{1,0:T(8,128)(2,1)S(1)}, bf16[288,512]{1,0:T(8,128)(2,1)S(1)}, u32[]{:S(2)}, u32[]{:S(2)}) collective-permute-start(bf16[288,512]{1,0:T(8,128)(2,1)S(1)} %bitcast.23), channel_id=1, source_target_pairs={{0,12},{1,49},{2,14},{3,51},{4,0},{5,53},{6,2},{7,55},{8,4},{9,57}... | collective-permute-start | bytes 884744 | tf_op jit(solution)/shard_map/ppermute | solution.py:686
  6.5 19.7 %collective-permute-start.2 = (bf16[288,512]{1,0:T(8,128)(2,1)S(1)}, bf16[288,512]{1,0:T(8,128)(2,1)S(1)}, u32[]{:S(2)}, u32[]{:S(2)}) collective-permute-start(bf16[288,512]{1,0:T(8,128)(2,1)S(1)} %bitcast.24), channel_id=1, source_target_pairs={{0,8},{1,33},{2,10},{3,35},{4,12},{5,37},{6,14},{7,39},{8,0},{9,41... | collective-permute-start | bytes 884744 | tf_op jit(solution)/shard_map/ppermute | solution.py:686
  9.5 16.6 %all-to-all-start = ((s32[32,1,16]{2,1,0:T(1,128)}), s32[32,1,16]{2,1,0:T(1,128)S(1)}, u32[]{:S(2)}, u32[]{:S(2)}) async-start(s32[32,1,16]{2,1,0:T(1,128)} %bitcast.5), calls=%async_computation | async-start | bytes 32768 | tf_op jit(solution)/shard_map/all_to_all | solution.py:698
  16.5 9.6 %collective-permute-start.3 = (s32[256]{0:T(256)S(1)}, s32[256]{0:T(256)S(1)}, u32[]{:S(2)}, u32[]{:S(2)}) collective-permute-start(s32[256]{0:T(256)S(1)} %get-tuple-element.82), channel_id=1, source_target_pairs={{0,64},{64,0},{1,65},{65,1},{2,66},{66,2},{3,67},{67,3},{4,68},{68... | collective-permute-start | bytes 3080 | tf_op jit(solution)/shard_map/ppermute | solution.py:705
  18.5 7.7 %copy-start.19 = (s32[5]{0:T(128)S(1)}, s32[5]{0:T(128)}, u32[]{:S(2)}) copy-start(s32[5]{0:T(128)} %stack.24.here_ref.refs_0_) | copy-start | bytes 64
  27.0 14.9 %copy-start.3 = (bf16[4,288,512]{2,1,0:T(8,128)(2,1)}, bf16[4,288,512]{2,1,0:T(8,128)(2,1)S(1)}, u32[]{:S(2)}) copy-start(bf16[4,288,512]{2,1,0:T(8,128)(2,1)S(1)} %stack.25.refs_0_.after_ref.refs_6_) | copy-start | bytes 3538948
  27.0 35.3 %collective-permute-start.5 = (bf16[256,4608]{1,0:T(8,128)(2,1)}, bf16[256,4608]{1,0:T(8,128)(2,1)}, u32[]{:S(2)}, u32[]{:S(2)}) collective-permute-start(bf16[256,4608]{1,0:T(8,128)(2,1)} %get-tuple-element.50.refs_2_), channel_id=1, source_target_pairs={{0,64},{1,67},{2,66},{3,65},{64,2},{65,1},{66,0},{67,3},{4,68},{5,... | collective-permute-start | bytes 7077896 | tf_op jit(solution)/shard_map/ppermute | solution.py:732
  28.6 16.7 %collective-permute-start.4 = (bf16[4,288,512]{2,1,0:T(8,128)(2,1)S(1)}, bf16[4,288,512]{2,1,0:T(8,128)(2,1)S(1)}, u32[]{:S(2)}, u32[]{:S(2)}) collective-permute-start(bf16[4,288,512]{2,1,0:T(8,128)(2,1)S(1)} %stack.25.refs_0_.after_ref.refs_6_), channel_id=1, source_target_pairs={{0,16},{1,5},{2,18},{3,7},{4,20},{5,9},{6,22},{7,11},{8,24},{9,13}... | collective-permute-start | bytes 3538952 | tf_op jit(solution)/shard_map/ppermute | solution.py:686
  30.0 1.2 copy-start.10
  31.2 1.2 copy-start.16
  33.7 1.4 copy-start.7
  35.2 10.1 %copy-start.24 = (bf16[1,1024]{1,0:T(2,128)(2,1)S(1)}, bf16[1,1024]{1,0:T(2,128)(2,1)}, u32[]{:S(2)}) copy-start(bf16[1,1024]{1,0:T(2,128)(2,1)} %param.13) | copy-start | bytes 6148
  35.2 45.3 %all-to-all-start.1 = ((bf16[32,32,1024]{2,1,0:T(8,128)(2,1)}), bf16[32,32,1024]{2,1,0:T(8,128)(2,1)}, u32[]{:S(2)}, u32[]{:S(2)}) async-start(bf16[32,32,1024]{2,1,0:T(8,128)(2,1)} %bitcast.21), calls=%async_computation.1 | async-start | bytes 4194304 | tf_op jit(solution)/shard_map/all_to_all | solution.py:719
  41.9 42.8 %collective-permute-start.6 = (bf16[4,288,512]{2,1,0:T(8,128)(2,1)S(1)}, bf16[4,288,512]{2,1,0:T(8,128)(2,1)}, u32[]{:S(2)}, u32[]{:S(2)}) collective-permute-start(bf16[4,288,512]{2,1,0:T(8,128)(2,1)S(1)} %stack.25.refs_0_.after_ref.refs_6_), channel_id=1, source_target_pairs={{0,48},{1,13},{2,50},{3,15},{4,52},{5,1},{6,54},{7,3},{8,56},{9,5}... | collective-permute-start | bytes 3538952 | tf_op jit(solution)/shard_map/ppermute | solution.py:686
  45.2 17.1 %copy-start.8 = (bf16[4,288,512]{2,1,0:T(8,128)(2,1)}, bf16[4,288,512]{2,1,0:T(8,128)(2,1)S(1)}, u32[]{:S(2)}) copy-start(bf16[4,288,512]{2,1,0:T(8,128)(2,1)S(1)} %collective-permute-done.4.refs_1_.refs_7_) | copy-start | bytes 3538948
  45.2 39.5 %collective-permute-start.7 = (bf16[4,288,512]{2,1,0:T(8,128)(2,1)S(1)}, bf16[4,288,512]{2,1,0:T(8,128)(2,1)}, u32[]{:S(2)}, u32[]{:S(2)}) collective-permute-start(bf16[4,288,512]{2,1,0:T(8,128)(2,1)S(1)} %collective-permute-done.4.refs_1_.refs_7_), channel_id=1, source_target_pairs={{0,16},{1,5},{2,18},{3,7},{4,20},{5,9},{6,22},{7,11},{8,24},{9,13}... | collective-permute-start | bytes 3538952 | tf_op jit(solution)/shard_map/ppermute | solution.py:686
  67.8 16.9 %copy-start.20 = (s32[5]{0:T(128)S(1)}, s32[5]{0:T(128)}, u32[]{:S(2)}) copy-start(s32[5]{0:T(128)} %stack.24.here_ref.refs_0_) | copy-start | bytes 64
  80.5 1.2 copy-start.5
  81.7 3.0 %copy-start.6 = (f32[512,512]{1,0:T(8,128)S(1)}, f32[512,512]{1,0:T(8,128)}, u32[]{:S(2)}) copy-start(f32[512,512]{1,0:T(8,128)} %multiply.1.after_ref.acc_hbm) | copy-start | bytes 3145732
  84.7 16.0 %copy-start.4 = (bf16[4,288,512]{2,1,0:T(8,128)(2,1)S(1)}, bf16[4,288,512]{2,1,0:T(8,128)(2,1)}, u32[]{:S(2)}) copy-start(bf16[4,288,512]{2,1,0:T(8,128)(2,1)} %copy-done.3) | copy-start | bytes 3538948
  84.7 16.0 %copy-start.9 = (bf16[4,288,512]{2,1,0:T(8,128)(2,1)S(1)}, bf16[4,288,512]{2,1,0:T(8,128)(2,1)}, u32[]{:S(2)}) copy-start(bf16[4,288,512]{2,1,0:T(8,128)(2,1)} %copy-done.8) | copy-start | bytes 3538948
  89.8 1.3 collective-permute-start.8
  91.1 7.2 %collective-permute-start.10 = (f32[8,512]{1,0:T(8,128)S(1)}, f32[8,512]{1,0:T(8,128)S(1)}, u32[]{:S(2)}, u32[]{:S(2)}) collective-permute-start(f32[8,512]{1,0:T(8,128)S(1)} %get-tuple-element.59.after_ref.refs_2_), channel_id=1, source_target_pairs={{0,2},{1,3},{2,0},{3,1},{64,66},{65,67},{66,64},{67,65},{4,6},{5,7... | collective-permute-start | bytes 49160 | tf_op jit(solution)/shard_map/ppermute | solution.py:674
  93.7 4.7 %collective-permute-start.11 = (f32[8,512]{1,0:T(8,128)S(1)}, f32[8,512]{1,0:T(8,128)S(1)}, u32[]{:S(2)}, u32[]{:S(2)}) collective-permute-start(f32[8,512]{1,0:T(8,128)S(1)} %get-tuple-element.58), channel_id=1, source_target_pairs={{0,66},{1,67},{2,64},{3,65},{64,0},{65,1},{66,2},{67,3},{4,70},{5,... | collective-permute-start | bytes 49160 | tf_op jit(solution)/shard_map/ppermute | solution.py:674
  96.9 3.8 %collective-permute-start.9 = (f32[8,512]{1,0:T(8,128)S(1)}, f32[8,512]{1,0:T(8,128)S(1)}, u32[]{:S(2)}, u32[]{:S(2)}) collective-permute-start(f32[8,512]{1,0:T(8,128)S(1)} %get-tuple-element.58), channel_id=1, source_target_pairs={{0,64},{1,65},{2,66},{3,67},{64,2},{65,3},{66,0},{67,1},{4,68},{5,... | collective-permute-start | bytes 49160 | tf_op jit(solution)/shard_map/ppermute | solution.py:674
  100.7 11.4 %collective-permute-start.12 = (bf16[512,512]{1,0:T(8,128)(2,1)S(1)}, bf16[512,512]{1,0:T(8,128)(2,1)S(1)}, u32[]{:S(2)}, u32[]{:S(2)}) collective-permute-start(bf16[512,512]{1,0:T(8,128)(2,1)S(1)} %get-tuple-element.66), channel_id=1, source_target_pairs={{0,64},{64,0},{1,65},{65,1},{2,66},{66,2},{3,67},{67,3},{4,68},{68... | collective-permute-start | bytes 1572872 | tf_op jit(solution)/shard_map/ppermute | solution.py:743
  106.3 14.8 %copy-start.1 = (bf16[256,4608]{1,0:T(8,128)(2,1)}, bf16[256,4608]{1,0:T(8,128)(2,1)S(1)}, u32[]{:S(2)}) copy-start(bf16[256,4608]{1,0:T(8,128)(2,1)S(1)} %get-tuple-element.67.own_ref) | copy-start | bytes 7077892
  112.1 7.1 %collective-permute-start.13 = (bf16[256,4608]{1,0:T(8,128)(2,1)S(1)}, bf16[256,4608]{1,0:T(8,128)(2,1)S(1)}, u32[]{:S(2)}, u32[]{:S(2)}) collective-permute-start(bf16[256,4608]{1,0:T(8,128)(2,1)S(1)} %get-tuple-element.68), channel_id=1, source_target_pairs={{0,1},{1,0},{2,3},{3,2},{4,5},{5,4},{6,7},{7,6},{8,9},{9,8},{10,11... | collective-permute-start | bytes 7077896 | tf_op jit(solution)/shard_map/ppermute | solution.py:747
  119.3 1.8 %copy-start.2 = (bf16[256,4608]{1,0:T(8,128)(2,1)}, bf16[256,4608]{1,0:T(8,128)(2,1)S(1)}, u32[]{:S(2)}) copy-start(bf16[256,4608]{1,0:T(8,128)(2,1)S(1)} %collective-permute-done.13.got_ref) | copy-start | bytes 7077892
  121.9 16.0 %collective-permute-start.14 = (bf16[64,4608]{1,0:T(8,128)(2,1)}, bf16[64,4608]{1,0:T(8,128)(2,1)S(1)}, u32[]{:S(2)}, u32[]{:S(2)}) collective-permute-start(bf16[64,4608]{1,0:T(8,128)(2,1)} %get-tuple-element.70), channel_id=1, source_target_pairs={{0,64},{1,65},{2,66},{3,67},{64,2},{65,3},{66,0},{67,1},{4,68},{5,... | collective-permute-start | bytes 1769480 | tf_op jit(solution)/shard_map/ppermute | solution.py:674
  121.9 16.0 %collective-permute-start.15 = (bf16[64,4608]{1,0:T(8,128)(2,1)}, bf16[64,4608]{1,0:T(8,128)(2,1)S(1)}, u32[]{:S(2)}, u32[]{:S(2)}) collective-permute-start(bf16[64,4608]{1,0:T(8,128)(2,1)} %get-tuple-element.72), channel_id=1, source_target_pairs={{0,66},{1,67},{2,64},{3,65},{64,0},{65,1},{66,2},{67,3},{4,70},{5,... | collective-permute-start | bytes 1769480 | tf_op jit(solution)/shard_map/ppermute | solution.py:674
  125.6 33.0 %all-to-all-start.2 = ((bf16[16,2,32,512]{3,2,1,0:T(8,128)(2,1)}), bf16[16,2,32,512]{3,2,1,0:T(8,128)(2,1)S(1)}, u32[]{:S(2)}, u32[]{:S(2)}) async-start(bf16[16,2,32,512]{3,2,1,0:T(8,128)(2,1)} %braid.1), calls=%async_computation.2 | async-start | bytes 2097152 | tf_op jit(solution)/shard_map/all_to_all | solution.py:754
  137.9 9.1 %copy-start.13 = (bf16[64,4608]{1,0:T(8,128)(2,1)}, bf16[64,4608]{1,0:T(8,128)(2,1)S(1)}, u32[]{:S(2)}) copy-start(bf16[64,4608]{1,0:T(8,128)(2,1)S(1)} %collective-permute-done.14.from_last_ref.early_ref) | copy-start | bytes 1769476
  137.9 9.1 %copy-start.12 = (bf16[64,4608]{1,0:T(8,128)(2,1)}, bf16[64,4608]{1,0:T(8,128)(2,1)S(1)}, u32[]{:S(2)}) copy-start(bf16[64,4608]{1,0:T(8,128)(2,1)S(1)} %collective-permute-done.15.from_next_ref.early_ref) | copy-start | bytes 1769476
  137.9 1.5 copy-start.18
  139.6 7.4 %collective-permute-start.16 = (bf16[32,4608]{1,0:T(8,128)(2,1)S(1)}, bf16[32,4608]{1,0:T(8,128)(2,1)S(1)}, u32[]{:S(2)}, u32[]{:S(2)}) collective-permute-start(bf16[32,4608]{1,0:T(8,128)(2,1)S(1)} %get-tuple-element.73), channel_id=1, source_target_pairs={{0,66},{1,67},{2,64},{3,65},{64,0},{65,1},{66,2},{67,3},{4,70},{5,... | collective-permute-start | bytes 884744 | tf_op jit(solution)/shard_map/ppermute | solution.py:674
  141.8 11.3 %collective-permute-start.18 = (bf16[32,4608]{1,0:T(8,128)(2,1)S(1)}, bf16[32,4608]{1,0:T(8,128)(2,1)S(1)}, u32[]{:S(2)}, u32[]{:S(2)}) collective-permute-start(bf16[32,4608]{1,0:T(8,128)(2,1)S(1)} %get-tuple-element.78), channel_id=1, source_target_pairs={{0,64},{1,65},{2,66},{3,67},{64,2},{65,3},{66,0},{67,1},{4,68},{5,... | collective-permute-start | bytes 884744 | tf_op jit(solution)/shard_map/ppermute | solution.py:674
  151.3 7.3 %copy-start.11 = (bf16[512,1024]{1,0:T(8,128)(2,1)S(1)}, bf16[512,1024]{1,0:T(8,128)(2,1)}, u32[]{:S(2)}) copy-start(bf16[512,1024]{1,0:T(8,128)(2,1)} %stream_ref.3) | copy-start | bytes 3145732
  151.3 7.3 %copy-start.21 = (s32[5]{0:T(128)S(1)}, s32[5]{0:T(128)}, u32[]{:S(2)}) copy-start(s32[5]{0:T(128)} %stack.24.here_ref.refs_0_) | copy-start | bytes 64
  151.3 12.5 %collective-permute-start.17 = (bf16[128,1152]{1,0:T(8,128)(2,1)}, bf16[128,1152]{1,0:T(8,128)(2,1)}, u32[]{:S(2)}, u32[]{:S(2)}) collective-permute-start(bf16[128,1152]{1,0:T(8,128)(2,1)} %finish.2.refs_1_), channel_id=1, source_target_pairs={{0,2},{1,3},{2,0},{3,1},{4,6},{5,7},{6,4},{7,5},{8,10},{9,11},{10,... | collective-permute-start | bytes 884744 | tf_op jit(solution)/shard_map/ppermute | solution.py:761
  157.5 6.2 %copy-start.14 = (bf16[128,1152]{1,0:T(8,128)(2,1)S(1)}, bf16[128,1152]{1,0:T(8,128)(2,1)}, u32[]{:S(2)}) copy-start(bf16[128,1152]{1,0:T(8,128)(2,1)} %finish.2.refs_1_) | copy-start | bytes 884740
  157.5 8.2 %collective-permute-start.19 = (bf16[128,1152]{1,0:T(8,128)(2,1)}, bf16[128,1152]{1,0:T(8,128)(2,1)}, u32[]{:S(2)}, u32[]{:S(2)}) collective-permute-start(bf16[128,1152]{1,0:T(8,128)(2,1)} %finish.3.refs_0_), channel_id=1, source_target_pairs={{0,2},{1,3},{2,0},{3,1},{4,6},{5,7},{6,4},{7,5},{8,10},{9,11},{10,... | collective-permute-start | bytes 884744 | tf_op jit(solution)/shard_map/ppermute | solution.py:761
  158.7 2.4 %copy-start.15 = (bf16[128,1152]{1,0:T(8,128)(2,1)S(1)}, bf16[128,1152]{1,0:T(8,128)(2,1)}, u32[]{:S(2)}) copy-start(bf16[128,1152]{1,0:T(8,128)(2,1)} %finish.3.refs_0_) | copy-start | bytes 884740
  161.0 7.9 %collective-permute-start.20 = (bf16[128,1152]{1,0:T(8,128)(2,1)S(1)}, bf16[128,1152]{1,0:T(8,128)(2,1)S(1)}, u32[]{:S(2)}, u32[]{:S(2)}) collective-permute-start(bf16[128,1152]{1,0:T(8,128)(2,1)S(1)} %copy-done.15), channel_id=1, source_target_pairs={{0,1},{1,0},{2,3},{3,2},{4,5},{5,4},{6,7},{7,6},{8,9},{9,8},{10,11... | collective-permute-start | bytes 884744 | tf_op jit(solution)/shard_map/ppermute | solution.py:763
  163.7 5.2 %collective-permute-start.21 = (bf16[128,1152]{1,0:T(8,128)(2,1)S(1)}, bf16[128,1152]{1,0:T(8,128)(2,1)S(1)}, u32[]{:S(2)}, u32[]{:S(2)}) collective-permute-start(bf16[128,1152]{1,0:T(8,128)(2,1)S(1)} %copy-done.14), channel_id=1, source_target_pairs={{0,1},{1,0},{2,3},{3,2},{4,5},{5,4},{6,7},{7,6},{8,9},{9,8},{10,11... | collective-permute-start | bytes 884744 | tf_op jit(solution)/shard_map/ppermute | solution.py:763
  165.7 4.6 %collective-permute-start.22 = (bf16[128,1152]{1,0:T(8,128)(2,1)}, bf16[128,1152]{1,0:T(8,128)(2,1)S(1)}, u32[]{:S(2)}, u32[]{:S(2)}) collective-permute-start(bf16[128,1152]{1,0:T(8,128)(2,1)} %collective-permute-done.19.refs_2_), channel_id=1, source_target_pairs={{0,1},{1,0},{2,3},{3,2},{4,5},{5,4},{6,7},{7,6},{8,9},{9,8},{10,11... | collective-permute-start | bytes 884744 | tf_op jit(solution)/shard_map/ppermute | solution.py:763
  168.9 1.8 %collective-permute-start.23 = (bf16[128,1152]{1,0:T(8,128)(2,1)}, bf16[128,1152]{1,0:T(8,128)(2,1)S(1)}, u32[]{:S(2)}, u32[]{:S(2)}) collective-permute-start(bf16[128,1152]{1,0:T(8,128)(2,1)} %collective-permute-done.17.refs_3_), channel_id=1, source_target_pairs={{0,1},{1,0},{2,3},{3,2},{4,5},{5,4},{6,7},{7,6},{8,9},{9,8},{10,11... | collective-permute-start | bytes 884744 | tf_op jit(solution)/shard_map/ppermute | solution.py:763
  (4 other events, 3.3 us)

commit v17 on v16

--- a/solution.py
+++ b/solution.py
@@ -124,17 +124,30 @@
     )(here, features, gain, bias)
 
 
-def collect_kernel(pos_ref, stream_ref, cot_ref, after_ref, out_ref):
+def collect_kernel(pos_ref, stream_hbm, cot_hbm, after_ref, out_hbm, stream_ref, cot_ref, out_ref, sems):
     slots = pos_ref.shape[0]
     rows, width = stream_ref.shape
     cut = width // 2
+    fetches = [
+        pltpu.make_async_copy(a, b, sems.at[i])
+        for i, (a, b) in enumerate(((stream_hbm, stream_ref), (cot_hbm, cot_ref)))
+    ]
+    for copy in fetches:
+        copy.start()
     pick = eq_hot((slots, rows), 1, pos_ref[...])
+    for copy in fetches:
+        copy.wait()
+    stores = []
     for img in range(2):
         at = slice(img * cut, (img + 1) * cut)
         for place, ref in enumerate((stream_ref, cot_ref)):
             out_ref[img, :, place * cut : (place + 1) * cut] = jnp.dot(
                 pick, ref[:, at], preferred_element_type=F32
             ).astype(BF)
+        stores.append(pltpu.make_async_copy(out_ref.at[img], out_hbm.at[img], sems.at[2 + img]))
+        stores[img].start()
+    for copy in stores:
+        copy.wait()
 
 
 def collect(pos, stream, cot, after):
@@ -142,10 +155,12 @@
     rows, width = stream.shape
     return pl.pallas_call(
         collect_kernel,
-        in_specs=[whole()] * 3 + [anywhere()],
-        out_specs=whole(),
+        in_specs=[whole()] + [anywhere()] * 3,
+        out_specs=anywhere(),
         out_shape=shape((2, slots, width), BF),
-        compiler_params=params(20),
+        scratch_shapes=[pltpu.VMEM((rows, width), BF)] * 2
+        + [pltpu.VMEM((2, slots, width), BF), pltpu.SemaphoreType.DMA((4,))],
+        compiler_params=params(58),
         cost_estimate=FREE,
         name="collect",
     )(pos, stream, cot, after)
@@ -264,7 +279,9 @@
 
 
 def multiply_kernel(here_ref, *refs):
-    stacks, lifted, (out_ref, *scratch) = refs[:EARLY], refs[EARLY : EARLY + 2], refs[EARLY + 2 :]
+    stacks, lifted, refs = refs[:EARLY], refs[EARLY : EARLY + 2], refs[EARLY + 2 :]
+    out_ref, done_ref, *scratch = refs
+    done_ref[...] = jnp.zeros_like(done_ref)
     out_ref[...] = product(here_ref, AWAY[:EARLY], stacks, lifted, *scratch)(None)
 
 
@@ -273,8 +290,8 @@
     return pl.pallas_call(
         multiply_kernel,
         in_specs=[scalars()] + [in_hbm()] * (len(stacks) + len(lifted)),
-        out_specs=whole(),
-        out_shape=shape((tokens, width), F32),
+        out_specs=[whole()] * 2,
+        out_shape=[shape((tokens, width), F32), shape((8, 128), F32)],
         scratch_shapes=product_scratch(stacks, lifted),
         compiler_params=params(60),
         cost_estimate=FREE,
@@ -468,7 +485,7 @@
     )(here, ngain, *stats, *stacks, state, cot)
 
 
-def pair_kernel(own_ref, got_ref, after_ref, next_ref, last_ref, keep_hbm, keep_ref, sem):
+def pair_kernel(own_ref, got_ref, after_ref, next_ref, last_ref):
     rows = own_ref.shape[0] // RING
     half = rows // 2
 
@@ -476,15 +493,10 @@
         at = slice(start, start + half)
         return (own_ref[at, :].astype(F32) + got_ref[at, :].astype(F32)).astype(BF)
 
-    keep_ref[:half] = total(rows)
-    keep_ref[half:] = total(3 * rows + half)
-    copy = pltpu.make_async_copy(keep_ref, keep_hbm, sem)
-    copy.start()
     next_ref[:half] = total(2 * rows)
     next_ref[half:] = total(rows + half)
     last_ref[:half] = total(2 * rows + half)
     last_ref[half:] = total(3 * rows)
-    copy.wait()
 
 
 def pair(own, got, after):
@@ -492,39 +504,46 @@
     return pl.pallas_call(
         pair_kernel,
         in_specs=[whole()] * 2 + [anywhere()],
-        out_specs=[whole()] * 2 + [anywhere()],
-        out_shape=[shape((rows, depth), BF)] * 3,
-        scratch_shapes=[pltpu.VMEM((rows, depth), BF), pltpu.SemaphoreType.DMA],
+        out_specs=[whole()] * 2,
+        out_shape=[shape((rows, depth), BF)] * 2,
         compiler_params=params(8),
         cost_estimate=FREE,
         name="pair",
     )(own, got, after)
 
 
-def relay_kernel(keep_hbm, from_last_ref, from_next_ref, next_ref, last_ref, keep_ref, sem):
-    copy = pltpu.make_async_copy(keep_hbm, keep_ref, sem)
-    copy.start()
-    copy.wait()
+def relay_kernel(own_hbm, got_hbm, from_last_ref, from_next_ref, next_ref, last_ref, kept_ref, sems):
     half = next_ref.shape[0]
-    for at, came_ref, out_ref in (
-        (slice(0, half), from_last_ref, next_ref),
-        (slice(half, 2 * half), from_next_ref, last_ref),
-    ):
-        out_ref[...] = (keep_ref[at, :].astype(F32) + came_ref[:half].astype(F32)).astype(BF)
-
-
-def relay(keep, from_last, from_next):
-    rows, depth = keep.shape
+    rows = 2 * half
+    copies = []
+    for place, start in enumerate((rows, 3 * rows + half)):
+        for core, ref in enumerate((own_hbm, got_hbm)):
+            copies.append(
+                pltpu.make_async_copy(
+                    ref.at[pl.ds(start, half)], kept_ref.at[place, core], sems.at[place, core]
+                )
+            )
+            copies[-1].start()
+    for copy in copies:
+        copy.wait()
+    for place, (came_ref, out_ref) in enumerate(((from_last_ref, next_ref), (from_next_ref, last_ref))):
+        kept = (kept_ref[place, 0].astype(F32) + kept_ref[place, 1].astype(F32)).astype(BF)
+        out_ref[...] = (kept.astype(F32) + came_ref[:half].astype(F32)).astype(BF)
+
+
+def relay(own, got, from_last, from_next):
+    rows, depth = from_last.shape
+    half = rows // 2
     return pl.pallas_call(
         relay_kernel,
-        in_specs=[in_hbm()] + [whole()] * 2,
+        in_specs=[anywhere()] * 2 + [whole()] * 2,
         out_specs=[whole()] * 2,
-        out_shape=[shape((rows // 2, depth), BF)] * 2,
-        scratch_shapes=[pltpu.VMEM((rows, depth), BF), pltpu.SemaphoreType.DMA],
-        compiler_params=params(8),
+        out_shape=[shape((half, depth), BF)] * 2,
+        scratch_shapes=[pltpu.VMEM((2, 2, half, depth), BF), pltpu.SemaphoreType.DMA((2, 2))],
+        compiler_params=params(60),
         cost_estimate=FREE,
         name="relay",
-    )(keep, from_last, from_next)
+    )(own, got, from_last, from_next)
 
 
 def finish_kernel(here_ref, own_ref, got_ref, early_ref, late_ref, xw_ref, stat_ref, gain_ref, out_ref):
@@ -732,8 +751,8 @@
     lifted = [lifted, lax.ppermute(lifted, ("img", "tp"), pairs)]
 
     own_gain = lax.dynamic_slice_in_dim(norm_gain, img * cut, cut, axis=1)
-    acc = multiply(here, stacks[:EARLY], lifted)
-    base, cot = unpack(paired, came, acc)
+    acc, done = multiply(here, stacks[:EARLY], lifted)
+    base, cot = unpack(paired, came, done)
     visual, state, sums = merge(here, own_gain, acc, base, cot, stacks[EARLY:], lifted)
 
     near, turned = add(sums, lax.ppermute(sums, "tp", core_pairs))
@@ -745,9 +764,9 @@
     own, other = backward(here, state, cot, own_gain, stats, stacks, full_width)
     own, other, crossed = lax.optimization_barrier((own, other, crossed))
     got = lax.ppermute(other, "tp", core_pairs)
-    to_next, to_last, keep = pair(own, got, crossed)
+    to_next, to_last = pair(own, got, crossed)
     from_last, from_next = along_x(to_next, 1), along_x(to_last, -1)
-    to_next, to_last = relay(keep, from_last, from_next)
+    to_next, to_last = relay(own, got, from_last, from_next)
     late_last, late_next = along_x(to_next, 1), along_x(to_last, -1)
 
     send = braid(stay, crossed, n_ctx)

time: 174 us -> 178 us (1.023)
  Pallas kernels: 45.5 us -> 52.6 us
  local copies, waits for them, and re-layouts: 11.6 us -> 9.54 us
  waiting for transfers between devices: 61.4 us -> 59.6 us
    pallas_call x2, Pallas kernels: 1.56 us -> 8.35 us  [the longest x1 4.85 us: collect(): pl.pallas_call(collect_kernel, in_specs=[whole()] + [anywhere()] * 3, out...]
    unnamed x50 -> x36, local copies, waits for them, and re-layouts: 9.93 us -> 6.42 us
    pallas_call x1, Pallas kernels: 0.84 us -> 2.81 us  [stack(): pl.pallas_call(stack_kernel, in_specs=[scalars()] + [in_hbm()] * RING, ou...]
  transfers between devices with their start and end apart: 27 -> 27, of which waited for: 12 -> 12; matrix products, arithmetic and copies ran while one was open for 1% -> 2% of each run, Pallas kernels for 20% -> 24%
where the time goes in v17:
time: 178 us; the launch traced here: 177 us
  waiting for transfers between devices  59.6 us (33%)
  starting transfers between devices  53 us (30%)
  Pallas kernels  52.6 us (30%)
  local copies, waits for them, and re-layouts  9.54 us (5%)
    ppermute x7, waiting for transfers between devices, along_x(): return lax.ppermute(array, ('img', 'tp'), pairs)  16.1 us
    ppermute x1, waiting for transfers between devices, shards(): lifted = [lifted, lax.ppermute(lifted, ('img', 'tp'), pairs)]  15.2 us
    all_to_all x1, waiting for transfers between devices, shards(): lax.all_to_all(held.reshape(owners, n_img * capacity, width), ('img', 'ct...  13.9 us
    ppermute x7, starting transfers between devices, along_x(): return lax.ppermute(array, ('img', 'tp'), pairs)  10.9 us
    ppermute x6, starting transfers between devices, along_ctx(): return lax.ppermute(array, ('ctx', 'tp'), pairs)  9.56 us
    pallas_call x1, Pallas kernels, layer_norm(): pl.pallas_call(norm_kernel, grid_spec=pltpu.PrefetchScalarGridSpec(num_sc...  7.64 us
    pallas_call x2, Pallas kernels, finish(): pl.pallas_call(finish_kernel, grid_spec=pltpu.PrefetchScalarGridSpec(num_...  7.21 us
    all_to_all x1, starting transfers between devices, shards(): lax.all_to_all(packed.reshape(owners, capacity), ('img', 'ctx'), split_ax...  7.1 us
  transfers between devices with their start and end apart: 27, of which 12 were waited for; matrix products, arithmetic and copies ran while one was open for 2% of the time, Pallas kernels for 24%

profile of v17, /device:TPU:1, one launch (start us, length us, event | category | flops | bytes accessed | tf_op | source)
XLA Modules:
  0.0 177.0 jit_solution(4654230035671291578)
XLA Ops:
  0.7 1.0 copy-done
  1.7 2.5 %collective-permute-start = (bf16[288,512]{1,0:T(8,128)(2,1)S(1)}, bf16[288,512]{1,0:T(8,128)(2,1)S(1)}, u32[]{:S(2)}, u32[]{:S(2)}) collective-permute-start(bf16[288,512]{1,0:T(8,128)(2,1)S(1)} %bitcast.21), channel_id=1, source_target_pairs={{0,4},{1,17},{2,6},{3,19},{4,8},{5,21},{6,10},{7,23},{8,12},{9,25}... | collective-permute-start | bytes 884744 | tf_op jit(solution)/shard_map/ppermute | solution.py:705
  4.3 2.2 %collective-permute-start.1 = (bf16[288,512]{1,0:T(8,128)(2,1)S(1)}, bf16[288,512]{1,0:T(8,128)(2,1)}, u32[]{:S(2)}, u32[]{:S(2)}) collective-permute-start(bf16[288,512]{1,0:T(8,128)(2,1)S(1)} %bitcast.22), channel_id=1, source_target_pairs={{0,12},{1,49},{2,14},{3,51},{4,0},{5,53},{6,2},{7,55},{8,4},{9,57}... | collective-permute-start | bytes 884744 | tf_op jit(solution)/shard_map/ppermute | solution.py:705
  6.5 1.2 collective-permute-start.2
  9.5 7.1 %all-to-all-start = ((s32[32,1,16]{2,1,0:T(1,128)}), s32[32,1,16]{2,1,0:T(1,128)}, u32[]{:S(2)}, u32[]{:S(2)}) async-start(s32[32,1,16]{2,1,0:T(1,128)} %bitcast.5), calls=%async_computation | async-start | bytes 32768 | tf_op jit(solution)/shard_map/all_to_all | solution.py:717
  16.6 1.2 collective-permute-start.3
  18.5 7.6 %layer_norm.1 = (bf16[256,4608]{1,0:T(8,128)(2,1)}, bf16[4,256,1152]{2,1,0:T(8,128)(2,1)}, f32[256,128]{1,0:T(8,128)}) custom-call(s32[5]{0:T(128)} %stack.24.here_ref.refs_0_, bf16[1024,1152]{1,0:T(8,128)(2,1)} %bitcast.26, bf16[4,1152]{1,0:T(4,128)(2,1)} %bitcast.29, bf16[4,1152]{1,0:T(4,128)(2,1)} %bitcast.33), custom_call_target="tpu_custom_call" | custom-call | tf_op jit(solution)/shard_map/layer_norm/pallas_call | solution.py:97
  26.2 2.8 %stack.25.refs_0_.after_ref.refs_6_ = bf16[4,288,512]{2,1,0:T(8,128)(2,1)} custom-call(s32[5]{0:T(128)S(1)} %copy-done.10, bf16[288,512]{1,0:T(8,128)(2,1)S(1)} %bitcast.24, bf16[288,512]{1,0:T(8,128)(2,1)S(1)} %collective-permute-done.refs_1_, bf16[288,512]{1,0:T(8,128)(2,1)} %collective-permute-done.1.refs_2_, bf16[288,512]{1,0:T(8,128)(2,1)} %collective-permute-done.2.refs_3_), custom_call_target="tpu_custom_call" | custom-call | tf_op jit(solution)/shard_map/stack/pallas_call | solution.py:210
  29.1 1.6 collective-permute-start.5
  30.7 1.2 collective-permute-start.4
  32.6 0.9 reshape.38.pos_ref
  33.4 4.9 %collect.1 = bf16[2,512,1024]{2,1,0:T(8,128)(2,1)} custom-call(s32[512,1]{1,0:T(8,128)} %reshape.38.pos_ref, bf16[512,1024]{1,0:T(8,128)(2,1)} %stream_ref.1, bf16[512,1024]{1,0:T(8,128)(2,1)} %bitcast.28, bf16[4,288,512]{2,1,0:T(8,128)(2,1)} %stack.25.refs_0_.after_ref.refs_6_), custom_call_target="tpu_custom_call" | custom-call | tf_op jit(solution)/shard_map/collect/pallas_call | solution.py:156
  38.3 6.6 %all-to-all-start.1 = ((bf16[32,32,1024]{2,1,0:T(8,128)(2,1)}), bf16[32,32,1024]{2,1,0:T(8,128)(2,1)}, u32[]{:S(2)}, u32[]{:S(2)}) async-start(bf16[32,32,1024]{2,1,0:T(8,128)(2,1)} %bitcast.25), calls=%async_computation.1 | async-start | bytes 4194304 | tf_op jit(solution)/shard_map/all_to_all | solution.py:738
  44.9 2.4 %collective-permute-start.6 = (bf16[4,288,512]{2,1,0:T(8,128)(2,1)}, bf16[4,288,512]{2,1,0:T(8,128)(2,1)}, u32[]{:S(2)}, u32[]{:S(2)}) collective-permute-start(bf16[4,288,512]{2,1,0:T(8,128)(2,1)} %stack.25.refs_0_.after_ref.refs_6_), channel_id=1, source_target_pairs={{0,48},{1,13},{2,50},{3,15},{4,52},{5,1},{6,54},{7,3},{8,56},{9,5}... | collective-permute-start | bytes 3538952 | tf_op jit(solution)/shard_map/ppermute | solution.py:705
  47.8 15.2 %collective-permute-done.5.refs_3_ = bf16[256,4608]{1,0:T(8,128)(2,1)} collective-permute-done((bf16[256,4608]{1,0:T(8,128)(2,1)S(1)}, bf16[256,4608]{1,0:T(8,128)(2,1)}, u32[]{:S(2)}, u32[]{:S(2)}) %collective-permute-start.5) | collective-permute-done | bytes 2359328 | tf_op jit(solution)/shard_map/ppermute | solution.py:751
  62.9 5.5 %multiply.1 = (f32[512,512]{1,0:T(8,128)}, f32[8,128]{1,0:T(8,128)}) custom-call(s32[5]{0:T(128)} %stack.24.here_ref.refs_0_, bf16[4,288,512]{2,1,0:T(8,128)(2,1)} %stack.25.refs_0_.after_ref.refs_6_, bf16[4,288,512]{2,1,0:T(8,128)(2,1)} %collective-permute-done.4.refs_1_.refs_7_, bf16[256,4608]{1,0:T(8,128)(2,1)} %get-tuple-element.51.refs_2_, ...), custom_call_target="tpu_custom_call" | custom-call | tf_op jit(solution)/shard_map/multiply/pallas_call | solution.py:290
  68.5 13.9 %all-to-all-done.1 = bf16[32,32,1024]{2,1,0:T(8,128)(2,1)} async-done(((bf16[32,32,1024]{2,1,0:T(8,128)(2,1)}), bf16[32,32,1024]{2,1,0:T(8,128)(2,1)}, u32[]{:S(2)}, u32[]{:S(2)}) %all-to-all-start.1) | async-done | bytes 2097184 | tf_op jit(solution)/shard_map/all_to_all | solution.py:738
  83.0 2.9 %unpack.1 = (bf16[512,512]{1,0:T(8,128)(2,1)S(1)}, bf16[512,512]{1,0:T(8,128)(2,1)S(1)}) custom-call(s32[512,1]{1,0:T(8,128)S(1)} %copy.28.slot_ref, bf16[1024,1024]{1,0:T(8,128)(2,1)} %bitcast.17.came_ref, f32[8,128]{1,0:T(8,128)S(1)} %copy-done.13), custom_call_target="tpu_custom_call" | custom-call | tf_op jit(solution)/shard_map/unpack/pallas_call | solution.py:184
  86.0 1.2 copy-done.9
  87.2 4.6 %merge.1 = (bf16[512,512]{1,0:T(8,128)(2,1)S(1)}, f32[512,512]{1,0:T(8,128)S(1)}, f32[8,512]{1,0:T(8,128)S(1)}) custom-call(s32[5]{0:T(128)S(1)} %copy-done.11, bf16[1,512]{1,0:T(2,128)(2,1)S(1)} %constant_dynamic-slice_fusion.1.ngain_ref.refs_1_, f32[512,512]{1,0:T(8,128)S(1)} %copy-done.9, bf16[512,512]{1,0:T(8,128)(2,1)S(1)} %get-tuple-element.55.base_hbm, ...), custom_call_target="tpu_custom_call" | custom-call | tf_op jit(solution)/shard_map/merge/pallas_call | solution.py:332
  91.9 1.2 collective-permute-done.8.got_ref
  93.1 2.6 %collective-permute-start.10 = (f32[8,512]{1,0:T(8,128)S(1)}, f32[8,512]{1,0:T(8,128)S(1)}, u32[]{:S(2)}, u32[]{:S(2)}) collective-permute-start(f32[8,512]{1,0:T(8,128)S(1)} %get-tuple-element.62.after_ref.refs_2_), channel_id=1, source_target_pairs={{0,2},{1,3},{2,0},{3,1},{64,66},{65,67},{66,64},{67,65},{4,6},{5,7... | collective-permute-start | bytes 49160 | tf_op jit(solution)/shard_map/ppermute | solution.py:693
  95.7 3.3 %collective-permute-start.11 = (f32[8,512]{1,0:T(8,128)S(1)}, f32[8,512]{1,0:T(8,128)S(1)}, u32[]{:S(2)}, u32[]{:S(2)}) collective-permute-start(f32[8,512]{1,0:T(8,128)S(1)} %get-tuple-element.61), channel_id=1, source_target_pairs={{0,66},{1,67},{2,64},{3,65},{64,0},{65,1},{66,2},{67,3},{4,70},{5,... | collective-permute-start | bytes 49160 | tf_op jit(solution)/shard_map/ppermute | solution.py:693
  98.9 1.4 pack.1
  100.4 2.4 %collective-permute-done.9.refs_3_ = f32[8,512]{1,0:T(8,128)S(1)} collective-permute-done((f32[8,512]{1,0:T(8,128)S(1)}, f32[8,512]{1,0:T(8,128)S(1)}, u32[]{:S(2)}, u32[]{:S(2)}) %collective-permute-start.9) | collective-permute-done | bytes 16416 | tf_op jit(solution)/shard_map/ppermute | solution.py:693
  102.7 6.0 %backward.1 = (bf16[256,4608]{1,0:T(8,128)(2,1)S(1)}, bf16[256,4608]{1,0:T(8,128)(2,1)S(1)}) custom-call(s32[5]{0:T(128)S(1)} %copy-done.11, bf16[1,512]{1,0:T(2,128)(2,1)S(1)} %constant_dynamic-slice_fusion.1.ngain_ref.refs_1_, f32[8,512]{1,0:T(8,128)S(1)} %get-tuple-element.62.after_ref.refs_2_, f32[8,512]{1,0:T(8,128)S(1)} %collective-permute-done.9.refs_3_, ...), custom_call_target="tpu_custom_call" | custom-call | tf_op jit(solution)/shard_map/backward/pallas_call | solution.py:468
  108.8 5.4 %collective-permute-done.12.after_ref.crossed_ref = bf16[512,512]{1,0:T(8,128)(2,1)S(1)} collective-permute-done((bf16[512,512]{1,0:T(8,128)(2,1)S(1)}, bf16[512,512]{1,0:T(8,128)(2,1)S(1)}, u32[]{:S(2)}, u32[]{:S(2)}) %collective-permute-start.12) | collective-permute-done | bytes 524320 | tf_op jit(solution)/shard_map/ppermute | solution.py:762
  114.1 3.0 %collective-permute-start.13 = (bf16[256,4608]{1,0:T(8,128)(2,1)S(1)}, bf16[256,4608]{1,0:T(8,128)(2,1)S(1)}, u32[]{:S(2)}, u32[]{:S(2)}) collective-permute-start(bf16[256,4608]{1,0:T(8,128)(2,1)S(1)} %get-tuple-element.71), channel_id=1, source_target_pairs={{0,1},{1,0},{2,3},{3,2},{4,5},{5,4},{6,7},{7,6},{8,9},{9,8},{10,11... | collective-permute-start | bytes 7077896 | tf_op jit(solution)/shard_map/ppermute | solution.py:766
  117.1 4.2 %collective-permute-done.13.got_ref.got_hbm = bf16[256,4608]{1,0:T(8,128)(2,1)S(1)} collective-permute-done((bf16[256,4608]{1,0:T(8,128)(2,1)S(1)}, bf16[256,4608]{1,0:T(8,128)(2,1)S(1)}, u32[]{:S(2)}, u32[]{:S(2)}) %collective-permute-start.13) | collective-permute-done | bytes 2359328 | tf_op jit(solution)/shard_map/ppermute | solution.py:766
  121.5 1.2 copy-done.2
  122.7 2.7 %collective-permute-start.15 = (bf16[64,4608]{1,0:T(8,128)(2,1)S(1)}, bf16[64,4608]{1,0:T(8,128)(2,1)S(1)}, u32[]{:S(2)}, u32[]{:S(2)}) collective-permute-start(bf16[64,4608]{1,0:T(8,128)(2,1)S(1)} %get-tuple-element.74), channel_id=1, source_target_pairs={{0,66},{1,67},{2,64},{3,65},{64,0},{65,1},{66,2},{67,3},{4,70},{5,... | collective-permute-start | bytes 1769480 | tf_op jit(solution)/shard_map/ppermute | solution.py:693
  125.4 1.0 braid.1
  126.4 3.7 %all-to-all-start.2 = ((bf16[16,2,32,512]{3,2,1,0:T(8,128)(2,1)}), bf16[16,2,32,512]{3,2,1,0:T(8,128)(2,1)S(1)}, u32[]{:S(2)}, u32[]{:S(2)}) async-start(bf16[16,2,32,512]{3,2,1,0:T(8,128)(2,1)} %braid.1), calls=%async_computation.2 | async-start | bytes 2097152 | tf_op jit(solution)/shard_map/all_to_all | solution.py:773
  130.1 8.5 %collective-permute-done.14.from_last_ref.early_ref = bf16[64,4608]{1,0:T(8,128)(2,1)} collective-permute-done((bf16[64,4608]{1,0:T(8,128)(2,1)S(1)}, bf16[64,4608]{1,0:T(8,128)(2,1)}, u32[]{:S(2)}, u32[]{:S(2)}) %collective-permute-start.14) | collective-permute-done | bytes 589856 | tf_op jit(solution)/shard_map/ppermute | solution.py:693
  138.6 0.8 copy-done.14
  139.4 3.5 %relay.1 = (bf16[32,4608]{1,0:T(8,128)(2,1)}, bf16[32,4608]{1,0:T(8,128)(2,1)}) custom-call(bf16[256,4608]{1,0:T(8,128)(2,1)} %copy-done.1, bf16[256,4608]{1,0:T(8,128)(2,1)} %copy-done.2, bf16[64,4608]{1,0:T(8,128)(2,1)} %collective-permute-done.14.from_last_ref.early_ref, bf16[64,4608]{1,0:T(8,128)(2,1)} %copy-done.14), custom_call_target="tpu_custom_call" | custom-call | tf_op jit(solution)/shard_map/relay/pallas_call | solution.py:537
  142.9 2.3 %collective-permute-start.16 = (bf16[32,4608]{1,0:T(8,128)(2,1)}, bf16[32,4608]{1,0:T(8,128)(2,1)S(1)}, u32[]{:S(2)}, u32[]{:S(2)}) collective-permute-start(bf16[32,4608]{1,0:T(8,128)(2,1)} %get-tuple-element.75), channel_id=1, source_target_pairs={{0,66},{1,67},{2,64},{3,65},{64,0},{65,1},{66,2},{67,3},{4,70},{5,... | collective-permute-start | bytes 884744 | tf_op jit(solution)/shard_map/ppermute | solution.py:693
  145.2 5.3 %collective-permute-done.16.late_ref = bf16[32,4608]{1,0:T(8,128)(2,1)S(1)} collective-permute-done((bf16[32,4608]{1,0:T(8,128)(2,1)}, bf16[32,4608]{1,0:T(8,128)(2,1)S(1)}, u32[]{:S(2)}, u32[]{:S(2)}) %collective-permute-start.16) | collective-permute-done | bytes 294944 | tf_op jit(solution)/shard_map/ppermute | solution.py:693
  151.2 3.6 %finish.2.refs_1_ = bf16[128,1152]{1,0:T(8,128)(2,1)} custom-call(s32[5]{0:T(128)} %stack.24.here_ref.refs_0_, bf16[256,4608]{1,0:T(8,128)(2,1)} %copy-done.1, bf16[256,4608]{1,0:T(8,128)(2,1)} %copy-done.2, bf16[64,4608]{1,0:T(8,128)(2,1)} %collective-permute-done.14.from_last_ref.early_ref, bf16[32,4608]{1,0:T(8,128)(2,1)} %copy-done.16, ...), custom_call_target="tpu_custom_call" | custom-call | tf_op jit(solution)/shard_map/finish/pallas_call | solution.py:584
  154.8 2.0 %collective-permute-start.17 = (bf16[128,1152]{1,0:T(8,128)(2,1)}, bf16[128,1152]{1,0:T(8,128)(2,1)}, u32[]{:S(2)}, u32[]{:S(2)}) collective-permute-start(bf16[128,1152]{1,0:T(8,128)(2,1)} %finish.2.refs_1_), channel_id=1, source_target_pairs={{0,2},{1,3},{2,0},{3,1},{4,6},{5,7},{6,4},{7,5},{8,10},{9,11},{10,... | collective-permute-start | bytes 884744 | tf_op jit(solution)/shard_map/ppermute | solution.py:780
  157.5 3.6 %finish.3.refs_0_ = bf16[128,1152]{1,0:T(8,128)(2,1)} custom-call(s32[5]{0:T(128)} %stack.24.here_ref.refs_0_, bf16[256,4608]{1,0:T(8,128)(2,1)} %copy-done.1, bf16[256,4608]{1,0:T(8,128)(2,1)} %copy-done.2, bf16[64,4608]{1,0:T(8,128)(2,1)} %copy-done.14, bf16[32,4608]{1,0:T(8,128)(2,1)} %copy-done.15, bf16[4,256,1152]{2,1,0:T(8,128)(2,1)} %get-tuple-element.76.xw_ref, ...), custom_call_target="tpu_custom_call" | custom-call | tf_op jit(solution)/shard_map/finish/pallas_call | solution.py:584
  161.1 1.0 collective-permute-start.19
  162.2 2.4 %place.1 = bf16[512,1024]{1,0:T(8,128)(2,1)} custom-call(s32[5]{0:T(128)S(1)} %copy-done.12, s32[512,1]{1,0:T(8,128)S(1)} %copy-done.6, bf16[16,2,32,512]{3,2,1,0:T(8,128)(2,1)S(1)} %all-to-all-done.2.came_ref, bf16[512,1024]{1,0:T(8,128)(2,1)S(1)} %copy-done.5), custom_call_target="tpu_custom_call" | custom-call | tf_op jit(solution)/shard_map/place/pallas_call | solution.py:625
  164.6 2.8 %collective-permute-start.20 = (bf16[128,1152]{1,0:T(8,128)(2,1)S(1)}, bf16[128,1152]{1,0:T(8,128)(2,1)S(1)}, u32[]{:S(2)}, u32[]{:S(2)}) collective-permute-start(bf16[128,1152]{1,0:T(8,128)(2,1)S(1)} %copy-done.8), channel_id=1, source_target_pairs={{0,1},{1,0},{2,3},{3,2},{4,5},{5,4},{6,7},{7,6},{8,9},{9,8},{10,11... | collective-permute-start | bytes 884744 | tf_op jit(solution)/shard_map/ppermute | solution.py:782
  167.5 1.6 collective-permute-done.19.refs_2_
  169.1 3.3 %collective-permute-start.22 = (bf16[128,1152]{1,0:T(8,128)(2,1)}, bf16[128,1152]{1,0:T(8,128)(2,1)S(1)}, u32[]{:S(2)}, u32[]{:S(2)}) collective-permute-start(bf16[128,1152]{1,0:T(8,128)(2,1)} %collective-permute-done.19.refs_2_), channel_id=1, source_target_pairs={{0,1},{1,0},{2,3},{3,2},{4,5},{5,4},{6,7},{7,6},{8,9},{9,8},{10,11... | collective-permute-start | bytes 884744 | tf_op jit(solution)/shard_map/ppermute | solution.py:782
  172.4 1.4 collective-permute-done.22.refs_6_
  174.3 2.5 %lay.1 = bf16[1024,1152]{1,0:T(8,128)(2,1)} custom-call(s32[5]{0:T(128)S(1)} %copy-done.12, bf16[128,1152]{1,0:T(8,128)(2,1)S(1)} %copy-done.8, bf16[128,1152]{1,0:T(8,128)(2,1)S(1)} %copy-done.7, bf16[128,1152]{1,0:T(8,128)(2,1)} %collective-permute-done.19.refs_2_, bf16[128,1152]{1,0:T(8,128)(2,1)} %collective-permute-done.17.refs_3_, ...), custom_call_target="tpu_custom_call" | custom-call | tf_op jit(solution)/shard_map/lay/pallas_call | solution.py:653
  (71 shorter events, 6.7 us)
Async XLA Ops:
  0.6 1.1 copy-start
  1.7 24.5 %collective-permute-start = (bf16[288,512]{1,0:T(8,128)(2,1)S(1)}, bf16[288,512]{1,0:T(8,128)(2,1)S(1)}, u32[]{:S(2)}, u32[]{:S(2)}) collective-permute-start(bf16[288,512]{1,0:T(8,128)(2,1)S(1)} %bitcast.21), channel_id=1, source_target_pairs={{0,4},{1,17},{2,6},{3,19},{4,8},{5,21},{6,10},{7,23},{8,12},{9,25}... | collective-permute-start | bytes 884744 | tf_op jit(solution)/shard_map/ppermute | solution.py:705
  4.3 21.9 %collective-permute-start.1 = (bf16[288,512]{1,0:T(8,128)(2,1)S(1)}, bf16[288,512]{1,0:T(8,128)(2,1)}, u32[]{:S(2)}, u32[]{:S(2)}) collective-permute-start(bf16[288,512]{1,0:T(8,128)(2,1)S(1)} %bitcast.22), channel_id=1, source_target_pairs={{0,12},{1,49},{2,14},{3,51},{4,0},{5,53},{6,2},{7,55},{8,4},{9,57}... | collective-permute-start | bytes 884744 | tf_op jit(solution)/shard_map/ppermute | solution.py:705
  6.5 19.8 %collective-permute-start.2 = (bf16[288,512]{1,0:T(8,128)(2,1)S(1)}, bf16[288,512]{1,0:T(8,128)(2,1)}, u32[]{:S(2)}, u32[]{:S(2)}) collective-permute-start(bf16[288,512]{1,0:T(8,128)(2,1)S(1)} %bitcast.23), channel_id=1, source_target_pairs={{0,8},{1,33},{2,10},{3,35},{4,12},{5,37},{6,14},{7,39},{8,0},{9,41... | collective-permute-start | bytes 884744 | tf_op jit(solution)/shard_map/ppermute | solution.py:705
  9.5 16.7 %all-to-all-start = ((s32[32,1,16]{2,1,0:T(1,128)}), s32[32,1,16]{2,1,0:T(1,128)}, u32[]{:S(2)}, u32[]{:S(2)}) async-start(s32[32,1,16]{2,1,0:T(1,128)} %bitcast.5), calls=%async_computation | async-start | bytes 32768 | tf_op jit(solution)/shard_map/all_to_all | solution.py:717
  16.6 9.6 %collective-permute-start.3 = (s32[256]{0:T(256)S(1)}, s32[256]{0:T(256)S(1)}, u32[]{:S(2)}, u32[]{:S(2)}) collective-permute-start(s32[256]{0:T(256)S(1)} %get-tuple-element.84), channel_id=1, source_target_pairs={{0,64},{64,0},{1,65},{65,1},{2,66},{66,2},{3,67},{67,3},{4,68},{68... | collective-permute-start | bytes 3080 | tf_op jit(solution)/shard_map/ppermute | solution.py:724
  18.5 7.7 %copy-start.10 = (s32[5]{0:T(128)S(1)}, s32[5]{0:T(128)}, u32[]{:S(2)}) copy-start(s32[5]{0:T(128)} %stack.24.here_ref.refs_0_) | copy-start | bytes 64
  26.2 2.9 %copy-start.3 = (bf16[256,4608]{1,0:T(8,128)(2,1)S(1)}, bf16[256,4608]{1,0:T(8,128)(2,1)}, u32[]{:S(2)}) copy-start(bf16[256,4608]{1,0:T(8,128)(2,1)} %get-tuple-element.51.refs_2_) | copy-start | bytes 7077892
  29.1 33.9 %collective-permute-start.5 = (bf16[256,4608]{1,0:T(8,128)(2,1)S(1)}, bf16[256,4608]{1,0:T(8,128)(2,1)}, u32[]{:S(2)}, u32[]{:S(2)}) collective-permute-start(bf16[256,4608]{1,0:T(8,128)(2,1)S(1)} %copy-done.3), channel_id=1, source_target_pairs={{0,64},{1,67},{2,66},{3,65},{64,2},{65,1},{66,0},{67,3},{4,68},{5,... | collective-permute-start | bytes 7077896 | tf_op jit(solution)/shard_map/ppermute | solution.py:751
  30.7 16.9 %collective-permute-start.4 = (bf16[4,288,512]{2,1,0:T(8,128)(2,1)}, bf16[4,288,512]{2,1,0:T(8,128)(2,1)}, u32[]{:S(2)}, u32[]{:S(2)}) collective-permute-start(bf16[4,288,512]{2,1,0:T(8,128)(2,1)} %stack.25.refs_0_.after_ref.refs_6_), channel_id=1, source_target_pairs={{0,16},{1,5},{2,18},{3,7},{4,20},{5,9},{6,22},{7,11},{8,24},{9,13}... | collective-permute-start | bytes 3538952 | tf_op jit(solution)/shard_map/ppermute | solution.py:705
  38.3 9.3 %copy-start.17 = (bf16[1,1024]{1,0:T(2,128)(2,1)S(1)}, bf16[1,1024]{1,0:T(2,128)(2,1)}, u32[]{:S(2)}) copy-start(bf16[1,1024]{1,0:T(2,128)(2,1)} %param.13) | copy-start | bytes 6148
  38.3 44.0 %all-to-all-start.1 = ((bf16[32,32,1024]{2,1,0:T(8,128)(2,1)}), bf16[32,32,1024]{2,1,0:T(8,128)(2,1)}, u32[]{:S(2)}, u32[]{:S(2)}) async-start(bf16[32,32,1024]{2,1,0:T(8,128)(2,1)} %bitcast.25), calls=%async_computation.1 | async-start | bytes 4194304 | tf_op jit(solution)/shard_map/all_to_all | solution.py:738
  44.9 41.0 %collective-permute-start.6 = (bf16[4,288,512]{2,1,0:T(8,128)(2,1)}, bf16[4,288,512]{2,1,0:T(8,128)(2,1)}, u32[]{:S(2)}, u32[]{:S(2)}) collective-permute-start(bf16[4,288,512]{2,1,0:T(8,128)(2,1)} %stack.25.refs_0_.after_ref.refs_6_), channel_id=1, source_target_pairs={{0,48},{1,13},{2,50},{3,15},{4,52},{5,1},{6,54},{7,3},{8,56},{9,5}... | collective-permute-start | bytes 3538952 | tf_op jit(solution)/shard_map/ppermute | solution.py:705
  47.6 38.4 %collective-permute-start.7 = (bf16[4,288,512]{2,1,0:T(8,128)(2,1)}, bf16[4,288,512]{2,1,0:T(8,128)(2,1)}, u32[]{:S(2)}, u32[]{:S(2)}) collective-permute-start(bf16[4,288,512]{2,1,0:T(8,128)(2,1)} %collective-permute-done.4.refs_1_.refs_7_), channel_id=1, source_target_pairs={{0,16},{1,5},{2,18},{3,7},{4,20},{5,9},{6,22},{7,11},{8,24},{9,13}... | collective-permute-start | bytes 3538952 | tf_op jit(solution)/shard_map/ppermute | solution.py:705
  68.5 17.5 %copy-start.4 = (bf16[256,4608]{1,0:T(8,128)(2,1)S(1)}, bf16[256,4608]{1,0:T(8,128)(2,1)}, u32[]{:S(2)}) copy-start(bf16[256,4608]{1,0:T(8,128)(2,1)} %get-tuple-element.51.refs_2_) | copy-start | bytes 7077892
  68.5 17.5 %copy-start.11 = (s32[5]{0:T(128)S(1)}, s32[5]{0:T(128)}, u32[]{:S(2)}) copy-start(s32[5]{0:T(128)} %stack.24.here_ref.refs_0_) | copy-start | bytes 64
  82.4 0.7 copy-start.13
  86.0 1.2 copy-start.9
  91.8 1.3 collective-permute-start.8
  93.1 7.3 %collective-permute-start.10 = (f32[8,512]{1,0:T(8,128)S(1)}, f32[8,512]{1,0:T(8,128)S(1)}, u32[]{:S(2)}, u32[]{:S(2)}) collective-permute-start(f32[8,512]{1,0:T(8,128)S(1)} %get-tuple-element.62.after_ref.refs_2_), channel_id=1, source_target_pairs={{0,2},{1,3},{2,0},{3,1},{64,66},{65,67},{66,64},{67,65},{4,6},{5,7... | collective-permute-start | bytes 49160 | tf_op jit(solution)/shard_map/ppermute | solution.py:693
  95.7 4.7 %collective-permute-start.11 = (f32[8,512]{1,0:T(8,128)S(1)}, f32[8,512]{1,0:T(8,128)S(1)}, u32[]{:S(2)}, u32[]{:S(2)}) collective-permute-start(f32[8,512]{1,0:T(8,128)S(1)} %get-tuple-element.61), channel_id=1, source_target_pairs={{0,66},{1,67},{2,64},{3,65},{64,0},{65,1},{66,2},{67,3},{4,70},{5,... | collective-permute-start | bytes 49160 | tf_op jit(solution)/shard_map/ppermute | solution.py:693
  98.9 3.8 %collective-permute-start.9 = (f32[8,512]{1,0:T(8,128)S(1)}, f32[8,512]{1,0:T(8,128)S(1)}, u32[]{:S(2)}, u32[]{:S(2)}) collective-permute-start(f32[8,512]{1,0:T(8,128)S(1)} %get-tuple-element.61), channel_id=1, source_target_pairs={{0,64},{1,65},{2,66},{3,67},{64,2},{65,3},{66,0},{67,1},{4,68},{5,... | collective-permute-start | bytes 49160 | tf_op jit(solution)/shard_map/ppermute | solution.py:693
  102.7 11.4 %collective-permute-start.12 = (bf16[512,512]{1,0:T(8,128)(2,1)S(1)}, bf16[512,512]{1,0:T(8,128)(2,1)S(1)}, u32[]{:S(2)}, u32[]{:S(2)}) collective-permute-start(bf16[512,512]{1,0:T(8,128)(2,1)S(1)} %get-tuple-element.69), channel_id=1, source_target_pairs={{0,64},{64,0},{1,65},{65,1},{2,66},{66,2},{3,67},{67,3},{4,68},{68... | collective-permute-start | bytes 1572872 | tf_op jit(solution)/shard_map/ppermute | solution.py:762
  108.7 12.8 %copy-start.1 = (bf16[256,4608]{1,0:T(8,128)(2,1)}, bf16[256,4608]{1,0:T(8,128)(2,1)S(1)}, u32[]{:S(2)}) copy-start(bf16[256,4608]{1,0:T(8,128)(2,1)S(1)} %get-tuple-element.70.own_ref.own_hbm) | copy-start | bytes 7077892
  114.1 7.1 %collective-permute-start.13 = (bf16[256,4608]{1,0:T(8,128)(2,1)S(1)}, bf16[256,4608]{1,0:T(8,128)(2,1)S(1)}, u32[]{:S(2)}, u32[]{:S(2)}) collective-permute-start(bf16[256,4608]{1,0:T(8,128)(2,1)S(1)} %get-tuple-element.71), channel_id=1, source_target_pairs={{0,1},{1,0},{2,3},{3,2},{4,5},{5,4},{6,7},{7,6},{8,9},{9,8},{10,11... | collective-permute-start | bytes 7077896 | tf_op jit(solution)/shard_map/ppermute | solution.py:766
  121.2 1.4 copy-start.2
  122.7 15.9 %collective-permute-start.14 = (bf16[64,4608]{1,0:T(8,128)(2,1)S(1)}, bf16[64,4608]{1,0:T(8,128)(2,1)}, u32[]{:S(2)}, u32[]{:S(2)}) collective-permute-start(bf16[64,4608]{1,0:T(8,128)(2,1)S(1)} %get-tuple-element.73), channel_id=1, source_target_pairs={{0,64},{1,65},{2,66},{3,67},{64,2},{65,3},{66,0},{67,1},{4,68},{5,... | collective-permute-start | bytes 1769480 | tf_op jit(solution)/shard_map/ppermute | solution.py:693
  122.7 15.9 %collective-permute-start.15 = (bf16[64,4608]{1,0:T(8,128)(2,1)S(1)}, bf16[64,4608]{1,0:T(8,128)(2,1)S(1)}, u32[]{:S(2)}, u32[]{:S(2)}) collective-permute-start(bf16[64,4608]{1,0:T(8,128)(2,1)S(1)} %get-tuple-element.74), channel_id=1, source_target_pairs={{0,66},{1,67},{2,64},{3,65},{64,0},{65,1},{66,2},{67,3},{4,70},{5,... | collective-permute-start | bytes 1769480 | tf_op jit(solution)/shard_map/ppermute | solution.py:693
  126.4 35.8 %all-to-all-start.2 = ((bf16[16,2,32,512]{3,2,1,0:T(8,128)(2,1)}), bf16[16,2,32,512]{3,2,1,0:T(8,128)(2,1)S(1)}, u32[]{:S(2)}, u32[]{:S(2)}) async-start(bf16[16,2,32,512]{3,2,1,0:T(8,128)(2,1)} %braid.1), calls=%async_computation.2 | async-start | bytes 2097152 | tf_op jit(solution)/shard_map/all_to_all | solution.py:773
  138.6 0.8 copy-start.14
  142.9 7.6 %collective-permute-start.16 = (bf16[32,4608]{1,0:T(8,128)(2,1)}, bf16[32,4608]{1,0:T(8,128)(2,1)S(1)}, u32[]{:S(2)}, u32[]{:S(2)}) collective-permute-start(bf16[32,4608]{1,0:T(8,128)(2,1)} %get-tuple-element.75), channel_id=1, source_target_pairs={{0,66},{1,67},{2,64},{3,65},{64,0},{65,1},{66,2},{67,3},{4,70},{5,... | collective-permute-start | bytes 884744 | tf_op jit(solution)/shard_map/ppermute | solution.py:693
  145.2 11.6 %collective-permute-start.18 = (bf16[32,4608]{1,0:T(8,128)(2,1)}, bf16[32,4608]{1,0:T(8,128)(2,1)S(1)}, u32[]{:S(2)}, u32[]{:S(2)}) collective-permute-start(bf16[32,4608]{1,0:T(8,128)(2,1)} %get-tuple-element.80), channel_id=1, source_target_pairs={{0,64},{1,65},{2,66},{3,67},{64,2},{65,3},{66,0},{67,1},{4,68},{5,... | collective-permute-start | bytes 884744 | tf_op jit(solution)/shard_map/ppermute | solution.py:693
  150.5 0.7 copy-start.16
  154.8 7.4 %copy-start.5 = (bf16[512,1024]{1,0:T(8,128)(2,1)S(1)}, bf16[512,1024]{1,0:T(8,128)(2,1)}, u32[]{:S(2)}) copy-start(bf16[512,1024]{1,0:T(8,128)(2,1)} %stream_ref.1) | copy-start | bytes 3145732
  154.8 7.4 %copy-start.6 = (s32[512,1]{1,0:T(8,128)S(1)}, s32[512,1]{1,0:T(8,128)}, u32[]{:S(2)}) copy-start(s32[512,1]{1,0:T(8,128)} %reshape.38.pos_ref) | copy-start | bytes 6148
  154.8 7.4 %copy-start.12 = (s32[5]{0:T(128)S(1)}, s32[5]{0:T(128)}, u32[]{:S(2)}) copy-start(s32[5]{0:T(128)} %stack.24.here_ref.refs_0_) | copy-start | bytes 64
  154.8 12.7 %collective-permute-start.17 = (bf16[128,1152]{1,0:T(8,128)(2,1)}, bf16[128,1152]{1,0:T(8,128)(2,1)}, u32[]{:S(2)}, u32[]{:S(2)}) collective-permute-start(bf16[128,1152]{1,0:T(8,128)(2,1)} %finish.2.refs_1_), channel_id=1, source_target_pairs={{0,2},{1,3},{2,0},{3,1},{4,6},{5,7},{6,4},{7,5},{8,10},{9,11},{10,... | collective-permute-start | bytes 884744 | tf_op jit(solution)/shard_map/ppermute | solution.py:780
  156.8 0.7 copy-start.15
  161.1 3.4 %copy-start.8 = (bf16[128,1152]{1,0:T(8,128)(2,1)S(1)}, bf16[128,1152]{1,0:T(8,128)(2,1)}, u32[]{:S(2)}) copy-start(bf16[128,1152]{1,0:T(8,128)(2,1)} %finish.3.refs_0_) | copy-start | bytes 884740
  161.1 6.3 %copy-start.7 = (bf16[128,1152]{1,0:T(8,128)(2,1)S(1)}, bf16[128,1152]{1,0:T(8,128)(2,1)}, u32[]{:S(2)}) copy-start(bf16[128,1152]{1,0:T(8,128)(2,1)} %finish.2.refs_1_) | copy-start | bytes 884740
  161.1 8.0 %collective-permute-start.19 = (bf16[128,1152]{1,0:T(8,128)(2,1)}, bf16[128,1152]{1,0:T(8,128)(2,1)}, u32[]{:S(2)}, u32[]{:S(2)}) collective-permute-start(bf16[128,1152]{1,0:T(8,128)(2,1)} %finish.3.refs_0_), channel_id=1, source_target_pairs={{0,2},{1,3},{2,0},{3,1},{4,6},{5,7},{6,4},{7,5},{8,10},{9,11},{10,... | collective-permute-start | bytes 884744 | tf_op jit(solution)/shard_map/ppermute | solution.py:780
  164.6 7.9 %collective-permute-start.20 = (bf16[128,1152]{1,0:T(8,128)(2,1)S(1)}, bf16[128,1152]{1,0:T(8,128)(2,1)S(1)}, u32[]{:S(2)}, u32[]{:S(2)}) collective-permute-start(bf16[128,1152]{1,0:T(8,128)(2,1)S(1)} %copy-done.8), channel_id=1, source_target_pairs={{0,1},{1,0},{2,3},{3,2},{4,5},{5,4},{6,7},{7,6},{8,9},{9,8},{10,11... | collective-permute-start | bytes 884744 | tf_op jit(solution)/shard_map/ppermute | solution.py:782
  167.4 5.0 %collective-permute-start.21 = (bf16[128,1152]{1,0:T(8,128)(2,1)S(1)}, bf16[128,1152]{1,0:T(8,128)(2,1)S(1)}, u32[]{:S(2)}, u32[]{:S(2)}) collective-permute-start(bf16[128,1152]{1,0:T(8,128)(2,1)S(1)} %copy-done.7), channel_id=1, source_target_pairs={{0,1},{1,0},{2,3},{3,2},{4,5},{5,4},{6,7},{7,6},{8,9},{9,8},{10,11... | collective-permute-start | bytes 884744 | tf_op jit(solution)/shard_map/ppermute | solution.py:782
  169.1 4.7 %collective-permute-start.22 = (bf16[128,1152]{1,0:T(8,128)(2,1)}, bf16[128,1152]{1,0:T(8,128)(2,1)S(1)}, u32[]{:S(2)}, u32[]{:S(2)}) collective-permute-start(bf16[128,1152]{1,0:T(8,128)(2,1)} %collective-permute-done.19.refs_2_), channel_id=1, source_target_pairs={{0,1},{1,0},{2,3},{3,2},{4,5},{5,4},{6,7},{7,6},{8,9},{9,8},{10,11... | collective-permute-start | bytes 884744 | tf_op jit(solution)/shard_map/ppermute | solution.py:782
  172.4 1.8 %collective-permute-start.23 = (bf16[128,1152]{1,0:T(8,128)(2,1)}, bf16[128,1152]{1,0:T(8,128)(2,1)S(1)}, u32[]{:S(2)}, u32[]{:S(2)}) collective-permute-start(bf16[128,1152]{1,0:T(8,128)(2,1)} %collective-permute-done.17.refs_3_), channel_id=1, source_target_pairs={{0,1},{1,0},{2,3},{3,2},{4,5},{5,4},{6,7},{7,6},{8,9},{9,8},{10,11... | collective-permute-start | bytes 884744 | tf_op jit(solution)/shard_map/ppermute | solution.py:782

commit v18 on v16

--- a/solution.py
+++ b/solution.py
@@ -468,23 +468,18 @@
     )(here, ngain, *stats, *stacks, state, cot)
 
 
-def pair_kernel(own_ref, got_ref, after_ref, next_ref, last_ref, keep_hbm, keep_ref, sem):
+def both(own_ref, got_ref, start, count):
+    at = slice(start, start + count)
+    return (own_ref[at, :].astype(F32) + got_ref[at, :].astype(F32)).astype(BF)
+
+
+def pair_kernel(own_ref, got_ref, after_ref, next_ref, last_ref):
     rows = own_ref.shape[0] // RING
     half = rows // 2
-
-    def total(start):
-        at = slice(start, start + half)
-        return (own_ref[at, :].astype(F32) + got_ref[at, :].astype(F32)).astype(BF)
-
-    keep_ref[:half] = total(rows)
-    keep_ref[half:] = total(3 * rows + half)
-    copy = pltpu.make_async_copy(keep_ref, keep_hbm, sem)
-    copy.start()
-    next_ref[:half] = total(2 * rows)
-    next_ref[half:] = total(rows + half)
-    last_ref[:half] = total(2 * rows + half)
-    last_ref[half:] = total(3 * rows)
-    copy.wait()
+    next_ref[:half] = both(own_ref, got_ref, 2 * rows, half)
+    next_ref[half:] = both(own_ref, got_ref, rows + half, half)
+    last_ref[:half] = both(own_ref, got_ref, 2 * rows + half, half)
+    last_ref[half:] = both(own_ref, got_ref, 3 * rows, half)
 
 
 def pair(own, got, after):
@@ -492,39 +487,36 @@
     return pl.pallas_call(
         pair_kernel,
         in_specs=[whole()] * 2 + [anywhere()],
-        out_specs=[whole()] * 2 + [anywhere()],
-        out_shape=[shape((rows, depth), BF)] * 3,
-        scratch_shapes=[pltpu.VMEM((rows, depth), BF), pltpu.SemaphoreType.DMA],
+        out_specs=[whole()] * 2,
+        out_shape=[shape((rows, depth), BF)] * 2,
         compiler_params=params(8),
         cost_estimate=FREE,
         name="pair",
     )(own, got, after)
 
 
-def relay_kernel(keep_hbm, from_last_ref, from_next_ref, next_ref, last_ref, keep_ref, sem):
-    copy = pltpu.make_async_copy(keep_hbm, keep_ref, sem)
-    copy.start()
-    copy.wait()
+def relay_kernel(own_ref, got_ref, from_last_ref, from_next_ref, next_ref, last_ref):
     half = next_ref.shape[0]
-    for at, came_ref, out_ref in (
-        (slice(0, half), from_last_ref, next_ref),
-        (slice(half, 2 * half), from_next_ref, last_ref),
+    rows = 2 * half
+    for start, came_ref, out_ref in (
+        (rows, from_last_ref, next_ref),
+        (3 * rows + half, from_next_ref, last_ref),
     ):
-        out_ref[...] = (keep_ref[at, :].astype(F32) + came_ref[:half].astype(F32)).astype(BF)
-
-
-def relay(keep, from_last, from_next):
-    rows, depth = keep.shape
+        kept = both(own_ref, got_ref, start, half).astype(F32)
+        out_ref[...] = (kept + came_ref[:half].astype(F32)).astype(BF)
+
+
+def relay(own, got, from_last, from_next):
+    rows, depth = from_last.shape
     return pl.pallas_call(
         relay_kernel,
-        in_specs=[in_hbm()] + [whole()] * 2,
+        in_specs=[whole()] * 4,
         out_specs=[whole()] * 2,
         out_shape=[shape((rows // 2, depth), BF)] * 2,
-        scratch_shapes=[pltpu.VMEM((rows, depth), BF), pltpu.SemaphoreType.DMA],
         compiler_params=params(8),
         cost_estimate=FREE,
         name="relay",
-    )(keep, from_last, from_next)
+    )(own, got, from_last, from_next)
 
 
 def finish_kernel(here_ref, own_ref, got_ref, early_ref, late_ref, xw_ref, stat_ref, gain_ref, out_ref):
@@ -576,7 +568,7 @@
             out_specs=pl.BlockSpec((tokens * window, width), lambda i, h: (0, 0)),
         ),
         out_shape=shape((tokens * window, width), BF),
-        compiler_params=params(58),
+        compiler_params=params(12),
         cost_estimate=FREE,
         name="finish",
     )(here, own, got, early, late, xw, stat, gain)
@@ -745,9 +737,9 @@
     own, other = backward(here, state, cot, own_gain, stats, stacks, full_width)
     own, other, crossed = lax.optimization_barrier((own, other, crossed))
     got = lax.ppermute(other, "tp", core_pairs)
-    to_next, to_last, keep = pair(own, got, crossed)
+    to_next, to_last = pair(own, got, crossed)
     from_last, from_next = along_x(to_next, 1), along_x(to_last, -1)
-    to_next, to_last = relay(keep, from_last, from_next)
+    to_next, to_last = relay(own, got, from_last, from_next)
     late_last, late_next = along_x(to_next, 1), along_x(to_last, -1)
 
     send = braid(stay, crossed, n_ctx)

time: 174 us -> 173 us (level)
    unnamed x50 -> x42, local copies, waits for them, and re-layouts: 9.93 us -> 10.4 us
where the time goes in v18:
time: 173 us; the launch traced here: 172 us
  waiting for transfers between devices  60.3 us (35%)
  starting transfers between devices  53 us (31%)
  Pallas kernels  44.5 us (26%)
  local copies, waits for them, and re-layouts  12.1 us (7%)
    ppermute x1, waiting for transfers between devices, shards(): lifted = [lifted, lax.ppermute(lifted, ('img', 'tp'), pairs)]  16.9 us
    ppermute x7, waiting for transfers between devices, along_x(): return lax.ppermute(array, ('img', 'tp'), pairs)  15.2 us
    all_to_all x1, waiting for transfers between devices, shards(): lax.all_to_all(held.reshape(owners, n_img * capacity, width), ('img', 'ct...  12.7 us
    ppermute x7, starting transfers between devices, along_x(): return lax.ppermute(array, ('img', 'tp'), pairs)  10.9 us
    unnamed x42, local copies, waits for them, and re-layouts  10.4 us
    ppermute x6, starting transfers between devices, along_ctx(): return lax.ppermute(array, ('ctx', 'tp'), pairs)  9.65 us
    pallas_call x1, Pallas kernels, layer_norm(): pl.pallas_call(norm_kernel, grid_spec=pltpu.PrefetchScalarGridSpec(num_sc...  7.66 us
    all_to_all x1, starting transfers between devices, shards(): lax.all_to_all(packed.reshape(owners, capacity), ('img', 'ctx'), split_ax...  6.97 us
  transfers between devices with their start and end apart: 27, of which 12 were waited for; matrix products, arithmetic and copies ran while one was open for 1% of the time, Pallas kernels for 20%

profile of v18, /device:TPU:1, one launch (start us, length us, event | category | flops | bytes accessed | tf_op | source)
XLA Modules:
  0.0 172.1 jit_solution(12692695199324865282)
XLA Ops:
  0.7 1.0 copy-done
  1.7 2.5 %collective-permute-start = (bf16[288,512]{1,0:T(8,128)(2,1)S(1)}, bf16[288,512]{1,0:T(8,128)(2,1)S(1)}, u32[]{:S(2)}, u32[]{:S(2)}) collective-permute-start(bf16[288,512]{1,0:T(8,128)(2,1)S(1)} %bitcast.22), channel_id=1, source_target_pairs={{0,4},{1,17},{2,6},{3,19},{4,8},{5,21},{6,10},{7,23},{8,12},{9,25}... | collective-permute-start | bytes 884744 | tf_op jit(solution)/shard_map/ppermute | solution.py:678
  4.3 2.2 %collective-permute-start.1 = (bf16[288,512]{1,0:T(8,128)(2,1)S(1)}, bf16[288,512]{1,0:T(8,128)(2,1)S(1)}, u32[]{:S(2)}, u32[]{:S(2)}) collective-permute-start(bf16[288,512]{1,0:T(8,128)(2,1)S(1)} %bitcast.23), channel_id=1, source_target_pairs={{0,12},{1,49},{2,14},{3,51},{4,0},{5,53},{6,2},{7,55},{8,4},{9,57}... | collective-permute-start | bytes 884744 | tf_op jit(solution)/shard_map/ppermute | solution.py:678
  6.5 1.2 collective-permute-start.2
  9.5 7.0 %all-to-all-start = ((s32[32,1,16]{2,1,0:T(1,128)}), s32[32,1,16]{2,1,0:T(1,128)S(1)}, u32[]{:S(2)}, u32[]{:S(2)}) async-start(s32[32,1,16]{2,1,0:T(1,128)} %bitcast.5), calls=%async_computation | async-start | bytes 32768 | tf_op jit(solution)/shard_map/all_to_all | solution.py:690
  16.5 1.3 collective-permute-start.3
  18.5 7.7 %layer_norm.1 = (bf16[256,4608]{1,0:T(8,128)(2,1)}, bf16[4,256,1152]{2,1,0:T(8,128)(2,1)}, f32[256,128]{1,0:T(8,128)}) custom-call(s32[5]{0:T(128)} %stack.24.here_ref.refs_0_, bf16[1024,1152]{1,0:T(8,128)(2,1)} %bitcast.30, bf16[4,1152]{1,0:T(4,128)(2,1)} %bitcast.27, bf16[4,1152]{1,0:T(4,128)(2,1)} %bitcast.34), custom_call_target="tpu_custom_call" | custom-call | tf_op jit(solution)/shard_map/layer_norm/pallas_call | solution.py:97
  27.0 1.6 collective-permute-start.5
  28.6 1.2 collective-permute-start.4
  30.0 1.2 copy-done.13
  31.2 1.2 copy-done.15
  32.5 1.3 collect.1
  33.8 1.4 copy-done.9
  35.2 6.7 %all-to-all-start.1 = ((bf16[32,32,1024]{2,1,0:T(8,128)(2,1)}), bf16[32,32,1024]{2,1,0:T(8,128)(2,1)}, u32[]{:S(2)}, u32[]{:S(2)}) async-start(bf16[32,32,1024]{2,1,0:T(8,128)(2,1)} %bitcast.21), calls=%async_computation.1 | async-start | bytes 4194304 | tf_op jit(solution)/shard_map/all_to_all | solution.py:711
  41.9 2.4 %collective-permute-start.6 = (bf16[4,288,512]{2,1,0:T(8,128)(2,1)S(1)}, bf16[4,288,512]{2,1,0:T(8,128)(2,1)}, u32[]{:S(2)}, u32[]{:S(2)}) collective-permute-start(bf16[4,288,512]{2,1,0:T(8,128)(2,1)S(1)} %stack.25.refs_0_.after_ref.refs_6_), channel_id=1, source_target_pairs={{0,48},{1,13},{2,50},{3,15},{4,52},{5,1},{6,54},{7,3},{8,56},{9,5}... | collective-permute-start | bytes 3538952 | tf_op jit(solution)/shard_map/ppermute | solution.py:678
  45.5 16.9 %collective-permute-done.5.refs_3_ = bf16[256,4608]{1,0:T(8,128)(2,1)} collective-permute-done((bf16[256,4608]{1,0:T(8,128)(2,1)}, bf16[256,4608]{1,0:T(8,128)(2,1)}, u32[]{:S(2)}, u32[]{:S(2)}) %collective-permute-start.5) | collective-permute-done | bytes 2359328 | tf_op jit(solution)/shard_map/ppermute | solution.py:724
  62.3 5.5 %multiply.1.after_ref.acc_hbm = f32[512,512]{1,0:T(8,128)} custom-call(s32[5]{0:T(128)} %stack.24.here_ref.refs_0_, bf16[4,288,512]{2,1,0:T(8,128)(2,1)} %copy-done.4, bf16[4,288,512]{2,1,0:T(8,128)(2,1)} %copy-done.10, bf16[256,4608]{1,0:T(8,128)(2,1)} %get-tuple-element.49.refs_2_, bf16[256,4608]{1,0:T(8,128)(2,1)} %collective-permute-done.5.refs_3_), custom_call_target="tpu_custom_call" | custom-call | tf_op jit(solution)/shard_map/multiply/pallas_call | solution.py:273
  67.9 12.7 %all-to-all-done.1 = bf16[32,32,1024]{2,1,0:T(8,128)(2,1)} async-done(((bf16[32,32,1024]{2,1,0:T(8,128)(2,1)}), bf16[32,32,1024]{2,1,0:T(8,128)(2,1)}, u32[]{:S(2)}, u32[]{:S(2)}) %all-to-all-start.1) | async-done | bytes 2097184 | tf_op jit(solution)/shard_map/all_to_all | solution.py:711
  80.5 1.2 copy-done.7
  81.8 3.0 %unpack.1 = (bf16[512,512]{1,0:T(8,128)(2,1)S(1)}, bf16[512,512]{1,0:T(8,128)(2,1)S(1)}) custom-call(s32[512,1]{1,0:T(8,128)S(1)} %copy.28.slot_ref, bf16[1024,1024]{1,0:T(8,128)(2,1)} %bitcast.17.came_ref, f32[512,512]{1,0:T(8,128)S(1)} %copy-done.7), custom_call_target="tpu_custom_call" | custom-call | tf_op jit(solution)/shard_map/unpack/pallas_call | solution.py:169
  84.8 5.1 %merge.1 = (bf16[512,512]{1,0:T(8,128)(2,1)S(1)}, f32[512,512]{1,0:T(8,128)S(1)}, f32[8,512]{1,0:T(8,128)S(1)}) custom-call(s32[5]{0:T(128)S(1)} %copy-done.19, bf16[1,512]{1,0:T(2,128)(2,1)S(1)} %constant_dynamic-slice_fusion.1.ngain_ref.refs_1_, f32[512,512]{1,0:T(8,128)S(1)} %copy-done.8, bf16[512,512]{1,0:T(8,128)(2,1)S(1)} %get-tuple-element.51.base_hbm, ...), custom_call_target="tpu_custom_call" | custom-call | tf_op jit(solution)/shard_map/merge/pallas_call | solution.py:315
  90.0 1.2 collective-permute-done.8.got_ref
  91.1 2.6 %collective-permute-start.10 = (f32[8,512]{1,0:T(8,128)S(1)}, f32[8,512]{1,0:T(8,128)S(1)}, u32[]{:S(2)}, u32[]{:S(2)}) collective-permute-start(f32[8,512]{1,0:T(8,128)S(1)} %get-tuple-element.58.after_ref.refs_2_), channel_id=1, source_target_pairs={{0,2},{1,3},{2,0},{3,1},{64,66},{65,67},{66,64},{67,65},{4,6},{5,7... | collective-permute-start | bytes 49160 | tf_op jit(solution)/shard_map/ppermute | solution.py:666
  93.7 3.2 %collective-permute-start.11 = (f32[8,512]{1,0:T(8,128)S(1)}, f32[8,512]{1,0:T(8,128)S(1)}, u32[]{:S(2)}, u32[]{:S(2)}) collective-permute-start(f32[8,512]{1,0:T(8,128)S(1)} %get-tuple-element.57), channel_id=1, source_target_pairs={{0,66},{1,67},{2,64},{3,65},{64,0},{65,1},{66,2},{67,3},{4,70},{5,... | collective-permute-start | bytes 49160 | tf_op jit(solution)/shard_map/ppermute | solution.py:666
  97.0 1.4 pack.1
  98.4 2.4 %collective-permute-done.9.refs_3_ = f32[8,512]{1,0:T(8,128)S(1)} collective-permute-done((f32[8,512]{1,0:T(8,128)S(1)}, f32[8,512]{1,0:T(8,128)S(1)}, u32[]{:S(2)}, u32[]{:S(2)}) %collective-permute-start.9) | collective-permute-done | bytes 16416 | tf_op jit(solution)/shard_map/ppermute | solution.py:666
  100.8 5.5 %backward.1 = (bf16[256,4608]{1,0:T(8,128)(2,1)S(1)}, bf16[256,4608]{1,0:T(8,128)(2,1)S(1)}) custom-call(s32[5]{0:T(128)S(1)} %copy-done.19, bf16[1,512]{1,0:T(2,128)(2,1)S(1)} %constant_dynamic-slice_fusion.1.ngain_ref.refs_1_, f32[8,512]{1,0:T(8,128)S(1)} %get-tuple-element.58.after_ref.refs_2_, f32[8,512]{1,0:T(8,128)S(1)} %collective-permute-done.9.refs_3_, ...), custom_call_target="tpu_custom_call" | custom-call | tf_op jit(solution)/shard_map/backward/pallas_call | solution.py:451
  106.3 5.8 %collective-permute-done.12.after_ref.crossed_ref = bf16[512,512]{1,0:T(8,128)(2,1)S(1)} collective-permute-done((bf16[512,512]{1,0:T(8,128)(2,1)S(1)}, bf16[512,512]{1,0:T(8,128)(2,1)S(1)}, u32[]{:S(2)}, u32[]{:S(2)}) %collective-permute-start.12) | collective-permute-done | bytes 524320 | tf_op jit(solution)/shard_map/ppermute | solution.py:735
  112.1 3.0 %collective-permute-start.13 = (bf16[256,4608]{1,0:T(8,128)(2,1)S(1)}, bf16[256,4608]{1,0:T(8,128)(2,1)S(1)}, u32[]{:S(2)}, u32[]{:S(2)}) collective-permute-start(bf16[256,4608]{1,0:T(8,128)(2,1)S(1)} %get-tuple-element.67), channel_id=1, source_target_pairs={{0,1},{1,0},{2,3},{3,2},{4,5},{5,4},{6,7},{7,6},{8,9},{9,8},{10,11... | collective-permute-start | bytes 7077896 | tf_op jit(solution)/shard_map/ppermute | solution.py:739
  115.1 4.2 %collective-permute-done.13.got_ref = bf16[256,4608]{1,0:T(8,128)(2,1)S(1)} collective-permute-done((bf16[256,4608]{1,0:T(8,128)(2,1)S(1)}, bf16[256,4608]{1,0:T(8,128)(2,1)S(1)}, u32[]{:S(2)}, u32[]{:S(2)}) %collective-permute-start.13) | collective-permute-done | bytes 2359328 | tf_op jit(solution)/shard_map/ppermute | solution.py:739
  119.3 1.4 pair.1
  121.1 2.7 %collective-permute-start.15 = (bf16[64,4608]{1,0:T(8,128)(2,1)}, bf16[64,4608]{1,0:T(8,128)(2,1)}, u32[]{:S(2)}, u32[]{:S(2)}) collective-permute-start(bf16[64,4608]{1,0:T(8,128)(2,1)} %get-tuple-element.70), channel_id=1, source_target_pairs={{0,66},{1,67},{2,64},{3,65},{64,0},{65,1},{66,2},{67,3},{4,70},{5,... | collective-permute-start | bytes 1769480 | tf_op jit(solution)/shard_map/ppermute | solution.py:666
  124.8 4.5 %all-to-all-start.2 = ((bf16[16,2,32,512]{3,2,1,0:T(8,128)(2,1)}), bf16[16,2,32,512]{3,2,1,0:T(8,128)(2,1)}, u32[]{:S(2)}, u32[]{:S(2)}) async-start(bf16[16,2,32,512]{3,2,1,0:T(8,128)(2,1)} %copy-done.12), calls=%async_computation.2 | async-start | bytes 2097152 | tf_op jit(solution)/shard_map/all_to_all | solution.py:746
  129.3 7.9 %collective-permute-done.14.from_last_ref.early_ref = bf16[64,4608]{1,0:T(8,128)(2,1)} collective-permute-done((bf16[64,4608]{1,0:T(8,128)(2,1)}, bf16[64,4608]{1,0:T(8,128)(2,1)}, u32[]{:S(2)}, u32[]{:S(2)}) %collective-permute-start.14) | collective-permute-done | bytes 589856 | tf_op jit(solution)/shard_map/ppermute | solution.py:666
  137.1 1.7 copy-done.2
  138.8 1.7 relay.1
  140.5 2.4 %collective-permute-start.16 = (bf16[32,4608]{1,0:T(8,128)(2,1)S(1)}, bf16[32,4608]{1,0:T(8,128)(2,1)S(1)}, u32[]{:S(2)}, u32[]{:S(2)}) collective-permute-start(bf16[32,4608]{1,0:T(8,128)(2,1)S(1)} %get-tuple-element.71), channel_id=1, source_target_pairs={{0,66},{1,67},{2,64},{3,65},{64,0},{65,1},{66,2},{67,3},{4,70},{5,... | collective-permute-start | bytes 884744 | tf_op jit(solution)/shard_map/ppermute | solution.py:666
  142.9 4.9 %collective-permute-done.16.late_ref = bf16[32,4608]{1,0:T(8,128)(2,1)S(1)} collective-permute-done((bf16[32,4608]{1,0:T(8,128)(2,1)S(1)}, bf16[32,4608]{1,0:T(8,128)(2,1)S(1)}, u32[]{:S(2)}, u32[]{:S(2)}) %collective-permute-start.16) | collective-permute-done | bytes 294944 | tf_op jit(solution)/shard_map/ppermute | solution.py:666
  147.9 2.4 %finish.2.refs_1_ = bf16[128,1152]{1,0:T(8,128)(2,1)S(1)} custom-call(s32[5]{0:T(128)S(1)} %copy-done.19, bf16[256,4608]{1,0:T(8,128)(2,1)S(1)} %get-tuple-element.66.own_ref, bf16[256,4608]{1,0:T(8,128)(2,1)S(1)} %copy-done.3, bf16[64,4608]{1,0:T(8,128)(2,1)} %collective-permute-done.14.from_last_ref.early_ref, ...), custom_call_target="tpu_custom_call" | custom-call | tf_op jit(solution)/shard_map/finish/pallas_call | solution.py:557
  150.3 2.1 %collective-permute-start.17 = (bf16[128,1152]{1,0:T(8,128)(2,1)S(1)}, bf16[128,1152]{1,0:T(8,128)(2,1)}, u32[]{:S(2)}, u32[]{:S(2)}) collective-permute-start(bf16[128,1152]{1,0:T(8,128)(2,1)S(1)} %finish.2.refs_1_), channel_id=1, source_target_pairs={{0,2},{1,3},{2,0},{3,1},{4,6},{5,7},{6,4},{7,5},{8,10},{9,11},{10,... | collective-permute-start | bytes 884744 | tf_op jit(solution)/shard_map/ppermute | solution.py:753
  152.4 3.1 %finish.3.refs_0_ = bf16[128,1152]{1,0:T(8,128)(2,1)} custom-call(s32[5]{0:T(128)S(1)} %copy-done.19, bf16[256,4608]{1,0:T(8,128)(2,1)S(1)} %get-tuple-element.66.own_ref, bf16[256,4608]{1,0:T(8,128)(2,1)S(1)} %copy-done.3, bf16[64,4608]{1,0:T(8,128)(2,1)} %collective-permute-done.15.from_next_ref.early_ref, ...), custom_call_target="tpu_custom_call" | custom-call | tf_op jit(solution)/shard_map/finish/pallas_call | solution.py:557
  156.5 1.2 copy-done.14
  157.7 3.1 %place.1 = bf16[512,1024]{1,0:T(8,128)(2,1)} custom-call(s32[5]{0:T(128)S(1)} %copy-done.19, s32[512,1]{1,0:T(8,128)S(1)} %reshape.38.pos_ref, bf16[16,2,32,512]{3,2,1,0:T(8,128)(2,1)} %all-to-all-done.2.came_ref, bf16[512,1024]{1,0:T(8,128)(2,1)S(1)} %copy-done.14), custom_call_target="tpu_custom_call" | custom-call | tf_op jit(solution)/shard_map/place/pallas_call | solution.py:598
  160.7 2.8 %collective-permute-start.20 = (bf16[128,1152]{1,0:T(8,128)(2,1)}, bf16[128,1152]{1,0:T(8,128)(2,1)S(1)}, u32[]{:S(2)}, u32[]{:S(2)}) collective-permute-start(bf16[128,1152]{1,0:T(8,128)(2,1)} %finish.3.refs_0_), channel_id=1, source_target_pairs={{0,1},{1,0},{2,3},{3,2},{4,5},{5,4},{6,7},{7,6},{8,9},{9,8},{10,11... | collective-permute-start | bytes 884744 | tf_op jit(solution)/shard_map/ppermute | solution.py:755
  163.6 1.6 collective-permute-done.19.refs_2_
  165.2 2.4 %collective-permute-start.22 = (bf16[128,1152]{1,0:T(8,128)(2,1)S(1)}, bf16[128,1152]{1,0:T(8,128)(2,1)S(1)}, u32[]{:S(2)}, u32[]{:S(2)}) collective-permute-start(bf16[128,1152]{1,0:T(8,128)(2,1)S(1)} %collective-permute-done.19.refs_2_), channel_id=1, source_target_pairs={{0,1},{1,0},{2,3},{3,2},{4,5},{5,4},{6,7},{7,6},{8,9},{9,8},{10,11... | collective-permute-start | bytes 884744 | tf_op jit(solution)/shard_map/ppermute | solution.py:755
  167.6 1.6 collective-permute-done.22.refs_6_
  169.5 2.5 %lay.1 = bf16[1024,1152]{1,0:T(8,128)(2,1)} custom-call(s32[5]{0:T(128)S(1)} %copy-done.19, bf16[128,1152]{1,0:T(8,128)(2,1)} %finish.3.refs_0_, bf16[128,1152]{1,0:T(8,128)(2,1)S(1)} %finish.2.refs_1_, bf16[128,1152]{1,0:T(8,128)(2,1)S(1)} %collective-permute-done.19.refs_2_, bf16[128,1152]{1,0:T(8,128)(2,1)} %collective-permute-done.17.refs_3_, ...), custom_call_target="tpu_custom_call" | custom-call | tf_op jit(solution)/shard_map/lay/pallas_call | solution.py:626
  (77 shorter events, 7.4 us)
Async XLA Ops:
  0.6 1.1 copy-start
  1.7 24.4 %collective-permute-start = (bf16[288,512]{1,0:T(8,128)(2,1)S(1)}, bf16[288,512]{1,0:T(8,128)(2,1)S(1)}, u32[]{:S(2)}, u32[]{:S(2)}) collective-permute-start(bf16[288,512]{1,0:T(8,128)(2,1)S(1)} %bitcast.22), channel_id=1, source_target_pairs={{0,4},{1,17},{2,6},{3,19},{4,8},{5,21},{6,10},{7,23},{8,12},{9,25}... | collective-permute-start | bytes 884744 | tf_op jit(solution)/shard_map/ppermute | solution.py:678
  4.3 21.9 %collective-permute-start.1 = (bf16[288,512]{1,0:T(8,128)(2,1)S(1)}, bf16[288,512]{1,0:T(8,128)(2,1)S(1)}, u32[]{:S(2)}, u32[]{:S(2)}) collective-permute-start(bf16[288,512]{1,0:T(8,128)(2,1)S(1)} %bitcast.23), channel_id=1, source_target_pairs={{0,12},{1,49},{2,14},{3,51},{4,0},{5,53},{6,2},{7,55},{8,4},{9,57}... | collective-permute-start | bytes 884744 | tf_op jit(solution)/shard_map/ppermute | solution.py:678
  6.5 19.7 %collective-permute-start.2 = (bf16[288,512]{1,0:T(8,128)(2,1)S(1)}, bf16[288,512]{1,0:T(8,128)(2,1)S(1)}, u32[]{:S(2)}, u32[]{:S(2)}) collective-permute-start(bf16[288,512]{1,0:T(8,128)(2,1)S(1)} %bitcast.24), channel_id=1, source_target_pairs={{0,8},{1,33},{2,10},{3,35},{4,12},{5,37},{6,14},{7,39},{8,0},{9,41... | collective-permute-start | bytes 884744 | tf_op jit(solution)/shard_map/ppermute | solution.py:678
  9.5 16.6 %all-to-all-start = ((s32[32,1,16]{2,1,0:T(1,128)}), s32[32,1,16]{2,1,0:T(1,128)S(1)}, u32[]{:S(2)}, u32[]{:S(2)}) async-start(s32[32,1,16]{2,1,0:T(1,128)} %bitcast.5), calls=%async_computation | async-start | bytes 32768 | tf_op jit(solution)/shard_map/all_to_all | solution.py:690
  16.5 9.6 %collective-permute-start.3 = (s32[256]{0:T(256)S(1)}, s32[256]{0:T(256)S(1)}, u32[]{:S(2)}, u32[]{:S(2)}) collective-permute-start(s32[256]{0:T(256)S(1)} %get-tuple-element.80), channel_id=1, source_target_pairs={{0,64},{64,0},{1,65},{65,1},{2,66},{66,2},{3,67},{67,3},{4,68},{68... | collective-permute-start | bytes 3080 | tf_op jit(solution)/shard_map/ppermute | solution.py:697
  18.5 7.7 %copy-start.18 = (s32[5]{0:T(128)S(1)}, s32[5]{0:T(128)}, u32[]{:S(2)}) copy-start(s32[5]{0:T(128)} %stack.24.here_ref.refs_0_) | copy-start | bytes 64
  27.0 14.9 %copy-start.4 = (bf16[4,288,512]{2,1,0:T(8,128)(2,1)}, bf16[4,288,512]{2,1,0:T(8,128)(2,1)S(1)}, u32[]{:S(2)}) copy-start(bf16[4,288,512]{2,1,0:T(8,128)(2,1)S(1)} %stack.25.refs_0_.after_ref.refs_6_) | copy-start | bytes 3538948
  27.0 35.3 %collective-permute-start.5 = (bf16[256,4608]{1,0:T(8,128)(2,1)}, bf16[256,4608]{1,0:T(8,128)(2,1)}, u32[]{:S(2)}, u32[]{:S(2)}) collective-permute-start(bf16[256,4608]{1,0:T(8,128)(2,1)} %get-tuple-element.49.refs_2_), channel_id=1, source_target_pairs={{0,64},{1,67},{2,66},{3,65},{64,2},{65,1},{66,0},{67,3},{4,68},{5,... | collective-permute-start | bytes 7077896 | tf_op jit(solution)/shard_map/ppermute | solution.py:724
  28.6 16.7 %collective-permute-start.4 = (bf16[4,288,512]{2,1,0:T(8,128)(2,1)S(1)}, bf16[4,288,512]{2,1,0:T(8,128)(2,1)S(1)}, u32[]{:S(2)}, u32[]{:S(2)}) collective-permute-start(bf16[4,288,512]{2,1,0:T(8,128)(2,1)S(1)} %stack.25.refs_0_.after_ref.refs_6_), channel_id=1, source_target_pairs={{0,16},{1,5},{2,18},{3,7},{4,20},{5,9},{6,22},{7,11},{8,24},{9,13}... | collective-permute-start | bytes 3538952 | tf_op jit(solution)/shard_map/ppermute | solution.py:678
  30.0 1.2 copy-start.13
  31.2 1.2 copy-start.15
  33.8 1.4 copy-start.9
  35.2 10.1 %copy-start.20 = (bf16[1,1024]{1,0:T(2,128)(2,1)S(1)}, bf16[1,1024]{1,0:T(2,128)(2,1)}, u32[]{:S(2)}) copy-start(bf16[1,1024]{1,0:T(2,128)(2,1)} %param.13) | copy-start | bytes 6148
  35.2 45.4 %all-to-all-start.1 = ((bf16[32,32,1024]{2,1,0:T(8,128)(2,1)}), bf16[32,32,1024]{2,1,0:T(8,128)(2,1)}, u32[]{:S(2)}, u32[]{:S(2)}) async-start(bf16[32,32,1024]{2,1,0:T(8,128)(2,1)} %bitcast.21), calls=%async_computation.1 | async-start | bytes 4194304 | tf_op jit(solution)/shard_map/all_to_all | solution.py:711
  41.9 42.8 %collective-permute-start.6 = (bf16[4,288,512]{2,1,0:T(8,128)(2,1)S(1)}, bf16[4,288,512]{2,1,0:T(8,128)(2,1)}, u32[]{:S(2)}, u32[]{:S(2)}) collective-permute-start(bf16[4,288,512]{2,1,0:T(8,128)(2,1)S(1)} %stack.25.refs_0_.after_ref.refs_6_), channel_id=1, source_target_pairs={{0,48},{1,13},{2,50},{3,15},{4,52},{5,1},{6,54},{7,3},{8,56},{9,5}... | collective-permute-start | bytes 3538952 | tf_op jit(solution)/shard_map/ppermute | solution.py:678
  45.3 17.1 %copy-start.10 = (bf16[4,288,512]{2,1,0:T(8,128)(2,1)}, bf16[4,288,512]{2,1,0:T(8,128)(2,1)S(1)}, u32[]{:S(2)}) copy-start(bf16[4,288,512]{2,1,0:T(8,128)(2,1)S(1)} %collective-permute-done.4.refs_1_.refs_7_) | copy-start | bytes 3538948
  45.3 39.5 %collective-permute-start.7 = (bf16[4,288,512]{2,1,0:T(8,128)(2,1)S(1)}, bf16[4,288,512]{2,1,0:T(8,128)(2,1)}, u32[]{:S(2)}, u32[]{:S(2)}) collective-permute-start(bf16[4,288,512]{2,1,0:T(8,128)(2,1)S(1)} %collective-permute-done.4.refs_1_.refs_7_), channel_id=1, source_target_pairs={{0,16},{1,5},{2,18},{3,7},{4,20},{5,9},{6,22},{7,11},{8,24},{9,13}... | collective-permute-start | bytes 3538952 | tf_op jit(solution)/shard_map/ppermute | solution.py:678
  67.9 16.9 %copy-start.19 = (s32[5]{0:T(128)S(1)}, s32[5]{0:T(128)}, u32[]{:S(2)}) copy-start(s32[5]{0:T(128)} %stack.24.here_ref.refs_0_) | copy-start | bytes 64
  80.5 1.2 copy-start.7
  81.8 3.0 %copy-start.8 = (f32[512,512]{1,0:T(8,128)S(1)}, f32[512,512]{1,0:T(8,128)}, u32[]{:S(2)}) copy-start(f32[512,512]{1,0:T(8,128)} %multiply.1.after_ref.acc_hbm) | copy-start | bytes 3145732
  84.8 16.0 %copy-start.5 = (bf16[4,288,512]{2,1,0:T(8,128)(2,1)S(1)}, bf16[4,288,512]{2,1,0:T(8,128)(2,1)}, u32[]{:S(2)}) copy-start(bf16[4,288,512]{2,1,0:T(8,128)(2,1)} %copy-done.4) | copy-start | bytes 3538948
  84.8 16.0 %copy-start.11 = (bf16[4,288,512]{2,1,0:T(8,128)(2,1)S(1)}, bf16[4,288,512]{2,1,0:T(8,128)(2,1)}, u32[]{:S(2)}) copy-start(bf16[4,288,512]{2,1,0:T(8,128)(2,1)} %copy-done.10) | copy-start | bytes 3538948
  89.9 1.3 collective-permute-start.8
  91.1 7.2 %collective-permute-start.10 = (f32[8,512]{1,0:T(8,128)S(1)}, f32[8,512]{1,0:T(8,128)S(1)}, u32[]{:S(2)}, u32[]{:S(2)}) collective-permute-start(f32[8,512]{1,0:T(8,128)S(1)} %get-tuple-element.58.after_ref.refs_2_), channel_id=1, source_target_pairs={{0,2},{1,3},{2,0},{3,1},{64,66},{65,67},{66,64},{67,65},{4,6},{5,7... | collective-permute-start | bytes 49160 | tf_op jit(solution)/shard_map/ppermute | solution.py:666
  93.7 4.6 %collective-permute-start.11 = (f32[8,512]{1,0:T(8,128)S(1)}, f32[8,512]{1,0:T(8,128)S(1)}, u32[]{:S(2)}, u32[]{:S(2)}) collective-permute-start(f32[8,512]{1,0:T(8,128)S(1)} %get-tuple-element.57), channel_id=1, source_target_pairs={{0,66},{1,67},{2,64},{3,65},{64,0},{65,1},{66,2},{67,3},{4,70},{5,... | collective-permute-start | bytes 49160 | tf_op jit(solution)/shard_map/ppermute | solution.py:666
  97.0 3.8 %collective-permute-start.9 = (f32[8,512]{1,0:T(8,128)S(1)}, f32[8,512]{1,0:T(8,128)S(1)}, u32[]{:S(2)}, u32[]{:S(2)}) collective-permute-start(f32[8,512]{1,0:T(8,128)S(1)} %get-tuple-element.57), channel_id=1, source_target_pairs={{0,64},{1,65},{2,66},{3,67},{64,2},{65,3},{66,0},{67,1},{4,68},{5,... | collective-permute-start | bytes 49160 | tf_op jit(solution)/shard_map/ppermute | solution.py:666
  100.8 11.4 %collective-permute-start.12 = (bf16[512,512]{1,0:T(8,128)(2,1)S(1)}, bf16[512,512]{1,0:T(8,128)(2,1)S(1)}, u32[]{:S(2)}, u32[]{:S(2)}) collective-permute-start(bf16[512,512]{1,0:T(8,128)(2,1)S(1)} %get-tuple-element.65), channel_id=1, source_target_pairs={{0,64},{64,0},{1,65},{65,1},{2,66},{66,2},{3,67},{67,3},{4,68},{68... | collective-permute-start | bytes 1572872 | tf_op jit(solution)/shard_map/ppermute | solution.py:735
  112.1 7.1 %collective-permute-start.13 = (bf16[256,4608]{1,0:T(8,128)(2,1)S(1)}, bf16[256,4608]{1,0:T(8,128)(2,1)S(1)}, u32[]{:S(2)}, u32[]{:S(2)}) collective-permute-start(bf16[256,4608]{1,0:T(8,128)(2,1)S(1)} %get-tuple-element.67), channel_id=1, source_target_pairs={{0,1},{1,0},{2,3},{3,2},{4,5},{5,4},{6,7},{7,6},{8,9},{9,8},{10,11... | collective-permute-start | bytes 7077896 | tf_op jit(solution)/shard_map/ppermute | solution.py:739
  119.3 1.8 %copy-start.1 = (bf16[256,4608]{1,0:T(8,128)(2,1)}, bf16[256,4608]{1,0:T(8,128)(2,1)S(1)}, u32[]{:S(2)}) copy-start(bf16[256,4608]{1,0:T(8,128)(2,1)S(1)} %collective-permute-done.13.got_ref) | copy-start | bytes 7077892
  121.1 16.1 %collective-permute-start.14 = (bf16[64,4608]{1,0:T(8,128)(2,1)}, bf16[64,4608]{1,0:T(8,128)(2,1)}, u32[]{:S(2)}, u32[]{:S(2)}) collective-permute-start(bf16[64,4608]{1,0:T(8,128)(2,1)} %get-tuple-element.69), channel_id=1, source_target_pairs={{0,64},{1,65},{2,66},{3,67},{64,2},{65,3},{66,0},{67,1},{4,68},{5,... | collective-permute-start | bytes 1769480 | tf_op jit(solution)/shard_map/ppermute | solution.py:666
  121.1 16.1 %collective-permute-start.15 = (bf16[64,4608]{1,0:T(8,128)(2,1)}, bf16[64,4608]{1,0:T(8,128)(2,1)}, u32[]{:S(2)}, u32[]{:S(2)}) collective-permute-start(bf16[64,4608]{1,0:T(8,128)(2,1)} %get-tuple-element.70), channel_id=1, source_target_pairs={{0,66},{1,67},{2,64},{3,65},{64,0},{65,1},{66,2},{67,3},{4,70},{5,... | collective-permute-start | bytes 1769480 | tf_op jit(solution)/shard_map/ppermute | solution.py:666
  123.8 1.0 copy-start.12
  124.8 23.1 %copy-start.17 = (bf16[1,4,1152]{2,1,0:T(4,128)(2,1)S(1)}, bf16[1,4,1152]{2,1,0:T(4,128)(2,1)}, u32[]{:S(2)}) copy-start(bf16[1,4,1152]{2,1,0:T(4,128)(2,1)} %param.9) | copy-start | bytes 27652
  124.8 31.7 %all-to-all-start.2 = ((bf16[16,2,32,512]{3,2,1,0:T(8,128)(2,1)}), bf16[16,2,32,512]{3,2,1,0:T(8,128)(2,1)}, u32[]{:S(2)}, u32[]{:S(2)}) async-start(bf16[16,2,32,512]{3,2,1,0:T(8,128)(2,1)} %copy-done.12), calls=%async_computation.2 | async-start | bytes 2097152 | tf_op jit(solution)/shard_map/all_to_all | solution.py:746
  137.1 1.7 copy-start.2
  138.8 9.0 %copy-start.3 = (bf16[256,4608]{1,0:T(8,128)(2,1)S(1)}, bf16[256,4608]{1,0:T(8,128)(2,1)}, u32[]{:S(2)}) copy-start(bf16[256,4608]{1,0:T(8,128)(2,1)} %copy-done.1) | copy-start | bytes 7077892
  138.8 9.0 %copy-start.6 = (bf16[4,256,1152]{2,1,0:T(8,128)(2,1)S(1)}, bf16[4,256,1152]{2,1,0:T(8,128)(2,1)}, u32[]{:S(2)}) copy-start(bf16[4,256,1152]{2,1,0:T(8,128)(2,1)} %get-tuple-element.72.xw_ref) | copy-start | bytes 7077892
  138.8 9.0 %copy-start.16 = (f32[256,128]{1,0:T(8,128)S(1)}, f32[256,128]{1,0:T(8,128)}, u32[]{:S(2)}) copy-start(f32[256,128]{1,0:T(8,128)} %get-tuple-element.73.stat_ref) | copy-start | bytes 393220
  140.5 7.4 %collective-permute-start.16 = (bf16[32,4608]{1,0:T(8,128)(2,1)S(1)}, bf16[32,4608]{1,0:T(8,128)(2,1)S(1)}, u32[]{:S(2)}, u32[]{:S(2)}) collective-permute-start(bf16[32,4608]{1,0:T(8,128)(2,1)S(1)} %get-tuple-element.71), channel_id=1, source_target_pairs={{0,66},{1,67},{2,64},{3,65},{64,0},{65,1},{66,2},{67,3},{4,70},{5,... | collective-permute-start | bytes 884744 | tf_op jit(solution)/shard_map/ppermute | solution.py:666
  142.9 9.5 %collective-permute-start.18 = (bf16[32,4608]{1,0:T(8,128)(2,1)S(1)}, bf16[32,4608]{1,0:T(8,128)(2,1)S(1)}, u32[]{:S(2)}, u32[]{:S(2)}) collective-permute-start(bf16[32,4608]{1,0:T(8,128)(2,1)S(1)} %get-tuple-element.76), channel_id=1, source_target_pairs={{0,64},{1,65},{2,66},{3,67},{64,2},{65,3},{66,0},{67,1},{4,68},{5,... | collective-permute-start | bytes 884744 | tf_op jit(solution)/shard_map/ppermute | solution.py:666
  150.3 13.3 %collective-permute-start.17 = (bf16[128,1152]{1,0:T(8,128)(2,1)S(1)}, bf16[128,1152]{1,0:T(8,128)(2,1)}, u32[]{:S(2)}, u32[]{:S(2)}) collective-permute-start(bf16[128,1152]{1,0:T(8,128)(2,1)S(1)} %finish.2.refs_1_), channel_id=1, source_target_pairs={{0,2},{1,3},{2,0},{3,1},{4,6},{5,7},{6,4},{7,5},{8,10},{9,11},{10,... | collective-permute-start | bytes 884744 | tf_op jit(solution)/shard_map/ppermute | solution.py:753
  155.5 9.7 %collective-permute-start.19 = (bf16[128,1152]{1,0:T(8,128)(2,1)}, bf16[128,1152]{1,0:T(8,128)(2,1)S(1)}, u32[]{:S(2)}, u32[]{:S(2)}) collective-permute-start(bf16[128,1152]{1,0:T(8,128)(2,1)} %finish.3.refs_0_), channel_id=1, source_target_pairs={{0,2},{1,3},{2,0},{3,1},{4,6},{5,7},{6,4},{7,5},{8,10},{9,11},{10,... | collective-permute-start | bytes 884744 | tf_op jit(solution)/shard_map/ppermute | solution.py:753
  156.5 1.2 copy-start.14
  160.7 6.9 %collective-permute-start.20 = (bf16[128,1152]{1,0:T(8,128)(2,1)}, bf16[128,1152]{1,0:T(8,128)(2,1)S(1)}, u32[]{:S(2)}, u32[]{:S(2)}) collective-permute-start(bf16[128,1152]{1,0:T(8,128)(2,1)} %finish.3.refs_0_), channel_id=1, source_target_pairs={{0,1},{1,0},{2,3},{3,2},{4,5},{5,4},{6,7},{7,6},{8,9},{9,8},{10,11... | collective-permute-start | bytes 884744 | tf_op jit(solution)/shard_map/ppermute | solution.py:755
  163.6 4.1 %collective-permute-start.21 = (bf16[128,1152]{1,0:T(8,128)(2,1)S(1)}, bf16[128,1152]{1,0:T(8,128)(2,1)S(1)}, u32[]{:S(2)}, u32[]{:S(2)}) collective-permute-start(bf16[128,1152]{1,0:T(8,128)(2,1)S(1)} %finish.2.refs_1_), channel_id=1, source_target_pairs={{0,1},{1,0},{2,3},{3,2},{4,5},{5,4},{6,7},{7,6},{8,9},{9,8},{10,11... | collective-permute-start | bytes 884744 | tf_op jit(solution)/shard_map/ppermute | solution.py:755
  165.2 4.0 %collective-permute-start.22 = (bf16[128,1152]{1,0:T(8,128)(2,1)S(1)}, bf16[128,1152]{1,0:T(8,128)(2,1)S(1)}, u32[]{:S(2)}, u32[]{:S(2)}) collective-permute-start(bf16[128,1152]{1,0:T(8,128)(2,1)S(1)} %collective-permute-done.19.refs_2_), channel_id=1, source_target_pairs={{0,1},{1,0},{2,3},{3,2},{4,5},{5,4},{6,7},{7,6},{8,9},{9,8},{10,11... | collective-permute-start | bytes 884744 | tf_op jit(solution)/shard_map/ppermute | solution.py:755
  167.6 1.8 %collective-permute-start.23 = (bf16[128,1152]{1,0:T(8,128)(2,1)}, bf16[128,1152]{1,0:T(8,128)(2,1)S(1)}, u32[]{:S(2)}, u32[]{:S(2)}) collective-permute-start(bf16[128,1152]{1,0:T(8,128)(2,1)} %collective-permute-done.17.refs_3_), channel_id=1, source_target_pairs={{0,1},{1,0},{2,3},{3,2},{4,5},{5,4},{6,7},{7,6},{8,9},{9,8},{10,11... | collective-permute-start | bytes 884744 | tf_op jit(solution)/shard_map/ppermute | solution.py:755

commit v19 on v18

--- a/solution.py
+++ b/solution.py
@@ -151,32 +151,6 @@
     )(pos, stream, cot, after)
 
 
-def unpack_kernel(slot_ref, came_ref, after_ref, base_ref, cot_ref):
-    tokens, width = base_ref.shape
-    slots = came_ref.shape[0]
-    take = eq_hot((tokens, slots), 1, slot_ref[...])
-    for start, out_ref in ((0, base_ref), (width, cot_ref)):
-        out_ref[...] = jnp.dot(
-            take, came_ref[:, start : start + width], preferred_element_type=F32
-        ).astype(BF)
-
-
-def unpack(slot_col, came, after):
-    tokens = slot_col.shape[0]
-    slots, both = came.shape
-    width = both // 2
-    outs = [shape((tokens, width), BF)] * 2
-    return pl.pallas_call(
-        unpack_kernel,
-        in_specs=[whole()] * 2 + [anywhere()],
-        out_specs=[whole()] * 2,
-        out_shape=outs,
-        compiler_params=params(12),
-        cost_estimate=FREE,
-        name="unpack",
-    )(slot_col, came, after)
-
-
 def stack_kernel(here_ref, *refs):
     out_ref, sems = refs[RING:]
     first = jnp.where(here_ref[0] == 0, here_ref[4], here_ref[3])
@@ -198,7 +172,7 @@
         out_specs=whole(),
         out_shape=shape((RING, rows, width), BF),
         scratch_shapes=[pltpu.SemaphoreType.DMA((RING,))],
-        compiler_params=params(6),
+        compiler_params=params(60),
         cost_estimate=FREE,
         name="stack",
     )(here, *blocks)
@@ -282,24 +256,29 @@
     )(here, *stacks, *lifted)
 
 
-def merge_kernel(here_ref, ngain_ref, acc_hbm, base_hbm, cot_hbm, *refs):
+def merge_kernel(here_ref, ngain_ref, slot_ref, acc_hbm, came_hbm, *refs):
     stacks, lifted, refs = refs[: RING - EARLY], refs[RING - EARLY : RING - EARLY + 2], refs[RING - EARLY + 2 :]
-    visual_ref, state_ref, stat_ref, acc_ref, base_ref, cot_ref, row_sems, *scratch = refs
+    visual_ref, state_ref, cot_ref, stat_ref, acc_ref, came_ref, row_sems, *scratch = refs
     run = product(here_ref, AWAY[EARLY:], stacks, lifted, *scratch)
     copies = [
         pltpu.make_async_copy(a, b, row_sems.at[i])
-        for i, (a, b) in enumerate(((acc_hbm, acc_ref), (base_hbm, base_ref), (cot_hbm, cot_ref)))
+        for i, (a, b) in enumerate(((came_hbm, came_ref), (acc_hbm, acc_ref)))
     ]
     for copy in copies:
         copy.start()
+    tokens, width = cot_ref.shape
+    take = eq_hot((tokens, came_ref.shape[0]), 1, slot_ref[...])
     total = run(None)
     for copy in copies:
         copy.wait()
+    base = jnp.dot(take, came_ref[:, :width], preferred_element_type=F32)
+    cot = jnp.dot(take, came_ref[:, width:], preferred_element_type=F32)
+    cot_ref[...] = cot.astype(BF)
     visual = (acc_ref[...] + total).astype(BF)
     visual_ref[...] = visual
-    state = base_ref[...].astype(F32) + visual.astype(F32)
+    state = base + visual.astype(F32)
     state_ref[...] = state
-    up = ngain_ref[...].astype(F32) * cot_ref[...].astype(F32)
+    up = ngain_ref[...].astype(F32) * cot
     lane = lax.broadcasted_iota(jnp.int32, (state.shape[0], 128), 1)
     sums = jnp.where(
         lane == 0,
@@ -309,25 +288,29 @@
     stat_ref[...] = sums.T[: stat_ref.shape[0]]
 
 
-def merge(here, ngain, acc, base, cot, stacks, lifted):
-    tokens, width = base.shape
-    outs = [shape((tokens, width), BF), shape((tokens, width), F32), shape((8, tokens), F32)]
+def merge(here, ngain, slot_col, acc, came, stacks, lifted):
+    tokens, width = acc.shape
+    outs = [
+        shape((tokens, width), BF),
+        shape((tokens, width), F32),
+        shape((tokens, width), BF),
+        shape((8, tokens), F32),
+    ]
     return pl.pallas_call(
         merge_kernel,
-        in_specs=[scalars(), whole()] + [in_hbm()] * (3 + len(stacks) + len(lifted)),
-        out_specs=[whole()] * 3,
+        in_specs=[scalars()] + [whole()] * 2 + [in_hbm()] * (2 + len(stacks) + len(lifted)),
+        out_specs=[whole()] * 4,
         out_shape=outs,
         scratch_shapes=[
             pltpu.VMEM((tokens, width), F32),
-            pltpu.VMEM((tokens, width), BF),
-            pltpu.VMEM((tokens, width), BF),
-            pltpu.SemaphoreType.DMA((3,)),
+            pltpu.VMEM(came.shape, BF),
+            pltpu.SemaphoreType.DMA((2,)),
         ]
         + product_scratch(stacks, lifted),
-        compiler_params=params(24),
+        compiler_params=params(28),
         cost_estimate=FREE,
         name="merge",
-    )(here, ngain, acc, base, cot, *stacks, *lifted)
+    )(here, ngain, slot_col, acc, came, *stacks, *lifted)
 
 
 def add_kernel(sums_ref, got_ref, near_ref, turned_ref):
@@ -725,8 +708,7 @@
 
     own_gain = lax.dynamic_slice_in_dim(norm_gain, img * cut, cut, axis=1)
     acc = multiply(here, stacks[:EARLY], lifted)
-    base, cot = unpack(paired, came, acc)
-    visual, state, sums = merge(here, own_gain, acc, base, cot, stacks[EARLY:], lifted)
+    visual, state, cot, sums = merge(here, own_gain, paired, acc, came, stacks[EARLY:], lifted)
 
     near, turned = add(sums, lax.ppermute(sums, "tp", core_pairs))
     stats = [near] + [along_x(near if by == 2 else turned, by) for by in (1, 2, 3)]

time: 173 us -> 173 us (level)
  waiting for transfers between devices: 60.3 us -> 55.2 us
  starting transfers between devices: 53 us -> 57.6 us
    ppermute x6, waiting for transfers between devices: 0.92 us -> 15.4 us  [along_ctx(): return lax.ppermute(array, ('ctx', 'tp'), pairs)]
    all_to_all x1, waiting for transfers between devices: 12.7 us -> 0.78 us  [shards(): lax.all_to_all(held.reshape(owners, n_img * capacity, width), ('img', 'ct...]
    ppermute x7, waiting for transfers between devices: 15.2 us -> 12 us  [along_x(): return lax.ppermute(array, ('img', 'tp'), pairs)]
    ppermute x1, starting transfers between devices: 0.09 us -> 3.03 us  [shards(): near, turned = add(sums, lax.ppermute(sums, 'tp', core_pairs))]
    pallas_call x2 -> x1, Pallas kernels: 8.04 us -> 5.9 us  [merge(): pl.pallas_call(merge_kernel, in_specs=[scalars()] + [whole()] * 2 + [in_h...]
    pallas_call x1, Pallas kernels: 0.84 us -> 2.99 us  [stack(): pl.pallas_call(stack_kernel, in_specs=[scalars()] + [in_hbm()] * RING, ou...]
    unnamed x42 -> x44, local copies, waits for them, and re-layouts: 10.4 us -> 11.2 us
  transfers between devices with their start and end apart: 27 -> 27, of which waited for: 12 -> 13; matrix products, arithmetic and copies ran while one was open for 1% -> 1% of each run, Pallas kernels for 20% -> 18%
where the time goes in v19:
time: 173 us; the launch traced here: 172 us
  starting transfers between devices  57.6 us (33%)
  waiting for transfers between devices  55.2 us (32%)
  Pallas kernels  44.4 us (26%)
  local copies, waits for them, and re-layouts  12.9 us (7%)
    ppermute x1, waiting for transfers between devices, shards(): lifted = [lifted, lax.ppermute(lifted, ('img', 'tp'), pairs)]  15.5 us
    ppermute x6, waiting for transfers between devices, along_ctx(): return lax.ppermute(array, ('ctx', 'tp'), pairs)  15.4 us
    ppermute x7, waiting for transfers between devices, along_x(): return lax.ppermute(array, ('img', 'tp'), pairs)  12 us
    unnamed x44, local copies, waits for them, and re-layouts  11.2 us
    ppermute x7, starting transfers between devices, along_x(): return lax.ppermute(array, ('img', 'tp'), pairs)  10.3 us
    ppermute x6, starting transfers between devices, along_ctx(): return lax.ppermute(array, ('ctx', 'tp'), pairs)  9.6 us
    pallas_call x1, Pallas kernels, layer_norm(): pl.pallas_call(norm_kernel, grid_spec=pltpu.PrefetchScalarGridSpec(num_sc...  7.66 us
    all_to_all x1, starting transfers between devices, shards(): lax.all_to_all(held.reshape(owners, n_img * capacity, width), ('img', 'ct...  6.78 us
  transfers between devices with their start and end apart: 27, of which 13 were waited for; matrix products, arithmetic and copies ran while one was open for 1% of the time, Pallas kernels for 18%

profile of v19, /device:TPU:1, one launch (start us, length us, event | category | flops | bytes accessed | tf_op | source)
XLA Modules:
  0.0 172.4 jit_solution(16415679877744935510)
XLA Ops:
  0.7 1.0 copy-done
  1.7 4.5 %collective-permute-start.2 = (bf16[288,512]{1,0:T(8,128)(2,1)S(1)}, bf16[288,512]{1,0:T(8,128)(2,1)S(1)}, u32[]{:S(2)}, u32[]{:S(2)}) collective-permute-start(bf16[288,512]{1,0:T(8,128)(2,1)S(1)} %bitcast.28), channel_id=1, source_target_pairs={{0,8},{1,33},{2,10},{3,35},{4,12},{5,37},{6,14},{7,39},{8,0},{9,41... | collective-permute-start | bytes 884744 | tf_op jit(solution)/shard_map/ppermute | solution.py:661
  6.7 1.0 collective-permute-start
  8.7 1.3 collective-permute-start.3
  10.8 5.9 %all-to-all-start = ((s32[32,1,16]{2,1,0:T(1,128)}), s32[32,1,16]{2,1,0:T(1,128)S(1)}, u32[]{:S(2)}, u32[]{:S(2)}) async-start(s32[32,1,16]{2,1,0:T(1,128)} %bitcast.5), calls=%async_computation | async-start | bytes 32768 | tf_op jit(solution)/shard_map/all_to_all | solution.py:673
  17.5 7.7 %layer_norm.1 = (bf16[256,4608]{1,0:T(8,128)(2,1)}, bf16[4,256,1152]{2,1,0:T(8,128)(2,1)}, f32[256,128]{1,0:T(8,128)}) custom-call(s32[5]{0:T(128)} %stack.24.here_ref.refs_0_, bf16[1024,1152]{1,0:T(8,128)(2,1)} %bitcast.26, bf16[4,1152]{1,0:T(4,128)(2,1)} %bitcast.23, bf16[4,1152]{1,0:T(4,128)(2,1)} %bitcast.34), custom_call_target="tpu_custom_call" | custom-call | tf_op jit(solution)/shard_map/layer_norm/pallas_call | solution.py:97
  25.9 3.0 %stack.25.refs_0_.after_ref.refs_6_ = bf16[4,288,512]{2,1,0:T(8,128)(2,1)} custom-call(s32[5]{0:T(128)} %stack.24.here_ref.refs_0_, bf16[288,512]{1,0:T(8,128)(2,1)} %bitcast.31, bf16[288,512]{1,0:T(8,128)(2,1)} %collective-permute-done.refs_1_, bf16[288,512]{1,0:T(8,128)(2,1)} %collective-permute-done.1.refs_2_, bf16[288,512]{1,0:T(8,128)(2,1)} %copy-done.20), custom_call_target="tpu_custom_call" | custom-call | tf_op jit(solution)/shard_map/stack/pallas_call | solution.py:169
  28.9 2.8 %collective-permute-start.5 = (bf16[256,4608]{1,0:T(8,128)(2,1)}, bf16[256,4608]{1,0:T(8,128)(2,1)}, u32[]{:S(2)}, u32[]{:S(2)}) collective-permute-start(bf16[256,4608]{1,0:T(8,128)(2,1)} %get-tuple-element.48.refs_2_), channel_id=1, source_target_pairs={{0,64},{1,67},{2,66},{3,65},{64,2},{65,1},{66,0},{67,3},{4,68},{5,... | collective-permute-start | bytes 7077896 | tf_op jit(solution)/shard_map/ppermute | solution.py:707
  31.7 1.2 collective-permute-start.4
  33.1 1.3 copy-done.4
  34.4 1.3 collect.1
  35.7 1.4 copy-done.8
  37.1 6.8 %all-to-all-start.1 = ((bf16[32,32,1024]{2,1,0:T(8,128)(2,1)}), bf16[32,32,1024]{2,1,0:T(8,128)(2,1)}, u32[]{:S(2)}, u32[]{:S(2)}) async-start(bf16[32,32,1024]{2,1,0:T(8,128)(2,1)} %bitcast.21), calls=%async_computation.1 | async-start | bytes 4194304 | tf_op jit(solution)/shard_map/all_to_all | solution.py:694
  43.9 2.4 %collective-permute-start.6 = (bf16[4,288,512]{2,1,0:T(8,128)(2,1)S(1)}, bf16[4,288,512]{2,1,0:T(8,128)(2,1)S(1)}, u32[]{:S(2)}, u32[]{:S(2)}) collective-permute-start(bf16[4,288,512]{2,1,0:T(8,128)(2,1)S(1)} %copy-done.5), channel_id=1, source_target_pairs={{0,48},{1,13},{2,50},{3,15},{4,52},{5,1},{6,54},{7,3},{8,56},{9,5}... | collective-permute-start | bytes 3538952 | tf_op jit(solution)/shard_map/ppermute | solution.py:661
  46.3 2.3 %collective-permute-done.4.refs_1_.refs_7_ = bf16[4,288,512]{2,1,0:T(8,128)(2,1)} collective-permute-done((bf16[4,288,512]{2,1,0:T(8,128)(2,1)}, bf16[4,288,512]{2,1,0:T(8,128)(2,1)}, u32[]{:S(2)}, u32[]{:S(2)}) %collective-permute-start.4) | collective-permute-done | bytes 1179680 | tf_op jit(solution)/shard_map/ppermute | solution.py:661
  48.8 15.5 %collective-permute-done.5.refs_3_ = bf16[256,4608]{1,0:T(8,128)(2,1)} collective-permute-done((bf16[256,4608]{1,0:T(8,128)(2,1)}, bf16[256,4608]{1,0:T(8,128)(2,1)}, u32[]{:S(2)}, u32[]{:S(2)}) %collective-permute-start.5) | collective-permute-done | bytes 2359328 | tf_op jit(solution)/shard_map/ppermute | solution.py:707
  64.3 5.5 %multiply.1.acc_hbm = f32[512,512]{1,0:T(8,128)} custom-call(s32[5]{0:T(128)} %stack.24.here_ref.refs_0_, bf16[4,288,512]{2,1,0:T(8,128)(2,1)} %stack.25.refs_0_.after_ref.refs_6_, bf16[4,288,512]{2,1,0:T(8,128)(2,1)} %collective-permute-done.4.refs_1_.refs_7_, bf16[256,4608]{1,0:T(8,128)(2,1)} %get-tuple-element.48.refs_2_, ...), custom_call_target="tpu_custom_call" | custom-call | tf_op jit(solution)/shard_map/multiply/pallas_call | solution.py:247
  69.8 11.8 %collective-permute-done.6.refs_0_.refs_8_ = bf16[4,288,512]{2,1,0:T(8,128)(2,1)S(1)} collective-permute-done((bf16[4,288,512]{2,1,0:T(8,128)(2,1)S(1)}, bf16[4,288,512]{2,1,0:T(8,128)(2,1)S(1)}, u32[]{:S(2)}, u32[]{:S(2)}) %collective-permute-start.6) | collective-permute-done | bytes 1179680 | tf_op jit(solution)/shard_map/ppermute | solution.py:661
  82.3 1.3 collective-permute-done.7.refs_1_.refs_9_
  83.7 1.2 copy-done.14
  84.9 5.9 %merge.1 = (bf16[512,512]{1,0:T(8,128)(2,1)S(1)}, f32[512,512]{1,0:T(8,128)S(1)}, bf16[512,512]{1,0:T(8,128)(2,1)S(1)}, f32[8,512]{1,0:T(8,128)S(1)}) custom-call(s32[5]{0:T(128)S(1)} %copy-done.18, bf16[1,512]{1,0:T(2,128)(2,1)S(1)} %constant_dynamic-slice_fusion.1.ngain_ref.refs_1_, s32[512,1]{1,0:T(8,128)S(1)} %copy.28.slot_ref, ...), custom_call_target="tpu_custom_call" | custom-call | tf_op jit(solution)/shard_map/merge/pallas_call | solution.py:299
  90.8 3.0 %collective-permute-start.8 = (f32[8,512]{1,0:T(8,128)S(1)}, f32[8,512]{1,0:T(8,128)S(1)}, u32[]{:S(2)}, u32[]{:S(2)}) collective-permute-start(f32[8,512]{1,0:T(8,128)S(1)} %get-tuple-element.51.sums_ref), channel_id=1, source_target_pairs={{0,1},{1,0},{2,3},{3,2},{4,5},{5,4},{6,7},{7,6},{8,9},{9,8},{10,11... | collective-permute-start | bytes 49160 | tf_op jit(solution)/shard_map/ppermute | solution.py:713
  94.7 2.8 %collective-permute-start.11 = (f32[8,512]{1,0:T(8,128)S(1)}, f32[8,512]{1,0:T(8,128)S(1)}, u32[]{:S(2)}, u32[]{:S(2)}) collective-permute-start(f32[8,512]{1,0:T(8,128)S(1)} %get-tuple-element.54), channel_id=1, source_target_pairs={{0,66},{1,67},{2,64},{3,65},{64,0},{65,1},{66,2},{67,3},{4,70},{5,... | collective-permute-start | bytes 49160 | tf_op jit(solution)/shard_map/ppermute | solution.py:649
  97.5 2.5 %collective-permute-start.10 = (f32[8,512]{1,0:T(8,128)S(1)}, f32[8,512]{1,0:T(8,128)S(1)}, u32[]{:S(2)}, u32[]{:S(2)}) collective-permute-start(f32[8,512]{1,0:T(8,128)S(1)} %get-tuple-element.55.after_ref.refs_2_), channel_id=1, source_target_pairs={{0,2},{1,3},{2,0},{3,1},{64,66},{65,67},{66,64},{67,65},{4,6},{5,7... | collective-permute-start | bytes 49160 | tf_op jit(solution)/shard_map/ppermute | solution.py:649
  100.0 1.4 pack.1
  102.3 1.3 copy-done.10
  103.6 5.4 %backward.1 = (bf16[256,4608]{1,0:T(8,128)(2,1)S(1)}, bf16[256,4608]{1,0:T(8,128)(2,1)S(1)}) custom-call(s32[5]{0:T(128)S(1)} %copy-done.18, bf16[1,512]{1,0:T(2,128)(2,1)S(1)} %constant_dynamic-slice_fusion.1.ngain_ref.refs_1_, f32[8,512]{1,0:T(8,128)S(1)} %get-tuple-element.55.after_ref.refs_2_, f32[8,512]{1,0:T(8,128)S(1)} %collective-permute-done.9.refs_3_, ...), custom_call_target="tpu_custom_call" | custom-call | tf_op jit(solution)/shard_map/backward/pallas_call | solution.py:434
  109.0 4.2 %collective-permute-done.12.after_ref.crossed_ref = bf16[512,512]{1,0:T(8,128)(2,1)S(1)} collective-permute-done((bf16[512,512]{1,0:T(8,128)(2,1)S(1)}, bf16[512,512]{1,0:T(8,128)(2,1)S(1)}, u32[]{:S(2)}, u32[]{:S(2)}) %collective-permute-start.12) | collective-permute-done | bytes 524320 | tf_op jit(solution)/shard_map/ppermute | solution.py:717
  113.2 2.7 %collective-permute-start.13 = (bf16[256,4608]{1,0:T(8,128)(2,1)S(1)}, bf16[256,4608]{1,0:T(8,128)(2,1)S(1)}, u32[]{:S(2)}, u32[]{:S(2)}) collective-permute-start(bf16[256,4608]{1,0:T(8,128)(2,1)S(1)} %get-tuple-element.65), channel_id=1, source_target_pairs={{0,1},{1,0},{2,3},{3,2},{4,5},{5,4},{6,7},{7,6},{8,9},{9,8},{10,11... | collective-permute-start | bytes 7077896 | tf_op jit(solution)/shard_map/ppermute | solution.py:721
  115.9 4.2 %collective-permute-done.13.got_ref = bf16[256,4608]{1,0:T(8,128)(2,1)S(1)} collective-permute-done((bf16[256,4608]{1,0:T(8,128)(2,1)S(1)}, bf16[256,4608]{1,0:T(8,128)(2,1)S(1)}, u32[]{:S(2)}, u32[]{:S(2)}) %collective-permute-start.13) | collective-permute-done | bytes 2359328 | tf_op jit(solution)/shard_map/ppermute | solution.py:721
  120.1 1.4 pair.1
  122.6 2.0 %collective-permute-start.15 = (bf16[64,4608]{1,0:T(8,128)(2,1)}, bf16[64,4608]{1,0:T(8,128)(2,1)}, u32[]{:S(2)}, u32[]{:S(2)}) collective-permute-start(bf16[64,4608]{1,0:T(8,128)(2,1)} %get-tuple-element.68), channel_id=1, source_target_pairs={{0,66},{1,67},{2,64},{3,65},{64,0},{65,1},{66,2},{67,3},{4,70},{5,... | collective-permute-start | bytes 1769480 | tf_op jit(solution)/shard_map/ppermute | solution.py:649
  125.6 5.6 %all-to-all-start.2 = ((bf16[16,2,32,512]{3,2,1,0:T(8,128)(2,1)}), bf16[16,2,32,512]{3,2,1,0:T(8,128)(2,1)}, u32[]{:S(2)}, u32[]{:S(2)}) async-start(bf16[16,2,32,512]{3,2,1,0:T(8,128)(2,1)} %copy-done.11), calls=%async_computation.2 | async-start | bytes 2097152 | tf_op jit(solution)/shard_map/all_to_all | solution.py:728
  131.2 6.7 %collective-permute-done.14.from_last_ref.early_ref = bf16[64,4608]{1,0:T(8,128)(2,1)} collective-permute-done((bf16[64,4608]{1,0:T(8,128)(2,1)}, bf16[64,4608]{1,0:T(8,128)(2,1)}, u32[]{:S(2)}, u32[]{:S(2)}) %collective-permute-start.14) | collective-permute-done | bytes 589856 | tf_op jit(solution)/shard_map/ppermute | solution.py:649
  137.9 1.7 copy-done.2
  139.6 1.7 relay.1
  141.3 2.4 %collective-permute-start.16 = (bf16[32,4608]{1,0:T(8,128)(2,1)S(1)}, bf16[32,4608]{1,0:T(8,128)(2,1)S(1)}, u32[]{:S(2)}, u32[]{:S(2)}) collective-permute-start(bf16[32,4608]{1,0:T(8,128)(2,1)S(1)} %get-tuple-element.69), channel_id=1, source_target_pairs={{0,66},{1,67},{2,64},{3,65},{64,0},{65,1},{66,2},{67,3},{4,70},{5,... | collective-permute-start | bytes 884744 | tf_op jit(solution)/shard_map/ppermute | solution.py:649
  143.7 5.1 %collective-permute-done.16.late_ref = bf16[32,4608]{1,0:T(8,128)(2,1)S(1)} collective-permute-done((bf16[32,4608]{1,0:T(8,128)(2,1)S(1)}, bf16[32,4608]{1,0:T(8,128)(2,1)S(1)}, u32[]{:S(2)}, u32[]{:S(2)}) %collective-permute-start.16) | collective-permute-done | bytes 294944 | tf_op jit(solution)/shard_map/ppermute | solution.py:649
  148.8 2.4 %finish.2.refs_1_ = bf16[128,1152]{1,0:T(8,128)(2,1)S(1)} custom-call(s32[5]{0:T(128)S(1)} %copy-done.18, bf16[256,4608]{1,0:T(8,128)(2,1)S(1)} %get-tuple-element.64.own_ref, bf16[256,4608]{1,0:T(8,128)(2,1)S(1)} %copy-done.3, bf16[64,4608]{1,0:T(8,128)(2,1)} %collective-permute-done.14.from_last_ref.early_ref, ...), custom_call_target="tpu_custom_call" | custom-call | tf_op jit(solution)/shard_map/finish/pallas_call | solution.py:540
  151.2 2.1 %collective-permute-start.17 = (bf16[128,1152]{1,0:T(8,128)(2,1)S(1)}, bf16[128,1152]{1,0:T(8,128)(2,1)}, u32[]{:S(2)}, u32[]{:S(2)}) collective-permute-start(bf16[128,1152]{1,0:T(8,128)(2,1)S(1)} %finish.2.refs_1_), channel_id=1, source_target_pairs={{0,2},{1,3},{2,0},{3,1},{4,6},{5,7},{6,4},{7,5},{8,10},{9,11},{10,... | collective-permute-start | bytes 884744 | tf_op jit(solution)/shard_map/ppermute | solution.py:735
  153.3 3.1 %finish.3.refs_0_ = bf16[128,1152]{1,0:T(8,128)(2,1)} custom-call(s32[5]{0:T(128)S(1)} %copy-done.18, bf16[256,4608]{1,0:T(8,128)(2,1)S(1)} %get-tuple-element.64.own_ref, bf16[256,4608]{1,0:T(8,128)(2,1)S(1)} %copy-done.3, bf16[64,4608]{1,0:T(8,128)(2,1)} %collective-permute-done.15.from_next_ref.early_ref, ...), custom_call_target="tpu_custom_call" | custom-call | tf_op jit(solution)/shard_map/finish/pallas_call | solution.py:540
  157.4 1.2 copy-done.13
  158.6 3.1 %place.1 = bf16[512,1024]{1,0:T(8,128)(2,1)} custom-call(s32[5]{0:T(128)S(1)} %copy-done.18, s32[512,1]{1,0:T(8,128)S(1)} %reshape.38.pos_ref, bf16[16,2,32,512]{3,2,1,0:T(8,128)(2,1)} %all-to-all-done.2.came_ref, bf16[512,1024]{1,0:T(8,128)(2,1)S(1)} %copy-done.13), custom_call_target="tpu_custom_call" | custom-call | tf_op jit(solution)/shard_map/place/pallas_call | solution.py:581
  161.6 2.7 %collective-permute-start.21 = (bf16[128,1152]{1,0:T(8,128)(2,1)S(1)}, bf16[128,1152]{1,0:T(8,128)(2,1)S(1)}, u32[]{:S(2)}, u32[]{:S(2)}) collective-permute-start(bf16[128,1152]{1,0:T(8,128)(2,1)S(1)} %finish.2.refs_1_), channel_id=1, source_target_pairs={{0,1},{1,0},{2,3},{3,2},{4,5},{5,4},{6,7},{7,6},{8,9},{9,8},{10,11... | collective-permute-start | bytes 884744 | tf_op jit(solution)/shard_map/ppermute | solution.py:737
  164.9 1.1 collective-permute-done.19.refs_2_
  166.0 2.5 %collective-permute-start.22 = (bf16[128,1152]{1,0:T(8,128)(2,1)S(1)}, bf16[128,1152]{1,0:T(8,128)(2,1)S(1)}, u32[]{:S(2)}, u32[]{:S(2)}) collective-permute-start(bf16[128,1152]{1,0:T(8,128)(2,1)S(1)} %collective-permute-done.19.refs_2_), channel_id=1, source_target_pairs={{0,1},{1,0},{2,3},{3,2},{4,5},{5,4},{6,7},{7,6},{8,9},{9,8},{10,11... | collective-permute-start | bytes 884744 | tf_op jit(solution)/shard_map/ppermute | solution.py:737
  168.5 1.2 collective-permute-done.22.refs_6_
  169.7 2.5 %lay.1 = bf16[1024,1152]{1,0:T(8,128)(2,1)} custom-call(s32[5]{0:T(128)S(1)} %copy-done.18, bf16[128,1152]{1,0:T(8,128)(2,1)} %finish.3.refs_0_, bf16[128,1152]{1,0:T(8,128)(2,1)S(1)} %finish.2.refs_1_, bf16[128,1152]{1,0:T(8,128)(2,1)S(1)} %collective-permute-done.19.refs_2_, bf16[128,1152]{1,0:T(8,128)(2,1)} %collective-permute-done.17.refs_3_, ...), custom_call_target="tpu_custom_call" | custom-call | tf_op jit(solution)/shard_map/lay/pallas_call | solution.py:609
  (78 shorter events, 10.2 us)
Async XLA Ops:
  0.6 1.1 copy-start
  1.7 23.5 %copy-start.19 = (bf16[1,4,72,512]{3,2,1,0:T(8,128)(2,1)}, bf16[1,4,72,512]{3,2,1,0:T(8,128)(2,1)S(1)}, u32[]{:S(2)}) copy-start(bf16[1,4,72,512]{3,2,1,0:T(8,128)(2,1)S(1)} %constant_dynamic-slice_fusion) | copy-start | bytes 884740
  1.7 23.4 %collective-permute-start.2 = (bf16[288,512]{1,0:T(8,128)(2,1)S(1)}, bf16[288,512]{1,0:T(8,128)(2,1)S(1)}, u32[]{:S(2)}, u32[]{:S(2)}) collective-permute-start(bf16[288,512]{1,0:T(8,128)(2,1)S(1)} %bitcast.28), channel_id=1, source_target_pairs={{0,8},{1,33},{2,10},{3,35},{4,12},{5,37},{6,14},{7,39},{8,0},{9,41... | collective-permute-start | bytes 884744 | tf_op jit(solution)/shard_map/ppermute | solution.py:661
  6.2 18.9 %collective-permute-start.1 = (bf16[288,512]{1,0:T(8,128)(2,1)S(1)}, bf16[288,512]{1,0:T(8,128)(2,1)}, u32[]{:S(2)}, u32[]{:S(2)}) collective-permute-start(bf16[288,512]{1,0:T(8,128)(2,1)S(1)} %bitcast.29), channel_id=1, source_target_pairs={{0,12},{1,49},{2,14},{3,51},{4,0},{5,53},{6,2},{7,55},{8,4},{9,57}... | collective-permute-start | bytes 884744 | tf_op jit(solution)/shard_map/ppermute | solution.py:661
  6.7 18.5 %collective-permute-start = (bf16[288,512]{1,0:T(8,128)(2,1)S(1)}, bf16[288,512]{1,0:T(8,128)(2,1)}, u32[]{:S(2)}, u32[]{:S(2)}) collective-permute-start(bf16[288,512]{1,0:T(8,128)(2,1)S(1)} %bitcast.30), channel_id=1, source_target_pairs={{0,4},{1,17},{2,6},{3,19},{4,8},{5,21},{6,10},{7,23},{8,12},{9,25}... | collective-permute-start | bytes 884744 | tf_op jit(solution)/shard_map/ppermute | solution.py:661
  8.7 16.4 %collective-permute-start.3 = (s32[256]{0:T(256)S(1)}, s32[256]{0:T(256)S(1)}, u32[]{:S(2)}, u32[]{:S(2)}) collective-permute-start(s32[256]{0:T(256)S(1)} %get-tuple-element.78), channel_id=1, source_target_pairs={{0,64},{64,0},{1,65},{65,1},{2,66},{66,2},{3,67},{67,3},{4,68},{68... | collective-permute-start | bytes 3080 | tf_op jit(solution)/shard_map/ppermute | solution.py:680
  10.8 14.3 %all-to-all-start = ((s32[32,1,16]{2,1,0:T(1,128)}), s32[32,1,16]{2,1,0:T(1,128)S(1)}, u32[]{:S(2)}, u32[]{:S(2)}) async-start(s32[32,1,16]{2,1,0:T(1,128)} %bitcast.5), calls=%async_computation | async-start | bytes 32768 | tf_op jit(solution)/shard_map/all_to_all | solution.py:673
  17.5 15.6 %copy-start.12 = (bf16[512,1024]{1,0:T(8,128)(2,1)S(1)}, bf16[512,1024]{1,0:T(8,128)(2,1)}, u32[]{:S(2)}) copy-start(bf16[512,1024]{1,0:T(8,128)(2,1)} %stream_ref.3) | copy-start | bytes 3145732
  17.5 15.6 %copy-start.15 = (bf16[1,512,1024]{2,1,0:T(8,128)(2,1)S(1)}, bf16[1,512,1024]{2,1,0:T(8,128)(2,1)}, u32[]{:S(2)}) copy-start(bf16[1,512,1024]{2,1,0:T(8,128)(2,1)} %param.14) | copy-start | bytes 3145732
  28.9 35.4 %collective-permute-start.5 = (bf16[256,4608]{1,0:T(8,128)(2,1)}, bf16[256,4608]{1,0:T(8,128)(2,1)}, u32[]{:S(2)}, u32[]{:S(2)}) collective-permute-start(bf16[256,4608]{1,0:T(8,128)(2,1)} %get-tuple-element.48.refs_2_), channel_id=1, source_target_pairs={{0,64},{1,67},{2,66},{3,65},{64,2},{65,1},{66,0},{67,3},{4,68},{5,... | collective-permute-start | bytes 7077896 | tf_op jit(solution)/shard_map/ppermute | solution.py:707
  31.7 16.9 %collective-permute-start.4 = (bf16[4,288,512]{2,1,0:T(8,128)(2,1)}, bf16[4,288,512]{2,1,0:T(8,128)(2,1)}, u32[]{:S(2)}, u32[]{:S(2)}) collective-permute-start(bf16[4,288,512]{2,1,0:T(8,128)(2,1)} %stack.25.refs_0_.after_ref.refs_6_), channel_id=1, source_target_pairs={{0,16},{1,5},{2,18},{3,7},{4,20},{5,9},{6,22},{7,11},{8,24},{9,13}... | collective-permute-start | bytes 3538952 | tf_op jit(solution)/shard_map/ppermute | solution.py:661
  33.1 1.3 copy-start.4
  35.7 1.4 copy-start.8
  37.1 6.8 %copy-start.5 = (bf16[4,288,512]{2,1,0:T(8,128)(2,1)S(1)}, bf16[4,288,512]{2,1,0:T(8,128)(2,1)}, u32[]{:S(2)}) copy-start(bf16[4,288,512]{2,1,0:T(8,128)(2,1)} %stack.25.refs_0_.after_ref.refs_6_) | copy-start | bytes 3538948
  37.1 11.5 %copy-start.21 = (bf16[1,1024]{1,0:T(2,128)(2,1)S(1)}, bf16[1,1024]{1,0:T(2,128)(2,1)}, u32[]{:S(2)}) copy-start(bf16[1,1024]{1,0:T(2,128)(2,1)} %param.13) | copy-start | bytes 6148
  37.1 45.3 %all-to-all-start.1 = ((bf16[32,32,1024]{2,1,0:T(8,128)(2,1)}), bf16[32,32,1024]{2,1,0:T(8,128)(2,1)}, u32[]{:S(2)}, u32[]{:S(2)}) async-start(bf16[32,32,1024]{2,1,0:T(8,128)(2,1)} %bitcast.21), calls=%async_computation.1 | async-start | bytes 4194304 | tf_op jit(solution)/shard_map/all_to_all | solution.py:694
  43.9 37.7 %collective-permute-start.6 = (bf16[4,288,512]{2,1,0:T(8,128)(2,1)S(1)}, bf16[4,288,512]{2,1,0:T(8,128)(2,1)S(1)}, u32[]{:S(2)}, u32[]{:S(2)}) collective-permute-start(bf16[4,288,512]{2,1,0:T(8,128)(2,1)S(1)} %copy-done.5), channel_id=1, source_target_pairs={{0,48},{1,13},{2,50},{3,15},{4,52},{5,1},{6,54},{7,3},{8,56},{9,5}... | collective-permute-start | bytes 3538952 | tf_op jit(solution)/shard_map/ppermute | solution.py:661
  48.6 35.1 %collective-permute-start.7 = (bf16[4,288,512]{2,1,0:T(8,128)(2,1)}, bf16[4,288,512]{2,1,0:T(8,128)(2,1)}, u32[]{:S(2)}, u32[]{:S(2)}) collective-permute-start(bf16[4,288,512]{2,1,0:T(8,128)(2,1)} %collective-permute-done.4.refs_1_.refs_7_), channel_id=1, source_target_pairs={{0,16},{1,5},{2,18},{3,7},{4,20},{5,9},{6,22},{7,11},{8,24},{9,13}... | collective-permute-start | bytes 3538952 | tf_op jit(solution)/shard_map/ppermute | solution.py:661
  48.8 34.9 %copy-start.18 = (s32[5]{0:T(128)S(1)}, s32[5]{0:T(128)}, u32[]{:S(2)}) copy-start(s32[5]{0:T(128)} %stack.24.here_ref.refs_0_) | copy-start | bytes 64
  81.6 9.3 %copy-start.9 = (bf16[4,288,512]{2,1,0:T(8,128)(2,1)}, bf16[4,288,512]{2,1,0:T(8,128)(2,1)S(1)}, u32[]{:S(2)}) copy-start(bf16[4,288,512]{2,1,0:T(8,128)(2,1)S(1)} %collective-permute-done.6.refs_0_.refs_8_) | copy-start | bytes 3538948
  83.7 1.2 copy-start.14
  84.9 17.4 %copy-start.6 = (bf16[4,288,512]{2,1,0:T(8,128)(2,1)S(1)}, bf16[4,288,512]{2,1,0:T(8,128)(2,1)}, u32[]{:S(2)}) copy-start(bf16[4,288,512]{2,1,0:T(8,128)(2,1)} %stack.25.refs_0_.after_ref.refs_6_) | copy-start | bytes 3538948
  90.8 3.9 %collective-permute-start.8 = (f32[8,512]{1,0:T(8,128)S(1)}, f32[8,512]{1,0:T(8,128)S(1)}, u32[]{:S(2)}, u32[]{:S(2)}) collective-permute-start(f32[8,512]{1,0:T(8,128)S(1)} %get-tuple-element.51.sums_ref), channel_id=1, source_target_pairs={{0,1},{1,0},{2,3},{3,2},{4,5},{5,4},{6,7},{7,6},{8,9},{9,8},{10,11... | collective-permute-start | bytes 49160 | tf_op jit(solution)/shard_map/ppermute | solution.py:713
  94.7 6.6 %collective-permute-start.11 = (f32[8,512]{1,0:T(8,128)S(1)}, f32[8,512]{1,0:T(8,128)S(1)}, u32[]{:S(2)}, u32[]{:S(2)}) collective-permute-start(f32[8,512]{1,0:T(8,128)S(1)} %get-tuple-element.54), channel_id=1, source_target_pairs={{0,66},{1,67},{2,64},{3,65},{64,0},{65,1},{66,2},{67,3},{4,70},{5,... | collective-permute-start | bytes 49160 | tf_op jit(solution)/shard_map/ppermute | solution.py:649
  97.5 3.9 %collective-permute-start.9 = (f32[8,512]{1,0:T(8,128)S(1)}, f32[8,512]{1,0:T(8,128)S(1)}, u32[]{:S(2)}, u32[]{:S(2)}) collective-permute-start(f32[8,512]{1,0:T(8,128)S(1)} %get-tuple-element.54), channel_id=1, source_target_pairs={{0,64},{1,65},{2,66},{3,67},{64,2},{65,3},{66,0},{67,1},{4,68},{5,... | collective-permute-start | bytes 49160 | tf_op jit(solution)/shard_map/ppermute | solution.py:649
  97.5 4.1 %collective-permute-start.10 = (f32[8,512]{1,0:T(8,128)S(1)}, f32[8,512]{1,0:T(8,128)S(1)}, u32[]{:S(2)}, u32[]{:S(2)}) collective-permute-start(f32[8,512]{1,0:T(8,128)S(1)} %get-tuple-element.55.after_ref.refs_2_), channel_id=1, source_target_pairs={{0,2},{1,3},{2,0},{3,1},{64,66},{65,67},{66,64},{67,65},{4,6},{5,7... | collective-permute-start | bytes 49160 | tf_op jit(solution)/shard_map/ppermute | solution.py:649
  101.6 11.6 %collective-permute-start.12 = (bf16[512,512]{1,0:T(8,128)(2,1)S(1)}, bf16[512,512]{1,0:T(8,128)(2,1)S(1)}, u32[]{:S(2)}, u32[]{:S(2)}) collective-permute-start(bf16[512,512]{1,0:T(8,128)(2,1)S(1)} %get-tuple-element.63), channel_id=1, source_target_pairs={{0,64},{64,0},{1,65},{65,1},{2,66},{66,2},{3,67},{67,3},{4,68},{68... | collective-permute-start | bytes 1572872 | tf_op jit(solution)/shard_map/ppermute | solution.py:717
  102.3 1.3 copy-start.10
  113.2 6.9 %collective-permute-start.13 = (bf16[256,4608]{1,0:T(8,128)(2,1)S(1)}, bf16[256,4608]{1,0:T(8,128)(2,1)S(1)}, u32[]{:S(2)}, u32[]{:S(2)}) collective-permute-start(bf16[256,4608]{1,0:T(8,128)(2,1)S(1)} %get-tuple-element.65), channel_id=1, source_target_pairs={{0,1},{1,0},{2,3},{3,2},{4,5},{5,4},{6,7},{7,6},{8,9},{9,8},{10,11... | collective-permute-start | bytes 7077896 | tf_op jit(solution)/shard_map/ppermute | solution.py:721
  120.1 1.8 %copy-start.1 = (bf16[256,4608]{1,0:T(8,128)(2,1)}, bf16[256,4608]{1,0:T(8,128)(2,1)S(1)}, u32[]{:S(2)}) copy-start(bf16[256,4608]{1,0:T(8,128)(2,1)S(1)} %collective-permute-done.13.got_ref) | copy-start | bytes 7077892
  121.9 16.1 %collective-permute-start.14 = (bf16[64,4608]{1,0:T(8,128)(2,1)}, bf16[64,4608]{1,0:T(8,128)(2,1)}, u32[]{:S(2)}, u32[]{:S(2)}) collective-permute-start(bf16[64,4608]{1,0:T(8,128)(2,1)} %get-tuple-element.67), channel_id=1, source_target_pairs={{0,64},{1,65},{2,66},{3,67},{64,2},{65,3},{66,0},{67,1},{4,68},{5,... | collective-permute-start | bytes 1769480 | tf_op jit(solution)/shard_map/ppermute | solution.py:649
  122.6 15.4 %collective-permute-start.15 = (bf16[64,4608]{1,0:T(8,128)(2,1)}, bf16[64,4608]{1,0:T(8,128)(2,1)}, u32[]{:S(2)}, u32[]{:S(2)}) collective-permute-start(bf16[64,4608]{1,0:T(8,128)(2,1)} %get-tuple-element.68), channel_id=1, source_target_pairs={{0,66},{1,67},{2,64},{3,65},{64,0},{65,1},{66,2},{67,3},{4,70},{5,... | collective-permute-start | bytes 1769480 | tf_op jit(solution)/shard_map/ppermute | solution.py:649
  124.6 1.0 copy-start.11
  125.6 23.2 %copy-start.17 = (bf16[1,4,1152]{2,1,0:T(4,128)(2,1)S(1)}, bf16[1,4,1152]{2,1,0:T(4,128)(2,1)}, u32[]{:S(2)}) copy-start(bf16[1,4,1152]{2,1,0:T(4,128)(2,1)} %param.9) | copy-start | bytes 27652
  125.6 31.8 %all-to-all-start.2 = ((bf16[16,2,32,512]{3,2,1,0:T(8,128)(2,1)}), bf16[16,2,32,512]{3,2,1,0:T(8,128)(2,1)}, u32[]{:S(2)}, u32[]{:S(2)}) async-start(bf16[16,2,32,512]{3,2,1,0:T(8,128)(2,1)} %copy-done.11), calls=%async_computation.2 | async-start | bytes 2097152 | tf_op jit(solution)/shard_map/all_to_all | solution.py:728
  137.9 1.7 copy-start.2
  139.6 9.1 %copy-start.3 = (bf16[256,4608]{1,0:T(8,128)(2,1)S(1)}, bf16[256,4608]{1,0:T(8,128)(2,1)}, u32[]{:S(2)}) copy-start(bf16[256,4608]{1,0:T(8,128)(2,1)} %copy-done.1) | copy-start | bytes 7077892
  139.6 9.1 %copy-start.7 = (bf16[4,256,1152]{2,1,0:T(8,128)(2,1)S(1)}, bf16[4,256,1152]{2,1,0:T(8,128)(2,1)}, u32[]{:S(2)}) copy-start(bf16[4,256,1152]{2,1,0:T(8,128)(2,1)} %get-tuple-element.70.xw_ref) | copy-start | bytes 7077892
  139.6 9.2 %copy-start.16 = (f32[256,128]{1,0:T(8,128)S(1)}, f32[256,128]{1,0:T(8,128)}, u32[]{:S(2)}) copy-start(f32[256,128]{1,0:T(8,128)} %get-tuple-element.71.stat_ref) | copy-start | bytes 393220
  141.3 7.5 %collective-permute-start.16 = (bf16[32,4608]{1,0:T(8,128)(2,1)S(1)}, bf16[32,4608]{1,0:T(8,128)(2,1)S(1)}, u32[]{:S(2)}, u32[]{:S(2)}) collective-permute-start(bf16[32,4608]{1,0:T(8,128)(2,1)S(1)} %get-tuple-element.69), channel_id=1, source_target_pairs={{0,66},{1,67},{2,64},{3,65},{64,0},{65,1},{66,2},{67,3},{4,70},{5,... | collective-permute-start | bytes 884744 | tf_op jit(solution)/shard_map/ppermute | solution.py:649
  143.7 9.6 %collective-permute-start.18 = (bf16[32,4608]{1,0:T(8,128)(2,1)S(1)}, bf16[32,4608]{1,0:T(8,128)(2,1)S(1)}, u32[]{:S(2)}, u32[]{:S(2)}) collective-permute-start(bf16[32,4608]{1,0:T(8,128)(2,1)S(1)} %get-tuple-element.74), channel_id=1, source_target_pairs={{0,64},{1,65},{2,66},{3,67},{64,2},{65,3},{66,0},{67,1},{4,68},{5,... | collective-permute-start | bytes 884744 | tf_op jit(solution)/shard_map/ppermute | solution.py:649
  151.2 13.2 %collective-permute-start.17 = (bf16[128,1152]{1,0:T(8,128)(2,1)S(1)}, bf16[128,1152]{1,0:T(8,128)(2,1)}, u32[]{:S(2)}, u32[]{:S(2)}) collective-permute-start(bf16[128,1152]{1,0:T(8,128)(2,1)S(1)} %finish.2.refs_1_), channel_id=1, source_target_pairs={{0,2},{1,3},{2,0},{3,1},{4,6},{5,7},{6,4},{7,5},{8,10},{9,11},{10,... | collective-permute-start | bytes 884744 | tf_op jit(solution)/shard_map/ppermute | solution.py:735
  156.4 9.6 %collective-permute-start.19 = (bf16[128,1152]{1,0:T(8,128)(2,1)}, bf16[128,1152]{1,0:T(8,128)(2,1)S(1)}, u32[]{:S(2)}, u32[]{:S(2)}) collective-permute-start(bf16[128,1152]{1,0:T(8,128)(2,1)} %finish.3.refs_0_), channel_id=1, source_target_pairs={{0,2},{1,3},{2,0},{3,1},{4,6},{5,7},{6,4},{7,5},{8,10},{9,11},{10,... | collective-permute-start | bytes 884744 | tf_op jit(solution)/shard_map/ppermute | solution.py:735
  157.4 1.2 copy-start.13
  161.6 6.9 %collective-permute-start.21 = (bf16[128,1152]{1,0:T(8,128)(2,1)S(1)}, bf16[128,1152]{1,0:T(8,128)(2,1)S(1)}, u32[]{:S(2)}, u32[]{:S(2)}) collective-permute-start(bf16[128,1152]{1,0:T(8,128)(2,1)S(1)} %finish.2.refs_1_), channel_id=1, source_target_pairs={{0,1},{1,0},{2,3},{3,2},{4,5},{5,4},{6,7},{7,6},{8,9},{9,8},{10,11... | collective-permute-start | bytes 884744 | tf_op jit(solution)/shard_map/ppermute | solution.py:737
  164.4 4.2 %collective-permute-start.20 = (bf16[128,1152]{1,0:T(8,128)(2,1)}, bf16[128,1152]{1,0:T(8,128)(2,1)S(1)}, u32[]{:S(2)}, u32[]{:S(2)}) collective-permute-start(bf16[128,1152]{1,0:T(8,128)(2,1)} %finish.3.refs_0_), channel_id=1, source_target_pairs={{0,1},{1,0},{2,3},{3,2},{4,5},{5,4},{6,7},{7,6},{8,9},{9,8},{10,11... | collective-permute-start | bytes 884744 | tf_op jit(solution)/shard_map/ppermute | solution.py:737
  164.4 4.2 %collective-permute-start.23 = (bf16[128,1152]{1,0:T(8,128)(2,1)}, bf16[128,1152]{1,0:T(8,128)(2,1)S(1)}, u32[]{:S(2)}, u32[]{:S(2)}) collective-permute-start(bf16[128,1152]{1,0:T(8,128)(2,1)} %collective-permute-done.17.refs_3_), channel_id=1, source_target_pairs={{0,1},{1,0},{2,3},{3,2},{4,5},{5,4},{6,7},{7,6},{8,9},{9,8},{10,11... | collective-permute-start | bytes 884744 | tf_op jit(solution)/shard_map/ppermute | solution.py:737
  166.0 3.8 %collective-permute-start.22 = (bf16[128,1152]{1,0:T(8,128)(2,1)S(1)}, bf16[128,1152]{1,0:T(8,128)(2,1)S(1)}, u32[]{:S(2)}, u32[]{:S(2)}) collective-permute-start(bf16[128,1152]{1,0:T(8,128)(2,1)S(1)} %collective-permute-done.19.refs_2_), channel_id=1, source_target_pairs={{0,1},{1,0},{2,3},{3,2},{4,5},{5,4},{6,7},{7,6},{8,9},{9,8},{10,11... | collective-permute-start | bytes 884744 | tf_op jit(solution)/shard_map/ppermute | solution.py:737
  (1 other events, 0.7 us)

commit v20 on v18

--- a/solution.py
+++ b/solution.py
@@ -398,8 +398,8 @@
 
 def backward_kernel(full_width, here_ref, ngain_ref, *refs):
     stats, stacks, refs = refs[:RING], refs[RING : 2 * RING], refs[2 * RING :]
-    state_hbm, cot_hbm, own_ref, other_ref = refs[:4]
-    picked_ref, sums_ref, state_ref, cot_ref, held_ref, row_sems, sems = refs[4:]
+    state_hbm, cot_hbm, own_ref, rest_ref, other_ref, other_rest_ref = refs[:6]
+    picked_ref, sums_ref, state_ref, cot_ref, held_ref, row_sems, sems = refs[6:]
     row_copies = [
         pltpu.make_async_copy(a, b, row_sems.at[i])
         for i, (a, b) in enumerate(((state_hbm, state_ref), (cot_hbm, cot_ref)))
@@ -441,8 +441,11 @@
             (((1,), (1,)), ((), ())),
             preferred_element_type=F32,
         )
-        own_ref[:, cols] = both[: tokens // 2].astype(BF)
-        other_ref[:, cols] = both[tokens // 2 :].astype(BF)
+        start = 0
+        for out_ref in (own_ref, rest_ref, other_ref, other_rest_ref):
+            count = out_ref.shape[0]
+            out_ref[:, cols] = both[start : start + count].astype(BF)
+            start += count
 
 
 def backward(here, state, cot, ngain, stats, stacks, full_width):
@@ -451,8 +454,8 @@
     return pl.pallas_call(
         lambda *refs: backward_kernel(full_width, *refs),
         in_specs=[scalars()] + [whole()] * (1 + RING) + [in_hbm()] * (RING + 2),
-        out_specs=[whole()] * 2,
-        out_shape=[shape((tokens // 2, depth), BF)] * 2,
+        out_specs=[whole()] * 4,
+        out_shape=[shape((n * tokens // 8, depth), BF) for n in (1, RING - 1, 1, RING - 1)],
         scratch_shapes=[
             pltpu.VMEM((tokens, width), BF),
             pltpu.VMEM((tokens, 8), F32),
@@ -474,16 +477,16 @@
 
 
 def pair_kernel(own_ref, got_ref, after_ref, next_ref, last_ref):
-    rows = own_ref.shape[0] // RING
+    rows = own_ref.shape[0] // (RING - 1)
     half = rows // 2
-    next_ref[:half] = both(own_ref, got_ref, 2 * rows, half)
-    next_ref[half:] = both(own_ref, got_ref, rows + half, half)
-    last_ref[:half] = both(own_ref, got_ref, 2 * rows + half, half)
-    last_ref[half:] = both(own_ref, got_ref, 3 * rows, half)
+    next_ref[:half] = both(own_ref, got_ref, rows, half)
+    next_ref[half:] = both(own_ref, got_ref, half, half)
+    last_ref[:half] = both(own_ref, got_ref, rows + half, half)
+    last_ref[half:] = both(own_ref, got_ref, 2 * rows, half)
 
 
 def pair(own, got, after):
-    rows, depth = got.shape[0] // RING, got.shape[1]
+    rows, depth = got.shape[0] // (RING - 1), got.shape[1]
     return pl.pallas_call(
         pair_kernel,
         in_specs=[whole()] * 2 + [anywhere()],
@@ -499,8 +502,8 @@
     half = next_ref.shape[0]
     rows = 2 * half
     for start, came_ref, out_ref in (
-        (rows, from_last_ref, next_ref),
-        (3 * rows + half, from_next_ref, last_ref),
+        (0, from_last_ref, next_ref),
+        (2 * rows + half, from_next_ref, last_ref),
     ):
         kept = both(own_ref, got_ref, start, half).astype(F32)
         out_ref[...] = (kept + came_ref[:half].astype(F32)).astype(BF)
@@ -734,12 +737,15 @@
     cross, stats = lax.optimization_barrier((cross, stats))
     crossed = lax.ppermute(cross, "img", flip)
 
-    own, other = backward(here, state, cot, own_gain, stats, stacks, full_width)
-    own, other, crossed = lax.optimization_barrier((own, other, crossed))
+    own, rest, other, other_rest = backward(here, state, cot, own_gain, stats, stacks, full_width)
+    own, rest, other, other_rest, crossed = lax.optimization_barrier(
+        (own, rest, other, other_rest, crossed)
+    )
+    got_rest = lax.ppermute(other_rest, "tp", core_pairs)
     got = lax.ppermute(other, "tp", core_pairs)
-    to_next, to_last = pair(own, got, crossed)
+    to_next, to_last = pair(rest, got_rest, crossed)
     from_last, from_next = along_x(to_next, 1), along_x(to_last, -1)
-    to_next, to_last = relay(own, got, from_last, from_next)
+    to_next, to_last = relay(rest, got_rest, from_last, from_next)
     late_last, late_next = along_x(to_next, 1), along_x(to_last, -1)
 
     send = braid(stay, crossed, n_ctx)

time: 173 us -> 173 us (level)
    ppermute x1, waiting for transfers between devices: 4.16 us -> 0.01 us  [shards(): got = lax.ppermute(other, 'tp', core_pairs)]
    ppermute x0 -> x1, waiting for transfers between devices: none -> 3.32 us  [shards(): got_rest = lax.ppermute(other_rest, 'tp', core_pairs)]
    ppermute x0 -> x1, starting transfers between devices: none -> 2.98 us  [shards(): got_rest = lax.ppermute(other_rest, 'tp', core_pairs)]
    ppermute x2, waiting for transfers between devices: 1.64 us -> 3.62 us  [shards(): beyond = [lax.ppermute(x, 'tp', far_pairs) for x in out]]
    unnamed x42 -> x50, local copies, waits for them, and re-layouts: 10.4 us -> 9.94 us
  transfers between devices with their start and end apart: 27 -> 28, of which waited for: 12 -> 12; matrix products, arithmetic and copies ran while one was open for 1% -> 1% of each run, Pallas kernels for 20% -> 20%
where the time goes in v20:
time: 173 us; the launch traced here: 172 us
  waiting for transfers between devices  60.7 us (35%)
  starting transfers between devices  53.6 us (31%)
  Pallas kernels  43.6 us (25%)
  local copies, waits for them, and re-layouts  11.6 us (7%)
    ppermute x1, waiting for transfers between devices, shards(): lifted = [lifted, lax.ppermute(lifted, ('img', 'tp'), pairs)]  16.7 us
    ppermute x7, waiting for transfers between devices, along_x(): return lax.ppermute(array, ('img', 'tp'), pairs)  14.6 us
    all_to_all x1, waiting for transfers between devices, shards(): lax.all_to_all(held.reshape(owners, n_img * capacity, width), ('img', 'ct...  12.8 us
    ppermute x7, starting transfers between devices, along_x(): return lax.ppermute(array, ('img', 'tp'), pairs)  11 us
    unnamed x50, local copies, waits for them, and re-layouts  9.94 us
    ppermute x6, starting transfers between devices, along_ctx(): return lax.ppermute(array, ('ctx', 'tp'), pairs)  9.65 us
    pallas_call x1, Pallas kernels, layer_norm(): pl.pallas_call(norm_kernel, grid_spec=pltpu.PrefetchScalarGridSpec(num_sc...  7.6 us
    all_to_all x1, starting transfers between devices, shards(): lax.all_to_all(packed.reshape(owners, capacity), ('img', 'ctx'), split_ax...  6.97 us
  transfers between devices with their start and end apart: 28, of which 12 were waited for; matrix products, arithmetic and copies ran while one was open for 1% of the time, Pallas kernels for 20%

profile of v20, /device:TPU:1, one launch (start us, length us, event | category | flops | bytes accessed | tf_op | source)
XLA Modules:
  0.0 171.9 jit_solution(11826235557317150945)
XLA Ops:
  1.7 2.5 %collective-permute-start = (bf16[288,512]{1,0:T(8,128)(2,1)S(1)}, bf16[288,512]{1,0:T(8,128)(2,1)S(1)}, u32[]{:S(2)}, u32[]{:S(2)}) collective-permute-start(bf16[288,512]{1,0:T(8,128)(2,1)S(1)} %bitcast.22), channel_id=1, source_target_pairs={{0,4},{1,17},{2,6},{3,19},{4,8},{5,21},{6,10},{7,23},{8,12},{9,25}... | collective-permute-start | bytes 884744 | tf_op jit(solution)/shard_map/ppermute | solution.py:681
  4.3 2.2 %collective-permute-start.1 = (bf16[288,512]{1,0:T(8,128)(2,1)S(1)}, bf16[288,512]{1,0:T(8,128)(2,1)S(1)}, u32[]{:S(2)}, u32[]{:S(2)}) collective-permute-start(bf16[288,512]{1,0:T(8,128)(2,1)S(1)} %bitcast.23), channel_id=1, source_target_pairs={{0,12},{1,49},{2,14},{3,51},{4,0},{5,53},{6,2},{7,55},{8,4},{9,57}... | collective-permute-start | bytes 884744 | tf_op jit(solution)/shard_map/ppermute | solution.py:681
  6.5 1.2 collective-permute-start.2
  9.5 7.0 %all-to-all-start = ((s32[32,1,16]{2,1,0:T(1,128)}), s32[32,1,16]{2,1,0:T(1,128)S(1)}, u32[]{:S(2)}, u32[]{:S(2)}) async-start(s32[32,1,16]{2,1,0:T(1,128)} %bitcast.5), calls=%async_computation | async-start | bytes 32768 | tf_op jit(solution)/shard_map/all_to_all | solution.py:693
  16.5 1.3 collective-permute-start.3
  18.5 7.6 %layer_norm.1 = (bf16[256,4608]{1,0:T(8,128)(2,1)}, bf16[4,256,1152]{2,1,0:T(8,128)(2,1)}, f32[256,128]{1,0:T(8,128)}) custom-call(s32[5]{0:T(128)} %stack.24.here_ref.refs_0_, bf16[1024,1152]{1,0:T(8,128)(2,1)} %bitcast.30, bf16[4,1152]{1,0:T(4,128)(2,1)} %bitcast.27, bf16[4,1152]{1,0:T(4,128)(2,1)} %bitcast.34), custom_call_target="tpu_custom_call" | custom-call | tf_op jit(solution)/shard_map/layer_norm/pallas_call | solution.py:97
  27.0 1.6 collective-permute-start.5
  28.6 1.2 collective-permute-start.4
  30.0 1.3 copy-done.12
  31.3 1.2 copy-done.18
  32.5 1.3 collect.1
  33.8 1.4 copy-done.6
  35.2 6.7 %all-to-all-start.1 = ((bf16[32,32,1024]{2,1,0:T(8,128)(2,1)}), bf16[32,32,1024]{2,1,0:T(8,128)(2,1)}, u32[]{:S(2)}, u32[]{:S(2)}) async-start(bf16[32,32,1024]{2,1,0:T(8,128)(2,1)} %bitcast.21), calls=%async_computation.1 | async-start | bytes 4194304 | tf_op jit(solution)/shard_map/all_to_all | solution.py:714
  42.0 2.4 %collective-permute-start.6 = (bf16[4,288,512]{2,1,0:T(8,128)(2,1)S(1)}, bf16[4,288,512]{2,1,0:T(8,128)(2,1)}, u32[]{:S(2)}, u32[]{:S(2)}) collective-permute-start(bf16[4,288,512]{2,1,0:T(8,128)(2,1)S(1)} %stack.25.refs_0_.after_ref.refs_6_), channel_id=1, source_target_pairs={{0,48},{1,13},{2,50},{3,15},{4,52},{5,1},{6,54},{7,3},{8,56},{9,5}... | collective-permute-start | bytes 3538952 | tf_op jit(solution)/shard_map/ppermute | solution.py:681
  45.4 16.7 %collective-permute-done.5.refs_3_ = bf16[256,4608]{1,0:T(8,128)(2,1)} collective-permute-done((bf16[256,4608]{1,0:T(8,128)(2,1)}, bf16[256,4608]{1,0:T(8,128)(2,1)}, u32[]{:S(2)}, u32[]{:S(2)}) %collective-permute-start.5) | collective-permute-done | bytes 2359328 | tf_op jit(solution)/shard_map/ppermute | solution.py:727
  62.2 5.5 %multiply.1.after_ref.acc_hbm = f32[512,512]{1,0:T(8,128)} custom-call(s32[5]{0:T(128)} %stack.24.here_ref.refs_0_, bf16[4,288,512]{2,1,0:T(8,128)(2,1)} %copy-done.1, bf16[4,288,512]{2,1,0:T(8,128)(2,1)} %copy-done.9, bf16[256,4608]{1,0:T(8,128)(2,1)} %get-tuple-element.53.refs_2_, bf16[256,4608]{1,0:T(8,128)(2,1)} %collective-permute-done.5.refs_3_), custom_call_target="tpu_custom_call" | custom-call | tf_op jit(solution)/shard_map/multiply/pallas_call | solution.py:273
  67.7 12.8 %all-to-all-done.1 = bf16[32,32,1024]{2,1,0:T(8,128)(2,1)} async-done(((bf16[32,32,1024]{2,1,0:T(8,128)(2,1)}), bf16[32,32,1024]{2,1,0:T(8,128)(2,1)}, u32[]{:S(2)}, u32[]{:S(2)}) %all-to-all-start.1) | async-done | bytes 2097184 | tf_op jit(solution)/shard_map/all_to_all | solution.py:714
  80.5 1.2 copy-done.4
  81.7 3.0 %unpack.1 = (bf16[512,512]{1,0:T(8,128)(2,1)S(1)}, bf16[512,512]{1,0:T(8,128)(2,1)S(1)}) custom-call(s32[512,1]{1,0:T(8,128)S(1)} %copy.28.slot_ref, bf16[1024,1024]{1,0:T(8,128)(2,1)} %bitcast.17.came_ref, f32[512,512]{1,0:T(8,128)S(1)} %copy-done.4), custom_call_target="tpu_custom_call" | custom-call | tf_op jit(solution)/shard_map/unpack/pallas_call | solution.py:169
  84.7 5.1 %merge.1 = (bf16[512,512]{1,0:T(8,128)(2,1)S(1)}, f32[512,512]{1,0:T(8,128)S(1)}, f32[8,512]{1,0:T(8,128)S(1)}) custom-call(s32[5]{0:T(128)S(1)} %copy-done.22, bf16[1,512]{1,0:T(2,128)(2,1)S(1)} %constant_dynamic-slice_fusion.1.ngain_ref.refs_1_, f32[512,512]{1,0:T(8,128)S(1)} %copy-done.5, bf16[512,512]{1,0:T(8,128)(2,1)S(1)} %get-tuple-element.55.base_hbm, ...), custom_call_target="tpu_custom_call" | custom-call | tf_op jit(solution)/shard_map/merge/pallas_call | solution.py:315
  89.9 1.2 collective-permute-done.8.got_ref
  91.1 2.6 %collective-permute-start.10 = (f32[8,512]{1,0:T(8,128)S(1)}, f32[8,512]{1,0:T(8,128)S(1)}, u32[]{:S(2)}, u32[]{:S(2)}) collective-permute-start(f32[8,512]{1,0:T(8,128)S(1)} %get-tuple-element.62.after_ref.refs_2_), channel_id=1, source_target_pairs={{0,2},{1,3},{2,0},{3,1},{64,66},{65,67},{66,64},{67,65},{4,6},{5,7... | collective-permute-start | bytes 49160 | tf_op jit(solution)/shard_map/ppermute | solution.py:669
  93.7 3.2 %collective-permute-start.11 = (f32[8,512]{1,0:T(8,128)S(1)}, f32[8,512]{1,0:T(8,128)S(1)}, u32[]{:S(2)}, u32[]{:S(2)}) collective-permute-start(f32[8,512]{1,0:T(8,128)S(1)} %get-tuple-element.61), channel_id=1, source_target_pairs={{0,66},{1,67},{2,64},{3,65},{64,0},{65,1},{66,2},{67,3},{4,70},{5,... | collective-permute-start | bytes 49160 | tf_op jit(solution)/shard_map/ppermute | solution.py:669
  97.0 1.4 pack.1
  98.4 2.4 %collective-permute-done.9.refs_3_ = f32[8,512]{1,0:T(8,128)S(1)} collective-permute-done((f32[8,512]{1,0:T(8,128)S(1)}, f32[8,512]{1,0:T(8,128)S(1)}, u32[]{:S(2)}, u32[]{:S(2)}) %collective-permute-start.9) | collective-permute-done | bytes 16416 | tf_op jit(solution)/shard_map/ppermute | solution.py:669
  100.8 5.5 %backward.1 = (bf16[64,4608]{1,0:T(8,128)(2,1)S(1)}, bf16[192,4608]{1,0:T(8,128)(2,1)S(1)}, bf16[64,4608]{1,0:T(8,128)(2,1)S(1)}, bf16[192,4608]{1,0:T(8,128)(2,1)S(1)}) custom-call(s32[5]{0:T(128)S(1)} %copy-done.22, bf16[1,512]{1,0:T(2,128)(2,1)S(1)} %constant_dynamic-slice_fusion.1.ngain_ref.refs_1_, f32[8,512]{1,0:T(8,128)S(1)} %get-tuple-element.62.after_ref.refs_2_, ...), custom_call_target="tpu_custom_call" | custom-call | tf_op jit(solution)/shard_map/backward/pallas_call | solution.py:454
  106.3 5.8 %collective-permute-done.12.after_ref.crossed_ref = bf16[512,512]{1,0:T(8,128)(2,1)S(1)} collective-permute-done((bf16[512,512]{1,0:T(8,128)(2,1)S(1)}, bf16[512,512]{1,0:T(8,128)(2,1)S(1)}, u32[]{:S(2)}, u32[]{:S(2)}) %collective-permute-start.12) | collective-permute-done | bytes 524320 | tf_op jit(solution)/shard_map/ppermute | solution.py:738
  112.1 3.0 %collective-permute-start.14 = (bf16[192,4608]{1,0:T(8,128)(2,1)S(1)}, bf16[192,4608]{1,0:T(8,128)(2,1)S(1)}, u32[]{:S(2)}, u32[]{:S(2)}) collective-permute-start(bf16[192,4608]{1,0:T(8,128)(2,1)S(1)} %get-tuple-element.75), channel_id=1, source_target_pairs={{0,1},{1,0},{2,3},{3,2},{4,5},{5,4},{6,7},{7,6},{8,9},{9,8},{10,11... | collective-permute-start | bytes 5308424 | tf_op jit(solution)/shard_map/ppermute | solution.py:744
  115.1 3.3 %collective-permute-done.14.got_ref = bf16[192,4608]{1,0:T(8,128)(2,1)S(1)} collective-permute-done((bf16[192,4608]{1,0:T(8,128)(2,1)S(1)}, bf16[192,4608]{1,0:T(8,128)(2,1)S(1)}, u32[]{:S(2)}, u32[]{:S(2)}) %collective-permute-start.14) | collective-permute-done | bytes 1769504 | tf_op jit(solution)/shard_map/ppermute | solution.py:744
  118.4 1.2 pair.1
  119.7 1.2 copy-done.7
  120.9 2.7 %collective-permute-start.16 = (bf16[64,4608]{1,0:T(8,128)(2,1)}, bf16[64,4608]{1,0:T(8,128)(2,1)}, u32[]{:S(2)}, u32[]{:S(2)}) collective-permute-start(bf16[64,4608]{1,0:T(8,128)(2,1)} %get-tuple-element.78), channel_id=1, source_target_pairs={{0,66},{1,67},{2,64},{3,65},{64,0},{65,1},{66,2},{67,3},{4,70},{5,... | collective-permute-start | bytes 1769480 | tf_op jit(solution)/shard_map/ppermute | solution.py:669
  124.6 3.8 %all-to-all-start.2 = ((bf16[16,2,32,512]{3,2,1,0:T(8,128)(2,1)}), bf16[16,2,32,512]{3,2,1,0:T(8,128)(2,1)S(1)}, u32[]{:S(2)}, u32[]{:S(2)}) async-start(bf16[16,2,32,512]{3,2,1,0:T(8,128)(2,1)} %copy-done.11), calls=%async_computation.2 | async-start | bytes 2097152 | tf_op jit(solution)/shard_map/all_to_all | solution.py:752
  128.4 1.3 collective-permute-start.13
  129.7 7.3 %collective-permute-done.15.from_last_ref.early_ref = bf16[64,4608]{1,0:T(8,128)(2,1)} collective-permute-done((bf16[64,4608]{1,0:T(8,128)(2,1)}, bf16[64,4608]{1,0:T(8,128)(2,1)}, u32[]{:S(2)}, u32[]{:S(2)}) %collective-permute-start.15) | collective-permute-done | bytes 589856 | tf_op jit(solution)/shard_map/ppermute | solution.py:669
  136.9 1.5 copy-done.8
  138.4 1.6 relay.1
  140.0 2.4 %collective-permute-start.17 = (bf16[32,4608]{1,0:T(8,128)(2,1)S(1)}, bf16[32,4608]{1,0:T(8,128)(2,1)S(1)}, u32[]{:S(2)}, u32[]{:S(2)}) collective-permute-start(bf16[32,4608]{1,0:T(8,128)(2,1)S(1)} %get-tuple-element.79), channel_id=1, source_target_pairs={{0,66},{1,67},{2,64},{3,65},{64,0},{65,1},{66,2},{67,3},{4,70},{5,... | collective-permute-start | bytes 884744 | tf_op jit(solution)/shard_map/ppermute | solution.py:669
  142.4 4.9 %collective-permute-done.17.late_ref = bf16[32,4608]{1,0:T(8,128)(2,1)S(1)} collective-permute-done((bf16[32,4608]{1,0:T(8,128)(2,1)S(1)}, bf16[32,4608]{1,0:T(8,128)(2,1)S(1)}, u32[]{:S(2)}, u32[]{:S(2)}) %collective-permute-start.17) | collective-permute-done | bytes 294944 | tf_op jit(solution)/shard_map/ppermute | solution.py:669
  147.4 2.4 %finish.2.refs_1_ = bf16[128,1152]{1,0:T(8,128)(2,1)S(1)} custom-call(s32[5]{0:T(128)S(1)} %copy-done.22, bf16[64,4608]{1,0:T(8,128)(2,1)S(1)} %copy-done.17, bf16[64,4608]{1,0:T(8,128)(2,1)S(1)} %collective-permute-done.13.got_ref, bf16[64,4608]{1,0:T(8,128)(2,1)} %collective-permute-done.15.from_last_ref.early_ref, ...), custom_call_target="tpu_custom_call" | custom-call | tf_op jit(solution)/shard_map/finish/pallas_call | solution.py:560
  149.8 2.1 %collective-permute-start.18 = (bf16[128,1152]{1,0:T(8,128)(2,1)S(1)}, bf16[128,1152]{1,0:T(8,128)(2,1)}, u32[]{:S(2)}, u32[]{:S(2)}) collective-permute-start(bf16[128,1152]{1,0:T(8,128)(2,1)S(1)} %finish.2.refs_1_), channel_id=1, source_target_pairs={{0,2},{1,3},{2,0},{3,1},{4,6},{5,7},{6,4},{7,5},{8,10},{9,11},{10,... | collective-permute-start | bytes 884744 | tf_op jit(solution)/shard_map/ppermute | solution.py:759
  151.9 3.1 %finish.3.refs_0_ = bf16[128,1152]{1,0:T(8,128)(2,1)} custom-call(s32[5]{0:T(128)S(1)} %copy-done.22, bf16[64,4608]{1,0:T(8,128)(2,1)S(1)} %copy-done.17, bf16[64,4608]{1,0:T(8,128)(2,1)S(1)} %collective-permute-done.13.got_ref, bf16[64,4608]{1,0:T(8,128)(2,1)} %collective-permute-done.16.from_next_ref.early_ref, ...), custom_call_target="tpu_custom_call" | custom-call | tf_op jit(solution)/shard_map/finish/pallas_call | solution.py:560
  156.0 2.4 %place.1 = bf16[512,1024]{1,0:T(8,128)(2,1)} custom-call(s32[5]{0:T(128)S(1)} %copy-done.22, s32[512,1]{1,0:T(8,128)S(1)} %copy-done.15, bf16[16,2,32,512]{3,2,1,0:T(8,128)(2,1)S(1)} %all-to-all-done.2.came_ref, bf16[512,1024]{1,0:T(8,128)(2,1)S(1)} %copy-done.13), custom_call_target="tpu_custom_call" | custom-call | tf_op jit(solution)/shard_map/place/pallas_call | solution.py:601
  158.4 2.8 %collective-permute-start.21 = (bf16[128,1152]{1,0:T(8,128)(2,1)}, bf16[128,1152]{1,0:T(8,128)(2,1)S(1)}, u32[]{:S(2)}, u32[]{:S(2)}) collective-permute-start(bf16[128,1152]{1,0:T(8,128)(2,1)} %finish.3.refs_0_), channel_id=1, source_target_pairs={{0,1},{1,0},{2,3},{3,2},{4,5},{5,4},{6,7},{7,6},{8,9},{9,8},{10,11... | collective-permute-start | bytes 884744 | tf_op jit(solution)/shard_map/ppermute | solution.py:761
  161.2 3.6 %collective-permute-done.20.refs_2_ = bf16[128,1152]{1,0:T(8,128)(2,1)} collective-permute-done((bf16[128,1152]{1,0:T(8,128)(2,1)}, bf16[128,1152]{1,0:T(8,128)(2,1)}, u32[]{:S(2)}, u32[]{:S(2)}) %collective-permute-start.20) | collective-permute-done | bytes 294944 | tf_op jit(solution)/shard_map/ppermute | solution.py:759
  164.8 2.4 %collective-permute-start.23 = (bf16[128,1152]{1,0:T(8,128)(2,1)}, bf16[128,1152]{1,0:T(8,128)(2,1)S(1)}, u32[]{:S(2)}, u32[]{:S(2)}) collective-permute-start(bf16[128,1152]{1,0:T(8,128)(2,1)} %collective-permute-done.20.refs_2_), channel_id=1, source_target_pairs={{0,1},{1,0},{2,3},{3,2},{4,5},{5,4},{6,7},{7,6},{8,9},{9,8},{10,11... | collective-permute-start | bytes 884744 | tf_op jit(solution)/shard_map/ppermute | solution.py:761
  167.3 1.4 collective-permute-done.23.refs_6_
  169.1 2.6 %lay.1 = bf16[1024,1152]{1,0:T(8,128)(2,1)} custom-call(s32[5]{0:T(128)S(1)} %copy-done.22, bf16[128,1152]{1,0:T(8,128)(2,1)} %finish.3.refs_0_, bf16[128,1152]{1,0:T(8,128)(2,1)S(1)} %finish.2.refs_1_, bf16[128,1152]{1,0:T(8,128)(2,1)} %collective-permute-done.20.refs_2_, bf16[128,1152]{1,0:T(8,128)(2,1)} %collective-permute-done.18.refs_3_, ...), custom_call_target="tpu_custom_call" | custom-call | tf_op jit(solution)/shard_map/lay/pallas_call | solution.py:629
  (87 shorter events, 8.2 us)
Async XLA Ops:
  1.7 24.4 %collective-permute-start = (bf16[288,512]{1,0:T(8,128)(2,1)S(1)}, bf16[288,512]{1,0:T(8,128)(2,1)S(1)}, u32[]{:S(2)}, u32[]{:S(2)}) collective-permute-start(bf16[288,512]{1,0:T(8,128)(2,1)S(1)} %bitcast.22), channel_id=1, source_target_pairs={{0,4},{1,17},{2,6},{3,19},{4,8},{5,21},{6,10},{7,23},{8,12},{9,25}... | collective-permute-start | bytes 884744 | tf_op jit(solution)/shard_map/ppermute | solution.py:681
  4.3 21.8 %collective-permute-start.1 = (bf16[288,512]{1,0:T(8,128)(2,1)S(1)}, bf16[288,512]{1,0:T(8,128)(2,1)S(1)}, u32[]{:S(2)}, u32[]{:S(2)}) collective-permute-start(bf16[288,512]{1,0:T(8,128)(2,1)S(1)} %bitcast.23), channel_id=1, source_target_pairs={{0,12},{1,49},{2,14},{3,51},{4,0},{5,53},{6,2},{7,55},{8,4},{9,57}... | collective-permute-start | bytes 884744 | tf_op jit(solution)/shard_map/ppermute | solution.py:681
  6.5 19.6 %collective-permute-start.2 = (bf16[288,512]{1,0:T(8,128)(2,1)S(1)}, bf16[288,512]{1,0:T(8,128)(2,1)S(1)}, u32[]{:S(2)}, u32[]{:S(2)}) collective-permute-start(bf16[288,512]{1,0:T(8,128)(2,1)S(1)} %bitcast.24), channel_id=1, source_target_pairs={{0,8},{1,33},{2,10},{3,35},{4,12},{5,37},{6,14},{7,39},{8,0},{9,41... | collective-permute-start | bytes 884744 | tf_op jit(solution)/shard_map/ppermute | solution.py:681
  9.5 16.6 %all-to-all-start = ((s32[32,1,16]{2,1,0:T(1,128)}), s32[32,1,16]{2,1,0:T(1,128)S(1)}, u32[]{:S(2)}, u32[]{:S(2)}) async-start(s32[32,1,16]{2,1,0:T(1,128)} %bitcast.5), calls=%async_computation | async-start | bytes 32768 | tf_op jit(solution)/shard_map/all_to_all | solution.py:693
  16.5 9.6 %collective-permute-start.3 = (s32[256]{0:T(256)S(1)}, s32[256]{0:T(256)S(1)}, u32[]{:S(2)}, u32[]{:S(2)}) collective-permute-start(s32[256]{0:T(256)S(1)} %get-tuple-element.88), channel_id=1, source_target_pairs={{0,64},{64,0},{1,65},{65,1},{2,66},{66,2},{3,67},{67,3},{4,68},{68... | collective-permute-start | bytes 3080 | tf_op jit(solution)/shard_map/ppermute | solution.py:700
  18.5 7.6 %copy-start.21 = (s32[5]{0:T(128)S(1)}, s32[5]{0:T(128)}, u32[]{:S(2)}) copy-start(s32[5]{0:T(128)} %stack.24.here_ref.refs_0_) | copy-start | bytes 64
  27.0 15.0 %copy-start.1 = (bf16[4,288,512]{2,1,0:T(8,128)(2,1)}, bf16[4,288,512]{2,1,0:T(8,128)(2,1)S(1)}, u32[]{:S(2)}) copy-start(bf16[4,288,512]{2,1,0:T(8,128)(2,1)S(1)} %stack.25.refs_0_.after_ref.refs_6_) | copy-start | bytes 3538948
  27.0 35.2 %collective-permute-start.5 = (bf16[256,4608]{1,0:T(8,128)(2,1)}, bf16[256,4608]{1,0:T(8,128)(2,1)}, u32[]{:S(2)}, u32[]{:S(2)}) collective-permute-start(bf16[256,4608]{1,0:T(8,128)(2,1)} %get-tuple-element.53.refs_2_), channel_id=1, source_target_pairs={{0,64},{1,67},{2,66},{3,65},{64,2},{65,1},{66,0},{67,3},{4,68},{5,... | collective-permute-start | bytes 7077896 | tf_op jit(solution)/shard_map/ppermute | solution.py:727
  28.6 16.7 %collective-permute-start.4 = (bf16[4,288,512]{2,1,0:T(8,128)(2,1)S(1)}, bf16[4,288,512]{2,1,0:T(8,128)(2,1)S(1)}, u32[]{:S(2)}, u32[]{:S(2)}) collective-permute-start(bf16[4,288,512]{2,1,0:T(8,128)(2,1)S(1)} %stack.25.refs_0_.after_ref.refs_6_), channel_id=1, source_target_pairs={{0,16},{1,5},{2,18},{3,7},{4,20},{5,9},{6,22},{7,11},{8,24},{9,13}... | collective-permute-start | bytes 3538952 | tf_op jit(solution)/shard_map/ppermute | solution.py:681
  30.0 3.9 %copy-start.14 = (s32[512,1]{1,0:T(8,128)}, s32[512,1]{1,0:T(8,128)S(1)}, u32[]{:S(2)}) copy-start(s32[512,1]{1,0:T(8,128)S(1)} %reshape.38.pos_ref) | copy-start | bytes 6148
  30.0 1.3 copy-start.12
  33.8 1.4 copy-start.6
  35.2 10.0 %copy-start.24 = (bf16[1,1024]{1,0:T(2,128)(2,1)S(1)}, bf16[1,1024]{1,0:T(2,128)(2,1)}, u32[]{:S(2)}) copy-start(bf16[1,1024]{1,0:T(2,128)(2,1)} %param.13) | copy-start | bytes 6148
  35.2 45.2 %all-to-all-start.1 = ((bf16[32,32,1024]{2,1,0:T(8,128)(2,1)}), bf16[32,32,1024]{2,1,0:T(8,128)(2,1)}, u32[]{:S(2)}, u32[]{:S(2)}) async-start(bf16[32,32,1024]{2,1,0:T(8,128)(2,1)} %bitcast.21), calls=%async_computation.1 | async-start | bytes 4194304 | tf_op jit(solution)/shard_map/all_to_all | solution.py:714
  42.0 42.7 %collective-permute-start.6 = (bf16[4,288,512]{2,1,0:T(8,128)(2,1)S(1)}, bf16[4,288,512]{2,1,0:T(8,128)(2,1)}, u32[]{:S(2)}, u32[]{:S(2)}) collective-permute-start(bf16[4,288,512]{2,1,0:T(8,128)(2,1)S(1)} %stack.25.refs_0_.after_ref.refs_6_), channel_id=1, source_target_pairs={{0,48},{1,13},{2,50},{3,15},{4,52},{5,1},{6,54},{7,3},{8,56},{9,5}... | collective-permute-start | bytes 3538952 | tf_op jit(solution)/shard_map/ppermute | solution.py:681
  45.2 16.9 %copy-start.9 = (bf16[4,288,512]{2,1,0:T(8,128)(2,1)}, bf16[4,288,512]{2,1,0:T(8,128)(2,1)S(1)}, u32[]{:S(2)}) copy-start(bf16[4,288,512]{2,1,0:T(8,128)(2,1)S(1)} %collective-permute-done.4.refs_1_.refs_7_) | copy-start | bytes 3538948
  45.2 39.5 %collective-permute-start.7 = (bf16[4,288,512]{2,1,0:T(8,128)(2,1)S(1)}, bf16[4,288,512]{2,1,0:T(8,128)(2,1)}, u32[]{:S(2)}, u32[]{:S(2)}) collective-permute-start(bf16[4,288,512]{2,1,0:T(8,128)(2,1)S(1)} %collective-permute-done.4.refs_1_.refs_7_), channel_id=1, source_target_pairs={{0,16},{1,5},{2,18},{3,7},{4,20},{5,9},{6,22},{7,11},{8,24},{9,13}... | collective-permute-start | bytes 3538952 | tf_op jit(solution)/shard_map/ppermute | solution.py:681
  67.7 17.0 %copy-start.22 = (s32[5]{0:T(128)S(1)}, s32[5]{0:T(128)}, u32[]{:S(2)}) copy-start(s32[5]{0:T(128)} %stack.24.here_ref.refs_0_) | copy-start | bytes 64
  81.7 3.0 %copy-start.5 = (f32[512,512]{1,0:T(8,128)S(1)}, f32[512,512]{1,0:T(8,128)}, u32[]{:S(2)}) copy-start(f32[512,512]{1,0:T(8,128)} %multiply.1.after_ref.acc_hbm) | copy-start | bytes 3145732
  84.7 16.0 %copy-start.2 = (bf16[4,288,512]{2,1,0:T(8,128)(2,1)S(1)}, bf16[4,288,512]{2,1,0:T(8,128)(2,1)}, u32[]{:S(2)}) copy-start(bf16[4,288,512]{2,1,0:T(8,128)(2,1)} %copy-done.1) | copy-start | bytes 3538948
  84.7 16.0 %copy-start.10 = (bf16[4,288,512]{2,1,0:T(8,128)(2,1)S(1)}, bf16[4,288,512]{2,1,0:T(8,128)(2,1)}, u32[]{:S(2)}) copy-start(bf16[4,288,512]{2,1,0:T(8,128)(2,1)} %copy-done.9) | copy-start | bytes 3538948
  89.8 1.3 collective-permute-start.8
  91.1 7.3 %collective-permute-start.10 = (f32[8,512]{1,0:T(8,128)S(1)}, f32[8,512]{1,0:T(8,128)S(1)}, u32[]{:S(2)}, u32[]{:S(2)}) collective-permute-start(f32[8,512]{1,0:T(8,128)S(1)} %get-tuple-element.62.after_ref.refs_2_), channel_id=1, source_target_pairs={{0,2},{1,3},{2,0},{3,1},{64,66},{65,67},{66,64},{67,65},{4,6},{5,7... | collective-permute-start | bytes 49160 | tf_op jit(solution)/shard_map/ppermute | solution.py:669
  93.7 4.7 %collective-permute-start.11 = (f32[8,512]{1,0:T(8,128)S(1)}, f32[8,512]{1,0:T(8,128)S(1)}, u32[]{:S(2)}, u32[]{:S(2)}) collective-permute-start(f32[8,512]{1,0:T(8,128)S(1)} %get-tuple-element.61), channel_id=1, source_target_pairs={{0,66},{1,67},{2,64},{3,65},{64,0},{65,1},{66,2},{67,3},{4,70},{5,... | collective-permute-start | bytes 49160 | tf_op jit(solution)/shard_map/ppermute | solution.py:669
  97.0 3.8 %collective-permute-start.9 = (f32[8,512]{1,0:T(8,128)S(1)}, f32[8,512]{1,0:T(8,128)S(1)}, u32[]{:S(2)}, u32[]{:S(2)}) collective-permute-start(f32[8,512]{1,0:T(8,128)S(1)} %get-tuple-element.61), channel_id=1, source_target_pairs={{0,64},{1,65},{2,66},{3,67},{64,2},{65,3},{66,0},{67,1},{4,68},{5,... | collective-permute-start | bytes 49160 | tf_op jit(solution)/shard_map/ppermute | solution.py:669
  100.8 11.4 %collective-permute-start.12 = (bf16[512,512]{1,0:T(8,128)(2,1)S(1)}, bf16[512,512]{1,0:T(8,128)(2,1)S(1)}, u32[]{:S(2)}, u32[]{:S(2)}) collective-permute-start(bf16[512,512]{1,0:T(8,128)(2,1)S(1)} %get-tuple-element.71), channel_id=1, source_target_pairs={{0,64},{64,0},{1,65},{65,1},{2,66},{66,2},{3,67},{67,3},{4,68},{68... | collective-permute-start | bytes 1572872 | tf_op jit(solution)/shard_map/ppermute | solution.py:738
  106.3 17.2 %copy-start.16 = (bf16[64,4608]{1,0:T(8,128)(2,1)}, bf16[64,4608]{1,0:T(8,128)(2,1)S(1)}, u32[]{:S(2)}) copy-start(bf16[64,4608]{1,0:T(8,128)(2,1)S(1)} %get-tuple-element.72.own_ref) | copy-start | bytes 1769476
  106.3 17.2 %copy-start.23 = (bf16[64,4608]{1,0:T(8,128)(2,1)}, bf16[64,4608]{1,0:T(8,128)(2,1)S(1)}, u32[]{:S(2)}) copy-start(bf16[64,4608]{1,0:T(8,128)(2,1)S(1)} %get-tuple-element.73) | copy-start | bytes 1769476
  112.1 6.3 %collective-permute-start.14 = (bf16[192,4608]{1,0:T(8,128)(2,1)S(1)}, bf16[192,4608]{1,0:T(8,128)(2,1)S(1)}, u32[]{:S(2)}, u32[]{:S(2)}) collective-permute-start(bf16[192,4608]{1,0:T(8,128)(2,1)S(1)} %get-tuple-element.75), channel_id=1, source_target_pairs={{0,1},{1,0},{2,3},{3,2},{4,5},{5,4},{6,7},{7,6},{8,9},{9,8},{10,11... | collective-permute-start | bytes 5308424 | tf_op jit(solution)/shard_map/ppermute | solution.py:744
  120.9 16.1 %collective-permute-start.15 = (bf16[64,4608]{1,0:T(8,128)(2,1)}, bf16[64,4608]{1,0:T(8,128)(2,1)}, u32[]{:S(2)}, u32[]{:S(2)}) collective-permute-start(bf16[64,4608]{1,0:T(8,128)(2,1)} %get-tuple-element.77), channel_id=1, source_target_pairs={{0,64},{1,65},{2,66},{3,67},{64,2},{65,3},{66,0},{67,1},{4,68},{5,... | collective-permute-start | bytes 1769480 | tf_op jit(solution)/shard_map/ppermute | solution.py:669
  120.9 16.1 %collective-permute-start.16 = (bf16[64,4608]{1,0:T(8,128)(2,1)}, bf16[64,4608]{1,0:T(8,128)(2,1)}, u32[]{:S(2)}, u32[]{:S(2)}) collective-permute-start(bf16[64,4608]{1,0:T(8,128)(2,1)} %get-tuple-element.78), channel_id=1, source_target_pairs={{0,66},{1,67},{2,64},{3,65},{64,0},{65,1},{66,2},{67,3},{4,70},{5,... | collective-permute-start | bytes 1769480 | tf_op jit(solution)/shard_map/ppermute | solution.py:669
  124.6 22.8 %copy-start.19 = (f32[256,128]{1,0:T(8,128)S(1)}, f32[256,128]{1,0:T(8,128)}, u32[]{:S(2)}) copy-start(f32[256,128]{1,0:T(8,128)} %get-tuple-element.81.stat_ref) | copy-start | bytes 393220
  124.6 22.8 %copy-start.20 = (bf16[1,4,1152]{2,1,0:T(4,128)(2,1)S(1)}, bf16[1,4,1152]{2,1,0:T(4,128)(2,1)}, u32[]{:S(2)}) copy-start(bf16[1,4,1152]{2,1,0:T(4,128)(2,1)} %param.9) | copy-start | bytes 27652
  124.6 31.4 %all-to-all-start.2 = ((bf16[16,2,32,512]{3,2,1,0:T(8,128)(2,1)}), bf16[16,2,32,512]{3,2,1,0:T(8,128)(2,1)S(1)}, u32[]{:S(2)}, u32[]{:S(2)}) async-start(bf16[16,2,32,512]{3,2,1,0:T(8,128)(2,1)} %copy-done.11), calls=%async_computation.2 | async-start | bytes 2097152 | tf_op jit(solution)/shard_map/all_to_all | solution.py:752
  128.4 19.0 %copy-start.3 = (bf16[4,256,1152]{2,1,0:T(8,128)(2,1)S(1)}, bf16[4,256,1152]{2,1,0:T(8,128)(2,1)}, u32[]{:S(2)}) copy-start(bf16[4,256,1152]{2,1,0:T(8,128)(2,1)} %get-tuple-element.80.xw_ref) | copy-start | bytes 7077892
  128.4 14.0 %collective-permute-start.13 = (bf16[64,4608]{1,0:T(8,128)(2,1)}, bf16[64,4608]{1,0:T(8,128)(2,1)S(1)}, u32[]{:S(2)}, u32[]{:S(2)}) collective-permute-start(bf16[64,4608]{1,0:T(8,128)(2,1)} %copy-done.23), channel_id=1, source_target_pairs={{0,1},{1,0},{2,3},{3,2},{4,5},{5,4},{6,7},{7,6},{8,9},{9,8},{10,11... | collective-permute-start | bytes 1769480 | tf_op jit(solution)/shard_map/ppermute | solution.py:745
  136.9 1.5 copy-start.8
  138.4 9.0 %copy-start.17 = (bf16[64,4608]{1,0:T(8,128)(2,1)S(1)}, bf16[64,4608]{1,0:T(8,128)(2,1)}, u32[]{:S(2)}) copy-start(bf16[64,4608]{1,0:T(8,128)(2,1)} %copy-done.16) | copy-start | bytes 1769476
  140.0 7.4 %collective-permute-start.17 = (bf16[32,4608]{1,0:T(8,128)(2,1)S(1)}, bf16[32,4608]{1,0:T(8,128)(2,1)S(1)}, u32[]{:S(2)}, u32[]{:S(2)}) collective-permute-start(bf16[32,4608]{1,0:T(8,128)(2,1)S(1)} %get-tuple-element.79), channel_id=1, source_target_pairs={{0,66},{1,67},{2,64},{3,65},{64,0},{65,1},{66,2},{67,3},{4,70},{5,... | collective-permute-start | bytes 884744 | tf_op jit(solution)/shard_map/ppermute | solution.py:669
  142.4 9.5 %collective-permute-start.19 = (bf16[32,4608]{1,0:T(8,128)(2,1)S(1)}, bf16[32,4608]{1,0:T(8,128)(2,1)S(1)}, u32[]{:S(2)}, u32[]{:S(2)}) collective-permute-start(bf16[32,4608]{1,0:T(8,128)(2,1)S(1)} %get-tuple-element.84), channel_id=1, source_target_pairs={{0,64},{1,65},{2,66},{3,67},{64,2},{65,3},{66,0},{67,1},{4,68},{5,... | collective-permute-start | bytes 884744 | tf_op jit(solution)/shard_map/ppermute | solution.py:669
  149.8 6.2 %copy-start.13 = (bf16[512,1024]{1,0:T(8,128)(2,1)S(1)}, bf16[512,1024]{1,0:T(8,128)(2,1)}, u32[]{:S(2)}) copy-start(bf16[512,1024]{1,0:T(8,128)(2,1)} %stream_ref.3) | copy-start | bytes 3145732
  149.8 6.2 %copy-start.15 = (s32[512,1]{1,0:T(8,128)S(1)}, s32[512,1]{1,0:T(8,128)}, u32[]{:S(2)}) copy-start(s32[512,1]{1,0:T(8,128)} %copy-done.14) | copy-start | bytes 6148
  149.8 11.4 %collective-permute-start.18 = (bf16[128,1152]{1,0:T(8,128)(2,1)S(1)}, bf16[128,1152]{1,0:T(8,128)(2,1)}, u32[]{:S(2)}, u32[]{:S(2)}) collective-permute-start(bf16[128,1152]{1,0:T(8,128)(2,1)S(1)} %finish.2.refs_1_), channel_id=1, source_target_pairs={{0,2},{1,3},{2,0},{3,1},{4,6},{5,7},{6,4},{7,5},{8,10},{9,11},{10,... | collective-permute-start | bytes 884744 | tf_op jit(solution)/shard_map/ppermute | solution.py:759
  155.1 9.8 %collective-permute-start.20 = (bf16[128,1152]{1,0:T(8,128)(2,1)}, bf16[128,1152]{1,0:T(8,128)(2,1)}, u32[]{:S(2)}, u32[]{:S(2)}) collective-permute-start(bf16[128,1152]{1,0:T(8,128)(2,1)} %finish.3.refs_0_), channel_id=1, source_target_pairs={{0,2},{1,3},{2,0},{3,1},{4,6},{5,7},{6,4},{7,5},{8,10},{9,11},{10,... | collective-permute-start | bytes 884744 | tf_op jit(solution)/shard_map/ppermute | solution.py:759
  158.4 8.9 %collective-permute-start.21 = (bf16[128,1152]{1,0:T(8,128)(2,1)}, bf16[128,1152]{1,0:T(8,128)(2,1)S(1)}, u32[]{:S(2)}, u32[]{:S(2)}) collective-permute-start(bf16[128,1152]{1,0:T(8,128)(2,1)} %finish.3.refs_0_), channel_id=1, source_target_pairs={{0,1},{1,0},{2,3},{3,2},{4,5},{5,4},{6,7},{7,6},{8,9},{9,8},{10,11... | collective-permute-start | bytes 884744 | tf_op jit(solution)/shard_map/ppermute | solution.py:761
  161.2 6.1 %collective-permute-start.22 = (bf16[128,1152]{1,0:T(8,128)(2,1)S(1)}, bf16[128,1152]{1,0:T(8,128)(2,1)S(1)}, u32[]{:S(2)}, u32[]{:S(2)}) collective-permute-start(bf16[128,1152]{1,0:T(8,128)(2,1)S(1)} %finish.2.refs_1_), channel_id=1, source_target_pairs={{0,1},{1,0},{2,3},{3,2},{4,5},{5,4},{6,7},{7,6},{8,9},{9,8},{10,11... | collective-permute-start | bytes 884744 | tf_op jit(solution)/shard_map/ppermute | solution.py:761
  164.8 3.8 %collective-permute-start.23 = (bf16[128,1152]{1,0:T(8,128)(2,1)}, bf16[128,1152]{1,0:T(8,128)(2,1)S(1)}, u32[]{:S(2)}, u32[]{:S(2)}) collective-permute-start(bf16[128,1152]{1,0:T(8,128)(2,1)} %collective-permute-done.20.refs_2_), channel_id=1, source_target_pairs={{0,1},{1,0},{2,3},{3,2},{4,5},{5,4},{6,7},{7,6},{8,9},{9,8},{10,11... | collective-permute-start | bytes 884744 | tf_op jit(solution)/shard_map/ppermute | solution.py:761
  167.3 1.8 %collective-permute-start.24 = (bf16[128,1152]{1,0:T(8,128)(2,1)}, bf16[128,1152]{1,0:T(8,128)(2,1)S(1)}, u32[]{:S(2)}, u32[]{:S(2)}) collective-permute-start(bf16[128,1152]{1,0:T(8,128)(2,1)} %collective-permute-done.18.refs_3_), channel_id=1, source_target_pairs={{0,1},{1,0},{2,3},{3,2},{4,5},{5,4},{6,7},{7,6},{8,9},{9,8},{10,11... | collective-permute-start | bytes 884744 | tf_op jit(solution)/shard_map/ppermute | solution.py:761
  (5 other events, 5.7 us)

commit v21 on v20

--- a/solution.py
+++ b/solution.py
@@ -92,7 +92,7 @@
     rows, width = features.shape
     window = gain.shape[0]
     merged = rows // window
-    block = 64
+    block = 32
     steps = merged // block
     return pl.pallas_call(
         norm_kernel,

time: 173 us -> 175 us (1.012)
  Pallas kernels: 43.6 us -> 45.6 us
    pallas_call x1, Pallas kernels: 7.6 us -> 9.6 us  [layer_norm(): pl.pallas_call(norm_kernel, grid_spec=pltpu.PrefetchScalarGridSpec(num_sc...]
  transfers between devices with their start and end apart: 28 -> 28, of which waited for: 12 -> 12; matrix products, arithmetic and copies ran while one was open for 1% -> 1% of each run, Pallas kernels for 20% -> 21%
where the time goes in v21:
time: 175 us; the launch traced here: 174 us
  waiting for transfers between devices  60.7 us (35%)
  starting transfers between devices  53.6 us (31%)
  Pallas kernels  45.6 us (26%)
  local copies, waits for them, and re-layouts  11.6 us (7%)
    ppermute x1, waiting for transfers between devices, shards(): lifted = [lifted, lax.ppermute(lifted, ('img', 'tp'), pairs)]  16.8 us
    ppermute x7, waiting for transfers between devices, along_x(): return lax.ppermute(array, ('img', 'tp'), pairs)  14.6 us
    all_to_all x1, waiting for transfers between devices, shards(): lax.all_to_all(held.reshape(owners, n_img * capacity, width), ('img', 'ct...  12.8 us
    ppermute x7, starting transfers between devices, along_x(): return lax.ppermute(array, ('img', 'tp'), pairs)  10.9 us
    unnamed x50, local copies, waits for them, and re-layouts  9.94 us
    ppermute x6, starting transfers between devices, along_ctx(): return lax.ppermute(array, ('ctx', 'tp'), pairs)  9.66 us
    pallas_call x1, Pallas kernels, layer_norm(): pl.pallas_call(norm_kernel, grid_spec=pltpu.PrefetchScalarGridSpec(num_sc...  9.6 us
    all_to_all x1, starting transfers between devices, shards(): lax.all_to_all(packed.reshape(owners, capacity), ('img', 'ctx'), split_ax...  6.97 us
  transfers between devices with their start and end apart: 28, of which 12 were waited for; matrix products, arithmetic and copies ran while one was open for 1% of the time, Pallas kernels for 21%

profile of v21, /device:TPU:1, one launch (start us, length us, event | category | flops | bytes accessed | tf_op | source)
XLA Modules:
  0.0 173.8 jit_solution(5366117749359648166)
XLA Ops:
  1.7 2.5 %collective-permute-start = (bf16[288,512]{1,0:T(8,128)(2,1)S(1)}, bf16[288,512]{1,0:T(8,128)(2,1)S(1)}, u32[]{:S(2)}, u32[]{:S(2)}) collective-permute-start(bf16[288,512]{1,0:T(8,128)(2,1)S(1)} %bitcast.22), channel_id=1, source_target_pairs={{0,4},{1,17},{2,6},{3,19},{4,8},{5,21},{6,10},{7,23},{8,12},{9,25}... | collective-permute-start | bytes 884744 | tf_op jit(solution)/shard_map/ppermute | solution.py:681
  4.3 2.2 %collective-permute-start.1 = (bf16[288,512]{1,0:T(8,128)(2,1)S(1)}, bf16[288,512]{1,0:T(8,128)(2,1)S(1)}, u32[]{:S(2)}, u32[]{:S(2)}) collective-permute-start(bf16[288,512]{1,0:T(8,128)(2,1)S(1)} %bitcast.23), channel_id=1, source_target_pairs={{0,12},{1,49},{2,14},{3,51},{4,0},{5,53},{6,2},{7,55},{8,4},{9,57}... | collective-permute-start | bytes 884744 | tf_op jit(solution)/shard_map/ppermute | solution.py:681
  6.5 1.2 collective-permute-start.2
  9.5 7.0 %all-to-all-start = ((s32[32,1,16]{2,1,0:T(1,128)}), s32[32,1,16]{2,1,0:T(1,128)S(1)}, u32[]{:S(2)}, u32[]{:S(2)}) async-start(s32[32,1,16]{2,1,0:T(1,128)} %bitcast.5), calls=%async_computation | async-start | bytes 32768 | tf_op jit(solution)/shard_map/all_to_all | solution.py:693
  16.5 1.3 collective-permute-start.3
  18.5 9.6 %layer_norm.1 = (bf16[256,4608]{1,0:T(8,128)(2,1)}, bf16[4,256,1152]{2,1,0:T(8,128)(2,1)}, f32[256,128]{1,0:T(8,128)}) custom-call(s32[5]{0:T(128)} %stack.24.here_ref.refs_0_, bf16[1024,1152]{1,0:T(8,128)(2,1)} %bitcast.30, bf16[4,1152]{1,0:T(4,128)(2,1)} %bitcast.27, bf16[4,1152]{1,0:T(4,128)(2,1)} %bitcast.34), custom_call_target="tpu_custom_call" | custom-call | tf_op jit(solution)/shard_map/layer_norm/pallas_call | solution.py:97
  29.0 1.6 collective-permute-start.5
  30.6 1.2 collective-permute-start.4
  32.0 1.3 copy-done.12
  33.3 1.2 copy-done.18
  34.5 1.3 collect.1
  35.9 1.4 copy-done.6
  37.3 6.7 %all-to-all-start.1 = ((bf16[32,32,1024]{2,1,0:T(8,128)(2,1)}), bf16[32,32,1024]{2,1,0:T(8,128)(2,1)}, u32[]{:S(2)}, u32[]{:S(2)}) async-start(bf16[32,32,1024]{2,1,0:T(8,128)(2,1)} %bitcast.21), calls=%async_computation.1 | async-start | bytes 4194304 | tf_op jit(solution)/shard_map/all_to_all | solution.py:714
  44.0 2.4 %collective-permute-start.6 = (bf16[4,288,512]{2,1,0:T(8,128)(2,1)S(1)}, bf16[4,288,512]{2,1,0:T(8,128)(2,1)}, u32[]{:S(2)}, u32[]{:S(2)}) collective-permute-start(bf16[4,288,512]{2,1,0:T(8,128)(2,1)S(1)} %stack.25.refs_0_.after_ref.refs_6_), channel_id=1, source_target_pairs={{0,48},{1,13},{2,50},{3,15},{4,52},{5,1},{6,54},{7,3},{8,56},{9,5}... | collective-permute-start | bytes 3538952 | tf_op jit(solution)/shard_map/ppermute | solution.py:681
  47.4 16.8 %collective-permute-done.5.refs_3_ = bf16[256,4608]{1,0:T(8,128)(2,1)} collective-permute-done((bf16[256,4608]{1,0:T(8,128)(2,1)}, bf16[256,4608]{1,0:T(8,128)(2,1)}, u32[]{:S(2)}, u32[]{:S(2)}) %collective-permute-start.5) | collective-permute-done | bytes 2359328 | tf_op jit(solution)/shard_map/ppermute | solution.py:727
  64.2 5.5 %multiply.1.after_ref.acc_hbm = f32[512,512]{1,0:T(8,128)} custom-call(s32[5]{0:T(128)} %stack.24.here_ref.refs_0_, bf16[4,288,512]{2,1,0:T(8,128)(2,1)} %copy-done.1, bf16[4,288,512]{2,1,0:T(8,128)(2,1)} %copy-done.9, bf16[256,4608]{1,0:T(8,128)(2,1)} %get-tuple-element.53.refs_2_, bf16[256,4608]{1,0:T(8,128)(2,1)} %collective-permute-done.5.refs_3_), custom_call_target="tpu_custom_call" | custom-call | tf_op jit(solution)/shard_map/multiply/pallas_call | solution.py:273
  69.7 12.8 %all-to-all-done.1 = bf16[32,32,1024]{2,1,0:T(8,128)(2,1)} async-done(((bf16[32,32,1024]{2,1,0:T(8,128)(2,1)}), bf16[32,32,1024]{2,1,0:T(8,128)(2,1)}, u32[]{:S(2)}, u32[]{:S(2)}) %all-to-all-start.1) | async-done | bytes 2097184 | tf_op jit(solution)/shard_map/all_to_all | solution.py:714
  82.5 1.2 copy-done.4
  83.7 3.0 %unpack.1 = (bf16[512,512]{1,0:T(8,128)(2,1)S(1)}, bf16[512,512]{1,0:T(8,128)(2,1)S(1)}) custom-call(s32[512,1]{1,0:T(8,128)S(1)} %copy.28.slot_ref, bf16[1024,1024]{1,0:T(8,128)(2,1)} %bitcast.17.came_ref, f32[512,512]{1,0:T(8,128)S(1)} %copy-done.4), custom_call_target="tpu_custom_call" | custom-call | tf_op jit(solution)/shard_map/unpack/pallas_call | solution.py:169
  86.7 5.1 %merge.1 = (bf16[512,512]{1,0:T(8,128)(2,1)S(1)}, f32[512,512]{1,0:T(8,128)S(1)}, f32[8,512]{1,0:T(8,128)S(1)}) custom-call(s32[5]{0:T(128)S(1)} %copy-done.22, bf16[1,512]{1,0:T(2,128)(2,1)S(1)} %constant_dynamic-slice_fusion.1.ngain_ref.refs_1_, f32[512,512]{1,0:T(8,128)S(1)} %copy-done.5, bf16[512,512]{1,0:T(8,128)(2,1)S(1)} %get-tuple-element.55.base_hbm, ...), custom_call_target="tpu_custom_call" | custom-call | tf_op jit(solution)/shard_map/merge/pallas_call | solution.py:315
  91.9 1.2 collective-permute-done.8.got_ref
  93.1 2.6 %collective-permute-start.10 = (f32[8,512]{1,0:T(8,128)S(1)}, f32[8,512]{1,0:T(8,128)S(1)}, u32[]{:S(2)}, u32[]{:S(2)}) collective-permute-start(f32[8,512]{1,0:T(8,128)S(1)} %get-tuple-element.62.after_ref.refs_2_), channel_id=1, source_target_pairs={{0,2},{1,3},{2,0},{3,1},{64,66},{65,67},{66,64},{67,65},{4,6},{5,7... | collective-permute-start | bytes 49160 | tf_op jit(solution)/shard_map/ppermute | solution.py:669
  95.7 3.2 %collective-permute-start.11 = (f32[8,512]{1,0:T(8,128)S(1)}, f32[8,512]{1,0:T(8,128)S(1)}, u32[]{:S(2)}, u32[]{:S(2)}) collective-permute-start(f32[8,512]{1,0:T(8,128)S(1)} %get-tuple-element.61), channel_id=1, source_target_pairs={{0,66},{1,67},{2,64},{3,65},{64,0},{65,1},{66,2},{67,3},{4,70},{5,... | collective-permute-start | bytes 49160 | tf_op jit(solution)/shard_map/ppermute | solution.py:669
  98.9 1.4 pack.1
  100.4 2.4 %collective-permute-done.9.refs_3_ = f32[8,512]{1,0:T(8,128)S(1)} collective-permute-done((f32[8,512]{1,0:T(8,128)S(1)}, f32[8,512]{1,0:T(8,128)S(1)}, u32[]{:S(2)}, u32[]{:S(2)}) %collective-permute-start.9) | collective-permute-done | bytes 16416 | tf_op jit(solution)/shard_map/ppermute | solution.py:669
  102.7 5.5 %backward.1 = (bf16[64,4608]{1,0:T(8,128)(2,1)S(1)}, bf16[192,4608]{1,0:T(8,128)(2,1)S(1)}, bf16[64,4608]{1,0:T(8,128)(2,1)S(1)}, bf16[192,4608]{1,0:T(8,128)(2,1)S(1)}) custom-call(s32[5]{0:T(128)S(1)} %copy-done.22, bf16[1,512]{1,0:T(2,128)(2,1)S(1)} %constant_dynamic-slice_fusion.1.ngain_ref.refs_1_, f32[8,512]{1,0:T(8,128)S(1)} %get-tuple-element.62.after_ref.refs_2_, ...), custom_call_target="tpu_custom_call" | custom-call | tf_op jit(solution)/shard_map/backward/pallas_call | solution.py:454
  108.3 5.8 %collective-permute-done.12.after_ref.crossed_ref = bf16[512,512]{1,0:T(8,128)(2,1)S(1)} collective-permute-done((bf16[512,512]{1,0:T(8,128)(2,1)S(1)}, bf16[512,512]{1,0:T(8,128)(2,1)S(1)}, u32[]{:S(2)}, u32[]{:S(2)}) %collective-permute-start.12) | collective-permute-done | bytes 524320 | tf_op jit(solution)/shard_map/ppermute | solution.py:738
  114.1 3.0 %collective-permute-start.14 = (bf16[192,4608]{1,0:T(8,128)(2,1)S(1)}, bf16[192,4608]{1,0:T(8,128)(2,1)S(1)}, u32[]{:S(2)}, u32[]{:S(2)}) collective-permute-start(bf16[192,4608]{1,0:T(8,128)(2,1)S(1)} %get-tuple-element.75), channel_id=1, source_target_pairs={{0,1},{1,0},{2,3},{3,2},{4,5},{5,4},{6,7},{7,6},{8,9},{9,8},{10,11... | collective-permute-start | bytes 5308424 | tf_op jit(solution)/shard_map/ppermute | solution.py:744
  117.1 3.3 %collective-permute-done.14.got_ref = bf16[192,4608]{1,0:T(8,128)(2,1)S(1)} collective-permute-done((bf16[192,4608]{1,0:T(8,128)(2,1)S(1)}, bf16[192,4608]{1,0:T(8,128)(2,1)S(1)}, u32[]{:S(2)}, u32[]{:S(2)}) %collective-permute-start.14) | collective-permute-done | bytes 1769504 | tf_op jit(solution)/shard_map/ppermute | solution.py:744
  120.4 1.2 pair.1
  121.6 1.2 copy-done.7
  122.8 2.7 %collective-permute-start.16 = (bf16[64,4608]{1,0:T(8,128)(2,1)}, bf16[64,4608]{1,0:T(8,128)(2,1)}, u32[]{:S(2)}, u32[]{:S(2)}) collective-permute-start(bf16[64,4608]{1,0:T(8,128)(2,1)} %get-tuple-element.78), channel_id=1, source_target_pairs={{0,66},{1,67},{2,64},{3,65},{64,0},{65,1},{66,2},{67,3},{4,70},{5,... | collective-permute-start | bytes 1769480 | tf_op jit(solution)/shard_map/ppermute | solution.py:669
  126.6 3.8 %all-to-all-start.2 = ((bf16[16,2,32,512]{3,2,1,0:T(8,128)(2,1)}), bf16[16,2,32,512]{3,2,1,0:T(8,128)(2,1)S(1)}, u32[]{:S(2)}, u32[]{:S(2)}) async-start(bf16[16,2,32,512]{3,2,1,0:T(8,128)(2,1)} %copy-done.11), calls=%async_computation.2 | async-start | bytes 2097152 | tf_op jit(solution)/shard_map/all_to_all | solution.py:752
  130.4 1.2 collective-permute-start.13
  131.6 7.3 %collective-permute-done.15.from_last_ref.early_ref = bf16[64,4608]{1,0:T(8,128)(2,1)} collective-permute-done((bf16[64,4608]{1,0:T(8,128)(2,1)}, bf16[64,4608]{1,0:T(8,128)(2,1)}, u32[]{:S(2)}, u32[]{:S(2)}) %collective-permute-start.15) | collective-permute-done | bytes 589856 | tf_op jit(solution)/shard_map/ppermute | solution.py:669
  138.9 1.5 copy-done.8
  140.4 1.6 relay.1
  142.0 2.4 %collective-permute-start.17 = (bf16[32,4608]{1,0:T(8,128)(2,1)S(1)}, bf16[32,4608]{1,0:T(8,128)(2,1)S(1)}, u32[]{:S(2)}, u32[]{:S(2)}) collective-permute-start(bf16[32,4608]{1,0:T(8,128)(2,1)S(1)} %get-tuple-element.79), channel_id=1, source_target_pairs={{0,66},{1,67},{2,64},{3,65},{64,0},{65,1},{66,2},{67,3},{4,70},{5,... | collective-permute-start | bytes 884744 | tf_op jit(solution)/shard_map/ppermute | solution.py:669
  144.4 4.9 %collective-permute-done.17.late_ref = bf16[32,4608]{1,0:T(8,128)(2,1)S(1)} collective-permute-done((bf16[32,4608]{1,0:T(8,128)(2,1)S(1)}, bf16[32,4608]{1,0:T(8,128)(2,1)S(1)}, u32[]{:S(2)}, u32[]{:S(2)}) %collective-permute-start.17) | collective-permute-done | bytes 294944 | tf_op jit(solution)/shard_map/ppermute | solution.py:669
  149.3 2.4 %finish.2.refs_1_ = bf16[128,1152]{1,0:T(8,128)(2,1)S(1)} custom-call(s32[5]{0:T(128)S(1)} %copy-done.22, bf16[64,4608]{1,0:T(8,128)(2,1)S(1)} %copy-done.17, bf16[64,4608]{1,0:T(8,128)(2,1)S(1)} %collective-permute-done.13.got_ref, bf16[64,4608]{1,0:T(8,128)(2,1)} %collective-permute-done.15.from_last_ref.early_ref, ...), custom_call_target="tpu_custom_call" | custom-call | tf_op jit(solution)/shard_map/finish/pallas_call | solution.py:560
  151.8 2.1 %collective-permute-start.18 = (bf16[128,1152]{1,0:T(8,128)(2,1)S(1)}, bf16[128,1152]{1,0:T(8,128)(2,1)}, u32[]{:S(2)}, u32[]{:S(2)}) collective-permute-start(bf16[128,1152]{1,0:T(8,128)(2,1)S(1)} %finish.2.refs_1_), channel_id=1, source_target_pairs={{0,2},{1,3},{2,0},{3,1},{4,6},{5,7},{6,4},{7,5},{8,10},{9,11},{10,... | collective-permute-start | bytes 884744 | tf_op jit(solution)/shard_map/ppermute | solution.py:759
  153.9 3.1 %finish.3.refs_0_ = bf16[128,1152]{1,0:T(8,128)(2,1)} custom-call(s32[5]{0:T(128)S(1)} %copy-done.22, bf16[64,4608]{1,0:T(8,128)(2,1)S(1)} %copy-done.17, bf16[64,4608]{1,0:T(8,128)(2,1)S(1)} %collective-permute-done.13.got_ref, bf16[64,4608]{1,0:T(8,128)(2,1)} %collective-permute-done.16.from_next_ref.early_ref, ...), custom_call_target="tpu_custom_call" | custom-call | tf_op jit(solution)/shard_map/finish/pallas_call | solution.py:560
  158.0 2.4 %place.1 = bf16[512,1024]{1,0:T(8,128)(2,1)} custom-call(s32[5]{0:T(128)S(1)} %copy-done.22, s32[512,1]{1,0:T(8,128)S(1)} %copy-done.15, bf16[16,2,32,512]{3,2,1,0:T(8,128)(2,1)S(1)} %all-to-all-done.2.came_ref, bf16[512,1024]{1,0:T(8,128)(2,1)S(1)} %copy-done.13), custom_call_target="tpu_custom_call" | custom-call | tf_op jit(solution)/shard_map/place/pallas_call | solution.py:601
  160.4 2.8 %collective-permute-start.21 = (bf16[128,1152]{1,0:T(8,128)(2,1)}, bf16[128,1152]{1,0:T(8,128)(2,1)S(1)}, u32[]{:S(2)}, u32[]{:S(2)}) collective-permute-start(bf16[128,1152]{1,0:T(8,128)(2,1)} %finish.3.refs_0_), channel_id=1, source_target_pairs={{0,1},{1,0},{2,3},{3,2},{4,5},{5,4},{6,7},{7,6},{8,9},{9,8},{10,11... | collective-permute-start | bytes 884744 | tf_op jit(solution)/shard_map/ppermute | solution.py:761
  163.2 3.6 %collective-permute-done.20.refs_2_ = bf16[128,1152]{1,0:T(8,128)(2,1)} collective-permute-done((bf16[128,1152]{1,0:T(8,128)(2,1)}, bf16[128,1152]{1,0:T(8,128)(2,1)}, u32[]{:S(2)}, u32[]{:S(2)}) %collective-permute-start.20) | collective-permute-done | bytes 294944 | tf_op jit(solution)/shard_map/ppermute | solution.py:759
  166.8 2.4 %collective-permute-start.23 = (bf16[128,1152]{1,0:T(8,128)(2,1)}, bf16[128,1152]{1,0:T(8,128)(2,1)S(1)}, u32[]{:S(2)}, u32[]{:S(2)}) collective-permute-start(bf16[128,1152]{1,0:T(8,128)(2,1)} %collective-permute-done.20.refs_2_), channel_id=1, source_target_pairs={{0,1},{1,0},{2,3},{3,2},{4,5},{5,4},{6,7},{7,6},{8,9},{9,8},{10,11... | collective-permute-start | bytes 884744 | tf_op jit(solution)/shard_map/ppermute | solution.py:761
  169.2 1.4 collective-permute-done.23.refs_6_
  171.1 2.6 %lay.1 = bf16[1024,1152]{1,0:T(8,128)(2,1)} custom-call(s32[5]{0:T(128)S(1)} %copy-done.22, bf16[128,1152]{1,0:T(8,128)(2,1)} %finish.3.refs_0_, bf16[128,1152]{1,0:T(8,128)(2,1)S(1)} %finish.2.refs_1_, bf16[128,1152]{1,0:T(8,128)(2,1)} %collective-permute-done.20.refs_2_, bf16[128,1152]{1,0:T(8,128)(2,1)} %collective-permute-done.18.refs_3_, ...), custom_call_target="tpu_custom_call" | custom-call | tf_op jit(solution)/shard_map/lay/pallas_call | solution.py:629
  (87 shorter events, 8.2 us)
Async XLA Ops:
  1.7 26.4 %collective-permute-start = (bf16[288,512]{1,0:T(8,128)(2,1)S(1)}, bf16[288,512]{1,0:T(8,128)(2,1)S(1)}, u32[]{:S(2)}, u32[]{:S(2)}) collective-permute-start(bf16[288,512]{1,0:T(8,128)(2,1)S(1)} %bitcast.22), channel_id=1, source_target_pairs={{0,4},{1,17},{2,6},{3,19},{4,8},{5,21},{6,10},{7,23},{8,12},{9,25}... | collective-permute-start | bytes 884744 | tf_op jit(solution)/shard_map/ppermute | solution.py:681
  4.3 23.8 %collective-permute-start.1 = (bf16[288,512]{1,0:T(8,128)(2,1)S(1)}, bf16[288,512]{1,0:T(8,128)(2,1)S(1)}, u32[]{:S(2)}, u32[]{:S(2)}) collective-permute-start(bf16[288,512]{1,0:T(8,128)(2,1)S(1)} %bitcast.23), channel_id=1, source_target_pairs={{0,12},{1,49},{2,14},{3,51},{4,0},{5,53},{6,2},{7,55},{8,4},{9,57}... | collective-permute-start | bytes 884744 | tf_op jit(solution)/shard_map/ppermute | solution.py:681
  6.5 21.7 %collective-permute-start.2 = (bf16[288,512]{1,0:T(8,128)(2,1)S(1)}, bf16[288,512]{1,0:T(8,128)(2,1)S(1)}, u32[]{:S(2)}, u32[]{:S(2)}) collective-permute-start(bf16[288,512]{1,0:T(8,128)(2,1)S(1)} %bitcast.24), channel_id=1, source_target_pairs={{0,8},{1,33},{2,10},{3,35},{4,12},{5,37},{6,14},{7,39},{8,0},{9,41... | collective-permute-start | bytes 884744 | tf_op jit(solution)/shard_map/ppermute | solution.py:681
  9.5 18.6 %all-to-all-start = ((s32[32,1,16]{2,1,0:T(1,128)}), s32[32,1,16]{2,1,0:T(1,128)S(1)}, u32[]{:S(2)}, u32[]{:S(2)}) async-start(s32[32,1,16]{2,1,0:T(1,128)} %bitcast.5), calls=%async_computation | async-start | bytes 32768 | tf_op jit(solution)/shard_map/all_to_all | solution.py:693
  16.5 11.6 %collective-permute-start.3 = (s32[256]{0:T(256)S(1)}, s32[256]{0:T(256)S(1)}, u32[]{:S(2)}, u32[]{:S(2)}) collective-permute-start(s32[256]{0:T(256)S(1)} %get-tuple-element.88), channel_id=1, source_target_pairs={{0,64},{64,0},{1,65},{65,1},{2,66},{66,2},{3,67},{67,3},{4,68},{68... | collective-permute-start | bytes 3080 | tf_op jit(solution)/shard_map/ppermute | solution.py:700
  18.5 9.6 %copy-start.21 = (s32[5]{0:T(128)S(1)}, s32[5]{0:T(128)}, u32[]{:S(2)}) copy-start(s32[5]{0:T(128)} %stack.24.here_ref.refs_0_) | copy-start | bytes 64
  29.0 15.0 %copy-start.1 = (bf16[4,288,512]{2,1,0:T(8,128)(2,1)}, bf16[4,288,512]{2,1,0:T(8,128)(2,1)S(1)}, u32[]{:S(2)}) copy-start(bf16[4,288,512]{2,1,0:T(8,128)(2,1)S(1)} %stack.25.refs_0_.after_ref.refs_6_) | copy-start | bytes 3538948
  29.0 35.2 %collective-permute-start.5 = (bf16[256,4608]{1,0:T(8,128)(2,1)}, bf16[256,4608]{1,0:T(8,128)(2,1)}, u32[]{:S(2)}, u32[]{:S(2)}) collective-permute-start(bf16[256,4608]{1,0:T(8,128)(2,1)} %get-tuple-element.53.refs_2_), channel_id=1, source_target_pairs={{0,64},{1,67},{2,66},{3,65},{64,2},{65,1},{66,0},{67,3},{4,68},{5,... | collective-permute-start | bytes 7077896 | tf_op jit(solution)/shard_map/ppermute | solution.py:727
  30.6 16.7 %collective-permute-start.4 = (bf16[4,288,512]{2,1,0:T(8,128)(2,1)S(1)}, bf16[4,288,512]{2,1,0:T(8,128)(2,1)S(1)}, u32[]{:S(2)}, u32[]{:S(2)}) collective-permute-start(bf16[4,288,512]{2,1,0:T(8,128)(2,1)S(1)} %stack.25.refs_0_.after_ref.refs_6_), channel_id=1, source_target_pairs={{0,16},{1,5},{2,18},{3,7},{4,20},{5,9},{6,22},{7,11},{8,24},{9,13}... | collective-permute-start | bytes 3538952 | tf_op jit(solution)/shard_map/ppermute | solution.py:681
  32.0 3.9 %copy-start.14 = (s32[512,1]{1,0:T(8,128)}, s32[512,1]{1,0:T(8,128)S(1)}, u32[]{:S(2)}) copy-start(s32[512,1]{1,0:T(8,128)S(1)} %reshape.38.pos_ref) | copy-start | bytes 6148
  32.0 1.3 copy-start.12
  35.9 1.4 copy-start.6
  37.3 10.0 %copy-start.24 = (bf16[1,1024]{1,0:T(2,128)(2,1)S(1)}, bf16[1,1024]{1,0:T(2,128)(2,1)}, u32[]{:S(2)}) copy-start(bf16[1,1024]{1,0:T(2,128)(2,1)} %param.13) | copy-start | bytes 6148
  37.3 45.2 %all-to-all-start.1 = ((bf16[32,32,1024]{2,1,0:T(8,128)(2,1)}), bf16[32,32,1024]{2,1,0:T(8,128)(2,1)}, u32[]{:S(2)}, u32[]{:S(2)}) async-start(bf16[32,32,1024]{2,1,0:T(8,128)(2,1)} %bitcast.21), calls=%async_computation.1 | async-start | bytes 4194304 | tf_op jit(solution)/shard_map/all_to_all | solution.py:714
  44.0 42.7 %collective-permute-start.6 = (bf16[4,288,512]{2,1,0:T(8,128)(2,1)S(1)}, bf16[4,288,512]{2,1,0:T(8,128)(2,1)}, u32[]{:S(2)}, u32[]{:S(2)}) collective-permute-start(bf16[4,288,512]{2,1,0:T(8,128)(2,1)S(1)} %stack.25.refs_0_.after_ref.refs_6_), channel_id=1, source_target_pairs={{0,48},{1,13},{2,50},{3,15},{4,52},{5,1},{6,54},{7,3},{8,56},{9,5}... | collective-permute-start | bytes 3538952 | tf_op jit(solution)/shard_map/ppermute | solution.py:681
  47.2 17.0 %copy-start.9 = (bf16[4,288,512]{2,1,0:T(8,128)(2,1)}, bf16[4,288,512]{2,1,0:T(8,128)(2,1)S(1)}, u32[]{:S(2)}) copy-start(bf16[4,288,512]{2,1,0:T(8,128)(2,1)S(1)} %collective-permute-done.4.refs_1_.refs_7_) | copy-start | bytes 3538948
  47.2 39.5 %collective-permute-start.7 = (bf16[4,288,512]{2,1,0:T(8,128)(2,1)S(1)}, bf16[4,288,512]{2,1,0:T(8,128)(2,1)}, u32[]{:S(2)}, u32[]{:S(2)}) collective-permute-start(bf16[4,288,512]{2,1,0:T(8,128)(2,1)S(1)} %collective-permute-done.4.refs_1_.refs_7_), channel_id=1, source_target_pairs={{0,16},{1,5},{2,18},{3,7},{4,20},{5,9},{6,22},{7,11},{8,24},{9,13}... | collective-permute-start | bytes 3538952 | tf_op jit(solution)/shard_map/ppermute | solution.py:681
  69.7 17.0 %copy-start.22 = (s32[5]{0:T(128)S(1)}, s32[5]{0:T(128)}, u32[]{:S(2)}) copy-start(s32[5]{0:T(128)} %stack.24.here_ref.refs_0_) | copy-start | bytes 64
  83.7 3.0 %copy-start.5 = (f32[512,512]{1,0:T(8,128)S(1)}, f32[512,512]{1,0:T(8,128)}, u32[]{:S(2)}) copy-start(f32[512,512]{1,0:T(8,128)} %multiply.1.after_ref.acc_hbm) | copy-start | bytes 3145732
  86.7 16.0 %copy-start.2 = (bf16[4,288,512]{2,1,0:T(8,128)(2,1)S(1)}, bf16[4,288,512]{2,1,0:T(8,128)(2,1)}, u32[]{:S(2)}) copy-start(bf16[4,288,512]{2,1,0:T(8,128)(2,1)} %copy-done.1) | copy-start | bytes 3538948
  86.7 16.0 %copy-start.10 = (bf16[4,288,512]{2,1,0:T(8,128)(2,1)S(1)}, bf16[4,288,512]{2,1,0:T(8,128)(2,1)}, u32[]{:S(2)}) copy-start(bf16[4,288,512]{2,1,0:T(8,128)(2,1)} %copy-done.9) | copy-start | bytes 3538948
  91.8 1.3 collective-permute-start.8
  93.1 7.2 %collective-permute-start.10 = (f32[8,512]{1,0:T(8,128)S(1)}, f32[8,512]{1,0:T(8,128)S(1)}, u32[]{:S(2)}, u32[]{:S(2)}) collective-permute-start(f32[8,512]{1,0:T(8,128)S(1)} %get-tuple-element.62.after_ref.refs_2_), channel_id=1, source_target_pairs={{0,2},{1,3},{2,0},{3,1},{64,66},{65,67},{66,64},{67,65},{4,6},{5,7... | collective-permute-start | bytes 49160 | tf_op jit(solution)/shard_map/ppermute | solution.py:669
  95.7 4.7 %collective-permute-start.11 = (f32[8,512]{1,0:T(8,128)S(1)}, f32[8,512]{1,0:T(8,128)S(1)}, u32[]{:S(2)}, u32[]{:S(2)}) collective-permute-start(f32[8,512]{1,0:T(8,128)S(1)} %get-tuple-element.61), channel_id=1, source_target_pairs={{0,66},{1,67},{2,64},{3,65},{64,0},{65,1},{66,2},{67,3},{4,70},{5,... | collective-permute-start | bytes 49160 | tf_op jit(solution)/shard_map/ppermute | solution.py:669
  98.9 3.8 %collective-permute-start.9 = (f32[8,512]{1,0:T(8,128)S(1)}, f32[8,512]{1,0:T(8,128)S(1)}, u32[]{:S(2)}, u32[]{:S(2)}) collective-permute-start(f32[8,512]{1,0:T(8,128)S(1)} %get-tuple-element.61), channel_id=1, source_target_pairs={{0,64},{1,65},{2,66},{3,67},{64,2},{65,3},{66,0},{67,1},{4,68},{5,... | collective-permute-start | bytes 49160 | tf_op jit(solution)/shard_map/ppermute | solution.py:669
  102.7 11.4 %collective-permute-start.12 = (bf16[512,512]{1,0:T(8,128)(2,1)S(1)}, bf16[512,512]{1,0:T(8,128)(2,1)S(1)}, u32[]{:S(2)}, u32[]{:S(2)}) collective-permute-start(bf16[512,512]{1,0:T(8,128)(2,1)S(1)} %get-tuple-element.71), channel_id=1, source_target_pairs={{0,64},{64,0},{1,65},{65,1},{2,66},{66,2},{3,67},{67,3},{4,68},{68... | collective-permute-start | bytes 1572872 | tf_op jit(solution)/shard_map/ppermute | solution.py:738
  108.3 17.2 %copy-start.16 = (bf16[64,4608]{1,0:T(8,128)(2,1)}, bf16[64,4608]{1,0:T(8,128)(2,1)S(1)}, u32[]{:S(2)}) copy-start(bf16[64,4608]{1,0:T(8,128)(2,1)S(1)} %get-tuple-element.72.own_ref) | copy-start | bytes 1769476
  108.3 17.2 %copy-start.23 = (bf16[64,4608]{1,0:T(8,128)(2,1)}, bf16[64,4608]{1,0:T(8,128)(2,1)S(1)}, u32[]{:S(2)}) copy-start(bf16[64,4608]{1,0:T(8,128)(2,1)S(1)} %get-tuple-element.73) | copy-start | bytes 1769476
  114.1 6.3 %collective-permute-start.14 = (bf16[192,4608]{1,0:T(8,128)(2,1)S(1)}, bf16[192,4608]{1,0:T(8,128)(2,1)S(1)}, u32[]{:S(2)}, u32[]{:S(2)}) collective-permute-start(bf16[192,4608]{1,0:T(8,128)(2,1)S(1)} %get-tuple-element.75), channel_id=1, source_target_pairs={{0,1},{1,0},{2,3},{3,2},{4,5},{5,4},{6,7},{7,6},{8,9},{9,8},{10,11... | collective-permute-start | bytes 5308424 | tf_op jit(solution)/shard_map/ppermute | solution.py:744
  122.8 16.1 %collective-permute-start.15 = (bf16[64,4608]{1,0:T(8,128)(2,1)}, bf16[64,4608]{1,0:T(8,128)(2,1)}, u32[]{:S(2)}, u32[]{:S(2)}) collective-permute-start(bf16[64,4608]{1,0:T(8,128)(2,1)} %get-tuple-element.77), channel_id=1, source_target_pairs={{0,64},{1,65},{2,66},{3,67},{64,2},{65,3},{66,0},{67,1},{4,68},{5,... | collective-permute-start | bytes 1769480 | tf_op jit(solution)/shard_map/ppermute | solution.py:669
  122.8 16.1 %collective-permute-start.16 = (bf16[64,4608]{1,0:T(8,128)(2,1)}, bf16[64,4608]{1,0:T(8,128)(2,1)}, u32[]{:S(2)}, u32[]{:S(2)}) collective-permute-start(bf16[64,4608]{1,0:T(8,128)(2,1)} %get-tuple-element.78), channel_id=1, source_target_pairs={{0,66},{1,67},{2,64},{3,65},{64,0},{65,1},{66,2},{67,3},{4,70},{5,... | collective-permute-start | bytes 1769480 | tf_op jit(solution)/shard_map/ppermute | solution.py:669
  126.6 22.8 %copy-start.19 = (f32[256,128]{1,0:T(8,128)S(1)}, f32[256,128]{1,0:T(8,128)}, u32[]{:S(2)}) copy-start(f32[256,128]{1,0:T(8,128)} %get-tuple-element.81.stat_ref) | copy-start | bytes 393220
  126.6 22.8 %copy-start.20 = (bf16[1,4,1152]{2,1,0:T(4,128)(2,1)S(1)}, bf16[1,4,1152]{2,1,0:T(4,128)(2,1)}, u32[]{:S(2)}) copy-start(bf16[1,4,1152]{2,1,0:T(4,128)(2,1)} %param.9) | copy-start | bytes 27652
  126.6 31.4 %all-to-all-start.2 = ((bf16[16,2,32,512]{3,2,1,0:T(8,128)(2,1)}), bf16[16,2,32,512]{3,2,1,0:T(8,128)(2,1)S(1)}, u32[]{:S(2)}, u32[]{:S(2)}) async-start(bf16[16,2,32,512]{3,2,1,0:T(8,128)(2,1)} %copy-done.11), calls=%async_computation.2 | async-start | bytes 2097152 | tf_op jit(solution)/shard_map/all_to_all | solution.py:752
  130.4 19.0 %copy-start.3 = (bf16[4,256,1152]{2,1,0:T(8,128)(2,1)S(1)}, bf16[4,256,1152]{2,1,0:T(8,128)(2,1)}, u32[]{:S(2)}) copy-start(bf16[4,256,1152]{2,1,0:T(8,128)(2,1)} %get-tuple-element.80.xw_ref) | copy-start | bytes 7077892
  130.4 14.0 %collective-permute-start.13 = (bf16[64,4608]{1,0:T(8,128)(2,1)}, bf16[64,4608]{1,0:T(8,128)(2,1)S(1)}, u32[]{:S(2)}, u32[]{:S(2)}) collective-permute-start(bf16[64,4608]{1,0:T(8,128)(2,1)} %copy-done.23), channel_id=1, source_target_pairs={{0,1},{1,0},{2,3},{3,2},{4,5},{5,4},{6,7},{7,6},{8,9},{9,8},{10,11... | collective-permute-start | bytes 1769480 | tf_op jit(solution)/shard_map/ppermute | solution.py:745
  138.9 1.5 copy-start.8
  140.4 9.0 %copy-start.17 = (bf16[64,4608]{1,0:T(8,128)(2,1)S(1)}, bf16[64,4608]{1,0:T(8,128)(2,1)}, u32[]{:S(2)}) copy-start(bf16[64,4608]{1,0:T(8,128)(2,1)} %copy-done.16) | copy-start | bytes 1769476
  142.0 7.4 %collective-permute-start.17 = (bf16[32,4608]{1,0:T(8,128)(2,1)S(1)}, bf16[32,4608]{1,0:T(8,128)(2,1)S(1)}, u32[]{:S(2)}, u32[]{:S(2)}) collective-permute-start(bf16[32,4608]{1,0:T(8,128)(2,1)S(1)} %get-tuple-element.79), channel_id=1, source_target_pairs={{0,66},{1,67},{2,64},{3,65},{64,0},{65,1},{66,2},{67,3},{4,70},{5,... | collective-permute-start | bytes 884744 | tf_op jit(solution)/shard_map/ppermute | solution.py:669
  144.4 9.5 %collective-permute-start.19 = (bf16[32,4608]{1,0:T(8,128)(2,1)S(1)}, bf16[32,4608]{1,0:T(8,128)(2,1)S(1)}, u32[]{:S(2)}, u32[]{:S(2)}) collective-permute-start(bf16[32,4608]{1,0:T(8,128)(2,1)S(1)} %get-tuple-element.84), channel_id=1, source_target_pairs={{0,64},{1,65},{2,66},{3,67},{64,2},{65,3},{66,0},{67,1},{4,68},{5,... | collective-permute-start | bytes 884744 | tf_op jit(solution)/shard_map/ppermute | solution.py:669
  151.8 6.2 %copy-start.13 = (bf16[512,1024]{1,0:T(8,128)(2,1)S(1)}, bf16[512,1024]{1,0:T(8,128)(2,1)}, u32[]{:S(2)}) copy-start(bf16[512,1024]{1,0:T(8,128)(2,1)} %stream_ref.3) | copy-start | bytes 3145732
  151.8 6.2 %copy-start.15 = (s32[512,1]{1,0:T(8,128)S(1)}, s32[512,1]{1,0:T(8,128)}, u32[]{:S(2)}) copy-start(s32[512,1]{1,0:T(8,128)} %copy-done.14) | copy-start | bytes 6148
  151.8 11.4 %collective-permute-start.18 = (bf16[128,1152]{1,0:T(8,128)(2,1)S(1)}, bf16[128,1152]{1,0:T(8,128)(2,1)}, u32[]{:S(2)}, u32[]{:S(2)}) collective-permute-start(bf16[128,1152]{1,0:T(8,128)(2,1)S(1)} %finish.2.refs_1_), channel_id=1, source_target_pairs={{0,2},{1,3},{2,0},{3,1},{4,6},{5,7},{6,4},{7,5},{8,10},{9,11},{10,... | collective-permute-start | bytes 884744 | tf_op jit(solution)/shard_map/ppermute | solution.py:759
  157.0 9.7 %collective-permute-start.20 = (bf16[128,1152]{1,0:T(8,128)(2,1)}, bf16[128,1152]{1,0:T(8,128)(2,1)}, u32[]{:S(2)}, u32[]{:S(2)}) collective-permute-start(bf16[128,1152]{1,0:T(8,128)(2,1)} %finish.3.refs_0_), channel_id=1, source_target_pairs={{0,2},{1,3},{2,0},{3,1},{4,6},{5,7},{6,4},{7,5},{8,10},{9,11},{10,... | collective-permute-start | bytes 884744 | tf_op jit(solution)/shard_map/ppermute | solution.py:759
  160.4 8.9 %collective-permute-start.21 = (bf16[128,1152]{1,0:T(8,128)(2,1)}, bf16[128,1152]{1,0:T(8,128)(2,1)S(1)}, u32[]{:S(2)}, u32[]{:S(2)}) collective-permute-start(bf16[128,1152]{1,0:T(8,128)(2,1)} %finish.3.refs_0_), channel_id=1, source_target_pairs={{0,1},{1,0},{2,3},{3,2},{4,5},{5,4},{6,7},{7,6},{8,9},{9,8},{10,11... | collective-permute-start | bytes 884744 | tf_op jit(solution)/shard_map/ppermute | solution.py:761
  163.2 6.1 %collective-permute-start.22 = (bf16[128,1152]{1,0:T(8,128)(2,1)S(1)}, bf16[128,1152]{1,0:T(8,128)(2,1)S(1)}, u32[]{:S(2)}, u32[]{:S(2)}) collective-permute-start(bf16[128,1152]{1,0:T(8,128)(2,1)S(1)} %finish.2.refs_1_), channel_id=1, source_target_pairs={{0,1},{1,0},{2,3},{3,2},{4,5},{5,4},{6,7},{7,6},{8,9},{9,8},{10,11... | collective-permute-start | bytes 884744 | tf_op jit(solution)/shard_map/ppermute | solution.py:761
  166.8 3.9 %collective-permute-start.23 = (bf16[128,1152]{1,0:T(8,128)(2,1)}, bf16[128,1152]{1,0:T(8,128)(2,1)S(1)}, u32[]{:S(2)}, u32[]{:S(2)}) collective-permute-start(bf16[128,1152]{1,0:T(8,128)(2,1)} %collective-permute-done.20.refs_2_), channel_id=1, source_target_pairs={{0,1},{1,0},{2,3},{3,2},{4,5},{5,4},{6,7},{7,6},{8,9},{9,8},{10,11... | collective-permute-start | bytes 884744 | tf_op jit(solution)/shard_map/ppermute | solution.py:761
  169.2 1.8 %collective-permute-start.24 = (bf16[128,1152]{1,0:T(8,128)(2,1)}, bf16[128,1152]{1,0:T(8,128)(2,1)S(1)}, u32[]{:S(2)}, u32[]{:S(2)}) collective-permute-start(bf16[128,1152]{1,0:T(8,128)(2,1)} %collective-permute-done.18.refs_3_), channel_id=1, source_target_pairs={{0,1},{1,0},{2,3},{3,2},{4,5},{5,4},{6,7},{7,6},{8,9},{9,8},{10,11... | collective-permute-start | bytes 884744 | tf_op jit(solution)/shard_map/ppermute | solution.py:761
  (5 other events, 5.7 us)
